TPU v7x, 32 devices: a whole 2x2x4 slice. The times are simulated.
32 devices in a mesh: expert: 4 (over x, core), dp: 8 (over z, y).
Axes of the slice: x: 2, y: 2, z: 4, core: 2. Of those that a mesh axis runs over, the one named last changes fastest.
Arguments:
- out_grad: bfloat16 [2048, 3072], P(('expert', 'dp')), may hold values from -6 to 6
- gate_saved: bfloat16 [2048, 2, 8192], P('expert', None, 'dp'), may hold values from -6 to 6
- up_saved: bfloat16 [2048, 2, 8192], P('expert', None, 'dp'), may hold values from -6 to 6
- routing: int32 [2048, 2], P('expert'), may hold values from 0 to 3, all different within a row; in each aligned block of 512 rows (0 to 511, 512 to 1023, ...) at most 512 rows name the same one
- down_weight: bfloat16 [4, 3072, 8192], P('expert', None, 'dp'), may hold values from -0.0625 to 0.0625
- momentum: bfloat16 [4, 3072, 8192], P('expert', 'dp'), may hold values from -60 to 60
Outputs:
- d_gate: bfloat16 [2048, 2, 8192], P('expert', None, 'dp')
- d_up: bfloat16 [2048, 2, 8192], P('expert', None, 'dp')
- new_weight: float32 [4, 3072, 8192], P('expert', 'dp')
- new_momentum: bfloat16 [4, 3072, 8192], P('expert', 'dp')
Inputs may be any that keep to these rules, and one draw needn't show every extreme that they name: `routing`: in each aligned block of 512 tokens (one group), the 2 experts of a token differ, no expert is named by more than 512 tokens, a bound that some block reaches.
All inputs are finite; a program needn't handle non-finite values.
Results may differ from a plain program's by a relative error of at most 0.0015.
Values may be sent and summed in bfloat16 or wider, within the bound.
No kernel may reach another device: no remote copies, remote signals or barrier semaphores. Data moves between devices by JAX's collectives and lax.ppermute only.
A program may use at most 128 MiB of HBM per device.

v0:
```python
import jax
import jax.numpy as jnp
from jax import lax
from jax.sharding import PartitionSpec as P

beta_first = 0.9
beta_second = 0.99
step_rate = 0.01
decay_rate = 1.0
sign_width = 10.0


def shifted(array, axis, by):
    size = lax.axis_size(axis)
    return lax.ppermute(array, axis, [(i, (i + by) % size) for i in range(size)])


def slot_table(flat_route, experts, capacity):
    count_rows = flat_route.shape[0]
    onehot = (flat_route[:, None] == jnp.arange(experts, dtype=jnp.int32)[None, :]).astype(
        jnp.int32
    )
    before = jnp.cumsum(onehot, axis=0) - onehot
    place = jnp.sum(before * onehot, axis=1)
    table = jnp.full((experts, capacity), count_rows, jnp.int32)
    table = table.at[flat_route, place].set(jnp.arange(count_rows, dtype=jnp.int32))
    return (table, jnp.sum(onehot, axis=0))


def body(out_grad, gate_saved, up_saved, routing, down_weight, momentum):
    grads_all = lax.all_gather(out_grad, "dp", axis=0, tiled=True)
    group_tok, topk, cols = gate_saved.shape
    count_rows = group_tok * topk
    width = grads_all.shape[1]
    experts = lax.axis_size("expert")
    capacity = min(group_tok, 2 * count_rows // experts)
    gate_rows = gate_saved.reshape(count_rows, cols).astype(jnp.float32)
    up_rows = up_saved.reshape(count_rows, cols).astype(jnp.float32)
    sigma = jax.nn.sigmoid(gate_rows)
    hidden = (gate_rows * sigma * up_rows).astype(jnp.bfloat16)
    hidden_pad = jnp.concatenate([hidden, jnp.zeros((1, cols), jnp.bfloat16)], axis=0)
    grads_pad = jnp.concatenate([grads_all, jnp.zeros((1, width), jnp.bfloat16)], axis=0)
    table, counts = slot_table(routing.reshape(count_rows), experts, capacity)
    mine = lax.axis_index("expert")
    weight_now = down_weight[0]
    carried = jnp.zeros((width, cols), jnp.bfloat16)
    deriv = jnp.zeros((count_rows + 1, cols), jnp.float32)
    for step in range(experts):
        process_deriv = deriv
        slots = table[(mine - step) % experts]
        block_deriv = process_deriv
        upstream = grads_pad[slots // topk]
        picked = hidden_pad[slots]
        block_deriv = block_deriv.at[slots].set(
            jnp.dot(upstream, weight_now, preferred_element_type=jnp.float32)
        )
        total = lax.dot_general(
            upstream, picked, (((0,), (0,)), ((), ())), preferred_element_type=jnp.float32
        )
        process_deriv = block_deriv
        carried, deriv = ((carried.astype(jnp.float32) + total).astype(jnp.bfloat16), process_deriv)
        if step + 1 < experts:
            weight_now, carried = shifted((weight_now, carried), "expert", 1)
        else:
            carried = shifted(carried, "expert", 1)
    dh_rows = deriv[:count_rows]
    d_up = (dh_rows * gate_rows * sigma).astype(jnp.bfloat16).reshape(group_tok, topk, cols)
    d_gate = (
        (dh_rows * up_rows * sigma * (1.0 + gate_rows * (1.0 - sigma)))
        .astype(jnp.bfloat16)
        .reshape(group_tok, topk, cols)
    )
    shard_grad, shard_weight = (
        lax.all_to_all(carried[None], "dp", split_axis=1, concat_axis=2, tiled=True),
        lax.all_to_all(down_weight, "dp", split_axis=1, concat_axis=2, tiled=True),
    )
    grad = shard_grad.astype(jnp.float32)
    moment = momentum.astype(jnp.float32)
    mix = beta_first * moment + (1.0 - beta_first) * grad
    new_weight = shard_weight.astype(jnp.float32) * (
        1.0 - step_rate * decay_rate
    ) - step_rate * jnp.tanh(mix / sign_width)
    new_momentum = (beta_second * moment + (1.0 - beta_second) * grad).astype(jnp.bfloat16)
    return (d_gate, d_up, new_weight, new_momentum)


def solution(mesh):
    placed = (
        P(("expert", "dp"), None),
        P("expert", None, "dp"),
        P("expert", None, "dp"),
        P("expert", None),
        P("expert", None, "dp"),
        P("expert", "dp", None),
    )
    return jax.shard_map(
        body,
        mesh=mesh,
        in_specs=placed,
        out_specs=(
            P("expert", None, "dp"),
            P("expert", None, "dp"),
            P("expert", "dp", None),
            P("expert", "dp", None),
        ),
        check_vma=False,
    )
```

profile of v0, /device:TPU:8, one launch (start us, length us, event | category | flops | bytes accessed | tf_op | source)
XLA Modules:
  0.0 941.0 jit_solution(14713749490861396869)
XLA Ops:
  7.3 70.7 %collective-permute-done = bf16[3072,1024]{1,0:T(8,128)(2,1)} collective-permute-done((bf16[3072,1024]{1,0:T(8,128)(2,1)}, bf16[3072,1024]{1,0:T(8,128)(2,1)}, u32[]{:S(2)}, u32[]{:S(2)}) %collective-permute-start) | collective-permute-done | bytes 6291488 | tf_op jit(solution)/shard_map/ppermute | solution.py:15
  78.0 70.7 %collective-permute-done.1 = bf16[3072,1024]{1,0:T(8,128)(2,1)} collective-permute-done((bf16[3072,1024]{1,0:T(8,128)(2,1)}, bf16[3072,1024]{1,0:T(8,128)(2,1)}, u32[]{:S(2)}, u32[]{:S(2)}) %collective-permute-start.1) | collective-permute-done | bytes 6291488 | tf_op jit(solution)/shard_map/ppermute | solution.py:15
  148.7 0.8 copy.19
  150.1 1.1 reduce-window.6
  151.2 0.2 slice_reduce_fusion
  151.4 0.2 reduce-window.9
  151.7 0.7 multiply_reduce_fusion
  152.5 0.8 and_reduce_fusion
  153.3 4.6 scatter_custom_fusion.4
  157.9 4.4 reshape.550
  162.3 2.6 reshape.549
  165.0 2.1 concatenate.10
  167.2 3.9 gather_fusion
  171.0 3.8 gather_fusion.1
  174.8 3.8 gather_fusion.2
  178.7 3.8 gather_fusion.3
  182.5 8.5 fusion.15
  191.0 6.2 scatter_custom_fusion
  197.2 7.5 fusion.17
  204.7 7.6 scatter_fusion
  212.3 7.5 fusion.18
  219.8 7.7 scatter_fusion.1
  227.6 7.5 fusion.19
  235.1 7.4 scatter_fusion.2
  242.5 7.3 multiply_convert_fusion.1
  250.0 2.1 gather_fusion.4
  252.1 7.3 convolution_convert_fusion
  259.3 1.6 collective-permute-start.3
  260.9 2.0 gather_fusion.5
  263.0 67.1 %collective-permute-done.3 = bf16[3072,1024]{1,0:T(8,128)(2,1)} collective-permute-done((bf16[3072,1024]{1,0:T(8,128)(2,1)}, bf16[3072,1024]{1,0:T(8,128)(2,1)}, u32[]{:S(2)}, u32[]{:S(2)}) %collective-permute-start.3) | collective-permute-done | bytes 6291488 | tf_op jit(solution)/shard_map/ppermute | solution.py:15
  330.0 8.2 add_convert_fusion.2
  338.3 0.2 collective-permute-start.4
  338.5 2.1 gather_fusion.6
  340.6 8.5 fusion.20
  349.1 60.1 %collective-permute-done.4 = bf16[3072,1024]{1,0:T(8,128)(2,1)} collective-permute-done((bf16[3072,1024]{1,0:T(8,128)(2,1)}, bf16[3072,1024]{1,0:T(8,128)(2,1)}, u32[]{:S(2)}, u32[]{:S(2)}) %collective-permute-start.4) | collective-permute-done | bytes 6291488 | tf_op jit(solution)/shard_map/ppermute | solution.py:15
  409.2 11.5 %add_convert_fusion.1 = bf16[3072,1024]{1,0:T(8,128)(2,1)} fusion(f32[3072,1024]{1,0:T(8,128)} %fusion.20, bf16[3072,1024]{1,0:T(8,128)(2,1)} %collective-permute-done.4), kind=kLoop, calls=%fused_computation.25 | loop fusion | flops 9437184 | bytes 25165824 | tf_op jit(solution)/shard_map/convert_element_type | solution.py:61
  420.7 12.0 %copy.32 = bf16[1,3072,1024]{2,0,1:T(2,128)(2,1)} copy(bf16[1,3072,1024]{2,1,0:T(8,128)(2,1)} %param.10) | data formatting | bytes 12582912 | tf_op args[4]
  432.7 0.5 broadcast.504
  433.2 37.8 %reduce.7 = bf16[3072,1024]{1,0:T(8,128)(2,1)} reduce(bf16[3072,1,1024]{2,1,0:T(2,128)(2,1)} %bitcast.124, bf16[]{:T(256)} %broadcast.504), dimensions={1}, to_apply=%bitcast.114.reduce_sub_computation | reduce | bytes 12582914
  471.0 9.4 reshape.658
  480.4 6.7 all-to-all-start
  487.1 2.1 gather_fusion.7
  489.2 8.5 fusion.21
  497.7 11.5 %add_convert_fusion = bf16[3072,1024]{1,0:T(8,128)(2,1)} fusion(f32[3072,1024]{1,0:T(8,128)} %fusion.21, bf16[3072,1024]{1,0:T(8,128)(2,1)} %collective-permute-done.5), kind=kLoop, calls=%fused_computation.24 | loop fusion | flops 9437184 | bytes 25165824 | tf_op jit(solution)/shard_map/convert_element_type | solution.py:61
  509.2 1.0 collective-permute-start.6
  510.2 69.6 %collective-permute-done.6 = bf16[3072,1024]{1,0:T(8,128)(2,1)S(1)} collective-permute-done((bf16[3072,1024]{1,0:T(8,128)(2,1)}, bf16[3072,1024]{1,0:T(8,128)(2,1)S(1)}, u32[]{:S(2)}, u32[]{:S(2)}) %collective-permute-start.6) | collective-permute-done | bytes 6291488 | tf_op jit(solution)/shard_map/ppermute | solution.py:15
  579.8 42.4 %copy.31 = bf16[1,3072,1024]{2,0,1:T(2,128)(2,1)} copy(bf16[1,3072,1024]{2,1,0:T(8,128)(2,1)S(1)} %bitcast.127) | data formatting | bytes 12582912 | tf_op jit(solution)/shard_map/broadcast_in_dim | solution.py:74
  622.3 37.9 %reduce.6 = bf16[3072,1024]{1,0:T(8,128)(2,1)} reduce(bf16[3072,1,1024]{2,1,0:T(2,128)(2,1)} %bitcast.125, bf16[]{:T(256)} %broadcast.504), dimensions={1}, to_apply=%bitcast.113.reduce_sub_computation | reduce | bytes 12582914
  660.1 9.4 %reshape.660 = bf16[8,2,196608]{2,1,0:T(2,128)(2,1)} reshape(bf16[3072,1024]{1,0:T(8,128)(2,1)} %reduce.6) | data formatting | bytes 12582912
  669.6 6.2 all-to-all-start.1
  675.8 11.0 %reshape.659 = bf16[3072,1,1024]{2,1,0:T(2,128)(2,1)} reshape(bf16[8,2,196608]{2,1,0:T(2,128)(2,1)} %all-to-all-done) | data formatting | bytes 12582912
  686.8 19.7 %convert_multiply_fusion.4 = f32[1,3072,1024]{2,0,1:T(1,128)} fusion(bf16[3072,1,1024]{2,1,0:T(2,128)(2,1)} %reshape.659), kind=kLoop, calls=%fused_computation.27 | loop fusion | flops 6291456 | bytes 18874368 | tf_op jit(solution)/shard_map/mul | solution.py:80
  706.4 16.6 %copy.23 = f32[1,384,8,1024]{3,2,1,0:T(8,128)} copy(f32[1,384,8,1024]{3,0,1,2:T(1,128)} %bitcast.121) | data formatting | bytes 25165824 | tf_op jit(solution)/shard_map/mul | solution.py:80
  723.1 13.8 %mul.114 = f32[1,384,8192]{2,1,0:T(8,128)} reshape(f32[1,384,8,1024]{3,2,1,0:T(8,128)} %copy.23) | data formatting | bytes 25165824 | tf_op jit(solution)/shard_map/mul | solution.py:80
  736.9 4.3 reshape.544
  741.1 2.2 reshape.543
  743.3 67.5 %all-to-all-done.1 = bf16[8,2,196608]{2,1,0:T(2,128)(2,1)} async-done(((bf16[8,2,196608]{2,1,0:T(2,128)(2,1)}), bf16[8,2,196608]{2,1,0:T(2,128)(2,1)}, u32[]{:S(2)}, u32[]{:S(2)}) %all-to-all-start.1) | async-done | bytes 6291488 | tf_op jit(solution)/shard_map/all_to_all | solution.py:74
  810.8 11.0 %reshape.661 = bf16[3072,1,1024]{2,1,0:T(2,128)(2,1)} reshape(bf16[8,2,196608]{2,1,0:T(2,128)(2,1)} %all-to-all-done.1) | data formatting | bytes 12582912
  821.8 28.7 %convert_multiply_fusion.2 = (f32[1,3072,1024]{2,0,1:T(1,128)}, f32[1,3072,1024]{2,0,1:T(1,128)}) fusion(bf16[3072,1,1024]{2,1,0:T(2,128)(2,1)} %reshape.661), kind=kLoop, calls=%fused_computation.22 | loop fusion | flops 9437184 | bytes 31457280 | tf_op jit(solution)/shard_map/mul | solution.py:83
  850.4 16.6 %copy.26 = f32[1,384,8,1024]{3,2,1,0:T(8,128)} copy(f32[1,384,8,1024]{3,0,1,2:T(1,128)} %bitcast.123) | data formatting | bytes 25165824 | tf_op jit(solution)/shard_map/mul | solution.py:83
  867.1 14.0 %mul.130 = f32[1,384,8192]{2,1,0:T(8,128)} reshape(f32[1,384,8,1024]{3,2,1,0:T(8,128)} %copy.26) | data formatting | bytes 25165824 | tf_op jit(solution)/shard_map/mul | solution.py:83
  881.1 16.6 %copy.25 = f32[1,384,8,1024]{3,2,1,0:T(8,128)} copy(f32[1,384,8,1024]{3,0,1,2:T(1,128)} %bitcast.122) | data formatting | bytes 25165824 | tf_op jit(solution)/shard_map/mul | solution.py:79
  897.8 13.8 %mul.123 = f32[1,384,8192]{2,1,0:T(8,128)} reshape(f32[1,384,8,1024]{3,2,1,0:T(8,128)} %copy.25) | data formatting | bytes 25165824 | tf_op jit(solution)/shard_map/mul | solution.py:79
  911.6 22.3 %fusion.6 = (bf16[1,384,8192]{2,1,0:T(8,128)(2,1)}, f32[1,384,8192]{2,1,0:T(8,128)}) fusion(f32[1,384,8192]{2,1,0:T(8,128)} %mul.130, bf16[1,384,8192]{2,1,0:T(8,128)(2,1)} %param.11, f32[1,384,8192]{2,1,0:T(8,128)} %mul.114, f32[1,384,8192]{2,1,0:T(8,128)} %mul.123), kind=kLoop, calls=%fused_computation.21 | loop fusion | flops 28311552 | bytes 62914560 | tf_op jit(solution)/shard_map/convert_element_type | solution.py:83
  (40 shorter events, 1.1 us)
Async XLA Ops:
  7.2 155.1 %copy-start.4 = (bf16[512,2,1024]{2,1,0:T(2,128)(2,1)S(1)}, bf16[512,2,1024]{2,1,0:T(2,128)(2,1)}, u32[]{:S(2)}) copy-start(bf16[512,2,1024]{2,1,0:T(2,128)(2,1)} %param.8) | copy-start | bytes 6291460
  7.2 157.8 %all-gather.2.cloned.1.call-start = ((), (), s32[]{:S(2)}) async-start(), calls=%async_computation.2 | async-start | bytes 3538944 | tf_op jit(solution)/shard_map/all_gather | solution.py:31
  7.2 70.8 %collective-permute-start = (bf16[3072,1024]{1,0:T(8,128)(2,1)}, bf16[3072,1024]{1,0:T(8,128)(2,1)}, u32[]{:S(2)}, u32[]{:S(2)}) collective-permute-start(bf16[3072,1024]{1,0:T(8,128)(2,1)} %bitcast.126), channel_id=1, source_target_pairs={{0,8},{8,16},{16,24},{24,0},{1,9},{9,17},{17,25},{25,1},{2,10},{10... | collective-permute-start | bytes 18874376 | tf_op jit(solution)/shard_map/ppermute | solution.py:15
  78.0 70.7 %collective-permute-start.1 = (bf16[3072,1024]{1,0:T(8,128)(2,1)}, bf16[3072,1024]{1,0:T(8,128)(2,1)}, u32[]{:S(2)}, u32[]{:S(2)}) collective-permute-start(bf16[3072,1024]{1,0:T(8,128)(2,1)} %collective-permute-done), channel_id=1, source_target_pairs={{0,8},{8,16},{16,24},{24,0},{1,9},{9,17},{17,25},{25,1},{2,10},{10... | collective-permute-start | bytes 18874376 | tf_op jit(solution)/shard_map/ppermute | solution.py:15
  148.7 78.8 %collective-permute-start.2 = (bf16[3072,1024]{1,0:T(8,128)(2,1)}, bf16[3072,1024]{1,0:T(8,128)(2,1)}, u32[]{:S(2)}, u32[]{:S(2)}) collective-permute-start(bf16[3072,1024]{1,0:T(8,128)(2,1)} %collective-permute-done.1), channel_id=1, source_target_pairs={{0,8},{8,16},{16,24},{24,0},{1,9},{9,17},{17,25},{25,1},{2,10},{10... | collective-permute-start | bytes 18874376 | tf_op jit(solution)/shard_map/ppermute | solution.py:15
  191.0 6.2 copy-start.3
  204.7 7.6 copy-start.2
  219.8 7.8 copy-start.1
  259.3 70.7 %collective-permute-start.3 = (bf16[3072,1024]{1,0:T(8,128)(2,1)}, bf16[3072,1024]{1,0:T(8,128)(2,1)}, u32[]{:S(2)}, u32[]{:S(2)}) collective-permute-start(bf16[3072,1024]{1,0:T(8,128)(2,1)} %convolution_convert_fusion), channel_id=1, source_target_pairs={{0,8},{8,16},{16,24},{24,0},{1,9},{9,17},{17,25},{25,1},{2,10},{10... | collective-permute-start | bytes 18874376 | tf_op jit(solution)/shard_map/ppermute | solution.py:15
  338.3 70.9 %collective-permute-start.4 = (bf16[3072,1024]{1,0:T(8,128)(2,1)}, bf16[3072,1024]{1,0:T(8,128)(2,1)}, u32[]{:S(2)}, u32[]{:S(2)}) collective-permute-start(bf16[3072,1024]{1,0:T(8,128)(2,1)} %add_convert_fusion.2), channel_id=1, source_target_pairs={{0,8},{8,16},{16,24},{24,0},{1,9},{9,17},{17,25},{25,1},{2,10},{10... | collective-permute-start | bytes 18874376 | tf_op jit(solution)/shard_map/ppermute | solution.py:15
  420.7 77.1 %collective-permute-start.5 = (bf16[3072,1024]{1,0:T(8,128)(2,1)}, bf16[3072,1024]{1,0:T(8,128)(2,1)}, u32[]{:S(2)}, u32[]{:S(2)}) collective-permute-start(bf16[3072,1024]{1,0:T(8,128)(2,1)} %add_convert_fusion.1), channel_id=1, source_target_pairs={{0,8},{8,16},{16,24},{24,0},{1,9},{9,17},{17,25},{25,1},{2,10},{10... | collective-permute-start | bytes 18874376 | tf_op jit(solution)/shard_map/ppermute | solution.py:15
  480.4 189.2 %all-to-all-start = ((bf16[8,2,196608]{2,1,0:T(2,128)(2,1)}), bf16[8,2,196608]{2,1,0:T(2,128)(2,1)}, u32[]{:S(2)}, u32[]{:S(2)}) async-start(bf16[8,2,196608]{2,1,0:T(2,128)(2,1)} %reshape.658), calls=%async_computation | async-start | bytes 12582912 | tf_op jit(solution)/shard_map/all_to_all | solution.py:75
  509.2 70.6 %collective-permute-start.6 = (bf16[3072,1024]{1,0:T(8,128)(2,1)}, bf16[3072,1024]{1,0:T(8,128)(2,1)S(1)}, u32[]{:S(2)}, u32[]{:S(2)}) collective-permute-start(bf16[3072,1024]{1,0:T(8,128)(2,1)} %add_convert_fusion), channel_id=1, source_target_pairs={{0,8},{8,16},{16,24},{24,0},{1,9},{9,17},{17,25},{25,1},{2,10},{10... | collective-permute-start | bytes 18874376 | tf_op jit(solution)/shard_map/ppermute | solution.py:15
  669.6 141.2 %all-to-all-start.1 = ((bf16[8,2,196608]{2,1,0:T(2,128)(2,1)}), bf16[8,2,196608]{2,1,0:T(2,128)(2,1)}, u32[]{:S(2)}, u32[]{:S(2)}) async-start(bf16[8,2,196608]{2,1,0:T(2,128)(2,1)} %reshape.660), calls=%async_computation.1 | async-start | bytes 12582912 | tf_op jit(solution)/shard_map/all_to_all | solution.py:74
  736.8 4.3 copy-start
Sparse Core Ops, SparseCore 0:
  78.1 61.8 all-gather.1
where the time goes:
time: 950 us; the launch traced here: 941 us
  waiting for transfers between devices  406 us (43%)
  local copies, waits for them, and re-layouts  262 us (28%)
  other arithmetic  180 us (19%)
  matrix products  63.5 us (7%)
  starting transfers between devices  15.9 us (2%)
  between operations  14.6 us (2%)
    ppermute x7, waiting for transfers between devices, shifted(): lax.ppermute(array, axis, [(i, (i + by) % size) for i in range(size)])  338 us
    unnamed x6, other arithmetic  77.2 us
    all_to_all x1, waiting for transfers between devices, body(): lax.all_to_all(carried[None], 'dp', split_axis=1, concat_axis=2, tiled=True)  67.5 us
    unnamed x18, local copies, waits for them, and re-layouts  58.7 us
    broadcast_in_dim x1, local copies, waits for them, and re-layouts, body(): carried[None]  42.4 us
    dot_general x4, matrix products, body(): lax.dot_general(upstream, picked, (((0,), (0,)), ((), ())), preferred_ele...  32.5 us
    dot_general x4, matrix products, body(): jnp.dot(upstream, weight_now, preferred_element_type=jnp.float32)  31 us
    mul x2, local copies, waits for them, and re-layouts, body(): (1.0 - beta_second) * grad  30.7 us
  transfers between devices with their start and end apart: 10, of which 6 were waited for; matrix products, arithmetic and copies ran while one was open for 35% of the time, Pallas kernels for 0%

commit v1 on v0

v1 whole, which is shorter than its diff:
```python
import functools

import jax
import jax.numpy as jnp
from jax import lax
from jax.experimental import pallas as pl
from jax.experimental.pallas import tpu as pltpu
from jax.sharding import PartitionSpec as P

beta_first = 0.9
beta_second = 0.99
step_rate = 0.01
decay_rate = 1.0
sign_width = 10.0


def swapped(array, axis, mask):
    size = lax.axis_size(axis)
    return lax.ppermute(array, axis, [(i, i ^ mask) for i in range(size)])


def update_kernel(grad_ref, weight_ref, momentum_ref, new_weight_ref, new_momentum_ref):
    grad = grad_ref[0].astype(jnp.float32)
    moment = momentum_ref[0].astype(jnp.float32)
    weight = weight_ref[0].astype(jnp.float32)
    mix = beta_first * moment + (1.0 - beta_first) * grad
    new_weight_ref[0] = weight * (1.0 - step_rate * decay_rate) - step_rate * jnp.tanh(
        mix / sign_width
    )
    new_momentum_ref[0] = (beta_second * moment + (1.0 - beta_second) * grad).astype(
        jnp.bfloat16
    )


def update(grad, weight, momentum):
    sources, rows, cols = grad.shape
    block = pl.BlockSpec((1, rows, cols), lambda s: (s, 0, 0))
    wide = pl.BlockSpec((1, rows, cols), lambda s: (0, 0, s))
    return pl.pallas_call(
        update_kernel,
        grid=(sources,),
        in_specs=[block, block, wide],
        out_specs=[wide, wide],
        out_shape=[
            jax.ShapeDtypeStruct(momentum.shape, jnp.float32),
            jax.ShapeDtypeStruct(momentum.shape, jnp.bfloat16),
        ],
        compiler_params=pltpu.CompilerParams(vmem_limit_bytes=32 * 1024 * 1024),
        cost_estimate=pl.CostEstimate(
            flops=10 * momentum.size, bytes_accessed=12 * momentum.size, transcendentals=momentum.size
        ),
        name="lion_step",
    )(grad, weight, momentum)


def body(out_grad, gate_saved, up_saved, routing, down_weight, momentum):
    experts = lax.axis_size("expert")
    shards = lax.axis_size("dp")
    group_tok, topk, cols = gate_saved.shape
    width = out_grad.shape[1]
    rows = momentum.shape[1]
    mine = lax.axis_index("expert")

    weight_shards = lax.all_to_all(
        down_weight.reshape(shards, rows, cols), "dp", split_axis=0, concat_axis=0, tiled=True
    )

    tokens = {0: lax.all_gather(out_grad, "dp", axis=0, tiled=True)}
    for m in sorted(range(1, experts), key=lambda m: (bin(m).count("1"), -m)):
        low = m & -m
        tokens[m] = swapped(tokens[m ^ low], "expert", low)

    gate = gate_saved.astype(jnp.float32)
    up = up_saved.astype(jnp.float32)
    sigma = jax.nn.sigmoid(gate)
    hidden = (gate * sigma * up).astype(jnp.bfloat16)

    rows_of = {}
    for m in range(experts):
        chosen = (routing == (mine ^ m))[:, :, None]
        picked = jnp.sum(jnp.where(chosen, hidden, jnp.zeros_like(hidden)), axis=1)
        rows_of[m] = swapped(picked, "expert", m) if m else picked

    weight = down_weight[0]
    deriv = jnp.zeros(gate.shape, jnp.float32)
    term = jnp.zeros((width, cols), jnp.float32)
    for m in range(experts):
        part = jnp.dot(tokens[m], weight, preferred_element_type=jnp.float32)
        back = swapped(part, "expert", m) if m else part
        chosen = (routing == (mine ^ m))[:, :, None]
        deriv = jnp.where(chosen, back[:, None, :], deriv)
        term = term + lax.dot_general(
            tokens[m], rows_of[m], (((0,), (0,)), ((), ())), preferred_element_type=jnp.float32
        )

    grad_shards = lax.all_to_all(
        term.astype(jnp.bfloat16).reshape(shards, rows, cols),
        "dp",
        split_axis=0,
        concat_axis=0,
        tiled=True,
    )
    d_up = (deriv * gate * sigma).astype(jnp.bfloat16)
    d_gate = (deriv * up * sigma * (1.0 + gate * (1.0 - sigma))).astype(jnp.bfloat16)
    new_weight, new_momentum = update(grad_shards, weight_shards, momentum)
    return (d_gate, d_up, new_weight, new_momentum)


def solution(mesh):
    placed = (
        P(("expert", "dp"), None),
        P("expert", None, "dp"),
        P("expert", None, "dp"),
        P("expert", None),
        P("expert", None, "dp"),
        P("expert", "dp", None),
    )
    return jax.shard_map(
        body,
        mesh=mesh,
        in_specs=placed,
        out_specs=(
            P("expert", None, "dp"),
            P("expert", None, "dp"),
            P("expert", "dp", None),
            P("expert", "dp", None),
        ),
        check_vma=False,
    )
```

time: 950 us -> 528 us (0.56)
  local copies, waits for them, and re-layouts: 262 us -> 12.2 us
  waiting for transfers between devices: 406 us -> 229 us
  other arithmetic: 180 us -> 36.6 us
  blocking collectives: 0 us -> 143 us
  Pallas kernels: 0 us -> 12 us
    ppermute x7 -> x9, waiting for transfers between devices: 338 us -> 165 us  [swapped(): return lax.ppermute(array, axis, [(i, i ^ mask) for i in range(size)])]
    all_to_all x0 -> x1, blocking collectives: none -> 143 us  [body(): lax.all_to_all(term.astype(jnp.bfloat16).reshape(shards, rows, cols), 'dp...]
    mul x6 -> x0, local copies, waits for them, and re-layouts: 91.5 us -> none  [the longest x2 30.7 us: body(): (1.0 - beta_second) * grad]
    unnamed x6 -> x1, other arithmetic: 77.2 us -> 0.01 us
    all_to_all x2 -> x1, waiting for transfers between devices: 67.5 us -> 0.01 us  [body(): lax.all_to_all(down_weight.reshape(shards, rows, cols), 'dp', split_axis=...]
    all_gather x1, waiting for transfers between devices: 0.02 us -> 63.9 us  [body(): tokens = {0: lax.all_gather(out_grad, 'dp', axis=0, tiled=True)}]
    unnamed x18 -> x26, local copies, waits for them, and re-layouts: 58.7 us -> 2.84 us
    mul x2 -> x0, other arithmetic: 48.4 us -> none  [the longest x1 28.7 us: body(): (1.0 - beta_second) * grad]
  transfers between devices with their start and end apart: 10 -> 11, of which waited for: 6 -> 6; matrix products, arithmetic and copies ran while one was open for 35% -> 22% of each run, Pallas kernels for 0% -> 0%
where the time goes in v1:
time: 528 us; the launch traced here: 525 us
  waiting for transfers between devices  229 us (43%)
  blocking collectives  143 us (27%)
  matrix products  67.4 us (13%)
  other arithmetic  36.6 us (7%)
  between operations  14.2 us (3%)
  local copies, waits for them, and re-layouts  12.2 us (2%)
  Pallas kernels  12 us (2%)
  starting transfers between devices  11.2 us (2%)
    ppermute x9, waiting for transfers between devices, swapped(): return lax.ppermute(array, axis, [(i, i ^ mask) for i in range(size)])  165 us
    all_to_all x1, blocking collectives, body(): lax.all_to_all(term.astype(jnp.bfloat16).reshape(shards, rows, cols), 'dp...  143 us
    all_gather x1, waiting for transfers between devices, body(): tokens = {0: lax.all_gather(out_grad, 'dp', axis=0, tiled=True)}  63.9 us
    dot_general x4, matrix products, body(): lax.dot_general(tokens[m], rows_of[m], (((0,), (0,)), ((), ())), preferre...  38.4 us
    dot_general x4, matrix products, body(): part = jnp.dot(tokens[m], weight, preferred_element_type=jnp.float32)  29 us
    reduce_sum x1, other arithmetic, body(): picked = jnp.sum(jnp.where(chosen, hidden, jnp.zeros_like(hidden)), axis=1)  18.4 us
    convert_element_type x1, other arithmetic, body(): d_up = (deriv * gate * sigma).astype(jnp.bfloat16)  18.3 us
    pallas_call x1, Pallas kernels, update(): pl.pallas_call(update_kernel, grid=(sources,), in_specs=[block, block, wi...  12 us
  transfers between devices with their start and end apart: 11, of which 6 were waited for; matrix products, arithmetic and copies ran while one was open for 22% of the time, Pallas kernels for 0%

profile of v1, /device:TPU:8, one launch (start us, length us, event | category | flops | bytes accessed | tf_op | source)
XLA Modules:
  0.0 525.4 jit_solution(7143549998737674478)
XLA Ops:
  7.2 0.0 all-gather.2.cloned.1.call-start
  7.2 0.7 all-gather.2.cloned.1.call-update
  7.9 63.9 %all-gather.2.cloned.1.call-done = bf16[512,3072]{1,0:T(8,128)(2,1)} async-done(((bf16[64,3072]{1,0:T(8,128)(2,1)}), bf16[512,3072]{1,0:T(8,128)(2,1)}) %all-gather.2.cloned.1.call-update) | async-done | bytes 3145744 | tf_op jit(solution)/shard_map/all_gather | solution.py:68
  71.8 1.5 collective-permute-start
  73.3 0.0 collective-permute-start.4
  73.3 67.4 %collective-permute-done = bf16[512,3072]{1,0:T(8,128)(2,1)S(1)} collective-permute-done((bf16[512,3072]{1,0:T(8,128)(2,1)}, bf16[512,3072]{1,0:T(8,128)(2,1)S(1)}, u32[]{:S(2)}, u32[]{:S(2)}) %collective-permute-start) | collective-permute-done | bytes 3145760 | tf_op jit(solution)/shard_map/ppermute | solution.py:19
  140.6 0.0 copy-start.9
  140.6 0.0 collective-permute-start.1
  140.6 0.0 collective-permute-done.4
  140.6 0.0 copy-start.7
  140.6 0.0 slice-start
  140.6 9.9 %fusion.3 = f32[512,1024]{1,0:T(8,128)} fusion(bf16[512,3072]{1,0:T(8,128)(2,1)S(1)} %collective-permute-done.4, bf16[1,3072,1024]{2,1,0:T(8,128)(2,1)} %param.10), kind=kOutput, calls=%fused_computation.8 | convolution fusion | flops 3221225472 | bytes 11534336 | tf_op jit(solution)/shard_map/dot_general | solution.py:88
  150.5 0.0 copy-done.7
  150.5 0.0 slice-start.1
  150.5 0.0 collective-permute-start.5
  150.5 0.0 copy-done.9
  150.5 7.7 %fusion.5 = f32[512,1024]{1,0:T(8,128)} fusion(bf16[512,3072]{1,0:T(8,128)(2,1)S(1)} %collective-permute-done, bf16[1,3072,1024]{2,1,0:T(8,128)(2,1)} %param.10), kind=kOutput, calls=%fused_computation.10 | convolution fusion | flops 3221225472 | bytes 11534336 | tf_op jit(solution)/shard_map/dot_general | solution.py:88
  158.2 1.5 collective-permute-start.3
  159.7 0.0 collective-permute-done.1
  159.7 0.0 slice-done
  159.7 0.0 slice-done.1
  159.7 0.0 copy-start.1
  159.7 4.8 fusion.7
  164.6 0.0 copy-done.1
  164.6 0.2 collective-permute-start.2
  164.8 0.0 copy-start.6
  164.8 5.8 %all-to-all-start.1 = ((bf16[8,384,1024]{2,1,0:T(8,128)(2,1)}), bf16[8,384,1024]{2,1,0:T(8,128)(2,1)}, u32[]{:S(2)}, u32[]{:S(2)}) async-start(bf16[8,384,1024]{2,1,0:T(8,128)(2,1)} %bitcast.26), calls=%async_computation.1 | async-start | bytes 12582912 | tf_op jit(solution)/shard_map/all_to_all | solution.py:64
  170.6 0.0 copy-done.6
  170.6 0.2 copy.13
  170.8 0.2 copy.12
  171.0 0.2 copy.11
  171.2 0.2 copy.10
  171.4 0.0 copy-start.3
  171.4 0.0 copy-start.4
  171.4 6.6 %fusion.1 = f32[512,1024]{1,0:T(8,128)S(1)} fusion(bf16[512,3072]{1,0:T(8,128)(2,1)} %all-gather.2.cloned.1.call-done, bf16[1,3072,1024]{2,1,0:T(8,128)(2,1)} %param.10), kind=kOutput, calls=%fused_computation.6 | convolution fusion | flops 3221225472 | bytes 11534336 | tf_op jit(solution)/shard_map/dot_general | solution.py:88
  178.0 0.0 collective-permute-done.5
  178.1 0.0 copy-start.5
  178.1 28.9 %collective-permute-done.3 = f32[512,1024]{1,0:T(8,128)} collective-permute-done((f32[512,1024]{1,0:T(8,128)}, f32[512,1024]{1,0:T(8,128)}, u32[]{:S(2)}, u32[]{:S(2)}) %collective-permute-start.3) | collective-permute-done | bytes 2097184 | tf_op jit(solution)/shard_map/ppermute | solution.py:19
  207.0 0.0 copy-done.5
  207.0 43.8 %collective-permute-done.2 = f32[512,1024]{1,0:T(8,128)} collective-permute-done((f32[512,1024]{1,0:T(8,128)}, f32[512,1024]{1,0:T(8,128)}, u32[]{:S(2)}, u32[]{:S(2)}) %collective-permute-start.2) | collective-permute-done | bytes 2097184 | tf_op jit(solution)/shard_map/ppermute | solution.py:19
  250.8 0.0 copy-done.3
  250.8 0.0 copy-done.4
  250.8 18.3 %fusion.18 = (bf16[512,2,1024]{2,1,0:T(2,128)(2,1)}, bf16[512,2,1024]{2,1,0:T(2,128)(2,1)}, bf16[512,2,1024]{2,1,0:T(2,128)(2,1)S(1)}) fusion(bf16[512,2,1024]{2,1,0:T(2,128)(2,1)S(1)} %copy-done.3, pred[512,2]{1,0:T(8,128)(4,1)S(1)} %copy.13, pred[512,2]{1,0:T(8,128)(4,1)S(1)} %copy.12, pred[512,2]{1,0:T(8,128)(4,1)S(1)} %copy.11, ...), kind=kLoop, calls=%fused_computation.25 | loop fusion | flops 23068672 | bytes 18878464 | tf_op jit(solution)/shard_map/convert_element_type | solution.py:103
  269.1 18.4 %fusion.19 = (bf16[512,1024]{1,0:T(8,128)(2,1)}, bf16[512,1024]{1,0:T(8,128)(2,1)}, bf16[512,1024]{1,0:T(8,128)(2,1)}, bf16[512,1024]{1,0:T(8,128)(2,1)S(1)}) fusion(bf16[512,2,1024]{2,1,0:T(2,128)(2,1)S(1)} %get-tuple-element.14, pred[512,2]{1,0:T(8,128)(4,1)S(1)} %copy.10, pred[512,2]{1,0:T(8,128)(4,1)S(1)} %copy.11, pred[512,2]{1,0:T(8,128)(4,1)S(1)} %copy.12, ...), kind=kLoop, calls=%fused_computation.31 | loop fusion | flops 6291456 | bytes 6295552 | tf_op jit(solution)/shard_map/reduce_sum | solution.py:81
  287.4 1.5 collective-permute-start.7
  288.9 0.4 collective-permute-start.6
  289.3 0.3 collective-permute-start.8
  289.6 0.0 copy-start.10
  289.6 8.4 %fusion.23 = f32[1024,3072]{1,0:T(8,128)} fusion(bf16[512,1024]{1,0:T(8,128)(2,1)S(1)} %get-tuple-element.11, bf16[512,3072]{1,0:T(8,128)(2,1)} %all-gather.2.cloned.1.call-done), kind=kOutput, calls=%fused_computation.39 | convolution fusion | flops 3221225472 | bytes 16777216 | tf_op jit(solution)/shard_map/dot_general | solution.py:92
  298.0 0.0 copy-start.8
  298.0 15.7 %collective-permute-done.7 = bf16[512,1024]{1,0:T(8,128)(2,1)S(1)} collective-permute-done((bf16[512,1024]{1,0:T(8,128)(2,1)}, bf16[512,1024]{1,0:T(8,128)(2,1)S(1)}, u32[]{:S(2)}, u32[]{:S(2)}) %collective-permute-start.7) | collective-permute-done | bytes 1048608 | tf_op jit(solution)/shard_map/ppermute | solution.py:19
  313.7 0.0 copy-done.10
  313.7 6.6 %fusion.25 = f32[1024,3072]{1,0:T(8,128)} fusion(bf16[512,1024]{1,0:T(8,128)(2,1)S(1)} %collective-permute-done.7, bf16[512,3072]{1,0:T(8,128)(2,1)S(1)} %copy-done.10), kind=kOutput, calls=%fused_computation.41 | convolution fusion | flops 3221225472 | bytes 16777216 | tf_op jit(solution)/shard_map/dot_general | solution.py:92
  320.3 0.0 collective-permute-done.6
  320.3 0.0 copy-done.8
  320.3 6.4 %fusion.24 = f32[1024,3072]{1,0:T(8,128)} fusion(bf16[512,1024]{1,0:T(8,128)(2,1)S(1)} %collective-permute-done.6, bf16[512,3072]{1,0:T(8,128)(2,1)S(1)} %copy-done.8), kind=kOutput, calls=%fused_computation.40 | convolution fusion | flops 3221225472 | bytes 16777216 | tf_op jit(solution)/shard_map/dot_general | solution.py:92
  326.7 9.0 %collective-permute-done.8 = bf16[512,1024]{1,0:T(8,128)(2,1)} collective-permute-done((bf16[512,1024]{1,0:T(8,128)(2,1)}, bf16[512,1024]{1,0:T(8,128)(2,1)}, u32[]{:S(2)}, u32[]{:S(2)}) %collective-permute-start.8) | collective-permute-done | bytes 1048608 | tf_op jit(solution)/shard_map/ppermute | solution.py:19
  335.7 0.0 copy-done.2
  335.7 16.9 %fusion = bf16[3072,1024]{0,1:T(8,128)(2,1)} fusion(f32[1024,3072]{1,0:T(8,128)} %fusion.25, f32[1024,3072]{1,0:T(8,128)} %fusion.23, f32[1024,3072]{1,0:T(8,128)} %fusion.24, bf16[512,1024]{1,0:T(8,128)(2,1)} %collective-permute-done.8, bf16[512,3072]{1,0:T(8,128)(2,1)S(1)} %copy-done.2), kind=kOutput, calls=%fused_computation.5 | convolution fusion | flops 3233808384 | bytes 48234496 | tf_op jit(solution)/shard_map/dot_general | solution.py:92
  352.6 8.6 %copy.14 = bf16[3072,1024]{1,0:T(8,128)(2,1)} copy(bf16[3072,1024]{0,1:T(8,128)(2,1)} %fusion) | data formatting | bytes 12582912 | tf_op jit(solution)/shard_map/convert_element_type | solution.py:97
  361.3 0.0 all-to-all-done.1.weight_ref
  361.3 142.6 %all_to_all.10.grad_ref = bf16[8,384,1024]{2,1,0:T(8,128)(2,1)S(1)} all-to-all(bf16[8,384,1024]{2,1,0:T(8,128)(2,1)} %bitcast.25), channel_id=1, replica_groups=mesh['expert'=4,'dp'=8] {'dp'}, dimensions={0} | all-to-all | bytes 12582912 | tf_op jit(solution)/shard_map/all_to_all | solution.py:96
  503.8 2.8 copy-done
  506.6 12.0 %lion_step.1 = (f32[1,384,8192]{2,1,0:T(8,128)}, bf16[1,384,8192]{2,1,0:T(8,128)(2,1)}) custom-call(bf16[8,384,1024]{2,1,0:T(8,128)(2,1)S(1)} %all_to_all.10.grad_ref, bf16[8,384,1024]{2,1,0:T(8,128)(2,1)} %all-to-all-done.1.weight_ref, bf16[1,384,8192]{2,1,0:T(8,128)(2,1)S(1)} %copy-done), custom_call_target="tpu_custom_call" | custom-call | flops 31457280 | bytes 37748736 | tf_op jit(solution)/shard_map/lion_step/pallas_call | solution.py:39
  (4 shorter events, 0.0 us)
Async XLA Ops:
  7.2 64.6 %all-gather.2.cloned.1.call-start = ((), (), s32[]{:S(2)}) async-start(), calls=%async_computation.2 | async-start | bytes 3538944 | tf_op jit(solution)/shard_map/all_gather | solution.py:68
  71.8 68.8 %collective-permute-start = (bf16[512,3072]{1,0:T(8,128)(2,1)}, bf16[512,3072]{1,0:T(8,128)(2,1)S(1)}, u32[]{:S(2)}, u32[]{:S(2)}) collective-permute-start(bf16[512,3072]{1,0:T(8,128)(2,1)} %all-gather.2.cloned.1.call-done), channel_id=1, source_target_pairs={{0,16},{8,24},{16,0},{24,8},{1,17},{9,25},{17,1},{25,9},{2,18},{10... | collective-permute-start | bytes 9437192 | tf_op jit(solution)/shard_map/ppermute | solution.py:19
  73.3 67.4 %collective-permute-start.4 = (bf16[512,3072]{1,0:T(8,128)(2,1)}, bf16[512,3072]{1,0:T(8,128)(2,1)S(1)}, u32[]{:S(2)}, u32[]{:S(2)}) collective-permute-start(bf16[512,3072]{1,0:T(8,128)(2,1)} %all-gather.2.cloned.1.call-done), channel_id=1, source_target_pairs={{0,8},{8,0},{16,24},{24,16},{1,9},{9,1},{17,25},{25,17},{2,10},{10... | collective-permute-start | bytes 9437192 | tf_op jit(solution)/shard_map/ppermute | solution.py:19
  140.6 9.9 %copy-start.9 = (bf16[512,3072]{1,0:T(8,128)(2,1)}, bf16[512,3072]{1,0:T(8,128)(2,1)S(1)}, u32[]{:S(2)}) copy-start(bf16[512,3072]{1,0:T(8,128)(2,1)S(1)} %collective-permute-done) | copy-start | bytes 9437188
  140.6 19.1 %collective-permute-start.1 = (bf16[512,3072]{1,0:T(8,128)(2,1)S(1)}, bf16[512,3072]{1,0:T(8,128)(2,1)S(1)}, u32[]{:S(2)}, u32[]{:S(2)}) collective-permute-start(bf16[512,3072]{1,0:T(8,128)(2,1)S(1)} %collective-permute-done), channel_id=1, source_target_pairs={{0,8},{8,0},{16,24},{24,16},{1,9},{9,1},{17,25},{25,17},{2,10},{10... | collective-permute-start | bytes 9437192 | tf_op jit(solution)/shard_map/ppermute | solution.py:19
  140.6 9.9 %copy-start.7 = (bf16[512,3072]{1,0:T(8,128)(2,1)}, bf16[512,3072]{1,0:T(8,128)(2,1)S(1)}, u32[]{:S(2)}) copy-start(bf16[512,3072]{1,0:T(8,128)(2,1)S(1)} %collective-permute-done.4) | copy-start | bytes 9437188
  140.6 19.1 %slice-start = ((s8[6291456]{0:T(1024)(128)(4,1)}), s8[4194304]{0:T(1024)(128)(4,1)S(1)}, s32[]{:S(2)}) async-start(s8[6291456]{0:T(1024)(128)(4,1)} %bitcast.27), calls=%async_computation.3 | async-start | bytes 8388608
  150.5 9.2 %slice-start.1 = ((s8[6291456]{0:T(1024)(128)(4,1)}), s8[2097152]{0:T(1024)(128)(4,1)S(1)}, s32[]{:S(2)}) async-start(s8[6291456]{0:T(1024)(128)(4,1)} %bitcast.27), calls=%async_computation.4 | async-start | bytes 4194304
  150.5 27.5 %collective-permute-start.5 = (f32[512,1024]{1,0:T(8,128)}, f32[512,1024]{1,0:T(8,128)S(1)}, u32[]{:S(2)}, u32[]{:S(2)}) collective-permute-start(f32[512,1024]{1,0:T(8,128)} %fusion.3), channel_id=1, source_target_pairs={{0,8},{8,0},{16,24},{24,16},{1,9},{9,1},{17,25},{25,17},{2,10},{10... | collective-permute-start | bytes 6291464 | tf_op jit(solution)/shard_map/ppermute | solution.py:19
  158.2 48.8 %collective-permute-start.3 = (f32[512,1024]{1,0:T(8,128)}, f32[512,1024]{1,0:T(8,128)}, u32[]{:S(2)}, u32[]{:S(2)}) collective-permute-start(f32[512,1024]{1,0:T(8,128)} %fusion.5), channel_id=1, source_target_pairs={{0,16},{8,24},{16,0},{24,8},{1,17},{9,25},{17,1},{25,9},{2,18},{10... | collective-permute-start | bytes 6291464 | tf_op jit(solution)/shard_map/ppermute | solution.py:19
  159.7 4.8 copy-start.1
  164.6 86.3 %collective-permute-start.2 = (f32[512,1024]{1,0:T(8,128)}, f32[512,1024]{1,0:T(8,128)}, u32[]{:S(2)}, u32[]{:S(2)}) collective-permute-start(f32[512,1024]{1,0:T(8,128)} %fusion.7), channel_id=1, source_target_pairs={{0,24},{8,16},{16,8},{24,0},{1,25},{9,17},{17,9},{25,1},{2,26},{10... | collective-permute-start | bytes 6291464 | tf_op jit(solution)/shard_map/ppermute | solution.py:19
  164.8 5.8 %copy-start.6 = (s32[512,2]{0,1:T(2,128)S(1)}, s32[512,2]{0,1:T(2,128)}, u32[]{:S(2)}) copy-start(s32[512,2]{0,1:T(2,128)} %param.9) | copy-start | bytes 12292
  164.8 196.5 %all-to-all-start.1 = ((bf16[8,384,1024]{2,1,0:T(8,128)(2,1)}), bf16[8,384,1024]{2,1,0:T(8,128)(2,1)}, u32[]{:S(2)}, u32[]{:S(2)}) async-start(bf16[8,384,1024]{2,1,0:T(8,128)(2,1)} %bitcast.26), calls=%async_computation.1 | async-start | bytes 12582912 | tf_op jit(solution)/shard_map/all_to_all | solution.py:64
  171.4 79.4 %copy-start.3 = (bf16[512,2,1024]{2,1,0:T(2,128)(2,1)S(1)}, bf16[512,2,1024]{2,1,0:T(2,128)(2,1)}, u32[]{:S(2)}) copy-start(bf16[512,2,1024]{2,1,0:T(2,128)(2,1)} %param.7) | copy-start | bytes 6291460
  171.4 79.4 %copy-start.4 = (bf16[512,2,1024]{2,1,0:T(2,128)(2,1)S(1)}, bf16[512,2,1024]{2,1,0:T(2,128)(2,1)}, u32[]{:S(2)}) copy-start(bf16[512,2,1024]{2,1,0:T(2,128)(2,1)} %param.8) | copy-start | bytes 6291460
  178.1 29.0 %copy-start.5 = (f32[512,1024]{1,0:T(8,128)}, f32[512,1024]{1,0:T(8,128)S(1)}, u32[]{:S(2)}) copy-start(f32[512,1024]{1,0:T(8,128)S(1)} %collective-permute-done.5) | copy-start | bytes 6291460
  287.4 26.2 %collective-permute-start.7 = (bf16[512,1024]{1,0:T(8,128)(2,1)}, bf16[512,1024]{1,0:T(8,128)(2,1)S(1)}, u32[]{:S(2)}, u32[]{:S(2)}) collective-permute-start(bf16[512,1024]{1,0:T(8,128)(2,1)} %get-tuple-element.9), channel_id=1, source_target_pairs={{0,16},{8,24},{16,0},{24,8},{1,17},{9,25},{17,1},{25,9},{2,18},{10... | collective-permute-start | bytes 3145736 | tf_op jit(solution)/shard_map/ppermute | solution.py:19
  288.9 31.4 %collective-permute-start.6 = (bf16[512,1024]{1,0:T(8,128)(2,1)}, bf16[512,1024]{1,0:T(8,128)(2,1)S(1)}, u32[]{:S(2)}, u32[]{:S(2)}) collective-permute-start(bf16[512,1024]{1,0:T(8,128)(2,1)} %get-tuple-element.10), channel_id=1, source_target_pairs={{0,8},{8,0},{16,24},{24,16},{1,9},{9,1},{17,25},{25,17},{2,10},{10... | collective-permute-start | bytes 3145736 | tf_op jit(solution)/shard_map/ppermute | solution.py:19
  289.3 46.4 %collective-permute-start.8 = (bf16[512,1024]{1,0:T(8,128)(2,1)}, bf16[512,1024]{1,0:T(8,128)(2,1)}, u32[]{:S(2)}, u32[]{:S(2)}) collective-permute-start(bf16[512,1024]{1,0:T(8,128)(2,1)} %get-tuple-element.8), channel_id=1, source_target_pairs={{0,24},{8,16},{16,8},{24,0},{1,25},{9,17},{17,9},{25,1},{2,26},{10... | collective-permute-start | bytes 3145736 | tf_op jit(solution)/shard_map/ppermute | solution.py:19
  289.6 24.1 %copy-start.10 = (bf16[512,3072]{1,0:T(8,128)(2,1)S(1)}, bf16[512,3072]{1,0:T(8,128)(2,1)}, u32[]{:S(2)}) copy-start(bf16[512,3072]{1,0:T(8,128)(2,1)} %copy-done.9) | copy-start | bytes 9437188
  298.0 22.3 %copy-start.8 = (bf16[512,3072]{1,0:T(8,128)(2,1)S(1)}, bf16[512,3072]{1,0:T(8,128)(2,1)}, u32[]{:S(2)}) copy-start(bf16[512,3072]{1,0:T(8,128)(2,1)} %copy-done.7) | copy-start | bytes 9437188
  320.3 15.4 %copy-start.2 = (bf16[512,3072]{1,0:T(8,128)(2,1)S(1)}, bf16[512,3072]{1,0:T(8,128)(2,1)}, u32[]{:S(2)}) copy-start(bf16[512,3072]{1,0:T(8,128)(2,1)} %copy-done.1) | copy-start | bytes 9437188
  503.8 2.8 copy-start
Sparse Core Ops, SparseCore 0:
  10.2 61.5 all-gather.1

commit v2 on v1

--- a/solution.py
+++ b/solution.py
@@ -19,7 +19,8 @@
     return lax.ppermute(array, axis, [(i, i ^ mask) for i in range(size)])
 
 
-def update_kernel(grad_ref, weight_ref, momentum_ref, new_weight_ref, new_momentum_ref):
+def update_kernel(grad_ref, weight_ref, momentum_ref, *refs):
+    new_weight_ref, new_momentum_ref = refs[-2:]
     grad = grad_ref[0].astype(jnp.float32)
     moment = momentum_ref[0].astype(jnp.float32)
     weight = weight_ref[0].astype(jnp.float32)
@@ -32,25 +33,91 @@
     )
 
 
-def update(grad, weight, momentum):
+def update(part, parts, grad, weight, momentum, done):
     sources, rows, cols = grad.shape
-    block = pl.BlockSpec((1, rows, cols), lambda s: (s, 0, 0))
-    wide = pl.BlockSpec((1, rows, cols), lambda s: (0, 0, s))
+    own = pl.BlockSpec((1, rows, cols), lambda s: (s, 0, 0))
+    half = pl.BlockSpec((1, rows, cols), lambda s: (s, 0, part))
+    wide = pl.BlockSpec((1, rows, cols), lambda s: (0, 0, s * parts + part))
+    size = grad.size
     return pl.pallas_call(
         update_kernel,
         grid=(sources,),
-        in_specs=[block, block, wide],
+        in_specs=[own, half, wide] + [pl.BlockSpec(memory_space=pl.ANY)] * len(done),
         out_specs=[wide, wide],
         out_shape=[
             jax.ShapeDtypeStruct(momentum.shape, jnp.float32),
             jax.ShapeDtypeStruct(momentum.shape, jnp.bfloat16),
         ],
+        input_output_aliases={3 + i: i for i in range(len(done))},
+        compiler_params=pltpu.CompilerParams(vmem_limit_bytes=32 * 1024 * 1024),
+        cost_estimate=pl.CostEstimate(flops=10 * size, bytes_accessed=12 * size, transcendentals=size),
+        name="lion_step",
+    )(grad, weight, momentum, *done)
+
+
+def term_kernel(count, *refs):
+    tokens, hidden, out_ref = refs[:count], refs[count : 2 * count], refs[-1]
+    total = None
+    for token_ref, hidden_ref in zip(tokens, hidden):
+        one = lax.dot_general(
+            token_ref[...],
+            hidden_ref[...],
+            (((0,), (0,)), ((), ())),
+            preferred_element_type=jnp.float32,
+        )
+        total = one if total is None else total + one
+    out_ref[...] = total.astype(jnp.bfloat16)
+
+
+def term_of(part, parts, tokens, hidden):
+    group_tok, width = tokens[0].shape
+    cols = hidden[0].shape[1] // parts
+    tall = width // 8
+    count = len(tokens)
+    return pl.pallas_call(
+        functools.partial(term_kernel, count),
+        grid=(width // tall,),
+        in_specs=[pl.BlockSpec((group_tok, tall), lambda i: (0, i))] * count
+        + [pl.BlockSpec((group_tok, cols), lambda i: (0, part))] * count,
+        out_specs=pl.BlockSpec((tall, cols), lambda i: (i, 0)),
+        out_shape=jax.ShapeDtypeStruct((width, cols), jnp.bfloat16),
+        compiler_params=pltpu.CompilerParams(vmem_limit_bytes=40 * 1024 * 1024),
+        cost_estimate=pl.CostEstimate(
+            flops=2 * count * group_tok * width * cols,
+            bytes_accessed=2 * (count * group_tok * (width + cols) + width * cols),
+            transcendentals=0,
+        ),
+        name="group_terms",
+    )(*tokens, *hidden)
+
+
+def deriv_kernel(tokens_ref, weight_ref, out_ref):
+    out_ref[...] = jnp.dot(
+        tokens_ref[...], weight_ref[...], preferred_element_type=jnp.float32
+    )
+
+
+def deriv_of(tokens, weight):
+    group_tok, width = tokens.shape
+    cols = weight.shape[1]
+    wide = 256 if cols % 256 == 0 else cols
+    return pl.pallas_call(
+        deriv_kernel,
+        grid=(cols // wide,),
+        in_specs=[
+            pl.BlockSpec((group_tok, width), lambda i: (0, 0)),
+            pl.BlockSpec((width, wide), lambda i: (0, i)),
+        ],
+        out_specs=pl.BlockSpec((group_tok, wide), lambda i: (0, i)),
+        out_shape=jax.ShapeDtypeStruct((group_tok, cols), jnp.float32),
         compiler_params=pltpu.CompilerParams(vmem_limit_bytes=32 * 1024 * 1024),
         cost_estimate=pl.CostEstimate(
-            flops=10 * momentum.size, bytes_accessed=12 * momentum.size, transcendentals=momentum.size
+            flops=2 * group_tok * width * cols,
+            bytes_accessed=2 * (group_tok + cols) * width + 4 * group_tok * cols,
+            transcendentals=0,
         ),
-        name="lion_step",
-    )(grad, weight, momentum)
+        name="hidden_deriv",
+    )(tokens, weight)
 
 
 def body(out_grad, gate_saved, up_saved, routing, down_weight, momentum):
@@ -81,28 +148,36 @@
         picked = jnp.sum(jnp.where(chosen, hidden, jnp.zeros_like(hidden)), axis=1)
         rows_of[m] = swapped(picked, "expert", m) if m else picked
 
-    weight = down_weight[0]
+    weight_shards, rows_of = lax.optimization_barrier((weight_shards, rows_of))
+    each = range(experts)
+    parts = 2 if cols % 256 == 0 else 1
+    terms = [
+        term_of(part, parts, [tokens[m] for m in each], [rows_of[m] for m in each])
+        for part in range(parts)
+    ]
+
+    weight, gate_saved, up_saved, first = lax.optimization_barrier(
+        (down_weight[0], gate_saved, up_saved, terms[0])
+    )
+    gate = gate_saved.astype(jnp.float32)
+    up = up_saved.astype(jnp.float32)
+    sigma = jax.nn.sigmoid(gate)
     deriv = jnp.zeros(gate.shape, jnp.float32)
-    term = jnp.zeros((width, cols), jnp.float32)
-    for m in range(experts):
-        part = jnp.dot(tokens[m], weight, preferred_element_type=jnp.float32)
+    for m in each:
+        part = deriv_of(tokens[m], weight)
         back = swapped(part, "expert", m) if m else part
         chosen = (routing == (mine ^ m))[:, :, None]
         deriv = jnp.where(chosen, back[:, None, :], deriv)
-        term = term + lax.dot_general(
-            tokens[m], rows_of[m], (((0,), (0,)), ((), ())), preferred_element_type=jnp.float32
-        )
-
-    grad_shards = lax.all_to_all(
-        term.astype(jnp.bfloat16).reshape(shards, rows, cols),
-        "dp",
-        split_axis=0,
-        concat_axis=0,
-        tiled=True,
-    )
     d_up = (deriv * gate * sigma).astype(jnp.bfloat16)
     d_gate = (deriv * up * sigma * (1.0 + gate * (1.0 - sigma))).astype(jnp.bfloat16)
-    new_weight, new_momentum = update(grad_shards, weight_shards, momentum)
+
+    done = ()
+    for part, term in enumerate([first] + terms[1:]):
+        grad_shards = lax.all_to_all(
+            term.reshape(shards, rows, cols // parts), "dp", split_axis=0, concat_axis=0, tiled=True
+        )
+        done = update(part, parts, grad_shards, weight_shards, momentum, done)
+    new_weight, new_momentum = done
     return (d_gate, d_up, new_weight, new_momentum)
 
 

time: 528 us -> 507 us (0.960)
  blocking collectives: 143 us -> 0 us
  waiting for transfers between devices: 229 us -> 333 us
  matrix products: 67.4 us -> 0 us
  Pallas kernels: 12 us -> 65 us
  starting transfers between devices: 11.2 us -> 27.5 us
  other arithmetic: 36.6 us -> 45.3 us
    all_to_all x1 -> x0, blocking collectives: 143 us -> none  [body(): lax.all_to_all(term.astype(jnp.bfloat16).reshape(shards, rows, cols), 'dp...]
    all_gather x1, waiting for transfers between devices: 63.9 us -> 152 us  [body(): tokens = {0: lax.all_gather(out_grad, 'dp', axis=0, tiled=True)}]
    dot_general x8 -> x0, matrix products: 67.4 us -> none  [the longest x4 38.4 us: body(): lax.dot_general(tokens[m], rows_of[m], (((0,), (0,)), ((), ())), preferre...]
    pallas_call x1 -> x8, Pallas kernels: 12 us -> 65 us  [the longest x4 26.7 us: deriv_of(): pl.pallas_call(deriv_kernel, grid=(cols // wide,), in_specs=[pl.BlockSpec...]
    all_to_all x0 -> x2, waiting for transfers between devices: none -> 39.8 us  [body(): lax.all_to_all(term.reshape(shards, rows, cols // parts), 'dp', split_axi...]
    ppermute x9, waiting for transfers between devices: 165 us -> 140 us  [swapped(): return lax.ppermute(array, axis, [(i, i ^ mask) for i in range(size)])]
    all_to_all x0 -> x2, starting transfers between devices: none -> 15.2 us  [body(): lax.all_to_all(term.reshape(shards, rows, cols // parts), 'dp', split_axi...]
    unnamed x26 -> x44, local copies, waits for them, and re-layouts: 2.84 us -> 16.1 us
  transfers between devices with their start and end apart: 11 -> 13, of which waited for: 6 -> 7; matrix products, arithmetic and copies ran while one was open for 22% -> 9% of each run, Pallas kernels for 0% -> 9%
where the time goes in v2:
time: 507 us; the launch traced here: 502 us
  waiting for transfers between devices  333 us (66%)
  Pallas kernels  65 us (13%)
  other arithmetic  45.3 us (9%)
  starting transfers between devices  27.5 us (5%)
  local copies, waits for them, and re-layouts  16.9 us (3%)
  between operations  14.2 us (3%)
    all_gather x1, waiting for transfers between devices, body(): tokens = {0: lax.all_gather(out_grad, 'dp', axis=0, tiled=True)}  152 us
    ppermute x9, waiting for transfers between devices, swapped(): return lax.ppermute(array, axis, [(i, i ^ mask) for i in range(size)])  140 us
    all_to_all x2, waiting for transfers between devices, body(): lax.all_to_all(term.reshape(shards, rows, cols // parts), 'dp', split_axi...  39.8 us
    reduce_sum x1, other arithmetic, body(): picked = jnp.sum(jnp.where(chosen, hidden, jnp.zeros_like(hidden)), axis=1)  29 us
    pallas_call x4, Pallas kernels, deriv_of(): pl.pallas_call(deriv_kernel, grid=(cols // wide,), in_specs=[pl.BlockSpec...  26.7 us
    pallas_call x2, Pallas kernels, term_of(): pl.pallas_call(functools.partial(term_kernel, count), grid=(width // tall...  20.8 us
    pallas_call x2, Pallas kernels, update(): pl.pallas_call(update_kernel, grid=(sources,), in_specs=[own, half, wide]...  17.4 us
    convert_element_type x1, other arithmetic, body(): d_up = (deriv * gate * sigma).astype(jnp.bfloat16)  16.3 us
  transfers between devices with their start and end apart: 13, of which 7 were waited for; matrix products, arithmetic and copies ran while one was open for 9% of the time, Pallas kernels for 9%

profile of v2, /device:TPU:8, one launch (start us, length us, event | category | flops | bytes accessed | tf_op | source)
XLA Modules:
  0.0 501.7 jit_solution(619503915627470125)
XLA Ops:
  7.2 0.0 all-gather.2.cloned.1.call-start
  7.2 0.7 all-gather.2.cloned.1.call-update
  7.9 0.0 copy-start.19
  7.9 0.0 copy-start.18
  7.9 6.4 %all-to-all-start = ((bf16[8,384,1024]{2,1,0:T(8,128)(2,1)}), bf16[8,384,1024]{2,1,0:T(8,128)(2,1)}, u32[]{:S(2)}, u32[]{:S(2)}) async-start(bf16[8,384,1024]{2,1,0:T(8,128)(2,1)} %bitcast.6), calls=%async_computation | async-start | bytes 12582912 | tf_op jit(solution)/shard_map/all_to_all | solution.py:131
  14.3 151.9 %all-gather.2.cloned.1.call-done.refs_0_.tokens_ref = bf16[512,3072]{1,0:T(8,128)(2,1)} async-done(((bf16[64,3072]{1,0:T(8,128)(2,1)}), bf16[512,3072]{1,0:T(8,128)(2,1)}) %all-gather.2.cloned.1.call-update) | async-done | bytes 3145744 | tf_op jit(solution)/shard_map/all_gather | solution.py:135
  166.2 1.5 collective-permute-start
  167.8 0.0 copy-done.19
  167.8 0.2 copy.13
  168.0 0.2 copy.12
  168.2 0.2 copy.15
  168.4 0.2 copy.14
  168.6 0.1 collective-permute-start.2
  168.7 68.0 %collective-permute-done.refs_2_.tokens_ref = bf16[512,3072]{1,0:T(8,128)(2,1)} collective-permute-done((bf16[512,3072]{1,0:T(8,128)(2,1)}, bf16[512,3072]{1,0:T(8,128)(2,1)}, u32[]{:S(2)}, u32[]{:S(2)}) %collective-permute-start) | collective-permute-done | bytes 3145760 | tf_op jit(solution)/shard_map/ppermute | solution.py:19
  236.6 0.0 collective-permute-start.1
  236.6 0.0 copy-done.18
  236.6 29.0 %fusion.12 = (bf16[512,1024]{1,0:T(8,128)(2,1)}, bf16[512,1024]{1,0:T(8,128)(2,1)}, bf16[512,1024]{1,0:T(8,128)(2,1)S(1)}, bf16[512,1024]{1,0:T(8,128)(2,1)S(1)}) fusion(pred[512,2]{1,0:T(8,128)(4,1)S(1)} %copy.12, pred[512,2]{1,0:T(8,128)(4,1)S(1)} %copy.15, pred[512,2]{1,0:T(8,128)(4,1)S(1)} %copy.14, pred[512,2]{1,0:T(8,128)(4,1)S(1)} %copy.13, ...), kind=kLoop, calls=%fused_computation.22 | loop fusion | flops 14680064 | bytes 8392704 | tf_op jit(solution)/shard_map/reduce_sum | solution.py:148
  265.7 1.6 collective-permute-start.5
  267.3 0.5 collective-permute-start.4
  267.8 0.0 collective-permute-start.3
  267.8 23.3 %collective-permute-done.5.refs_7_ = bf16[512,1024]{1,0:T(8,128)(2,1)S(1)} collective-permute-done((bf16[512,1024]{1,0:T(8,128)(2,1)}, bf16[512,1024]{1,0:T(8,128)(2,1)S(1)}, u32[]{:S(2)}, u32[]{:S(2)}) %collective-permute-start.5) | collective-permute-done | bytes 1048608 | tf_op jit(solution)/shard_map/ppermute | solution.py:19
  291.1 22.7 %collective-permute-done.4.refs_6_ = bf16[512,1024]{1,0:T(8,128)(2,1)S(1)} collective-permute-done((bf16[512,1024]{1,0:T(8,128)(2,1)}, bf16[512,1024]{1,0:T(8,128)(2,1)S(1)}, u32[]{:S(2)}, u32[]{:S(2)}) %collective-permute-start.4) | collective-permute-done | bytes 1048608 | tf_op jit(solution)/shard_map/ppermute | solution.py:19
  313.8 0.0 collective-permute-done.3.refs_5_
  313.8 1.0 copy-done.15
  314.8 0.0 all-to-all-done.weight_ref
  314.8 0.0 collective-permute-done.2.refs_1_.tokens_ref
  314.8 0.0 collective-permute-done.1.refs_3_.tokens_ref
  314.9 0.0 copy-start.9
  314.9 1.9 copy-done.9
  316.7 1.2 copy-done.16
  318.0 10.4 %group_terms.2 = bf16[3072,512]{1,0:T(8,128)(2,1)S(1)} custom-call(bf16[512,3072]{1,0:T(8,128)(2,1)S(1)} %copy-done.9, bf16[512,3072]{1,0:T(8,128)(2,1)} %collective-permute-done.2.refs_1_.tokens_ref, bf16[512,3072]{1,0:T(8,128)(2,1)} %collective-permute-done.refs_2_.tokens_ref, bf16[512,3072]{1,0:T(8,128)(2,1)} %collective-permute-done.1.refs_3_.tokens_ref, ...), custom_call_target="tpu_custom_call" | custom-call | flops 6442450944 | bytes 17825792 | tf_op jit(solution)/shard_map/group_terms/pallas_call | solution.py:77
  328.4 0.0 copy-done.7
  328.4 0.0 copy-done.11
  328.4 0.0 copy-start.5
  328.4 1.7 copy-done.5
  330.1 8.3 %all-to-all-start.2 = ((bf16[8,384,512]{2,1,0:T(8,128)(2,1)}), bf16[8,384,512]{2,1,0:T(8,128)(2,1)S(1)}, u32[]{:S(2)}, u32[]{:S(2)}) async-start(bf16[8,384,512]{2,1,0:T(8,128)(2,1)} %bitcast.12), calls=%async_computation.2 | async-start | bytes 6291456 | tf_op jit(solution)/shard_map/all_to_all | solution.py:176
  338.3 2.8 copy-done.3
  341.1 7.3 %hidden_deriv.4 = f32[512,1024]{1,0:T(8,128)} custom-call(bf16[512,3072]{1,0:T(8,128)(2,1)} %collective-permute-done.1.refs_3_.tokens_ref, bf16[3072,1024]{1,0:T(8,128)(2,1)S(1)} %bitcast.7), custom_call_target="tpu_custom_call" | custom-call | flops 3221225472 | bytes 11534336 | tf_op jit(solution)/shard_map/hidden_deriv/pallas_call | solution.py:104
  348.4 0.3 collective-permute-start.6
  348.7 7.3 %hidden_deriv.5 = f32[512,1024]{1,0:T(8,128)} custom-call(bf16[512,3072]{1,0:T(8,128)(2,1)} %collective-permute-done.refs_2_.tokens_ref, bf16[3072,1024]{1,0:T(8,128)(2,1)S(1)} %bitcast.8), custom_call_target="tpu_custom_call" | custom-call | flops 3221225472 | bytes 11534336 | tf_op jit(solution)/shard_map/hidden_deriv/pallas_call | solution.py:104
  356.0 1.2 collective-permute-start.7
  357.2 7.3 %hidden_deriv.6 = f32[512,1024]{1,0:T(8,128)} custom-call(bf16[512,3072]{1,0:T(8,128)(2,1)} %collective-permute-done.2.refs_1_.tokens_ref, bf16[3072,1024]{1,0:T(8,128)(2,1)S(1)} %bitcast.9), custom_call_target="tpu_custom_call" | custom-call | flops 3221225472 | bytes 11534336 | tf_op jit(solution)/shard_map/hidden_deriv/pallas_call | solution.py:104
  364.5 0.7 collective-permute-start.8
  365.1 4.9 hidden_deriv.7
  370.0 0.0 copy-start.6
  370.1 1.3 copy-done.6
  371.4 0.0 copy-done.17
  371.4 10.4 %group_terms.3 = bf16[3072,512]{1,0:T(8,128)(2,1)S(1)} custom-call(bf16[512,3072]{1,0:T(8,128)(2,1)S(1)} %copy-done.10, bf16[512,3072]{1,0:T(8,128)(2,1)} %collective-permute-done.2.refs_1_.tokens_ref, bf16[512,3072]{1,0:T(8,128)(2,1)} %collective-permute-done.refs_2_.tokens_ref, bf16[512,3072]{1,0:T(8,128)(2,1)} %collective-permute-done.1.refs_3_.tokens_ref, ...), custom_call_target="tpu_custom_call" | custom-call | flops 6442450944 | bytes 17825792 | tf_op jit(solution)/shard_map/group_terms/pallas_call | solution.py:77
  381.8 0.0 copy-start.4
  381.8 1.7 copy-done.4
  383.5 23.0 %all-to-all-done.2.grad_ref = bf16[8,384,512]{2,1,0:T(8,128)(2,1)S(1)} async-done(((bf16[8,384,512]{2,1,0:T(8,128)(2,1)}), bf16[8,384,512]{2,1,0:T(8,128)(2,1)S(1)}, u32[]{:S(2)}, u32[]{:S(2)}) %all-to-all-start.2) | async-done | bytes 3145760 | tf_op jit(solution)/shard_map/all_to_all | solution.py:176
  406.5 1.7 copy-done.1
  408.2 6.9 %all-to-all-start.1 = ((bf16[8,384,512]{2,1,0:T(8,128)(2,1)}), bf16[8,384,512]{2,1,0:T(8,128)(2,1)}, u32[]{:S(2)}, u32[]{:S(2)}) async-start(bf16[8,384,512]{2,1,0:T(8,128)(2,1)} %bitcast.11), calls=%async_computation.1 | async-start | bytes 6291456 | tf_op jit(solution)/shard_map/all_to_all | solution.py:176
  415.1 0.0 collective-permute-done.6
  415.1 26.5 %collective-permute-done.7 = f32[512,1024]{1,0:T(8,128)} collective-permute-done((f32[512,1024]{1,0:T(8,128)}, f32[512,1024]{1,0:T(8,128)}, u32[]{:S(2)}, u32[]{:S(2)}) %collective-permute-start.7) | collective-permute-done | bytes 2097184 | tf_op jit(solution)/shard_map/ppermute | solution.py:19
  441.6 0.0 collective-permute-done.8
  441.6 16.3 %fusion.10 = (bf16[512,2,1024]{2,1,0:T(2,128)(2,1)}, bf16[512,2,1024]{2,1,0:T(2,128)(2,1)}) fusion(bf16[512,2,1024]{2,1,0:T(2,128)(2,1)} %param.7, pred[512,2]{1,0:T(8,128)(4,1)S(1)} %copy.13, pred[512,2]{1,0:T(8,128)(4,1)S(1)} %copy.14, pred[512,2]{1,0:T(8,128)(4,1)S(1)} %copy.15, pred[512,2]{1,0:T(8,128)(4,1)S(1)} %copy.12, f32[512,1024]{1,0:T(8,128)} %copy-done.6, ...), kind=kLoop, calls=%fused_computation.15 | loop fusion | flops 19922944 | bytes 16781312 | tf_op jit(solution)/shard_map/convert_element_type | solution.py:171
  457.9 0.0 slice-done
  457.9 0.0 slice-done.1
  457.9 0.0 copy-done.2
  458.0 8.1 %lion_step.2 = (f32[1,384,8192]{2,1,0:T(8,128)}, bf16[1,384,8192]{2,1,0:T(8,128)(2,1)}) custom-call(bf16[8,384,512]{2,1,0:T(8,128)(2,1)S(1)} %copy-done.2, bf16[8,384,1024]{2,1,0:T(8,128)(2,1)} %all-to-all-done.weight_ref, bf16[1,384,8192]{2,1,0:T(8,128)(2,1)S(1)} %bitcast.5), custom_call_target="tpu_custom_call" | custom-call | flops 15728640 | bytes 18874368 | tf_op jit(solution)/shard_map/lion_step/pallas_call | solution.py:42
  466.1 16.8 %all-to-all-done.1.grad_ref = bf16[8,384,512]{2,1,0:T(8,128)(2,1)} async-done(((bf16[8,384,512]{2,1,0:T(8,128)(2,1)}), bf16[8,384,512]{2,1,0:T(8,128)(2,1)}, u32[]{:S(2)}, u32[]{:S(2)}) %all-to-all-start.1) | async-done | bytes 3145760 | tf_op jit(solution)/shard_map/all_to_all | solution.py:176
  482.8 2.8 copy-done
  485.6 9.3 %lion_step.3 = (f32[1,384,8192]{2,1,0:T(8,128)}, bf16[1,384,8192]{2,1,0:T(8,128)(2,1)}) custom-call(bf16[8,384,512]{2,1,0:T(8,128)(2,1)} %all-to-all-done.1.grad_ref, bf16[8,384,1024]{2,1,0:T(8,128)(2,1)} %all-to-all-done.weight_ref, bf16[1,384,8192]{2,1,0:T(8,128)(2,1)S(1)} %copy-done, ...), custom_call_target="tpu_custom_call", output_to_operand_aliasing={{0}: (3, {}), {1}: (4, {})} | custom-call | flops 15728640 | bytes 18874368 | tf_op jit(solution)/shard_map/lion_step/pallas_call | solution.py:42
  (23 shorter events, 0.0 us)
Async XLA Ops:
  7.2 159.1 %all-gather.2.cloned.1.call-start = ((), (), s32[]{:S(2)}) async-start(), calls=%async_computation.3 | async-start | bytes 3538944 | tf_op jit(solution)/shard_map/all_gather | solution.py:135
  7.9 159.9 %copy-start.19 = (s32[512,2]{0,1:T(2,128)S(1)}, s32[512,2]{0,1:T(2,128)}, u32[]{:S(2)}) copy-start(s32[512,2]{0,1:T(2,128)} %param.9) | copy-start | bytes 12292
  7.9 228.7 %copy-start.18 = (bf16[512,2,1024]{2,1,0:T(2,128)(2,1)S(1)}, bf16[512,2,1024]{2,1,0:T(2,128)(2,1)}, u32[]{:S(2)}) copy-start(bf16[512,2,1024]{2,1,0:T(2,128)(2,1)} %param.7) | copy-start | bytes 6291460
  7.9 306.9 %all-to-all-start = ((bf16[8,384,1024]{2,1,0:T(8,128)(2,1)}), bf16[8,384,1024]{2,1,0:T(8,128)(2,1)}, u32[]{:S(2)}, u32[]{:S(2)}) async-start(bf16[8,384,1024]{2,1,0:T(8,128)(2,1)} %bitcast.6), calls=%async_computation | async-start | bytes 12582912 | tf_op jit(solution)/shard_map/all_to_all | solution.py:131
  166.2 70.4 %collective-permute-start = (bf16[512,3072]{1,0:T(8,128)(2,1)}, bf16[512,3072]{1,0:T(8,128)(2,1)}, u32[]{:S(2)}, u32[]{:S(2)}) collective-permute-start(bf16[512,3072]{1,0:T(8,128)(2,1)} %all-gather.2.cloned.1.call-done.refs_0_.tokens_ref), channel_id=1, source_target_pairs={{0,16},{8,24},{16,0},{24,8},{1,17},{9,25},{17,1},{25,9},{2,18},{10... | collective-permute-start | bytes 9437192 | tf_op jit(solution)/shard_map/ppermute | solution.py:19
  168.6 146.3 %collective-permute-start.2 = (bf16[512,3072]{1,0:T(8,128)(2,1)}, bf16[512,3072]{1,0:T(8,128)(2,1)}, u32[]{:S(2)}, u32[]{:S(2)}) collective-permute-start(bf16[512,3072]{1,0:T(8,128)(2,1)} %all-gather.2.cloned.1.call-done.refs_0_.tokens_ref), channel_id=1, source_target_pairs={{0,8},{8,0},{16,24},{24,16},{1,9},{9,1},{17,25},{25,17},{2,10},{10... | collective-permute-start | bytes 9437192 | tf_op jit(solution)/shard_map/ppermute | solution.py:19
  236.6 78.2 %collective-permute-start.1 = (bf16[512,3072]{1,0:T(8,128)(2,1)}, bf16[512,3072]{1,0:T(8,128)(2,1)}, u32[]{:S(2)}, u32[]{:S(2)}) collective-permute-start(bf16[512,3072]{1,0:T(8,128)(2,1)} %collective-permute-done.refs_2_.tokens_ref), channel_id=1, source_target_pairs={{0,8},{8,0},{16,24},{24,16},{1,9},{9,1},{17,25},{25,17},{2,10},{10... | collective-permute-start | bytes 9437192 | tf_op jit(solution)/shard_map/ppermute | solution.py:19
  265.7 62.7 %copy-start.7 = (bf16[512,1024]{1,0:T(8,128)(2,1)}, bf16[512,1024]{1,0:T(8,128)(2,1)S(1)}, u32[]{:S(2)}) copy-start(bf16[512,1024]{1,0:T(8,128)(2,1)S(1)} %get-tuple-element.17.refs_4_) | copy-start | bytes 3145732
  265.7 25.5 %collective-permute-start.5 = (bf16[512,1024]{1,0:T(8,128)(2,1)}, bf16[512,1024]{1,0:T(8,128)(2,1)S(1)}, u32[]{:S(2)}, u32[]{:S(2)}) collective-permute-start(bf16[512,1024]{1,0:T(8,128)(2,1)} %get-tuple-element.30), channel_id=1, source_target_pairs={{0,24},{8,16},{16,8},{24,0},{1,25},{9,17},{17,9},{25,1},{2,26},{10... | collective-permute-start | bytes 3145736 | tf_op jit(solution)/shard_map/ppermute | solution.py:19
  267.3 46.5 %collective-permute-start.4 = (bf16[512,1024]{1,0:T(8,128)(2,1)}, bf16[512,1024]{1,0:T(8,128)(2,1)S(1)}, u32[]{:S(2)}, u32[]{:S(2)}) collective-permute-start(bf16[512,1024]{1,0:T(8,128)(2,1)} %get-tuple-element.31), channel_id=1, source_target_pairs={{0,16},{8,24},{16,0},{24,8},{1,17},{9,25},{17,1},{25,9},{2,18},{10... | collective-permute-start | bytes 3145736 | tf_op jit(solution)/shard_map/ppermute | solution.py:19
  267.8 46.0 %collective-permute-start.3 = (bf16[512,1024]{1,0:T(8,128)(2,1)S(1)}, bf16[512,1024]{1,0:T(8,128)(2,1)S(1)}, u32[]{:S(2)}, u32[]{:S(2)}) collective-permute-start(bf16[512,1024]{1,0:T(8,128)(2,1)S(1)} %get-tuple-element.32), channel_id=1, source_target_pairs={{0,8},{8,0},{16,24},{24,16},{1,9},{9,1},{17,25},{25,17},{2,10},{10... | collective-permute-start | bytes 3145736 | tf_op jit(solution)/shard_map/ppermute | solution.py:19
  291.1 37.3 %copy-start.11 = (bf16[512,1024]{1,0:T(8,128)(2,1)}, bf16[512,1024]{1,0:T(8,128)(2,1)S(1)}, u32[]{:S(2)}) copy-start(bf16[512,1024]{1,0:T(8,128)(2,1)S(1)} %collective-permute-done.5.refs_7_) | copy-start | bytes 3145732
  313.8 14.6 %copy-start.13 = (bf16[512,1024]{1,0:T(8,128)(2,1)}, bf16[512,1024]{1,0:T(8,128)(2,1)S(1)}, u32[]{:S(2)}) copy-start(bf16[512,1024]{1,0:T(8,128)(2,1)S(1)} %collective-permute-done.4.refs_6_) | copy-start | bytes 3145732
  313.8 1.0 copy-start.15
  314.9 1.9 copy-start.9
  316.7 1.2 copy-start.16
  328.4 1.7 copy-start.5
  330.1 76.4 %all-to-all-start.2 = ((bf16[8,384,512]{2,1,0:T(8,128)(2,1)}), bf16[8,384,512]{2,1,0:T(8,128)(2,1)S(1)}, u32[]{:S(2)}, u32[]{:S(2)}) async-start(bf16[8,384,512]{2,1,0:T(8,128)(2,1)} %bitcast.12), calls=%async_computation.2 | async-start | bytes 6291456 | tf_op jit(solution)/shard_map/all_to_all | solution.py:176
  338.3 2.8 copy-start.3
  348.4 66.7 %collective-permute-start.6 = (f32[512,1024]{1,0:T(8,128)}, f32[512,1024]{1,0:T(8,128)}, u32[]{:S(2)}, u32[]{:S(2)}) collective-permute-start(f32[512,1024]{1,0:T(8,128)} %hidden_deriv.4), channel_id=1, source_target_pairs={{0,24},{8,16},{16,8},{24,0},{1,25},{9,17},{17,9},{25,1},{2,26},{10... | collective-permute-start | bytes 6291464 | tf_op jit(solution)/shard_map/ppermute | solution.py:19
  356.0 9.2 %copy-start.10 = (bf16[512,3072]{1,0:T(8,128)(2,1)S(1)}, bf16[512,3072]{1,0:T(8,128)(2,1)}, u32[]{:S(2)}) copy-start(bf16[512,3072]{1,0:T(8,128)(2,1)} %all-gather.2.cloned.1.call-done.refs_0_.tokens_ref) | copy-start | bytes 9437188
  356.0 85.6 %collective-permute-start.7 = (f32[512,1024]{1,0:T(8,128)}, f32[512,1024]{1,0:T(8,128)}, u32[]{:S(2)}, u32[]{:S(2)}) collective-permute-start(f32[512,1024]{1,0:T(8,128)} %hidden_deriv.5), channel_id=1, source_target_pairs={{0,16},{8,24},{16,0},{24,8},{1,17},{9,25},{17,1},{25,9},{2,18},{10... | collective-permute-start | bytes 6291464 | tf_op jit(solution)/shard_map/ppermute | solution.py:19
  364.5 6.9 %copy-start.8 = (bf16[512,1024]{1,0:T(8,128)(2,1)S(1)}, bf16[512,1024]{1,0:T(8,128)(2,1)}, u32[]{:S(2)}) copy-start(bf16[512,1024]{1,0:T(8,128)(2,1)} %copy-done.7) | copy-start | bytes 3145732
  364.5 6.9 %copy-start.12 = (bf16[512,1024]{1,0:T(8,128)(2,1)S(1)}, bf16[512,1024]{1,0:T(8,128)(2,1)}, u32[]{:S(2)}) copy-start(bf16[512,1024]{1,0:T(8,128)(2,1)} %copy-done.11) | copy-start | bytes 3145732
  364.5 6.9 %copy-start.14 = (bf16[512,1024]{1,0:T(8,128)(2,1)S(1)}, bf16[512,1024]{1,0:T(8,128)(2,1)}, u32[]{:S(2)}) copy-start(bf16[512,1024]{1,0:T(8,128)(2,1)} %copy-done.13) | copy-start | bytes 3145732
  364.5 6.9 %copy-start.17 = (bf16[512,1024]{1,0:T(8,128)(2,1)S(1)}, bf16[512,1024]{1,0:T(8,128)(2,1)}, u32[]{:S(2)}) copy-start(bf16[512,1024]{1,0:T(8,128)(2,1)} %copy-done.15) | copy-start | bytes 3145732
  364.5 77.1 %collective-permute-start.8 = (f32[512,1024]{1,0:T(8,128)}, f32[512,1024]{1,0:T(8,128)}, u32[]{:S(2)}, u32[]{:S(2)}) collective-permute-start(f32[512,1024]{1,0:T(8,128)} %hidden_deriv.6), channel_id=1, source_target_pairs={{0,8},{8,0},{16,24},{24,16},{1,9},{9,1},{17,25},{25,17},{2,10},{10... | collective-permute-start | bytes 6291464 | tf_op jit(solution)/shard_map/ppermute | solution.py:19
  370.0 1.3 copy-start.6
  381.8 1.7 copy-start.4
  406.5 1.7 copy-start.1
  408.2 49.7 %slice-start = ((s8[6291456]{0:T(1024)(128)(4,1)}), s8[2097152]{0:T(1024)(128)(4,1)S(1)}, s32[]{:S(2)}) async-start(s8[6291456]{0:T(1024)(128)(4,1)} %bitcast.4), calls=%async_computation.4 | async-start | bytes 4194304
  408.2 74.6 %all-to-all-start.1 = ((bf16[8,384,512]{2,1,0:T(8,128)(2,1)}), bf16[8,384,512]{2,1,0:T(8,128)(2,1)}, u32[]{:S(2)}, u32[]{:S(2)}) async-start(bf16[8,384,512]{2,1,0:T(8,128)(2,1)} %bitcast.11), calls=%async_computation.1 | async-start | bytes 6291456 | tf_op jit(solution)/shard_map/all_to_all | solution.py:176
  415.1 42.8 %slice-start.1 = ((s8[6291456]{0:T(1024)(128)(4,1)}), s8[4194304]{0:T(1024)(128)(4,1)S(1)}, s32[]{:S(2)}) async-start(s8[6291456]{0:T(1024)(128)(4,1)} %bitcast.4), calls=%async_computation.5 | async-start | bytes 8388608
  415.1 42.8 %copy-start.2 = (bf16[8,384,512]{2,1,0:T(8,128)(2,1)S(1)}, bf16[8,384,512]{2,1,0:T(8,128)(2,1)}, u32[]{:S(2)}) copy-start(bf16[8,384,512]{2,1,0:T(8,128)(2,1)} %copy-done.1) | copy-start | bytes 9437188
  482.8 2.8 copy-start
Sparse Core Ops, SparseCore 0:
  10.2 156.0 all-gather.1

commit v3 on v1

v3 whole, which is shorter than its diff:
```python
import functools

import jax
import jax.numpy as jnp
from jax import lax
from jax.experimental import pallas as pl
from jax.experimental.pallas import tpu as pltpu
from jax.sharding import PartitionSpec as P

beta_first = 0.9
beta_second = 0.99
step_rate = 0.01
decay_rate = 1.0
sign_width = 10.0
MIB = 1024 * 1024


def swapped(array, axis, mask):
    if mask == 0:
        return array
    size = lax.axis_size(axis)
    return lax.ppermute(array, axis, [(i, i ^ mask) for i in range(size)])


def after(value, *others):
    return lax.optimization_barrier((value, *others))[0]


def order_kernel(place_ref, mine_ref, theirs_ref, out_ref):
    out_ref[0, place_ref[0]] = mine_ref[0]
    out_ref[0, 1 - place_ref[0]] = theirs_ref[0]


def in_order(mine, theirs, bit):
    count, some, width = mine.shape
    one = pl.BlockSpec((1, some, width), lambda i, place: (i, 0, 0))
    both = pl.pallas_call(
        order_kernel,
        grid_spec=pltpu.PrefetchScalarGridSpec(
            num_scalar_prefetch=1,
            grid=(count,),
            in_specs=[one, one],
            out_specs=pl.BlockSpec((1, 2, some, width), lambda i, place: (i, 0, 0, 0)),
        ),
        out_shape=jax.ShapeDtypeStruct((count, 2, some, width), mine.dtype),
        cost_estimate=pl.CostEstimate(flops=0, bytes_accessed=8 * mine.size, transcendentals=0),
        name="side_by_side",
    )(bit.astype(jnp.int32).reshape(1), mine, theirs)
    return both.reshape(2 * count, some, width)


def pick(hidden, named_ref, out_refs):
    count_rows = hidden.shape[0]
    tokens = out_refs[0].shape[0]
    topk = count_rows // tokens
    token = lax.broadcasted_iota(jnp.int32, (tokens, count_rows), 0)
    row = lax.broadcasted_iota(jnp.int32, (tokens, count_rows), 1)
    here = (row >= token * topk) & (row < token * topk + topk)
    for m, out_ref in enumerate(out_refs):
        chosen = jnp.where(here & (named_ref[...] == m), 1.0, 0.0).astype(jnp.bfloat16)
        out_ref[...] = jnp.dot(chosen, hidden, preferred_element_type=jnp.float32).astype(
            jnp.bfloat16
        )


def hidden_kernel(gate_ref, up_ref, named_ref, hidden_ref, *out_refs):
    gate = gate_ref[...].astype(jnp.float32)
    up = up_ref[...].astype(jnp.float32)
    hidden = (gate * jax.nn.sigmoid(gate) * up).astype(jnp.bfloat16)
    hidden_ref[...] = hidden
    pick(hidden, named_ref, out_refs)


def pick_kernel(hidden_ref, named_ref, *out_refs):
    pick(hidden_ref[...], named_ref, out_refs)


def picked_rows(kernel, arrays, named, experts, topk, with_hidden):
    count_rows, cols = arrays[0].shape
    group_tok = count_rows // topk
    some = 128 if group_tok % 128 == 0 else group_tok
    row_block = pl.BlockSpec((some * topk, cols), lambda i: (i, 0))
    out_shape = [jax.ShapeDtypeStruct((group_tok, cols), jnp.bfloat16)] * experts
    out_specs = [pl.BlockSpec((some, cols), lambda i: (i, 0))] * experts
    if with_hidden:
        out_shape = [jax.ShapeDtypeStruct((count_rows, cols), jnp.bfloat16)] + out_shape
        out_specs = [row_block] + out_specs
    return pl.pallas_call(
        kernel,
        grid=(group_tok // some,),
        in_specs=[row_block] * len(arrays) + [pl.BlockSpec((1, some * topk), lambda i: (0, i))],
        out_specs=out_specs,
        out_shape=out_shape,
        compiler_params=pltpu.CompilerParams(vmem_limit_bytes=32 * MIB),
        cost_estimate=pl.CostEstimate(
            flops=2 * experts * count_rows * some * cols,
            bytes_accessed=2 * cols * (count_rows * (len(arrays) + 1) + experts * group_tok),
            transcendentals=count_rows * cols,
        ),
        name="hidden_rows",
    )(*arrays, named)


def term_kernel(count, place_ref, *refs):
    tokens, hidden, out_ref = refs[:count], refs[count : 2 * count], refs[-1]
    total = None
    for token_ref, hidden_ref in zip(tokens, hidden):
        one = lax.dot_general(
            token_ref[...],
            hidden_ref[...],
            (((0,), (0,)), ((), ())),
            preferred_element_type=jnp.float32,
        )
        total = one if total is None else total + one
    out_ref[...] = total.astype(jnp.bfloat16)


def terms(tokens, hidden, tall, first, steps):
    group_tok, width = tokens[0].shape
    cols = hidden[0].shape[1]
    count = len(tokens)
    return pl.pallas_call(
        functools.partial(term_kernel, count),
        grid_spec=pltpu.PrefetchScalarGridSpec(
            num_scalar_prefetch=1,
            grid=(steps,),
            in_specs=[pl.BlockSpec((group_tok, tall), lambda i, place: (0, place[0] + i))] * count
            + [pl.BlockSpec((group_tok, cols), lambda i, place: (0, 0))] * count,
            out_specs=pl.BlockSpec((tall, cols), lambda i, place: (i, 0)),
        ),
        out_shape=jax.ShapeDtypeStruct((steps * tall, cols), jnp.bfloat16),
        compiler_params=pltpu.CompilerParams(vmem_limit_bytes=40 * MIB),
        cost_estimate=pl.CostEstimate(
            flops=2 * count * group_tok * steps * tall * cols,
            bytes_accessed=2 * (count * group_tok * (steps * tall + cols) + steps * tall * cols),
            transcendentals=0,
        ),
        name="group_terms",
    )(first.reshape(1), *tokens, *hidden)


def deriv_kernel(place_ref, near_ref, far_ref, near_weight_ref, far_weight_ref, out_ref):
    out_ref[...] = jnp.dot(
        near_ref[...], near_weight_ref[...], preferred_element_type=jnp.float32
    ) + jnp.dot(far_ref[...], far_weight_ref[...], preferred_element_type=jnp.float32)


def deriv_of(near, far, weight, half):
    group_tok, width = near.shape
    cols = weight.shape[1]
    wide = 256 if cols % 256 == 0 else cols
    whole = pl.BlockSpec((group_tok, width), lambda i, place: (0, 0))
    return pl.pallas_call(
        deriv_kernel,
        grid_spec=pltpu.PrefetchScalarGridSpec(
            num_scalar_prefetch=1,
            grid=(cols // wide,),
            in_specs=[
                whole,
                whole,
                pl.BlockSpec((width, wide), lambda i, place: (place[0], i)),
                pl.BlockSpec((width, wide), lambda i, place: (1 - place[0], i)),
            ],
            out_specs=pl.BlockSpec((group_tok, wide), lambda i, place: (0, i)),
        ),
        out_shape=jax.ShapeDtypeStruct((group_tok, cols), jnp.float32),
        compiler_params=pltpu.CompilerParams(vmem_limit_bytes=32 * MIB),
        cost_estimate=pl.CostEstimate(
            flops=4 * group_tok * width * cols,
            bytes_accessed=4 * (group_tok + cols) * width + 4 * group_tok * cols,
            transcendentals=0,
        ),
        name="hidden_deriv",
    )(half.reshape(1), near, far, weight, weight)


def update_kernel(place_ref, grad_ref, weight_ref, momentum_ref, *refs):
    new_weight_ref, new_momentum_ref = refs[-2:]
    grad = grad_ref[...].astype(jnp.float32)
    moment = momentum_ref[0].astype(jnp.float32)
    weight = weight_ref[...].astype(jnp.float32)
    mix = beta_first * moment + (1.0 - beta_first) * grad
    new_weight_ref[0] = weight * (1.0 - step_rate * decay_rate) - step_rate * jnp.tanh(
        mix / sign_width
    )
    new_momentum_ref[0] = (beta_second * moment + (1.0 - beta_second) * grad).astype(
        jnp.bfloat16
    )


def update(source, grad, weight, momentum, done):
    rows, cols = grad.shape
    steps = 3 if rows % 48 == 0 else 1
    some = rows // steps
    own = pl.BlockSpec((some, cols), lambda i, place: (i, 0))
    wide = pl.BlockSpec((1, some, cols), lambda i, place: (0, i, place[0]))
    size = grad.size
    return pl.pallas_call(
        update_kernel,
        grid_spec=pltpu.PrefetchScalarGridSpec(
            num_scalar_prefetch=1,
            grid=(steps,),
            in_specs=[own, own, wide] + [pl.BlockSpec(memory_space=pl.ANY)] * len(done),
            out_specs=[wide, wide],
        ),
        out_shape=[
            jax.ShapeDtypeStruct(momentum.shape, jnp.float32),
            jax.ShapeDtypeStruct(momentum.shape, jnp.bfloat16),
        ],
        input_output_aliases={4 + i: i for i in range(len(done))},
        compiler_params=pltpu.CompilerParams(vmem_limit_bytes=32 * MIB),
        cost_estimate=pl.CostEstimate(flops=10 * size, bytes_accessed=12 * size, transcendentals=size),
        name="lion_step",
    )(source.reshape(1), grad, weight, momentum, *done)


def gathered(keep, give, experts, shards, place, mine):
    bit = shards // 2
    held = in_order(keep[None], swapped(give, "dp", bit)[None], (place & bit) != 0)
    while bit > 2:
        bit //= 2
        held = in_order(held, swapped(held, "dp", bit), (place & bit) != 0)
    groups = {0: held}
    for m in sorted(range(2, experts, 2), key=lambda m: (bin(m).count("1"), -m)):
        groups[m] = swapped(groups[m & (m - 1)], "expert", m & -m)
    if bit > 1:
        for m in groups:
            groups[m] = in_order(groups[m], swapped(groups[m], "dp", 1), (place & 1) != 0)
    for m in list(groups):
        groups[m] = groups[m].reshape(-1, keep.shape[1])
        if experts > 1:
            groups[m + 1] = swapped(groups[m], "expert", 1)
    return groups


def body(out_grad, gate_saved, up_saved, routing, down_weight, momentum):
    experts = lax.axis_size("expert")
    shards = lax.axis_size("dp")
    group_tok, topk, cols = gate_saved.shape
    width = out_grad.shape[1]
    rows = momentum.shape[1]
    mine = lax.axis_index("expert")
    place = lax.axis_index("dp")
    span = shards // 2
    half = place // span
    within = place % span
    each = range(experts)

    low, high = out_grad[:, : width // 2], out_grad[:, width // 2 :]
    near = jnp.where(half == 0, low, high)
    far = jnp.where(half == 0, high, low)
    near_tokens = gathered(near, far, experts, shards, place, mine)
    far_tokens = gathered(far, near, experts, shards, place, mine)

    named = (routing ^ mine).reshape(1, group_tok * topk)
    hidden, *own_rows = picked_rows(
        hidden_kernel,
        [gate_saved.reshape(-1, cols), up_saved.reshape(-1, cols)],
        named,
        experts,
        topk,
        True,
    )
    other_hidden = swapped(hidden, "dp", span)
    own_rows = [swapped(own_rows[m], "expert", m) for m in each]
    other_rows = picked_rows(pick_kernel, [other_hidden], named, experts, topk, False)
    other_rows = [swapped(other_rows[m], "expert", m) for m in each]

    near_list = [near_tokens[m] for m in each]

    def shard_terms(hidden_rows):
        if rows % 128 == 0:
            return [terms(near_list, hidden_rows, rows, within ^ m, 1) for m in range(span)]
        tall = width // 8
        total = terms(near_list, hidden_rows, tall, 0 * within, width // 2 // tall)
        return [
            lax.dynamic_slice_in_dim(total, (within ^ m) * rows, rows, axis=0) for m in range(span)
        ]

    own_terms = shard_terms(own_rows)
    other_terms = shard_terms(other_rows)
    grads = {}
    for m in range(span):
        grads[m] = swapped(own_terms[m], "dp", m)
        grads[m ^ span] = swapped(other_terms[m], "dp", m)

    weight = down_weight[0]
    late_weight = after(weight, other_hidden)
    weights = {}
    for m in range(shards):
        block = lax.dynamic_slice_in_dim(
            weight if m < span else late_weight, (place ^ m) * rows, rows, axis=0
        )
        weights[m] = swapped(block, "dp", m)

    back_weight, gate_saved, up_saved, _ = lax.optimization_barrier(
        (weight, gate_saved, up_saved, own_terms[0])
    )
    gate = gate_saved.astype(jnp.float32)
    up = up_saved.astype(jnp.float32)
    sigma = jax.nn.sigmoid(gate)
    deriv = jnp.zeros(gate.shape, jnp.float32)
    for m in [2 * i + j for j in range(2) for i in range(experts // 2)][::-1]:
        part = deriv_of(near_tokens[m], far_tokens[m], back_weight, half)
        chosen = (routing == (mine ^ m))[:, :, None]
        deriv = jnp.where(chosen, swapped(part, "expert", m)[:, None, :], deriv)
    d_up = (deriv * gate * sigma).astype(jnp.bfloat16)
    d_gate = (deriv * up * sigma * (1.0 + gate * (1.0 - sigma))).astype(jnp.bfloat16)

    done = ()
    for m in range(shards):
        done = update(place ^ m, grads[m], weights[m], momentum, done)
    new_weight, new_momentum = done
    return (d_gate, d_up, new_weight, new_momentum)


def solution(mesh):
    placed = (
        P(("expert", "dp"), None),
        P("expert", None, "dp"),
        P("expert", None, "dp"),
        P("expert", None),
        P("expert", None, "dp"),
        P("expert", "dp", None),
    )
    return jax.shard_map(
        body,
        mesh=mesh,
        in_specs=placed,
        out_specs=(
            P("expert", None, "dp"),
            P("expert", None, "dp"),
            P("expert", "dp", None),
            P("expert", "dp", None),
        ),
        check_vma=False,
    )
```

time: 528 us -> 418 us (0.79)
  blocking collectives: 143 us -> 0 us
  Pallas kernels: 12 us -> 110 us
  matrix products: 67.4 us -> 0 us
  starting transfers between devices: 11.2 us -> 37.6 us
  local copies, waits for them, and re-layouts: 12.2 us -> 35.9 us
  other arithmetic: 36.6 us -> 17.9 us
  waiting for transfers between devices: 229 us -> 211 us
  between operations: 14.2 us -> 1.2 us
    all_to_all x1 -> x0, blocking collectives: 143 us -> none  [body(): lax.all_to_all(term.astype(jnp.bfloat16).reshape(shards, rows, cols), 'dp...]
    pallas_call x1 -> x30, Pallas kernels: 12 us -> 110 us  [the longest x8 27.4 us: terms(): pl.pallas_call(functools.partial(term_kernel, count), grid_spec=pltpu.Pre...]
    dot_general x8 -> x0, matrix products: 67.4 us -> none  [the longest x4 38.4 us: body(): lax.dot_general(tokens[m], rows_of[m], (((0,), (0,)), ((), ())), preferre...]
    all_gather x1 -> x0, waiting for transfers between devices: 63.9 us -> none  [body(): tokens = {0: lax.all_gather(out_grad, 'dp', axis=0, tiled=True)}]
    ppermute x9 -> x37, waiting for transfers between devices: 165 us -> 211 us  [swapped(): return lax.ppermute(array, axis, [(i, i ^ mask) for i in range(size)])]
    ppermute x9 -> x37, starting transfers between devices: 5.32 us -> 37.6 us  [swapped(): return lax.ppermute(array, axis, [(i, i ^ mask) for i in range(size)])]
    reduce_sum x1 -> x0, other arithmetic: 18.4 us -> none  [body(): picked = jnp.sum(jnp.where(chosen, hidden, jnp.zeros_like(hidden)), axis=1)]
    unnamed x26 -> x102, local copies, waits for them, and re-layouts: 2.84 us -> 20.8 us
  transfers between devices with their start and end apart: 11 -> 37, of which waited for: 6 -> 15; matrix products, arithmetic and copies ran while one was open for 22% -> 4% of each run, Pallas kernels for 0% -> 26%
where the time goes in v3:
time: 418 us; the launch traced here: 414 us
  waiting for transfers between devices  211 us (50%)
  Pallas kernels  110 us (26%)
  starting transfers between devices  37.6 us (9%)
  local copies, waits for them, and re-layouts  35.9 us (9%)
  other arithmetic  17.9 us (4%)
    ppermute x37, waiting for transfers between devices, swapped(): return lax.ppermute(array, axis, [(i, i ^ mask) for i in range(size)])  211 us
    ppermute x37, starting transfers between devices, swapped(): return lax.ppermute(array, axis, [(i, i ^ mask) for i in range(size)])  37.6 us
    pallas_call x8, Pallas kernels, terms(): pl.pallas_call(functools.partial(term_kernel, count), grid_spec=pltpu.Pre...  27.4 us
    pallas_call x8, Pallas kernels, update(): pl.pallas_call(update_kernel, grid_spec=pltpu.PrefetchScalarGridSpec(num_...  26.5 us
    pallas_call x4, Pallas kernels, deriv_of(): pl.pallas_call(deriv_kernel, grid_spec=pltpu.PrefetchScalarGridSpec(num_s...  25.4 us
    pallas_call x8, Pallas kernels, in_order(): pl.pallas_call(order_kernel, grid_spec=pltpu.PrefetchScalarGridSpec(num_s...  22.1 us
    unnamed x102, local copies, waits for them, and re-layouts  20.8 us
    convert_element_type x1, other arithmetic, body(): d_up = (deriv * gate * sigma).astype(jnp.bfloat16)  16.2 us
  transfers between devices with their start and end apart: 37, of which 15 were waited for; matrix products, arithmetic and copies ran while one was open for 4% of the time, Pallas kernels for 26%

profile of v3, /device:TPU:8, one launch (start us, length us, event | category | flops | bytes accessed | tf_op | source)
XLA Modules:
  0.0 413.9 jit_solution(9130883021720067143)
XLA Ops:
  0.7 1.7 broadcast_select_fusion
  2.4 2.6 collective-permute-start
  5.0 8.3 %collective-permute-done = bf16[64,1536]{1,0:T(8,128)(2,1)S(1)} collective-permute-done((bf16[64,1536]{1,0:T(8,128)(2,1)S(1)}, bf16[64,1536]{1,0:T(8,128)(2,1)S(1)}, u32[]{:S(2)}, u32[]{:S(2)}) %collective-permute-start) | collective-permute-done | bytes 196640 | tf_op jit(solution)/shard_map/ppermute | solution.py:22
  13.9 1.8 side_by_side.8
  17.0 2.1 collective-permute-start.3
  19.1 3.7 dynamic-slice_bitcast_fusion
  22.7 2.0 collective-permute-start.34
  24.8 8.6 %collective-permute-done.3 = bf16[64,1536]{1,0:T(8,128)(2,1)S(1)} collective-permute-done((bf16[64,1536]{1,0:T(8,128)(2,1)}, bf16[64,1536]{1,0:T(8,128)(2,1)S(1)}, u32[]{:S(2)}, u32[]{:S(2)}) %collective-permute-start.3) | collective-permute-done | bytes 196640 | tf_op jit(solution)/shard_map/ppermute | solution.py:22
  34.1 1.8 side_by_side.11
  36.6 2.0 side_by_side.9
  40.1 3.0 collective-permute-start.32
  43.6 13.8 %collective-permute-done.4.theirs_ref = bf16[2,64,1536]{2,1,0:T(8,128)(2,1)S(1)} collective-permute-done((bf16[2,64,1536]{2,1,0:T(8,128)(2,1)}, bf16[2,64,1536]{2,1,0:T(8,128)(2,1)S(1)}, u32[]{:S(2)}, u32[]{:S(2)}) %collective-permute-start.4) | collective-permute-done | bytes 393248 | tf_op jit(solution)/shard_map/ppermute | solution.py:22
  58.1 2.0 side_by_side.12
  62.0 2.8 reshape.119.gate_ref
  64.7 4.1 reshape.120.up_ref
  68.8 1.6 copy-done.18
  70.4 3.7 hidden_rows.2
  76.1 3.4 collective-permute-start.20
  79.5 1.5 collective-permute-start.8
  82.1 18.2 %collective-permute-done.8.theirs_ref = bf16[4,64,1536]{2,1,0:T(8,128)(2,1)} collective-permute-done((bf16[4,64,1536]{2,1,0:T(8,128)(2,1)}, bf16[4,64,1536]{2,1,0:T(8,128)(2,1)}, u32[]{:S(2)}, u32[]{:S(2)}) %collective-permute-start.8) | collective-permute-done | bytes 786464 | tf_op jit(solution)/shard_map/ppermute | solution.py:22
  100.3 1.5 collective-permute-start.14
  101.8 3.6 side_by_side.10
  105.4 3.6 side_by_side.14
  109.1 8.1 %collective-permute-done.36.weight_ref = bf16[384,1024]{1,0:T(8,128)(2,1)} collective-permute-done((bf16[384,1024]{1,0:T(8,128)(2,1)}, bf16[384,1024]{1,0:T(8,128)(2,1)}, u32[]{:S(2)}, u32[]{:S(2)}) %collective-permute-start.36) | collective-permute-done | bytes 786464 | tf_op jit(solution)/shard_map/ppermute | solution.py:22
  117.9 13.0 %collective-permute-done.14.theirs_ref = bf16[4,64,1536]{2,1,0:T(8,128)(2,1)} collective-permute-done((bf16[4,64,1536]{2,1,0:T(8,128)(2,1)}, bf16[4,64,1536]{2,1,0:T(8,128)(2,1)}, u32[]{:S(2)}, u32[]{:S(2)}) %collective-permute-start.14) | collective-permute-done | bytes 786464 | tf_op jit(solution)/shard_map/ppermute | solution.py:22
  130.9 1.5 collective-permute-start.5
  132.4 3.6 side_by_side.15
  136.1 31.8 %collective-permute-done.20.hidden_ref = bf16[1024,1024]{1,0:T(8,128)(2,1)} collective-permute-done((bf16[1024,1024]{1,0:T(8,128)(2,1)}, bf16[1024,1024]{1,0:T(8,128)(2,1)}, u32[]{:S(2)}, u32[]{:S(2)}) %collective-permute-start.20) | collective-permute-done | bytes 2097184 | tf_op jit(solution)/shard_map/ppermute | solution.py:22
  167.9 3.6 constant_dynamic-slice_fusion
  171.5 3.5 collective-permute-start.30
  174.9 3.7 side_by_side.13
  180.2 4.8 %hidden_rows.3 = (bf16[512,1024]{1,0:T(8,128)(2,1)S(1)}, bf16[512,1024]{1,0:T(8,128)(2,1)}, bf16[512,1024]{1,0:T(8,128)(2,1)}, bf16[512,1024]{1,0:T(8,128)(2,1)}) custom-call(bf16[1024,1024]{1,0:T(8,128)(2,1)} %collective-permute-done.20.hidden_ref, s32[1,1024]{1,0:T(1,128)S(1)} %reshape.121.named_ref), custom_call_target="tpu_custom_call" | custom-call | flops 1073741824 | bytes 8388608 | tf_op jit(solution)/shard_map/hidden_rows/pallas_call | solution.py:88
  185.0 1.6 copy-done.5
  189.0 3.4 group_terms.8.grad_ref
  192.5 48.5 %collective-permute-done.30.weight_ref = bf16[384,1024]{1,0:T(8,128)(2,1)} collective-permute-done((bf16[384,1024]{1,0:T(8,128)(2,1)}, bf16[384,1024]{1,0:T(8,128)(2,1)}, u32[]{:S(2)}, u32[]{:S(2)}) %collective-permute-start.30) | collective-permute-done | bytes 786464 | tf_op jit(solution)/shard_map/ppermute | solution.py:22
  241.0 5.7 %hidden_deriv.5 = f32[512,1024]{1,0:T(8,128)} custom-call(s32[1]{0:T(128)} %bitcast.place_ref, bf16[512,1536]{1,0:T(8,128)(2,1)S(1)} %bitcast.64, bf16[512,1536]{1,0:T(8,128)(2,1)S(1)} %bitcast.75, bf16[3072,1024]{1,0:T(8,128)(2,1)S(1)} %bitcast.40, bf16[3072,1024]{1,0:T(8,128)(2,1)S(1)} %bitcast.41), custom_call_target="tpu_custom_call" | custom-call | flops 3221225472 | bytes 11534336 | tf_op jit(solution)/shard_map/hidden_deriv/pallas_call | solution.py:153
  246.7 11.1 %collective-permute-done.29.weight_ref = bf16[384,1024]{1,0:T(8,128)(2,1)} collective-permute-done((bf16[384,1024]{1,0:T(8,128)(2,1)}, bf16[384,1024]{1,0:T(8,128)(2,1)}, u32[]{:S(2)}, u32[]{:S(2)}) %collective-permute-start.29) | collective-permute-done | bytes 786464 | tf_op jit(solution)/shard_map/ppermute | solution.py:22
  258.4 18.5 %collective-permute-done.27.weight_ref = bf16[384,1024]{1,0:T(8,128)(2,1)} collective-permute-done((bf16[384,1024]{1,0:T(8,128)(2,1)}, bf16[384,1024]{1,0:T(8,128)(2,1)}, u32[]{:S(2)}, u32[]{:S(2)}) %collective-permute-start.27) | collective-permute-done | bytes 786464 | tf_op jit(solution)/shard_map/ppermute | solution.py:22
  276.8 4.2 %group_terms.13 = bf16[384,1024]{1,0:T(8,128)(2,1)} custom-call(s32[1]{0:T(128)} %bitcast.19.place_ref, bf16[512,1536]{1,0:T(8,128)(2,1)S(1)} %bitcast.54, bf16[512,1536]{1,0:T(8,128)(2,1)} %collective-permute-done.6.refs_1_.near_ref, bf16[512,1536]{1,0:T(8,128)(2,1)S(1)} %bitcast.65, bf16[512,1536]{1,0:T(8,128)(2,1)} %collective-permute-done.9.refs_3_.near_ref, ...), custom_call_target="tpu_custom_call" | custom-call | flops 1610612736 | bytes 6553600 | tf_op jit(solution)/shard_map/group_terms/pallas_call | solution.py:122
  281.1 3.3 group_terms.14
  284.4 7.4 %hidden_deriv.7 = f32[512,1024]{1,0:T(8,128)} custom-call(s32[1]{0:T(128)} %bitcast.place_ref, bf16[512,1536]{1,0:T(8,128)(2,1)} %collective-permute-done.9.refs_3_.near_ref, bf16[512,1536]{1,0:T(8,128)(2,1)} %collective-permute-done.18.far_ref, bf16[3072,1024]{1,0:T(8,128)(2,1)S(1)} %bitcast.42, bf16[3072,1024]{1,0:T(8,128)(2,1)S(1)} %bitcast.43), custom_call_target="tpu_custom_call" | custom-call | flops 3221225472 | bytes 11534336 | tf_op jit(solution)/shard_map/hidden_deriv/pallas_call | solution.py:153
  291.7 3.0 collective-permute-start.33
  294.7 3.3 group_terms.15
  298.6 7.3 %hidden_deriv.6 = f32[512,1024]{1,0:T(8,128)} custom-call(s32[1]{0:T(128)} %bitcast.place_ref, bf16[512,1536]{1,0:T(8,128)(2,1)} %collective-permute-done.6.refs_1_.near_ref, bf16[512,1536]{1,0:T(8,128)(2,1)} %collective-permute-done.16.far_ref, bf16[3072,1024]{1,0:T(8,128)(2,1)S(1)} %bitcast.44, bf16[3072,1024]{1,0:T(8,128)(2,1)S(1)} %bitcast.45), custom_call_target="tpu_custom_call" | custom-call | flops 3221225472 | bytes 11534336 | tf_op jit(solution)/shard_map/hidden_deriv/pallas_call | solution.py:153
  308.1 3.0 group_terms.10
  311.1 8.1 %collective-permute-done.33.grad_ref = bf16[384,1024]{1,0:T(8,128)(2,1)S(1)} collective-permute-done((bf16[384,1024]{1,0:T(8,128)(2,1)S(1)}, bf16[384,1024]{1,0:T(8,128)(2,1)S(1)}, u32[]{:S(2)}, u32[]{:S(2)}) %collective-permute-start.33) | collective-permute-done | bytes 786464 | tf_op jit(solution)/shard_map/ppermute | solution.py:22
  319.2 3.2 group_terms.11
  323.1 3.9 group_terms.9
  327.0 11.6 %collective-permute-done.26.grad_ref = bf16[384,1024]{1,0:T(8,128)(2,1)S(1)} collective-permute-done((bf16[384,1024]{1,0:T(8,128)(2,1)S(1)}, bf16[384,1024]{1,0:T(8,128)(2,1)S(1)}, u32[]{:S(2)}, u32[]{:S(2)}) %collective-permute-start.26) | collective-permute-done | bytes 786464 | tf_op jit(solution)/shard_map/ppermute | solution.py:22
  339.5 2.3 collective-permute-done.28.grad_ref
  345.0 2.8 copy-done
  350.0 2.2 lion_step.8
  354.3 3.1 group_terms.12.grad_ref
  358.8 4.9 %hidden_deriv.4 = f32[512,1024]{1,0:T(8,128)S(1)} custom-call(s32[1]{0:T(128)} %bitcast.place_ref, bf16[512,1536]{1,0:T(8,128)(2,1)S(1)} %bitcast.61, bf16[512,1536]{1,0:T(8,128)(2,1)S(1)} %bitcast.73, bf16[3072,1024]{1,0:T(8,128)(2,1)S(1)} %bitcast.48, bf16[3072,1024]{1,0:T(8,128)(2,1)S(1)} %bitcast.49), custom_call_target="tpu_custom_call" | custom-call | flops 3221225472 | bytes 11534336 | tf_op jit(solution)/shard_map/hidden_deriv/pallas_call | solution.py:153
  363.8 3.6 lion_step.9
  367.5 2.2 lion_step.10
  369.7 3.5 lion_step.11
  373.2 3.6 lion_step.12
  376.8 3.6 lion_step.13
  380.4 3.5 lion_step.14
  383.9 6.7 %collective-permute-done.25.weight_ref = bf16[384,1024]{1,0:T(8,128)(2,1)} collective-permute-done((bf16[384,1024]{1,0:T(8,128)(2,1)}, bf16[384,1024]{1,0:T(8,128)(2,1)}, u32[]{:S(2)}, u32[]{:S(2)}) %collective-permute-start.25) | collective-permute-done | bytes 786464 | tf_op jit(solution)/shard_map/ppermute | solution.py:22
  390.6 4.2 %lion_step.15 = (f32[1,384,8192]{2,1,0:T(8,128)}, bf16[1,384,8192]{2,1,0:T(8,128)(2,1)}) custom-call(s32[1]{0:T(128)} %bitcast.18.place_ref, bf16[384,1024]{1,0:T(8,128)(2,1)} %collective-permute-done.24.grad_ref, bf16[384,1024]{1,0:T(8,128)(2,1)} %collective-permute-done.25.weight_ref, ...), custom_call_target="tpu_custom_call", output_to_operand_aliasing={{0}: (4, {}), {1}: (5, {})} | custom-call | flops 3932160 | bytes 4718592 | tf_op jit(solution)/shard_map/lion_step/pallas_call | solution.py:198
  394.9 2.7 collective-permute-done.19
  397.6 16.2 %fusion.7 = (bf16[512,2,1024]{2,1,0:T(2,128)(2,1)}, bf16[512,2,1024]{2,1,0:T(2,128)(2,1)}) fusion(bf16[512,2,1024]{2,1,0:T(2,128)(2,1)S(1)} %copy-done.37, pred[512,2]{1,0:T(8,128)(4,1)S(1)} %copy.33, pred[512,2]{1,0:T(8,128)(4,1)S(1)} %copy.32, pred[512,2]{1,0:T(8,128)(4,1)S(1)} %copy.31, pred[512,2]{1,0:T(8,128)(4,1)S(1)} %copy.29, ...), kind=kLoop, calls=%fused_computation.10 | loop fusion | flops 19922944 | bytes 16781312 | tf_op jit(solution)/shard_map/convert_element_type | solution.py:307
  (159 shorter events, 29.5 us)
Async XLA Ops:
  2.4 31.0 %copy-start.39 = (bf16[64,1536]{1,0:T(8,128)(2,1)}, bf16[64,1536]{1,0:T(8,128)(2,1)S(1)}, u32[]{:S(2)}) copy-start(bf16[64,1536]{1,0:T(8,128)(2,1)S(1)} %get-tuple-element.72) | copy-start | bytes 589828
  2.4 10.8 %collective-permute-start = (bf16[64,1536]{1,0:T(8,128)(2,1)S(1)}, bf16[64,1536]{1,0:T(8,128)(2,1)S(1)}, u32[]{:S(2)}, u32[]{:S(2)}) collective-permute-start(bf16[64,1536]{1,0:T(8,128)(2,1)S(1)} %get-tuple-element.72), channel_id=1, source_target_pairs={{0,4},{1,5},{2,6},{3,7},{4,0},{5,1},{6,2},{7,3},{8,12},{9,13},{10,... | collective-permute-start | bytes 589832 | tf_op jit(solution)/shard_map/ppermute | solution.py:22
  15.7 20.2 %collective-permute-start.1 = (bf16[2,64,1536]{2,1,0:T(8,128)(2,1)}, bf16[2,64,1536]{2,1,0:T(8,128)(2,1)S(1)}, u32[]{:S(2)}, u32[]{:S(2)}) collective-permute-start(bf16[2,64,1536]{2,1,0:T(8,128)(2,1)} %bitcast.82), channel_id=1, source_target_pairs={{0,2},{1,3},{2,0},{3,1},{4,6},{5,7},{6,4},{7,5},{8,10},{9,11},{10,... | collective-permute-start | bytes 1179656 | tf_op jit(solution)/shard_map/ppermute | solution.py:22
  17.0 16.4 %collective-permute-start.3 = (bf16[64,1536]{1,0:T(8,128)(2,1)}, bf16[64,1536]{1,0:T(8,128)(2,1)S(1)}, u32[]{:S(2)}, u32[]{:S(2)}) collective-permute-start(bf16[64,1536]{1,0:T(8,128)(2,1)} %get-tuple-element.73), channel_id=1, source_target_pairs={{0,4},{1,5},{2,6},{3,7},{4,0},{5,1},{6,2},{7,3},{8,12},{9,13},{10,... | collective-permute-start | bytes 589832 | tf_op jit(solution)/shard_map/ppermute | solution.py:22
  19.1 42.5 %copy-start.44 = (s32[512,2]{0,1:T(2,128)S(1)}, s32[512,2]{0,1:T(2,128)}, u32[]{:S(2)}) copy-start(s32[512,2]{0,1:T(2,128)} %param.9) | copy-start | bytes 12292
  22.7 53.4 %collective-permute-start.34 = (bf16[384,1024]{1,0:T(8,128)(2,1)}, bf16[384,1024]{1,0:T(8,128)(2,1)S(1)}, u32[]{:S(2)}, u32[]{:S(2)}) collective-permute-start(bf16[384,1024]{1,0:T(8,128)(2,1)} %get-tuple-element.65), channel_id=1, source_target_pairs={{0,2},{1,3},{2,0},{3,1},{4,6},{5,7},{6,4},{7,5},{8,10},{9,11},{10,... | collective-permute-start | bytes 2359304 | tf_op jit(solution)/shard_map/ppermute | solution.py:22
  35.9 21.5 %collective-permute-start.4 = (bf16[2,64,1536]{2,1,0:T(8,128)(2,1)}, bf16[2,64,1536]{2,1,0:T(8,128)(2,1)S(1)}, u32[]{:S(2)}, u32[]{:S(2)}) collective-permute-start(bf16[2,64,1536]{2,1,0:T(8,128)(2,1)} %bitcast.84), channel_id=1, source_target_pairs={{0,2},{1,3},{2,0},{3,1},{4,6},{5,7},{6,4},{7,5},{8,10},{9,11},{10,... | collective-permute-start | bytes 1179656 | tf_op jit(solution)/shard_map/ppermute | solution.py:22
  38.6 40.9 %collective-permute-start.7 = (bf16[4,64,1536]{2,1,0:T(8,128)(2,1)}, bf16[4,64,1536]{2,1,0:T(8,128)(2,1)}, u32[]{:S(2)}, u32[]{:S(2)}) collective-permute-start(bf16[4,64,1536]{2,1,0:T(8,128)(2,1)} %bitcast.79), channel_id=1, source_target_pairs={{0,16},{8,24},{16,0},{24,8},{1,17},{9,25},{17,1},{25,9},{2,18},{10... | collective-permute-start | bytes 2359304 | tf_op jit(solution)/shard_map/ppermute | solution.py:22
  40.1 40.9 %collective-permute-start.32 = (bf16[384,1024]{1,0:T(8,128)(2,1)}, bf16[384,1024]{1,0:T(8,128)(2,1)}, u32[]{:S(2)}, u32[]{:S(2)}) collective-permute-start(bf16[384,1024]{1,0:T(8,128)(2,1)} %get-tuple-element.66), channel_id=1, source_target_pairs={{0,3},{1,2},{2,1},{3,0},{4,7},{5,6},{6,5},{7,4},{8,11},{9,10},{10,... | collective-permute-start | bytes 2359304 | tf_op jit(solution)/shard_map/ppermute | solution.py:22
  43.1 37.9 %collective-permute-start.2 = (bf16[4,64,1536]{2,1,0:T(8,128)(2,1)}, bf16[4,64,1536]{2,1,0:T(8,128)(2,1)}, u32[]{:S(2)}, u32[]{:S(2)}) collective-permute-start(bf16[4,64,1536]{2,1,0:T(8,128)(2,1)} %bitcast.80), channel_id=1, source_target_pairs={{0,1},{1,0},{2,3},{3,2},{4,5},{5,4},{6,7},{7,6},{8,9},{9,8},{10,11... | collective-permute-start | bytes 2359304 | tf_op jit(solution)/shard_map/ppermute | solution.py:22
  60.1 21.5 %collective-permute-start.13 = (bf16[4,64,1536]{2,1,0:T(8,128)(2,1)}, bf16[4,64,1536]{2,1,0:T(8,128)(2,1)}, u32[]{:S(2)}, u32[]{:S(2)}) collective-permute-start(bf16[4,64,1536]{2,1,0:T(8,128)(2,1)} %bitcast.76), channel_id=1, source_target_pairs={{0,16},{8,24},{16,0},{24,8},{1,17},{9,25},{17,1},{25,9},{2,18},{10... | collective-permute-start | bytes 2359304 | tf_op jit(solution)/shard_map/ppermute | solution.py:22
  76.1 59.9 %copy-start.24 = (bf16[384,1024]{1,0:T(8,128)(2,1)}, bf16[384,1024]{1,0:T(8,128)(2,1)S(1)}, u32[]{:S(2)}) copy-start(bf16[384,1024]{1,0:T(8,128)(2,1)S(1)} %collective-permute-done.34.weight_ref) | copy-start | bytes 2359300
  76.1 91.8 %collective-permute-start.20 = (bf16[1024,1024]{1,0:T(8,128)(2,1)}, bf16[1024,1024]{1,0:T(8,128)(2,1)}, u32[]{:S(2)}, u32[]{:S(2)}) collective-permute-start(bf16[1024,1024]{1,0:T(8,128)(2,1)} %get-tuple-element.40), channel_id=1, source_target_pairs={{0,4},{1,5},{2,6},{3,7},{4,0},{5,1},{6,2},{7,3},{8,12},{9,13},{10,... | collective-permute-start | bytes 6291464 | tf_op jit(solution)/shard_map/ppermute | solution.py:22
  79.5 20.8 %collective-permute-start.8 = (bf16[4,64,1536]{2,1,0:T(8,128)(2,1)}, bf16[4,64,1536]{2,1,0:T(8,128)(2,1)}, u32[]{:S(2)}, u32[]{:S(2)}) collective-permute-start(bf16[4,64,1536]{2,1,0:T(8,128)(2,1)} %collective-permute-done.7.mine_ref), channel_id=1, source_target_pairs={{0,1},{1,0},{2,3},{3,2},{4,5},{5,4},{6,7},{7,6},{8,9},{9,8},{10,11... | collective-permute-start | bytes 2359304 | tf_op jit(solution)/shard_map/ppermute | solution.py:22
  81.0 36.1 %collective-permute-start.10 = (bf16[512,1024]{1,0:T(8,128)(2,1)}, bf16[512,1024]{1,0:T(8,128)(2,1)S(1)}, u32[]{:S(2)}, u32[]{:S(2)}) collective-permute-start(bf16[512,1024]{1,0:T(8,128)(2,1)} %get-tuple-element.34), channel_id=1, source_target_pairs={{0,8},{8,0},{16,24},{24,16},{1,9},{9,1},{17,25},{25,17},{2,10},{10... | collective-permute-start | bytes 3145736 | tf_op jit(solution)/shard_map/ppermute | solution.py:22
  81.0 36.1 %collective-permute-start.36 = (bf16[384,1024]{1,0:T(8,128)(2,1)}, bf16[384,1024]{1,0:T(8,128)(2,1)}, u32[]{:S(2)}, u32[]{:S(2)}) collective-permute-start(bf16[384,1024]{1,0:T(8,128)(2,1)} %get-tuple-element.67), channel_id=1, source_target_pairs={{0,1},{1,0},{2,3},{3,2},{4,5},{5,4},{6,7},{7,6},{8,9},{9,8},{10,11... | collective-permute-start | bytes 2359304 | tf_op jit(solution)/shard_map/ppermute | solution.py:22
  81.6 36.1 %collective-permute-start.11 = (bf16[512,1024]{1,0:T(8,128)(2,1)}, bf16[512,1024]{1,0:T(8,128)(2,1)S(1)}, u32[]{:S(2)}, u32[]{:S(2)}) collective-permute-start(bf16[512,1024]{1,0:T(8,128)(2,1)} %get-tuple-element.35), channel_id=1, source_target_pairs={{0,16},{8,24},{16,0},{24,8},{1,17},{9,25},{17,1},{25,9},{2,18},{10... | collective-permute-start | bytes 3145736 | tf_op jit(solution)/shard_map/ppermute | solution.py:22
  100.3 30.6 %collective-permute-start.14 = (bf16[4,64,1536]{2,1,0:T(8,128)(2,1)}, bf16[4,64,1536]{2,1,0:T(8,128)(2,1)}, u32[]{:S(2)}, u32[]{:S(2)}) collective-permute-start(bf16[4,64,1536]{2,1,0:T(8,128)(2,1)} %collective-permute-done.13.mine_ref), channel_id=1, source_target_pairs={{0,1},{1,0},{2,3},{3,2},{4,5},{5,4},{6,7},{7,6},{8,9},{9,8},{10,11... | collective-permute-start | bytes 2359304 | tf_op jit(solution)/shard_map/ppermute | solution.py:22
  117.2 61.7 %collective-permute-start.6 = (bf16[512,1536]{1,0:T(8,128)(2,1)}, bf16[512,1536]{1,0:T(8,128)(2,1)}, u32[]{:S(2)}, u32[]{:S(2)}) collective-permute-start(bf16[512,1536]{1,0:T(8,128)(2,1)} %bitcast.52), channel_id=1, source_target_pairs={{0,8},{8,0},{16,24},{24,16},{1,9},{9,1},{17,25},{25,17},{2,10},{10... | collective-permute-start | bytes 4718600 | tf_op jit(solution)/shard_map/ppermute | solution.py:22
  117.2 50.7 %copy-start.6 = (bf16[512,1024]{1,0:T(8,128)(2,1)}, bf16[512,1024]{1,0:T(8,128)(2,1)S(1)}, u32[]{:S(2)}) copy-start(bf16[512,1024]{1,0:T(8,128)(2,1)S(1)} %collective-permute-done.10.refs_5_) | copy-start | bytes 3145732
  117.2 63.0 %collective-permute-start.9 = (bf16[512,1536]{1,0:T(8,128)(2,1)}, bf16[512,1536]{1,0:T(8,128)(2,1)}, u32[]{:S(2)}, u32[]{:S(2)}) collective-permute-start(bf16[512,1536]{1,0:T(8,128)(2,1)} %bitcast.62), channel_id=1, source_target_pairs={{0,8},{8,0},{16,24},{24,16},{1,9},{9,1},{17,25},{25,17},{2,10},{10... | collective-permute-start | bytes 4718600 | tf_op jit(solution)/shard_map/ppermute | solution.py:22
  117.7 50.2 %copy-start.8 = (bf16[512,1024]{1,0:T(8,128)(2,1)}, bf16[512,1024]{1,0:T(8,128)(2,1)S(1)}, u32[]{:S(2)}) copy-start(bf16[512,1024]{1,0:T(8,128)(2,1)S(1)} %collective-permute-done.11.refs_6_) | copy-start | bytes 3145732
  117.7 60.9 %collective-permute-start.12 = (bf16[512,1024]{1,0:T(8,128)(2,1)}, bf16[512,1024]{1,0:T(8,128)(2,1)}, u32[]{:S(2)}, u32[]{:S(2)}) collective-permute-start(bf16[512,1024]{1,0:T(8,128)(2,1)} %copy-done.36), channel_id=1, source_target_pairs={{0,24},{8,16},{16,8},{24,0},{1,25},{9,17},{17,9},{25,1},{2,26},{10... | collective-permute-start | bytes 3145736 | tf_op jit(solution)/shard_map/ppermute | solution.py:22
  130.9 40.5 %collective-permute-start.5 = (bf16[4,64,1536]{2,1,0:T(8,128)(2,1)}, bf16[4,64,1536]{2,1,0:T(8,128)(2,1)}, u32[]{:S(2)}, u32[]{:S(2)}) collective-permute-start(bf16[4,64,1536]{2,1,0:T(8,128)(2,1)} %bitcast.77), channel_id=1, source_target_pairs={{0,1},{1,0},{2,3},{3,2},{4,5},{5,4},{6,7},{7,6},{8,9},{9,8},{10,11... | collective-permute-start | bytes 2359304 | tf_op jit(solution)/shard_map/ppermute | solution.py:22
  167.9 113.2 %collective-permute-start.18 = (bf16[512,1536]{1,0:T(8,128)(2,1)}, bf16[512,1536]{1,0:T(8,128)(2,1)}, u32[]{:S(2)}, u32[]{:S(2)}) collective-permute-start(bf16[512,1536]{1,0:T(8,128)(2,1)} %bitcast.74), channel_id=1, source_target_pairs={{0,8},{8,0},{16,24},{24,16},{1,9},{9,1},{17,25},{25,17},{2,10},{10... | collective-permute-start | bytes 4718600 | tf_op jit(solution)/shard_map/ppermute | solution.py:22
  171.5 13.5 %copy-start.1 = (bf16[4,2,64,1536]{3,2,1,0:T(8,128)(2,1)S(1)}, bf16[4,2,64,1536]{3,2,1,0:T(8,128)(2,1)}, u32[]{:S(2)}) copy-start(bf16[4,2,64,1536]{3,2,1,0:T(8,128)(2,1)} %side_by_side.10) | copy-start | bytes 4718596
  171.5 13.5 %copy-start.3 = (bf16[4,2,64,1536]{3,2,1,0:T(8,128)(2,1)S(1)}, bf16[4,2,64,1536]{3,2,1,0:T(8,128)(2,1)}, u32[]{:S(2)}) copy-start(bf16[4,2,64,1536]{3,2,1,0:T(8,128)(2,1)} %side_by_side.14) | copy-start | bytes 4718596
  171.5 69.5 %collective-permute-start.30 = (bf16[384,1024]{1,0:T(8,128)(2,1)}, bf16[384,1024]{1,0:T(8,128)(2,1)}, u32[]{:S(2)}, u32[]{:S(2)}) collective-permute-start(bf16[384,1024]{1,0:T(8,128)(2,1)} %get-tuple-element.68), channel_id=1, source_target_pairs={{0,4},{1,5},{2,6},{3,7},{4,0},{5,1},{6,2},{7,3},{8,12},{9,13},{10,... | collective-permute-start | bytes 2359304 | tf_op jit(solution)/shard_map/ppermute | solution.py:22
  178.6 113.1 %collective-permute-start.16 = (bf16[512,1536]{1,0:T(8,128)(2,1)}, bf16[512,1536]{1,0:T(8,128)(2,1)}, u32[]{:S(2)}, u32[]{:S(2)}) collective-permute-start(bf16[512,1536]{1,0:T(8,128)(2,1)} %bitcast.72), channel_id=1, source_target_pairs={{0,8},{8,0},{16,24},{24,16},{1,9},{9,1},{17,25},{25,17},{2,10},{10... | collective-permute-start | bytes 4718600 | tf_op jit(solution)/shard_map/ppermute | solution.py:22
  178.8 79.0 %collective-permute-start.29 = (bf16[384,1024]{1,0:T(8,128)(2,1)}, bf16[384,1024]{1,0:T(8,128)(2,1)}, u32[]{:S(2)}, u32[]{:S(2)}) collective-permute-start(bf16[384,1024]{1,0:T(8,128)(2,1)} %get-tuple-element.69), channel_id=1, source_target_pairs={{0,5},{1,4},{2,7},{3,6},{4,1},{5,0},{6,3},{7,2},{8,13},{9,12},{10,... | collective-permute-start | bytes 2359304 | tf_op jit(solution)/shard_map/ppermute | solution.py:22
  180.1 96.7 %collective-permute-start.27 = (bf16[384,1024]{1,0:T(8,128)(2,1)}, bf16[384,1024]{1,0:T(8,128)(2,1)}, u32[]{:S(2)}, u32[]{:S(2)}) collective-permute-start(bf16[384,1024]{1,0:T(8,128)(2,1)} %get-tuple-element.70), channel_id=1, source_target_pairs={{0,6},{1,7},{2,4},{3,5},{4,2},{5,3},{6,0},{7,1},{8,14},{9,15},{10,... | collective-permute-start | bytes 2359304 | tf_op jit(solution)/shard_map/ppermute | solution.py:22
  180.1 60.9 %slice-start = ((s8[6291456]{0:T(1024)(128)(4,1)}), s8[4194304]{0:T(1024)(128)(4,1)S(1)}, s32[]{:S(2)}) async-start(s8[6291456]{0:T(1024)(128)(4,1)} %bitcast.38), calls=%async_computation | async-start | bytes 8388608
  185.0 138.1 %copy-start.10 = (bf16[512,1024]{1,0:T(8,128)(2,1)}, bf16[512,1024]{1,0:T(8,128)(2,1)S(1)}, u32[]{:S(2)}) copy-start(bf16[512,1024]{1,0:T(8,128)(2,1)S(1)} %get-tuple-element.41.refs_4_) | copy-start | bytes 3145732
  189.0 52.0 %slice-start.1 = ((s8[6291456]{0:T(1024)(128)(4,1)}), s8[2097152]{0:T(1024)(128)(4,1)S(1)}, s32[]{:S(2)}) async-start(s8[6291456]{0:T(1024)(128)(4,1)} %bitcast.38), calls=%async_computation.1 | async-start | bytes 4194304
  189.0 52.0 %copy-start.20 = (bf16[4,2,64,1536]{3,2,1,0:T(8,128)(2,1)S(1)}, bf16[4,2,64,1536]{3,2,1,0:T(8,128)(2,1)}, u32[]{:S(2)}) copy-start(bf16[4,2,64,1536]{3,2,1,0:T(8,128)(2,1)} %side_by_side.15) | copy-start | bytes 4718596
  192.5 54.3 %copy-start.21 = (bf16[384,1024]{1,0:T(8,128)(2,1)}, bf16[384,1024]{1,0:T(8,128)(2,1)S(1)}, u32[]{:S(2)}) copy-start(bf16[384,1024]{1,0:T(8,128)(2,1)S(1)} %group_terms.8.grad_ref) | copy-start | bytes 2359300
  241.0 57.1 %collective-permute-start.21 = (bf16[512,1024]{1,0:T(8,128)(2,1)}, bf16[512,1024]{1,0:T(8,128)(2,1)S(1)}, u32[]{:S(2)}, u32[]{:S(2)}) collective-permute-start(bf16[512,1024]{1,0:T(8,128)(2,1)} %get-tuple-element.42), channel_id=1, source_target_pairs={{0,8},{8,0},{16,24},{24,16},{1,9},{9,1},{17,25},{25,17},{2,10},{10... | collective-permute-start | bytes 3145736 | tf_op jit(solution)/shard_map/ppermute | solution.py:22
  257.8 48.1 %collective-permute-start.22 = (bf16[512,1024]{1,0:T(8,128)(2,1)}, bf16[512,1024]{1,0:T(8,128)(2,1)S(1)}, u32[]{:S(2)}, u32[]{:S(2)}) collective-permute-start(bf16[512,1024]{1,0:T(8,128)(2,1)} %get-tuple-element.43), channel_id=1, source_target_pairs={{0,16},{8,24},{16,0},{24,8},{1,17},{9,25},{17,1},{25,9},{2,18},{10... | collective-permute-start | bytes 3145736 | tf_op jit(solution)/shard_map/ppermute | solution.py:22
  276.8 30.5 %collective-permute-start.23 = (bf16[512,1024]{1,0:T(8,128)(2,1)}, bf16[512,1024]{1,0:T(8,128)(2,1)S(1)}, u32[]{:S(2)}, u32[]{:S(2)}) collective-permute-start(bf16[512,1024]{1,0:T(8,128)(2,1)} %get-tuple-element.44), channel_id=1, source_target_pairs={{0,24},{8,16},{16,8},{24,0},{1,25},{9,17},{17,9},{25,1},{2,26},{10... | collective-permute-start | bytes 3145736 | tf_op jit(solution)/shard_map/ppermute | solution.py:22
  281.1 26.3 %collective-permute-start.31 = (bf16[384,1024]{1,0:T(8,128)(2,1)}, bf16[384,1024]{1,0:T(8,128)(2,1)S(1)}, u32[]{:S(2)}, u32[]{:S(2)}) collective-permute-start(bf16[384,1024]{1,0:T(8,128)(2,1)} %group_terms.13), channel_id=1, source_target_pairs={{0,3},{1,2},{2,1},{3,0},{4,7},{5,6},{6,5},{7,4},{8,11},{9,10},{10,... | collective-permute-start | bytes 2359304 | tf_op jit(solution)/shard_map/ppermute | solution.py:22
  291.7 27.5 %collective-permute-start.33 = (bf16[384,1024]{1,0:T(8,128)(2,1)S(1)}, bf16[384,1024]{1,0:T(8,128)(2,1)S(1)}, u32[]{:S(2)}, u32[]{:S(2)}) collective-permute-start(bf16[384,1024]{1,0:T(8,128)(2,1)S(1)} %group_terms.14), channel_id=1, source_target_pairs={{0,2},{1,3},{2,0},{3,1},{4,6},{5,7},{6,4},{7,5},{8,10},{9,11},{10,... | collective-permute-start | bytes 2359304 | tf_op jit(solution)/shard_map/ppermute | solution.py:22
  298.1 25.0 %copy-start.12 = (bf16[512,1024]{1,0:T(8,128)(2,1)}, bf16[512,1024]{1,0:T(8,128)(2,1)S(1)}, u32[]{:S(2)}) copy-start(bf16[512,1024]{1,0:T(8,128)(2,1)S(1)} %collective-permute-done.21.refs_5_) | copy-start | bytes 3145732
  298.1 24.4 %collective-permute-start.35 = (bf16[384,1024]{1,0:T(8,128)(2,1)S(1)}, bf16[384,1024]{1,0:T(8,128)(2,1)S(1)}, u32[]{:S(2)}, u32[]{:S(2)}) collective-permute-start(bf16[384,1024]{1,0:T(8,128)(2,1)S(1)} %group_terms.15), channel_id=1, source_target_pairs={{0,1},{1,0},{2,3},{3,2},{4,5},{5,4},{6,7},{7,6},{8,9},{9,8},{10,11... | collective-permute-start | bytes 2359304 | tf_op jit(solution)/shard_map/ppermute | solution.py:22
  306.0 17.1 %copy-start.14 = (bf16[512,1024]{1,0:T(8,128)(2,1)}, bf16[512,1024]{1,0:T(8,128)(2,1)S(1)}, u32[]{:S(2)}) copy-start(bf16[512,1024]{1,0:T(8,128)(2,1)S(1)} %collective-permute-done.22.refs_6_) | copy-start | bytes 3145732
  306.0 88.9 %collective-permute-start.15 = (f32[512,1024]{1,0:T(8,128)}, f32[512,1024]{1,0:T(8,128)}, u32[]{:S(2)}, u32[]{:S(2)}) collective-permute-start(f32[512,1024]{1,0:T(8,128)} %hidden_deriv.5), channel_id=1, source_target_pairs={{0,16},{8,24},{16,0},{24,8},{1,17},{9,25},{17,1},{25,9},{2,18},{10... | collective-permute-start | bytes 6291464 | tf_op jit(solution)/shard_map/ppermute | solution.py:22
  307.3 15.8 %copy-start.16 = (bf16[512,1024]{1,0:T(8,128)(2,1)}, bf16[512,1024]{1,0:T(8,128)(2,1)S(1)}, u32[]{:S(2)}) copy-start(bf16[512,1024]{1,0:T(8,128)(2,1)S(1)} %collective-permute-done.23.refs_7_) | copy-start | bytes 3145732
  307.3 87.6 %collective-permute-start.17 = (f32[512,1024]{1,0:T(8,128)}, f32[512,1024]{1,0:T(8,128)}, u32[]{:S(2)}, u32[]{:S(2)}) collective-permute-start(f32[512,1024]{1,0:T(8,128)} %hidden_deriv.6), channel_id=1, source_target_pairs={{0,8},{8,0},{16,24},{24,16},{1,9},{9,1},{17,25},{25,17},{2,10},{10... | collective-permute-start | bytes 6291464 | tf_op jit(solution)/shard_map/ppermute | solution.py:22
  307.3 3.8 copy-start.26
  307.3 90.2 %collective-permute-start.19 = (f32[512,1024]{1,0:T(8,128)}, f32[512,1024]{1,0:T(8,128)}, u32[]{:S(2)}, u32[]{:S(2)}) collective-permute-start(f32[512,1024]{1,0:T(8,128)} %hidden_deriv.7), channel_id=1, source_target_pairs={{0,24},{8,16},{16,8},{24,0},{1,25},{9,17},{17,9},{25,1},{2,26},{10... | collective-permute-start | bytes 6291464 | tf_op jit(solution)/shard_map/ppermute | solution.py:22
  319.2 19.3 %collective-permute-start.26 = (bf16[384,1024]{1,0:T(8,128)(2,1)S(1)}, bf16[384,1024]{1,0:T(8,128)(2,1)S(1)}, u32[]{:S(2)}, u32[]{:S(2)}) collective-permute-start(bf16[384,1024]{1,0:T(8,128)(2,1)S(1)} %group_terms.10), channel_id=1, source_target_pairs={{0,2},{1,3},{2,0},{3,1},{4,6},{5,7},{6,4},{7,5},{8,10},{9,11},{10,... | collective-permute-start | bytes 2359304 | tf_op jit(solution)/shard_map/ppermute | solution.py:22
  322.5 4.5 %copy-start.32 = (bf16[384,1024]{1,0:T(8,128)(2,1)}, bf16[384,1024]{1,0:T(8,128)(2,1)S(1)}, u32[]{:S(2)}) copy-start(bf16[384,1024]{1,0:T(8,128)(2,1)S(1)} %collective-permute-done.35.grad_ref) | copy-start | bytes 2359300
  322.5 19.4 %collective-permute-start.28 = (bf16[384,1024]{1,0:T(8,128)(2,1)S(1)}, bf16[384,1024]{1,0:T(8,128)(2,1)S(1)}, u32[]{:S(2)}, u32[]{:S(2)}) collective-permute-start(bf16[384,1024]{1,0:T(8,128)(2,1)S(1)} %group_terms.11), channel_id=1, source_target_pairs={{0,1},{1,0},{2,3},{3,2},{4,5},{5,4},{6,7},{7,6},{8,9},{9,8},{10,11... | collective-permute-start | bytes 2359304 | tf_op jit(solution)/shard_map/ppermute | solution.py:22
  339.5 51.2 %collective-permute-start.25 = (bf16[384,1024]{1,0:T(8,128)(2,1)}, bf16[384,1024]{1,0:T(8,128)(2,1)}, u32[]{:S(2)}, u32[]{:S(2)}) collective-permute-start(bf16[384,1024]{1,0:T(8,128)(2,1)} %get-tuple-element.71), channel_id=1, source_target_pairs={{0,7},{1,6},{2,5},{3,4},{4,3},{5,2},{6,1},{7,0},{8,15},{9,14},{10,... | collective-permute-start | bytes 2359304 | tf_op jit(solution)/shard_map/ppermute | solution.py:22
  342.8 47.9 %collective-permute-start.24 = (bf16[384,1024]{1,0:T(8,128)(2,1)}, bf16[384,1024]{1,0:T(8,128)(2,1)}, u32[]{:S(2)}, u32[]{:S(2)}) collective-permute-start(bf16[384,1024]{1,0:T(8,128)(2,1)} %group_terms.9), channel_id=1, source_target_pairs={{0,3},{1,2},{2,1},{3,0},{4,7},{5,6},{6,5},{7,4},{8,11},{9,10},{10,... | collective-permute-start | bytes 2359304 | tf_op jit(solution)/shard_map/ppermute | solution.py:22
  350.0 7.3 %slice-start.2 = ((s8[6291456]{0:T(1024)(128)(4,1)}), s8[4194304]{0:T(1024)(128)(4,1)S(1)}, s32[]{:S(2)}) async-start(s8[6291456]{0:T(1024)(128)(4,1)} %bitcast.46), calls=%async_computation.2 | async-start | bytes 8388608
  354.2 9.5 %slice-start.4 = ((s8[6291456]{0:T(1024)(128)(4,1)}), s8[4194304]{0:T(1024)(128)(4,1)S(1)}, s32[]{:S(2)}) async-start(s8[6291456]{0:T(1024)(128)(4,1)} %bitcast.50), calls=%async_computation.4 | async-start | bytes 8388608
  358.8 5.0 %slice-start.5 = ((s8[6291456]{0:T(1024)(128)(4,1)}), s8[2097152]{0:T(1024)(128)(4,1)S(1)}, s32[]{:S(2)}) async-start(s8[6291456]{0:T(1024)(128)(4,1)} %bitcast.50), calls=%async_computation.5 | async-start | bytes 4194304
  358.8 5.0 %copy-start.33 = (bf16[384,1024]{1,0:T(8,128)(2,1)S(1)}, bf16[384,1024]{1,0:T(8,128)(2,1)}, u32[]{:S(2)}) copy-start(bf16[384,1024]{1,0:T(8,128)(2,1)} %copy-done.32) | copy-start | bytes 2359300
  363.8 3.7 copy-start.25
  363.8 3.6 copy-start.29
  373.2 3.6 copy-start.35
  376.8 3.6 copy-start.31
  390.6 7.0 %copy-start.37 = (bf16[512,2,1024]{2,1,0:T(2,128)(2,1)S(1)}, bf16[512,2,1024]{2,1,0:T(2,128)(2,1)}, u32[]{:S(2)}) copy-start(bf16[512,2,1024]{2,1,0:T(2,128)(2,1)} %param.7) | copy-start | bytes 6291460
  390.6 7.0 %copy-start.38 = (bf16[512,2,1024]{2,1,0:T(2,128)(2,1)S(1)}, bf16[512,2,1024]{2,1,0:T(2,128)(2,1)}, u32[]{:S(2)}) copy-start(bf16[512,2,1024]{2,1,0:T(2,128)(2,1)} %param.8) | copy-start | bytes 6291460
  (24 other events, 39.2 us)

commit v4 on v3

--- a/solution.py
+++ b/solution.py
@@ -174,49 +174,55 @@
     )(half.reshape(1), near, far, weight, weight)
 
 
-def update_kernel(place_ref, grad_ref, weight_ref, momentum_ref, *refs):
+def update_kernel(count, place_ref, weight_ref, momentum_ref, *refs):
+    grad_refs = refs[:count]
     new_weight_ref, new_momentum_ref = refs[-2:]
-    grad = grad_ref[...].astype(jnp.float32)
-    moment = momentum_ref[0].astype(jnp.float32)
-    weight = weight_ref[...].astype(jnp.float32)
-    mix = beta_first * moment + (1.0 - beta_first) * grad
-    new_weight_ref[0] = weight * (1.0 - step_rate * decay_rate) - step_rate * jnp.tanh(
-        mix / sign_width
-    )
-    new_momentum_ref[0] = (beta_second * moment + (1.0 - beta_second) * grad).astype(
-        jnp.bfloat16
-    )
-
-
-def update(source, grad, weight, momentum, done):
-    rows, cols = grad.shape
-    steps = 3 if rows % 48 == 0 else 1
-    some = rows // steps
-    own = pl.BlockSpec((some, cols), lambda i, place: (i, 0))
-    wide = pl.BlockSpec((1, some, cols), lambda i, place: (0, i, place[0]))
-    size = grad.size
+    for m, grad_ref in enumerate(grad_refs):
+
+        @pl.when(pl.program_id(0) == m)
+        def _():
+            grad = grad_ref[...].astype(jnp.float32)
+            moment = momentum_ref[0].astype(jnp.float32)
+            weight = weight_ref[0].astype(jnp.float32)
+            mix = beta_first * moment + (1.0 - beta_first) * grad
+            new_weight_ref[0] = weight * (1.0 - step_rate * decay_rate) - step_rate * jnp.tanh(
+                mix / sign_width
+            )
+            new_momentum_ref[0] = (beta_second * moment + (1.0 - beta_second) * grad).astype(
+                jnp.bfloat16
+            )
+
+
+def update(part, place, grads, weight, momentum, done):
+    count, rows, some = weight.shape
+    parts = grads[0].shape[1] // some
+    wide = pl.BlockSpec((1, rows, some), lambda m, place: (0, 0, (place[0] ^ m) * parts + part))
+    size = weight.size
     return pl.pallas_call(
-        update_kernel,
+        functools.partial(update_kernel, count),
         grid_spec=pltpu.PrefetchScalarGridSpec(
             num_scalar_prefetch=1,
-            grid=(steps,),
-            in_specs=[own, own, wide] + [pl.BlockSpec(memory_space=pl.ANY)] * len(done),
+            grid=(count,),
+            in_specs=[pl.BlockSpec((1, rows, some), lambda m, place: (place[0] ^ m, 0, 0)), wide]
+            + [pl.BlockSpec((rows, some), lambda m, place: (0, part))] * count
+            + [pl.BlockSpec(memory_space=pl.ANY)] * len(done),
             out_specs=[wide, wide],
         ),
         out_shape=[
             jax.ShapeDtypeStruct(momentum.shape, jnp.float32),
             jax.ShapeDtypeStruct(momentum.shape, jnp.bfloat16),
         ],
-        input_output_aliases={4 + i: i for i in range(len(done))},
-        compiler_params=pltpu.CompilerParams(vmem_limit_bytes=32 * MIB),
+        input_output_aliases={3 + count + i: i for i in range(len(done))},
+        compiler_params=pltpu.CompilerParams(vmem_limit_bytes=40 * MIB),
         cost_estimate=pl.CostEstimate(flops=10 * size, bytes_accessed=12 * size, transcendentals=size),
         name="lion_step",
-    )(source.reshape(1), grad, weight, momentum, *done)
-
-
-def gathered(keep, give, experts, shards, place, mine):
+    )(place.reshape(1), weight, momentum, *grads, *done)
+
+
+def gathered(keep, give, experts, shards, place, first):
     bit = shards // 2
-    held = in_order(keep[None], swapped(give, "dp", bit)[None], (place & bit) != 0)
+    theirs = after(swapped(give, "dp", bit), first)
+    held = in_order(keep[None], theirs[None], (place & bit) != 0)
     while bit > 2:
         bit //= 2
         held = in_order(held, swapped(held, "dp", bit), (place & bit) != 0)
@@ -249,9 +255,6 @@
     low, high = out_grad[:, : width // 2], out_grad[:, width // 2 :]
     near = jnp.where(half == 0, low, high)
     far = jnp.where(half == 0, high, low)
-    near_tokens = gathered(near, far, experts, shards, place, mine)
-    far_tokens = gathered(far, near, experts, shards, place, mine)
-
     named = (routing ^ mine).reshape(1, group_tok * topk)
     hidden, *own_rows = picked_rows(
         hidden_kernel,
@@ -261,9 +264,12 @@
         topk,
         True,
     )
+    near_tokens = gathered(near, far, experts, shards, place, hidden)
+    far_tokens = gathered(far, near, experts, shards, place, hidden)
     other_hidden = swapped(hidden, "dp", span)
     own_rows = [swapped(own_rows[m], "expert", m) for m in each]
     other_rows = picked_rows(pick_kernel, [other_hidden], named, experts, topk, False)
+    other_picked = other_rows[0]
     other_rows = [swapped(other_rows[m], "expert", m) for m in each]
 
     near_list = [near_tokens[m] for m in each]
@@ -285,16 +291,15 @@
         grads[m ^ span] = swapped(other_terms[m], "dp", m)
 
     weight = down_weight[0]
-    late_weight = after(weight, other_hidden)
-    weights = {}
-    for m in range(shards):
-        block = lax.dynamic_slice_in_dim(
-            weight if m < span else late_weight, (place ^ m) * rows, rows, axis=0
-        )
-        weights[m] = swapped(block, "dp", m)
-
-    back_weight, gate_saved, up_saved, _ = lax.optimization_barrier(
-        (weight, gate_saved, up_saved, own_terms[0])
+    parts = 2 if cols % 256 == 0 else 1
+    late_weight = after(down_weight, other_hidden).reshape(shards, rows, cols)
+    weights = [
+        lax.all_to_all(piece, "dp", split_axis=0, concat_axis=0, tiled=True)
+        for piece in jnp.split(late_weight, parts, axis=2)
+    ]
+
+    back_weight, gate_saved, up_saved, *_ = lax.optimization_barrier(
+        (weight, gate_saved, up_saved, own_terms, other_picked)
     )
     gate = gate_saved.astype(jnp.float32)
     up = up_saved.astype(jnp.float32)
@@ -308,8 +313,8 @@
     d_gate = (deriv * up * sigma * (1.0 + gate * (1.0 - sigma))).astype(jnp.bfloat16)
 
     done = ()
-    for m in range(shards):
-        done = update(place ^ m, grads[m], weights[m], momentum, done)
+    for part in range(parts):
+        done = update(part, place, [grads[m] for m in range(shards)], weights[part], momentum, done)
     new_weight, new_momentum = done
     return (d_gate, d_up, new_weight, new_momentum)
 

time: 418 us -> 601 us (1.44)
  waiting for transfers between devices: 211 us -> 389 us
  local copies, waits for them, and re-layouts: 35.9 us -> 46.1 us
  Pallas kernels: 110 us -> 103 us
    ppermute x37 -> x30, waiting for transfers between devices: 211 us -> 389 us  [swapped(): return lax.ppermute(array, axis, [(i, i ^ mask) for i in range(size)])]
    all_to_all x0 -> x2, starting transfers between devices: none -> 13.1 us  [body(): lax.all_to_all(piece, 'dp', split_axis=0, concat_axis=0, tiled=True)]
    unnamed x102 -> x100, local copies, waits for them, and re-layouts: 20.8 us -> 31.3 us
    ppermute x37 -> x30, starting transfers between devices: 37.6 us -> 30 us  [swapped(): return lax.ppermute(array, axis, [(i, i ^ mask) for i in range(size)])]
    pallas_call x8 -> x2, Pallas kernels: 26.5 us -> 19 us  [update(): pl.pallas_call(functools.partial(update_kernel, count), grid_spec=pltpu.P...]
    dynamic_slice x2 -> x0, local copies, waits for them, and re-layouts: 7.22 us -> none  [body(): lax.dynamic_slice_in_dim(weight if m < span else late_weight, (place ^ m)...]
    split x0 -> x1, local copies, waits for them, and re-layouts: none -> 6.81 us  [body(): jnp.split(late_weight, parts, axis=2)]
  transfers between devices with their start and end apart: 37 -> 32, of which waited for: 15 -> 12; matrix products, arithmetic and copies ran while one was open for 4% -> 4% of each run, Pallas kernels for 26% -> 15%
where the time goes in v4:
time: 601 us; the launch traced here: 600 us
  waiting for transfers between devices  389 us (65%)
  Pallas kernels  103 us (17%)
  local copies, waits for them, and re-layouts  46.1 us (8%)
  starting transfers between devices  43.1 us (7%)
  other arithmetic  17.7 us (3%)
    ppermute x30, waiting for transfers between devices, swapped(): return lax.ppermute(array, axis, [(i, i ^ mask) for i in range(size)])  389 us
    unnamed x100, local copies, waits for them, and re-layouts  31.3 us
    ppermute x30, starting transfers between devices, swapped(): return lax.ppermute(array, axis, [(i, i ^ mask) for i in range(size)])  30 us
    pallas_call x8, Pallas kernels, terms(): pl.pallas_call(functools.partial(term_kernel, count), grid_spec=pltpu.Pre...  29.5 us
    pallas_call x4, Pallas kernels, deriv_of(): pl.pallas_call(deriv_kernel, grid_spec=pltpu.PrefetchScalarGridSpec(num_s...  25.3 us
    pallas_call x8, Pallas kernels, in_order(): pl.pallas_call(order_kernel, grid_spec=pltpu.PrefetchScalarGridSpec(num_s...  22.3 us
    pallas_call x2, Pallas kernels, update(): pl.pallas_call(functools.partial(update_kernel, count), grid_spec=pltpu.P...  19 us
    convert_element_type x1, other arithmetic, body(): d_up = (deriv * gate * sigma).astype(jnp.bfloat16)  16.3 us
  transfers between devices with their start and end apart: 32, of which 12 were waited for; matrix products, arithmetic and copies ran while one was open for 4% of the time, Pallas kernels for 15%

profile of v4, /device:TPU:8, one launch (start us, length us, event | category | flops | bytes accessed | tf_op | source)
XLA Modules:
  0.0 599.7 jit_solution(11289988764191799928)
XLA Ops:
  1.7 2.8 reshape.93.gate_ref
  4.4 4.1 reshape.94.up_ref
  8.5 1.6 copy-done.10
  10.1 3.9 hidden_rows.2
  16.0 2.6 collective-permute-start.13
  19.7 97.3 %collective-permute-done = bf16[64,1536]{1,0:T(8,128)(2,1)S(1)} collective-permute-done((bf16[64,1536]{1,0:T(8,128)(2,1)S(1)}, bf16[64,1536]{1,0:T(8,128)(2,1)S(1)}, u32[]{:S(2)}, u32[]{:S(2)}) %collective-permute-start) | collective-permute-done | bytes 196640 | tf_op jit(solution)/shard_map/ppermute | solution.py:22
  117.7 1.8 side_by_side.8
  119.4 1.3 collective-permute-start.1
  120.7 9.9 %collective-permute-done.1.theirs_ref = bf16[2,64,1536]{2,1,0:T(8,128)(2,1)S(1)} collective-permute-done((bf16[2,64,1536]{2,1,0:T(8,128)(2,1)}, bf16[2,64,1536]{2,1,0:T(8,128)(2,1)S(1)}, u32[]{:S(2)}, u32[]{:S(2)}) %collective-permute-start.1) | collective-permute-done | bytes 393248 | tf_op jit(solution)/shard_map/ppermute | solution.py:22
  131.4 2.0 side_by_side.9
  133.4 1.5 collective-permute-start.7
  134.9 3.4 collective-permute-start.3
  138.3 7.7 %collective-permute-done.3 = bf16[64,1536]{1,0:T(8,128)(2,1)S(1)} collective-permute-done((bf16[64,1536]{1,0:T(8,128)(2,1)}, bf16[64,1536]{1,0:T(8,128)(2,1)S(1)}, u32[]{:S(2)}, u32[]{:S(2)}) %collective-permute-start.3) | collective-permute-done | bytes 196640 | tf_op jit(solution)/shard_map/ppermute | solution.py:22
  146.7 1.8 side_by_side.11
  148.5 1.2 collective-permute-start.4
  149.8 1.5 collective-permute-start.2
  151.3 8.5 %collective-permute-done.4.theirs_ref = bf16[2,64,1536]{2,1,0:T(8,128)(2,1)S(1)} collective-permute-done((bf16[2,64,1536]{2,1,0:T(8,128)(2,1)}, bf16[2,64,1536]{2,1,0:T(8,128)(2,1)S(1)}, u32[]{:S(2)}, u32[]{:S(2)}) %collective-permute-start.4) | collective-permute-done | bytes 393248 | tf_op jit(solution)/shard_map/ppermute | solution.py:22
  160.5 2.0 side_by_side.12
  163.0 1.5 collective-permute-start.8
  164.6 6.8 %fusion.8 = (bf16[8,384,512]{2,1,0:T(8,128)(2,1)}, bf16[8,384,512]{2,1,0:T(8,128)(2,1)}) fusion(bf16[8,384,1024]{2,1,0:T(8,128)(2,1)} %bitcast.23), kind=kLoop, calls=%fused_computation.19 | loop fusion | bytes 12582912 | tf_op jit(solution)/shard_map/split | solution.py:298
  171.4 6.1 %all-to-all-start.1 = ((bf16[8,384,512]{2,1,0:T(8,128)(2,1)}), bf16[8,384,512]{2,1,0:T(8,128)(2,1)}, u32[]{:S(2)}, u32[]{:S(2)}) async-start(bf16[8,384,512]{2,1,0:T(8,128)(2,1)} %get-tuple-element.44), calls=%async_computation.1 | async-start | bytes 6291456 | tf_op jit(solution)/shard_map/all_to_all | solution.py:297
  177.5 1.5 collective-permute-start.5
  179.0 3.6 side_by_side.10
  182.6 20.5 %collective-permute-done.8.theirs_ref = bf16[4,64,1536]{2,1,0:T(8,128)(2,1)} collective-permute-done((bf16[4,64,1536]{2,1,0:T(8,128)(2,1)}, bf16[4,64,1536]{2,1,0:T(8,128)(2,1)}, u32[]{:S(2)}, u32[]{:S(2)}) %collective-permute-start.8) | collective-permute-done | bytes 786464 | tf_op jit(solution)/shard_map/ppermute | solution.py:22
  203.2 3.6 side_by_side.14
  206.8 2.5 collective-permute-start.15
  209.9 26.9 %collective-permute-done.5.theirs_ref = bf16[4,64,1536]{2,1,0:T(8,128)(2,1)S(1)} collective-permute-done((bf16[4,64,1536]{2,1,0:T(8,128)(2,1)S(1)}, bf16[4,64,1536]{2,1,0:T(8,128)(2,1)S(1)}, u32[]{:S(2)}, u32[]{:S(2)}) %collective-permute-start.5) | collective-permute-done | bytes 786464 | tf_op jit(solution)/shard_map/ppermute | solution.py:22
  237.7 3.7 side_by_side.13
  241.3 13.0 %collective-permute-done.15.theirs_ref = bf16[4,64,1536]{2,1,0:T(8,128)(2,1)} collective-permute-done((bf16[4,64,1536]{2,1,0:T(8,128)(2,1)}, bf16[4,64,1536]{2,1,0:T(8,128)(2,1)}, u32[]{:S(2)}, u32[]{:S(2)}) %collective-permute-start.15) | collective-permute-done | bytes 786464 | tf_op jit(solution)/shard_map/ppermute | solution.py:22
  254.3 3.8 side_by_side.15
  258.6 1.6 copy-done.35
  260.2 2.9 hidden_rows.3
  264.1 3.6 group_terms.8.refs_0_
  268.6 3.6 group_terms.11
  273.2 3.7 group_terms.10
  277.8 3.7 group_terms.9
  281.6 5.7 hidden_deriv.5
  287.8 7.3 %hidden_deriv.6 = f32[512,1024]{1,0:T(8,128)} custom-call(s32[1]{0:T(128)} %bitcast.place_ref, bf16[512,1536]{1,0:T(8,128)(2,1)} %collective-permute-done.6.refs_1_.near_ref, bf16[512,1536]{1,0:T(8,128)(2,1)} %collective-permute-done.17.far_ref, bf16[3072,1024]{1,0:T(8,128)(2,1)S(1)} %bitcast.28, bf16[3072,1024]{1,0:T(8,128)(2,1)S(1)} %bitcast.29), custom_call_target="tpu_custom_call" | custom-call | flops 3221225472 | bytes 11534336 | tf_op jit(solution)/shard_map/hidden_deriv/pallas_call | solution.py:153
  295.4 7.3 %hidden_deriv.7 = f32[512,1024]{1,0:T(8,128)} custom-call(s32[1]{0:T(128)} %bitcast.place_ref, bf16[512,1536]{1,0:T(8,128)(2,1)} %collective-permute-done.9.refs_3_.near_ref, bf16[512,1536]{1,0:T(8,128)(2,1)} %collective-permute-done.19.far_ref, bf16[3072,1024]{1,0:T(8,128)(2,1)S(1)} %bitcast.30, bf16[3072,1024]{1,0:T(8,128)(2,1)S(1)} %bitcast.31), custom_call_target="tpu_custom_call" | custom-call | flops 3221225472 | bytes 11534336 | tf_op jit(solution)/shard_map/hidden_deriv/pallas_call | solution.py:153
  302.7 1.4 collective-permute-start.20
  307.4 96.0 %collective-permute-done.25.refs_6_ = bf16[512,1024]{1,0:T(8,128)(2,1)} collective-permute-done((bf16[512,1024]{1,0:T(8,128)(2,1)}, bf16[512,1024]{1,0:T(8,128)(2,1)}, u32[]{:S(2)}, u32[]{:S(2)}) %collective-permute-start.25) | collective-permute-done | bytes 1048608 | tf_op jit(solution)/shard_map/ppermute | solution.py:22
  403.4 1.5 collective-permute-start.21
  405.0 20.1 %collective-permute-done.26.refs_7_ = bf16[512,1024]{1,0:T(8,128)(2,1)} collective-permute-done((bf16[512,1024]{1,0:T(8,128)(2,1)}, bf16[512,1024]{1,0:T(8,128)(2,1)}, u32[]{:S(2)}, u32[]{:S(2)}) %collective-permute-start.26) | collective-permute-done | bytes 1048608 | tf_op jit(solution)/shard_map/ppermute | solution.py:22
  425.9 1.2 copy-done.7
  427.1 1.2 copy-done.9
  428.3 3.6 group_terms.12.refs_4_
  432.9 3.6 group_terms.15
  437.4 3.7 group_terms.14
  442.0 3.7 group_terms.13
  446.7 5.0 hidden_deriv.4
  451.7 1.3 copy-done.11
  453.0 7.0 %all-to-all-start = ((bf16[8,384,512]{2,1,0:T(8,128)(2,1)}), bf16[8,384,512]{2,1,0:T(8,128)(2,1)S(1)}, u32[]{:S(2)}, u32[]{:S(2)}) async-start(bf16[8,384,512]{2,1,0:T(8,128)(2,1)} %get-tuple-element.45), calls=%async_computation | async-start | bytes 6291456 | tf_op jit(solution)/shard_map/all_to_all | solution.py:297
  460.0 1.5 collective-permute-start.23
  461.6 1.9 collective-permute-start.28
  463.6 1.5 collective-permute-start.29
  465.0 16.3 %fusion.7 = (bf16[512,2,1024]{2,1,0:T(2,128)(2,1)}, bf16[512,2,1024]{2,1,0:T(2,128)(2,1)}) fusion(bf16[512,2,1024]{2,1,0:T(2,128)(2,1)} %param.7, pred[512,2]{1,0:T(8,128)(4,1)S(1)} %copy.21, pred[512,2]{1,0:T(8,128)(4,1)S(1)} %copy.20, pred[512,2]{1,0:T(8,128)(4,1)S(1)} %copy.19, pred[512,2]{1,0:T(8,128)(4,1)S(1)} %copy.17, ...), kind=kLoop, calls=%fused_computation.10 | loop fusion | flops 19922944 | bytes 16781312 | tf_op jit(solution)/shard_map/convert_element_type | solution.py:312
  481.3 56.7 %collective-permute-done.23.refs_3_ = bf16[384,1024]{1,0:T(8,128)(2,1)S(1)} collective-permute-done((bf16[384,1024]{1,0:T(8,128)(2,1)}, bf16[384,1024]{1,0:T(8,128)(2,1)S(1)}, u32[]{:S(2)}, u32[]{:S(2)}) %collective-permute-start.23) | collective-permute-done | bytes 786464 | tf_op jit(solution)/shard_map/ppermute | solution.py:22
  538.0 9.2 %collective-permute-done.28.refs_6_ = bf16[384,1024]{1,0:T(8,128)(2,1)S(1)} collective-permute-done((bf16[384,1024]{1,0:T(8,128)(2,1)}, bf16[384,1024]{1,0:T(8,128)(2,1)S(1)}, u32[]{:S(2)}, u32[]{:S(2)}) %collective-permute-start.28) | collective-permute-done | bytes 786464 | tf_op jit(solution)/shard_map/ppermute | solution.py:22
  547.2 23.2 %collective-permute-done.29.refs_7_ = bf16[384,1024]{1,0:T(8,128)(2,1)S(1)} collective-permute-done((bf16[384,1024]{1,0:T(8,128)(2,1)}, bf16[384,1024]{1,0:T(8,128)(2,1)S(1)}, u32[]{:S(2)}, u32[]{:S(2)}) %collective-permute-start.29) | collective-permute-done | bytes 786464 | tf_op jit(solution)/shard_map/ppermute | solution.py:22
  570.3 10.1 %lion_step.2 = (f32[1,384,8192]{2,1,0:T(8,128)}, bf16[1,384,8192]{2,1,0:T(8,128)(2,1)}) custom-call(s32[1]{0:T(128)} %bitcast.21.place_ref, bf16[8,384,512]{2,1,0:T(8,128)(2,1)} %all-to-all-done.1.weight_ref, bf16[1,384,8192]{2,1,0:T(8,128)(2,1)} %momentum_ref.3, bf16[384,1024]{1,0:T(8,128)(2,1)S(1)} %copy-done.13, ...), custom_call_target="tpu_custom_call" | custom-call | flops 15728640 | bytes 18874368 | tf_op jit(solution)/shard_map/lion_step/pallas_call | solution.py:201
  584.0 1.1 copy-done.14
  585.2 1.1 copy-done.17
  586.3 1.1 copy-done.21
  590.8 8.9 %lion_step.3 = (f32[1,384,8192]{2,1,0:T(8,128)}, bf16[1,384,8192]{2,1,0:T(8,128)(2,1)}) custom-call(s32[1]{0:T(128)} %bitcast.21.place_ref, bf16[8,384,512]{2,1,0:T(8,128)(2,1)S(1)} %all-to-all-done.weight_ref, bf16[1,384,8192]{2,1,0:T(8,128)(2,1)} %momentum_ref.3, bf16[384,1024]{1,0:T(8,128)(2,1)S(1)} %copy-done.14, ...), custom_call_target="tpu_custom_call", output_to_operand_aliasing={{0}: (11, {}), {1}: (12, {})} | custom-call | flops 15728640 | bytes 18874368 | tf_op jit(solution)/shard_map/lion_step/pallas_call | solution.py:201
  (139 shorter events, 28.6 us)
Async XLA Ops:
  8.5 1.6 copy-start.10
  10.1 8.5 %copy-start.40 = (bf16[64,3072]{1,0:T(8,128)(2,1)S(1)}, bf16[64,3072]{1,0:T(8,128)(2,1)}, u32[]{:S(2)}) copy-start(bf16[64,3072]{1,0:T(8,128)(2,1)} %param.6) | copy-start | bytes 1179652
  14.0 1.0 copy-start.2
  15.0 1.0 copy-start.36
  16.0 148.5 %collective-permute-start.13 = (bf16[1024,1024]{1,0:T(8,128)(2,1)}, bf16[1024,1024]{1,0:T(8,128)(2,1)S(1)}, u32[]{:S(2)}, u32[]{:S(2)}) collective-permute-start(bf16[1024,1024]{1,0:T(8,128)(2,1)} %get-tuple-element.23), channel_id=1, source_target_pairs={{0,4},{1,5},{2,6},{3,7},{4,0},{5,1},{6,2},{7,3},{8,12},{9,13},{10,... | collective-permute-start | bytes 6291464 | tf_op jit(solution)/shard_map/ppermute | solution.py:22
  19.3 126.7 %copy-start.38 = (bf16[64,1536]{1,0:T(8,128)(2,1)}, bf16[64,1536]{1,0:T(8,128)(2,1)S(1)}, u32[]{:S(2)}) copy-start(bf16[64,1536]{1,0:T(8,128)(2,1)S(1)} %get-tuple-element.46) | copy-start | bytes 589828
  19.3 97.6 %collective-permute-start = (bf16[64,1536]{1,0:T(8,128)(2,1)S(1)}, bf16[64,1536]{1,0:T(8,128)(2,1)S(1)}, u32[]{:S(2)}, u32[]{:S(2)}) collective-permute-start(bf16[64,1536]{1,0:T(8,128)(2,1)S(1)} %get-tuple-element.46), channel_id=1, source_target_pairs={{0,4},{1,5},{2,6},{3,7},{4,0},{5,1},{6,2},{7,3},{8,12},{9,13},{10,... | collective-permute-start | bytes 589832 | tf_op jit(solution)/shard_map/ppermute | solution.py:22
  119.4 11.2 %collective-permute-start.1 = (bf16[2,64,1536]{2,1,0:T(8,128)(2,1)}, bf16[2,64,1536]{2,1,0:T(8,128)(2,1)S(1)}, u32[]{:S(2)}, u32[]{:S(2)}) collective-permute-start(bf16[2,64,1536]{2,1,0:T(8,128)(2,1)} %bitcast.68), channel_id=1, source_target_pairs={{0,2},{1,3},{2,0},{3,1},{4,6},{5,7},{6,4},{7,5},{8,10},{9,11},{10,... | collective-permute-start | bytes 1179656 | tf_op jit(solution)/shard_map/ppermute | solution.py:22
  133.4 29.6 %collective-permute-start.7 = (bf16[4,64,1536]{2,1,0:T(8,128)(2,1)}, bf16[4,64,1536]{2,1,0:T(8,128)(2,1)}, u32[]{:S(2)}, u32[]{:S(2)}) collective-permute-start(bf16[4,64,1536]{2,1,0:T(8,128)(2,1)} %bitcast.63), channel_id=1, source_target_pairs={{0,16},{8,24},{16,0},{24,8},{1,17},{9,25},{17,1},{25,9},{2,18},{10... | collective-permute-start | bytes 2359304 | tf_op jit(solution)/shard_map/ppermute | solution.py:22
  134.9 11.1 %collective-permute-start.3 = (bf16[64,1536]{1,0:T(8,128)(2,1)}, bf16[64,1536]{1,0:T(8,128)(2,1)S(1)}, u32[]{:S(2)}, u32[]{:S(2)}) collective-permute-start(bf16[64,1536]{1,0:T(8,128)(2,1)} %get-tuple-element.47), channel_id=1, source_target_pairs={{0,4},{1,5},{2,6},{3,7},{4,0},{5,1},{6,2},{7,3},{8,12},{9,13},{10,... | collective-permute-start | bytes 589832 | tf_op jit(solution)/shard_map/ppermute | solution.py:22
  148.5 11.2 %collective-permute-start.4 = (bf16[2,64,1536]{2,1,0:T(8,128)(2,1)}, bf16[2,64,1536]{2,1,0:T(8,128)(2,1)S(1)}, u32[]{:S(2)}, u32[]{:S(2)}) collective-permute-start(bf16[2,64,1536]{2,1,0:T(8,128)(2,1)} %bitcast.66), channel_id=1, source_target_pairs={{0,2},{1,3},{2,0},{3,1},{4,6},{5,7},{6,4},{7,5},{8,10},{9,11},{10,... | collective-permute-start | bytes 1179656 | tf_op jit(solution)/shard_map/ppermute | solution.py:22
  149.8 59.6 %collective-permute-start.10 = (bf16[512,1024]{1,0:T(8,128)(2,1)}, bf16[512,1024]{1,0:T(8,128)(2,1)S(1)}, u32[]{:S(2)}, u32[]{:S(2)}) collective-permute-start(bf16[512,1024]{1,0:T(8,128)(2,1)} %copy-done.36), channel_id=1, source_target_pairs={{0,8},{8,0},{16,24},{24,16},{1,9},{9,1},{17,25},{25,17},{2,10},{10... | collective-permute-start | bytes 3145736 | tf_op jit(solution)/shard_map/ppermute | solution.py:22
  149.8 29.2 %collective-permute-start.2 = (bf16[4,64,1536]{2,1,0:T(8,128)(2,1)}, bf16[4,64,1536]{2,1,0:T(8,128)(2,1)}, u32[]{:S(2)}, u32[]{:S(2)}) collective-permute-start(bf16[4,64,1536]{2,1,0:T(8,128)(2,1)} %bitcast.64), channel_id=1, source_target_pairs={{0,1},{1,0},{2,3},{3,2},{4,5},{5,4},{6,7},{7,6},{8,9},{9,8},{10,11... | collective-permute-start | bytes 2359304 | tf_op jit(solution)/shard_map/ppermute | solution.py:22
  162.5 44.3 %collective-permute-start.14 = (bf16[4,64,1536]{2,1,0:T(8,128)(2,1)}, bf16[4,64,1536]{2,1,0:T(8,128)(2,1)}, u32[]{:S(2)}, u32[]{:S(2)}) collective-permute-start(bf16[4,64,1536]{2,1,0:T(8,128)(2,1)} %bitcast.60), channel_id=1, source_target_pairs={{0,16},{8,24},{16,0},{24,8},{1,17},{9,25},{17,1},{25,9},{2,18},{10... | collective-permute-start | bytes 2359304 | tf_op jit(solution)/shard_map/ppermute | solution.py:22
  163.0 40.1 %collective-permute-start.8 = (bf16[4,64,1536]{2,1,0:T(8,128)(2,1)}, bf16[4,64,1536]{2,1,0:T(8,128)(2,1)}, u32[]{:S(2)}, u32[]{:S(2)}) collective-permute-start(bf16[4,64,1536]{2,1,0:T(8,128)(2,1)} %collective-permute-done.7.mine_ref), channel_id=1, source_target_pairs={{0,1},{1,0},{2,3},{3,2},{4,5},{5,4},{6,7},{7,6},{8,9},{9,8},{10,11... | collective-permute-start | bytes 2359304 | tf_op jit(solution)/shard_map/ppermute | solution.py:22
  164.6 6.8 %copy-start.34 = (bf16[1024,1024]{1,0:T(8,128)(2,1)}, bf16[1024,1024]{1,0:T(8,128)(2,1)S(1)}, u32[]{:S(2)}) copy-start(bf16[1024,1024]{1,0:T(8,128)(2,1)S(1)} %collective-permute-done.13.hidden_ref) | copy-start | bytes 6291460
  171.4 6.1 %copy-start.37 = (bf16[2,2,64,1536]{3,2,1,0:T(8,128)(2,1)S(1)}, bf16[2,2,64,1536]{3,2,1,0:T(8,128)(2,1)}, u32[]{:S(2)}) copy-start(bf16[2,2,64,1536]{3,2,1,0:T(8,128)(2,1)} %side_by_side.12) | copy-start | bytes 2359300
  171.4 281.6 %all-to-all-start.1 = ((bf16[8,384,512]{2,1,0:T(8,128)(2,1)}), bf16[8,384,512]{2,1,0:T(8,128)(2,1)}, u32[]{:S(2)}, u32[]{:S(2)}) async-start(bf16[8,384,512]{2,1,0:T(8,128)(2,1)} %get-tuple-element.44), calls=%async_computation.1 | async-start | bytes 6291456 | tf_op jit(solution)/shard_map/all_to_all | solution.py:297
  177.5 59.2 %collective-permute-start.5 = (bf16[4,64,1536]{2,1,0:T(8,128)(2,1)S(1)}, bf16[4,64,1536]{2,1,0:T(8,128)(2,1)S(1)}, u32[]{:S(2)}, u32[]{:S(2)}) collective-permute-start(bf16[4,64,1536]{2,1,0:T(8,128)(2,1)S(1)} %bitcast.62), channel_id=1, source_target_pairs={{0,1},{1,0},{2,3},{3,2},{4,5},{5,4},{6,7},{7,6},{8,9},{9,8},{10,11... | collective-permute-start | bytes 2359304 | tf_op jit(solution)/shard_map/ppermute | solution.py:22
  182.6 81.5 %collective-permute-start.6 = (bf16[512,1536]{1,0:T(8,128)(2,1)}, bf16[512,1536]{1,0:T(8,128)(2,1)}, u32[]{:S(2)}, u32[]{:S(2)}) collective-permute-start(bf16[512,1536]{1,0:T(8,128)(2,1)} %bitcast.36), channel_id=1, source_target_pairs={{0,8},{8,0},{16,24},{24,16},{1,9},{9,1},{17,25},{25,17},{2,10},{10... | collective-permute-start | bytes 4718600 | tf_op jit(solution)/shard_map/ppermute | solution.py:22
  206.8 57.3 %collective-permute-start.9 = (bf16[512,1536]{1,0:T(8,128)(2,1)}, bf16[512,1536]{1,0:T(8,128)(2,1)}, u32[]{:S(2)}, u32[]{:S(2)}) collective-permute-start(bf16[512,1536]{1,0:T(8,128)(2,1)} %bitcast.46), channel_id=1, source_target_pairs={{0,8},{8,0},{16,24},{24,16},{1,9},{9,1},{17,25},{25,17},{2,10},{10... | collective-permute-start | bytes 4718600 | tf_op jit(solution)/shard_map/ppermute | solution.py:22
  206.8 47.5 %collective-permute-start.15 = (bf16[4,64,1536]{2,1,0:T(8,128)(2,1)}, bf16[4,64,1536]{2,1,0:T(8,128)(2,1)}, u32[]{:S(2)}, u32[]{:S(2)}) collective-permute-start(bf16[4,64,1536]{2,1,0:T(8,128)(2,1)} %collective-permute-done.14.mine_ref), channel_id=1, source_target_pairs={{0,1},{1,0},{2,3},{3,2},{4,5},{5,4},{6,7},{7,6},{8,9},{9,8},{10,11... | collective-permute-start | bytes 2359304 | tf_op jit(solution)/shard_map/ppermute | solution.py:22
  209.3 44.9 %copy-start.4 = (bf16[512,1024]{1,0:T(8,128)(2,1)}, bf16[512,1024]{1,0:T(8,128)(2,1)S(1)}, u32[]{:S(2)}) copy-start(bf16[512,1024]{1,0:T(8,128)(2,1)S(1)} %collective-permute-done.10.refs_5_) | copy-start | bytes 3145732
  209.3 48.8 %collective-permute-start.11 = (bf16[512,1024]{1,0:T(8,128)(2,1)}, bf16[512,1024]{1,0:T(8,128)(2,1)}, u32[]{:S(2)}, u32[]{:S(2)}) collective-permute-start(bf16[512,1024]{1,0:T(8,128)(2,1)} %get-tuple-element.28), channel_id=1, source_target_pairs={{0,16},{8,24},{16,0},{24,8},{1,17},{9,25},{17,1},{25,9},{2,18},{10... | collective-permute-start | bytes 3145736 | tf_op jit(solution)/shard_map/ppermute | solution.py:22
  236.8 27.3 %collective-permute-start.12 = (bf16[512,1024]{1,0:T(8,128)(2,1)}, bf16[512,1024]{1,0:T(8,128)(2,1)}, u32[]{:S(2)}, u32[]{:S(2)}) collective-permute-start(bf16[512,1024]{1,0:T(8,128)(2,1)} %get-tuple-element.29), channel_id=1, source_target_pairs={{0,24},{8,16},{16,8},{24,0},{1,25},{9,17},{17,9},{25,1},{2,26},{10... | collective-permute-start | bytes 3145736 | tf_op jit(solution)/shard_map/ppermute | solution.py:22
  254.3 9.8 %copy-start = (bf16[4,2,64,1536]{3,2,1,0:T(8,128)(2,1)S(1)}, bf16[4,2,64,1536]{3,2,1,0:T(8,128)(2,1)}, u32[]{:S(2)}) copy-start(bf16[4,2,64,1536]{3,2,1,0:T(8,128)(2,1)} %side_by_side.10) | copy-start | bytes 4718596
  254.3 9.8 %copy-start.1 = (bf16[4,2,64,1536]{3,2,1,0:T(8,128)(2,1)S(1)}, bf16[4,2,64,1536]{3,2,1,0:T(8,128)(2,1)}, u32[]{:S(2)}) copy-start(bf16[4,2,64,1536]{3,2,1,0:T(8,128)(2,1)} %side_by_side.14) | copy-start | bytes 4718596
  254.3 33.5 %collective-permute-start.17 = (bf16[512,1536]{1,0:T(8,128)(2,1)}, bf16[512,1536]{1,0:T(8,128)(2,1)}, u32[]{:S(2)}, u32[]{:S(2)}) collective-permute-start(bf16[512,1536]{1,0:T(8,128)(2,1)} %bitcast.56), channel_id=1, source_target_pairs={{0,8},{8,0},{16,24},{24,16},{1,9},{9,1},{17,25},{25,17},{2,10},{10... | collective-permute-start | bytes 4718600 | tf_op jit(solution)/shard_map/ppermute | solution.py:22
  258.1 37.2 %collective-permute-start.19 = (bf16[512,1536]{1,0:T(8,128)(2,1)}, bf16[512,1536]{1,0:T(8,128)(2,1)}, u32[]{:S(2)}, u32[]{:S(2)}) collective-permute-start(bf16[512,1536]{1,0:T(8,128)(2,1)} %bitcast.58), channel_id=1, source_target_pairs={{0,8},{8,0},{16,24},{24,16},{1,9},{9,1},{17,25},{25,17},{2,10},{10... | collective-permute-start | bytes 4718600 | tf_op jit(solution)/shard_map/ppermute | solution.py:22
  258.6 1.6 copy-start.35
  260.2 3.9 copy-start.3
  260.2 3.9 copy-start.5
  264.1 40.6 %collective-permute-start.24 = (bf16[512,1024]{1,0:T(8,128)(2,1)S(1)}, bf16[512,1024]{1,0:T(8,128)(2,1)S(1)}, u32[]{:S(2)}, u32[]{:S(2)}) collective-permute-start(bf16[512,1024]{1,0:T(8,128)(2,1)S(1)} %get-tuple-element.35), channel_id=1, source_target_pairs={{0,8},{8,0},{16,24},{24,16},{1,9},{9,1},{17,25},{25,17},{2,10},{10... | collective-permute-start | bytes 3145736 | tf_op jit(solution)/shard_map/ppermute | solution.py:22
  273.2 8.4 %slice-start = ((s8[6291456]{0:T(1024)(128)(4,1)}), s8[4194304]{0:T(1024)(128)(4,1)S(1)}, s32[]{:S(2)}) async-start(s8[6291456]{0:T(1024)(128)(4,1)} %bitcast.24), calls=%async_computation.2 | async-start | bytes 8388608
  277.8 3.8 slice-start.1
  277.8 3.8 copy-start.19
  281.6 5.7 copy-start.30
  287.3 174.2 %collective-permute-start.16 = (f32[512,1024]{1,0:T(8,128)}, f32[512,1024]{1,0:T(8,128)}, u32[]{:S(2)}, u32[]{:S(2)}) collective-permute-start(f32[512,1024]{1,0:T(8,128)} %hidden_deriv.5), channel_id=1, source_target_pairs={{0,16},{8,24},{16,0},{24,8},{1,17},{9,25},{17,1},{25,9},{2,18},{10... | collective-permute-start | bytes 6291464 | tf_op jit(solution)/shard_map/ppermute | solution.py:22
  295.2 11.5 %copy-start.45 = (s32[512,2]{0,1:T(2,128)S(1)}, s32[512,2]{0,1:T(2,128)}, u32[]{:S(2)}) copy-start(s32[512,2]{0,1:T(2,128)} %param.9) | copy-start | bytes 12292
  295.2 166.5 %collective-permute-start.18 = (f32[512,1024]{1,0:T(8,128)}, f32[512,1024]{1,0:T(8,128)}, u32[]{:S(2)}, u32[]{:S(2)}) collective-permute-start(f32[512,1024]{1,0:T(8,128)} %hidden_deriv.6), channel_id=1, source_target_pairs={{0,8},{8,0},{16,24},{24,16},{1,9},{9,1},{17,25},{25,17},{2,10},{10... | collective-permute-start | bytes 6291464 | tf_op jit(solution)/shard_map/ppermute | solution.py:22
  302.7 160.9 %collective-permute-start.20 = (f32[512,1024]{1,0:T(8,128)}, f32[512,1024]{1,0:T(8,128)}, u32[]{:S(2)}, u32[]{:S(2)}) collective-permute-start(f32[512,1024]{1,0:T(8,128)} %hidden_deriv.7), channel_id=1, source_target_pairs={{0,24},{8,16},{16,8},{24,0},{1,25},{9,17},{17,9},{25,1},{2,26},{10... | collective-permute-start | bytes 6291464 | tf_op jit(solution)/shard_map/ppermute | solution.py:22
  304.1 99.3 %collective-permute-start.25 = (bf16[512,1024]{1,0:T(8,128)(2,1)}, bf16[512,1024]{1,0:T(8,128)(2,1)}, u32[]{:S(2)}, u32[]{:S(2)}) collective-permute-start(bf16[512,1024]{1,0:T(8,128)(2,1)} %get-tuple-element.36), channel_id=1, source_target_pairs={{0,16},{8,24},{16,0},{24,8},{1,17},{9,25},{17,1},{25,9},{2,18},{10... | collective-permute-start | bytes 3145736 | tf_op jit(solution)/shard_map/ppermute | solution.py:22
  305.6 119.5 %collective-permute-start.26 = (bf16[512,1024]{1,0:T(8,128)(2,1)}, bf16[512,1024]{1,0:T(8,128)(2,1)}, u32[]{:S(2)}, u32[]{:S(2)}) collective-permute-start(bf16[512,1024]{1,0:T(8,128)(2,1)} %get-tuple-element.37), channel_id=1, source_target_pairs={{0,24},{8,16},{16,8},{24,0},{1,25},{9,17},{17,9},{25,1},{2,26},{10... | collective-permute-start | bytes 3145736 | tf_op jit(solution)/shard_map/ppermute | solution.py:22
  403.4 56.5 %collective-permute-start.21 = (bf16[384,1024]{1,0:T(8,128)(2,1)}, bf16[384,1024]{1,0:T(8,128)(2,1)}, u32[]{:S(2)}, u32[]{:S(2)}) collective-permute-start(bf16[384,1024]{1,0:T(8,128)(2,1)} %copy-done.30), channel_id=1, source_target_pairs={{0,1},{1,0},{2,3},{3,2},{4,5},{5,4},{6,7},{7,6},{8,9},{9,8},{10,11... | collective-permute-start | bytes 2359304 | tf_op jit(solution)/shard_map/ppermute | solution.py:22
  425.1 56.2 %collective-permute-start.22 = (bf16[384,1024]{1,0:T(8,128)(2,1)}, bf16[384,1024]{1,0:T(8,128)(2,1)}, u32[]{:S(2)}, u32[]{:S(2)}) collective-permute-start(bf16[384,1024]{1,0:T(8,128)(2,1)} %copy-done.29), channel_id=1, source_target_pairs={{0,2},{1,3},{2,0},{3,1},{4,6},{5,7},{6,4},{7,5},{8,10},{9,11},{10,... | collective-permute-start | bytes 2359304 | tf_op jit(solution)/shard_map/ppermute | solution.py:22
  425.9 1.2 copy-start.7
  427.1 1.2 copy-start.9
  437.4 9.3 %slice-start.2 = ((s8[6291456]{0:T(1024)(128)(4,1)}), s8[4194304]{0:T(1024)(128)(4,1)S(1)}, s32[]{:S(2)}) async-start(s8[6291456]{0:T(1024)(128)(4,1)} %bitcast.32), calls=%async_computation.4 | async-start | bytes 8388608
  442.0 4.7 slice-start.3
  442.0 4.7 copy-start.18
  451.7 1.3 copy-start.11
  453.0 131.0 %all-to-all-start = ((bf16[8,384,512]{2,1,0:T(8,128)(2,1)}), bf16[8,384,512]{2,1,0:T(8,128)(2,1)S(1)}, u32[]{:S(2)}, u32[]{:S(2)}) async-start(bf16[8,384,512]{2,1,0:T(8,128)(2,1)} %get-tuple-element.45), calls=%async_computation | async-start | bytes 6291456 | tf_op jit(solution)/shard_map/all_to_all | solution.py:297
  460.0 110.4 %copy-start.13 = (bf16[384,1024]{1,0:T(8,128)(2,1)S(1)}, bf16[384,1024]{1,0:T(8,128)(2,1)}, u32[]{:S(2)}) copy-start(bf16[384,1024]{1,0:T(8,128)(2,1)} %copy-done.12) | copy-start | bytes 2359300
  460.0 110.4 %copy-start.16 = (bf16[384,1024]{1,0:T(8,128)(2,1)S(1)}, bf16[384,1024]{1,0:T(8,128)(2,1)}, u32[]{:S(2)}) copy-start(bf16[384,1024]{1,0:T(8,128)(2,1)} %copy-done.15) | copy-start | bytes 2359300
  460.0 78.0 %collective-permute-start.23 = (bf16[384,1024]{1,0:T(8,128)(2,1)}, bf16[384,1024]{1,0:T(8,128)(2,1)S(1)}, u32[]{:S(2)}, u32[]{:S(2)}) collective-permute-start(bf16[384,1024]{1,0:T(8,128)(2,1)} %copy-done.28), channel_id=1, source_target_pairs={{0,3},{1,2},{2,1},{3,0},{4,7},{5,6},{6,5},{7,4},{8,11},{9,10},{10,... | collective-permute-start | bytes 2359304 | tf_op jit(solution)/shard_map/ppermute | solution.py:22
  461.5 76.5 %collective-permute-start.27 = (bf16[384,1024]{1,0:T(8,128)(2,1)}, bf16[384,1024]{1,0:T(8,128)(2,1)S(1)}, u32[]{:S(2)}, u32[]{:S(2)}) collective-permute-start(bf16[384,1024]{1,0:T(8,128)(2,1)} %copy-done.33), channel_id=1, source_target_pairs={{0,1},{1,0},{2,3},{3,2},{4,5},{5,4},{6,7},{7,6},{8,9},{9,8},{10,11... | collective-permute-start | bytes 2359304 | tf_op jit(solution)/shard_map/ppermute | solution.py:22
  461.6 85.6 %collective-permute-start.28 = (bf16[384,1024]{1,0:T(8,128)(2,1)}, bf16[384,1024]{1,0:T(8,128)(2,1)S(1)}, u32[]{:S(2)}, u32[]{:S(2)}) collective-permute-start(bf16[384,1024]{1,0:T(8,128)(2,1)} %copy-done.32), channel_id=1, source_target_pairs={{0,2},{1,3},{2,0},{3,1},{4,6},{5,7},{6,4},{7,5},{8,10},{9,11},{10,... | collective-permute-start | bytes 2359304 | tf_op jit(solution)/shard_map/ppermute | solution.py:22
  463.6 106.8 %collective-permute-start.29 = (bf16[384,1024]{1,0:T(8,128)(2,1)}, bf16[384,1024]{1,0:T(8,128)(2,1)S(1)}, u32[]{:S(2)}, u32[]{:S(2)}) collective-permute-start(bf16[384,1024]{1,0:T(8,128)(2,1)} %copy-done.31), channel_id=1, source_target_pairs={{0,3},{1,2},{2,1},{3,0},{4,7},{5,6},{6,5},{7,4},{8,11},{9,10},{10,... | collective-permute-start | bytes 2359304 | tf_op jit(solution)/shard_map/ppermute | solution.py:22
  584.0 1.1 copy-start.14
  585.2 1.1 copy-start.17
  586.3 1.1 copy-start.21
  587.4 1.1 copy-start.23
  588.6 1.1 copy-start.25
  589.7 1.1 copy-start.27
  (18 other events, 15.5 us)

commit v5 on v4

--- a/solution.py
+++ b/solution.py
@@ -91,7 +91,7 @@
         in_specs=[row_block] * len(arrays) + [pl.BlockSpec((1, some * topk), lambda i: (0, i))],
         out_specs=out_specs,
         out_shape=out_shape,
-        compiler_params=pltpu.CompilerParams(vmem_limit_bytes=32 * MIB),
+        compiler_params=pltpu.CompilerParams(vmem_limit_bytes=56 * MIB),
         cost_estimate=pl.CostEstimate(
             flops=2 * experts * count_rows * some * cols,
             bytes_accessed=2 * cols * (count_rows * (len(arrays) + 1) + experts * group_tok),
@@ -129,7 +129,7 @@
             out_specs=pl.BlockSpec((tall, cols), lambda i, place: (i, 0)),
         ),
         out_shape=jax.ShapeDtypeStruct((steps * tall, cols), jnp.bfloat16),
-        compiler_params=pltpu.CompilerParams(vmem_limit_bytes=40 * MIB),
+        compiler_params=pltpu.CompilerParams(vmem_limit_bytes=56 * MIB),
         cost_estimate=pl.CostEstimate(
             flops=2 * count * group_tok * steps * tall * cols,
             bytes_accessed=2 * (count * group_tok * (steps * tall + cols) + steps * tall * cols),
@@ -164,7 +164,7 @@
             out_specs=pl.BlockSpec((group_tok, wide), lambda i, place: (0, i)),
         ),
         out_shape=jax.ShapeDtypeStruct((group_tok, cols), jnp.float32),
-        compiler_params=pltpu.CompilerParams(vmem_limit_bytes=32 * MIB),
+        compiler_params=pltpu.CompilerParams(vmem_limit_bytes=56 * MIB),
         cost_estimate=pl.CostEstimate(
             flops=4 * group_tok * width * cols,
             bytes_accessed=4 * (group_tok + cols) * width + 4 * group_tok * cols,
@@ -213,16 +213,18 @@
             jax.ShapeDtypeStruct(momentum.shape, jnp.bfloat16),
         ],
         input_output_aliases={3 + count + i: i for i in range(len(done))},
-        compiler_params=pltpu.CompilerParams(vmem_limit_bytes=40 * MIB),
+        compiler_params=pltpu.CompilerParams(vmem_limit_bytes=56 * MIB),
         cost_estimate=pl.CostEstimate(flops=10 * size, bytes_accessed=12 * size, transcendentals=size),
         name="lion_step",
     )(place.reshape(1), weight, momentum, *grads, *done)
 
 
-def gathered(keep, give, experts, shards, place, first):
+def first_step(keep, theirs, shards, place):
+    return in_order(keep[None], theirs[None], (place & (shards // 2)) != 0)
+
+
+def gathered(held, experts, shards, place):
     bit = shards // 2
-    theirs = after(swapped(give, "dp", bit), first)
-    held = in_order(keep[None], theirs[None], (place & bit) != 0)
     while bit > 2:
         bit //= 2
         held = in_order(held, swapped(held, "dp", bit), (place & bit) != 0)
@@ -233,7 +235,7 @@
         for m in groups:
             groups[m] = in_order(groups[m], swapped(groups[m], "dp", 1), (place & 1) != 0)
     for m in list(groups):
-        groups[m] = groups[m].reshape(-1, keep.shape[1])
+        groups[m] = groups[m].reshape(-1, held.shape[2])
         if experts > 1:
             groups[m + 1] = swapped(groups[m], "expert", 1)
     return groups
@@ -255,21 +257,23 @@
     low, high = out_grad[:, : width // 2], out_grad[:, width // 2 :]
     near = jnp.where(half == 0, low, high)
     far = jnp.where(half == 0, high, low)
+    near_theirs = swapped(far, "dp", span)
+    far_theirs = swapped(near, "dp", span)
+
     named = (routing ^ mine).reshape(1, group_tok * topk)
+    gate_rows, up_rows, *_ = lax.optimization_barrier(
+        (gate_saved.reshape(-1, cols), up_saved.reshape(-1, cols), near, far)
+    )
     hidden, *own_rows = picked_rows(
-        hidden_kernel,
-        [gate_saved.reshape(-1, cols), up_saved.reshape(-1, cols)],
-        named,
-        experts,
-        topk,
-        True,
-    )
-    near_tokens = gathered(near, far, experts, shards, place, hidden)
-    far_tokens = gathered(far, near, experts, shards, place, hidden)
-    other_hidden = swapped(hidden, "dp", span)
+        hidden_kernel, [gate_rows, up_rows], named, experts, topk, True
+    )
+    near_held = first_step(near, after(near_theirs, hidden), shards, place)
+    far_held = first_step(far, after(far_theirs, hidden), shards, place)
+    near_tokens = gathered(near_held, experts, shards, place)
+    far_tokens = gathered(far_held, experts, shards, place)
+    other_hidden = swapped(after(hidden, near_held, far_held), "dp", span)
     own_rows = [swapped(own_rows[m], "expert", m) for m in each]
     other_rows = picked_rows(pick_kernel, [other_hidden], named, experts, topk, False)
-    other_picked = other_rows[0]
     other_rows = [swapped(other_rows[m], "expert", m) for m in each]
 
     near_list = [near_tokens[m] for m in each]
@@ -285,27 +289,30 @@
 
     own_terms = shard_terms(own_rows)
     other_terms = shard_terms(other_rows)
+    weight = down_weight[0]
+    parts = 2 if cols % 256 == 0 else 1
+    pieces = jnp.split(down_weight.reshape(shards, rows, cols), parts, axis=2)
+    weights = []
+    for part, piece in enumerate(pieces):
+        begun = [other_hidden] if part == 0 else [weights[-1], other_terms]
+        weights.append(
+            lax.all_to_all(after(piece, *begun), "dp", split_axis=0, concat_axis=0, tiled=True)
+        )
+
+    other_terms = after(other_terms, weights[0])
     grads = {}
     for m in range(span):
         grads[m] = swapped(own_terms[m], "dp", m)
         grads[m ^ span] = swapped(other_terms[m], "dp", m)
 
-    weight = down_weight[0]
-    parts = 2 if cols % 256 == 0 else 1
-    late_weight = after(down_weight, other_hidden).reshape(shards, rows, cols)
-    weights = [
-        lax.all_to_all(piece, "dp", split_axis=0, concat_axis=0, tiled=True)
-        for piece in jnp.split(late_weight, parts, axis=2)
-    ]
-
     back_weight, gate_saved, up_saved, *_ = lax.optimization_barrier(
-        (weight, gate_saved, up_saved, own_terms, other_picked)
+        (weight, gate_saved, up_saved, own_terms, other_rows[experts // 2])
     )
     gate = gate_saved.astype(jnp.float32)
     up = up_saved.astype(jnp.float32)
     sigma = jax.nn.sigmoid(gate)
     deriv = jnp.zeros(gate.shape, jnp.float32)
-    for m in [2 * i + j for j in range(2) for i in range(experts // 2)][::-1]:
+    for m in list(range(experts // 2, experts)) + list(range(experts // 2)):
         part = deriv_of(near_tokens[m], far_tokens[m], back_weight, half)
         chosen = (routing == (mine ^ m))[:, :, None]
         deriv = jnp.where(chosen, swapped(part, "expert", m)[:, None, :], deriv)

time: 601 us -> 573 us (0.953)
  waiting for transfers between devices: 389 us -> 361 us
  Pallas kernels: 103 us -> 129 us
  local copies, waits for them, and re-layouts: 46.1 us -> 22.6 us
    ppermute x30, waiting for transfers between devices: 389 us -> 361 us  [swapped(): return lax.ppermute(array, axis, [(i, i ^ mask) for i in range(size)])]
    unnamed x100 -> x42, local copies, waits for them, and re-layouts: 31.3 us -> 8.54 us
    pallas_call x8, Pallas kernels: 29.5 us -> 43.2 us  [terms(): pl.pallas_call(functools.partial(term_kernel, count), grid_spec=pltpu.Pre...]
    pallas_call x4, Pallas kernels: 25.3 us -> 31.7 us  [deriv_of(): pl.pallas_call(deriv_kernel, grid_spec=pltpu.PrefetchScalarGridSpec(num_s...]
  transfers between devices with their start and end apart: 32 -> 32, of which waited for: 12 -> 13; matrix products, arithmetic and copies ran while one was open for 4% -> 5% of each run, Pallas kernels for 15% -> 20%
where the time goes in v5:
time: 573 us; the launch traced here: 571 us
  waiting for transfers between devices  361 us (63%)
  Pallas kernels  129 us (23%)
  starting transfers between devices  39.7 us (7%)
  local copies, waits for them, and re-layouts  22.6 us (4%)
  other arithmetic  18.2 us (3%)
    ppermute x30, waiting for transfers between devices, swapped(): return lax.ppermute(array, axis, [(i, i ^ mask) for i in range(size)])  361 us
    pallas_call x8, Pallas kernels, terms(): pl.pallas_call(functools.partial(term_kernel, count), grid_spec=pltpu.Pre...  43.2 us
    pallas_call x4, Pallas kernels, deriv_of(): pl.pallas_call(deriv_kernel, grid_spec=pltpu.PrefetchScalarGridSpec(num_s...  31.7 us
    ppermute x30, starting transfers between devices, swapped(): return lax.ppermute(array, axis, [(i, i ^ mask) for i in range(size)])  28.3 us
    pallas_call x8, Pallas kernels, in_order(): pl.pallas_call(order_kernel, grid_spec=pltpu.PrefetchScalarGridSpec(num_s...  22.2 us
    pallas_call x2, Pallas kernels, update(): pl.pallas_call(functools.partial(update_kernel, count), grid_spec=pltpu.P...  21.4 us
    convert_element_type x1, other arithmetic, body(): d_up = (deriv * gate * sigma).astype(jnp.bfloat16)  16.3 us
  transfers between devices with their start and end apart: 32, of which 13 were waited for; matrix products, arithmetic and copies ran while one was open for 5% of the time, Pallas kernels for 20%

profile of v5, /device:TPU:8, one launch (start us, length us, event | category | flops | bytes accessed | tf_op | source)
XLA Modules:
  0.0 571.3 jit_solution(3509481588868481213)
XLA Ops:
  0.7 1.2 broadcast_select_fusion
  1.9 2.7 collective-permute-start
  6.5 4.1 reshape.93.gate_ref
  10.6 2.2 reshape.94.up_ref
  12.8 6.2 %hidden_rows.2 = (bf16[1024,1024]{1,0:T(8,128)(2,1)}, bf16[512,1024]{1,0:T(8,128)(2,1)}, bf16[512,1024]{1,0:T(8,128)(2,1)}, bf16[512,1024]{1,0:T(8,128)(2,1)}, bf16[512,1024]{1,0:T(8,128)(2,1)}) custom-call(bf16[1024,1024]{1,0:T(8,128)(2,1)} %reshape.93.gate_ref, bf16[1024,1024]{1,0:T(8,128)(2,1)} %reshape.94.up_ref, s32[1,1024]{1,0:T(1,128)} %reshape.95.named_ref), custom_call_target="tpu_custom_call" | custom-call | flops 1073741824 | bytes 10485760 | tf_op jit(solution)/shard_map/hidden_rows/pallas_call | solution.py:88
  19.0 2.2 collective-permute-done.4
  21.9 1.8 side_by_side.11
  23.7 1.8 side_by_side.8
  25.5 3.4 collective-permute-start.14
  28.9 51.7 %collective-permute-done.1.theirs_ref = bf16[2,64,1536]{2,1,0:T(8,128)(2,1)S(1)} collective-permute-done((bf16[2,64,1536]{2,1,0:T(8,128)(2,1)}, bf16[2,64,1536]{2,1,0:T(8,128)(2,1)S(1)}, u32[]{:S(2)}, u32[]{:S(2)}) %collective-permute-start.1) | collective-permute-done | bytes 393248 | tf_op jit(solution)/shard_map/ppermute | solution.py:22
  81.3 2.0 side_by_side.9
  83.3 1.2 collective-permute-start.8
  84.6 41.2 %collective-permute-done.5.theirs_ref = bf16[2,64,1536]{2,1,0:T(8,128)(2,1)S(1)} collective-permute-done((bf16[2,64,1536]{2,1,0:T(8,128)(2,1)}, bf16[2,64,1536]{2,1,0:T(8,128)(2,1)S(1)}, u32[]{:S(2)}, u32[]{:S(2)}) %collective-permute-start.5) | collective-permute-done | bytes 393248 | tf_op jit(solution)/shard_map/ppermute | solution.py:22
  126.5 2.0 side_by_side.12
  128.5 1.2 collective-permute-start.17
  129.7 1.5 collective-permute-start.2
  131.8 1.5 collective-permute-start.9
  133.3 6.1 %fusion.8 = (bf16[8,384,512]{2,1,0:T(8,128)(2,1)}, bf16[8,384,512]{2,1,0:T(8,128)(2,1)}) fusion(bf16[8,384,1024]{2,1,0:T(8,128)(2,1)} %bitcast.23), kind=kLoop, calls=%fused_computation.19 | loop fusion | bytes 12582912 | tf_op jit(solution)/shard_map/split | solution.py:294
  139.3 6.7 %all-to-all-start = ((bf16[8,384,512]{2,1,0:T(8,128)(2,1)}), bf16[8,384,512]{2,1,0:T(8,128)(2,1)}, u32[]{:S(2)}, u32[]{:S(2)}) async-start(bf16[8,384,512]{2,1,0:T(8,128)(2,1)} %get-tuple-element.45), calls=%async_computation | async-start | bytes 6291456 | tf_op jit(solution)/shard_map/all_to_all | solution.py:299
  146.1 2.2 collective-permute-done.17.mine_ref
  148.3 1.3 collective-permute-start.18
  149.5 16.8 %collective-permute-done.2.theirs_ref = bf16[4,64,1536]{2,1,0:T(8,128)(2,1)S(1)} collective-permute-done((bf16[4,64,1536]{2,1,0:T(8,128)(2,1)}, bf16[4,64,1536]{2,1,0:T(8,128)(2,1)S(1)}, u32[]{:S(2)}, u32[]{:S(2)}) %collective-permute-start.2) | collective-permute-done | bytes 786464 | tf_op jit(solution)/shard_map/ppermute | solution.py:22
  167.3 3.7 side_by_side.10
  170.9 38.5 %collective-permute-done.9.theirs_ref = bf16[4,64,1536]{2,1,0:T(8,128)(2,1)S(1)} collective-permute-done((bf16[4,64,1536]{2,1,0:T(8,128)(2,1)S(1)}, bf16[4,64,1536]{2,1,0:T(8,128)(2,1)S(1)}, u32[]{:S(2)}, u32[]{:S(2)}) %collective-permute-start.9) | collective-permute-done | bytes 786464 | tf_op jit(solution)/shard_map/ppermute | solution.py:22
  209.4 0.9 copy-done.15
  210.3 3.6 side_by_side.14
  213.9 1.0 copy-done.2
  215.8 3.7 side_by_side.13
  219.4 14.1 %collective-permute-done.18.theirs_ref = bf16[4,64,1536]{2,1,0:T(8,128)(2,1)} collective-permute-done((bf16[4,64,1536]{2,1,0:T(8,128)(2,1)}, bf16[4,64,1536]{2,1,0:T(8,128)(2,1)}, u32[]{:S(2)}, u32[]{:S(2)}) %collective-permute-start.18) | collective-permute-done | bytes 786464 | tf_op jit(solution)/shard_map/ppermute | solution.py:22
  233.5 3.7 side_by_side.15
  237.7 4.7 hidden_rows.3
  243.2 1.2 copy-done
  244.9 5.4 group_terms.8.refs_0_
  250.3 5.4 group_terms.11
  255.7 5.4 group_terms.10
  261.1 5.4 group_terms.9
  266.5 1.3 collective-permute-done.15.refs_6_
  267.8 8.0 %hidden_deriv.4 = f32[512,1024]{1,0:T(8,128)} custom-call(s32[1]{0:T(128)} %bitcast.place_ref, bf16[512,1536]{1,0:T(8,128)(2,1)} %copy-done, bf16[512,1536]{1,0:T(8,128)(2,1)} %collective-permute-done.7.far_ref, bf16[3072,1024]{1,0:T(8,128)(2,1)} %bitcast.24, bf16[3072,1024]{1,0:T(8,128)(2,1)} %bitcast.25), custom_call_target="tpu_custom_call" | custom-call | flops 3221225472 | bytes 11534336 | tf_op jit(solution)/shard_map/hidden_deriv/pallas_call | solution.py:153
  275.8 7.9 %hidden_deriv.6 = f32[512,1024]{1,0:T(8,128)} custom-call(s32[1]{0:T(128)} %bitcast.place_ref, bf16[512,1536]{1,0:T(8,128)(2,1)} %copy-done.1, bf16[512,1536]{1,0:T(8,128)(2,1)} %collective-permute-done.19.far_ref, bf16[3072,1024]{1,0:T(8,128)(2,1)} %bitcast.26, bf16[3072,1024]{1,0:T(8,128)(2,1)} %bitcast.27), custom_call_target="tpu_custom_call" | custom-call | flops 3221225472 | bytes 11534336 | tf_op jit(solution)/shard_map/hidden_deriv/pallas_call | solution.py:153
  283.8 0.9 collective-permute-start.20
  284.6 7.9 %hidden_deriv.7 = f32[512,1024]{1,0:T(8,128)} custom-call(s32[1]{0:T(128)} %bitcast.place_ref, bf16[512,1536]{1,0:T(8,128)(2,1)} %bitcast.47, bf16[512,1536]{1,0:T(8,128)(2,1)} %bitcast.55, bf16[3072,1024]{1,0:T(8,128)(2,1)} %bitcast.28, bf16[3072,1024]{1,0:T(8,128)(2,1)} %bitcast.29), custom_call_target="tpu_custom_call" | custom-call | flops 3221225472 | bytes 11534336 | tf_op jit(solution)/shard_map/hidden_deriv/pallas_call | solution.py:153
  292.5 1.2 collective-permute-start.21
  293.7 0.9 collective-permute-start.23
  295.4 1.2 collective-permute-done.22.refs_5_
  296.6 1.5 collective-permute-start.24
  298.1 100.6 %collective-permute-done.23.refs_7_ = bf16[512,1024]{1,0:T(8,128)(2,1)S(1)} collective-permute-done((bf16[512,1024]{1,0:T(8,128)(2,1)}, bf16[512,1024]{1,0:T(8,128)(2,1)S(1)}, u32[]{:S(2)}, u32[]{:S(2)}) %collective-permute-start.23) | collective-permute-done | bytes 1048608 | tf_op jit(solution)/shard_map/ppermute | solution.py:22
  398.7 2.4 collective-permute-start.25
  401.1 5.4 group_terms.15
  406.5 5.4 group_terms.14
  411.9 5.4 group_terms.13
  417.3 5.4 group_terms.12.refs_4_
  422.7 7.9 %hidden_deriv.5 = f32[512,1024]{1,0:T(8,128)} custom-call(s32[1]{0:T(128)} %bitcast.place_ref, bf16[512,1536]{1,0:T(8,128)(2,1)} %bitcast.41, bf16[512,1536]{1,0:T(8,128)(2,1)} %bitcast.53, bf16[3072,1024]{1,0:T(8,128)(2,1)} %bitcast.30, bf16[3072,1024]{1,0:T(8,128)(2,1)} %bitcast.31), custom_call_target="tpu_custom_call" | custom-call | flops 3221225472 | bytes 11534336 | tf_op jit(solution)/shard_map/hidden_deriv/pallas_call | solution.py:153
  430.5 4.6 all-to-all-start.1
  435.2 1.5 collective-permute-start.26
  437.0 1.6 collective-permute-start.28
  438.7 1.5 collective-permute-start.29
  440.1 16.3 %fusion.7 = (bf16[512,2,1024]{2,1,0:T(2,128)(2,1)}, bf16[512,2,1024]{2,1,0:T(2,128)(2,1)}) fusion(bf16[512,2,1024]{2,1,0:T(2,128)(2,1)} %param.7, pred[512,2]{1,0:T(8,128)(4,1)S(1)} %copy.21, pred[512,2]{1,0:T(8,128)(4,1)S(1)} %copy.20, pred[512,2]{1,0:T(8,128)(4,1)S(1)} %copy.19, pred[512,2]{1,0:T(8,128)(4,1)S(1)} %copy.17, ...), kind=kLoop, calls=%fused_computation.10 | loop fusion | flops 19922944 | bytes 16781312 | tf_op jit(solution)/shard_map/convert_element_type | solution.py:319
  456.4 57.8 %collective-permute-done.26.refs_3_ = bf16[384,1024]{1,0:T(8,128)(2,1)S(1)} collective-permute-done((bf16[384,1024]{1,0:T(8,128)(2,1)}, bf16[384,1024]{1,0:T(8,128)(2,1)S(1)}, u32[]{:S(2)}, u32[]{:S(2)}) %collective-permute-start.26) | collective-permute-done | bytes 786464 | tf_op jit(solution)/shard_map/ppermute | solution.py:22
  514.2 8.3 %collective-permute-done.28.refs_6_ = bf16[384,1024]{1,0:T(8,128)(2,1)S(1)} collective-permute-done((bf16[384,1024]{1,0:T(8,128)(2,1)}, bf16[384,1024]{1,0:T(8,128)(2,1)S(1)}, u32[]{:S(2)}, u32[]{:S(2)}) %collective-permute-start.28) | collective-permute-done | bytes 786464 | tf_op jit(solution)/shard_map/ppermute | solution.py:22
  522.5 24.9 %collective-permute-done.29.refs_7_ = bf16[384,1024]{1,0:T(8,128)(2,1)S(1)} collective-permute-done((bf16[384,1024]{1,0:T(8,128)(2,1)}, bf16[384,1024]{1,0:T(8,128)(2,1)S(1)}, u32[]{:S(2)}, u32[]{:S(2)}) %collective-permute-start.29) | collective-permute-done | bytes 786464 | tf_op jit(solution)/shard_map/ppermute | solution.py:22
  547.5 0.9 copy-done.10
  548.3 10.7 %lion_step.2 = (f32[1,384,8192]{2,1,0:T(8,128)}, bf16[1,384,8192]{2,1,0:T(8,128)(2,1)}) custom-call(s32[1]{0:T(128)} %bitcast.21.place_ref, bf16[8,384,512]{2,1,0:T(8,128)(2,1)} %all-to-all-done.weight_ref, bf16[1,384,8192]{2,1,0:T(8,128)(2,1)} %momentum_ref.3, bf16[384,1024]{1,0:T(8,128)(2,1)} %group_terms.8.refs_0_, ...), custom_call_target="tpu_custom_call" | custom-call | flops 15728640 | bytes 18874368 | tf_op jit(solution)/shard_map/lion_step/pallas_call | solution.py:201
  559.0 1.6 copy-done.5
  560.6 10.7 %lion_step.3 = (f32[1,384,8192]{2,1,0:T(8,128)}, bf16[1,384,8192]{2,1,0:T(8,128)(2,1)}) custom-call(s32[1]{0:T(128)} %bitcast.21.place_ref, bf16[8,384,512]{2,1,0:T(8,128)(2,1)} %copy-done.5, bf16[1,384,8192]{2,1,0:T(8,128)(2,1)} %momentum_ref.3, bf16[384,1024]{1,0:T(8,128)(2,1)} %group_terms.8.refs_0_, ...), custom_call_target="tpu_custom_call", output_to_operand_aliasing={{0}: (11, {}), {1}: (12, {})} | custom-call | flops 15728640 | bytes 18874368 | tf_op jit(solution)/shard_map/lion_step/pallas_call | solution.py:201
  (79 shorter events, 9.5 us)
Async XLA Ops:
  0.6 10.0 %copy-start.6 = (bf16[512,2,1024]{2,1,0:T(2,128)(2,1)S(1)}, bf16[512,2,1024]{2,1,0:T(2,128)(2,1)}, u32[]{:S(2)}) copy-start(bf16[512,2,1024]{2,1,0:T(2,128)(2,1)} %param.8) | copy-start | bytes 6291460
  1.9 10.9 %copy-start.11 = (bf16[64,1536]{1,0:T(8,128)(2,1)}, bf16[64,1536]{1,0:T(8,128)(2,1)S(1)}, u32[]{:S(2)}) copy-start(bf16[64,1536]{1,0:T(8,128)(2,1)S(1)} %get-tuple-element.63) | copy-start | bytes 589828
  1.9 10.9 %copy-start.12 = (bf16[64,1536]{1,0:T(8,128)(2,1)}, bf16[64,1536]{1,0:T(8,128)(2,1)S(1)}, u32[]{:S(2)}) copy-start(bf16[64,1536]{1,0:T(8,128)(2,1)S(1)} %get-tuple-element.62) | copy-start | bytes 589828
  1.9 19.3 %collective-permute-start = (bf16[64,1536]{1,0:T(8,128)(2,1)S(1)}, bf16[64,1536]{1,0:T(8,128)(2,1)S(1)}, u32[]{:S(2)}, u32[]{:S(2)}) collective-permute-start(bf16[64,1536]{1,0:T(8,128)(2,1)S(1)} %get-tuple-element.62), channel_id=1, source_target_pairs={{0,4},{1,5},{2,6},{3,7},{4,0},{5,1},{6,2},{7,3},{8,12},{9,13},{10,... | collective-permute-start | bytes 589832 | tf_op jit(solution)/shard_map/ppermute | solution.py:22
  4.5 16.7 %collective-permute-start.4 = (bf16[64,1536]{1,0:T(8,128)(2,1)S(1)}, bf16[64,1536]{1,0:T(8,128)(2,1)S(1)}, u32[]{:S(2)}, u32[]{:S(2)}) collective-permute-start(bf16[64,1536]{1,0:T(8,128)(2,1)S(1)} %get-tuple-element.63), channel_id=1, source_target_pairs={{0,4},{1,5},{2,6},{3,7},{4,0},{5,1},{6,2},{7,3},{8,12},{9,13},{10,... | collective-permute-start | bytes 589832 | tf_op jit(solution)/shard_map/ppermute | solution.py:22
  21.2 0.7 copy-start.19
  21.2 2.5 copy-start.18
  25.5 106.3 %collective-permute-start.14 = (bf16[1024,1024]{1,0:T(8,128)(2,1)}, bf16[1024,1024]{1,0:T(8,128)(2,1)}, u32[]{:S(2)}, u32[]{:S(2)}) collective-permute-start(bf16[1024,1024]{1,0:T(8,128)(2,1)} %get-tuple-element.40), channel_id=1, source_target_pairs={{0,4},{1,5},{2,6},{3,7},{4,0},{5,1},{6,2},{7,3},{8,12},{9,13},{10,... | collective-permute-start | bytes 6291464 | tf_op jit(solution)/shard_map/ppermute | solution.py:22
  28.9 51.7 %collective-permute-start.1 = (bf16[2,64,1536]{2,1,0:T(8,128)(2,1)}, bf16[2,64,1536]{2,1,0:T(8,128)(2,1)S(1)}, u32[]{:S(2)}, u32[]{:S(2)}) collective-permute-start(bf16[2,64,1536]{2,1,0:T(8,128)(2,1)} %bitcast.64), channel_id=1, source_target_pairs={{0,2},{1,3},{2,0},{3,1},{4,6},{5,7},{6,4},{7,5},{8,10},{9,11},{10,... | collective-permute-start | bytes 1179656 | tf_op jit(solution)/shard_map/ppermute | solution.py:22
  80.6 0.7 copy-start.16
  83.3 47.9 %collective-permute-start.8 = (bf16[4,64,1536]{2,1,0:T(8,128)(2,1)}, bf16[4,64,1536]{2,1,0:T(8,128)(2,1)S(1)}, u32[]{:S(2)}, u32[]{:S(2)}) collective-permute-start(bf16[4,64,1536]{2,1,0:T(8,128)(2,1)} %bitcast.59), channel_id=1, source_target_pairs={{0,16},{8,24},{16,0},{24,8},{1,17},{9,25},{17,1},{25,9},{2,18},{10... | collective-permute-start | bytes 2359304 | tf_op jit(solution)/shard_map/ppermute | solution.py:22
  84.6 41.2 %collective-permute-start.5 = (bf16[2,64,1536]{2,1,0:T(8,128)(2,1)}, bf16[2,64,1536]{2,1,0:T(8,128)(2,1)S(1)}, u32[]{:S(2)}, u32[]{:S(2)}) collective-permute-start(bf16[2,64,1536]{2,1,0:T(8,128)(2,1)} %bitcast.62), channel_id=1, source_target_pairs={{0,2},{1,3},{2,0},{3,1},{4,6},{5,7},{6,4},{7,5},{8,10},{9,11},{10,... | collective-permute-start | bytes 1179656 | tf_op jit(solution)/shard_map/ppermute | solution.py:22
  84.6 129.3 %collective-permute-start.11 = (bf16[512,1024]{1,0:T(8,128)(2,1)}, bf16[512,1024]{1,0:T(8,128)(2,1)S(1)}, u32[]{:S(2)}, u32[]{:S(2)}) collective-permute-start(bf16[512,1024]{1,0:T(8,128)(2,1)} %get-tuple-element.37), channel_id=1, source_target_pairs={{0,8},{8,0},{16,24},{24,16},{1,9},{9,1},{17,25},{25,17},{2,10},{10... | collective-permute-start | bytes 3145736 | tf_op jit(solution)/shard_map/ppermute | solution.py:22
  125.7 0.7 copy-start.17
  128.5 19.8 %collective-permute-start.17 = (bf16[4,64,1536]{2,1,0:T(8,128)(2,1)}, bf16[4,64,1536]{2,1,0:T(8,128)(2,1)}, u32[]{:S(2)}, u32[]{:S(2)}) collective-permute-start(bf16[4,64,1536]{2,1,0:T(8,128)(2,1)} %bitcast.56), channel_id=1, source_target_pairs={{0,16},{8,24},{16,0},{24,8},{1,17},{9,25},{17,1},{25,9},{2,18},{10... | collective-permute-start | bytes 2359304 | tf_op jit(solution)/shard_map/ppermute | solution.py:22
  129.7 36.7 %collective-permute-start.2 = (bf16[4,64,1536]{2,1,0:T(8,128)(2,1)}, bf16[4,64,1536]{2,1,0:T(8,128)(2,1)S(1)}, u32[]{:S(2)}, u32[]{:S(2)}) collective-permute-start(bf16[4,64,1536]{2,1,0:T(8,128)(2,1)} %bitcast.60), channel_id=1, source_target_pairs={{0,1},{1,0},{2,3},{3,2},{4,5},{5,4},{6,7},{7,6},{8,9},{9,8},{10,11... | collective-permute-start | bytes 2359304 | tf_op jit(solution)/shard_map/ppermute | solution.py:22
  131.2 8.1 %copy-start.13 = (bf16[4,64,1536]{2,1,0:T(8,128)(2,1)}, bf16[4,64,1536]{2,1,0:T(8,128)(2,1)S(1)}, u32[]{:S(2)}) copy-start(bf16[4,64,1536]{2,1,0:T(8,128)(2,1)S(1)} %collective-permute-done.8.mine_ref) | copy-start | bytes 2359300
  131.3 84.1 %collective-permute-start.6 = (bf16[4,64,1536]{2,1,0:T(8,128)(2,1)}, bf16[4,64,1536]{2,1,0:T(8,128)(2,1)}, u32[]{:S(2)}, u32[]{:S(2)}) collective-permute-start(bf16[4,64,1536]{2,1,0:T(8,128)(2,1)} %bitcast.57), channel_id=1, source_target_pairs={{0,1},{1,0},{2,3},{3,2},{4,5},{5,4},{6,7},{7,6},{8,9},{9,8},{10,11... | collective-permute-start | bytes 2359304 | tf_op jit(solution)/shard_map/ppermute | solution.py:22
  131.8 77.6 %collective-permute-start.9 = (bf16[4,64,1536]{2,1,0:T(8,128)(2,1)S(1)}, bf16[4,64,1536]{2,1,0:T(8,128)(2,1)S(1)}, u32[]{:S(2)}, u32[]{:S(2)}) collective-permute-start(bf16[4,64,1536]{2,1,0:T(8,128)(2,1)S(1)} %collective-permute-done.8.mine_ref), channel_id=1, source_target_pairs={{0,1},{1,0},{2,3},{3,2},{4,5},{5,4},{6,7},{7,6},{8,9},{9,8},{10,11... | collective-permute-start | bytes 2359304 | tf_op jit(solution)/shard_map/ppermute | solution.py:22
  139.3 291.2 %all-to-all-start = ((bf16[8,384,512]{2,1,0:T(8,128)(2,1)}), bf16[8,384,512]{2,1,0:T(8,128)(2,1)}, u32[]{:S(2)}, u32[]{:S(2)}) async-start(bf16[8,384,512]{2,1,0:T(8,128)(2,1)} %get-tuple-element.45), calls=%async_computation | async-start | bytes 6291456 | tf_op jit(solution)/shard_map/all_to_all | solution.py:299
  148.3 85.2 %collective-permute-start.18 = (bf16[4,64,1536]{2,1,0:T(8,128)(2,1)}, bf16[4,64,1536]{2,1,0:T(8,128)(2,1)}, u32[]{:S(2)}, u32[]{:S(2)}) collective-permute-start(bf16[4,64,1536]{2,1,0:T(8,128)(2,1)} %collective-permute-done.17.mine_ref), channel_id=1, source_target_pairs={{0,1},{1,0},{2,3},{3,2},{4,5},{5,4},{6,7},{7,6},{8,9},{9,8},{10,11... | collective-permute-start | bytes 2359304 | tf_op jit(solution)/shard_map/ppermute | solution.py:22
  166.4 0.9 copy-start.14
  166.4 70.8 %collective-permute-start.12 = (bf16[512,1024]{1,0:T(8,128)(2,1)}, bf16[512,1024]{1,0:T(8,128)(2,1)}, u32[]{:S(2)}, u32[]{:S(2)}) collective-permute-start(bf16[512,1024]{1,0:T(8,128)(2,1)} %get-tuple-element.38), channel_id=1, source_target_pairs={{0,16},{8,24},{16,0},{24,8},{1,17},{9,25},{17,1},{25,9},{2,18},{10... | collective-permute-start | bytes 3145736 | tf_op jit(solution)/shard_map/ppermute | solution.py:22
  209.4 0.9 copy-start.15
  210.2 33.0 %collective-permute-start.3 = (bf16[512,1536]{1,0:T(8,128)(2,1)}, bf16[512,1536]{1,0:T(8,128)(2,1)S(1)}, u32[]{:S(2)}, u32[]{:S(2)}) collective-permute-start(bf16[512,1536]{1,0:T(8,128)(2,1)} %bitcast.32), channel_id=1, source_target_pairs={{0,8},{8,0},{16,24},{24,16},{1,9},{9,1},{17,25},{25,17},{2,10},{10... | collective-permute-start | bytes 4718600 | tf_op jit(solution)/shard_map/ppermute | solution.py:22
  213.9 1.0 copy-start.2
  214.9 28.4 %collective-permute-start.10 = (bf16[512,1536]{1,0:T(8,128)(2,1)}, bf16[512,1536]{1,0:T(8,128)(2,1)S(1)}, u32[]{:S(2)}, u32[]{:S(2)}) collective-permute-start(bf16[512,1536]{1,0:T(8,128)(2,1)} %bitcast.42), channel_id=1, source_target_pairs={{0,8},{8,0},{16,24},{24,16},{1,9},{9,1},{17,25},{25,17},{2,10},{10... | collective-permute-start | bytes 4718600 | tf_op jit(solution)/shard_map/ppermute | solution.py:22
  215.4 27.0 %collective-permute-start.13 = (bf16[512,1024]{1,0:T(8,128)(2,1)}, bf16[512,1024]{1,0:T(8,128)(2,1)}, u32[]{:S(2)}, u32[]{:S(2)}) collective-permute-start(bf16[512,1024]{1,0:T(8,128)(2,1)} %get-tuple-element.39), channel_id=1, source_target_pairs={{0,24},{8,16},{16,8},{24,0},{1,25},{9,17},{17,9},{25,1},{2,26},{10... | collective-permute-start | bytes 3145736 | tf_op jit(solution)/shard_map/ppermute | solution.py:22
  233.5 34.3 %collective-permute-start.7 = (bf16[512,1536]{1,0:T(8,128)(2,1)}, bf16[512,1536]{1,0:T(8,128)(2,1)}, u32[]{:S(2)}, u32[]{:S(2)}) collective-permute-start(bf16[512,1536]{1,0:T(8,128)(2,1)} %bitcast.52), channel_id=1, source_target_pairs={{0,8},{8,0},{16,24},{24,16},{1,9},{9,1},{17,25},{25,17},{2,10},{10... | collective-permute-start | bytes 4718600 | tf_op jit(solution)/shard_map/ppermute | solution.py:22
  237.2 38.7 %collective-permute-start.19 = (bf16[512,1536]{1,0:T(8,128)(2,1)}, bf16[512,1536]{1,0:T(8,128)(2,1)}, u32[]{:S(2)}, u32[]{:S(2)}) collective-permute-start(bf16[512,1536]{1,0:T(8,128)(2,1)} %bitcast.54), channel_id=1, source_target_pairs={{0,8},{8,0},{16,24},{24,16},{1,9},{9,1},{17,25},{25,17},{2,10},{10... | collective-permute-start | bytes 4718600 | tf_op jit(solution)/shard_map/ppermute | solution.py:22
  242.4 25.5 %collective-permute-start.15 = (bf16[512,1024]{1,0:T(8,128)(2,1)}, bf16[512,1024]{1,0:T(8,128)(2,1)}, u32[]{:S(2)}, u32[]{:S(2)}) collective-permute-start(bf16[512,1024]{1,0:T(8,128)(2,1)} %get-tuple-element.41), channel_id=1, source_target_pairs={{0,16},{8,24},{16,0},{24,8},{1,17},{9,25},{17,1},{25,9},{2,18},{10... | collective-permute-start | bytes 3145736 | tf_op jit(solution)/shard_map/ppermute | solution.py:22
  243.2 1.2 copy-start
  243.2 1.7 copy-start.1
  275.8 160.8 %collective-permute-start.16 = (f32[512,1024]{1,0:T(8,128)}, f32[512,1024]{1,0:T(8,128)}, u32[]{:S(2)}, u32[]{:S(2)}) collective-permute-start(f32[512,1024]{1,0:T(8,128)} %hidden_deriv.4), channel_id=1, source_target_pairs={{0,8},{8,0},{16,24},{24,16},{1,9},{9,1},{17,25},{25,17},{2,10},{10... | collective-permute-start | bytes 6291464 | tf_op jit(solution)/shard_map/ppermute | solution.py:22
  283.8 10.9 %copy-start.20 = (s32[512,2]{0,1:T(2,128)S(1)}, s32[512,2]{0,1:T(2,128)}, u32[]{:S(2)}) copy-start(s32[512,2]{0,1:T(2,128)} %param.9) | copy-start | bytes 12292
  283.8 153.3 %collective-permute-start.20 = (f32[512,1024]{1,0:T(8,128)}, f32[512,1024]{1,0:T(8,128)}, u32[]{:S(2)}, u32[]{:S(2)}) collective-permute-start(f32[512,1024]{1,0:T(8,128)} %hidden_deriv.6), channel_id=1, source_target_pairs={{0,24},{8,16},{16,8},{24,0},{1,25},{9,17},{17,9},{25,1},{2,26},{10... | collective-permute-start | bytes 6291464 | tf_op jit(solution)/shard_map/ppermute | solution.py:22
  292.5 146.2 %collective-permute-start.21 = (f32[512,1024]{1,0:T(8,128)}, f32[512,1024]{1,0:T(8,128)}, u32[]{:S(2)}, u32[]{:S(2)}) collective-permute-start(f32[512,1024]{1,0:T(8,128)} %hidden_deriv.7), channel_id=1, source_target_pairs={{0,16},{8,24},{16,0},{24,8},{1,17},{9,25},{17,1},{25,9},{2,18},{10... | collective-permute-start | bytes 6291464 | tf_op jit(solution)/shard_map/ppermute | solution.py:22
  293.7 2.9 collective-permute-start.22
  293.7 105.0 %collective-permute-start.23 = (bf16[512,1024]{1,0:T(8,128)(2,1)}, bf16[512,1024]{1,0:T(8,128)(2,1)S(1)}, u32[]{:S(2)}, u32[]{:S(2)}) collective-permute-start(bf16[512,1024]{1,0:T(8,128)(2,1)} %get-tuple-element.48), channel_id=1, source_target_pairs={{0,24},{8,16},{16,8},{24,0},{1,25},{9,17},{17,9},{25,1},{2,26},{10... | collective-permute-start | bytes 3145736 | tf_op jit(solution)/shard_map/ppermute | solution.py:22
  296.6 104.5 %copy-start.3 = (bf16[512,1024]{1,0:T(8,128)(2,1)}, bf16[512,1024]{1,0:T(8,128)(2,1)S(1)}, u32[]{:S(2)}) copy-start(bf16[512,1024]{1,0:T(8,128)(2,1)S(1)} %collective-permute-done.22.refs_5_) | copy-start | bytes 3145732
  296.6 138.6 %collective-permute-start.24 = (bf16[384,1024]{1,0:T(8,128)(2,1)}, bf16[384,1024]{1,0:T(8,128)(2,1)}, u32[]{:S(2)}, u32[]{:S(2)}) collective-permute-start(bf16[384,1024]{1,0:T(8,128)(2,1)} %group_terms.9), channel_id=1, source_target_pairs={{0,1},{1,0},{2,3},{3,2},{4,5},{5,4},{6,7},{7,6},{8,9},{9,8},{10,11... | collective-permute-start | bytes 2359304 | tf_op jit(solution)/shard_map/ppermute | solution.py:22
  398.7 2.4 copy-start.4
  398.7 57.7 %collective-permute-start.25 = (bf16[384,1024]{1,0:T(8,128)(2,1)}, bf16[384,1024]{1,0:T(8,128)(2,1)}, u32[]{:S(2)}, u32[]{:S(2)}) collective-permute-start(bf16[384,1024]{1,0:T(8,128)(2,1)} %group_terms.10), channel_id=1, source_target_pairs={{0,2},{1,3},{2,0},{3,1},{4,6},{5,7},{6,4},{7,5},{8,10},{9,11},{10,... | collective-permute-start | bytes 2359304 | tf_op jit(solution)/shard_map/ppermute | solution.py:22
  430.5 128.5 %all-to-all-start.1 = ((bf16[8,384,512]{2,1,0:T(8,128)(2,1)}), bf16[8,384,512]{2,1,0:T(8,128)(2,1)S(1)}, u32[]{:S(2)}, u32[]{:S(2)}) async-start(bf16[8,384,512]{2,1,0:T(8,128)(2,1)} %get-tuple-element.49), calls=%async_computation.1 | async-start | bytes 6291456 | tf_op jit(solution)/shard_map/all_to_all | solution.py:299
  435.2 79.0 %collective-permute-start.26 = (bf16[384,1024]{1,0:T(8,128)(2,1)}, bf16[384,1024]{1,0:T(8,128)(2,1)S(1)}, u32[]{:S(2)}, u32[]{:S(2)}) collective-permute-start(bf16[384,1024]{1,0:T(8,128)(2,1)} %group_terms.11), channel_id=1, source_target_pairs={{0,3},{1,2},{2,1},{3,0},{4,7},{5,6},{6,5},{7,4},{8,11},{9,10},{10,... | collective-permute-start | bytes 2359304 | tf_op jit(solution)/shard_map/ppermute | solution.py:22
  436.6 77.6 %collective-permute-start.27 = (bf16[384,1024]{1,0:T(8,128)(2,1)}, bf16[384,1024]{1,0:T(8,128)(2,1)S(1)}, u32[]{:S(2)}, u32[]{:S(2)}) collective-permute-start(bf16[384,1024]{1,0:T(8,128)(2,1)} %group_terms.13), channel_id=1, source_target_pairs={{0,1},{1,0},{2,3},{3,2},{4,5},{5,4},{6,7},{7,6},{8,9},{9,8},{10,11... | collective-permute-start | bytes 2359304 | tf_op jit(solution)/shard_map/ppermute | solution.py:22
  437.0 85.5 %collective-permute-start.28 = (bf16[384,1024]{1,0:T(8,128)(2,1)}, bf16[384,1024]{1,0:T(8,128)(2,1)S(1)}, u32[]{:S(2)}, u32[]{:S(2)}) collective-permute-start(bf16[384,1024]{1,0:T(8,128)(2,1)} %group_terms.14), channel_id=1, source_target_pairs={{0,2},{1,3},{2,0},{3,1},{4,6},{5,7},{6,4},{7,5},{8,10},{9,11},{10,... | collective-permute-start | bytes 2359304 | tf_op jit(solution)/shard_map/ppermute | solution.py:22
  438.7 108.8 %collective-permute-start.29 = (bf16[384,1024]{1,0:T(8,128)(2,1)}, bf16[384,1024]{1,0:T(8,128)(2,1)S(1)}, u32[]{:S(2)}, u32[]{:S(2)}) collective-permute-start(bf16[384,1024]{1,0:T(8,128)(2,1)} %group_terms.15), channel_id=1, source_target_pairs={{0,3},{1,2},{2,1},{3,0},{4,7},{5,6},{6,5},{7,4},{8,11},{9,10},{10,... | collective-permute-start | bytes 2359304 | tf_op jit(solution)/shard_map/ppermute | solution.py:22
  514.2 33.3 %copy-start.7 = (bf16[384,1024]{1,0:T(8,128)(2,1)}, bf16[384,1024]{1,0:T(8,128)(2,1)S(1)}, u32[]{:S(2)}) copy-start(bf16[384,1024]{1,0:T(8,128)(2,1)S(1)} %collective-permute-done.26.refs_3_) | copy-start | bytes 2359300
  514.2 33.3 %copy-start.8 = (bf16[384,1024]{1,0:T(8,128)(2,1)}, bf16[384,1024]{1,0:T(8,128)(2,1)S(1)}, u32[]{:S(2)}) copy-start(bf16[384,1024]{1,0:T(8,128)(2,1)S(1)} %collective-permute-done.27.refs_5_) | copy-start | bytes 2359300
  522.5 24.9 %copy-start.9 = (bf16[384,1024]{1,0:T(8,128)(2,1)}, bf16[384,1024]{1,0:T(8,128)(2,1)S(1)}, u32[]{:S(2)}) copy-start(bf16[384,1024]{1,0:T(8,128)(2,1)S(1)} %collective-permute-done.28.refs_6_) | copy-start | bytes 2359300
  547.4 0.9 copy-start.10
  559.0 1.6 copy-start.5

commit v6 on v5

--- a/solution.py
+++ b/solution.py
@@ -49,18 +49,45 @@
     return both.reshape(2 * count, some, width)
 
 
+def place_kernel(place_ref, *refs):
+    for m, block_ref in enumerate(refs[:-1]):
+        refs[-1][place_ref[0] ^ m] = block_ref[...]
+
+
+def placed_blocks(blocks, place):
+    count = len(blocks)
+    return pl.pallas_call(
+        place_kernel,
+        grid_spec=pltpu.PrefetchScalarGridSpec(
+            num_scalar_prefetch=1,
+            grid=(1,),
+            in_specs=[pl.BlockSpec(blocks[0].shape, lambda i, place: (0, 0))] * count,
+            out_specs=pl.BlockSpec((count,) + blocks[0].shape, lambda i, place: (0, 0, 0)),
+        ),
+        out_shape=jax.ShapeDtypeStruct((count,) + blocks[0].shape, blocks[0].dtype),
+        compiler_params=pltpu.CompilerParams(vmem_limit_bytes=56 * MIB),
+        cost_estimate=pl.CostEstimate(
+            flops=0, bytes_accessed=4 * count * blocks[0].size, transcendentals=0
+        ),
+        name="placed_blocks",
+    )(place.reshape(1), *blocks)
+
+
 def pick(hidden, named_ref, out_refs):
     count_rows = hidden.shape[0]
-    tokens = out_refs[0].shape[0]
+    tokens = out_refs[0].shape[1]
     topk = count_rows // tokens
     token = lax.broadcasted_iota(jnp.int32, (tokens, count_rows), 0)
     row = lax.broadcasted_iota(jnp.int32, (tokens, count_rows), 1)
     here = (row >= token * topk) & (row < token * topk + topk)
-    for m, out_ref in enumerate(out_refs):
-        chosen = jnp.where(here & (named_ref[...] == m), 1.0, 0.0).astype(jnp.bfloat16)
-        out_ref[...] = jnp.dot(chosen, hidden, preferred_element_type=jnp.float32).astype(
-            jnp.bfloat16
-        )
+    m = 0
+    for out_ref in out_refs:
+        for i in range(out_ref.shape[0]):
+            chosen = jnp.where(here & (named_ref[...] == m), 1.0, 0.0).astype(jnp.bfloat16)
+            out_ref[i] = jnp.dot(chosen, hidden, preferred_element_type=jnp.float32).astype(
+                jnp.bfloat16
+            )
+            m += 1
 
 
 def hidden_kernel(gate_ref, up_ref, named_ref, hidden_ref, *out_refs):
@@ -80,8 +107,9 @@
     group_tok = count_rows // topk
     some = 128 if group_tok % 128 == 0 else group_tok
     row_block = pl.BlockSpec((some * topk, cols), lambda i: (i, 0))
-    out_shape = [jax.ShapeDtypeStruct((group_tok, cols), jnp.bfloat16)] * experts
-    out_specs = [pl.BlockSpec((some, cols), lambda i: (i, 0))] * experts
+    sizes = [1] + [1 << b for b in range(experts.bit_length() - 1)]
+    out_shape = [jax.ShapeDtypeStruct((n, group_tok, cols), jnp.bfloat16) for n in sizes]
+    out_specs = [pl.BlockSpec((n, some, cols), lambda i: (0, i, 0)) for n in sizes]
     if with_hidden:
         out_shape = [jax.ShapeDtypeStruct((count_rows, cols), jnp.bfloat16)] + out_shape
         out_specs = [row_block] + out_specs
@@ -101,8 +129,21 @@
     )(*arrays, named)
 
 
+def spread(picked, experts):
+    held = {0: {(1 << i) >> 1: rows for i, rows in enumerate(picked)}}
+    bit = experts // 2
+    while bit:
+        for group in list(held):
+            got = swapped(held[group][bit], "expert", bit)
+            held[group ^ bit] = {0: got[:1]}
+            for i in range(bit.bit_length() - 1):
+                held[group ^ bit][1 << i] = got[1 << i : 2 << i]
+        bit //= 2
+    return [held[m][0][0] for m in range(experts)]
+
+
 def term_kernel(count, place_ref, *refs):
-    tokens, hidden, out_ref = refs[:count], refs[count : 2 * count], refs[-1]
+    tokens, hidden, outs = refs[:count], refs[count : 2 * count], refs[2 * count :]
     total = None
     for token_ref, hidden_ref in zip(tokens, hidden):
         one = lax.dot_general(
@@ -112,10 +153,15 @@
             preferred_element_type=jnp.float32,
         )
         total = one if total is None else total + one
-    out_ref[...] = total.astype(jnp.bfloat16)
-
-
-def terms(tokens, hidden, tall, first, steps):
+    total = total.astype(jnp.bfloat16)
+    for m, out_ref in enumerate(outs):
+
+        @pl.when(pl.program_id(0) == m)
+        def _():
+            out_ref[...] = total
+
+
+def terms(tokens, hidden, tall, steps, block_of, place):
     group_tok, width = tokens[0].shape
     cols = hidden[0].shape[1]
     count = len(tokens)
@@ -124,11 +170,14 @@
         grid_spec=pltpu.PrefetchScalarGridSpec(
             num_scalar_prefetch=1,
             grid=(steps,),
-            in_specs=[pl.BlockSpec((group_tok, tall), lambda i, place: (0, place[0] + i))] * count
-            + [pl.BlockSpec((group_tok, cols), lambda i, place: (0, 0))] * count,
-            out_specs=pl.BlockSpec((tall, cols), lambda i, place: (i, 0)),
-        ),
-        out_shape=jax.ShapeDtypeStruct((steps * tall, cols), jnp.bfloat16),
+            in_specs=[
+                pl.BlockSpec((group_tok, tall), lambda m, place: (0, block_of(place[0], m)))
+            ]
+            * count
+            + [pl.BlockSpec((group_tok, cols), lambda m, place: (0, 0))] * count,
+            out_specs=[pl.BlockSpec((tall, cols), lambda m, place: (0, 0))] * steps,
+        ),
+        out_shape=[jax.ShapeDtypeStruct((tall, cols), jnp.bfloat16)] * steps,
         compiler_params=pltpu.CompilerParams(vmem_limit_bytes=56 * MIB),
         cost_estimate=pl.CostEstimate(
             flops=2 * count * group_tok * steps * tall * cols,
@@ -136,42 +185,36 @@
             transcendentals=0,
         ),
         name="group_terms",
-    )(first.reshape(1), *tokens, *hidden)
-
-
-def deriv_kernel(place_ref, near_ref, far_ref, near_weight_ref, far_weight_ref, out_ref):
+    )(place.reshape(1), *tokens, *hidden)
+
+
+def deriv_kernel(tokens_ref, weight_ref, out_ref):
     out_ref[...] = jnp.dot(
-        near_ref[...], near_weight_ref[...], preferred_element_type=jnp.float32
-    ) + jnp.dot(far_ref[...], far_weight_ref[...], preferred_element_type=jnp.float32)
-
-
-def deriv_of(near, far, weight, half):
-    group_tok, width = near.shape
+        tokens_ref[...], weight_ref[...], preferred_element_type=jnp.float32
+    )
+
+
+def deriv_of(tokens, weight):
+    group_tok, width = tokens.shape
     cols = weight.shape[1]
     wide = 256 if cols % 256 == 0 else cols
-    whole = pl.BlockSpec((group_tok, width), lambda i, place: (0, 0))
     return pl.pallas_call(
         deriv_kernel,
-        grid_spec=pltpu.PrefetchScalarGridSpec(
-            num_scalar_prefetch=1,
-            grid=(cols // wide,),
-            in_specs=[
-                whole,
-                whole,
-                pl.BlockSpec((width, wide), lambda i, place: (place[0], i)),
-                pl.BlockSpec((width, wide), lambda i, place: (1 - place[0], i)),
-            ],
-            out_specs=pl.BlockSpec((group_tok, wide), lambda i, place: (0, i)),
-        ),
+        grid=(cols // wide,),
+        in_specs=[
+            pl.BlockSpec((group_tok, width), lambda i: (0, 0)),
+            pl.BlockSpec((width, wide), lambda i: (0, i)),
+        ],
+        out_specs=pl.BlockSpec((group_tok, wide), lambda i: (0, i)),
         out_shape=jax.ShapeDtypeStruct((group_tok, cols), jnp.float32),
         compiler_params=pltpu.CompilerParams(vmem_limit_bytes=56 * MIB),
         cost_estimate=pl.CostEstimate(
-            flops=4 * group_tok * width * cols,
-            bytes_accessed=4 * (group_tok + cols) * width + 4 * group_tok * cols,
+            flops=2 * group_tok * width * cols,
+            bytes_accessed=2 * (group_tok + cols) * width + 4 * group_tok * cols,
             transcendentals=0,
         ),
         name="hidden_deriv",
-    )(half.reshape(1), near, far, weight, weight)
+    )(tokens, weight)
 
 
 def update_kernel(count, place_ref, weight_ref, momentum_ref, *refs):
@@ -219,26 +262,15 @@
     )(place.reshape(1), weight, momentum, *grads, *done)
 
 
-def first_step(keep, theirs, shards, place):
-    return in_order(keep[None], theirs[None], (place & (shards // 2)) != 0)
-
-
 def gathered(held, experts, shards, place):
-    bit = shards // 2
-    while bit > 2:
-        bit //= 2
-        held = in_order(held, swapped(held, "dp", bit), (place & bit) != 0)
     groups = {0: held}
     for m in sorted(range(2, experts, 2), key=lambda m: (bin(m).count("1"), -m)):
         groups[m] = swapped(groups[m & (m - 1)], "expert", m & -m)
-    if bit > 1:
-        for m in groups:
-            groups[m] = in_order(groups[m], swapped(groups[m], "dp", 1), (place & 1) != 0)
     for m in list(groups):
-        groups[m] = groups[m].reshape(-1, held.shape[2])
-        if experts > 1:
-            groups[m + 1] = swapped(groups[m], "expert", 1)
-    return groups
+        both = in_order(groups[m], swapped(groups[m], "dp", 1), (place & 1) != 0)
+        groups[m] = both.reshape(-1, held.shape[2])
+        groups[m + 1] = swapped(groups[m], "expert", 1)
+    return [groups[m] for m in range(experts)]
 
 
 def body(out_grad, gate_saved, up_saved, routing, down_weight, momentum):
@@ -250,45 +282,44 @@
     mine = lax.axis_index("expert")
     place = lax.axis_index("dp")
     span = shards // 2
-    half = place // span
-    within = place % span
     each = range(experts)
 
-    low, high = out_grad[:, : width // 2], out_grad[:, width // 2 :]
-    near = jnp.where(half == 0, low, high)
-    far = jnp.where(half == 0, high, low)
-    near_theirs = swapped(far, "dp", span)
-    far_theirs = swapped(near, "dp", span)
-
+    blocks = [swapped(out_grad, "dp", m) for m in range(0, shards, 2)]
     named = (routing ^ mine).reshape(1, group_tok * topk)
-    gate_rows, up_rows, *_ = lax.optimization_barrier(
-        (gate_saved.reshape(-1, cols), up_saved.reshape(-1, cols), near, far)
-    )
-    hidden, *own_rows = picked_rows(
-        hidden_kernel, [gate_rows, up_rows], named, experts, topk, True
-    )
-    near_held = first_step(near, after(near_theirs, hidden), shards, place)
-    far_held = first_step(far, after(far_theirs, hidden), shards, place)
-    near_tokens = gathered(near_held, experts, shards, place)
-    far_tokens = gathered(far_held, experts, shards, place)
-    other_hidden = swapped(after(hidden, near_held, far_held), "dp", span)
-    own_rows = [swapped(own_rows[m], "expert", m) for m in each]
-    other_rows = picked_rows(pick_kernel, [other_hidden], named, experts, topk, False)
-    other_rows = [swapped(other_rows[m], "expert", m) for m in each]
-
-    near_list = [near_tokens[m] for m in each]
+    hidden, *own_picked = picked_rows(
+        hidden_kernel,
+        [gate_saved.reshape(-1, cols), up_saved.reshape(-1, cols)],
+        named,
+        experts,
+        topk,
+        True,
+    )
+    held = placed_blocks([after(block, hidden) for block in blocks], place // 2)
+    hidden, own_picked, _ = lax.optimization_barrier((hidden, own_picked, held))
+    other_hidden = swapped(hidden, "dp", span)
+    tokens = gathered(held, experts, shards, place)
+    own_rows = spread(own_picked, experts)
+    other_picked = picked_rows(
+        pick_kernel, [after(other_hidden, tokens)], named, experts, topk, False
+    )
+    other_rows = spread(other_picked, experts)
 
     def shard_terms(hidden_rows):
         if rows % 128 == 0:
-            return [terms(near_list, hidden_rows, rows, within ^ m, 1) for m in range(span)]
+            return terms(tokens, hidden_rows, rows, span, lambda place, m: place ^ m, place)
         tall = width // 8
-        total = terms(near_list, hidden_rows, tall, 0 * within, width // 2 // tall)
+        total = terms(
+            tokens, hidden_rows, tall, 4, lambda place, m: place // span * 4 + m, place
+        )
+        total = jnp.concatenate(total, axis=0)
         return [
-            lax.dynamic_slice_in_dim(total, (within ^ m) * rows, rows, axis=0) for m in range(span)
+            lax.dynamic_slice_in_dim(total, (place % span ^ m) * rows, rows, axis=0)
+            for m in range(span)
         ]
 
     own_terms = shard_terms(own_rows)
     other_terms = shard_terms(other_rows)
+
     weight = down_weight[0]
     parts = 2 if cols % 256 == 0 else 1
     pieces = jnp.split(down_weight.reshape(shards, rows, cols), parts, axis=2)
@@ -306,14 +337,16 @@
         grads[m ^ span] = swapped(other_terms[m], "dp", m)
 
     back_weight, gate_saved, up_saved, *_ = lax.optimization_barrier(
-        (weight, gate_saved, up_saved, own_terms, other_rows[experts // 2])
+        (weight, gate_saved, up_saved, own_terms)
     )
     gate = gate_saved.astype(jnp.float32)
     up = up_saved.astype(jnp.float32)
     sigma = jax.nn.sigmoid(gate)
     deriv = jnp.zeros(gate.shape, jnp.float32)
     for m in list(range(experts // 2, experts)) + list(range(experts // 2)):
-        part = deriv_of(near_tokens[m], far_tokens[m], back_weight, half)
+        part = deriv_of(tokens[m], back_weight)
+        if m >= experts // 2:
+            part = after(part, other_rows[experts // 2])
         chosen = (routing == (mine ^ m))[:, :, None]
         deriv = jnp.where(chosen, swapped(part, "expert", m)[:, None, :], deriv)
     d_up = (deriv * gate * sigma).astype(jnp.bfloat16)

time: 573 us -> 463 us (0.81)
  waiting for transfers between devices: 361 us -> 281 us
  Pallas kernels: 129 us -> 99.3 us
    ppermute x30 -> x24, waiting for transfers between devices: 361 us -> 252 us  [swapped(): return lax.ppermute(array, axis, [(i, i ^ mask) for i in range(size)])]
    all_to_all x2, waiting for transfers between devices: 0.01 us -> 28.8 us  [body(): lax.all_to_all(after(piece, *begun), 'dp', split_axis=0, concat_axis=0, t...]
    pallas_call x8 -> x2, Pallas kernels: 43.2 us -> 24.5 us  [terms(): pl.pallas_call(functools.partial(term_kernel, count), grid_spec=pltpu.Pre...]
    pallas_call x8 -> x2, Pallas kernels: 22.2 us -> 8.31 us  [in_order(): pl.pallas_call(order_kernel, grid_spec=pltpu.PrefetchScalarGridSpec(num_s...]
    ppermute x30 -> x24, starting transfers between devices: 28.3 us -> 25 us  [swapped(): return lax.ppermute(array, axis, [(i, i ^ mask) for i in range(size)])]
    pallas_call x4 -> x5, Pallas kernels: 31.7 us -> 34.2 us  [the longest x4 31.6 us: deriv_of(): pl.pallas_call(deriv_kernel, grid=(cols // wide,), in_specs=[pl.BlockSpec...]
  transfers between devices with their start and end apart: 32 -> 26, of which waited for: 13 -> 12; matrix products, arithmetic and copies ran while one was open for 5% -> 8% of each run, Pallas kernels for 20% -> 19%
where the time goes in v6:
time: 463 us; the launch traced here: 459 us
  waiting for transfers between devices  281 us (61%)
  Pallas kernels  99.3 us (21%)
  starting transfers between devices  37.5 us (8%)
  local copies, waits for them, and re-layouts  23.5 us (5%)
  other arithmetic  16.8 us (4%)
    ppermute x24, waiting for transfers between devices, swapped(): return lax.ppermute(array, axis, [(i, i ^ mask) for i in range(size)])  252 us
    pallas_call x4, Pallas kernels, deriv_of(): pl.pallas_call(deriv_kernel, grid=(cols // wide,), in_specs=[pl.BlockSpec...  31.6 us
    all_to_all x2, waiting for transfers between devices, body(): lax.all_to_all(after(piece, *begun), 'dp', split_axis=0, concat_axis=0, t...  28.8 us
    ppermute x24, starting transfers between devices, swapped(): return lax.ppermute(array, axis, [(i, i ^ mask) for i in range(size)])  25 us
    pallas_call x2, Pallas kernels, terms(): pl.pallas_call(functools.partial(term_kernel, count), grid_spec=pltpu.Pre...  24.5 us
    pallas_call x2, Pallas kernels, update(): pl.pallas_call(functools.partial(update_kernel, count), grid_spec=pltpu.P...  21.4 us
    convert_element_type x1, other arithmetic, body(): d_up = (deriv * gate * sigma).astype(jnp.bfloat16)  16.1 us
    all_to_all x2, starting transfers between devices, body(): lax.all_to_all(after(piece, *begun), 'dp', split_axis=0, concat_axis=0, t...  12.4 us
  transfers between devices with their start and end apart: 26, of which 12 were waited for; matrix products, arithmetic and copies ran while one was open for 8% of the time, Pallas kernels for 19%

profile of v6, /device:TPU:8, one launch (start us, length us, event | category | flops | bytes accessed | tf_op | source)
XLA Modules:
  0.0 459.2 jit_solution(8458532849096169683)
XLA Ops:
  0.6 1.6 collective-permute-start.2
  2.3 1.1 collective-permute-start.1
  3.4 1.4 collective-permute-start
  4.8 0.7 broadcast_xor_fusion
  5.5 0.1 copy.18
  5.6 0.8 reshape.48.named_ref
  6.4 4.1 reshape.46.gate_ref
  10.5 2.2 reshape.47.up_ref
  12.7 6.2 %hidden_rows.2 = (bf16[1024,1024]{1,0:T(8,128)(2,1)}, bf16[1,512,1024]{2,1,0:T(8,128)(2,1)}, bf16[1,512,1024]{2,1,0:T(8,128)(2,1)}, bf16[2,512,1024]{2,1,0:T(8,128)(2,1)}) custom-call(bf16[1024,1024]{1,0:T(8,128)(2,1)} %reshape.46.gate_ref, bf16[1024,1024]{1,0:T(8,128)(2,1)} %reshape.47.up_ref, s32[1,1024]{1,0:T(1,128)} %reshape.48.named_ref), custom_call_target="tpu_custom_call" | custom-call | flops 1073741824 | bytes 10485760 | tf_op jit(solution)/shard_map/hidden_rows/pallas_call | solution.py:116
  18.9 10.7 %collective-permute-done.2.refs_3_ = bf16[64,3072]{1,0:T(8,128)(2,1)S(1)} collective-permute-done((bf16[64,3072]{1,0:T(8,128)(2,1)}, bf16[64,3072]{1,0:T(8,128)(2,1)S(1)}, u32[]{:S(2)}, u32[]{:S(2)}) %collective-permute-start.2) | collective-permute-done | bytes 393248 | tf_op jit(solution)/shard_map/ppermute | solution.py:22
  29.6 6.7 %collective-permute-done.1.refs_2_ = bf16[64,3072]{1,0:T(8,128)(2,1)S(1)} collective-permute-done((bf16[64,3072]{1,0:T(8,128)(2,1)}, bf16[64,3072]{1,0:T(8,128)(2,1)S(1)}, u32[]{:S(2)}, u32[]{:S(2)}) %collective-permute-start.1) | collective-permute-done | bytes 393248 | tf_op jit(solution)/shard_map/ppermute | solution.py:22
  36.3 0.7 copy-done.8
  37.0 0.1 copy-done.9
  37.1 2.6 placed_blocks.1.mine_ref
  39.7 1.5 collective-permute-start.5
  41.2 1.5 collective-permute-start.3
  42.7 32.5 %collective-permute-done.5.mine_ref = bf16[4,64,3072]{2,1,0:T(8,128)(2,1)S(1)} collective-permute-done((bf16[4,64,3072]{2,1,0:T(8,128)(2,1)}, bf16[4,64,3072]{2,1,0:T(8,128)(2,1)S(1)}, u32[]{:S(2)}, u32[]{:S(2)}) %collective-permute-start.5) | collective-permute-done | bytes 1572896 | tf_op jit(solution)/shard_map/ppermute | solution.py:22
  75.2 1.5 collective-permute-start.6
  76.7 0.2 collective-permute-done.3.theirs_ref
  76.9 4.2 side_by_side.2
  81.1 29.0 %collective-permute-done.6.theirs_ref = bf16[4,64,3072]{2,1,0:T(8,128)(2,1)S(1)} collective-permute-done((bf16[4,64,3072]{2,1,0:T(8,128)(2,1)S(1)}, bf16[4,64,3072]{2,1,0:T(8,128)(2,1)S(1)}, u32[]{:S(2)}, u32[]{:S(2)}) %collective-permute-start.6) | collective-permute-done | bytes 1572896 | tf_op jit(solution)/shard_map/ppermute | solution.py:22
  110.1 1.1 copy-done.6
  111.3 4.2 side_by_side.3
  115.4 3.3 collective-permute-start.12
  118.7 1.0 collective-permute-start.9
  119.7 6.0 %fusion.8 = (bf16[8,384,512]{2,1,0:T(8,128)(2,1)}, bf16[8,384,512]{2,1,0:T(8,128)(2,1)}) fusion(bf16[8,384,1024]{2,1,0:T(8,128)(2,1)} %bitcast.17), kind=kLoop, calls=%fused_computation.19 | loop fusion | bytes 12582912 | tf_op jit(solution)/shard_map/split | solution.py:325
  125.7 82.7 %collective-permute-done.12.hidden_ref = bf16[1024,1024]{1,0:T(8,128)(2,1)} collective-permute-done((bf16[1024,1024]{1,0:T(8,128)(2,1)}, bf16[1024,1024]{1,0:T(8,128)(2,1)}, u32[]{:S(2)}, u32[]{:S(2)}) %collective-permute-start.12) | collective-permute-done | bytes 2097184 | tf_op jit(solution)/shard_map/ppermute | solution.py:22
  208.4 7.1 %all-to-all-start = ((bf16[8,384,512]{2,1,0:T(8,128)(2,1)}), bf16[8,384,512]{2,1,0:T(8,128)(2,1)S(1)}, u32[]{:S(2)}, u32[]{:S(2)}) async-start(bf16[8,384,512]{2,1,0:T(8,128)(2,1)} %get-tuple-element.66), calls=%async_computation | async-start | bytes 6291456 | tf_op jit(solution)/shard_map/all_to_all | solution.py:330
  215.5 4.7 %hidden_rows.3 = (bf16[1,512,1024]{2,1,0:T(8,128)(2,1)}, bf16[1,512,1024]{2,1,0:T(8,128)(2,1)}, bf16[2,512,1024]{2,1,0:T(8,128)(2,1)}) custom-call(bf16[1024,1024]{1,0:T(8,128)(2,1)} %collective-permute-done.12.hidden_ref, s32[1,1024]{1,0:T(1,128)} %reshape.48.named_ref), custom_call_target="tpu_custom_call" | custom-call | flops 1073741824 | bytes 8388608 | tf_op jit(solution)/shard_map/hidden_rows/pallas_call | solution.py:116
  220.2 1.2 collective-permute-start.13
  221.5 2.7 fusion.10
  224.1 0.5 collective-permute-start.10
  224.7 42.9 %collective-permute-done.13 = bf16[2,512,1024]{2,1,0:T(8,128)(2,1)S(1)} collective-permute-done((bf16[2,512,1024]{2,1,0:T(8,128)(2,1)}, bf16[2,512,1024]{2,1,0:T(8,128)(2,1)S(1)}, u32[]{:S(2)}, u32[]{:S(2)}) %collective-permute-start.13) | collective-permute-done | bytes 2097184 | tf_op jit(solution)/shard_map/ppermute | solution.py:22
  267.6 1.2 fusion.9
  268.8 1.0 copy-done.13
  269.8 1.0 copy-done.14
  270.8 12.3 %group_terms.2 = (bf16[384,1024]{1,0:T(8,128)(2,1)}, bf16[384,1024]{1,0:T(8,128)(2,1)}, bf16[384,1024]{1,0:T(8,128)(2,1)}, bf16[384,1024]{1,0:T(8,128)(2,1)}) custom-call(s32[1]{0:T(128)} %bitcast.4.place_ref, bf16[512,3072]{1,0:T(8,128)(2,1)} %bitcast.23, bf16[512,3072]{1,0:T(8,128)(2,1)} %collective-permute-done.4.refs_1_.tokens_ref, ...), custom_call_target="tpu_custom_call" | custom-call | flops 6442450944 | bytes 13631488 | tf_op jit(solution)/shard_map/group_terms/pallas_call | solution.py:168
  283.1 1.5 collective-permute-start.18
  284.5 0.5 collective-permute-start.19
  285.1 7.9 %hidden_deriv.4 = f32[512,1024]{1,0:T(8,128)} custom-call(bf16[512,3072]{1,0:T(8,128)(2,1)} %collective-permute-done.4.refs_1_.tokens_ref, bf16[3072,1024]{1,0:T(8,128)(2,1)} %bitcast.18), custom_call_target="tpu_custom_call" | custom-call | flops 3221225472 | bytes 11534336 | tf_op jit(solution)/shard_map/hidden_deriv/pallas_call | solution.py:201
  293.0 7.9 %hidden_deriv.7 = f32[512,1024]{1,0:T(8,128)} custom-call(bf16[512,3072]{1,0:T(8,128)(2,1)} %bitcast.28, bf16[3072,1024]{1,0:T(8,128)(2,1)} %bitcast.19), custom_call_target="tpu_custom_call" | custom-call | flops 3221225472 | bytes 11534336 | tf_op jit(solution)/shard_map/hidden_deriv/pallas_call | solution.py:201
  300.8 7.9 %hidden_deriv.6 = f32[512,1024]{1,0:T(8,128)} custom-call(bf16[512,3072]{1,0:T(8,128)(2,1)} %collective-permute-done.7.refs_3_.tokens_ref, bf16[3072,1024]{1,0:T(8,128)(2,1)} %bitcast.20), custom_call_target="tpu_custom_call" | custom-call | flops 3221225472 | bytes 11534336 | tf_op jit(solution)/shard_map/hidden_deriv/pallas_call | solution.py:201
  308.7 1.2 collective-permute-start.14
  309.9 0.9 collective-permute-start.15
  310.8 12.2 %group_terms.3 = (bf16[384,1024]{1,0:T(8,128)(2,1)}, bf16[384,1024]{1,0:T(8,128)(2,1)}, bf16[384,1024]{1,0:T(8,128)(2,1)}, bf16[384,1024]{1,0:T(8,128)(2,1)}) custom-call(s32[1]{0:T(128)} %bitcast.4.place_ref, bf16[512,3072]{1,0:T(8,128)(2,1)} %bitcast.24, bf16[512,3072]{1,0:T(8,128)(2,1)} %collective-permute-done.4.refs_1_.tokens_ref, ...), custom_call_target="tpu_custom_call" | custom-call | flops 6442450944 | bytes 13631488 | tf_op jit(solution)/shard_map/group_terms/pallas_call | solution.py:168
  323.1 1.6 collective-permute-start.20
  324.6 1.6 collective-permute-start.21
  326.2 17.4 %collective-permute-done.20.refs_3_ = bf16[384,1024]{1,0:T(8,128)(2,1)} collective-permute-done((bf16[384,1024]{1,0:T(8,128)(2,1)}, bf16[384,1024]{1,0:T(8,128)(2,1)}, u32[]{:S(2)}, u32[]{:S(2)}) %collective-permute-start.20) | collective-permute-done | bytes 786464 | tf_op jit(solution)/shard_map/ppermute | solution.py:22
  343.6 1.6 collective-permute-start.22
  345.2 15.1 %collective-permute-done.21.refs_5_ = bf16[384,1024]{1,0:T(8,128)(2,1)} collective-permute-done((bf16[384,1024]{1,0:T(8,128)(2,1)}, bf16[384,1024]{1,0:T(8,128)(2,1)}, u32[]{:S(2)}, u32[]{:S(2)}) %collective-permute-start.21) | collective-permute-done | bytes 786464 | tf_op jit(solution)/shard_map/ppermute | solution.py:22
  360.4 1.5 collective-permute-start.23
  361.9 0.2 copy.17
  362.1 0.2 copy.19
  362.3 0.2 copy.21
  362.5 0.2 copy.20
  362.7 7.9 %hidden_deriv.5 = f32[512,1024]{1,0:T(8,128)} custom-call(bf16[512,3072]{1,0:T(8,128)(2,1)} %bitcast.25, bf16[3072,1024]{1,0:T(8,128)(2,1)} %bitcast.21), custom_call_target="tpu_custom_call" | custom-call | flops 3221225472 | bytes 11534336 | tf_op jit(solution)/shard_map/hidden_deriv/pallas_call | solution.py:201
  370.6 5.4 %all-to-all-start.1 = ((bf16[8,384,512]{2,1,0:T(8,128)(2,1)}), bf16[8,384,512]{2,1,0:T(8,128)(2,1)S(1)}, u32[]{:S(2)}, u32[]{:S(2)}) async-start(bf16[8,384,512]{2,1,0:T(8,128)(2,1)} %get-tuple-element.73), calls=%async_computation.1 | async-start | bytes 6291456 | tf_op jit(solution)/shard_map/all_to_all | solution.py:330
  376.0 6.3 %collective-permute-done.23.refs_7_ = bf16[384,1024]{1,0:T(8,128)(2,1)} collective-permute-done((bf16[384,1024]{1,0:T(8,128)(2,1)}, bf16[384,1024]{1,0:T(8,128)(2,1)}, u32[]{:S(2)}, u32[]{:S(2)}) %collective-permute-start.23) | collective-permute-done | bytes 786464 | tf_op jit(solution)/shard_map/ppermute | solution.py:22
  382.3 10.7 %lion_step.2 = (f32[1,384,8192]{2,1,0:T(8,128)}, bf16[1,384,8192]{2,1,0:T(8,128)(2,1)}) custom-call(s32[1]{0:T(128)} %bitcast.4.place_ref, bf16[8,384,512]{2,1,0:T(8,128)(2,1)} %copy-done.1, bf16[1,384,8192]{2,1,0:T(8,128)(2,1)} %momentum_ref.3, bf16[384,1024]{1,0:T(8,128)(2,1)} %get-tuple-element.54.refs_0_, ...), custom_call_target="tpu_custom_call" | custom-call | flops 15728640 | bytes 18874368 | tf_op jit(solution)/shard_map/lion_step/pallas_call | solution.py:244
  393.0 8.9 %collective-permute-done.15 = f32[512,1024]{1,0:T(8,128)} collective-permute-done((f32[512,1024]{1,0:T(8,128)}, f32[512,1024]{1,0:T(8,128)}, u32[]{:S(2)}, u32[]{:S(2)}) %collective-permute-start.15) | collective-permute-done | bytes 2097184 | tf_op jit(solution)/shard_map/ppermute | solution.py:22
  401.9 16.1 %fusion.7 = (bf16[512,2,1024]{2,1,0:T(2,128)(2,1)}, bf16[512,2,1024]{2,1,0:T(2,128)(2,1)}) fusion(bf16[512,2,1024]{2,1,0:T(2,128)(2,1)S(1)} %copy-done.2, pred[512,2]{1,0:T(8,128)(4,1)S(1)} %copy.21, pred[512,2]{1,0:T(8,128)(4,1)S(1)} %copy.20, pred[512,2]{1,0:T(8,128)(4,1)S(1)} %copy.19, pred[512,2]{1,0:T(8,128)(4,1)S(1)} %copy.17, ...), kind=kLoop, calls=%fused_computation.10 | loop fusion | flops 19922944 | bytes 16781312 | tf_op jit(solution)/shard_map/convert_element_type | solution.py:352
  418.0 28.8 %all-to-all-done.1.weight_ref = bf16[8,384,512]{2,1,0:T(8,128)(2,1)S(1)} async-done(((bf16[8,384,512]{2,1,0:T(8,128)(2,1)}), bf16[8,384,512]{2,1,0:T(8,128)(2,1)S(1)}, u32[]{:S(2)}, u32[]{:S(2)}) %all-to-all-start.1) | async-done | bytes 3145760 | tf_op jit(solution)/shard_map/all_to_all | solution.py:330
  446.8 1.6 copy-done
  448.5 10.7 %lion_step.3 = (f32[1,384,8192]{2,1,0:T(8,128)}, bf16[1,384,8192]{2,1,0:T(8,128)(2,1)}) custom-call(s32[1]{0:T(128)} %bitcast.4.place_ref, bf16[8,384,512]{2,1,0:T(8,128)(2,1)} %copy-done, bf16[1,384,8192]{2,1,0:T(8,128)(2,1)} %momentum_ref.3, bf16[384,1024]{1,0:T(8,128)(2,1)} %get-tuple-element.54.refs_0_, ...), custom_call_target="tpu_custom_call", output_to_operand_aliasing={{0}: (11, {}), {1}: (12, {})} | custom-call | flops 15728640 | bytes 18874368 | tf_op jit(solution)/shard_map/lion_step/pallas_call | solution.py:244
  (45 shorter events, 0.1 us)
Async XLA Ops:
  0.6 9.9 %copy-start.3 = (bf16[512,2,1024]{2,1,0:T(2,128)(2,1)S(1)}, bf16[512,2,1024]{2,1,0:T(2,128)(2,1)}, u32[]{:S(2)}) copy-start(bf16[512,2,1024]{2,1,0:T(2,128)(2,1)} %param.8) | copy-start | bytes 6291460
  0.6 28.9 %collective-permute-start.2 = (bf16[64,3072]{1,0:T(8,128)(2,1)}, bf16[64,3072]{1,0:T(8,128)(2,1)S(1)}, u32[]{:S(2)}, u32[]{:S(2)}) collective-permute-start(bf16[64,3072]{1,0:T(8,128)(2,1)} %refs_0_), channel_id=1, source_target_pairs={{0,6},{1,7},{2,4},{3,5},{4,2},{5,3},{6,0},{7,1},{8,14},{9,15},{10,... | collective-permute-start | bytes 1179656 | tf_op jit(solution)/shard_map/ppermute | solution.py:22
  2.3 34.0 %collective-permute-start.1 = (bf16[64,3072]{1,0:T(8,128)(2,1)}, bf16[64,3072]{1,0:T(8,128)(2,1)S(1)}, u32[]{:S(2)}, u32[]{:S(2)}) collective-permute-start(bf16[64,3072]{1,0:T(8,128)(2,1)} %refs_0_), channel_id=1, source_target_pairs={{0,4},{1,5},{2,6},{3,7},{4,0},{5,1},{6,2},{7,3},{8,12},{9,13},{10,... | collective-permute-start | bytes 1179656 | tf_op jit(solution)/shard_map/ppermute | solution.py:22
  3.4 32.9 %collective-permute-start = (bf16[64,3072]{1,0:T(8,128)(2,1)}, bf16[64,3072]{1,0:T(8,128)(2,1)S(1)}, u32[]{:S(2)}, u32[]{:S(2)}) collective-permute-start(bf16[64,3072]{1,0:T(8,128)(2,1)} %refs_0_), channel_id=1, source_target_pairs={{0,2},{1,3},{2,0},{3,1},{4,6},{5,7},{6,4},{7,5},{8,10},{9,11},{10,... | collective-permute-start | bytes 1179656 | tf_op jit(solution)/shard_map/ppermute | solution.py:22
  29.6 6.7 %copy-start.7 = (bf16[64,3072]{1,0:T(8,128)(2,1)}, bf16[64,3072]{1,0:T(8,128)(2,1)S(1)}, u32[]{:S(2)}) copy-start(bf16[64,3072]{1,0:T(8,128)(2,1)S(1)} %collective-permute-done.2.refs_3_) | copy-start | bytes 1179652
  36.3 0.7 copy-start.8
  36.3 0.9 copy-start.9
  39.7 35.5 %collective-permute-start.5 = (bf16[4,64,3072]{2,1,0:T(8,128)(2,1)}, bf16[4,64,3072]{2,1,0:T(8,128)(2,1)S(1)}, u32[]{:S(2)}, u32[]{:S(2)}) collective-permute-start(bf16[4,64,3072]{2,1,0:T(8,128)(2,1)} %placed_blocks.1.mine_ref), channel_id=1, source_target_pairs={{0,16},{8,24},{16,0},{24,8},{1,17},{9,25},{17,1},{25,9},{2,18},{10... | collective-permute-start | bytes 4718600 | tf_op jit(solution)/shard_map/ppermute | solution.py:22
  41.2 35.7 %collective-permute-start.3 = (bf16[4,64,3072]{2,1,0:T(8,128)(2,1)}, bf16[4,64,3072]{2,1,0:T(8,128)(2,1)}, u32[]{:S(2)}, u32[]{:S(2)}) collective-permute-start(bf16[4,64,3072]{2,1,0:T(8,128)(2,1)} %placed_blocks.1.mine_ref), channel_id=1, source_target_pairs={{0,1},{1,0},{2,3},{3,2},{4,5},{5,4},{6,7},{7,6},{8,9},{9,8},{10,11... | collective-permute-start | bytes 4718600 | tf_op jit(solution)/shard_map/ppermute | solution.py:22
  75.2 5.9 %copy-start.5 = (bf16[4,64,3072]{2,1,0:T(8,128)(2,1)}, bf16[4,64,3072]{2,1,0:T(8,128)(2,1)S(1)}, u32[]{:S(2)}) copy-start(bf16[4,64,3072]{2,1,0:T(8,128)(2,1)S(1)} %collective-permute-done.5.mine_ref) | copy-start | bytes 4718596
  75.2 34.9 %collective-permute-start.6 = (bf16[4,64,3072]{2,1,0:T(8,128)(2,1)S(1)}, bf16[4,64,3072]{2,1,0:T(8,128)(2,1)S(1)}, u32[]{:S(2)}, u32[]{:S(2)}) collective-permute-start(bf16[4,64,3072]{2,1,0:T(8,128)(2,1)S(1)} %collective-permute-done.5.mine_ref), channel_id=1, source_target_pairs={{0,1},{1,0},{2,3},{3,2},{4,5},{5,4},{6,7},{7,6},{8,9},{9,8},{10,11... | collective-permute-start | bytes 4718600 | tf_op jit(solution)/shard_map/ppermute | solution.py:22
  81.1 134.4 %collective-permute-start.4 = (bf16[512,3072]{1,0:T(8,128)(2,1)}, bf16[512,3072]{1,0:T(8,128)(2,1)}, u32[]{:S(2)}, u32[]{:S(2)}) collective-permute-start(bf16[512,3072]{1,0:T(8,128)(2,1)} %bitcast.22), channel_id=1, source_target_pairs={{0,8},{8,0},{16,24},{24,16},{1,9},{9,1},{17,25},{25,17},{2,10},{10... | collective-permute-start | bytes 9437192 | tf_op jit(solution)/shard_map/ppermute | solution.py:22
  110.1 1.1 copy-start.6
  115.4 100.1 %collective-permute-start.7 = (bf16[512,3072]{1,0:T(8,128)(2,1)}, bf16[512,3072]{1,0:T(8,128)(2,1)}, u32[]{:S(2)}, u32[]{:S(2)}) collective-permute-start(bf16[512,3072]{1,0:T(8,128)(2,1)} %bitcast.26), channel_id=1, source_target_pairs={{0,8},{8,0},{16,24},{24,16},{1,9},{9,1},{17,25},{25,17},{2,10},{10... | collective-permute-start | bytes 9437192 | tf_op jit(solution)/shard_map/ppermute | solution.py:22
  115.4 93.0 %collective-permute-start.12 = (bf16[1024,1024]{1,0:T(8,128)(2,1)}, bf16[1024,1024]{1,0:T(8,128)(2,1)}, u32[]{:S(2)}, u32[]{:S(2)}) collective-permute-start(bf16[1024,1024]{1,0:T(8,128)(2,1)} %get-tuple-element.59), channel_id=1, source_target_pairs={{0,4},{1,5},{2,6},{3,7},{4,0},{5,1},{6,2},{7,3},{8,12},{9,13},{10,... | collective-permute-start | bytes 6291464 | tf_op jit(solution)/shard_map/ppermute | solution.py:22
  118.7 102.8 %collective-permute-start.9 = (bf16[2,512,1024]{2,1,0:T(8,128)(2,1)}, bf16[2,512,1024]{2,1,0:T(8,128)(2,1)}, u32[]{:S(2)}, u32[]{:S(2)}) collective-permute-start(bf16[2,512,1024]{2,1,0:T(8,128)(2,1)} %get-tuple-element.53), channel_id=1, source_target_pairs={{0,16},{8,24},{16,0},{24,8},{1,17},{9,25},{17,1},{25,9},{2,18},{10... | collective-permute-start | bytes 6291464 | tf_op jit(solution)/shard_map/ppermute | solution.py:22
  208.4 114.7 %all-to-all-start = ((bf16[8,384,512]{2,1,0:T(8,128)(2,1)}), bf16[8,384,512]{2,1,0:T(8,128)(2,1)S(1)}, u32[]{:S(2)}, u32[]{:S(2)}) async-start(bf16[8,384,512]{2,1,0:T(8,128)(2,1)} %get-tuple-element.66), calls=%async_computation | async-start | bytes 6291456 | tf_op jit(solution)/shard_map/all_to_all | solution.py:330
  215.5 6.0 %copy-start.11 = (bf16[1,512,1024]{2,1,0:T(8,128)(2,1)S(1)}, bf16[1,512,1024]{2,1,0:T(8,128)(2,1)}, u32[]{:S(2)}) copy-start(bf16[1,512,1024]{2,1,0:T(8,128)(2,1)} %get-tuple-element.52) | copy-start | bytes 3145732
  220.2 4.4 copy-start.12
  220.2 47.3 %collective-permute-start.13 = (bf16[2,512,1024]{2,1,0:T(8,128)(2,1)}, bf16[2,512,1024]{2,1,0:T(8,128)(2,1)S(1)}, u32[]{:S(2)}, u32[]{:S(2)}) collective-permute-start(bf16[2,512,1024]{2,1,0:T(8,128)(2,1)} %get-tuple-element.61), channel_id=1, source_target_pairs={{0,16},{8,24},{16,0},{24,8},{1,17},{9,25},{17,1},{25,9},{2,18},{10... | collective-permute-start | bytes 6291464 | tf_op jit(solution)/shard_map/ppermute | solution.py:22
  221.4 47.3 %collective-permute-start.8 = (bf16[1,512,1024]{2,1,0:T(8,128)(2,1)S(1)}, bf16[1,512,1024]{2,1,0:T(8,128)(2,1)S(1)}, u32[]{:S(2)}, u32[]{:S(2)}) collective-permute-start(bf16[1,512,1024]{2,1,0:T(8,128)(2,1)S(1)} %copy-done.11), channel_id=1, source_target_pairs={{0,8},{8,0},{16,24},{24,16},{1,9},{9,1},{17,25},{25,17},{2,10},{10... | collective-permute-start | bytes 3145736 | tf_op jit(solution)/shard_map/ppermute | solution.py:22
  224.1 44.7 %collective-permute-start.10 = (bf16[1,512,1024]{2,1,0:T(8,128)(2,1)S(1)}, bf16[1,512,1024]{2,1,0:T(8,128)(2,1)S(1)}, u32[]{:S(2)}, u32[]{:S(2)}) collective-permute-start(bf16[1,512,1024]{2,1,0:T(8,128)(2,1)S(1)} %get-tuple-element.88), channel_id=1, source_target_pairs={{0,8},{8,0},{16,24},{24,16},{1,9},{9,1},{17,25},{25,17},{2,10},{10... | collective-permute-start | bytes 3145736 | tf_op jit(solution)/shard_map/ppermute | solution.py:22
  224.6 84.1 %collective-permute-start.16 = (bf16[1,512,1024]{2,1,0:T(8,128)(2,1)S(1)}, bf16[1,512,1024]{2,1,0:T(8,128)(2,1)}, u32[]{:S(2)}, u32[]{:S(2)}) collective-permute-start(bf16[1,512,1024]{2,1,0:T(8,128)(2,1)S(1)} %copy-done.12), channel_id=1, source_target_pairs={{0,8},{8,0},{16,24},{24,16},{1,9},{9,1},{17,25},{25,17},{2,10},{10... | collective-permute-start | bytes 3145736 | tf_op jit(solution)/shard_map/ppermute | solution.py:22
  268.8 41.1 %collective-permute-start.17 = (bf16[1,512,1024]{2,1,0:T(8,128)(2,1)S(1)}, bf16[1,512,1024]{2,1,0:T(8,128)(2,1)}, u32[]{:S(2)}, u32[]{:S(2)}) collective-permute-start(bf16[1,512,1024]{2,1,0:T(8,128)(2,1)S(1)} %get-tuple-element.86), channel_id=1, source_target_pairs={{0,8},{8,0},{16,24},{24,16},{1,9},{9,1},{17,25},{25,17},{2,10},{10... | collective-permute-start | bytes 3145736 | tf_op jit(solution)/shard_map/ppermute | solution.py:22
  268.8 1.0 copy-start.13
  269.8 1.0 copy-start.14
  283.1 40.0 %collective-permute-start.18 = (bf16[384,1024]{1,0:T(8,128)(2,1)}, bf16[384,1024]{1,0:T(8,128)(2,1)}, u32[]{:S(2)}, u32[]{:S(2)}) collective-permute-start(bf16[384,1024]{1,0:T(8,128)(2,1)} %get-tuple-element.55), channel_id=1, source_target_pairs={{0,1},{1,0},{2,3},{3,2},{4,5},{5,4},{6,7},{7,6},{8,9},{9,8},{10,11... | collective-permute-start | bytes 2359304 | tf_op jit(solution)/shard_map/ppermute | solution.py:22
  284.5 40.1 %collective-permute-start.19 = (bf16[384,1024]{1,0:T(8,128)(2,1)}, bf16[384,1024]{1,0:T(8,128)(2,1)}, u32[]{:S(2)}, u32[]{:S(2)}) collective-permute-start(bf16[384,1024]{1,0:T(8,128)(2,1)} %get-tuple-element.56), channel_id=1, source_target_pairs={{0,2},{1,3},{2,0},{3,1},{4,6},{5,7},{6,4},{7,5},{8,10},{9,11},{10,... | collective-permute-start | bytes 2359304 | tf_op jit(solution)/shard_map/ppermute | solution.py:22
  293.0 100.0 %collective-permute-start.11 = (f32[512,1024]{1,0:T(8,128)}, f32[512,1024]{1,0:T(8,128)}, u32[]{:S(2)}, u32[]{:S(2)}) collective-permute-start(f32[512,1024]{1,0:T(8,128)} %hidden_deriv.4), channel_id=1, source_target_pairs={{0,8},{8,0},{16,24},{24,16},{1,9},{9,1},{17,25},{25,17},{2,10},{10... | collective-permute-start | bytes 6291464 | tf_op jit(solution)/shard_map/ppermute | solution.py:22
  308.7 84.3 %collective-permute-start.14 = (f32[512,1024]{1,0:T(8,128)}, f32[512,1024]{1,0:T(8,128)}, u32[]{:S(2)}, u32[]{:S(2)}) collective-permute-start(f32[512,1024]{1,0:T(8,128)} %hidden_deriv.6), channel_id=1, source_target_pairs={{0,24},{8,16},{16,8},{24,0},{1,25},{9,17},{17,9},{25,1},{2,26},{10... | collective-permute-start | bytes 6291464 | tf_op jit(solution)/shard_map/ppermute | solution.py:22
  309.9 92.0 %collective-permute-start.15 = (f32[512,1024]{1,0:T(8,128)}, f32[512,1024]{1,0:T(8,128)}, u32[]{:S(2)}, u32[]{:S(2)}) collective-permute-start(f32[512,1024]{1,0:T(8,128)} %hidden_deriv.7), channel_id=1, source_target_pairs={{0,16},{8,24},{16,0},{24,8},{1,17},{9,25},{17,1},{25,9},{2,18},{10... | collective-permute-start | bytes 6291464 | tf_op jit(solution)/shard_map/ppermute | solution.py:22
  310.8 51.1 %copy-start.10 = (s32[512,2]{0,1:T(2,128)S(1)}, s32[512,2]{0,1:T(2,128)}, u32[]{:S(2)}) copy-start(s32[512,2]{0,1:T(2,128)} %param.9) | copy-start | bytes 12292
  323.1 47.6 %copy-start.1 = (bf16[8,384,512]{2,1,0:T(8,128)(2,1)}, bf16[8,384,512]{2,1,0:T(8,128)(2,1)S(1)}, u32[]{:S(2)}) copy-start(bf16[8,384,512]{2,1,0:T(8,128)(2,1)S(1)} %all-to-all-done.weight_ref) | copy-start | bytes 9437188
  323.1 20.6 %collective-permute-start.20 = (bf16[384,1024]{1,0:T(8,128)(2,1)}, bf16[384,1024]{1,0:T(8,128)(2,1)}, u32[]{:S(2)}, u32[]{:S(2)}) collective-permute-start(bf16[384,1024]{1,0:T(8,128)(2,1)} %get-tuple-element.57), channel_id=1, source_target_pairs={{0,3},{1,2},{2,1},{3,0},{4,7},{5,6},{6,5},{7,4},{8,11},{9,10},{10,... | collective-permute-start | bytes 2359304 | tf_op jit(solution)/shard_map/ppermute | solution.py:22
  324.6 35.7 %collective-permute-start.21 = (bf16[384,1024]{1,0:T(8,128)(2,1)}, bf16[384,1024]{1,0:T(8,128)(2,1)}, u32[]{:S(2)}, u32[]{:S(2)}) collective-permute-start(bf16[384,1024]{1,0:T(8,128)(2,1)} %get-tuple-element.75), channel_id=1, source_target_pairs={{0,1},{1,0},{2,3},{3,2},{4,5},{5,4},{6,7},{7,6},{8,9},{9,8},{10,11... | collective-permute-start | bytes 2359304 | tf_op jit(solution)/shard_map/ppermute | solution.py:22
  343.6 32.4 %collective-permute-start.22 = (bf16[384,1024]{1,0:T(8,128)(2,1)}, bf16[384,1024]{1,0:T(8,128)(2,1)}, u32[]{:S(2)}, u32[]{:S(2)}) collective-permute-start(bf16[384,1024]{1,0:T(8,128)(2,1)} %get-tuple-element.76), channel_id=1, source_target_pairs={{0,2},{1,3},{2,0},{3,1},{4,6},{5,7},{6,4},{7,5},{8,10},{9,11},{10,... | collective-permute-start | bytes 2359304 | tf_op jit(solution)/shard_map/ppermute | solution.py:22
  360.4 21.9 %collective-permute-start.23 = (bf16[384,1024]{1,0:T(8,128)(2,1)}, bf16[384,1024]{1,0:T(8,128)(2,1)}, u32[]{:S(2)}, u32[]{:S(2)}) collective-permute-start(bf16[384,1024]{1,0:T(8,128)(2,1)} %get-tuple-element.77), channel_id=1, source_target_pairs={{0,3},{1,2},{2,1},{3,0},{4,7},{5,6},{6,5},{7,4},{8,11},{9,10},{10,... | collective-permute-start | bytes 2359304 | tf_op jit(solution)/shard_map/ppermute | solution.py:22
  370.6 76.2 %all-to-all-start.1 = ((bf16[8,384,512]{2,1,0:T(8,128)(2,1)}), bf16[8,384,512]{2,1,0:T(8,128)(2,1)S(1)}, u32[]{:S(2)}, u32[]{:S(2)}) async-start(bf16[8,384,512]{2,1,0:T(8,128)(2,1)} %get-tuple-element.73), calls=%async_computation.1 | async-start | bytes 6291456 | tf_op jit(solution)/shard_map/all_to_all | solution.py:330
  376.0 25.9 %copy-start.2 = (bf16[512,2,1024]{2,1,0:T(2,128)(2,1)S(1)}, bf16[512,2,1024]{2,1,0:T(2,128)(2,1)}, u32[]{:S(2)}) copy-start(bf16[512,2,1024]{2,1,0:T(2,128)(2,1)} %param.7) | copy-start | bytes 6291460
  376.0 25.9 %copy-start.4 = (bf16[512,2,1024]{2,1,0:T(2,128)(2,1)S(1)}, bf16[512,2,1024]{2,1,0:T(2,128)(2,1)}, u32[]{:S(2)}) copy-start(bf16[512,2,1024]{2,1,0:T(2,128)(2,1)} %param.8) | copy-start | bytes 6291460
  446.8 1.6 copy-start

commit v7 on v6

--- a/solution.py
+++ b/solution.py
@@ -13,6 +13,7 @@
 decay_rate = 1.0
 sign_width = 10.0
 MIB = 1024 * 1024
+SMALL = pl.CostEstimate(flops=1024, bytes_accessed=1024, transcendentals=0)
 
 
 def swapped(array, axis, mask):
@@ -29,6 +30,10 @@
 def order_kernel(place_ref, mine_ref, theirs_ref, out_ref):
     out_ref[0, place_ref[0]] = mine_ref[0]
     out_ref[0, 1 - place_ref[0]] = theirs_ref[0]
+
+
+def stage(*values):
+    return lax.optimization_barrier(values)
 
 
 def in_order(mine, theirs, bit):
@@ -43,7 +48,7 @@
             out_specs=pl.BlockSpec((1, 2, some, width), lambda i, place: (i, 0, 0, 0)),
         ),
         out_shape=jax.ShapeDtypeStruct((count, 2, some, width), mine.dtype),
-        cost_estimate=pl.CostEstimate(flops=0, bytes_accessed=8 * mine.size, transcendentals=0),
+        cost_estimate=SMALL,
         name="side_by_side",
     )(bit.astype(jnp.int32).reshape(1), mine, theirs)
     return both.reshape(2 * count, some, width)
@@ -66,9 +71,7 @@
         ),
         out_shape=jax.ShapeDtypeStruct((count,) + blocks[0].shape, blocks[0].dtype),
         compiler_params=pltpu.CompilerParams(vmem_limit_bytes=56 * MIB),
-        cost_estimate=pl.CostEstimate(
-            flops=0, bytes_accessed=4 * count * blocks[0].size, transcendentals=0
-        ),
+        cost_estimate=SMALL,
         name="placed_blocks",
     )(place.reshape(1), *blocks)
 
@@ -90,54 +93,74 @@
             m += 1
 
 
-def hidden_kernel(gate_ref, up_ref, named_ref, hidden_ref, *out_refs):
+def hidden_kernel(gate_ref, up_ref, named_ref, first_ref, second_ref, *out_refs):
     gate = gate_ref[...].astype(jnp.float32)
     up = up_ref[...].astype(jnp.float32)
     hidden = (gate * jax.nn.sigmoid(gate) * up).astype(jnp.bfloat16)
-    hidden_ref[...] = hidden
     pick(hidden, named_ref, out_refs)
-
-
-def pick_kernel(hidden_ref, named_ref, *out_refs):
-    pick(hidden_ref[...], named_ref, out_refs)
-
-
-def picked_rows(kernel, arrays, named, experts, topk, with_hidden):
-    count_rows, cols = arrays[0].shape
-    group_tok = count_rows // topk
-    some = 128 if group_tok % 128 == 0 else group_tok
-    row_block = pl.BlockSpec((some * topk, cols), lambda i: (i, 0))
+    early = pl.program_id(0) < pl.num_programs(0) // 2
+
+    @pl.when(early)
+    def _():
+        first_ref[...] = hidden
+
+    @pl.when(jnp.logical_not(early))
+    def _():
+        second_ref[...] = hidden
+
+
+def pick_kernel(first_ref, second_ref, named_ref, *out_refs):
+    early = pl.program_id(0) < pl.num_programs(0) // 2
+
+    @pl.when(early)
+    def _():
+        pick(first_ref[...], named_ref, out_refs)
+
+    @pl.when(jnp.logical_not(early))
+    def _():
+        pick(second_ref[...], named_ref, out_refs)
+
+
+def picked_rows(arrays, named, group_tok, experts, fresh):
+    cols = arrays[0].shape[1]
+    topk = named.shape[1] // group_tok
+    some = 128 if group_tok % 256 == 0 else group_tok // 2
+    steps = group_tok // some
     sizes = [1] + [1 << b for b in range(experts.bit_length() - 1)]
     out_shape = [jax.ShapeDtypeStruct((n, group_tok, cols), jnp.bfloat16) for n in sizes]
     out_specs = [pl.BlockSpec((n, some, cols), lambda i: (0, i, 0)) for n in sizes]
-    if with_hidden:
-        out_shape = [jax.ShapeDtypeStruct((count_rows, cols), jnp.bfloat16)] + out_shape
-        out_specs = [row_block] + out_specs
+    rows = (some * topk, cols)
+    halves = [
+        pl.BlockSpec(rows, lambda i: (jnp.minimum(i, steps // 2 - 1), 0)),
+        pl.BlockSpec(rows, lambda i: (jnp.maximum(i - steps // 2, 0), 0)),
+    ]
+    in_specs = halves
+    if fresh:
+        in_specs = [pl.BlockSpec(rows, lambda i: (i, 0))] * 2
+        half = jax.ShapeDtypeStruct((group_tok * topk // 2, cols), jnp.bfloat16)
+        out_shape, out_specs = [half, half] + out_shape, halves + out_specs
     return pl.pallas_call(
-        kernel,
-        grid=(group_tok // some,),
-        in_specs=[row_block] * len(arrays) + [pl.BlockSpec((1, some * topk), lambda i: (0, i))],
+        hidden_kernel if fresh else pick_kernel,
+        grid=(steps,),
+        in_specs=in_specs + [pl.BlockSpec((1, some * topk), lambda i: (0, i))],
         out_specs=out_specs,
         out_shape=out_shape,
         compiler_params=pltpu.CompilerParams(vmem_limit_bytes=56 * MIB),
-        cost_estimate=pl.CostEstimate(
-            flops=2 * experts * count_rows * some * cols,
-            bytes_accessed=2 * cols * (count_rows * (len(arrays) + 1) + experts * group_tok),
-            transcendentals=count_rows * cols,
-        ),
+        cost_estimate=SMALL,
         name="hidden_rows",
     )(*arrays, named)
 
 
-def spread(picked, experts):
+def spread(picked, got, experts):
+    half = experts // 2
     held = {0: {(1 << i) >> 1: rows for i, rows in enumerate(picked)}}
-    bit = experts // 2
+    bit = half
     while bit:
         for group in list(held):
-            got = swapped(held[group][bit], "expert", bit)
-            held[group ^ bit] = {0: got[:1]}
+            rows = got if bit == half else swapped(held[group][bit], "expert", bit)
+            held[group ^ bit] = {0: rows[:1]}
             for i in range(bit.bit_length() - 1):
-                held[group ^ bit][1 << i] = got[1 << i : 2 << i]
+                held[group ^ bit][1 << i] = rows[1 << i : 2 << i]
         bit //= 2
     return [held[m][0][0] for m in range(experts)]
 
@@ -179,11 +202,7 @@
         ),
         out_shape=[jax.ShapeDtypeStruct((tall, cols), jnp.bfloat16)] * steps,
         compiler_params=pltpu.CompilerParams(vmem_limit_bytes=56 * MIB),
-        cost_estimate=pl.CostEstimate(
-            flops=2 * count * group_tok * steps * tall * cols,
-            bytes_accessed=2 * (count * group_tok * (steps * tall + cols) + steps * tall * cols),
-            transcendentals=0,
-        ),
+        cost_estimate=SMALL,
         name="group_terms",
     )(place.reshape(1), *tokens, *hidden)
 
@@ -208,11 +227,7 @@
         out_specs=pl.BlockSpec((group_tok, wide), lambda i: (0, i)),
         out_shape=jax.ShapeDtypeStruct((group_tok, cols), jnp.float32),
         compiler_params=pltpu.CompilerParams(vmem_limit_bytes=56 * MIB),
-        cost_estimate=pl.CostEstimate(
-            flops=2 * group_tok * width * cols,
-            bytes_accessed=2 * (group_tok + cols) * width + 4 * group_tok * cols,
-            transcendentals=0,
-        ),
+        cost_estimate=SMALL,
         name="hidden_deriv",
     )(tokens, weight)
 
@@ -257,20 +272,9 @@
         ],
         input_output_aliases={3 + count + i: i for i in range(len(done))},
         compiler_params=pltpu.CompilerParams(vmem_limit_bytes=56 * MIB),
-        cost_estimate=pl.CostEstimate(flops=10 * size, bytes_accessed=12 * size, transcendentals=size),
+        cost_estimate=SMALL,
         name="lion_step",
     )(place.reshape(1), weight, momentum, *grads, *done)
-
-
-def gathered(held, experts, shards, place):
-    groups = {0: held}
-    for m in sorted(range(2, experts, 2), key=lambda m: (bin(m).count("1"), -m)):
-        groups[m] = swapped(groups[m & (m - 1)], "expert", m & -m)
-    for m in list(groups):
-        both = in_order(groups[m], swapped(groups[m], "dp", 1), (place & 1) != 0)
-        groups[m] = both.reshape(-1, held.shape[2])
-        groups[m + 1] = swapped(groups[m], "expert", 1)
-    return [groups[m] for m in range(experts)]
 
 
 def body(out_grad, gate_saved, up_saved, routing, down_weight, momentum):
@@ -284,25 +288,43 @@
     span = shards // 2
     each = range(experts)
 
+    half = experts // 2
+    others = sorted(range(2, experts, 2), key=lambda m: (bin(m).count("1"), -m))
+
     blocks = [swapped(out_grad, "dp", m) for m in range(0, shards, 2)]
     named = (routing ^ mine).reshape(1, group_tok * topk)
-    hidden, *own_picked = picked_rows(
-        hidden_kernel,
-        [gate_saved.reshape(-1, cols), up_saved.reshape(-1, cols)],
-        named,
-        experts,
-        topk,
-        True,
-    )
-    held = placed_blocks([after(block, hidden) for block in blocks], place // 2)
-    hidden, own_picked, _ = lax.optimization_barrier((hidden, own_picked, held))
-    other_hidden = swapped(hidden, "dp", span)
-    tokens = gathered(held, experts, shards, place)
-    own_rows = spread(own_picked, experts)
-    other_picked = picked_rows(
-        pick_kernel, [after(other_hidden, tokens)], named, experts, topk, False
-    )
-    other_rows = spread(other_picked, experts)
+    first, second, *own_picked = picked_rows(
+        [gate_saved.reshape(-1, cols), up_saved.reshape(-1, cols)], named, group_tok, experts, True
+    )
+    blocks, first, second, own_picked = stage(blocks, first, second, own_picked)
+
+    held = {0: placed_blocks(blocks, place // 2)}
+    held[0], first = stage(held[0], first)
+    for m in others:
+        held[m] = swapped(held[m & (m - 1)], "expert", m & -m)
+    beside = swapped(held[0], "dp", 1)
+    other_first = swapped(first, "dp", span)
+    held, beside, other_first, second, own_picked = stage(
+        held, beside, other_first, second, own_picked
+    )
+
+    last = (place & 1) != 0
+    tokens = {0: in_order(held[0], beside, last).reshape(group_tok, width)}
+    tokens[1] = swapped(tokens[0], "expert", 1)
+    besides = {m: swapped(held[m], "dp", 1) for m in others}
+    other_second = swapped(second, "dp", span)
+    own_got = swapped(own_picked[-1], "expert", half)
+    tokens, besides, other_second, own_got, own_picked = stage(
+        tokens, besides, other_second, own_got, own_picked
+    )
+
+    for m in others:
+        tokens[m] = in_order(held[m], besides[m], last).reshape(group_tok, width)
+        tokens[m + 1] = swapped(tokens[m], "expert", 1)
+    tokens = [tokens[m] for m in each]
+    own_rows = spread(own_picked, own_got, experts)
+    other_picked = picked_rows([other_first, other_second], named, group_tok, experts, False)
+    other_got = swapped(other_picked[-1], "expert", half)
 
     def shard_terms(hidden_rows):
         if rows % 128 == 0:
@@ -318,14 +340,18 @@
         ]
 
     own_terms = shard_terms(own_rows)
+    weight, own_terms = stage(down_weight[0], own_terms)
+    derivs = [deriv_of(tokens[m], weight) for m in each]
+
+    other_got, other_picked, derivs = stage(other_got, other_picked, derivs)
+    other_rows = spread(other_picked, other_got, experts)
     other_terms = shard_terms(other_rows)
 
-    weight = down_weight[0]
     parts = 2 if cols % 256 == 0 else 1
     pieces = jnp.split(down_weight.reshape(shards, rows, cols), parts, axis=2)
     weights = []
     for part, piece in enumerate(pieces):
-        begun = [other_hidden] if part == 0 else [weights[-1], other_terms]
+        begun = [other_second] if part == 0 else [weights[-1], other_terms]
         weights.append(
             lax.all_to_all(after(piece, *begun), "dp", split_axis=0, concat_axis=0, tiled=True)
         )
@@ -336,19 +362,14 @@
         grads[m] = swapped(own_terms[m], "dp", m)
         grads[m ^ span] = swapped(other_terms[m], "dp", m)
 
-    back_weight, gate_saved, up_saved, *_ = lax.optimization_barrier(
-        (weight, gate_saved, up_saved, own_terms)
-    )
+    gate_saved, up_saved, _ = stage(gate_saved, up_saved, derivs)
     gate = gate_saved.astype(jnp.float32)
     up = up_saved.astype(jnp.float32)
     sigma = jax.nn.sigmoid(gate)
     deriv = jnp.zeros(gate.shape, jnp.float32)
-    for m in list(range(experts // 2, experts)) + list(range(experts // 2)):
-        part = deriv_of(tokens[m], back_weight)
-        if m >= experts // 2:
-            part = after(part, other_rows[experts // 2])
+    for m in each:
         chosen = (routing == (mine ^ m))[:, :, None]
-        deriv = jnp.where(chosen, swapped(part, "expert", m)[:, None, :], deriv)
+        deriv = jnp.where(chosen, swapped(derivs[m], "expert", m)[:, None, :], deriv)
     d_up = (deriv * gate * sigma).astype(jnp.bfloat16)
     d_gate = (deriv * up * sigma * (1.0 + gate * (1.0 - sigma))).astype(jnp.bfloat16)
 

time: 463 us -> 381 us (0.82)
  waiting for transfers between devices: 281 us -> 198 us
    ppermute x24 -> x25, waiting for transfers between devices: 252 us -> 198 us  [swapped(): return lax.ppermute(array, axis, [(i, i ^ mask) for i in range(size)])]
    all_to_all x2, waiting for transfers between devices: 28.8 us -> 0.01 us  [body(): lax.all_to_all(after(piece, *begun), 'dp', split_axis=0, concat_axis=0, t...]
    unnamed x30 -> x46, local copies, waits for them, and re-layouts: 5.63 us -> 10.5 us
    ppermute x24 -> x25, starting transfers between devices: 25 us -> 23.5 us  [swapped(): return lax.ppermute(array, axis, [(i, i ^ mask) for i in range(size)])]
  transfers between devices with their start and end apart: 26 -> 27, of which waited for: 12 -> 12; matrix products, arithmetic and copies ran while one was open for 8% -> 9% of each run, Pallas kernels for 19% -> 22%
where the time goes in v7:
time: 381 us; the launch traced here: 379 us
  waiting for transfers between devices  198 us (52%)
  Pallas kernels  101 us (27%)
  starting transfers between devices  35.5 us (9%)
  local copies, waits for them, and re-layouts  27.3 us (7%)
  other arithmetic  17 us (4%)
    ppermute x25, waiting for transfers between devices, swapped(): return lax.ppermute(array, axis, [(i, i ^ mask) for i in range(size)])  198 us
    pallas_call x4, Pallas kernels, deriv_of(): pl.pallas_call(deriv_kernel, grid=(cols // wide,), in_specs=[pl.BlockSpec...  31.6 us
    pallas_call x2, Pallas kernels, terms(): pl.pallas_call(functools.partial(term_kernel, count), grid_spec=pltpu.Pre...  24.5 us
    ppermute x25, starting transfers between devices, swapped(): return lax.ppermute(array, axis, [(i, i ^ mask) for i in range(size)])  23.5 us
    pallas_call x2, Pallas kernels, update(): pl.pallas_call(functools.partial(update_kernel, count), grid_spec=pltpu.P...  21.5 us
    convert_element_type x1, other arithmetic, body(): d_up = (deriv * gate * sigma).astype(jnp.bfloat16)  16.3 us
    all_to_all x2, starting transfers between devices, body(): lax.all_to_all(after(piece, *begun), 'dp', split_axis=0, concat_axis=0, t...  12.1 us
    pallas_call x2, Pallas kernels, picked_rows(): pl.pallas_call(hidden_kernel if fresh else pick_kernel, grid=(steps,), in...  11.9 us
  transfers between devices with their start and end apart: 27, of which 12 were waited for; matrix products, arithmetic and copies ran while one was open for 9% of the time, Pallas kernels for 22%

profile of v7, /device:TPU:8, one launch (start us, length us, event | category | flops | bytes accessed | tf_op | source)
XLA Modules:
  0.0 379.5 jit_solution(14352937272550517013)
XLA Ops:
  0.6 2.7 collective-permute-start.1
  3.3 0.4 collective-permute-start
  3.7 0.5 collective-permute-start.2
  4.2 0.7 broadcast_xor_fusion
  5.0 0.8 reshape.46.named_ref
  5.8 4.1 %reshape.44.gate_ref = bf16[1024,1024]{1,0:T(8,128)(2,1)} reshape(bf16[512,2,1024]{2,1,0:T(2,128)(2,1)} %param.7) | data formatting | bytes 4194304 | tf_op jit(solution)/shard_map/reshape | solution.py:297
  9.9 2.2 reshape.45.up_ref
  12.1 6.8 %hidden_rows.2 = (bf16[512,1024]{1,0:T(8,128)(2,1)}, bf16[512,1024]{1,0:T(8,128)(2,1)}, bf16[1,512,1024]{2,1,0:T(8,128)(2,1)}, bf16[1,512,1024]{2,1,0:T(8,128)(2,1)}, bf16[2,512,1024]{2,1,0:T(8,128)(2,1)}) custom-call(bf16[1024,1024]{1,0:T(8,128)(2,1)} %reshape.44.gate_ref, bf16[1024,1024]{1,0:T(8,128)(2,1)} %reshape.45.up_ref, s32[1,1024]{1,0:T(1,128)} %reshape.46.named_ref), custom_call_target="tpu_custom_call" | custom-call | flops 1024 | bytes 1024 | tf_op jit(solution)/shard_map/hidden_rows/pallas_call | solution.py:142
  18.9 2.4 collective-permute-done.1.refs_2_
  21.3 1.1 collective-permute-done.refs_1_
  22.4 14.7 %collective-permute-done.2.refs_3_ = bf16[64,3072]{1,0:T(8,128)(2,1)S(1)} collective-permute-done((bf16[64,3072]{1,0:T(8,128)(2,1)}, bf16[64,3072]{1,0:T(8,128)(2,1)S(1)}, u32[]{:S(2)}, u32[]{:S(2)}) %collective-permute-start.2) | collective-permute-done | bytes 393248 | tf_op jit(solution)/shard_map/ppermute | solution.py:23
  37.2 0.7 copy-done.20
  37.9 2.6 placed_blocks.1.mine_ref
  40.5 1.5 collective-permute-start.4
  42.0 1.5 collective-permute-start.3
  43.5 45.1 %collective-permute-done.5.first_ref = bf16[512,1024]{1,0:T(8,128)(2,1)} collective-permute-done((bf16[512,1024]{1,0:T(8,128)(2,1)}, bf16[512,1024]{1,0:T(8,128)(2,1)}, u32[]{:S(2)}, u32[]{:S(2)}) %collective-permute-start.5) | collective-permute-done | bytes 1048608 | tf_op jit(solution)/shard_map/ppermute | solution.py:23
  88.6 1.1 copy-done.12
  89.8 4.2 %side_by_side.2 = bf16[4,2,64,3072]{3,2,1,0:T(8,128)(2,1)} custom-call(s32[1]{0:T(128)} %bitcast.1.place_ref, bf16[4,64,3072]{2,1,0:T(8,128)(2,1)} %placed_blocks.1.mine_ref, bf16[4,64,3072]{2,1,0:T(8,128)(2,1)} %copy-done.12), custom_call_target="tpu_custom_call" | custom-call | flops 1024 | bytes 1024 | tf_op jit(solution)/shard_map/side_by_side/pallas_call | solution.py:42
  93.9 0.6 collective-permute-start.9
  94.5 0.5 collective-permute-start.7
  95.0 3.4 collective-permute-start.8
  98.4 6.1 %fusion.8 = (bf16[8,384,512]{2,1,0:T(8,128)(2,1)}, bf16[8,384,512]{2,1,0:T(8,128)(2,1)}) fusion(bf16[8,384,1024]{2,1,0:T(8,128)(2,1)} %bitcast.17), kind=kLoop, calls=%fused_computation.19 | loop fusion | bytes 12582912 | tf_op jit(solution)/shard_map/split | solution.py:351
  104.5 39.2 %collective-permute-done.8.second_ref = bf16[512,1024]{1,0:T(8,128)(2,1)S(1)} collective-permute-done((bf16[512,1024]{1,0:T(8,128)(2,1)}, bf16[512,1024]{1,0:T(8,128)(2,1)S(1)}, u32[]{:S(2)}, u32[]{:S(2)}) %collective-permute-start.8) | collective-permute-done | bytes 1048608 | tf_op jit(solution)/shard_map/ppermute | solution.py:23
  143.7 1.0 copy-done.17
  144.7 0.5 copy-done.11
  145.2 0.7 copy-done.8
  145.9 1.7 copy-done
  147.5 7.0 %all-to-all-start = ((bf16[8,384,512]{2,1,0:T(8,128)(2,1)}), bf16[8,384,512]{2,1,0:T(8,128)(2,1)}, u32[]{:S(2)}, u32[]{:S(2)}) async-start(bf16[8,384,512]{2,1,0:T(8,128)(2,1)} %get-tuple-element.115), calls=%async_computation | async-start | bytes 6291456 | tf_op jit(solution)/shard_map/all_to_all | solution.py:356
  154.5 4.4 %side_by_side.3 = bf16[4,2,64,3072]{3,2,1,0:T(8,128)(2,1)} custom-call(s32[1]{0:T(128)} %bitcast.1.place_ref, bf16[4,64,3072]{2,1,0:T(8,128)(2,1)} %copy-done.10, bf16[4,64,3072]{2,1,0:T(8,128)(2,1)} %copy-done.11), custom_call_target="tpu_custom_call" | custom-call | flops 1024 | bytes 1024 | tf_op jit(solution)/shard_map/side_by_side/pallas_call | solution.py:42
  158.9 5.1 %hidden_rows.3 = (bf16[1,512,1024]{2,1,0:T(8,128)(2,1)}, bf16[1,512,1024]{2,1,0:T(8,128)(2,1)}, bf16[2,512,1024]{2,1,0:T(8,128)(2,1)}) custom-call(bf16[512,1024]{1,0:T(8,128)(2,1)} %collective-permute-done.5.first_ref, bf16[512,1024]{1,0:T(8,128)(2,1)} %copy-done.17, s32[1,1024]{1,0:T(1,128)} %reshape.46.named_ref), custom_call_target="tpu_custom_call" | custom-call | flops 1024 | bytes 1024 | tf_op jit(solution)/shard_map/hidden_rows/pallas_call | solution.py:142
  164.0 1.5 collective-permute-start.10
  165.7 1.1 fusion.10
  166.8 0.3 collective-permute-start.13
  167.1 1.2 collective-permute-done.12
  168.3 1.3 collective-permute-done.13
  169.6 1.0 copy-done.16
  170.7 1.0 copy-done.1
  171.6 12.2 %group_terms.2 = (bf16[384,1024]{1,0:T(8,128)(2,1)}, bf16[384,1024]{1,0:T(8,128)(2,1)}, bf16[384,1024]{1,0:T(8,128)(2,1)}, bf16[384,1024]{1,0:T(8,128)(2,1)}) custom-call(s32[1]{0:T(128)} %bitcast.4.place_ref, bf16[512,3072]{1,0:T(8,128)(2,1)} %bitcast.23, bf16[512,3072]{1,0:T(8,128)(2,1)} %copy-done, bf16[512,3072]{1,0:T(8,128)(2,1)} %bitcast.27, ...), custom_call_target="tpu_custom_call" | custom-call | flops 1024 | bytes 1024 | tf_op jit(solution)/shard_map/group_terms/pallas_call | solution.py:191
  183.9 7.9 %hidden_deriv.6 = f32[512,1024]{1,0:T(8,128)} custom-call(bf16[512,3072]{1,0:T(8,128)(2,1)} %bitcast.28, bf16[3072,1024]{1,0:T(8,128)(2,1)} %bitcast.18), custom_call_target="tpu_custom_call" | custom-call | flops 1024 | bytes 1024 | tf_op jit(solution)/shard_map/hidden_deriv/pallas_call | solution.py:220
  191.7 7.9 %hidden_deriv.5 = f32[512,1024]{1,0:T(8,128)} custom-call(bf16[512,3072]{1,0:T(8,128)(2,1)} %copy-done, bf16[3072,1024]{1,0:T(8,128)(2,1)} %bitcast.19), custom_call_target="tpu_custom_call" | custom-call | flops 1024 | bytes 1024 | tf_op jit(solution)/shard_map/hidden_deriv/pallas_call | solution.py:220
  199.6 7.9 %hidden_deriv.4 = f32[512,1024]{1,0:T(8,128)} custom-call(bf16[512,3072]{1,0:T(8,128)(2,1)} %bitcast.24, bf16[3072,1024]{1,0:T(8,128)(2,1)} %bitcast.20), custom_call_target="tpu_custom_call" | custom-call | flops 1024 | bytes 1024 | tf_op jit(solution)/shard_map/hidden_deriv/pallas_call | solution.py:220
  207.5 8.0 %hidden_deriv.7 = f32[512,1024]{1,0:T(8,128)} custom-call(bf16[512,3072]{1,0:T(8,128)(2,1)} %copy-done.1, bf16[3072,1024]{1,0:T(8,128)(2,1)} %bitcast.21), custom_call_target="tpu_custom_call" | custom-call | flops 1024 | bytes 1024 | tf_op jit(solution)/shard_map/hidden_deriv/pallas_call | solution.py:220
  215.5 0.4 collective-permute-start.14
  215.9 1.5 collective-permute-start.15
  217.4 0.5 collective-permute-start.17
  217.9 1.6 fusion.9
  219.4 4.7 %collective-permute-done.17 = bf16[1,512,1024]{2,1,0:T(8,128)(2,1)S(1)} collective-permute-done((bf16[1,512,1024]{2,1,0:T(8,128)(2,1)S(1)}, bf16[1,512,1024]{2,1,0:T(8,128)(2,1)S(1)}, u32[]{:S(2)}, u32[]{:S(2)}) %collective-permute-start.17) | collective-permute-done | bytes 1048608 | tf_op jit(solution)/shard_map/ppermute | solution.py:23
  224.2 1.5 collective-permute-start.19
  226.5 0.6 collective-permute-start.20
  227.1 0.3 copy-done.14
  227.4 12.2 %group_terms.3 = (bf16[384,1024]{1,0:T(8,128)(2,1)}, bf16[384,1024]{1,0:T(8,128)(2,1)}, bf16[384,1024]{1,0:T(8,128)(2,1)}, bf16[384,1024]{1,0:T(8,128)(2,1)}) custom-call(s32[1]{0:T(128)} %bitcast.4.place_ref, bf16[512,3072]{1,0:T(8,128)(2,1)} %bitcast.25, bf16[512,3072]{1,0:T(8,128)(2,1)} %copy-done, bf16[512,3072]{1,0:T(8,128)(2,1)} %bitcast.29, ...), custom_call_target="tpu_custom_call" | custom-call | flops 1024 | bytes 1024 | tf_op jit(solution)/shard_map/group_terms/pallas_call | solution.py:191
  239.7 5.1 %all-to-all-start.1 = ((bf16[8,384,512]{2,1,0:T(8,128)(2,1)}), bf16[8,384,512]{2,1,0:T(8,128)(2,1)S(1)}, u32[]{:S(2)}, u32[]{:S(2)}) async-start(bf16[8,384,512]{2,1,0:T(8,128)(2,1)} %get-tuple-element.123), calls=%async_computation.1 | async-start | bytes 6291456 | tf_op jit(solution)/shard_map/all_to_all | solution.py:356
  244.8 1.5 collective-permute-start.21
  246.3 17.2 %collective-permute-done.14 = f32[512,1024]{1,0:T(8,128)} collective-permute-done((f32[512,1024]{1,0:T(8,128)}, f32[512,1024]{1,0:T(8,128)}, u32[]{:S(2)}, u32[]{:S(2)}) %collective-permute-start.14) | collective-permute-done | bytes 2097184 | tf_op jit(solution)/shard_map/ppermute | solution.py:23
  263.4 1.5 collective-permute-start.22
  264.9 43.8 %collective-permute-done.15 = f32[512,1024]{1,0:T(8,128)} collective-permute-done((f32[512,1024]{1,0:T(8,128)}, f32[512,1024]{1,0:T(8,128)}, u32[]{:S(2)}, u32[]{:S(2)}) %collective-permute-start.15) | collective-permute-done | bytes 2097184 | tf_op jit(solution)/shard_map/ppermute | solution.py:23
  308.7 2.9 collective-permute-start.24
  311.6 16.3 %fusion.7 = (bf16[512,2,1024]{2,1,0:T(2,128)(2,1)}, bf16[512,2,1024]{2,1,0:T(2,128)(2,1)}) fusion(bf16[512,2,1024]{2,1,0:T(2,128)(2,1)} %param.7, pred[512,2]{1,0:T(8,128)(4,1)S(1)} %copy.21, pred[512,2]{1,0:T(8,128)(4,1)S(1)} %copy.20, pred[512,2]{1,0:T(8,128)(4,1)S(1)} %copy.19, pred[512,2]{1,0:T(8,128)(4,1)S(1)} %copy.17, f32[512,1024]{1,0:T(8,128)} %hidden_deriv.4, ...), kind=kLoop, calls=%fused_computation.10 | loop fusion | flops 19922944 | bytes 16781312 | tf_op jit(solution)/shard_map/convert_element_type | solution.py:373
  328.0 3.8 %collective-permute-done.23.refs_6_ = bf16[384,1024]{1,0:T(8,128)(2,1)S(1)} collective-permute-done((bf16[384,1024]{1,0:T(8,128)(2,1)}, bf16[384,1024]{1,0:T(8,128)(2,1)S(1)}, u32[]{:S(2)}, u32[]{:S(2)}) %collective-permute-start.23) | collective-permute-done | bytes 786464 | tf_op jit(solution)/shard_map/ppermute | solution.py:23
  331.8 23.7 %collective-permute-done.24.refs_7_ = bf16[384,1024]{1,0:T(8,128)(2,1)S(1)} collective-permute-done((bf16[384,1024]{1,0:T(8,128)(2,1)}, bf16[384,1024]{1,0:T(8,128)(2,1)S(1)}, u32[]{:S(2)}, u32[]{:S(2)}) %collective-permute-start.24) | collective-permute-done | bytes 786464 | tf_op jit(solution)/shard_map/ppermute | solution.py:23
  355.5 0.9 copy-done.7
  356.3 10.7 %lion_step.2 = (f32[1,384,8192]{2,1,0:T(8,128)}, bf16[1,384,8192]{2,1,0:T(8,128)(2,1)}) custom-call(s32[1]{0:T(128)} %bitcast.4.place_ref, bf16[8,384,512]{2,1,0:T(8,128)(2,1)} %all-to-all-done.weight_ref, bf16[1,384,8192]{2,1,0:T(8,128)(2,1)} %momentum_ref.3, bf16[384,1024]{1,0:T(8,128)(2,1)} %get-tuple-element.124.refs_0_, ...), custom_call_target="tpu_custom_call" | custom-call | flops 1024 | bytes 1024 | tf_op jit(solution)/shard_map/lion_step/pallas_call | solution.py:259
  367.1 1.6 copy-done.2
  368.7 10.8 %lion_step.3 = (f32[1,384,8192]{2,1,0:T(8,128)}, bf16[1,384,8192]{2,1,0:T(8,128)(2,1)}) custom-call(s32[1]{0:T(128)} %bitcast.4.place_ref, bf16[8,384,512]{2,1,0:T(8,128)(2,1)} %copy-done.2, bf16[1,384,8192]{2,1,0:T(8,128)(2,1)} %momentum_ref.3, bf16[384,1024]{1,0:T(8,128)(2,1)} %get-tuple-element.124.refs_0_, ...), custom_call_target="tpu_custom_call", output_to_operand_aliasing={{0}: (11, {}), {1}: (12, {})} | custom-call | flops 1024 | bytes 1024 | tf_op jit(solution)/shard_map/lion_step/pallas_call | solution.py:259
  (63 shorter events, 1.3 us)
Async XLA Ops:
  0.6 9.3 %copy-start.3 = (bf16[512,2,1024]{2,1,0:T(2,128)(2,1)S(1)}, bf16[512,2,1024]{2,1,0:T(2,128)(2,1)}, u32[]{:S(2)}) copy-start(bf16[512,2,1024]{2,1,0:T(2,128)(2,1)} %param.8) | copy-start | bytes 6291460
  0.6 20.6 %collective-permute-start.1 = (bf16[64,3072]{1,0:T(8,128)(2,1)}, bf16[64,3072]{1,0:T(8,128)(2,1)S(1)}, u32[]{:S(2)}, u32[]{:S(2)}) collective-permute-start(bf16[64,3072]{1,0:T(8,128)(2,1)} %refs_0_), channel_id=1, source_target_pairs={{0,4},{1,5},{2,6},{3,7},{4,0},{5,1},{6,2},{7,3},{8,12},{9,13},{10,... | collective-permute-start | bytes 1179656 | tf_op jit(solution)/shard_map/ppermute | solution.py:23
  3.3 19.1 %collective-permute-start = (bf16[64,3072]{1,0:T(8,128)(2,1)}, bf16[64,3072]{1,0:T(8,128)(2,1)S(1)}, u32[]{:S(2)}, u32[]{:S(2)}) collective-permute-start(bf16[64,3072]{1,0:T(8,128)(2,1)} %refs_0_), channel_id=1, source_target_pairs={{0,2},{1,3},{2,0},{3,1},{4,6},{5,7},{6,4},{7,5},{8,10},{9,11},{10,... | collective-permute-start | bytes 1179656 | tf_op jit(solution)/shard_map/ppermute | solution.py:23
  3.7 33.4 %collective-permute-start.2 = (bf16[64,3072]{1,0:T(8,128)(2,1)}, bf16[64,3072]{1,0:T(8,128)(2,1)S(1)}, u32[]{:S(2)}, u32[]{:S(2)}) collective-permute-start(bf16[64,3072]{1,0:T(8,128)(2,1)} %refs_0_), channel_id=1, source_target_pairs={{0,6},{1,7},{2,4},{3,5},{4,2},{5,3},{6,0},{7,1},{8,14},{9,15},{10,... | collective-permute-start | bytes 1179656 | tf_op jit(solution)/shard_map/ppermute | solution.py:23
  21.3 15.9 %copy-start.18 = (bf16[64,3072]{1,0:T(8,128)(2,1)}, bf16[64,3072]{1,0:T(8,128)(2,1)S(1)}, u32[]{:S(2)}) copy-start(bf16[64,3072]{1,0:T(8,128)(2,1)S(1)} %collective-permute-done.1.refs_2_) | copy-start | bytes 1179652
  22.4 14.8 %copy-start.19 = (bf16[64,3072]{1,0:T(8,128)(2,1)}, bf16[64,3072]{1,0:T(8,128)(2,1)S(1)}, u32[]{:S(2)}) copy-start(bf16[64,3072]{1,0:T(8,128)(2,1)S(1)} %collective-permute-done.refs_1_) | copy-start | bytes 1179652
  37.2 0.8 copy-start.20
  40.5 48.1 %collective-permute-start.4 = (bf16[4,64,3072]{2,1,0:T(8,128)(2,1)}, bf16[4,64,3072]{2,1,0:T(8,128)(2,1)S(1)}, u32[]{:S(2)}, u32[]{:S(2)}) collective-permute-start(bf16[4,64,3072]{2,1,0:T(8,128)(2,1)} %placed_blocks.1.mine_ref), channel_id=1, source_target_pairs={{0,1},{1,0},{2,3},{3,2},{4,5},{5,4},{6,7},{7,6},{8,9},{9,8},{10,11... | collective-permute-start | bytes 4718600 | tf_op jit(solution)/shard_map/ppermute | solution.py:23
  42.0 46.6 %collective-permute-start.3 = (bf16[4,64,3072]{2,1,0:T(8,128)(2,1)}, bf16[4,64,3072]{2,1,0:T(8,128)(2,1)S(1)}, u32[]{:S(2)}, u32[]{:S(2)}) collective-permute-start(bf16[4,64,3072]{2,1,0:T(8,128)(2,1)} %placed_blocks.1.mine_ref), channel_id=1, source_target_pairs={{0,16},{8,24},{16,0},{24,8},{1,17},{9,25},{17,1},{25,9},{2,18},{10... | collective-permute-start | bytes 4718600 | tf_op jit(solution)/shard_map/ppermute | solution.py:23
  43.5 45.1 %collective-permute-start.5 = (bf16[512,1024]{1,0:T(8,128)(2,1)}, bf16[512,1024]{1,0:T(8,128)(2,1)}, u32[]{:S(2)}, u32[]{:S(2)}) collective-permute-start(bf16[512,1024]{1,0:T(8,128)(2,1)} %get-tuple-element.81), channel_id=1, source_target_pairs={{0,4},{1,5},{2,6},{3,7},{4,0},{5,1},{6,2},{7,3},{8,12},{9,13},{10,... | collective-permute-start | bytes 3145736 | tf_op jit(solution)/shard_map/ppermute | solution.py:23
  88.6 1.1 copy-start.12
  88.6 5.3 %copy-start.10 = (bf16[4,64,3072]{2,1,0:T(8,128)(2,1)}, bf16[4,64,3072]{2,1,0:T(8,128)(2,1)S(1)}, u32[]{:S(2)}) copy-start(bf16[4,64,3072]{2,1,0:T(8,128)(2,1)S(1)} %collective-permute-done.3.mine_ref) | copy-start | bytes 4718596
  93.9 49.8 %collective-permute-start.6 = (bf16[512,3072]{1,0:T(8,128)(2,1)}, bf16[512,3072]{1,0:T(8,128)(2,1)S(1)}, u32[]{:S(2)}, u32[]{:S(2)}) collective-permute-start(bf16[512,3072]{1,0:T(8,128)(2,1)} %bitcast.22), channel_id=1, source_target_pairs={{0,8},{8,0},{16,24},{24,16},{1,9},{9,1},{17,25},{25,17},{2,10},{10... | collective-permute-start | bytes 9437192 | tf_op jit(solution)/shard_map/ppermute | solution.py:23
  93.9 49.7 %collective-permute-start.9 = (bf16[2,512,1024]{2,1,0:T(8,128)(2,1)}, bf16[2,512,1024]{2,1,0:T(8,128)(2,1)S(1)}, u32[]{:S(2)}, u32[]{:S(2)}) collective-permute-start(bf16[2,512,1024]{2,1,0:T(8,128)(2,1)} %get-tuple-element.91), channel_id=1, source_target_pairs={{0,16},{8,24},{16,0},{24,8},{1,17},{9,25},{17,1},{25,9},{2,18},{10... | collective-permute-start | bytes 6291464 | tf_op jit(solution)/shard_map/ppermute | solution.py:23
  94.5 49.1 %collective-permute-start.7 = (bf16[4,64,3072]{2,1,0:T(8,128)(2,1)}, bf16[4,64,3072]{2,1,0:T(8,128)(2,1)S(1)}, u32[]{:S(2)}, u32[]{:S(2)}) collective-permute-start(bf16[4,64,3072]{2,1,0:T(8,128)(2,1)} %copy-done.10), channel_id=1, source_target_pairs={{0,1},{1,0},{2,3},{3,2},{4,5},{5,4},{6,7},{7,6},{8,9},{9,8},{10,11... | collective-permute-start | bytes 4718600 | tf_op jit(solution)/shard_map/ppermute | solution.py:23
  95.0 48.6 %collective-permute-start.8 = (bf16[512,1024]{1,0:T(8,128)(2,1)}, bf16[512,1024]{1,0:T(8,128)(2,1)S(1)}, u32[]{:S(2)}, u32[]{:S(2)}) collective-permute-start(bf16[512,1024]{1,0:T(8,128)(2,1)} %get-tuple-element.90), channel_id=1, source_target_pairs={{0,4},{1,5},{2,6},{3,7},{4,0},{5,1},{6,2},{7,3},{8,12},{9,13},{10,... | collective-permute-start | bytes 3145736 | tf_op jit(solution)/shard_map/ppermute | solution.py:23
  143.7 1.0 copy-start.17
  143.7 1.5 copy-start.11
  143.7 2.2 copy-start.8
  145.8 1.7 copy-start
  147.5 92.2 %all-to-all-start = ((bf16[8,384,512]{2,1,0:T(8,128)(2,1)}), bf16[8,384,512]{2,1,0:T(8,128)(2,1)}, u32[]{:S(2)}, u32[]{:S(2)}) async-start(bf16[8,384,512]{2,1,0:T(8,128)(2,1)} %get-tuple-element.115), calls=%async_computation | async-start | bytes 6291456 | tf_op jit(solution)/shard_map/all_to_all | solution.py:356
  154.5 11.2 %copy-start.9 = (bf16[2,512,1024]{2,1,0:T(8,128)(2,1)S(1)}, bf16[2,512,1024]{2,1,0:T(8,128)(2,1)}, u32[]{:S(2)}) copy-start(bf16[2,512,1024]{2,1,0:T(8,128)(2,1)} %copy-done.8) | copy-start | bytes 6291460
  158.9 10.8 %collective-permute-start.11 = (bf16[512,3072]{1,0:T(8,128)(2,1)}, bf16[512,3072]{1,0:T(8,128)(2,1)S(1)}, u32[]{:S(2)}, u32[]{:S(2)}) collective-permute-start(bf16[512,3072]{1,0:T(8,128)(2,1)} %bitcast.26), channel_id=1, source_target_pairs={{0,8},{8,0},{16,24},{24,16},{1,9},{9,1},{17,25},{25,17},{2,10},{10... | collective-permute-start | bytes 9437192 | tf_op jit(solution)/shard_map/ppermute | solution.py:23
  164.0 51.5 %collective-permute-start.10 = (bf16[2,512,1024]{2,1,0:T(8,128)(2,1)}, bf16[2,512,1024]{2,1,0:T(8,128)(2,1)S(1)}, u32[]{:S(2)}, u32[]{:S(2)}) collective-permute-start(bf16[2,512,1024]{2,1,0:T(8,128)(2,1)} %get-tuple-element.95), channel_id=1, source_target_pairs={{0,16},{8,24},{16,0},{24,8},{1,17},{9,25},{17,1},{25,9},{2,18},{10... | collective-permute-start | bytes 6291464 | tf_op jit(solution)/shard_map/ppermute | solution.py:23
  165.5 2.9 collective-permute-start.12
  166.8 2.8 collective-permute-start.13
  168.3 1.3 copy-start.15
  169.6 1.0 copy-start.16
  169.6 2.0 copy-start.1
  207.5 9.9 %copy-start.22 = (bf16[1,512,1024]{2,1,0:T(8,128)(2,1)S(1)}, bf16[1,512,1024]{2,1,0:T(8,128)(2,1)}, u32[]{:S(2)}) copy-start(bf16[1,512,1024]{2,1,0:T(8,128)(2,1)} %get-tuple-element.117) | copy-start | bytes 3145732
  215.5 10.1 %copy-start.21 = (s32[512,2]{0,1:T(2,128)S(1)}, s32[512,2]{0,1:T(2,128)}, u32[]{:S(2)}) copy-start(s32[512,2]{0,1:T(2,128)} %param.9) | copy-start | bytes 12292
  215.5 47.9 %collective-permute-start.14 = (f32[512,1024]{1,0:T(8,128)}, f32[512,1024]{1,0:T(8,128)}, u32[]{:S(2)}, u32[]{:S(2)}) collective-permute-start(f32[512,1024]{1,0:T(8,128)} %hidden_deriv.7), channel_id=1, source_target_pairs={{0,24},{8,16},{16,8},{24,0},{1,25},{9,17},{17,9},{25,1},{2,26},{10... | collective-permute-start | bytes 6291464 | tf_op jit(solution)/shard_map/ppermute | solution.py:23
  215.9 92.8 %collective-permute-start.15 = (f32[512,1024]{1,0:T(8,128)}, f32[512,1024]{1,0:T(8,128)}, u32[]{:S(2)}, u32[]{:S(2)}) collective-permute-start(f32[512,1024]{1,0:T(8,128)} %hidden_deriv.6), channel_id=1, source_target_pairs={{0,16},{8,24},{16,0},{24,8},{1,17},{9,25},{17,1},{25,9},{2,18},{10... | collective-permute-start | bytes 6291464 | tf_op jit(solution)/shard_map/ppermute | solution.py:23
  217.4 91.3 %collective-permute-start.16 = (f32[512,1024]{1,0:T(8,128)}, f32[512,1024]{1,0:T(8,128)}, u32[]{:S(2)}, u32[]{:S(2)}) collective-permute-start(f32[512,1024]{1,0:T(8,128)} %hidden_deriv.5), channel_id=1, source_target_pairs={{0,8},{8,0},{16,24},{24,16},{1,9},{9,1},{17,25},{25,17},{2,10},{10... | collective-permute-start | bytes 6291464 | tf_op jit(solution)/shard_map/ppermute | solution.py:23
  217.4 6.8 %collective-permute-start.17 = (bf16[1,512,1024]{2,1,0:T(8,128)(2,1)S(1)}, bf16[1,512,1024]{2,1,0:T(8,128)(2,1)S(1)}, u32[]{:S(2)}, u32[]{:S(2)}) collective-permute-start(bf16[1,512,1024]{2,1,0:T(8,128)(2,1)S(1)} %copy-done.22), channel_id=1, source_target_pairs={{0,8},{8,0},{16,24},{24,16},{1,9},{9,1},{17,25},{25,17},{2,10},{10... | collective-permute-start | bytes 3145736 | tf_op jit(solution)/shard_map/ppermute | solution.py:23
  219.4 7.0 %collective-permute-start.18 = (bf16[1,512,1024]{2,1,0:T(8,128)(2,1)}, bf16[1,512,1024]{2,1,0:T(8,128)(2,1)S(1)}, u32[]{:S(2)}, u32[]{:S(2)}) collective-permute-start(bf16[1,512,1024]{2,1,0:T(8,128)(2,1)} %get-tuple-element.140), channel_id=1, source_target_pairs={{0,8},{8,0},{16,24},{24,16},{1,9},{9,1},{17,25},{25,17},{2,10},{10... | collective-permute-start | bytes 3145736 | tf_op jit(solution)/shard_map/ppermute | solution.py:23
  224.2 2.9 copy-start.13
  224.2 20.6 %collective-permute-start.19 = (bf16[384,1024]{1,0:T(8,128)(2,1)}, bf16[384,1024]{1,0:T(8,128)(2,1)}, u32[]{:S(2)}, u32[]{:S(2)}) collective-permute-start(bf16[384,1024]{1,0:T(8,128)(2,1)} %get-tuple-element.125), channel_id=1, source_target_pairs={{0,1},{1,0},{2,3},{3,2},{4,5},{5,4},{6,7},{7,6},{8,9},{9,8},{10,11... | collective-permute-start | bytes 2359304 | tf_op jit(solution)/shard_map/ppermute | solution.py:23
  226.5 1.0 copy-start.14
  226.5 101.5 %collective-permute-start.20 = (bf16[384,1024]{1,0:T(8,128)(2,1)}, bf16[384,1024]{1,0:T(8,128)(2,1)}, u32[]{:S(2)}, u32[]{:S(2)}) collective-permute-start(bf16[384,1024]{1,0:T(8,128)(2,1)} %get-tuple-element.126), channel_id=1, source_target_pairs={{0,2},{1,3},{2,0},{3,1},{4,6},{5,7},{6,4},{7,5},{8,10},{9,11},{10,... | collective-permute-start | bytes 2359304 | tf_op jit(solution)/shard_map/ppermute | solution.py:23
  239.7 127.4 %all-to-all-start.1 = ((bf16[8,384,512]{2,1,0:T(8,128)(2,1)}), bf16[8,384,512]{2,1,0:T(8,128)(2,1)S(1)}, u32[]{:S(2)}, u32[]{:S(2)}) async-start(bf16[8,384,512]{2,1,0:T(8,128)(2,1)} %get-tuple-element.123), calls=%async_computation.1 | async-start | bytes 6291456 | tf_op jit(solution)/shard_map/all_to_all | solution.py:356
  244.8 83.1 %collective-permute-start.21 = (bf16[384,1024]{1,0:T(8,128)(2,1)}, bf16[384,1024]{1,0:T(8,128)(2,1)S(1)}, u32[]{:S(2)}, u32[]{:S(2)}) collective-permute-start(bf16[384,1024]{1,0:T(8,128)(2,1)} %get-tuple-element.127), channel_id=1, source_target_pairs={{0,3},{1,2},{2,1},{3,0},{4,7},{5,6},{6,5},{7,4},{8,11},{9,10},{10,... | collective-permute-start | bytes 2359304 | tf_op jit(solution)/shard_map/ppermute | solution.py:23
  263.4 64.5 %collective-permute-start.22 = (bf16[384,1024]{1,0:T(8,128)(2,1)}, bf16[384,1024]{1,0:T(8,128)(2,1)S(1)}, u32[]{:S(2)}, u32[]{:S(2)}) collective-permute-start(bf16[384,1024]{1,0:T(8,128)(2,1)} %get-tuple-element.129), channel_id=1, source_target_pairs={{0,1},{1,0},{2,3},{3,2},{4,5},{5,4},{6,7},{7,6},{8,9},{9,8},{10,11... | collective-permute-start | bytes 2359304 | tf_op jit(solution)/shard_map/ppermute | solution.py:23
  308.7 23.1 %collective-permute-start.23 = (bf16[384,1024]{1,0:T(8,128)(2,1)}, bf16[384,1024]{1,0:T(8,128)(2,1)S(1)}, u32[]{:S(2)}, u32[]{:S(2)}) collective-permute-start(bf16[384,1024]{1,0:T(8,128)(2,1)} %get-tuple-element.130), channel_id=1, source_target_pairs={{0,2},{1,3},{2,0},{3,1},{4,6},{5,7},{6,4},{7,5},{8,10},{9,11},{10,... | collective-permute-start | bytes 2359304 | tf_op jit(solution)/shard_map/ppermute | solution.py:23
  308.7 46.7 %collective-permute-start.24 = (bf16[384,1024]{1,0:T(8,128)(2,1)}, bf16[384,1024]{1,0:T(8,128)(2,1)S(1)}, u32[]{:S(2)}, u32[]{:S(2)}) collective-permute-start(bf16[384,1024]{1,0:T(8,128)(2,1)} %get-tuple-element.131), channel_id=1, source_target_pairs={{0,3},{1,2},{2,1},{3,0},{4,7},{5,6},{6,5},{7,4},{8,11},{9,10},{10,... | collective-permute-start | bytes 2359304 | tf_op jit(solution)/shard_map/ppermute | solution.py:23
  327.9 27.5 %copy-start.4 = (bf16[384,1024]{1,0:T(8,128)(2,1)}, bf16[384,1024]{1,0:T(8,128)(2,1)S(1)}, u32[]{:S(2)}) copy-start(bf16[384,1024]{1,0:T(8,128)(2,1)S(1)} %collective-permute-done.21.refs_3_) | copy-start | bytes 2359300
  328.0 27.5 %copy-start.5 = (bf16[384,1024]{1,0:T(8,128)(2,1)}, bf16[384,1024]{1,0:T(8,128)(2,1)S(1)}, u32[]{:S(2)}) copy-start(bf16[384,1024]{1,0:T(8,128)(2,1)S(1)} %collective-permute-done.22.refs_5_) | copy-start | bytes 2359300
  331.8 23.7 %copy-start.6 = (bf16[384,1024]{1,0:T(8,128)(2,1)}, bf16[384,1024]{1,0:T(8,128)(2,1)S(1)}, u32[]{:S(2)}) copy-start(bf16[384,1024]{1,0:T(8,128)(2,1)S(1)} %collective-permute-done.23.refs_6_) | copy-start | bytes 2359300
  355.5 0.9 copy-start.7
  367.1 1.6 copy-start.2

commit v8 on v7

--- a/solution.py
+++ b/solution.py
@@ -83,72 +83,83 @@
     token = lax.broadcasted_iota(jnp.int32, (tokens, count_rows), 0)
     row = lax.broadcasted_iota(jnp.int32, (tokens, count_rows), 1)
     here = (row >= token * topk) & (row < token * topk + topk)
+    named = named_ref[pl.ds(pl.program_id(0), 1), :]
     m = 0
     for out_ref in out_refs:
         for i in range(out_ref.shape[0]):
-            chosen = jnp.where(here & (named_ref[...] == m), 1.0, 0.0).astype(jnp.bfloat16)
+            chosen = jnp.where(here & (named == m), 1.0, 0.0).astype(jnp.bfloat16)
             out_ref[i] = jnp.dot(chosen, hidden, preferred_element_type=jnp.float32).astype(
                 jnp.bfloat16
             )
             m += 1
 
 
-def hidden_kernel(gate_ref, up_ref, named_ref, first_ref, second_ref, *out_refs):
+EIGHTHS = (3, 4, 1)
+
+
+def of_part(step, body):
+    begin = 0
+    for part, count in enumerate(EIGHTHS):
+        inside = (step >= begin) & (step < begin + count)
+        pl.when(inside)(functools.partial(body, part))
+        begin += count
+
+
+def hidden_kernel(gate_ref, up_ref, named_ref, *refs):
+    part_refs, out_refs = refs[: len(EIGHTHS)], refs[len(EIGHTHS) :]
     gate = gate_ref[...].astype(jnp.float32)
     up = up_ref[...].astype(jnp.float32)
     hidden = (gate * jax.nn.sigmoid(gate) * up).astype(jnp.bfloat16)
     pick(hidden, named_ref, out_refs)
-    early = pl.program_id(0) < pl.num_programs(0) // 2
-
-    @pl.when(early)
-    def _():
-        first_ref[...] = hidden
-
-    @pl.when(jnp.logical_not(early))
-    def _():
-        second_ref[...] = hidden
-
-
-def pick_kernel(first_ref, second_ref, named_ref, *out_refs):
-    early = pl.program_id(0) < pl.num_programs(0) // 2
-
-    @pl.when(early)
-    def _():
-        pick(first_ref[...], named_ref, out_refs)
-
-    @pl.when(jnp.logical_not(early))
-    def _():
-        pick(second_ref[...], named_ref, out_refs)
+
+    def write(part):
+        part_refs[part][...] = hidden
+
+    of_part(pl.program_id(0), write)
+
+
+def pick_kernel(*refs):
+    part_refs, named_ref = refs[: len(EIGHTHS)], refs[len(EIGHTHS)]
+
+    def read(part):
+        pick(part_refs[part][...], named_ref, refs[len(EIGHTHS) + 1 :])
+
+    of_part(pl.program_id(0), read)
 
 
 def picked_rows(arrays, named, group_tok, experts, fresh):
     cols = arrays[0].shape[1]
     topk = named.shape[1] // group_tok
-    some = 128 if group_tok % 256 == 0 else group_tok // 2
-    steps = group_tok // some
+    steps = sum(EIGHTHS)
+    some = group_tok // steps
     sizes = [1] + [1 << b for b in range(experts.bit_length() - 1)]
     out_shape = [jax.ShapeDtypeStruct((n, group_tok, cols), jnp.bfloat16) for n in sizes]
     out_specs = [pl.BlockSpec((n, some, cols), lambda i: (0, i, 0)) for n in sizes]
     rows = (some * topk, cols)
-    halves = [
-        pl.BlockSpec(rows, lambda i: (jnp.minimum(i, steps // 2 - 1), 0)),
-        pl.BlockSpec(rows, lambda i: (jnp.maximum(i - steps // 2, 0), 0)),
+    in_parts = [
+        pl.BlockSpec(
+            rows,
+            lambda i, begin=sum(EIGHTHS[:p]), count=count: (jnp.clip(i - begin, 0, count - 1), 0),
+        )
+        for p, count in enumerate(EIGHTHS)
     ]
-    in_specs = halves
+    in_specs = in_parts
     if fresh:
         in_specs = [pl.BlockSpec(rows, lambda i: (i, 0))] * 2
-        half = jax.ShapeDtypeStruct((group_tok * topk // 2, cols), jnp.bfloat16)
-        out_shape, out_specs = [half, half] + out_shape, halves + out_specs
+        out_shape = [
+            jax.ShapeDtypeStruct((n * some * topk, cols), jnp.bfloat16) for n in EIGHTHS
+        ] + out_shape
+        out_specs = in_parts + out_specs
     return pl.pallas_call(
         hidden_kernel if fresh else pick_kernel,
         grid=(steps,),
-        in_specs=in_specs + [pl.BlockSpec((1, some * topk), lambda i: (0, i))],
+        in_specs=in_specs + [pl.BlockSpec((steps, some * topk), lambda i: (0, 0))],
         out_specs=out_specs,
         out_shape=out_shape,
         compiler_params=pltpu.CompilerParams(vmem_limit_bytes=56 * MIB),
         cost_estimate=SMALL,
         name="hidden_rows",
-    )(*arrays, named)
+    )(*arrays, named.reshape(steps, some * topk))
 
 
 def spread(picked, got, experts):
@@ -227,7 +238,11 @@
         out_specs=pl.BlockSpec((group_tok, wide), lambda i: (0, i)),
         out_shape=jax.ShapeDtypeStruct((group_tok, cols), jnp.float32),
         compiler_params=pltpu.CompilerParams(vmem_limit_bytes=56 * MIB),
-        cost_estimate=SMALL,
+        cost_estimate=pl.CostEstimate(
+            flops=2 * group_tok * width * cols,
+            bytes_accessed=2 * (group_tok + cols) * width + 4 * group_tok * cols,
+            transcendentals=0,
+        ),
         name="hidden_deriv",
     )(tokens, weight)
 
@@ -252,10 +267,10 @@
 
 
 def update(part, place, grads, weight, momentum, done):
-    count, rows, some = weight.shape
+    _, rows, some = weight.shape
+    count = len(grads)
     parts = grads[0].shape[1] // some
     wide = pl.BlockSpec((1, rows, some), lambda m, place: (0, 0, (place[0] ^ m) * parts + part))
-    size = weight.size
     return pl.pallas_call(
         functools.partial(update_kernel, count),
         grid_spec=pltpu.PrefetchScalarGridSpec(
@@ -293,37 +308,42 @@
 
     blocks = [swapped(out_grad, "dp", m) for m in range(0, shards, 2)]
     named = (routing ^ mine).reshape(1, group_tok * topk)
-    first, second, *own_picked = picked_rows(
+    hidden = picked_rows(
         [gate_saved.reshape(-1, cols), up_saved.reshape(-1, cols)], named, group_tok, experts, True
     )
-    blocks, first, second, own_picked = stage(blocks, first, second, own_picked)
+    own_parts, own_picked = hidden[: len(EIGHTHS)], hidden[len(EIGHTHS) :]
+    blocks, own_parts, own_picked = stage(blocks, own_parts, own_picked)
 
     held = {0: placed_blocks(blocks, place // 2)}
-    held[0], first = stage(held[0], first)
+    held[0], own_parts = stage(held[0], own_parts)
     for m in others:
         held[m] = swapped(held[m & (m - 1)], "expert", m & -m)
-    beside = swapped(held[0], "dp", 1)
-    other_first = swapped(first, "dp", span)
-    held, beside, other_first, second, own_picked = stage(
-        held, beside, other_first, second, own_picked
+    beside = {0: swapped(held[0], "dp", 1)}
+    other_parts = [swapped(own_parts[0], "dp", span)]
+    held, beside, other_parts, own_parts, own_picked = stage(
+        held, beside, other_parts, own_parts, own_picked
     )
 
     last = (place & 1) != 0
-    tokens = {0: in_order(held[0], beside, last).reshape(group_tok, width)}
+    for m in others:
+        beside[m] = swapped(held[m], "dp", 1)
+    other_parts.append(swapped(own_parts[1], "dp", span))
+    own_got = swapped(own_picked[-1], "expert", half)
+    tokens = {0: in_order(held[0], beside[0], last).reshape(group_tok, width)}
     tokens[1] = swapped(tokens[0], "expert", 1)
-    besides = {m: swapped(held[m], "dp", 1) for m in others}
-    other_second = swapped(second, "dp", span)
-    own_got = swapped(own_picked[-1], "expert", half)
-    tokens, besides, other_second, own_got, own_picked = stage(
-        tokens, besides, other_second, own_got, own_picked
+    tokens, beside, own_got, own_picked, own_parts, other_parts = stage(
+        tokens, beside, own_got, own_picked, own_parts, other_parts
     )
 
     for m in others:
-        tokens[m] = in_order(held[m], besides[m], last).reshape(group_tok, width)
+        tokens[m] = in_order(held[m], beside[m], last).reshape(group_tok, width)
         tokens[m + 1] = swapped(tokens[m], "expert", 1)
     tokens = [tokens[m] for m in each]
+    other_parts.append(swapped(own_parts[2], "dp", span))
     own_rows = spread(own_picked, own_got, experts)
-    other_picked = picked_rows([other_first, other_second], named, group_tok, experts, False)
+    tokens, own_rows, other_parts = stage(tokens, own_rows, other_parts)
+
+    other_picked = picked_rows(other_parts, named, group_tok, experts, False)
     other_got = swapped(other_picked[-1], "expert", half)
 
     def shard_terms(hidden_rows):
@@ -344,23 +364,22 @@
     derivs = [deriv_of(tokens[m], weight) for m in each]
 
     other_got, other_picked, derivs = stage(other_got, other_picked, derivs)
+    own_grads = [swapped(own_terms[m], "dp", m) for m in range(span)]
     other_rows = spread(other_picked, other_got, experts)
+    other_rows, own_grads = stage(other_rows, own_grads)
     other_terms = shard_terms(other_rows)
 
     parts = 2 if cols % 256 == 0 else 1
     pieces = jnp.split(down_weight.reshape(shards, rows, cols), parts, axis=2)
     weights = []
     for part, piece in enumerate(pieces):
-        begun = [other_second] if part == 0 else [weights[-1], other_terms]
+        begun = [other_parts] if part == 0 else [weights[-1], other_terms]
         weights.append(
             lax.all_to_all(after(piece, *begun), "dp", split_axis=0, concat_axis=0, tiled=True)
         )
 
     other_terms = after(other_terms, weights[0])
-    grads = {}
-    for m in range(span):
-        grads[m] = swapped(own_terms[m], "dp", m)
-        grads[m ^ span] = swapped(other_terms[m], "dp", m)
+    other_grads = [swapped(other_terms[m], "dp", m) for m in range(span)]
 
     gate_saved, up_saved, _ = stage(gate_saved, up_saved, derivs)
     gate = gate_saved.astype(jnp.float32)
@@ -374,8 +393,12 @@
     d_gate = (deriv * up * sigma * (1.0 + gate * (1.0 - sigma))).astype(jnp.bfloat16)
 
     done = ()
-    for part in range(parts):
-        done = update(part, place, [grads[m] for m in range(shards)], weights[part], momentum, done)
+    for part, grads, off in [
+        (part, grads, off)
+        for part in range(parts)
+        for grads, off in ((own_grads, 0), (other_grads, span))
+    ]:
+        done = update(part, place ^ off, grads, weights[part], momentum, done)
     new_weight, new_momentum = done
     return (d_gate, d_up, new_weight, new_momentum)
 

time: 381 us -> 398 us (1.045)
  waiting for transfers between devices: 198 us -> 208 us
  Pallas kernels: 101 us -> 106 us
    ppermute x25 -> x26, waiting for transfers between devices: 198 us -> 208 us  [swapped(): return lax.ppermute(array, axis, [(i, i ^ mask) for i in range(size)])]
    unnamed x46 -> x38, local copies, waits for them, and re-layouts: 10.5 us -> 7.37 us
    ppermute x25 -> x26, starting transfers between devices: 23.5 us -> 25.5 us  [swapped(): return lax.ppermute(array, axis, [(i, i ^ mask) for i in range(size)])]
    pallas_call x2 -> x4, Pallas kernels: 21.5 us -> 23 us  [update(): pl.pallas_call(functools.partial(update_kernel, count), grid_spec=pltpu.P...]
  transfers between devices with their start and end apart: 27 -> 28, of which waited for: 12 -> 15; matrix products, arithmetic and copies ran while one was open for 9% -> 9% of each run, Pallas kernels for 22% -> 21%
where the time goes in v8:
time: 398 us; the launch traced here: 395 us
  waiting for transfers between devices  208 us (52%)
  Pallas kernels  106 us (27%)
  starting transfers between devices  39.2 us (10%)
  local copies, waits for them, and re-layouts  24 us (6%)
  other arithmetic  17 us (4%)
    ppermute x26, waiting for transfers between devices, swapped(): return lax.ppermute(array, axis, [(i, i ^ mask) for i in range(size)])  208 us
    pallas_call x4, Pallas kernels, deriv_of(): pl.pallas_call(deriv_kernel, grid=(cols // wide,), in_specs=[pl.BlockSpec...  31.6 us
    ppermute x26, starting transfers between devices, swapped(): return lax.ppermute(array, axis, [(i, i ^ mask) for i in range(size)])  25.5 us
    pallas_call x2, Pallas kernels, terms(): pl.pallas_call(functools.partial(term_kernel, count), grid_spec=pltpu.Pre...  24.6 us
    pallas_call x4, Pallas kernels, update(): pl.pallas_call(functools.partial(update_kernel, count), grid_spec=pltpu.P...  23 us
    convert_element_type x1, other arithmetic, body(): d_up = (deriv * gate * sigma).astype(jnp.bfloat16)  16.3 us
    pallas_call x2, Pallas kernels, picked_rows(): pl.pallas_call(hidden_kernel if fresh else pick_kernel, grid=(steps,), in...  15.5 us
    all_to_all x2, starting transfers between devices, body(): lax.all_to_all(after(piece, *begun), 'dp', split_axis=0, concat_axis=0, t...  13.7 us
  transfers between devices with their start and end apart: 28, of which 15 were waited for; matrix products, arithmetic and copies ran while one was open for 9% of the time, Pallas kernels for 21%

profile of v8, /device:TPU:8, one launch (start us, length us, event | category | flops | bytes accessed | tf_op | source)
XLA Modules:
  0.0 394.8 jit_solution(4593606506043881765)
XLA Ops:
  0.6 2.7 collective-permute-start.1
  3.7 0.5 collective-permute-start.2
  4.2 0.7 broadcast_xor_fusion
  5.0 0.8 reshape_reshape.10.named_ref.refs_3_
  5.8 4.1 %reshape.47.gate_ref = bf16[1024,1024]{1,0:T(8,128)(2,1)} reshape(bf16[512,2,1024]{2,1,0:T(2,128)(2,1)} %param.7) | data formatting | bytes 4194304 | tf_op jit(solution)/shard_map/reshape | solution.py:312
  9.9 2.2 reshape.48.up_ref
  12.1 8.5 %hidden_rows.2 = (bf16[384,1024]{1,0:T(8,128)(2,1)}, bf16[512,1024]{1,0:T(8,128)(2,1)}, bf16[128,1024]{1,0:T(8,128)(2,1)}, bf16[1,512,1024]{2,1,0:T(8,128)(2,1)}...) custom-call(bf16[1024,1024]{1,0:T(8,128)(2,1)} %reshape.47.gate_ref, bf16[1024,1024]{1,0:T(8,128)(2,1)} %reshape.48.up_ref, ...), custom_call_target="tpu_custom_call" | custom-call | flops 1024 | bytes 1024 | tf_op jit(solution)/shard_map/hidden_rows/pallas_call | solution.py:153
  20.6 0.7 collective-permute-done.1.refs_2_
  21.3 1.1 collective-permute-done.refs_1_
  22.4 14.7 %collective-permute-done.2.refs_3_ = bf16[64,3072]{1,0:T(8,128)(2,1)S(1)} collective-permute-done((bf16[64,3072]{1,0:T(8,128)(2,1)}, bf16[64,3072]{1,0:T(8,128)(2,1)S(1)}, u32[]{:S(2)}, u32[]{:S(2)}) %collective-permute-start.2) | collective-permute-done | bytes 393248 | tf_op jit(solution)/shard_map/ppermute | solution.py:23
  37.2 0.7 copy-done.12
  37.9 2.6 placed_blocks.1.mine_ref
  40.5 1.5 collective-permute-start.4
  42.0 1.5 collective-permute-start.3
  43.5 33.9 %collective-permute-done.5.refs_0_ = bf16[384,1024]{1,0:T(8,128)(2,1)} collective-permute-done((bf16[384,1024]{1,0:T(8,128)(2,1)}, bf16[384,1024]{1,0:T(8,128)(2,1)}, u32[]{:S(2)}, u32[]{:S(2)}) %collective-permute-start.5) | collective-permute-done | bytes 786464 | tf_op jit(solution)/shard_map/ppermute | solution.py:23
  77.4 0.9 collective-permute-done.3.mine_ref
  78.5 4.5 %side_by_side.2 = bf16[4,2,64,3072]{3,2,1,0:T(8,128)(2,1)} custom-call(s32[1]{0:T(128)} %bitcast.place_ref, bf16[4,64,3072]{2,1,0:T(8,128)(2,1)} %placed_blocks.1.mine_ref, bf16[4,64,3072]{2,1,0:T(8,128)(2,1)} %copy-done.7), custom_call_target="tpu_custom_call" | custom-call | flops 1024 | bytes 1024 | tf_op jit(solution)/shard_map/side_by_side/pallas_call | solution.py:42
  83.0 1.6 collective-permute-start.8
  84.6 0.8 collective-permute-start.7
  85.4 1.8 collective-permute-start.9
  87.2 45.2 %collective-permute-done.9.refs_1_ = bf16[512,1024]{1,0:T(8,128)(2,1)S(1)} collective-permute-done((bf16[512,1024]{1,0:T(8,128)(2,1)}, bf16[512,1024]{1,0:T(8,128)(2,1)S(1)}, u32[]{:S(2)}, u32[]{:S(2)}) %collective-permute-start.9) | collective-permute-done | bytes 1048608 | tf_op jit(solution)/shard_map/ppermute | solution.py:23
  132.5 1.0 copy-done.9
  133.4 0.5 copy-done.8
  133.9 4.2 %side_by_side.3 = bf16[4,2,64,3072]{3,2,1,0:T(8,128)(2,1)} custom-call(s32[1]{0:T(128)} %bitcast.place_ref, bf16[4,64,3072]{2,1,0:T(8,128)(2,1)} %copy-done.6, bf16[4,64,3072]{2,1,0:T(8,128)(2,1)} %copy-done.8), custom_call_target="tpu_custom_call" | custom-call | flops 1024 | bytes 1024 | tf_op jit(solution)/shard_map/side_by_side/pallas_call | solution.py:42
  138.1 0.5 collective-permute-start.11
  138.6 1.1 fusion.10
  139.8 3.3 collective-permute-start.13
  143.1 6.0 %fusion.8 = (bf16[8,384,512]{2,1,0:T(8,128)(2,1)}, bf16[8,384,512]{2,1,0:T(8,128)(2,1)}) fusion(bf16[8,384,1024]{2,1,0:T(8,128)(2,1)} %bitcast.26), kind=kLoop, calls=%fused_computation.19 | loop fusion | bytes 12582912 | tf_op jit(solution)/shard_map/split | solution.py:373
  149.1 5.2 %collective-permute-done.13.refs_2_ = bf16[128,1024]{1,0:T(8,128)(2,1)S(1)} collective-permute-done((bf16[128,1024]{1,0:T(8,128)(2,1)S(1)}, bf16[128,1024]{1,0:T(8,128)(2,1)S(1)}, u32[]{:S(2)}, u32[]{:S(2)}) %collective-permute-start.13) | collective-permute-done | bytes 262176 | tf_op jit(solution)/shard_map/ppermute | solution.py:23
  154.3 0.7 copy-done.13
  155.0 6.7 %all-to-all-start = ((bf16[8,384,512]{2,1,0:T(8,128)(2,1)}), bf16[8,384,512]{2,1,0:T(8,128)(2,1)S(1)}, u32[]{:S(2)}, u32[]{:S(2)}) async-start(bf16[8,384,512]{2,1,0:T(8,128)(2,1)} %get-tuple-element.163), calls=%async_computation | async-start | bytes 6291456 | tf_op jit(solution)/shard_map/all_to_all | solution.py:378
  161.7 7.0 %hidden_rows.3 = (bf16[1,512,1024]{2,1,0:T(8,128)(2,1)}, bf16[1,512,1024]{2,1,0:T(8,128)(2,1)}, bf16[2,512,1024]{2,1,0:T(8,128)(2,1)}) custom-call(bf16[384,1024]{1,0:T(8,128)(2,1)} %collective-permute-done.5.refs_0_, bf16[512,1024]{1,0:T(8,128)(2,1)} %copy-done.9, bf16[128,1024]{1,0:T(8,128)(2,1)} %copy-done.13, s32[8,128]{1,0:T(8,128)} %reshape_reshape.10.named_ref.refs_3_), custom_call_target="tpu_custom_call" | custom-call | flops 1024 | bytes 1024 | tf_op jit(solution)/shard_map/hidden_rows/pallas_call | solution.py:153
  168.7 1.1 collective-permute-start.14
  169.8 12.3 %group_terms.2 = (bf16[384,1024]{1,0:T(8,128)(2,1)}, bf16[384,1024]{1,0:T(8,128)(2,1)}, bf16[384,1024]{1,0:T(8,128)(2,1)}, bf16[384,1024]{1,0:T(8,128)(2,1)}) custom-call(s32[1]{0:T(128)} %bitcast.9.place_ref, bf16[512,3072]{1,0:T(8,128)(2,1)} %bitcast.19, bf16[512,3072]{1,0:T(8,128)(2,1)} %collective-permute-done.6.refs_1_.tokens_ref, ...), custom_call_target="tpu_custom_call" | custom-call | flops 1024 | bytes 1024 | tf_op jit(solution)/shard_map/group_terms/pallas_call | solution.py:202
  182.1 1.5 collective-permute-start.20
  183.6 7.9 %hidden_deriv.7 = f32[512,1024]{1,0:T(8,128)} custom-call(bf16[512,3072]{1,0:T(8,128)(2,1)} %collective-permute-done.10.refs_3_.tokens_ref, bf16[3072,1024]{1,0:T(8,128)(2,1)} %bitcast.27), custom_call_target="tpu_custom_call" | custom-call | flops 3221225472 | bytes 11534336 | tf_op jit(solution)/shard_map/hidden_deriv/pallas_call | solution.py:231
  191.5 7.9 %hidden_deriv.6 = f32[512,1024]{1,0:T(8,128)} custom-call(bf16[512,3072]{1,0:T(8,128)(2,1)} %bitcast.24, bf16[3072,1024]{1,0:T(8,128)(2,1)} %bitcast.28), custom_call_target="tpu_custom_call" | custom-call | flops 3221225472 | bytes 11534336 | tf_op jit(solution)/shard_map/hidden_deriv/pallas_call | solution.py:231
  199.3 7.9 %hidden_deriv.5 = f32[512,1024]{1,0:T(8,128)} custom-call(bf16[512,3072]{1,0:T(8,128)(2,1)} %collective-permute-done.6.refs_1_.tokens_ref, bf16[3072,1024]{1,0:T(8,128)(2,1)} %bitcast.29), custom_call_target="tpu_custom_call" | custom-call | flops 3221225472 | bytes 11534336 | tf_op jit(solution)/shard_map/hidden_deriv/pallas_call | solution.py:231
  207.2 8.0 %hidden_deriv.4 = f32[512,1024]{1,0:T(8,128)} custom-call(bf16[512,3072]{1,0:T(8,128)(2,1)} %bitcast.20, bf16[3072,1024]{1,0:T(8,128)(2,1)} %bitcast.30), custom_call_target="tpu_custom_call" | custom-call | flops 3221225472 | bytes 11534336 | tf_op jit(solution)/shard_map/hidden_deriv/pallas_call | solution.py:231
  215.2 0.8 collective-permute-done.14
  216.0 1.4 collective-permute-start.16
  217.3 0.5 collective-permute-start.17
  218.1 2.6 collective-permute-start.22
  220.8 1.5 fusion.9
  222.3 24.9 %collective-permute-done.21.refs_2_ = bf16[384,1024]{1,0:T(8,128)(2,1)} collective-permute-done((bf16[384,1024]{1,0:T(8,128)(2,1)S(1)}, bf16[384,1024]{1,0:T(8,128)(2,1)}, u32[]{:S(2)}, u32[]{:S(2)}) %collective-permute-start.21) | collective-permute-done | bytes 786464 | tf_op jit(solution)/shard_map/ppermute | solution.py:23
  247.1 16.8 %collective-permute-done.22.refs_3_ = bf16[384,1024]{1,0:T(8,128)(2,1)} collective-permute-done((bf16[384,1024]{1,0:T(8,128)(2,1)S(1)}, bf16[384,1024]{1,0:T(8,128)(2,1)}, u32[]{:S(2)}, u32[]{:S(2)}) %collective-permute-start.22) | collective-permute-done | bytes 786464 | tf_op jit(solution)/shard_map/ppermute | solution.py:23
  264.7 2.1 collective-permute-done.19
  266.9 12.4 %group_terms.3 = (bf16[384,1024]{1,0:T(8,128)(2,1)}, bf16[384,1024]{1,0:T(8,128)(2,1)}, bf16[384,1024]{1,0:T(8,128)(2,1)}, bf16[384,1024]{1,0:T(8,128)(2,1)}) custom-call(s32[1]{0:T(128)} %bitcast.9.place_ref, bf16[512,3072]{1,0:T(8,128)(2,1)} %bitcast.21, bf16[512,3072]{1,0:T(8,128)(2,1)} %collective-permute-done.6.refs_1_.tokens_ref, ...), custom_call_target="tpu_custom_call" | custom-call | flops 1024 | bytes 1024 | tf_op jit(solution)/shard_map/group_terms/pallas_call | solution.py:202
  279.3 1.6 copy-done.1
  280.9 7.0 %all-to-all-start.1 = ((bf16[8,384,512]{2,1,0:T(8,128)(2,1)}), bf16[8,384,512]{2,1,0:T(8,128)(2,1)S(1)}, u32[]{:S(2)}, u32[]{:S(2)}) async-start(bf16[8,384,512]{2,1,0:T(8,128)(2,1)} %get-tuple-element.179), calls=%async_computation.1 | async-start | bytes 6291456 | tf_op jit(solution)/shard_map/all_to_all | solution.py:378
  287.9 1.5 collective-permute-start.23
  289.4 0.6 collective-permute-start.24
  290.0 1.5 collective-permute-start.25
  291.4 17.5 %collective-permute-done.16 = f32[512,1024]{1,0:T(8,128)} collective-permute-done((f32[512,1024]{1,0:T(8,128)}, f32[512,1024]{1,0:T(8,128)}, u32[]{:S(2)}, u32[]{:S(2)}) %collective-permute-start.16) | collective-permute-done | bytes 2097184 | tf_op jit(solution)/shard_map/ppermute | solution.py:23
  308.9 16.3 %fusion.7 = (bf16[512,2,1024]{2,1,0:T(2,128)(2,1)}, bf16[512,2,1024]{2,1,0:T(2,128)(2,1)}) fusion(bf16[512,2,1024]{2,1,0:T(2,128)(2,1)} %param.7, pred[512,2]{1,0:T(8,128)(4,1)S(1)} %copy.25, pred[512,2]{1,0:T(8,128)(4,1)S(1)} %copy.24, pred[512,2]{1,0:T(8,128)(4,1)S(1)} %copy.23, pred[512,2]{1,0:T(8,128)(4,1)S(1)} %copy.21, f32[512,1024]{1,0:T(8,128)} %hidden_deriv.4, ...), kind=kLoop, calls=%fused_computation.10 | loop fusion | flops 19922944 | bytes 16781312 | tf_op jit(solution)/shard_map/convert_element_type | solution.py:392
  325.2 5.8 %lion_step.4 = (f32[1,384,8192]{2,1,0:T(8,128)}, bf16[1,384,8192]{2,1,0:T(8,128)(2,1)}) custom-call(s32[1]{0:T(128)} %bitcast.9.place_ref, bf16[8,384,512]{2,1,0:T(8,128)(2,1)} %copy-done.1, bf16[1,384,8192]{2,1,0:T(8,128)(2,1)} %momentum_ref.7, bf16[384,1024]{1,0:T(8,128)(2,1)} %get-tuple-element.184.refs_0_, ...), custom_call_target="tpu_custom_call" | custom-call | flops 1024 | bytes 1024 | tf_op jit(solution)/shard_map/lion_step/pallas_call | solution.py:274
  331.0 7.8 %collective-permute-done.23.refs_1_ = bf16[384,1024]{1,0:T(8,128)(2,1)S(1)} collective-permute-done((bf16[384,1024]{1,0:T(8,128)(2,1)}, bf16[384,1024]{1,0:T(8,128)(2,1)S(1)}, u32[]{:S(2)}, u32[]{:S(2)}) %collective-permute-start.23) | collective-permute-done | bytes 786464 | tf_op jit(solution)/shard_map/ppermute | solution.py:23
  338.8 19.6 %collective-permute-done.24.refs_2_ = bf16[384,1024]{1,0:T(8,128)(2,1)S(1)} collective-permute-done((bf16[384,1024]{1,0:T(8,128)(2,1)}, bf16[384,1024]{1,0:T(8,128)(2,1)S(1)}, u32[]{:S(2)}, u32[]{:S(2)}) %collective-permute-start.24) | collective-permute-done | bytes 786464 | tf_op jit(solution)/shard_map/ppermute | solution.py:23
  358.4 16.6 %collective-permute-done.25.refs_3_ = bf16[384,1024]{1,0:T(8,128)(2,1)S(1)} collective-permute-done((bf16[384,1024]{1,0:T(8,128)(2,1)}, bf16[384,1024]{1,0:T(8,128)(2,1)S(1)}, u32[]{:S(2)}, u32[]{:S(2)}) %collective-permute-start.25) | collective-permute-done | bytes 786464 | tf_op jit(solution)/shard_map/ppermute | solution.py:23
  375.0 0.9 copy-done.5
  375.9 5.7 %lion_step.5 = (f32[1,384,8192]{2,1,0:T(8,128)}, bf16[1,384,8192]{2,1,0:T(8,128)(2,1)}) custom-call(s32[1]{0:T(128)} %bitcast.10.place_ref, bf16[8,384,512]{2,1,0:T(8,128)(2,1)} %copy-done.1, bf16[1,384,8192]{2,1,0:T(8,128)(2,1)} %momentum_ref.7, bf16[384,1024]{1,0:T(8,128)(2,1)} %get-tuple-element.180.refs_0_, ...), custom_call_target="tpu_custom_call", output_to_operand_aliasing={{0}: (7, {}), {1}: (8, {})} | custom-call | flops 1024 | bytes 1024 | tf_op jit(solution)/shard_map/lion_step/pallas_call | solution.py:274
  381.6 1.6 copy-done
  383.2 5.7 %lion_step.6 = (f32[1,384,8192]{2,1,0:T(8,128)}, bf16[1,384,8192]{2,1,0:T(8,128)(2,1)}) custom-call(s32[1]{0:T(128)} %bitcast.9.place_ref, bf16[8,384,512]{2,1,0:T(8,128)(2,1)} %copy-done, bf16[1,384,8192]{2,1,0:T(8,128)(2,1)} %momentum_ref.7, bf16[384,1024]{1,0:T(8,128)(2,1)} %get-tuple-element.184.refs_0_, ...), custom_call_target="tpu_custom_call", output_to_operand_aliasing={{0}: (7, {}), {1}: (8, {})} | custom-call | flops 1024 | bytes 1024 | tf_op jit(solution)/shard_map/lion_step/pallas_call | solution.py:274
  389.0 5.8 %lion_step.7 = (f32[1,384,8192]{2,1,0:T(8,128)}, bf16[1,384,8192]{2,1,0:T(8,128)(2,1)}) custom-call(s32[1]{0:T(128)} %bitcast.10.place_ref, bf16[8,384,512]{2,1,0:T(8,128)(2,1)} %copy-done, bf16[1,384,8192]{2,1,0:T(8,128)(2,1)} %momentum_ref.7, bf16[384,1024]{1,0:T(8,128)(2,1)} %get-tuple-element.180.refs_0_, ...), custom_call_target="tpu_custom_call", output_to_operand_aliasing={{0}: (7, {}), {1}: (8, {})} | custom-call | flops 1024 | bytes 1024 | tf_op jit(solution)/shard_map/lion_step/pallas_call | solution.py:274
  (59 shorter events, 2.1 us)
Async XLA Ops:
  0.6 9.3 %copy-start.2 = (bf16[512,2,1024]{2,1,0:T(2,128)(2,1)S(1)}, bf16[512,2,1024]{2,1,0:T(2,128)(2,1)}, u32[]{:S(2)}) copy-start(bf16[512,2,1024]{2,1,0:T(2,128)(2,1)} %param.8) | copy-start | bytes 6291460
  0.6 20.6 %collective-permute-start.1 = (bf16[64,3072]{1,0:T(8,128)(2,1)}, bf16[64,3072]{1,0:T(8,128)(2,1)S(1)}, u32[]{:S(2)}, u32[]{:S(2)}) collective-permute-start(bf16[64,3072]{1,0:T(8,128)(2,1)} %refs_0_), channel_id=1, source_target_pairs={{0,4},{1,5},{2,6},{3,7},{4,0},{5,1},{6,2},{7,3},{8,12},{9,13},{10,... | collective-permute-start | bytes 1179656 | tf_op jit(solution)/shard_map/ppermute | solution.py:23
  3.3 19.1 %collective-permute-start = (bf16[64,3072]{1,0:T(8,128)(2,1)}, bf16[64,3072]{1,0:T(8,128)(2,1)S(1)}, u32[]{:S(2)}, u32[]{:S(2)}) collective-permute-start(bf16[64,3072]{1,0:T(8,128)(2,1)} %refs_0_), channel_id=1, source_target_pairs={{0,2},{1,3},{2,0},{3,1},{4,6},{5,7},{6,4},{7,5},{8,10},{9,11},{10,... | collective-permute-start | bytes 1179656 | tf_op jit(solution)/shard_map/ppermute | solution.py:23
  3.7 33.4 %collective-permute-start.2 = (bf16[64,3072]{1,0:T(8,128)(2,1)}, bf16[64,3072]{1,0:T(8,128)(2,1)S(1)}, u32[]{:S(2)}, u32[]{:S(2)}) collective-permute-start(bf16[64,3072]{1,0:T(8,128)(2,1)} %refs_0_), channel_id=1, source_target_pairs={{0,6},{1,7},{2,4},{3,5},{4,2},{5,3},{6,0},{7,1},{8,14},{9,15},{10,... | collective-permute-start | bytes 1179656 | tf_op jit(solution)/shard_map/ppermute | solution.py:23
  21.3 15.9 %copy-start.10 = (bf16[64,3072]{1,0:T(8,128)(2,1)}, bf16[64,3072]{1,0:T(8,128)(2,1)S(1)}, u32[]{:S(2)}) copy-start(bf16[64,3072]{1,0:T(8,128)(2,1)S(1)} %collective-permute-done.1.refs_2_) | copy-start | bytes 1179652
  22.4 14.8 %copy-start.11 = (bf16[64,3072]{1,0:T(8,128)(2,1)}, bf16[64,3072]{1,0:T(8,128)(2,1)S(1)}, u32[]{:S(2)}) copy-start(bf16[64,3072]{1,0:T(8,128)(2,1)S(1)} %collective-permute-done.refs_1_) | copy-start | bytes 1179652
  37.2 0.8 copy-start.12
  40.5 36.9 %collective-permute-start.4 = (bf16[4,64,3072]{2,1,0:T(8,128)(2,1)}, bf16[4,64,3072]{2,1,0:T(8,128)(2,1)S(1)}, u32[]{:S(2)}, u32[]{:S(2)}) collective-permute-start(bf16[4,64,3072]{2,1,0:T(8,128)(2,1)} %placed_blocks.1.mine_ref), channel_id=1, source_target_pairs={{0,1},{1,0},{2,3},{3,2},{4,5},{5,4},{6,7},{7,6},{8,9},{9,8},{10,11... | collective-permute-start | bytes 4718600 | tf_op jit(solution)/shard_map/ppermute | solution.py:23
  42.0 36.2 %collective-permute-start.3 = (bf16[4,64,3072]{2,1,0:T(8,128)(2,1)}, bf16[4,64,3072]{2,1,0:T(8,128)(2,1)S(1)}, u32[]{:S(2)}, u32[]{:S(2)}) collective-permute-start(bf16[4,64,3072]{2,1,0:T(8,128)(2,1)} %placed_blocks.1.mine_ref), channel_id=1, source_target_pairs={{0,16},{8,24},{16,0},{24,8},{1,17},{9,25},{17,1},{25,9},{2,18},{10... | collective-permute-start | bytes 4718600 | tf_op jit(solution)/shard_map/ppermute | solution.py:23
  43.5 33.9 %collective-permute-start.5 = (bf16[384,1024]{1,0:T(8,128)(2,1)}, bf16[384,1024]{1,0:T(8,128)(2,1)}, u32[]{:S(2)}, u32[]{:S(2)}) collective-permute-start(bf16[384,1024]{1,0:T(8,128)(2,1)} %get-tuple-element.114), channel_id=1, source_target_pairs={{0,4},{1,5},{2,6},{3,7},{4,0},{5,1},{6,2},{7,3},{8,12},{9,13},{10,... | collective-permute-start | bytes 2359304 | tf_op jit(solution)/shard_map/ppermute | solution.py:23
  77.4 1.1 copy-start.7
  78.3 4.7 %copy-start.6 = (bf16[4,64,3072]{2,1,0:T(8,128)(2,1)}, bf16[4,64,3072]{2,1,0:T(8,128)(2,1)S(1)}, u32[]{:S(2)}) copy-start(bf16[4,64,3072]{2,1,0:T(8,128)(2,1)S(1)} %collective-permute-done.3.mine_ref) | copy-start | bytes 4718596
  83.0 55.1 %copy-start.15 = (bf16[1,512,1024]{2,1,0:T(8,128)(2,1)S(1)}, bf16[1,512,1024]{2,1,0:T(8,128)(2,1)}, u32[]{:S(2)}) copy-start(bf16[1,512,1024]{2,1,0:T(8,128)(2,1)} %get-tuple-element.133) | copy-start | bytes 3145732
  83.0 50.9 %collective-permute-start.6 = (bf16[512,3072]{1,0:T(8,128)(2,1)}, bf16[512,3072]{1,0:T(8,128)(2,1)}, u32[]{:S(2)}, u32[]{:S(2)}) collective-permute-start(bf16[512,3072]{1,0:T(8,128)(2,1)} %bitcast.18), channel_id=1, source_target_pairs={{0,8},{8,0},{16,24},{24,16},{1,9},{9,1},{17,25},{25,17},{2,10},{10... | collective-permute-start | bytes 9437192 | tf_op jit(solution)/shard_map/ppermute | solution.py:23
  83.0 49.4 %collective-permute-start.8 = (bf16[2,512,1024]{2,1,0:T(8,128)(2,1)}, bf16[2,512,1024]{2,1,0:T(8,128)(2,1)S(1)}, u32[]{:S(2)}, u32[]{:S(2)}) collective-permute-start(bf16[2,512,1024]{2,1,0:T(8,128)(2,1)} %get-tuple-element.123), channel_id=1, source_target_pairs={{0,16},{8,24},{16,0},{24,8},{1,17},{9,25},{17,1},{25,9},{2,18},{10... | collective-permute-start | bytes 6291464 | tf_op jit(solution)/shard_map/ppermute | solution.py:23
  84.6 47.9 %collective-permute-start.7 = (bf16[4,64,3072]{2,1,0:T(8,128)(2,1)}, bf16[4,64,3072]{2,1,0:T(8,128)(2,1)S(1)}, u32[]{:S(2)}, u32[]{:S(2)}) collective-permute-start(bf16[4,64,3072]{2,1,0:T(8,128)(2,1)} %copy-done.6), channel_id=1, source_target_pairs={{0,1},{1,0},{2,3},{3,2},{4,5},{5,4},{6,7},{7,6},{8,9},{9,8},{10,11... | collective-permute-start | bytes 4718600 | tf_op jit(solution)/shard_map/ppermute | solution.py:23
  85.4 47.0 %collective-permute-start.9 = (bf16[512,1024]{1,0:T(8,128)(2,1)}, bf16[512,1024]{1,0:T(8,128)(2,1)S(1)}, u32[]{:S(2)}, u32[]{:S(2)}) collective-permute-start(bf16[512,1024]{1,0:T(8,128)(2,1)} %get-tuple-element.126), channel_id=1, source_target_pairs={{0,4},{1,5},{2,6},{3,7},{4,0},{5,1},{6,2},{7,3},{8,12},{9,13},{10,... | collective-permute-start | bytes 3145736 | tf_op jit(solution)/shard_map/ppermute | solution.py:23
  132.4 1.0 copy-start.9
  132.4 1.5 copy-start.8
  138.1 1.7 copy-start.18
  138.1 16.2 %collective-permute-start.10 = (bf16[512,3072]{1,0:T(8,128)(2,1)}, bf16[512,3072]{1,0:T(8,128)(2,1)}, u32[]{:S(2)}, u32[]{:S(2)}) collective-permute-start(bf16[512,3072]{1,0:T(8,128)(2,1)} %bitcast.22), channel_id=1, source_target_pairs={{0,8},{8,0},{16,24},{24,16},{1,9},{9,1},{17,25},{25,17},{2,10},{10... | collective-permute-start | bytes 9437192 | tf_op jit(solution)/shard_map/ppermute | solution.py:23
  138.1 16.2 %collective-permute-start.11 = (bf16[1,512,1024]{2,1,0:T(8,128)(2,1)S(1)}, bf16[1,512,1024]{2,1,0:T(8,128)(2,1)}, u32[]{:S(2)}, u32[]{:S(2)}) collective-permute-start(bf16[1,512,1024]{2,1,0:T(8,128)(2,1)S(1)} %copy-done.15), channel_id=1, source_target_pairs={{0,8},{8,0},{16,24},{24,16},{1,9},{9,1},{17,25},{25,17},{2,10},{10... | collective-permute-start | bytes 3145736 | tf_op jit(solution)/shard_map/ppermute | solution.py:23
  139.7 14.6 %collective-permute-start.12 = (bf16[1,512,1024]{2,1,0:T(8,128)(2,1)S(1)}, bf16[1,512,1024]{2,1,0:T(8,128)(2,1)}, u32[]{:S(2)}, u32[]{:S(2)}) collective-permute-start(bf16[1,512,1024]{2,1,0:T(8,128)(2,1)S(1)} %get-tuple-element.202), channel_id=1, source_target_pairs={{0,8},{8,0},{16,24},{24,16},{1,9},{9,1},{17,25},{25,17},{2,10},{10... | collective-permute-start | bytes 3145736 | tf_op jit(solution)/shard_map/ppermute | solution.py:23
  139.8 14.5 %collective-permute-start.13 = (bf16[128,1024]{1,0:T(8,128)(2,1)S(1)}, bf16[128,1024]{1,0:T(8,128)(2,1)S(1)}, u32[]{:S(2)}, u32[]{:S(2)}) collective-permute-start(bf16[128,1024]{1,0:T(8,128)(2,1)S(1)} %copy-done.18), channel_id=1, source_target_pairs={{0,4},{1,5},{2,6},{3,7},{4,0},{5,1},{6,2},{7,3},{8,12},{9,13},{10,... | collective-permute-start | bytes 786440 | tf_op jit(solution)/shard_map/ppermute | solution.py:23
  154.3 0.7 copy-start.13
  155.0 124.2 %all-to-all-start = ((bf16[8,384,512]{2,1,0:T(8,128)(2,1)}), bf16[8,384,512]{2,1,0:T(8,128)(2,1)S(1)}, u32[]{:S(2)}, u32[]{:S(2)}) async-start(bf16[8,384,512]{2,1,0:T(8,128)(2,1)} %get-tuple-element.163), calls=%async_computation | async-start | bytes 6291456 | tf_op jit(solution)/shard_map/all_to_all | solution.py:378
  168.7 47.3 %collective-permute-start.14 = (bf16[2,512,1024]{2,1,0:T(8,128)(2,1)}, bf16[2,512,1024]{2,1,0:T(8,128)(2,1)S(1)}, u32[]{:S(2)}, u32[]{:S(2)}) collective-permute-start(bf16[2,512,1024]{2,1,0:T(8,128)(2,1)} %get-tuple-element.141), channel_id=1, source_target_pairs={{0,16},{8,24},{16,0},{24,8},{1,17},{9,25},{17,1},{25,9},{2,18},{10... | collective-permute-start | bytes 6291464 | tf_op jit(solution)/shard_map/ppermute | solution.py:23
  182.1 36.0 %collective-permute-start.20 = (bf16[384,1024]{1,0:T(8,128)(2,1)}, bf16[384,1024]{1,0:T(8,128)(2,1)}, u32[]{:S(2)}, u32[]{:S(2)}) collective-permute-start(bf16[384,1024]{1,0:T(8,128)(2,1)} %get-tuple-element.168), channel_id=1, source_target_pairs={{0,1},{1,0},{2,3},{3,2},{4,5},{5,4},{6,7},{7,6},{8,9},{9,8},{10,11... | collective-permute-start | bytes 2359304 | tf_op jit(solution)/shard_map/ppermute | solution.py:23
  207.2 10.7 %copy-start.17 = (bf16[384,1024]{1,0:T(8,128)(2,1)S(1)}, bf16[384,1024]{1,0:T(8,128)(2,1)}, u32[]{:S(2)}) copy-start(bf16[384,1024]{1,0:T(8,128)(2,1)} %get-tuple-element.169) | copy-start | bytes 2359300
  207.2 11.0 %copy-start.16 = (bf16[384,1024]{1,0:T(8,128)(2,1)S(1)}, bf16[384,1024]{1,0:T(8,128)(2,1)}, u32[]{:S(2)}) copy-start(bf16[384,1024]{1,0:T(8,128)(2,1)} %get-tuple-element.170) | copy-start | bytes 2359300
  215.2 48.7 %copy-start.14 = (s32[512,2]{0,1:T(2,128)S(1)}, s32[512,2]{0,1:T(2,128)}, u32[]{:S(2)}) copy-start(s32[512,2]{0,1:T(2,128)} %param.9) | copy-start | bytes 12292
  216.0 74.0 %collective-permute-start.15 = (f32[512,1024]{1,0:T(8,128)}, f32[512,1024]{1,0:T(8,128)}, u32[]{:S(2)}, u32[]{:S(2)}) collective-permute-start(f32[512,1024]{1,0:T(8,128)} %hidden_deriv.7), channel_id=1, source_target_pairs={{0,24},{8,16},{16,8},{24,0},{1,25},{9,17},{17,9},{25,1},{2,26},{10... | collective-permute-start | bytes 6291464 | tf_op jit(solution)/shard_map/ppermute | solution.py:23
  216.0 92.9 %collective-permute-start.16 = (f32[512,1024]{1,0:T(8,128)}, f32[512,1024]{1,0:T(8,128)}, u32[]{:S(2)}, u32[]{:S(2)}) collective-permute-start(f32[512,1024]{1,0:T(8,128)} %hidden_deriv.6), channel_id=1, source_target_pairs={{0,16},{8,24},{16,0},{24,8},{1,17},{9,25},{17,1},{25,9},{2,18},{10... | collective-permute-start | bytes 6291464 | tf_op jit(solution)/shard_map/ppermute | solution.py:23
  217.3 91.6 %collective-permute-start.17 = (f32[512,1024]{1,0:T(8,128)}, f32[512,1024]{1,0:T(8,128)}, u32[]{:S(2)}, u32[]{:S(2)}) collective-permute-start(f32[512,1024]{1,0:T(8,128)} %hidden_deriv.5), channel_id=1, source_target_pairs={{0,8},{8,0},{16,24},{24,16},{1,9},{9,1},{17,25},{25,17},{2,10},{10... | collective-permute-start | bytes 6291464 | tf_op jit(solution)/shard_map/ppermute | solution.py:23
  217.9 29.3 %collective-permute-start.21 = (bf16[384,1024]{1,0:T(8,128)(2,1)S(1)}, bf16[384,1024]{1,0:T(8,128)(2,1)}, u32[]{:S(2)}, u32[]{:S(2)}) collective-permute-start(bf16[384,1024]{1,0:T(8,128)(2,1)S(1)} %copy-done.17), channel_id=1, source_target_pairs={{0,2},{1,3},{2,0},{3,1},{4,6},{5,7},{6,4},{7,5},{8,10},{9,11},{10,... | collective-permute-start | bytes 2359304 | tf_op jit(solution)/shard_map/ppermute | solution.py:23
  218.1 45.7 %collective-permute-start.22 = (bf16[384,1024]{1,0:T(8,128)(2,1)S(1)}, bf16[384,1024]{1,0:T(8,128)(2,1)}, u32[]{:S(2)}, u32[]{:S(2)}) collective-permute-start(bf16[384,1024]{1,0:T(8,128)(2,1)S(1)} %copy-done.16), channel_id=1, source_target_pairs={{0,3},{1,2},{2,1},{3,0},{4,7},{5,6},{6,5},{7,4},{8,11},{9,10},{10,... | collective-permute-start | bytes 2359304 | tf_op jit(solution)/shard_map/ppermute | solution.py:23
  247.1 17.6 %collective-permute-start.18 = (bf16[1,512,1024]{2,1,0:T(8,128)(2,1)}, bf16[1,512,1024]{2,1,0:T(8,128)(2,1)}, u32[]{:S(2)}, u32[]{:S(2)}) collective-permute-start(bf16[1,512,1024]{2,1,0:T(8,128)(2,1)} %get-tuple-element.165), channel_id=1, source_target_pairs={{0,8},{8,0},{16,24},{24,16},{1,9},{9,1},{17,25},{25,17},{2,10},{10... | collective-permute-start | bytes 3145736 | tf_op jit(solution)/shard_map/ppermute | solution.py:23
  263.9 3.0 collective-permute-start.19
  279.3 1.7 copy-start.1
  280.9 100.7 %all-to-all-start.1 = ((bf16[8,384,512]{2,1,0:T(8,128)(2,1)}), bf16[8,384,512]{2,1,0:T(8,128)(2,1)S(1)}, u32[]{:S(2)}, u32[]{:S(2)}) async-start(bf16[8,384,512]{2,1,0:T(8,128)(2,1)} %get-tuple-element.179), calls=%async_computation.1 | async-start | bytes 6291456 | tf_op jit(solution)/shard_map/all_to_all | solution.py:378
  287.9 50.8 %collective-permute-start.23 = (bf16[384,1024]{1,0:T(8,128)(2,1)}, bf16[384,1024]{1,0:T(8,128)(2,1)S(1)}, u32[]{:S(2)}, u32[]{:S(2)}) collective-permute-start(bf16[384,1024]{1,0:T(8,128)(2,1)} %get-tuple-element.181), channel_id=1, source_target_pairs={{0,1},{1,0},{2,3},{3,2},{4,5},{5,4},{6,7},{7,6},{8,9},{9,8},{10,11... | collective-permute-start | bytes 2359304 | tf_op jit(solution)/shard_map/ppermute | solution.py:23
  289.4 68.9 %collective-permute-start.24 = (bf16[384,1024]{1,0:T(8,128)(2,1)}, bf16[384,1024]{1,0:T(8,128)(2,1)S(1)}, u32[]{:S(2)}, u32[]{:S(2)}) collective-permute-start(bf16[384,1024]{1,0:T(8,128)(2,1)} %get-tuple-element.182), channel_id=1, source_target_pairs={{0,2},{1,3},{2,0},{3,1},{4,6},{5,7},{6,4},{7,5},{8,10},{9,11},{10,... | collective-permute-start | bytes 2359304 | tf_op jit(solution)/shard_map/ppermute | solution.py:23
  290.0 85.0 %collective-permute-start.25 = (bf16[384,1024]{1,0:T(8,128)(2,1)}, bf16[384,1024]{1,0:T(8,128)(2,1)S(1)}, u32[]{:S(2)}, u32[]{:S(2)}) collective-permute-start(bf16[384,1024]{1,0:T(8,128)(2,1)} %get-tuple-element.183), channel_id=1, source_target_pairs={{0,3},{1,2},{2,1},{3,0},{4,7},{5,6},{6,5},{7,4},{8,11},{9,10},{10,... | collective-permute-start | bytes 2359304 | tf_op jit(solution)/shard_map/ppermute | solution.py:23
  338.8 36.2 %copy-start.3 = (bf16[384,1024]{1,0:T(8,128)(2,1)}, bf16[384,1024]{1,0:T(8,128)(2,1)S(1)}, u32[]{:S(2)}) copy-start(bf16[384,1024]{1,0:T(8,128)(2,1)S(1)} %collective-permute-done.23.refs_1_) | copy-start | bytes 2359300
  358.4 16.6 %copy-start.4 = (bf16[384,1024]{1,0:T(8,128)(2,1)}, bf16[384,1024]{1,0:T(8,128)(2,1)S(1)}, u32[]{:S(2)}) copy-start(bf16[384,1024]{1,0:T(8,128)(2,1)S(1)} %collective-permute-done.24.refs_2_) | copy-start | bytes 2359300
  375.0 0.9 copy-start.5
  381.6 1.6 copy-start

commit v9 on v7

v9 whole, which is shorter than its diff:
```python
import functools

import jax
import jax.numpy as jnp
from jax import lax
from jax.experimental import pallas as pl
from jax.experimental.pallas import tpu as pltpu
from jax.sharding import PartitionSpec as P

beta_first = 0.9
beta_second = 0.99
step_rate = 0.01
decay_rate = 1.0
sign_width = 10.0
MIB = 1024 * 1024
SMALL = pl.CostEstimate(flops=1024, bytes_accessed=1024, transcendentals=0)


def swapped(array, axis, mask):
    if mask == 0:
        return array
    size = lax.axis_size(axis)
    return lax.ppermute(array, axis, [(i, i ^ mask) for i in range(size)])


def after(value, *others):
    return lax.optimization_barrier((value, *others))[0]


def order_kernel(place_ref, mine_ref, theirs_ref, out_ref):
    out_ref[0, place_ref[0]] = mine_ref[0]
    out_ref[0, 1 - place_ref[0]] = theirs_ref[0]


def stage(*values):
    return lax.optimization_barrier(values)


def in_order(mine, theirs, bit):
    count, some, width = mine.shape
    one = pl.BlockSpec((1, some, width), lambda i, place: (i, 0, 0))
    both = pl.pallas_call(
        order_kernel,
        grid_spec=pltpu.PrefetchScalarGridSpec(
            num_scalar_prefetch=1,
            grid=(count,),
            in_specs=[one, one],
            out_specs=pl.BlockSpec((1, 2, some, width), lambda i, place: (i, 0, 0, 0)),
        ),
        out_shape=jax.ShapeDtypeStruct((count, 2, some, width), mine.dtype),
        cost_estimate=SMALL,
        name="side_by_side",
    )(bit.astype(jnp.int32).reshape(1), mine, theirs)
    return both.reshape(2 * count, some, width)


def place_kernel(place_ref, *refs):
    for m, block_ref in enumerate(refs[:-1]):
        refs[-1][place_ref[0] ^ m] = block_ref[...]


def placed_blocks(blocks, place):
    count = len(blocks)
    return pl.pallas_call(
        place_kernel,
        grid_spec=pltpu.PrefetchScalarGridSpec(
            num_scalar_prefetch=1,
            grid=(1,),
            in_specs=[pl.BlockSpec(blocks[0].shape, lambda i, place: (0, 0))] * count,
            out_specs=pl.BlockSpec((count,) + blocks[0].shape, lambda i, place: (0, 0, 0)),
        ),
        out_shape=jax.ShapeDtypeStruct((count,) + blocks[0].shape, blocks[0].dtype),
        compiler_params=pltpu.CompilerParams(vmem_limit_bytes=56 * MIB),
        cost_estimate=SMALL,
        name="placed_blocks",
    )(place.reshape(1), *blocks)


def pick(hidden, named_ref, out_refs):
    count_rows = hidden.shape[0]
    tokens = out_refs[0].shape[1]
    topk = count_rows // tokens
    token = lax.broadcasted_iota(jnp.int32, (tokens, count_rows), 0)
    row = lax.broadcasted_iota(jnp.int32, (tokens, count_rows), 1)
    here = (row >= token * topk) & (row < token * topk + topk)
    named = named_ref[pl.ds(pl.program_id(0), 1), :]
    m = 0
    for out_ref in out_refs:
        for i in range(out_ref.shape[0]):
            chosen = jnp.where(here & (named == m), 1.0, 0.0).astype(jnp.bfloat16)
            out_ref[i] = jnp.dot(chosen, hidden, preferred_element_type=jnp.float32).astype(
                jnp.bfloat16
            )
            m += 1


def hidden_kernel(gate_ref, up_ref, named_ref, *out_refs):
    gate = gate_ref[...].astype(jnp.float32)
    up = up_ref[...].astype(jnp.float32)
    pick((gate * jax.nn.sigmoid(gate) * up).astype(jnp.bfloat16), named_ref, out_refs)


def picked_rows(gate, up, named, group_tok, experts):
    cols = gate.shape[1]
    topk = named.shape[1] // group_tok
    steps = 4
    some = group_tok // steps
    sizes = [1] + [1 << b for b in range(experts.bit_length() - 1)]
    rows = pl.BlockSpec((some * topk, cols), lambda i: (i, 0))
    return pl.pallas_call(
        hidden_kernel,
        grid=(steps,),
        in_specs=[rows, rows, pl.BlockSpec((steps, some * topk), lambda i: (0, 0))],
        out_specs=[pl.BlockSpec((n, some, cols), lambda i: (0, i, 0)) for n in sizes],
        out_shape=[jax.ShapeDtypeStruct((n, group_tok, cols), jnp.bfloat16) for n in sizes],
        compiler_params=pltpu.CompilerParams(vmem_limit_bytes=56 * MIB),
        cost_estimate=SMALL,
        name="hidden_rows",
    )(gate, up, named.reshape(steps, some * topk))


def spread(picked, got, experts):
    half = experts // 2
    held = {0: {(1 << i) >> 1: rows for i, rows in enumerate(picked)}}
    bit = half
    while bit:
        for group in list(held):
            rows = got if bit == half else swapped(held[group][bit], "expert", bit)
            held[group ^ bit] = {0: rows[:1]}
            for i in range(bit.bit_length() - 1):
                held[group ^ bit][1 << i] = rows[1 << i : 2 << i]
        bit //= 2
    return [held[m][0][0] for m in range(experts)]


def term_kernel(count, *refs):
    tokens, hidden, out_ref = refs[:count], refs[count : 2 * count], refs[-1]
    total = None
    for token_ref, hidden_ref in zip(tokens, hidden):
        one = lax.dot_general(
            token_ref[...],
            hidden_ref[...],
            (((0,), (0,)), ((), ())),
            preferred_element_type=jnp.float32,
        )
        total = one if total is None else total + one
    out_ref[...] = total.astype(jnp.bfloat16)


def terms(part, parts, tokens, hidden):
    group_tok, width = tokens[0].shape
    cols = hidden[0].shape[1] // parts
    tall = width // 8
    count = len(tokens)
    return pl.pallas_call(
        functools.partial(term_kernel, count),
        grid=(width // tall,),
        in_specs=[pl.BlockSpec((group_tok, tall), lambda i: (0, i))] * count
        + [pl.BlockSpec((group_tok, cols), lambda i: (0, part))] * count,
        out_specs=pl.BlockSpec((tall, cols), lambda i: (i, 0)),
        out_shape=jax.ShapeDtypeStruct((width, cols), jnp.bfloat16),
        compiler_params=pltpu.CompilerParams(vmem_limit_bytes=56 * MIB),
        cost_estimate=SMALL,
        name="group_terms",
    )(*tokens, *hidden)


def deriv_kernel(tokens_ref, weight_ref, out_ref):
    out_ref[...] = jnp.dot(
        tokens_ref[...], weight_ref[...], preferred_element_type=jnp.float32
    )


def deriv_of(tokens, weight):
    group_tok, width = tokens.shape
    cols = weight.shape[1]
    wide = 256 if cols % 256 == 0 else cols
    return pl.pallas_call(
        deriv_kernel,
        grid=(cols // wide,),
        in_specs=[
            pl.BlockSpec((group_tok, width), lambda i: (0, 0)),
            pl.BlockSpec((width, wide), lambda i: (0, i)),
        ],
        out_specs=pl.BlockSpec((group_tok, wide), lambda i: (0, i)),
        out_shape=jax.ShapeDtypeStruct((group_tok, cols), jnp.float32),
        compiler_params=pltpu.CompilerParams(vmem_limit_bytes=56 * MIB),
        cost_estimate=pl.CostEstimate(
            flops=2 * group_tok * width * cols,
            bytes_accessed=2 * (group_tok + cols) * width + 4 * group_tok * cols,
            transcendentals=0,
        ),
        name="hidden_deriv",
    )(tokens, weight)


def update_kernel(grad_ref, weight_ref, momentum_ref, *refs):
    new_weight_ref, new_momentum_ref = refs[-2:]
    grad = grad_ref[0].astype(jnp.float32)
    moment = momentum_ref[0].astype(jnp.float32)
    weight = weight_ref[0].astype(jnp.float32)
    mix = beta_first * moment + (1.0 - beta_first) * grad
    new_weight_ref[0] = weight * (1.0 - step_rate * decay_rate) - step_rate * jnp.tanh(
        mix / sign_width
    )
    new_momentum_ref[0] = (beta_second * moment + (1.0 - beta_second) * grad).astype(
        jnp.bfloat16
    )


def update(part, parts, grad, weight, momentum, done):
    count, rows, some = weight.shape
    own = pl.BlockSpec((1, rows, some), lambda m: (m, 0, 0))
    wide = pl.BlockSpec((1, rows, some), lambda m: (0, 0, m * parts + part))
    return pl.pallas_call(
        update_kernel,
        grid=(count,),
        in_specs=[own, own, wide] + [pl.BlockSpec(memory_space=pl.ANY)] * len(done),
        out_specs=[wide, wide],
        out_shape=[
            jax.ShapeDtypeStruct(momentum.shape, jnp.float32),
            jax.ShapeDtypeStruct(momentum.shape, jnp.bfloat16),
        ],
        input_output_aliases={3 + i: i for i in range(len(done))},
        compiler_params=pltpu.CompilerParams(vmem_limit_bytes=56 * MIB),
        cost_estimate=SMALL,
        name="lion_step",
    )(grad, weight, momentum, *done)


def body(out_grad, gate_saved, up_saved, routing, down_weight, momentum):
    experts = lax.axis_size("expert")
    shards = lax.axis_size("dp")
    group_tok, topk, cols = gate_saved.shape
    width = out_grad.shape[1]
    rows = momentum.shape[1]
    mine = lax.axis_index("expert")
    place = lax.axis_index("dp")
    each = range(experts)

    half = experts // 2
    others = sorted(range(2, experts, 2), key=lambda m: (bin(m).count("1"), -m))

    parts = 2 if cols % 256 == 0 else 1

    def to_owners(array, *begun):
        array = after(array.reshape(shards, rows, cols // parts), *begun)
        return lax.all_to_all(array, "dp", split_axis=0, concat_axis=0, tiled=True)

    blocks = [swapped(out_grad, "dp", m) for m in range(0, shards, 2)]
    named = (routing ^ mine).reshape(1, group_tok * topk)
    picked = picked_rows(
        gate_saved.reshape(-1, cols), up_saved.reshape(-1, cols), named, group_tok, experts
    )
    pieces = jnp.split(down_weight[0], parts, axis=1)
    weights = [to_owners(pieces[0], picked)]
    blocks, picked = stage(blocks, picked)

    held = {0: placed_blocks(blocks, place // 2)}
    for m in others:
        held[m] = swapped(held[m & (m - 1)], "expert", m & -m)
    beside = {0: swapped(held[0], "dp", 1)}
    held, beside, picked, weights = stage(held, beside, picked, weights)

    for piece in pieces[1:]:
        weights.append(to_owners(piece, weights))
    last = (place & 1) != 0
    for m in others:
        beside[m] = swapped(held[m], "dp", 1)
    got = swapped(picked[-1], "expert", half)
    tokens = {}
    for m in [0] + others:
        tokens[m] = in_order(held[m], beside[m], last).reshape(group_tok, width)
        tokens[m + 1] = swapped(tokens[m], "expert", 1)
    tokens = [tokens[m] for m in each]
    hidden = spread(picked, got, experts)
    tokens, hidden = stage(tokens, hidden)

    term = terms(0, parts, tokens, hidden)
    weight, term = stage(down_weight[0], term)
    derivs = [deriv_of(tokens[m], weight) for m in each]
    backs = [swapped(derivs[m], "expert", m) for m in each]
    grads = [to_owners(term, weights)]
    for part in range(1, parts):
        term = terms(part, parts, tokens, after(hidden, derivs))
        grads.append(to_owners(term, grads, backs[half]))

    gate_saved, up_saved, _ = stage(gate_saved, up_saved, derivs)
    gate = gate_saved.astype(jnp.float32)
    up = up_saved.astype(jnp.float32)
    sigma = jax.nn.sigmoid(gate)
    deriv = jnp.zeros(gate.shape, jnp.float32)
    for m in each:
        chosen = (routing == (mine ^ m))[:, :, None]
        deriv = jnp.where(chosen, backs[m][:, None, :], deriv)
    d_up = (deriv * gate * sigma).astype(jnp.bfloat16)
    d_gate = (deriv * up * sigma * (1.0 + gate * (1.0 - sigma))).astype(jnp.bfloat16)

    done = ()
    for part in range(parts):
        done = update(part, parts, grads[part], weights[part], momentum, done)
    new_weight, new_momentum = done
    return (d_gate, d_up, new_weight, new_momentum)


def solution(mesh):
    placed = (
        P(("expert", "dp"), None),
        P("expert", None, "dp"),
        P("expert", None, "dp"),
        P("expert", None),
        P("expert", None, "dp"),
        P("expert", "dp", None),
    )
    return jax.shard_map(
        body,
        mesh=mesh,
        in_specs=placed,
        out_specs=(
            P("expert", None, "dp"),
            P("expert", None, "dp"),
            P("expert", "dp", None),
            P("expert", "dp", None),
        ),
        check_vma=False,
    )
```

time: 381 us -> 439 us (1.15)
  waiting for transfers between devices: 198 us -> 262 us
  Pallas kernels: 101 us -> 93.9 us
    ppermute x25 -> x14, waiting for transfers between devices: 198 us -> 231 us  [swapped(): return lax.ppermute(array, axis, [(i, i ^ mask) for i in range(size)])]
    all_to_all x2 -> x4, waiting for transfers between devices: 0.01 us -> 30.9 us  [to_owners(): return lax.all_to_all(array, 'dp', split_axis=0, concat_axis=0, tiled=True)]
    ppermute x25 -> x14, starting transfers between devices: 23.5 us -> 12.1 us  [swapped(): return lax.ppermute(array, axis, [(i, i ^ mask) for i in range(size)])]
    all_to_all x2 -> x4, starting transfers between devices: 12.1 us -> 23.4 us  [to_owners(): return lax.all_to_all(array, 'dp', split_axis=0, concat_axis=0, tiled=True)]
    pallas_call x6 -> x5, Pallas kernels: 57.8 us -> 51.5 us  [the longest x2 25.7 us: terms(): pl.pallas_call(functools.partial(term_kernel, count), grid=(width // tall...]
    unnamed x46 -> x20, local copies, waits for them, and re-layouts: 10.5 us -> 7.8 us
  transfers between devices with their start and end apart: 27 -> 18, of which waited for: 12 -> 10; matrix products, arithmetic and copies ran while one was open for 9% -> 5% of each run, Pallas kernels for 22% -> 18%
where the time goes in v9:
time: 439 us; the launch traced here: 434 us
  waiting for transfers between devices  262 us (60%)
  Pallas kernels  93.9 us (21%)
  starting transfers between devices  35.4 us (8%)
  local copies, waits for them, and re-layouts  24.4 us (6%)
  other arithmetic  17.1 us (4%)
    ppermute x14, waiting for transfers between devices, swapped(): return lax.ppermute(array, axis, [(i, i ^ mask) for i in range(size)])  231 us
    pallas_call x4, Pallas kernels, deriv_of(): pl.pallas_call(deriv_kernel, grid=(cols // wide,), in_specs=[pl.BlockSpec...  31.5 us
    all_to_all x4, waiting for transfers between devices, to_owners(): return lax.all_to_all(array, 'dp', split_axis=0, concat_axis=0, tiled=True)  30.9 us
    pallas_call x2, Pallas kernels, terms(): pl.pallas_call(functools.partial(term_kernel, count), grid=(width // tall...  25.7 us
    all_to_all x4, starting transfers between devices, to_owners(): return lax.all_to_all(array, 'dp', split_axis=0, concat_axis=0, tiled=True)  23.4 us
    pallas_call x2, Pallas kernels, update(): pl.pallas_call(update_kernel, grid=(count,), in_specs=[own, own, wide] +...  20.3 us
    convert_element_type x1, other arithmetic, body(): d_up = (deriv * gate * sigma).astype(jnp.bfloat16)  16.3 us
    ppermute x14, starting transfers between devices, swapped(): return lax.ppermute(array, axis, [(i, i ^ mask) for i in range(size)])  12.1 us
  transfers between devices with their start and end apart: 18, of which 10 were waited for; matrix products, arithmetic and copies ran while one was open for 5% of the time, Pallas kernels for 18%

profile of v9, /device:TPU:8, one launch (start us, length us, event | category | flops | bytes accessed | tf_op | source)
XLA Modules:
  0.0 433.9 jit_solution(10673410397427549629)
XLA Ops:
  0.6 0.0 copy-start.4
  0.6 0.8 broadcast_xor_fusion
  1.5 0.1 copy.18
  1.6 0.8 reshape_reshape.9.named_ref
  2.4 4.1 reshape.46.gate_ref
  6.5 2.2 reshape.47.up_ref
  8.7 5.9 %fusion.8 = (bf16[3072,512]{1,0:T(8,128)(2,1)}, bf16[3072,512]{1,0:T(8,128)(2,1)}) fusion(bf16[3072,1024]{1,0:T(8,128)(2,1)} %bitcast.26), kind=kLoop, calls=%fused_computation.18 | loop fusion | bytes 12582912 | tf_op jit(solution)/shard_map/split | solution.py:255
  14.7 5.5 %hidden_rows.1 = (bf16[1,512,1024]{2,1,0:T(8,128)(2,1)}, bf16[1,512,1024]{2,1,0:T(8,128)(2,1)}, bf16[2,512,1024]{2,1,0:T(8,128)(2,1)}) custom-call(bf16[1024,1024]{1,0:T(8,128)(2,1)} %reshape.46.gate_ref, bf16[1024,1024]{1,0:T(8,128)(2,1)} %reshape.47.up_ref, s32[4,256]{1,0:T(4,128)} %reshape_reshape.9.named_ref), custom_call_target="tpu_custom_call" | custom-call | flops 1024 | bytes 1024 | tf_op jit(solution)/shard_map/hidden_rows/pallas_call | solution.py:110
  20.2 6.4 %all-to-all-start = ((bf16[8,384,512]{2,1,0:T(8,128)(2,1)}), bf16[8,384,512]{2,1,0:T(8,128)(2,1)S(1)}, u32[]{:S(2)}, u32[]{:S(2)}) async-start(bf16[8,384,512]{2,1,0:T(8,128)(2,1)} %bitcast.25), calls=%async_computation | async-start | bytes 6291456 | tf_op jit(solution)/shard_map/all_to_all | solution.py:248
  26.6 2.4 collective-permute-start.1
  29.0 0.6 collective-permute-start
  29.5 0.6 collective-permute-start.2
  30.1 90.0 %collective-permute-done.1.refs_2_ = bf16[64,3072]{1,0:T(8,128)(2,1)} collective-permute-done((bf16[64,3072]{1,0:T(8,128)(2,1)S(1)}, bf16[64,3072]{1,0:T(8,128)(2,1)}, u32[]{:S(2)}, u32[]{:S(2)}) %collective-permute-start.1) | collective-permute-done | bytes 393248 | tf_op jit(solution)/shard_map/ppermute | solution.py:23
  120.1 0.0 collective-permute-done.refs_1_
  120.1 9.5 %collective-permute-done.2.refs_3_ = bf16[64,3072]{1,0:T(8,128)(2,1)} collective-permute-done((bf16[64,3072]{1,0:T(8,128)(2,1)S(1)}, bf16[64,3072]{1,0:T(8,128)(2,1)}, u32[]{:S(2)}, u32[]{:S(2)}) %collective-permute-start.2) | collective-permute-done | bytes 393248 | tf_op jit(solution)/shard_map/ppermute | solution.py:23
  129.6 2.6 placed_blocks.1.mine_ref
  132.2 1.5 collective-permute-start.4
  133.7 1.5 collective-permute-start.3
  135.2 32.4 %collective-permute-done.4.theirs_ref = bf16[4,64,3072]{2,1,0:T(8,128)(2,1)S(1)} collective-permute-done((bf16[4,64,3072]{2,1,0:T(8,128)(2,1)}, bf16[4,64,3072]{2,1,0:T(8,128)(2,1)S(1)}, u32[]{:S(2)}, u32[]{:S(2)}) %collective-permute-start.4) | collective-permute-done | bytes 1572896 | tf_op jit(solution)/shard_map/ppermute | solution.py:23
  167.6 1.1 copy-done.7
  168.7 0.4 collective-permute-done.3.mine_ref
  169.1 0.0 all-to-all-done.weight_ref
  169.1 1.7 copy-done.2
  170.8 5.1 %all-to-all-start.1 = ((bf16[8,384,512]{2,1,0:T(8,128)(2,1)}), bf16[8,384,512]{2,1,0:T(8,128)(2,1)}, u32[]{:S(2)}, u32[]{:S(2)}) async-start(bf16[8,384,512]{2,1,0:T(8,128)(2,1)} %bitcast.24), calls=%async_computation.1 | async-start | bytes 6291456 | tf_op jit(solution)/shard_map/all_to_all | solution.py:248
  175.9 1.5 collective-permute-start.6
  177.3 1.5 collective-permute-start.9
  178.8 4.2 side_by_side.2
  183.0 61.6 %collective-permute-done.6.theirs_ref = bf16[4,64,3072]{2,1,0:T(8,128)(2,1)} collective-permute-done((bf16[4,64,3072]{2,1,0:T(8,128)(2,1)}, bf16[4,64,3072]{2,1,0:T(8,128)(2,1)}, u32[]{:S(2)}, u32[]{:S(2)}) %collective-permute-start.6) | collective-permute-done | bytes 1572896 | tf_op jit(solution)/shard_map/ppermute | solution.py:23
  244.6 4.2 side_by_side.3
  248.8 0.0 collective-permute-start.7
  248.8 0.5 collective-permute-start.8
  249.3 2.7 fusion.9
  252.0 0.0 collective-permute-start.10
  252.0 5.6 %collective-permute-done.8 = bf16[1,512,1024]{2,1,0:T(8,128)(2,1)S(1)} collective-permute-done((bf16[1,512,1024]{2,1,0:T(8,128)(2,1)}, bf16[1,512,1024]{2,1,0:T(8,128)(2,1)S(1)}, u32[]{:S(2)}, u32[]{:S(2)}) %collective-permute-start.8) | collective-permute-done | bytes 1048608 | tf_op jit(solution)/shard_map/ppermute | solution.py:23
  257.7 0.0 collective-permute-done.10
  257.7 0.0 collective-permute-done.5.refs_1_.tokens_ref
  257.7 0.0 copy-start
  257.7 1.0 copy-done.6
  258.7 0.3 copy-done.5
  258.9 1.1 copy-done
  260.0 1.0 copy-done.1
  261.0 12.9 %group_terms.2 = bf16[3072,512]{1,0:T(8,128)(2,1)} custom-call(bf16[512,3072]{1,0:T(8,128)(2,1)} %bitcast.15, bf16[512,3072]{1,0:T(8,128)(2,1)} %copy-done, bf16[512,3072]{1,0:T(8,128)(2,1)} %bitcast.19, bf16[512,3072]{1,0:T(8,128)(2,1)} %copy-done.1, bf16[512,1024]{1,0:T(8,128)(2,1)} %bitcast.31, bf16[512,1024]{1,0:T(8,128)(2,1)} %bitcast.33, ...), custom_call_target="tpu_custom_call" | custom-call | flops 1024 | bytes 1024 | tf_op jit(solution)/shard_map/group_terms/pallas_call | solution.py:155
  273.9 0.0 all-to-all-done.1.weight_ref
  273.9 5.1 %all-to-all-start.2 = ((bf16[8,384,512]{2,1,0:T(8,128)(2,1)}), bf16[8,384,512]{2,1,0:T(8,128)(2,1)S(1)}, u32[]{:S(2)}, u32[]{:S(2)}) async-start(bf16[8,384,512]{2,1,0:T(8,128)(2,1)} %bitcast.22), calls=%async_computation.2 | async-start | bytes 6291456 | tf_op jit(solution)/shard_map/all_to_all | solution.py:248
  279.0 7.9 %hidden_deriv.5 = f32[512,1024]{1,0:T(8,128)} custom-call(bf16[512,3072]{1,0:T(8,128)(2,1)} %bitcast.20, bf16[3072,1024]{1,0:T(8,128)(2,1)} %bitcast.27), custom_call_target="tpu_custom_call" | custom-call | flops 3221225472 | bytes 11534336 | tf_op jit(solution)/shard_map/hidden_deriv/pallas_call | solution.py:178
  286.8 1.5 collective-permute-start.12
  288.3 7.9 %hidden_deriv.6 = f32[512,1024]{1,0:T(8,128)} custom-call(bf16[512,3072]{1,0:T(8,128)(2,1)} %copy-done, bf16[3072,1024]{1,0:T(8,128)(2,1)} %bitcast.28), custom_call_target="tpu_custom_call" | custom-call | flops 3221225472 | bytes 11534336 | tf_op jit(solution)/shard_map/hidden_deriv/pallas_call | solution.py:178
  296.2 7.9 %hidden_deriv.4 = f32[512,1024]{1,0:T(8,128)} custom-call(bf16[512,3072]{1,0:T(8,128)(2,1)} %copy-done.1, bf16[3072,1024]{1,0:T(8,128)(2,1)} %bitcast.29), custom_call_target="tpu_custom_call" | custom-call | flops 3221225472 | bytes 11534336 | tf_op jit(solution)/shard_map/hidden_deriv/pallas_call | solution.py:178
  304.1 0.6 collective-permute-start.13
  304.7 0.2 copy.17
  304.9 0.2 copy.19
  305.1 0.2 copy.21
  305.3 0.2 copy.20
  305.5 7.9 %hidden_deriv.7 = f32[512,1024]{1,0:T(8,128)} custom-call(bf16[512,3072]{1,0:T(8,128)(2,1)} %bitcast.16, bf16[3072,1024]{1,0:T(8,128)(2,1)} %bitcast.30), custom_call_target="tpu_custom_call" | custom-call | flops 3221225472 | bytes 11534336 | tf_op jit(solution)/shard_map/hidden_deriv/pallas_call | solution.py:178
  313.4 12.8 %group_terms.3 = bf16[3072,512]{1,0:T(8,128)(2,1)} custom-call(bf16[512,3072]{1,0:T(8,128)(2,1)} %bitcast.17, bf16[512,3072]{1,0:T(8,128)(2,1)} %copy-done, bf16[512,3072]{1,0:T(8,128)(2,1)} %bitcast.21, bf16[512,3072]{1,0:T(8,128)(2,1)} %copy-done.1, bf16[512,1024]{1,0:T(8,128)(2,1)} %bitcast.32, bf16[512,1024]{1,0:T(8,128)(2,1)} %bitcast.34, ...), custom_call_target="tpu_custom_call" | custom-call | flops 1024 | bytes 1024 | tf_op jit(solution)/shard_map/group_terms/pallas_call | solution.py:155
  326.3 9.4 %collective-permute-done.12 = f32[512,1024]{1,0:T(8,128)} collective-permute-done((f32[512,1024]{1,0:T(8,128)}, f32[512,1024]{1,0:T(8,128)}, u32[]{:S(2)}, u32[]{:S(2)}) %collective-permute-start.12) | collective-permute-done | bytes 2097184 | tf_op jit(solution)/shard_map/ppermute | solution.py:23
  335.7 11.8 %all-to-all-done.2.grad_ref = bf16[8,384,512]{2,1,0:T(8,128)(2,1)S(1)} async-done(((bf16[8,384,512]{2,1,0:T(8,128)(2,1)}), bf16[8,384,512]{2,1,0:T(8,128)(2,1)S(1)}, u32[]{:S(2)}, u32[]{:S(2)}) %all-to-all-start.2) | async-done | bytes 3145760 | tf_op jit(solution)/shard_map/all_to_all | solution.py:248
  347.5 1.6 copy-done.3
  349.2 6.8 %all-to-all-start.3 = ((bf16[8,384,512]{2,1,0:T(8,128)(2,1)}), bf16[8,384,512]{2,1,0:T(8,128)(2,1)}, u32[]{:S(2)}, u32[]{:S(2)}) async-start(bf16[8,384,512]{2,1,0:T(8,128)(2,1)} %bitcast.23), calls=%async_computation.3 | async-start | bytes 6291456 | tf_op jit(solution)/shard_map/all_to_all | solution.py:248
  356.0 22.2 %collective-permute-done.11 = f32[512,1024]{1,0:T(8,128)} collective-permute-done((f32[512,1024]{1,0:T(8,128)}, f32[512,1024]{1,0:T(8,128)}, u32[]{:S(2)}, u32[]{:S(2)}) %collective-permute-start.11) | collective-permute-done | bytes 2097184 | tf_op jit(solution)/shard_map/ppermute | solution.py:23
  378.2 16.3 %fusion.7 = (bf16[512,2,1024]{2,1,0:T(2,128)(2,1)}, bf16[512,2,1024]{2,1,0:T(2,128)(2,1)}) fusion(bf16[512,2,1024]{2,1,0:T(2,128)(2,1)} %param.7, pred[512,2]{1,0:T(8,128)(4,1)S(1)} %copy.21, pred[512,2]{1,0:T(8,128)(4,1)S(1)} %copy.20, pred[512,2]{1,0:T(8,128)(4,1)S(1)} %copy.19, pred[512,2]{1,0:T(8,128)(4,1)S(1)} %copy.17, f32[512,1024]{1,0:T(8,128)} %hidden_deriv.7, ...), kind=kLoop, calls=%fused_computation.10 | loop fusion | flops 19922944 | bytes 16781312 | tf_op jit(solution)/shard_map/convert_element_type | solution.py:296
  394.5 10.1 %lion_step.2 = (f32[1,384,8192]{2,1,0:T(8,128)}, bf16[1,384,8192]{2,1,0:T(8,128)(2,1)}) custom-call(bf16[8,384,512]{2,1,0:T(8,128)(2,1)} %copy-done.3, bf16[8,384,512]{2,1,0:T(8,128)(2,1)} %copy-done.2, bf16[1,384,8192]{2,1,0:T(8,128)(2,1)} %momentum_ref.3), custom_call_target="tpu_custom_call" | custom-call | flops 1024 | bytes 1024 | tf_op jit(solution)/shard_map/lion_step/pallas_call | solution.py:215
  404.7 19.1 %all-to-all-done.3.grad_ref = bf16[8,384,512]{2,1,0:T(8,128)(2,1)} async-done(((bf16[8,384,512]{2,1,0:T(8,128)(2,1)}), bf16[8,384,512]{2,1,0:T(8,128)(2,1)}, u32[]{:S(2)}, u32[]{:S(2)}) %all-to-all-start.3) | async-done | bytes 3145760 | tf_op jit(solution)/shard_map/all_to_all | solution.py:248
  423.7 10.1 %lion_step.3 = (f32[1,384,8192]{2,1,0:T(8,128)}, bf16[1,384,8192]{2,1,0:T(8,128)(2,1)}) custom-call(bf16[8,384,512]{2,1,0:T(8,128)(2,1)} %all-to-all-done.3.grad_ref, bf16[8,384,512]{2,1,0:T(8,128)(2,1)} %all-to-all-done.1.weight_ref, bf16[1,384,8192]{2,1,0:T(8,128)(2,1)} %momentum_ref.3, ...), custom_call_target="tpu_custom_call", output_to_operand_aliasing={{0}: (3, {}), {1}: (4, {})} | custom-call | flops 1024 | bytes 1024 | tf_op jit(solution)/shard_map/lion_step/pallas_call | solution.py:215
  (17 shorter events, 0.0 us)
Async XLA Ops:
  0.6 5.9 %copy-start.4 = (bf16[512,2,1024]{2,1,0:T(2,128)(2,1)S(1)}, bf16[512,2,1024]{2,1,0:T(2,128)(2,1)}, u32[]{:S(2)}) copy-start(bf16[512,2,1024]{2,1,0:T(2,128)(2,1)} %param.8) | copy-start | bytes 6291460
  20.2 6.4 %copy-start.8 = (bf16[64,3072]{1,0:T(8,128)(2,1)S(1)}, bf16[64,3072]{1,0:T(8,128)(2,1)}, u32[]{:S(2)}) copy-start(bf16[64,3072]{1,0:T(8,128)(2,1)} %refs_0_) | copy-start | bytes 1179652
  20.2 148.9 %all-to-all-start = ((bf16[8,384,512]{2,1,0:T(8,128)(2,1)}), bf16[8,384,512]{2,1,0:T(8,128)(2,1)S(1)}, u32[]{:S(2)}, u32[]{:S(2)}) async-start(bf16[8,384,512]{2,1,0:T(8,128)(2,1)} %bitcast.25), calls=%async_computation | async-start | bytes 6291456 | tf_op jit(solution)/shard_map/all_to_all | solution.py:248
  26.6 93.5 %collective-permute-start.1 = (bf16[64,3072]{1,0:T(8,128)(2,1)S(1)}, bf16[64,3072]{1,0:T(8,128)(2,1)}, u32[]{:S(2)}, u32[]{:S(2)}) collective-permute-start(bf16[64,3072]{1,0:T(8,128)(2,1)S(1)} %copy-done.8), channel_id=1, source_target_pairs={{0,4},{1,5},{2,6},{3,7},{4,0},{5,1},{6,2},{7,3},{8,12},{9,13},{10,... | collective-permute-start | bytes 1179656 | tf_op jit(solution)/shard_map/ppermute | solution.py:23
  29.0 91.2 %collective-permute-start = (bf16[64,3072]{1,0:T(8,128)(2,1)S(1)}, bf16[64,3072]{1,0:T(8,128)(2,1)}, u32[]{:S(2)}, u32[]{:S(2)}) collective-permute-start(bf16[64,3072]{1,0:T(8,128)(2,1)S(1)} %copy-done.8), channel_id=1, source_target_pairs={{0,2},{1,3},{2,0},{3,1},{4,6},{5,7},{6,4},{7,5},{8,10},{9,11},{10,... | collective-permute-start | bytes 1179656 | tf_op jit(solution)/shard_map/ppermute | solution.py:23
  29.5 100.1 %collective-permute-start.2 = (bf16[64,3072]{1,0:T(8,128)(2,1)S(1)}, bf16[64,3072]{1,0:T(8,128)(2,1)}, u32[]{:S(2)}, u32[]{:S(2)}) collective-permute-start(bf16[64,3072]{1,0:T(8,128)(2,1)S(1)} %copy-done.8), channel_id=1, source_target_pairs={{0,6},{1,7},{2,4},{3,5},{4,2},{5,3},{6,0},{7,1},{8,14},{9,15},{10,... | collective-permute-start | bytes 1179656 | tf_op jit(solution)/shard_map/ppermute | solution.py:23
  132.2 35.3 %collective-permute-start.4 = (bf16[4,64,3072]{2,1,0:T(8,128)(2,1)}, bf16[4,64,3072]{2,1,0:T(8,128)(2,1)S(1)}, u32[]{:S(2)}, u32[]{:S(2)}) collective-permute-start(bf16[4,64,3072]{2,1,0:T(8,128)(2,1)} %placed_blocks.1.mine_ref), channel_id=1, source_target_pairs={{0,1},{1,0},{2,3},{3,2},{4,5},{5,4},{6,7},{7,6},{8,9},{9,8},{10,11... | collective-permute-start | bytes 4718600 | tf_op jit(solution)/shard_map/ppermute | solution.py:23
  133.7 35.4 %collective-permute-start.3 = (bf16[4,64,3072]{2,1,0:T(8,128)(2,1)}, bf16[4,64,3072]{2,1,0:T(8,128)(2,1)}, u32[]{:S(2)}, u32[]{:S(2)}) collective-permute-start(bf16[4,64,3072]{2,1,0:T(8,128)(2,1)} %placed_blocks.1.mine_ref), channel_id=1, source_target_pairs={{0,16},{8,24},{16,0},{24,8},{1,17},{9,25},{17,1},{25,9},{2,18},{10... | collective-permute-start | bytes 4718600 | tf_op jit(solution)/shard_map/ppermute | solution.py:23
  167.6 1.1 copy-start.7
  169.1 1.7 copy-start.2
  170.8 103.1 %all-to-all-start.1 = ((bf16[8,384,512]{2,1,0:T(8,128)(2,1)}), bf16[8,384,512]{2,1,0:T(8,128)(2,1)}, u32[]{:S(2)}, u32[]{:S(2)}) async-start(bf16[8,384,512]{2,1,0:T(8,128)(2,1)} %bitcast.24), calls=%async_computation.1 | async-start | bytes 6291456 | tf_op jit(solution)/shard_map/all_to_all | solution.py:248
  175.9 68.7 %collective-permute-start.6 = (bf16[4,64,3072]{2,1,0:T(8,128)(2,1)}, bf16[4,64,3072]{2,1,0:T(8,128)(2,1)}, u32[]{:S(2)}, u32[]{:S(2)}) collective-permute-start(bf16[4,64,3072]{2,1,0:T(8,128)(2,1)} %collective-permute-done.3.mine_ref), channel_id=1, source_target_pairs={{0,1},{1,0},{2,3},{3,2},{4,5},{5,4},{6,7},{7,6},{8,9},{9,8},{10,11... | collective-permute-start | bytes 4718600 | tf_op jit(solution)/shard_map/ppermute | solution.py:23
  177.3 72.0 %collective-permute-start.9 = (bf16[2,512,1024]{2,1,0:T(8,128)(2,1)}, bf16[2,512,1024]{2,1,0:T(8,128)(2,1)}, u32[]{:S(2)}, u32[]{:S(2)}) collective-permute-start(bf16[2,512,1024]{2,1,0:T(8,128)(2,1)} %get-tuple-element.61), channel_id=1, source_target_pairs={{0,16},{8,24},{16,0},{24,8},{1,17},{9,25},{17,1},{25,9},{2,18},{10... | collective-permute-start | bytes 6291464 | tf_op jit(solution)/shard_map/ppermute | solution.py:23
  183.0 74.7 %collective-permute-start.5 = (bf16[512,3072]{1,0:T(8,128)(2,1)}, bf16[512,3072]{1,0:T(8,128)(2,1)S(1)}, u32[]{:S(2)}, u32[]{:S(2)}) collective-permute-start(bf16[512,3072]{1,0:T(8,128)(2,1)} %bitcast.14), channel_id=1, source_target_pairs={{0,8},{8,0},{16,24},{24,16},{1,9},{9,1},{17,25},{25,17},{2,10},{10... | collective-permute-start | bytes 9437192 | tf_op jit(solution)/shard_map/ppermute | solution.py:23
  248.8 8.9 %collective-permute-start.7 = (bf16[512,3072]{1,0:T(8,128)(2,1)}, bf16[512,3072]{1,0:T(8,128)(2,1)S(1)}, u32[]{:S(2)}, u32[]{:S(2)}) collective-permute-start(bf16[512,3072]{1,0:T(8,128)(2,1)} %bitcast.18), channel_id=1, source_target_pairs={{0,8},{8,0},{16,24},{24,16},{1,9},{9,1},{17,25},{25,17},{2,10},{10... | collective-permute-start | bytes 9437192 | tf_op jit(solution)/shard_map/ppermute | solution.py:23
  248.8 8.9 %collective-permute-start.8 = (bf16[1,512,1024]{2,1,0:T(8,128)(2,1)}, bf16[1,512,1024]{2,1,0:T(8,128)(2,1)S(1)}, u32[]{:S(2)}, u32[]{:S(2)}) collective-permute-start(bf16[1,512,1024]{2,1,0:T(8,128)(2,1)} %get-tuple-element.60), channel_id=1, source_target_pairs={{0,8},{8,0},{16,24},{24,16},{1,9},{9,1},{17,25},{25,17},{2,10},{10... | collective-permute-start | bytes 3145736 | tf_op jit(solution)/shard_map/ppermute | solution.py:23
  252.0 5.7 %collective-permute-start.10 = (bf16[1,512,1024]{2,1,0:T(8,128)(2,1)S(1)}, bf16[1,512,1024]{2,1,0:T(8,128)(2,1)S(1)}, u32[]{:S(2)}, u32[]{:S(2)}) collective-permute-start(bf16[1,512,1024]{2,1,0:T(8,128)(2,1)S(1)} %get-tuple-element.90), channel_id=1, source_target_pairs={{0,8},{8,0},{16,24},{24,16},{1,9},{9,1},{17,25},{25,17},{2,10},{10... | collective-permute-start | bytes 3145736 | tf_op jit(solution)/shard_map/ppermute | solution.py:23
  257.7 1.3 copy-start.5
  257.7 1.0 copy-start.6
  257.7 2.3 copy-start
  258.7 2.3 copy-start.1
  273.9 73.7 %all-to-all-start.2 = ((bf16[8,384,512]{2,1,0:T(8,128)(2,1)}), bf16[8,384,512]{2,1,0:T(8,128)(2,1)S(1)}, u32[]{:S(2)}, u32[]{:S(2)}) async-start(bf16[8,384,512]{2,1,0:T(8,128)(2,1)} %bitcast.22), calls=%async_computation.2 | async-start | bytes 6291456 | tf_op jit(solution)/shard_map/all_to_all | solution.py:248
  286.8 48.9 %collective-permute-start.12 = (f32[512,1024]{1,0:T(8,128)}, f32[512,1024]{1,0:T(8,128)}, u32[]{:S(2)}, u32[]{:S(2)}) collective-permute-start(f32[512,1024]{1,0:T(8,128)} %hidden_deriv.5), channel_id=1, source_target_pairs={{0,16},{8,24},{16,0},{24,8},{1,17},{9,25},{17,1},{25,9},{2,18},{10... | collective-permute-start | bytes 6291464 | tf_op jit(solution)/shard_map/ppermute | solution.py:23
  296.2 8.5 %copy-start.9 = (s32[512,2]{0,1:T(2,128)S(1)}, s32[512,2]{0,1:T(2,128)}, u32[]{:S(2)}) copy-start(s32[512,2]{0,1:T(2,128)} %param.9) | copy-start | bytes 12292
  304.1 74.1 %collective-permute-start.11 = (f32[512,1024]{1,0:T(8,128)}, f32[512,1024]{1,0:T(8,128)}, u32[]{:S(2)}, u32[]{:S(2)}) collective-permute-start(f32[512,1024]{1,0:T(8,128)} %hidden_deriv.4), channel_id=1, source_target_pairs={{0,24},{8,16},{16,8},{24,0},{1,25},{9,17},{17,9},{25,1},{2,26},{10... | collective-permute-start | bytes 6291464 | tf_op jit(solution)/shard_map/ppermute | solution.py:23
  304.1 74.1 %collective-permute-start.13 = (f32[512,1024]{1,0:T(8,128)}, f32[512,1024]{1,0:T(8,128)}, u32[]{:S(2)}, u32[]{:S(2)}) collective-permute-start(f32[512,1024]{1,0:T(8,128)} %hidden_deriv.6), channel_id=1, source_target_pairs={{0,8},{8,0},{16,24},{24,16},{1,9},{9,1},{17,25},{25,17},{2,10},{10... | collective-permute-start | bytes 6291464 | tf_op jit(solution)/shard_map/ppermute | solution.py:23
  347.5 1.6 copy-start.3
  349.2 74.6 %all-to-all-start.3 = ((bf16[8,384,512]{2,1,0:T(8,128)(2,1)}), bf16[8,384,512]{2,1,0:T(8,128)(2,1)}, u32[]{:S(2)}, u32[]{:S(2)}) async-start(bf16[8,384,512]{2,1,0:T(8,128)(2,1)} %bitcast.23), calls=%async_computation.3 | async-start | bytes 6291456 | tf_op jit(solution)/shard_map/all_to_all | solution.py:248

commit v10 on v9

--- a/solution.py
+++ b/solution.py
@@ -194,38 +194,47 @@
     )(tokens, weight)
 
 
-def update_kernel(grad_ref, weight_ref, momentum_ref, *refs):
+def update_kernel(count, place_ref, grad_ref, momentum_ref, *refs):
+    weight_refs = refs[:count]
     new_weight_ref, new_momentum_ref = refs[-2:]
-    grad = grad_ref[0].astype(jnp.float32)
-    moment = momentum_ref[0].astype(jnp.float32)
-    weight = weight_ref[0].astype(jnp.float32)
-    mix = beta_first * moment + (1.0 - beta_first) * grad
-    new_weight_ref[0] = weight * (1.0 - step_rate * decay_rate) - step_rate * jnp.tanh(
-        mix / sign_width
-    )
-    new_momentum_ref[0] = (beta_second * moment + (1.0 - beta_second) * grad).astype(
-        jnp.bfloat16
-    )
-
-
-def update(part, parts, grad, weight, momentum, done):
-    count, rows, some = weight.shape
-    own = pl.BlockSpec((1, rows, some), lambda m: (m, 0, 0))
-    wide = pl.BlockSpec((1, rows, some), lambda m: (0, 0, m * parts + part))
-    return pl.pallas_call(
-        update_kernel,
-        grid=(count,),
-        in_specs=[own, own, wide] + [pl.BlockSpec(memory_space=pl.ANY)] * len(done),
-        out_specs=[wide, wide],
+    for m, weight_ref in enumerate(weight_refs):
+
+        @pl.when(pl.program_id(0) == m)
+        def _():
+            grad = grad_ref[0].astype(jnp.float32)
+            moment = momentum_ref[0].astype(jnp.float32)
+            weight = weight_ref[...].astype(jnp.float32)
+            mix = beta_first * moment + (1.0 - beta_first) * grad
+            new_weight_ref[0] = weight * (1.0 - step_rate * decay_rate) - step_rate * jnp.tanh(
+                mix / sign_width
+            )
+            new_momentum_ref[0] = (beta_second * moment + (1.0 - beta_second) * grad).astype(
+                jnp.bfloat16
+            )
+
+
+def update(part, parts, place, grad, weights, momentum, done):
+    count, rows, some = grad.shape
+    wide = pl.BlockSpec((1, rows, some), lambda m, place: (0, 0, (place[0] ^ m) * parts + part))
+    return pl.pallas_call(
+        functools.partial(update_kernel, count),
+        grid_spec=pltpu.PrefetchScalarGridSpec(
+            num_scalar_prefetch=1,
+            grid=(count,),
+            in_specs=[pl.BlockSpec((1, rows, some), lambda m, place: (place[0] ^ m, 0, 0)), wide]
+            + [pl.BlockSpec((rows, some), lambda m, place: (0, part))] * count
+            + [pl.BlockSpec(memory_space=pl.ANY)] * len(done),
+            out_specs=[wide, wide],
+        ),
         out_shape=[
             jax.ShapeDtypeStruct(momentum.shape, jnp.float32),
             jax.ShapeDtypeStruct(momentum.shape, jnp.bfloat16),
         ],
-        input_output_aliases={3 + i: i for i in range(len(done))},
+        input_output_aliases={3 + count + i: i for i in range(len(done))},
         compiler_params=pltpu.CompilerParams(vmem_limit_bytes=56 * MIB),
         cost_estimate=SMALL,
         name="lion_step",
-    )(grad, weight, momentum, *done)
+    )(place.reshape(1), grad, momentum, *weights, *done)
 
 
 def body(out_grad, gate_saved, up_saved, routing, down_weight, momentum):
@@ -247,43 +256,83 @@
         array = after(array.reshape(shards, rows, cols // parts), *begun)
         return lax.all_to_all(array, "dp", split_axis=0, concat_axis=0, tiled=True)
 
+    weight = down_weight[0]
+    tuned = shards == 8
+
+    def block_for(m, begin=0, count=rows):
+        return lax.dynamic_slice_in_dim(weight, (place ^ m) * rows + begin, count, axis=0)
+
     blocks = [swapped(out_grad, "dp", m) for m in range(0, shards, 2)]
     named = (routing ^ mine).reshape(1, group_tok * topk)
     picked = picked_rows(
         gate_saved.reshape(-1, cols), up_saved.reshape(-1, cols), named, group_tok, experts
     )
-    pieces = jnp.split(down_weight[0], parts, axis=1)
-    weights = [to_owners(pieces[0], picked)]
+    if tuned:
+        cut = rows // 2
+        mixed = jnp.concatenate([block_for(4), block_for(5, 0, cut)], axis=0)
+        mixed, rest, six, seven = stage(mixed, block_for(5, cut, rows - cut), block_for(6), block_for(7))
+        mixed = swapped(after(mixed, blocks[1]), "dp", 4)
     blocks, picked = stage(blocks, picked)
 
     held = {0: placed_blocks(blocks, place // 2)}
     for m in others:
         held[m] = swapped(held[m & (m - 1)], "expert", m & -m)
     beside = {0: swapped(held[0], "dp", 1)}
-    held, beside, picked, weights = stage(held, beside, picked, weights)
-
-    for piece in pieces[1:]:
-        weights.append(to_owners(piece, weights))
+    held, beside, picked = stage(held, beside, picked)
+    if tuned:
+        mixed, rest, six, held, beside, picked = stage(mixed, rest, six, held, beside, picked)
+
     last = (place & 1) != 0
     for m in others:
         beside[m] = swapped(held[m], "dp", 1)
     got = swapped(picked[-1], "expert", half)
-    tokens = {}
-    for m in [0] + others:
+    tokens = {0: in_order(held[0], beside[0], last).reshape(group_tok, width)}
+    tokens[1] = swapped(tokens[0], "expert", 1)
+    tokens, beside, got, picked = stage(tokens, beside, got, picked)
+    if tuned:
+        rest = swapped(rest, "dp", 4)
+        six = swapped(six, "dp", 6)
+        rest, six, seven, tokens, beside, got, picked = stage(
+            rest, six, seven, tokens, beside, got, picked
+        )
+
+    for m in others:
         tokens[m] = in_order(held[m], beside[m], last).reshape(group_tok, width)
         tokens[m + 1] = swapped(tokens[m], "expert", 1)
     tokens = [tokens[m] for m in each]
     hidden = spread(picked, got, experts)
-    tokens, hidden = stage(tokens, hidden)
+    if tuned:
+        one, five, weight = stage(
+            block_for(1), jnp.concatenate([mixed[rows:], rest], axis=0), weight
+        )
+        one = swapped(after(one, rest), "dp", 1)
+        seven = swapped(seven, "dp", 7)
+        tokens, hidden, one, five = stage(tokens, hidden, one, five)
+        five = swapped(five, "dp", 1)
+        first_weights, last_weights = [seven, five], []
+        weights = [block_for(0), one, None, None, mixed[:rows], five, six, seven]
+        for m in (2, 3):
+            weights[m] = swapped(after(block_for(m), hidden), "dp", m)
+            last_weights.append(weights[m])
+    else:
+        tokens, hidden = stage(tokens, hidden)
+        every = lax.all_to_all(
+            weight.reshape(shards, rows, cols), "dp", split_axis=0, concat_axis=0, tiled=True
+        )
+        first_weights, last_weights = [every], []
+        weights = [
+            lax.dynamic_index_in_dim(every, place ^ m, axis=0, keepdims=False)
+            for m in range(shards)
+        ]
 
     term = terms(0, parts, tokens, hidden)
-    weight, term = stage(down_weight[0], term)
+    weight, term = stage(weight, term)
     derivs = [deriv_of(tokens[m], weight) for m in each]
     backs = [swapped(derivs[m], "expert", m) for m in each]
-    grads = [to_owners(term, weights)]
+    grads = [to_owners(term, first_weights)]
     for part in range(1, parts):
         term = terms(part, parts, tokens, after(hidden, derivs))
-        grads.append(to_owners(term, grads, backs[half]))
+        grads.append(to_owners(term, grads, last_weights, backs[half]))
 
     gate_saved, up_saved, _ = stage(gate_saved, up_saved, derivs)
     gate = gate_saved.astype(jnp.float32)
@@ -298,7 +347,7 @@
 
     done = ()
     for part in range(parts):
-        done = update(part, parts, grads[part], weights[part], momentum, done)
+        done = update(part, parts, place, grads[part], weights, momentum, done)
     new_weight, new_momentum = done
     return (d_gate, d_up, new_weight, new_momentum)
 

time: 439 us -> 410 us (0.934)
  waiting for transfers between devices: 262 us -> 226 us
    ppermute x14 -> x22, waiting for transfers between devices: 231 us -> 191 us  [swapped(): return lax.ppermute(array, axis, [(i, i ^ mask) for i in range(size)])]
    ppermute x14 -> x22, starting transfers between devices: 12.1 us -> 23.3 us  [swapped(): return lax.ppermute(array, axis, [(i, i ^ mask) for i in range(size)])]
    all_to_all x4 -> x2, starting transfers between devices: 23.4 us -> 12.5 us  [to_owners(): return lax.all_to_all(array, 'dp', split_axis=0, concat_axis=0, tiled=True)]
    dynamic_slice x0 -> x3, local copies, waits for them, and re-layouts: none -> 7.63 us  [block_for(): lax.dynamic_slice_in_dim(weight, (place ^ m) * rows + begin, count, axis=0)]
    split x1 -> x0, local copies, waits for them, and re-layouts: 5.95 us -> none  [body(): pieces = jnp.split(down_weight[0], parts, axis=1)]
    all_to_all x4 -> x2, waiting for transfers between devices: 30.9 us -> 35.1 us  [to_owners(): return lax.all_to_all(array, 'dp', split_axis=0, concat_axis=0, tiled=True)]
  transfers between devices with their start and end apart: 18 -> 24, of which waited for: 10 -> 16; matrix products, arithmetic and copies ran while one was open for 5% -> 10% of each run, Pallas kernels for 18% -> 18%
where the time goes in v10:
time: 410 us; the launch traced here: 404 us
  waiting for transfers between devices  226 us (55%)
  Pallas kernels  95.6 us (23%)
  starting transfers between devices  35.8 us (9%)
  local copies, waits for them, and re-layouts  28.5 us (7%)
  other arithmetic  18.1 us (4%)
    ppermute x22, waiting for transfers between devices, swapped(): return lax.ppermute(array, axis, [(i, i ^ mask) for i in range(size)])  191 us
    all_to_all x2, waiting for transfers between devices, to_owners(): return lax.all_to_all(array, 'dp', split_axis=0, concat_axis=0, tiled=True)  35.1 us
    pallas_call x4, Pallas kernels, deriv_of(): pl.pallas_call(deriv_kernel, grid=(cols // wide,), in_specs=[pl.BlockSpec...  31.5 us
    pallas_call x2, Pallas kernels, terms(): pl.pallas_call(functools.partial(term_kernel, count), grid=(width // tall...  25.7 us
    ppermute x22, starting transfers between devices, swapped(): return lax.ppermute(array, axis, [(i, i ^ mask) for i in range(size)])  23.3 us
    pallas_call x2, Pallas kernels, update(): pl.pallas_call(functools.partial(update_kernel, count), grid_spec=pltpu.P...  21.5 us
    convert_element_type x1, other arithmetic, body(): d_up = (deriv * gate * sigma).astype(jnp.bfloat16)  16.3 us
    all_to_all x2, starting transfers between devices, to_owners(): return lax.all_to_all(array, 'dp', split_axis=0, concat_axis=0, tiled=True)  12.5 us
  transfers between devices with their start and end apart: 24, of which 16 were waited for; matrix products, arithmetic and copies ran while one was open for 10% of the time, Pallas kernels for 18%

profile of v10, /device:TPU:8, one launch (start us, length us, event | category | flops | bytes accessed | tf_op | source)
XLA Modules:
  0.0 404.4 jit_solution(3627752153294947325)
XLA Ops:
  0.6 2.7 collective-permute-start.2
  3.3 0.4 collective-permute-start
  3.7 0.5 collective-permute-start.3
  4.2 0.7 broadcast_xor_fusion
  5.0 0.8 reshape_reshape.9.named_ref
  5.8 4.1 %reshape.48.gate_ref = bf16[1024,1024]{1,0:T(8,128)(2,1)} reshape(bf16[512,2,1024]{2,1,0:T(2,128)(2,1)} %param.7) | data formatting | bytes 4194304 | tf_op jit(solution)/shard_map/reshape | solution.py:268
  9.9 2.2 reshape.49.up_ref
  12.1 5.5 %hidden_rows.1 = (bf16[1,512,1024]{2,1,0:T(8,128)(2,1)}, bf16[1,512,1024]{2,1,0:T(8,128)(2,1)}, bf16[2,512,1024]{2,1,0:T(8,128)(2,1)}) custom-call(bf16[1024,1024]{1,0:T(8,128)(2,1)} %reshape.48.gate_ref, bf16[1024,1024]{1,0:T(8,128)(2,1)} %reshape.49.up_ref, s32[4,256]{1,0:T(4,128)} %reshape_reshape.9.named_ref), custom_call_target="tpu_custom_call" | custom-call | flops 1024 | bytes 1024 | tf_op jit(solution)/shard_map/hidden_rows/pallas_call | solution.py:110
  17.6 3.6 collective-permute-done.2.refs_2_
  21.2 1.1 collective-permute-done.refs_1_
  22.4 14.7 %collective-permute-done.3.refs_3_ = bf16[64,3072]{1,0:T(8,128)(2,1)S(1)} collective-permute-done((bf16[64,3072]{1,0:T(8,128)(2,1)}, bf16[64,3072]{1,0:T(8,128)(2,1)S(1)}, u32[]{:S(2)}, u32[]{:S(2)}) %collective-permute-start.3) | collective-permute-done | bytes 393248 | tf_op jit(solution)/shard_map/ppermute | solution.py:23
  37.1 0.8 copy-done.19
  37.9 2.6 placed_blocks.1.mine_ref
  40.5 1.5 collective-permute-start.5
  42.0 1.5 collective-permute-start.4
  43.5 1.2 dynamic-slice_bitcast_fusion.4
  44.7 3.4 dynamic-slice_bitcast_fusion
  48.1 1.1 pad_maximum_fusion
  49.2 27.9 %collective-permute-done.5.theirs_ref = bf16[4,64,3072]{2,1,0:T(8,128)(2,1)} collective-permute-done((bf16[4,64,3072]{2,1,0:T(8,128)(2,1)}, bf16[4,64,3072]{2,1,0:T(8,128)(2,1)}, u32[]{:S(2)}, u32[]{:S(2)}) %collective-permute-start.5) | collective-permute-done | bytes 1572896 | tf_op jit(solution)/shard_map/ppermute | solution.py:23
  77.1 1.1 collective-permute-done.4.mine_ref
  78.3 21.7 %collective-permute-done.1 = bf16[576,1024]{1,0:T(8,128)(2,1)S(1)} collective-permute-done((bf16[576,1024]{1,0:T(8,128)(2,1)}, bf16[576,1024]{1,0:T(8,128)(2,1)S(1)}, u32[]{:S(2)}, u32[]{:S(2)}) %collective-permute-start.1) | collective-permute-done | bytes 1179680 | tf_op jit(solution)/shard_map/ppermute | solution.py:23
  99.9 4.6 %side_by_side.2 = bf16[4,2,64,3072]{3,2,1,0:T(8,128)(2,1)} custom-call(s32[1]{0:T(128)} %bitcast.6.place_ref, bf16[4,64,3072]{2,1,0:T(8,128)(2,1)} %placed_blocks.1.mine_ref, bf16[4,64,3072]{2,1,0:T(8,128)(2,1)} %collective-permute-done.5.theirs_ref), custom_call_target="tpu_custom_call" | custom-call | flops 1024 | bytes 1024 | tf_op jit(solution)/shard_map/side_by_side/pallas_call | solution.py:42
  104.6 0.6 collective-permute-start.10
  105.2 0.5 collective-permute-start.9
  105.7 2.4 collective-permute-start.7
  108.1 4.2 %collective-permute-start.6 = (bf16[192,1024]{1,0:T(8,128)(2,1)S(1)}, bf16[192,1024]{1,0:T(8,128)(2,1)S(1)}, u32[]{:S(2)}, u32[]{:S(2)}) collective-permute-start(bf16[192,1024]{1,0:T(8,128)(2,1)S(1)} %get-tuple-element.99), channel_id=1, source_target_pairs={{0,4},{1,5},{2,6},{3,7},{4,0},{5,1},{6,2},{7,3},{8,12},{9,13},{10,... | collective-permute-start | bytes 1179656 | tf_op jit(solution)/shard_map/ppermute | solution.py:23
  112.2 29.6 %collective-permute-done.9.theirs_ref = bf16[4,64,3072]{2,1,0:T(8,128)(2,1)S(1)} collective-permute-done((bf16[4,64,3072]{2,1,0:T(8,128)(2,1)}, bf16[4,64,3072]{2,1,0:T(8,128)(2,1)S(1)}, u32[]{:S(2)}, u32[]{:S(2)}) %collective-permute-start.9) | collective-permute-done | bytes 1572896 | tf_op jit(solution)/shard_map/ppermute | solution.py:23
  141.9 11.0 %collective-permute-done.10 = bf16[2,512,1024]{2,1,0:T(8,128)(2,1)S(1)} collective-permute-done((bf16[2,512,1024]{2,1,0:T(8,128)(2,1)}, bf16[2,512,1024]{2,1,0:T(8,128)(2,1)S(1)}, u32[]{:S(2)}, u32[]{:S(2)}) %collective-permute-start.10) | collective-permute-done | bytes 2097184 | tf_op jit(solution)/shard_map/ppermute | solution.py:23
  152.8 1.3 copy-done.10
  154.2 4.7 %collective-permute-done.6 = bf16[192,1024]{1,0:T(8,128)(2,1)S(1)} collective-permute-done((bf16[192,1024]{1,0:T(8,128)(2,1)S(1)}, bf16[192,1024]{1,0:T(8,128)(2,1)S(1)}, u32[]{:S(2)}, u32[]{:S(2)}) %collective-permute-start.6) | collective-permute-done | bytes 393248 | tf_op jit(solution)/shard_map/ppermute | solution.py:23
  158.8 0.7 copy-done.15
  159.6 4.2 %side_by_side.3 = bf16[4,2,64,3072]{3,2,1,0:T(8,128)(2,1)} custom-call(s32[1]{0:T(128)} %bitcast.6.place_ref, bf16[4,64,3072]{2,1,0:T(8,128)(2,1)} %copy-done.12, bf16[4,64,3072]{2,1,0:T(8,128)(2,1)} %copy-done.13), custom_call_target="tpu_custom_call" | custom-call | flops 1024 | bytes 1024 | tf_op jit(solution)/shard_map/side_by_side/pallas_call | solution.py:42
  163.9 0.5 collective-permute-start.12
  164.4 2.8 fusion.8
  167.3 1.6 collective-permute-start.14
  168.9 0.2 collective-permute-start.18
  169.1 20.7 %collective-permute-done.14.refs_1_ = bf16[384,1024]{1,0:T(8,128)(2,1)S(1)} collective-permute-done((bf16[384,1024]{1,0:T(8,128)(2,1)S(1)}, bf16[384,1024]{1,0:T(8,128)(2,1)S(1)}, u32[]{:S(2)}, u32[]{:S(2)}) %collective-permute-start.14) | collective-permute-done | bytes 786464 | tf_op jit(solution)/shard_map/ppermute | solution.py:23
  189.9 0.9 copy-done.7
  190.7 1.5 collective-permute-start.19
  192.4 12.8 %group_terms.2 = bf16[3072,512]{1,0:T(8,128)(2,1)} custom-call(bf16[512,3072]{1,0:T(8,128)(2,1)} %bitcast.26, bf16[512,3072]{1,0:T(8,128)(2,1)} %copy-done, bf16[512,3072]{1,0:T(8,128)(2,1)} %bitcast.30, bf16[512,3072]{1,0:T(8,128)(2,1)} %copy-done.1, bf16[512,1024]{1,0:T(8,128)(2,1)} %bitcast.40, bf16[512,1024]{1,0:T(8,128)(2,1)} %bitcast.42, ...), custom_call_target="tpu_custom_call" | custom-call | flops 1024 | bytes 1024 | tf_op jit(solution)/shard_map/group_terms/pallas_call | solution.py:155
  205.2 1.4 collective-permute-done.18.refs_7_
  206.6 16.7 %collective-permute-done.19.refs_5_ = bf16[384,1024]{1,0:T(8,128)(2,1)S(1)} collective-permute-done((bf16[384,1024]{1,0:T(8,128)(2,1)S(1)}, bf16[384,1024]{1,0:T(8,128)(2,1)S(1)}, u32[]{:S(2)}, u32[]{:S(2)}) %collective-permute-start.19) | collective-permute-done | bytes 786464 | tf_op jit(solution)/shard_map/ppermute | solution.py:23
  223.3 0.9 copy-done.9
  224.3 7.8 %all-to-all-start = ((bf16[8,384,512]{2,1,0:T(8,128)(2,1)}), bf16[8,384,512]{2,1,0:T(8,128)(2,1)S(1)}, u32[]{:S(2)}, u32[]{:S(2)}) async-start(bf16[8,384,512]{2,1,0:T(8,128)(2,1)} %bitcast.33), calls=%async_computation | async-start | bytes 6291456 | tf_op jit(solution)/shard_map/all_to_all | solution.py:257
  232.1 7.9 %hidden_deriv.5 = f32[512,1024]{1,0:T(8,128)} custom-call(bf16[512,3072]{1,0:T(8,128)(2,1)} %bitcast.31, bf16[3072,1024]{1,0:T(8,128)(2,1)} %bitcast.35), custom_call_target="tpu_custom_call" | custom-call | flops 3221225472 | bytes 11534336 | tf_op jit(solution)/shard_map/hidden_deriv/pallas_call | solution.py:178
  240.0 1.5 collective-permute-start.16
  241.5 7.9 %hidden_deriv.6 = f32[512,1024]{1,0:T(8,128)} custom-call(bf16[512,3072]{1,0:T(8,128)(2,1)} %copy-done, bf16[3072,1024]{1,0:T(8,128)(2,1)} %bitcast.36), custom_call_target="tpu_custom_call" | custom-call | flops 3221225472 | bytes 11534336 | tf_op jit(solution)/shard_map/hidden_deriv/pallas_call | solution.py:178
  249.3 7.9 %hidden_deriv.4 = f32[512,1024]{1,0:T(8,128)} custom-call(bf16[512,3072]{1,0:T(8,128)(2,1)} %copy-done.1, bf16[3072,1024]{1,0:T(8,128)(2,1)} %bitcast.37), custom_call_target="tpu_custom_call" | custom-call | flops 3221225472 | bytes 11534336 | tf_op jit(solution)/shard_map/hidden_deriv/pallas_call | solution.py:178
  257.2 0.6 collective-permute-start.17
  257.9 3.1 constant_dynamic-slice_fusion
  261.0 2.9 collective-permute-start.21
  264.7 2.1 slice.15.refs_4_
  266.7 7.9 %hidden_deriv.7 = f32[512,1024]{1,0:T(8,128)} custom-call(bf16[512,3072]{1,0:T(8,128)(2,1)} %bitcast.27, bf16[3072,1024]{1,0:T(8,128)(2,1)} %bitcast.39), custom_call_target="tpu_custom_call" | custom-call | flops 3221225472 | bytes 11534336 | tf_op jit(solution)/shard_map/hidden_deriv/pallas_call | solution.py:178
  274.7 12.9 %group_terms.3 = bf16[3072,512]{1,0:T(8,128)(2,1)} custom-call(bf16[512,3072]{1,0:T(8,128)(2,1)} %bitcast.28, bf16[512,3072]{1,0:T(8,128)(2,1)} %copy-done, bf16[512,3072]{1,0:T(8,128)(2,1)} %bitcast.32, bf16[512,3072]{1,0:T(8,128)(2,1)} %copy-done.1, bf16[512,1024]{1,0:T(8,128)(2,1)} %bitcast.41, bf16[512,1024]{1,0:T(8,128)(2,1)} %bitcast.43, ...), custom_call_target="tpu_custom_call" | custom-call | flops 1024 | bytes 1024 | tf_op jit(solution)/shard_map/group_terms/pallas_call | solution.py:155
  287.5 14.6 %collective-permute-done.20.refs_2_ = bf16[384,1024]{1,0:T(8,128)(2,1)} collective-permute-done((bf16[384,1024]{1,0:T(8,128)(2,1)}, bf16[384,1024]{1,0:T(8,128)(2,1)}, u32[]{:S(2)}, u32[]{:S(2)}) %collective-permute-start.20) | collective-permute-done | bytes 786464 | tf_op jit(solution)/shard_map/ppermute | solution.py:23
  302.1 15.7 %collective-permute-done.21.refs_3_ = bf16[384,1024]{1,0:T(8,128)(2,1)} collective-permute-done((bf16[384,1024]{1,0:T(8,128)(2,1)}, bf16[384,1024]{1,0:T(8,128)(2,1)}, u32[]{:S(2)}, u32[]{:S(2)}) %collective-permute-start.21) | collective-permute-done | bytes 786464 | tf_op jit(solution)/shard_map/ppermute | solution.py:23
  317.8 1.6 copy-done.3
  319.4 4.6 %all-to-all-start.1 = ((bf16[8,384,512]{2,1,0:T(8,128)(2,1)}), bf16[8,384,512]{2,1,0:T(8,128)(2,1)S(1)}, u32[]{:S(2)}, u32[]{:S(2)}) async-start(bf16[8,384,512]{2,1,0:T(8,128)(2,1)} %bitcast.34), calls=%async_computation.1 | async-start | bytes 6291456 | tf_op jit(solution)/shard_map/all_to_all | solution.py:257
  324.1 5.9 %collective-permute-done.15 = f32[512,1024]{1,0:T(8,128)} collective-permute-done((f32[512,1024]{1,0:T(8,128)}, f32[512,1024]{1,0:T(8,128)}, u32[]{:S(2)}, u32[]{:S(2)}) %collective-permute-start.15) | collective-permute-done | bytes 2097184 | tf_op jit(solution)/shard_map/ppermute | solution.py:23
  330.0 16.3 %fusion.7 = (bf16[512,2,1024]{2,1,0:T(2,128)(2,1)}, bf16[512,2,1024]{2,1,0:T(2,128)(2,1)}) fusion(bf16[512,2,1024]{2,1,0:T(2,128)(2,1)} %param.7, pred[512,2]{1,0:T(8,128)(4,1)S(1)} %copy.21, pred[512,2]{1,0:T(8,128)(4,1)S(1)} %copy.20, pred[512,2]{1,0:T(8,128)(4,1)S(1)} %copy.19, pred[512,2]{1,0:T(8,128)(4,1)S(1)} %copy.17, f32[512,1024]{1,0:T(8,128)} %hidden_deriv.7, ...), kind=kLoop, calls=%fused_computation.10 | loop fusion | flops 19922944 | bytes 16781312 | tf_op jit(solution)/shard_map/convert_element_type | solution.py:345
  346.3 10.8 %lion_step.2 = (f32[1,384,8192]{2,1,0:T(8,128)}, bf16[1,384,8192]{2,1,0:T(8,128)(2,1)}) custom-call(s32[1]{0:T(128)} %bitcast.15.place_ref, bf16[8,384,512]{2,1,0:T(8,128)(2,1)} %copy-done.3, bf16[1,384,8192]{2,1,0:T(8,128)(2,1)} %momentum_ref.3, bf16[384,1024]{1,0:T(8,128)(2,1)} %get-tuple-element.156.refs_0_, bf16[384,1024]{1,0:T(8,128)(2,1)} %copy-done.7, ...), custom_call_target="tpu_custom_call" | custom-call | flops 1024 | bytes 1024 | tf_op jit(solution)/shard_map/lion_step/pallas_call | solution.py:219
  357.1 35.1 %all-to-all-done.1.grad_ref = bf16[8,384,512]{2,1,0:T(8,128)(2,1)S(1)} async-done(((bf16[8,384,512]{2,1,0:T(8,128)(2,1)}), bf16[8,384,512]{2,1,0:T(8,128)(2,1)S(1)}, u32[]{:S(2)}, u32[]{:S(2)}) %all-to-all-start.1) | async-done | bytes 3145760 | tf_op jit(solution)/shard_map/all_to_all | solution.py:257
  392.1 1.6 copy-done.2
  393.7 10.7 %lion_step.3 = (f32[1,384,8192]{2,1,0:T(8,128)}, bf16[1,384,8192]{2,1,0:T(8,128)(2,1)}) custom-call(s32[1]{0:T(128)} %bitcast.15.place_ref, bf16[8,384,512]{2,1,0:T(8,128)(2,1)} %copy-done.2, bf16[1,384,8192]{2,1,0:T(8,128)(2,1)} %momentum_ref.3, bf16[384,1024]{1,0:T(8,128)(2,1)} %get-tuple-element.156.refs_0_, ...), custom_call_target="tpu_custom_call", output_to_operand_aliasing={{0}: (11, {}), {1}: (12, {})} | custom-call | flops 1024 | bytes 1024 | tf_op jit(solution)/shard_map/lion_step/pallas_call | solution.py:219
  (58 shorter events, 1.5 us)
Async XLA Ops:
  0.6 20.6 %collective-permute-start.2 = (bf16[64,3072]{1,0:T(8,128)(2,1)}, bf16[64,3072]{1,0:T(8,128)(2,1)S(1)}, u32[]{:S(2)}, u32[]{:S(2)}) collective-permute-start(bf16[64,3072]{1,0:T(8,128)(2,1)} %refs_0_), channel_id=1, source_target_pairs={{0,4},{1,5},{2,6},{3,7},{4,0},{5,1},{6,2},{7,3},{8,12},{9,13},{10,... | collective-permute-start | bytes 1179656 | tf_op jit(solution)/shard_map/ppermute | solution.py:23
  3.3 19.1 %collective-permute-start = (bf16[64,3072]{1,0:T(8,128)(2,1)}, bf16[64,3072]{1,0:T(8,128)(2,1)S(1)}, u32[]{:S(2)}, u32[]{:S(2)}) collective-permute-start(bf16[64,3072]{1,0:T(8,128)(2,1)} %refs_0_), channel_id=1, source_target_pairs={{0,2},{1,3},{2,0},{3,1},{4,6},{5,7},{6,4},{7,5},{8,10},{9,11},{10,... | collective-permute-start | bytes 1179656 | tf_op jit(solution)/shard_map/ppermute | solution.py:23
  3.7 33.4 %collective-permute-start.3 = (bf16[64,3072]{1,0:T(8,128)(2,1)}, bf16[64,3072]{1,0:T(8,128)(2,1)S(1)}, u32[]{:S(2)}, u32[]{:S(2)}) collective-permute-start(bf16[64,3072]{1,0:T(8,128)(2,1)} %refs_0_), channel_id=1, source_target_pairs={{0,6},{1,7},{2,4},{3,5},{4,2},{5,3},{6,0},{7,1},{8,14},{9,15},{10,... | collective-permute-start | bytes 1179656 | tf_op jit(solution)/shard_map/ppermute | solution.py:23
  4.9 5.0 %copy-start.4 = (bf16[512,2,1024]{2,1,0:T(2,128)(2,1)S(1)}, bf16[512,2,1024]{2,1,0:T(2,128)(2,1)}, u32[]{:S(2)}) copy-start(bf16[512,2,1024]{2,1,0:T(2,128)(2,1)} %param.8) | copy-start | bytes 6291460
  21.2 15.9 %copy-start.17 = (bf16[64,3072]{1,0:T(8,128)(2,1)}, bf16[64,3072]{1,0:T(8,128)(2,1)S(1)}, u32[]{:S(2)}) copy-start(bf16[64,3072]{1,0:T(8,128)(2,1)S(1)} %collective-permute-done.2.refs_2_) | copy-start | bytes 1179652
  22.4 14.8 %copy-start.18 = (bf16[64,3072]{1,0:T(8,128)(2,1)}, bf16[64,3072]{1,0:T(8,128)(2,1)S(1)}, u32[]{:S(2)}) copy-start(bf16[64,3072]{1,0:T(8,128)(2,1)S(1)} %collective-permute-done.refs_1_) | copy-start | bytes 1179652
  37.1 0.8 copy-start.19
  40.5 36.6 %collective-permute-start.5 = (bf16[4,64,3072]{2,1,0:T(8,128)(2,1)}, bf16[4,64,3072]{2,1,0:T(8,128)(2,1)}, u32[]{:S(2)}, u32[]{:S(2)}) collective-permute-start(bf16[4,64,3072]{2,1,0:T(8,128)(2,1)} %placed_blocks.1.mine_ref), channel_id=1, source_target_pairs={{0,1},{1,0},{2,3},{3,2},{4,5},{5,4},{6,7},{7,6},{8,9},{9,8},{10,11... | collective-permute-start | bytes 4718600 | tf_op jit(solution)/shard_map/ppermute | solution.py:23
  42.0 36.2 %collective-permute-start.4 = (bf16[4,64,3072]{2,1,0:T(8,128)(2,1)}, bf16[4,64,3072]{2,1,0:T(8,128)(2,1)S(1)}, u32[]{:S(2)}, u32[]{:S(2)}) collective-permute-start(bf16[4,64,3072]{2,1,0:T(8,128)(2,1)} %placed_blocks.1.mine_ref), channel_id=1, source_target_pairs={{0,16},{8,24},{16,0},{24,8},{1,17},{9,25},{17,1},{25,9},{2,18},{10... | collective-permute-start | bytes 4718600 | tf_op jit(solution)/shard_map/ppermute | solution.py:23
  49.2 50.7 %collective-permute-start.1 = (bf16[576,1024]{1,0:T(8,128)(2,1)}, bf16[576,1024]{1,0:T(8,128)(2,1)S(1)}, u32[]{:S(2)}, u32[]{:S(2)}) collective-permute-start(bf16[576,1024]{1,0:T(8,128)(2,1)} %pad_maximum_fusion), channel_id=1, source_target_pairs={{0,4},{1,5},{2,6},{3,7},{4,0},{5,1},{6,2},{7,3},{8,12},{9,13},{10,... | collective-permute-start | bytes 3538952 | tf_op jit(solution)/shard_map/ppermute | solution.py:23
  78.3 26.2 %copy-start.12 = (bf16[4,64,3072]{2,1,0:T(8,128)(2,1)}, bf16[4,64,3072]{2,1,0:T(8,128)(2,1)S(1)}, u32[]{:S(2)}) copy-start(bf16[4,64,3072]{2,1,0:T(8,128)(2,1)S(1)} %collective-permute-done.4.mine_ref) | copy-start | bytes 4718596
  99.9 4.6 %copy-start.11 = (bf16[576,1024]{1,0:T(8,128)(2,1)}, bf16[576,1024]{1,0:T(8,128)(2,1)S(1)}, u32[]{:S(2)}) copy-start(bf16[576,1024]{1,0:T(8,128)(2,1)S(1)} %collective-permute-done.1) | copy-start | bytes 3538948
  104.5 48.3 %collective-permute-start.8 = (bf16[512,3072]{1,0:T(8,128)(2,1)}, bf16[512,3072]{1,0:T(8,128)(2,1)S(1)}, u32[]{:S(2)}, u32[]{:S(2)}) collective-permute-start(bf16[512,3072]{1,0:T(8,128)(2,1)} %bitcast.25), channel_id=1, source_target_pairs={{0,8},{8,0},{16,24},{24,16},{1,9},{9,1},{17,25},{25,17},{2,10},{10... | collective-permute-start | bytes 9437192 | tf_op jit(solution)/shard_map/ppermute | solution.py:23
  104.6 48.3 %collective-permute-start.10 = (bf16[2,512,1024]{2,1,0:T(8,128)(2,1)}, bf16[2,512,1024]{2,1,0:T(8,128)(2,1)S(1)}, u32[]{:S(2)}, u32[]{:S(2)}) collective-permute-start(bf16[2,512,1024]{2,1,0:T(8,128)(2,1)} %get-tuple-element.105), channel_id=1, source_target_pairs={{0,16},{8,24},{16,0},{24,8},{1,17},{9,25},{17,1},{25,9},{2,18},{10... | collective-permute-start | bytes 6291464 | tf_op jit(solution)/shard_map/ppermute | solution.py:23
  105.2 36.7 %collective-permute-start.9 = (bf16[4,64,3072]{2,1,0:T(8,128)(2,1)}, bf16[4,64,3072]{2,1,0:T(8,128)(2,1)S(1)}, u32[]{:S(2)}, u32[]{:S(2)}) collective-permute-start(bf16[4,64,3072]{2,1,0:T(8,128)(2,1)} %copy-done.12), channel_id=1, source_target_pairs={{0,1},{1,0},{2,3},{3,2},{4,5},{5,4},{6,7},{7,6},{8,9},{9,8},{10,11... | collective-permute-start | bytes 4718600 | tf_op jit(solution)/shard_map/ppermute | solution.py:23
  105.7 53.9 %collective-permute-start.7 = (bf16[384,1024]{1,0:T(8,128)(2,1)}, bf16[384,1024]{1,0:T(8,128)(2,1)}, u32[]{:S(2)}, u32[]{:S(2)}) collective-permute-start(bf16[384,1024]{1,0:T(8,128)(2,1)} %get-tuple-element.100), channel_id=1, source_target_pairs={{0,6},{1,7},{2,4},{3,5},{4,2},{5,3},{6,0},{7,1},{8,14},{9,15},{10,... | collective-permute-start | bytes 2359304 | tf_op jit(solution)/shard_map/ppermute | solution.py:23
  108.1 50.8 %collective-permute-start.6 = (bf16[192,1024]{1,0:T(8,128)(2,1)S(1)}, bf16[192,1024]{1,0:T(8,128)(2,1)S(1)}, u32[]{:S(2)}, u32[]{:S(2)}) collective-permute-start(bf16[192,1024]{1,0:T(8,128)(2,1)S(1)} %get-tuple-element.99), channel_id=1, source_target_pairs={{0,4},{1,5},{2,6},{3,7},{4,0},{5,1},{6,2},{7,3},{8,12},{9,13},{10,... | collective-permute-start | bytes 1179656 | tf_op jit(solution)/shard_map/ppermute | solution.py:23
  141.9 17.0 %copy-start.13 = (bf16[4,64,3072]{2,1,0:T(8,128)(2,1)}, bf16[4,64,3072]{2,1,0:T(8,128)(2,1)S(1)}, u32[]{:S(2)}) copy-start(bf16[4,64,3072]{2,1,0:T(8,128)(2,1)S(1)} %collective-permute-done.9.theirs_ref) | copy-start | bytes 4718596
  152.8 1.3 copy-start.10
  154.2 9.6 %copy-start = (bf16[512,3072]{1,0:T(8,128)(2,1)}, bf16[512,3072]{1,0:T(8,128)(2,1)S(1)}, u32[]{:S(2)}) copy-start(bf16[512,3072]{1,0:T(8,128)(2,1)S(1)} %collective-permute-done.8.refs_1_.tokens_ref) | copy-start | bytes 9437188
  158.8 0.7 copy-start.15
  163.8 3.4 slice-start
  163.8 3.4 copy-start.16
  163.8 3.5 copy-start.14
  163.8 26.1 %collective-permute-start.11 = (bf16[512,3072]{1,0:T(8,128)(2,1)}, bf16[512,3072]{1,0:T(8,128)(2,1)S(1)}, u32[]{:S(2)}, u32[]{:S(2)}) collective-permute-start(bf16[512,3072]{1,0:T(8,128)(2,1)} %bitcast.29), channel_id=1, source_target_pairs={{0,8},{8,0},{16,24},{24,16},{1,9},{9,1},{17,25},{25,17},{2,10},{10... | collective-permute-start | bytes 9437192 | tf_op jit(solution)/shard_map/ppermute | solution.py:23
  163.9 26.0 %collective-permute-start.12 = (bf16[1,512,1024]{2,1,0:T(8,128)(2,1)}, bf16[1,512,1024]{2,1,0:T(8,128)(2,1)S(1)}, u32[]{:S(2)}, u32[]{:S(2)}) collective-permute-start(bf16[1,512,1024]{2,1,0:T(8,128)(2,1)} %get-tuple-element.118), channel_id=1, source_target_pairs={{0,8},{8,0},{16,24},{24,16},{1,9},{9,1},{17,25},{25,17},{2,10},{10... | collective-permute-start | bytes 3145736 | tf_op jit(solution)/shard_map/ppermute | solution.py:23
  167.1 22.7 %collective-permute-start.13 = (bf16[1,512,1024]{2,1,0:T(8,128)(2,1)S(1)}, bf16[1,512,1024]{2,1,0:T(8,128)(2,1)S(1)}, u32[]{:S(2)}, u32[]{:S(2)}) collective-permute-start(bf16[1,512,1024]{2,1,0:T(8,128)(2,1)S(1)} %get-tuple-element.165), channel_id=1, source_target_pairs={{0,8},{8,0},{16,24},{24,16},{1,9},{9,1},{17,25},{25,17},{2,10},{10... | collective-permute-start | bytes 3145736 | tf_op jit(solution)/shard_map/ppermute | solution.py:23
  167.3 22.5 %collective-permute-start.14 = (bf16[384,1024]{1,0:T(8,128)(2,1)S(1)}, bf16[384,1024]{1,0:T(8,128)(2,1)S(1)}, u32[]{:S(2)}, u32[]{:S(2)}) collective-permute-start(bf16[384,1024]{1,0:T(8,128)(2,1)S(1)} %copy-done.14), channel_id=1, source_target_pairs={{0,1},{1,0},{2,3},{3,2},{4,5},{5,4},{6,7},{7,6},{8,9},{9,8},{10,11... | collective-permute-start | bytes 2359304 | tf_op jit(solution)/shard_map/ppermute | solution.py:23
  168.9 37.7 %collective-permute-start.18 = (bf16[384,1024]{1,0:T(8,128)(2,1)}, bf16[384,1024]{1,0:T(8,128)(2,1)S(1)}, u32[]{:S(2)}, u32[]{:S(2)}) collective-permute-start(bf16[384,1024]{1,0:T(8,128)(2,1)} %get-tuple-element.142), channel_id=1, source_target_pairs={{0,7},{1,6},{2,5},{3,4},{4,3},{5,2},{6,1},{7,0},{8,15},{9,14},{10,... | collective-permute-start | bytes 2359304 | tf_op jit(solution)/shard_map/ppermute | solution.py:23
  189.8 0.9 copy-start.7
  189.8 2.4 copy-start.5
  189.8 2.4 copy-start.6
  190.7 1.7 copy-start.1
  190.7 32.6 %collective-permute-start.19 = (bf16[384,1024]{1,0:T(8,128)(2,1)S(1)}, bf16[384,1024]{1,0:T(8,128)(2,1)S(1)}, u32[]{:S(2)}, u32[]{:S(2)}) collective-permute-start(bf16[384,1024]{1,0:T(8,128)(2,1)S(1)} %pad_maximum_fusion.1), channel_id=1, source_target_pairs={{0,1},{1,0},{2,3},{3,2},{4,5},{5,4},{6,7},{7,6},{8,9},{9,8},{10,11... | collective-permute-start | bytes 2359304 | tf_op jit(solution)/shard_map/ppermute | solution.py:23
  206.6 16.8 %copy-start.8 = (bf16[384,1024]{1,0:T(8,128)(2,1)}, bf16[384,1024]{1,0:T(8,128)(2,1)S(1)}, u32[]{:S(2)}) copy-start(bf16[384,1024]{1,0:T(8,128)(2,1)S(1)} %collective-permute-done.18.refs_7_) | copy-start | bytes 2359300
  223.3 0.9 copy-start.9
  224.3 93.5 %all-to-all-start = ((bf16[8,384,512]{2,1,0:T(8,128)(2,1)}), bf16[8,384,512]{2,1,0:T(8,128)(2,1)S(1)}, u32[]{:S(2)}, u32[]{:S(2)}) async-start(bf16[8,384,512]{2,1,0:T(8,128)(2,1)} %bitcast.33), calls=%async_computation | async-start | bytes 6291456 | tf_op jit(solution)/shard_map/all_to_all | solution.py:257
  240.0 77.9 %collective-permute-start.16 = (f32[512,1024]{1,0:T(8,128)}, f32[512,1024]{1,0:T(8,128)}, u32[]{:S(2)}, u32[]{:S(2)}) collective-permute-start(f32[512,1024]{1,0:T(8,128)} %hidden_deriv.5), channel_id=1, source_target_pairs={{0,16},{8,24},{16,0},{24,8},{1,17},{9,25},{17,1},{25,9},{2,18},{10... | collective-permute-start | bytes 6291464 | tf_op jit(solution)/shard_map/ppermute | solution.py:23
  257.2 72.8 %collective-permute-start.15 = (f32[512,1024]{1,0:T(8,128)}, f32[512,1024]{1,0:T(8,128)}, u32[]{:S(2)}, u32[]{:S(2)}) collective-permute-start(f32[512,1024]{1,0:T(8,128)} %hidden_deriv.4), channel_id=1, source_target_pairs={{0,24},{8,16},{16,8},{24,0},{1,25},{9,17},{17,9},{25,1},{2,26},{10... | collective-permute-start | bytes 6291464 | tf_op jit(solution)/shard_map/ppermute | solution.py:23
  257.2 72.8 %collective-permute-start.17 = (f32[512,1024]{1,0:T(8,128)}, f32[512,1024]{1,0:T(8,128)}, u32[]{:S(2)}, u32[]{:S(2)}) collective-permute-start(f32[512,1024]{1,0:T(8,128)} %hidden_deriv.6), channel_id=1, source_target_pairs={{0,8},{8,0},{16,24},{24,16},{1,9},{9,1},{17,25},{25,17},{2,10},{10... | collective-permute-start | bytes 6291464 | tf_op jit(solution)/shard_map/ppermute | solution.py:23
  257.9 6.0 %copy-start.20 = (s32[512,2]{0,1:T(2,128)S(1)}, s32[512,2]{0,1:T(2,128)}, u32[]{:S(2)}) copy-start(s32[512,2]{0,1:T(2,128)} %param.9) | copy-start | bytes 12292
  260.9 41.2 %collective-permute-start.20 = (bf16[384,1024]{1,0:T(8,128)(2,1)}, bf16[384,1024]{1,0:T(8,128)(2,1)}, u32[]{:S(2)}, u32[]{:S(2)}) collective-permute-start(bf16[384,1024]{1,0:T(8,128)(2,1)} %get-tuple-element.145), channel_id=1, source_target_pairs={{0,2},{1,3},{2,0},{3,1},{4,6},{5,7},{6,4},{7,5},{8,10},{9,11},{10,... | collective-permute-start | bytes 2359304 | tf_op jit(solution)/shard_map/ppermute | solution.py:23
  261.0 56.9 %collective-permute-start.21 = (bf16[384,1024]{1,0:T(8,128)(2,1)}, bf16[384,1024]{1,0:T(8,128)(2,1)}, u32[]{:S(2)}, u32[]{:S(2)}) collective-permute-start(bf16[384,1024]{1,0:T(8,128)(2,1)} %get-tuple-element.146), channel_id=1, source_target_pairs={{0,3},{1,2},{2,1},{3,0},{4,7},{5,6},{6,5},{7,4},{8,11},{9,10},{10,... | collective-permute-start | bytes 2359304 | tf_op jit(solution)/shard_map/ppermute | solution.py:23
  317.8 1.6 copy-start.3
  319.4 72.7 %all-to-all-start.1 = ((bf16[8,384,512]{2,1,0:T(8,128)(2,1)}), bf16[8,384,512]{2,1,0:T(8,128)(2,1)S(1)}, u32[]{:S(2)}, u32[]{:S(2)}) async-start(bf16[8,384,512]{2,1,0:T(8,128)(2,1)} %bitcast.34), calls=%async_computation.1 | async-start | bytes 6291456 | tf_op jit(solution)/shard_map/all_to_all | solution.py:257
  392.1 1.6 copy-start.2

commit v11 on v10

--- a/solution.py
+++ b/solution.py
@@ -259,71 +259,52 @@
     weight = down_weight[0]
     tuned = shards == 8
 
-    def block_for(m, begin=0, count=rows):
-        return lax.dynamic_slice_in_dim(weight, (place ^ m) * rows + begin, count, axis=0)
+    def sent(m, *begun):
+        return swapped(after(cuts[m], *begun), "dp", m)
 
     blocks = [swapped(out_grad, "dp", m) for m in range(0, shards, 2)]
     named = (routing ^ mine).reshape(1, group_tok * topk)
     picked = picked_rows(
         gate_saved.reshape(-1, cols), up_saved.reshape(-1, cols), named, group_tok, experts
     )
+    cuts = [
+        lax.dynamic_slice_in_dim(weight, (place ^ m) * rows, rows, axis=0)
+        for m in range(shards if tuned else 1)
+    ]
+    blocks, picked, cuts = stage(blocks, picked, cuts)
+
+    held = placed_blocks(blocks, place // 2)
+    beside = swapped(held, "dp", 1)
+    got = swapped(picked[-1], "expert", half)
+    weights = {0: cuts[0]}
     if tuned:
-        cut = rows // 2
-        mixed = jnp.concatenate([block_for(4), block_for(5, 0, cut)], axis=0)
-        mixed, rest, six, seven = stage(mixed, block_for(5, cut, rows - cut), block_for(6), block_for(7))
-        mixed = swapped(after(mixed, blocks[1]), "dp", 4)
-    blocks, picked = stage(blocks, picked)
-
-    held = {0: placed_blocks(blocks, place // 2)}
+        weights[4] = sent(4)
+    held, beside, got, picked, weights, cuts = stage(held, beside, got, picked, weights, cuts)
+
+    tokens = {0: in_order(held, beside, (place & 1) != 0).reshape(group_tok, width)}
     for m in others:
-        held[m] = swapped(held[m & (m - 1)], "expert", m & -m)
-    beside = {0: swapped(held[0], "dp", 1)}
-    held, beside, picked = stage(held, beside, picked)
+        tokens[m] = swapped(tokens[m & (m - 1)], "expert", m & -m)
+    tokens[1] = swapped(tokens[0], "expert", 1)
+    hidden = spread(picked, got, experts)
     if tuned:
-        mixed, rest, six, held, beside, picked = stage(mixed, rest, six, held, beside, picked)
-
-    last = (place & 1) != 0
+        for m in (6, 5, 1):
+            weights[m] = sent(m)
+    tokens, hidden, weights, cuts = stage(tokens, hidden, weights, cuts)
+
     for m in others:
-        beside[m] = swapped(held[m], "dp", 1)
-    got = swapped(picked[-1], "expert", half)
-    tokens = {0: in_order(held[0], beside[0], last).reshape(group_tok, width)}
-    tokens[1] = swapped(tokens[0], "expert", 1)
-    tokens, beside, got, picked = stage(tokens, beside, got, picked)
-    if tuned:
-        rest = swapped(rest, "dp", 4)
-        six = swapped(six, "dp", 6)
-        rest, six, seven, tokens, beside, got, picked = stage(
-            rest, six, seven, tokens, beside, got, picked
-        )
-
-    for m in others:
-        tokens[m] = in_order(held[m], beside[m], last).reshape(group_tok, width)
         tokens[m + 1] = swapped(tokens[m], "expert", 1)
     tokens = [tokens[m] for m in each]
-    hidden = spread(picked, got, experts)
     if tuned:
-        one, five, weight = stage(
-            block_for(1), jnp.concatenate([mixed[rows:], rest], axis=0), weight
-        )
-        one = swapped(after(one, rest), "dp", 1)
-        seven = swapped(seven, "dp", 7)
-        tokens, hidden, one, five = stage(tokens, hidden, one, five)
-        five = swapped(five, "dp", 1)
-        first_weights, last_weights = [seven, five], []
-        weights = [block_for(0), one, None, None, mixed[:rows], five, six, seven]
-        for m in (2, 3):
-            weights[m] = swapped(after(block_for(m), hidden), "dp", m)
-            last_weights.append(weights[m])
+        for m in (7, 2, 3):
+            weights[m] = sent(m)
+        first_weights, last_weights = weights[7], (weights[2], weights[3])
     else:
-        tokens, hidden = stage(tokens, hidden)
         every = lax.all_to_all(
             weight.reshape(shards, rows, cols), "dp", split_axis=0, concat_axis=0, tiled=True
         )
-        first_weights, last_weights = [every], []
-        weights = [
-            lax.dynamic_index_in_dim(every, place ^ m, axis=0, keepdims=False)
-            for m in range(shards)
-        ]
+        first_weights, last_weights = every, ()
+        for m in range(1, shards):
+            weights[m] = lax.dynamic_index_in_dim(every, place ^ m, axis=0, keepdims=False)
 
     term = terms(0, parts, tokens, hidden)
     weight, term = stage(weight, term)
@@ -332,7 +313,7 @@
     grads = [to_owners(term, first_weights)]
     for part in range(1, parts):
         term = terms(part, parts, tokens, after(hidden, derivs))
-        grads.append(to_owners(term, grads, last_weights, backs[half]))
+        grads.append(to_owners(term, grads, last_weights))
 
     gate_saved, up_saved, _ = stage(gate_saved, up_saved, derivs)
     gate = gate_saved.astype(jnp.float32)
@@ -347,7 +328,9 @@
 
     done = ()
     for part in range(parts):
-        done = update(part, parts, place, grads[part], weights, momentum, done)
+        done = update(
+            part, parts, place, grads[part], [weights[m] for m in range(shards)], momentum, done
+        )
     new_weight, new_momentum = done
     return (d_gate, d_up, new_weight, new_momentum)
 

time: 410 us -> 398 us (0.971)
  local copies, waits for them, and re-layouts: 28.5 us -> 21.4 us
  starting transfers between devices: 35.8 us -> 29.4 us
  waiting for transfers between devices: 226 us -> 232 us
    ppermute x22 -> x20, waiting for transfers between devices: 191 us -> 215 us  [swapped(): return lax.ppermute(array, axis, [(i, i ^ mask) for i in range(size)])]
    all_to_all x2, waiting for transfers between devices: 35.1 us -> 17.1 us  [to_owners(): return lax.all_to_all(array, 'dp', split_axis=0, concat_axis=0, tiled=True)]
    pallas_call x2 -> x1, Pallas kernels: 8.77 us -> 4.72 us  [in_order(): pl.pallas_call(order_kernel, grid_spec=pltpu.PrefetchScalarGridSpec(num_s...]
    ppermute x22 -> x20, starting transfers between devices: 23.3 us -> 19.6 us  [swapped(): return lax.ppermute(array, axis, [(i, i ^ mask) for i in range(size)])]
  transfers between devices with their start and end apart: 24 -> 22, of which waited for: 16 -> 13; matrix products, arithmetic and copies ran while one was open for 10% -> 8% of each run, Pallas kernels for 18% -> 19%
where the time goes in v11:
time: 398 us; the launch traced here: 392 us
  waiting for transfers between devices  232 us (58%)
  Pallas kernels  91.5 us (23%)
  starting transfers between devices  29.4 us (7%)
  local copies, waits for them, and re-layouts  21.4 us (5%)
  other arithmetic  17 us (4%)
    ppermute x20, waiting for transfers between devices, swapped(): return lax.ppermute(array, axis, [(i, i ^ mask) for i in range(size)])  215 us
    pallas_call x4, Pallas kernels, deriv_of(): pl.pallas_call(deriv_kernel, grid=(cols // wide,), in_specs=[pl.BlockSpec...  31.5 us
    pallas_call x2, Pallas kernels, terms(): pl.pallas_call(functools.partial(term_kernel, count), grid=(width // tall...  25.7 us
    pallas_call x2, Pallas kernels, update(): pl.pallas_call(functools.partial(update_kernel, count), grid_spec=pltpu.P...  21.4 us
    ppermute x20, starting transfers between devices, swapped(): return lax.ppermute(array, axis, [(i, i ^ mask) for i in range(size)])  19.6 us
    all_to_all x2, waiting for transfers between devices, to_owners(): return lax.all_to_all(array, 'dp', split_axis=0, concat_axis=0, tiled=True)  17.1 us
    convert_element_type x1, other arithmetic, body(): d_up = (deriv * gate * sigma).astype(jnp.bfloat16)  16.3 us
    all_to_all x2, starting transfers between devices, to_owners(): return lax.all_to_all(array, 'dp', split_axis=0, concat_axis=0, tiled=True)  9.88 us
  transfers between devices with their start and end apart: 22, of which 13 were waited for; matrix products, arithmetic and copies ran while one was open for 8% of the time, Pallas kernels for 19%

profile of v11, /device:TPU:8, one launch (start us, length us, event | category | flops | bytes accessed | tf_op | source)
XLA Modules:
  0.0 392.5 jit_solution(11693671288137292947)
XLA Ops:
  0.6 0.0 copy-start.4
  0.6 2.7 collective-permute-start.1
  3.3 0.4 collective-permute-start
  3.7 0.5 collective-permute-start.2
  4.2 0.7 broadcast_xor_fusion
  4.9 0.1 copy.18
  5.0 0.8 reshape_reshape.6.named_ref
  5.8 4.1 %reshape.51.gate_ref = bf16[1024,1024]{1,0:T(8,128)(2,1)} reshape(bf16[512,2,1024]{2,1,0:T(2,128)(2,1)} %param.7) | data formatting | bytes 4194304 | tf_op jit(solution)/shard_map/reshape | solution.py:268
  9.9 2.2 reshape.52.up_ref
  12.1 5.5 %hidden_rows.1 = (bf16[1,512,1024]{2,1,0:T(8,128)(2,1)}, bf16[1,512,1024]{2,1,0:T(8,128)(2,1)}, bf16[2,512,1024]{2,1,0:T(8,128)(2,1)}) custom-call(bf16[1024,1024]{1,0:T(8,128)(2,1)} %reshape.51.gate_ref, bf16[1024,1024]{1,0:T(8,128)(2,1)} %reshape.52.up_ref, s32[4,256]{1,0:T(4,128)} %reshape_reshape.6.named_ref), custom_call_target="tpu_custom_call" | custom-call | flops 1024 | bytes 1024 | tf_op jit(solution)/shard_map/hidden_rows/pallas_call | solution.py:110
  17.6 5.5 %dynamic-slice_bitcast_fusion = (bf16[384,1024]{1,0:T(8,128)(2,1)}, bf16[384,1024]{1,0:T(8,128)(2,1)}, bf16[384,1024]{1,0:T(8,128)(2,1)}, bf16[384,1024]{1,0:T(8...) fusion(bf16[1,3072,1024]{2,1,0:T(8,128)(2,1)} %param.10, ...), kind=kLoop, calls=%fused_computation.13 | loop fusion | bytes 12582944 | tf_op jit(solution)/shard_map/dynamic_slice | solution.py:271
  23.2 14.0 %collective-permute-done.2.refs_3_ = bf16[64,3072]{1,0:T(8,128)(2,1)} collective-permute-done((bf16[64,3072]{1,0:T(8,128)(2,1)}, bf16[64,3072]{1,0:T(8,128)(2,1)}, u32[]{:S(2)}, u32[]{:S(2)}) %collective-permute-start.2) | collective-permute-done | bytes 393248 | tf_op jit(solution)/shard_map/ppermute | solution.py:23
  37.2 1.5 collective-permute-start.4
  38.6 2.6 placed_blocks.1.mine_ref
  41.2 1.5 collective-permute-start.3
  42.8 0.0 collective-permute-start.5
  42.8 33.9 %collective-permute-done.5.refs_4_ = bf16[384,1024]{1,0:T(8,128)(2,1)S(1)} collective-permute-done((bf16[384,1024]{1,0:T(8,128)(2,1)}, bf16[384,1024]{1,0:T(8,128)(2,1)S(1)}, u32[]{:S(2)}, u32[]{:S(2)}) %collective-permute-start.5) | collective-permute-done | bytes 786464 | tf_op jit(solution)/shard_map/ppermute | solution.py:23
  76.6 1.0 collective-permute-done.3.theirs_ref
  77.6 7.3 %collective-permute-done.4 = bf16[2,512,1024]{2,1,0:T(8,128)(2,1)S(1)} collective-permute-done((bf16[2,512,1024]{2,1,0:T(8,128)(2,1)}, bf16[2,512,1024]{2,1,0:T(8,128)(2,1)S(1)}, u32[]{:S(2)}, u32[]{:S(2)}) %collective-permute-start.4) | collective-permute-done | bytes 2097184 | tf_op jit(solution)/shard_map/ppermute | solution.py:23
  84.9 4.7 %side_by_side.1 = bf16[4,2,64,3072]{3,2,1,0:T(8,128)(2,1)} custom-call(s32[1]{0:T(128)} %bitcast.place_ref, bf16[4,64,3072]{2,1,0:T(8,128)(2,1)} %placed_blocks.1.mine_ref, bf16[4,64,3072]{2,1,0:T(8,128)(2,1)} %collective-permute-done.3.theirs_ref), custom_call_target="tpu_custom_call" | custom-call | flops 1024 | bytes 1024 | tf_op jit(solution)/shard_map/side_by_side/pallas_call | solution.py:42
  89.7 1.6 collective-permute-start.7
  91.2 2.5 collective-permute-start.12
  93.7 0.0 collective-permute-start.11
  93.7 0.2 collective-permute-start.8
  93.9 2.8 fusion.8
  96.7 43.9 %collective-permute-done.12.refs_6_ = bf16[384,1024]{1,0:T(8,128)(2,1)S(1)} collective-permute-done((bf16[384,1024]{1,0:T(8,128)(2,1)}, bf16[384,1024]{1,0:T(8,128)(2,1)S(1)}, u32[]{:S(2)}, u32[]{:S(2)}) %collective-permute-start.12) | collective-permute-done | bytes 786464 | tf_op jit(solution)/shard_map/ppermute | solution.py:23
  140.6 0.1 collective-permute-start.9
  140.7 13.9 %collective-permute-done.11.refs_5_ = bf16[384,1024]{1,0:T(8,128)(2,1)S(1)} collective-permute-done((bf16[384,1024]{1,0:T(8,128)(2,1)}, bf16[384,1024]{1,0:T(8,128)(2,1)S(1)}, u32[]{:S(2)}, u32[]{:S(2)}) %collective-permute-start.11) | collective-permute-done | bytes 786464 | tf_op jit(solution)/shard_map/ppermute | solution.py:23
  154.6 1.3 collective-permute-start.10
  156.0 18.2 %collective-permute-done.10.refs_1_ = bf16[384,1024]{1,0:T(8,128)(2,1)S(1)} collective-permute-done((bf16[384,1024]{1,0:T(8,128)(2,1)S(1)}, bf16[384,1024]{1,0:T(8,128)(2,1)S(1)}, u32[]{:S(2)}, u32[]{:S(2)}) %collective-permute-start.10) | collective-permute-done | bytes 786464 | tf_op jit(solution)/shard_map/ppermute | solution.py:23
  174.2 0.0 collective-permute-done.6.refs_1_.tokens_ref
  174.2 0.0 copy-start.1
  174.2 0.9 copy-done.6
  175.2 0.0 collective-permute-start.13
  175.2 2.5 collective-permute-start.17
  177.7 3.3 collective-permute-done.13.refs_3_.tokens_ref
  181.0 12.8 %group_terms.2 = bf16[3072,512]{1,0:T(8,128)(2,1)} custom-call(bf16[512,3072]{1,0:T(8,128)(2,1)} %bitcast.30, bf16[512,3072]{1,0:T(8,128)(2,1)} %copy-done.1, bf16[512,3072]{1,0:T(8,128)(2,1)} %copy-done, bf16[512,3072]{1,0:T(8,128)(2,1)} %collective-permute-done.13.refs_3_.tokens_ref, bf16[512,1024]{1,0:T(8,128)(2,1)} %bitcast.39, ...), custom_call_target="tpu_custom_call" | custom-call | flops 1024 | bytes 1024 | tf_op jit(solution)/shard_map/group_terms/pallas_call | solution.py:155
  193.8 19.3 %collective-permute-done.17.refs_7_ = bf16[384,1024]{1,0:T(8,128)(2,1)S(1)} collective-permute-done((bf16[384,1024]{1,0:T(8,128)(2,1)}, bf16[384,1024]{1,0:T(8,128)(2,1)S(1)}, u32[]{:S(2)}, u32[]{:S(2)}) %collective-permute-start.17) | collective-permute-done | bytes 786464 | tf_op jit(solution)/shard_map/ppermute | solution.py:23
  213.1 0.9 copy-done.11
  214.0 5.2 %all-to-all-start = ((bf16[8,384,512]{2,1,0:T(8,128)(2,1)}), bf16[8,384,512]{2,1,0:T(8,128)(2,1)S(1)}, u32[]{:S(2)}, u32[]{:S(2)}) async-start(bf16[8,384,512]{2,1,0:T(8,128)(2,1)} %bitcast.33), calls=%async_computation | async-start | bytes 6291456 | tf_op jit(solution)/shard_map/all_to_all | solution.py:257
  219.2 7.9 %hidden_deriv.6 = f32[512,1024]{1,0:T(8,128)} custom-call(bf16[512,3072]{1,0:T(8,128)(2,1)} %copy-done.1, bf16[3072,1024]{1,0:T(8,128)(2,1)} %bitcast.35), custom_call_target="tpu_custom_call" | custom-call | flops 3221225472 | bytes 11534336 | tf_op jit(solution)/shard_map/hidden_deriv/pallas_call | solution.py:178
  227.1 7.9 %hidden_deriv.5 = f32[512,1024]{1,0:T(8,128)} custom-call(bf16[512,3072]{1,0:T(8,128)(2,1)} %copy-done, bf16[3072,1024]{1,0:T(8,128)(2,1)} %bitcast.36), custom_call_target="tpu_custom_call" | custom-call | flops 3221225472 | bytes 11534336 | tf_op jit(solution)/shard_map/hidden_deriv/pallas_call | solution.py:178
  234.9 7.9 %hidden_deriv.4 = f32[512,1024]{1,0:T(8,128)} custom-call(bf16[512,3072]{1,0:T(8,128)(2,1)} %collective-permute-done.13.refs_3_.tokens_ref, bf16[3072,1024]{1,0:T(8,128)(2,1)} %bitcast.37), custom_call_target="tpu_custom_call" | custom-call | flops 3221225472 | bytes 11534336 | tf_op jit(solution)/shard_map/hidden_deriv/pallas_call | solution.py:178
  242.8 0.2 collective-permute-start.14
  243.0 1.3 collective-permute-start.15
  244.4 0.3 collective-permute-start.16
  244.7 0.0 collective-permute-start.18
  244.7 2.9 collective-permute-start.19
  247.6 0.2 copy.17
  247.8 0.2 copy.19
  248.0 0.2 copy.21
  248.2 0.2 copy.20
  248.4 7.9 %hidden_deriv.7 = f32[512,1024]{1,0:T(8,128)} custom-call(bf16[512,3072]{1,0:T(8,128)(2,1)} %bitcast.31, bf16[3072,1024]{1,0:T(8,128)(2,1)} %bitcast.38), custom_call_target="tpu_custom_call" | custom-call | flops 3221225472 | bytes 11534336 | tf_op jit(solution)/shard_map/hidden_deriv/pallas_call | solution.py:178
  256.4 12.9 %group_terms.3 = bf16[3072,512]{1,0:T(8,128)(2,1)} custom-call(bf16[512,3072]{1,0:T(8,128)(2,1)} %bitcast.32, bf16[512,3072]{1,0:T(8,128)(2,1)} %copy-done.1, bf16[512,3072]{1,0:T(8,128)(2,1)} %copy-done, bf16[512,3072]{1,0:T(8,128)(2,1)} %collective-permute-done.13.refs_3_.tokens_ref, bf16[512,1024]{1,0:T(8,128)(2,1)} %bitcast.40, ...), custom_call_target="tpu_custom_call" | custom-call | flops 1024 | bytes 1024 | tf_op jit(solution)/shard_map/group_terms/pallas_call | solution.py:155
  269.3 20.3 %collective-permute-done.18.refs_2_ = bf16[384,1024]{1,0:T(8,128)(2,1)} collective-permute-done((bf16[384,1024]{1,0:T(8,128)(2,1)}, bf16[384,1024]{1,0:T(8,128)(2,1)}, u32[]{:S(2)}, u32[]{:S(2)}) %collective-permute-start.18) | collective-permute-done | bytes 786464 | tf_op jit(solution)/shard_map/ppermute | solution.py:23
  289.6 16.3 %collective-permute-done.19.refs_3_ = bf16[384,1024]{1,0:T(8,128)(2,1)} collective-permute-done((bf16[384,1024]{1,0:T(8,128)(2,1)}, bf16[384,1024]{1,0:T(8,128)(2,1)}, u32[]{:S(2)}, u32[]{:S(2)}) %collective-permute-start.19) | collective-permute-done | bytes 786464 | tf_op jit(solution)/shard_map/ppermute | solution.py:23
  305.8 1.6 copy-done.3
  307.5 4.6 %all-to-all-start.1 = ((bf16[8,384,512]{2,1,0:T(8,128)(2,1)}), bf16[8,384,512]{2,1,0:T(8,128)(2,1)S(1)}, u32[]{:S(2)}, u32[]{:S(2)}) async-start(bf16[8,384,512]{2,1,0:T(8,128)(2,1)} %bitcast.34), calls=%async_computation.1 | async-start | bytes 6291456 | tf_op jit(solution)/shard_map/all_to_all | solution.py:257
  312.1 23.9 %collective-permute-done.15 = f32[512,1024]{1,0:T(8,128)} collective-permute-done((f32[512,1024]{1,0:T(8,128)}, f32[512,1024]{1,0:T(8,128)}, u32[]{:S(2)}, u32[]{:S(2)}) %collective-permute-start.15) | collective-permute-done | bytes 2097184 | tf_op jit(solution)/shard_map/ppermute | solution.py:23
  336.0 16.3 %fusion.7 = (bf16[512,2,1024]{2,1,0:T(2,128)(2,1)}, bf16[512,2,1024]{2,1,0:T(2,128)(2,1)}) fusion(bf16[512,2,1024]{2,1,0:T(2,128)(2,1)} %param.7, pred[512,2]{1,0:T(8,128)(4,1)S(1)} %copy.21, pred[512,2]{1,0:T(8,128)(4,1)S(1)} %copy.20, pred[512,2]{1,0:T(8,128)(4,1)S(1)} %copy.19, pred[512,2]{1,0:T(8,128)(4,1)S(1)} %copy.17, f32[512,1024]{1,0:T(8,128)} %hidden_deriv.7, ...), kind=kLoop, calls=%fused_computation.10 | loop fusion | flops 19922944 | bytes 16781312 | tf_op jit(solution)/shard_map/convert_element_type | solution.py:326
  352.3 10.7 %lion_step.2 = (f32[1,384,8192]{2,1,0:T(8,128)}, bf16[1,384,8192]{2,1,0:T(8,128)(2,1)}) custom-call(s32[1]{0:T(128)} %bitcast.16.place_ref, bf16[8,384,512]{2,1,0:T(8,128)(2,1)} %copy-done.3, bf16[1,384,8192]{2,1,0:T(8,128)(2,1)} %momentum_ref.3, bf16[384,1024]{1,0:T(8,128)(2,1)} %get-tuple-element.115.refs_0_, bf16[384,1024]{1,0:T(8,128)(2,1)} %copy-done.10, ...), custom_call_target="tpu_custom_call" | custom-call | flops 1024 | bytes 1024 | tf_op jit(solution)/shard_map/lion_step/pallas_call | solution.py:219
  363.1 17.1 %all-to-all-done.1.grad_ref = bf16[8,384,512]{2,1,0:T(8,128)(2,1)S(1)} async-done(((bf16[8,384,512]{2,1,0:T(8,128)(2,1)}), bf16[8,384,512]{2,1,0:T(8,128)(2,1)S(1)}, u32[]{:S(2)}, u32[]{:S(2)}) %all-to-all-start.1) | async-done | bytes 3145760 | tf_op jit(solution)/shard_map/all_to_all | solution.py:257
  380.2 1.6 copy-done.2
  381.8 10.7 %lion_step.3 = (f32[1,384,8192]{2,1,0:T(8,128)}, bf16[1,384,8192]{2,1,0:T(8,128)(2,1)}) custom-call(s32[1]{0:T(128)} %bitcast.16.place_ref, bf16[8,384,512]{2,1,0:T(8,128)(2,1)} %copy-done.2, bf16[1,384,8192]{2,1,0:T(8,128)(2,1)} %momentum_ref.3, bf16[384,1024]{1,0:T(8,128)(2,1)} %get-tuple-element.115.refs_0_, ...), custom_call_target="tpu_custom_call", output_to_operand_aliasing={{0}: (11, {}), {1}: (12, {})} | custom-call | flops 1024 | bytes 1024 | tf_op jit(solution)/shard_map/lion_step/pallas_call | solution.py:219
  (38 shorter events, 0.1 us)
Async XLA Ops:
  0.6 9.3 %copy-start.4 = (bf16[512,2,1024]{2,1,0:T(2,128)(2,1)S(1)}, bf16[512,2,1024]{2,1,0:T(2,128)(2,1)}, u32[]{:S(2)}) copy-start(bf16[512,2,1024]{2,1,0:T(2,128)(2,1)} %param.8) | copy-start | bytes 6291460
  0.6 22.5 %collective-permute-start.1 = (bf16[64,3072]{1,0:T(8,128)(2,1)}, bf16[64,3072]{1,0:T(8,128)(2,1)S(1)}, u32[]{:S(2)}, u32[]{:S(2)}) collective-permute-start(bf16[64,3072]{1,0:T(8,128)(2,1)} %refs_0_), channel_id=1, source_target_pairs={{0,4},{1,5},{2,6},{3,7},{4,0},{5,1},{6,2},{7,3},{8,12},{9,13},{10,... | collective-permute-start | bytes 1179656 | tf_op jit(solution)/shard_map/ppermute | solution.py:23
  3.3 19.9 %collective-permute-start = (bf16[64,3072]{1,0:T(8,128)(2,1)}, bf16[64,3072]{1,0:T(8,128)(2,1)S(1)}, u32[]{:S(2)}, u32[]{:S(2)}) collective-permute-start(bf16[64,3072]{1,0:T(8,128)(2,1)} %refs_0_), channel_id=1, source_target_pairs={{0,2},{1,3},{2,0},{3,1},{4,6},{5,7},{6,4},{7,5},{8,10},{9,11},{10,... | collective-permute-start | bytes 1179656 | tf_op jit(solution)/shard_map/ppermute | solution.py:23
  3.7 33.4 %collective-permute-start.2 = (bf16[64,3072]{1,0:T(8,128)(2,1)}, bf16[64,3072]{1,0:T(8,128)(2,1)}, u32[]{:S(2)}, u32[]{:S(2)}) collective-permute-start(bf16[64,3072]{1,0:T(8,128)(2,1)} %refs_0_), channel_id=1, source_target_pairs={{0,6},{1,7},{2,4},{3,5},{4,2},{5,3},{6,0},{7,1},{8,14},{9,15},{10,... | collective-permute-start | bytes 1179656 | tf_op jit(solution)/shard_map/ppermute | solution.py:23
  23.1 15.5 %copy-start.14 = (bf16[64,3072]{1,0:T(8,128)(2,1)}, bf16[64,3072]{1,0:T(8,128)(2,1)S(1)}, u32[]{:S(2)}) copy-start(bf16[64,3072]{1,0:T(8,128)(2,1)S(1)} %collective-permute-done.1.refs_2_) | copy-start | bytes 1179652
  23.2 14.0 %copy-start.15 = (bf16[64,3072]{1,0:T(8,128)(2,1)}, bf16[64,3072]{1,0:T(8,128)(2,1)S(1)}, u32[]{:S(2)}) copy-start(bf16[64,3072]{1,0:T(8,128)(2,1)S(1)} %collective-permute-done.refs_1_) | copy-start | bytes 1179652
  37.2 47.8 %collective-permute-start.4 = (bf16[2,512,1024]{2,1,0:T(8,128)(2,1)}, bf16[2,512,1024]{2,1,0:T(8,128)(2,1)S(1)}, u32[]{:S(2)}, u32[]{:S(2)}) collective-permute-start(bf16[2,512,1024]{2,1,0:T(8,128)(2,1)} %get-tuple-element.71), channel_id=1, source_target_pairs={{0,16},{8,24},{16,0},{24,8},{1,17},{9,25},{17,1},{25,9},{2,18},{10... | collective-permute-start | bytes 6291464 | tf_op jit(solution)/shard_map/ppermute | solution.py:23
  41.2 36.4 %collective-permute-start.3 = (bf16[4,64,3072]{2,1,0:T(8,128)(2,1)}, bf16[4,64,3072]{2,1,0:T(8,128)(2,1)}, u32[]{:S(2)}, u32[]{:S(2)}) collective-permute-start(bf16[4,64,3072]{2,1,0:T(8,128)(2,1)} %placed_blocks.1.mine_ref), channel_id=1, source_target_pairs={{0,1},{1,0},{2,3},{3,2},{4,5},{5,4},{6,7},{7,6},{8,9},{9,8},{10,11... | collective-permute-start | bytes 4718600 | tf_op jit(solution)/shard_map/ppermute | solution.py:23
  42.8 33.9 %collective-permute-start.5 = (bf16[384,1024]{1,0:T(8,128)(2,1)}, bf16[384,1024]{1,0:T(8,128)(2,1)S(1)}, u32[]{:S(2)}, u32[]{:S(2)}) collective-permute-start(bf16[384,1024]{1,0:T(8,128)(2,1)} %get-tuple-element.75), channel_id=1, source_target_pairs={{0,4},{1,5},{2,6},{3,7},{4,0},{5,1},{6,2},{7,3},{8,12},{9,13},{10,... | collective-permute-start | bytes 2359304 | tf_op jit(solution)/shard_map/ppermute | solution.py:23
  76.6 13.0 %copy-start.7 = (bf16[384,1024]{1,0:T(8,128)(2,1)}, bf16[384,1024]{1,0:T(8,128)(2,1)S(1)}, u32[]{:S(2)}) copy-start(bf16[384,1024]{1,0:T(8,128)(2,1)S(1)} %collective-permute-done.5.refs_4_) | copy-start | bytes 2359300
  84.9 4.7 %copy-start.12 = (bf16[2,512,1024]{2,1,0:T(8,128)(2,1)}, bf16[2,512,1024]{2,1,0:T(8,128)(2,1)S(1)}, u32[]{:S(2)}) copy-start(bf16[2,512,1024]{2,1,0:T(8,128)(2,1)S(1)} %collective-permute-done.4) | copy-start | bytes 6291460
  89.6 65.0 %copy-start.13 = (bf16[384,1024]{1,0:T(8,128)(2,1)S(1)}, bf16[384,1024]{1,0:T(8,128)(2,1)}, u32[]{:S(2)}) copy-start(bf16[384,1024]{1,0:T(8,128)(2,1)} %get-tuple-element.88) | copy-start | bytes 2359300
  89.7 84.5 %collective-permute-start.7 = (bf16[512,3072]{1,0:T(8,128)(2,1)}, bf16[512,3072]{1,0:T(8,128)(2,1)S(1)}, u32[]{:S(2)}, u32[]{:S(2)}) collective-permute-start(bf16[512,3072]{1,0:T(8,128)(2,1)} %bitcast.28), channel_id=1, source_target_pairs={{0,16},{8,24},{16,0},{24,8},{1,17},{9,25},{17,1},{25,9},{2,18},{10... | collective-permute-start | bytes 9437192 | tf_op jit(solution)/shard_map/ppermute | solution.py:23
  91.2 83.0 %collective-permute-start.6 = (bf16[512,3072]{1,0:T(8,128)(2,1)}, bf16[512,3072]{1,0:T(8,128)(2,1)S(1)}, u32[]{:S(2)}, u32[]{:S(2)}) collective-permute-start(bf16[512,3072]{1,0:T(8,128)(2,1)} %bitcast.29), channel_id=1, source_target_pairs={{0,8},{8,0},{16,24},{24,16},{1,9},{9,1},{17,25},{25,17},{2,10},{10... | collective-permute-start | bytes 9437192 | tf_op jit(solution)/shard_map/ppermute | solution.py:23
  91.2 49.4 %collective-permute-start.12 = (bf16[384,1024]{1,0:T(8,128)(2,1)}, bf16[384,1024]{1,0:T(8,128)(2,1)S(1)}, u32[]{:S(2)}, u32[]{:S(2)}) collective-permute-start(bf16[384,1024]{1,0:T(8,128)(2,1)} %get-tuple-element.91), channel_id=1, source_target_pairs={{0,6},{1,7},{2,4},{3,5},{4,2},{5,3},{6,0},{7,1},{8,14},{9,15},{10,... | collective-permute-start | bytes 2359304 | tf_op jit(solution)/shard_map/ppermute | solution.py:23
  93.7 60.9 %collective-permute-start.11 = (bf16[384,1024]{1,0:T(8,128)(2,1)}, bf16[384,1024]{1,0:T(8,128)(2,1)S(1)}, u32[]{:S(2)}, u32[]{:S(2)}) collective-permute-start(bf16[384,1024]{1,0:T(8,128)(2,1)} %get-tuple-element.90), channel_id=1, source_target_pairs={{0,5},{1,4},{2,7},{3,6},{4,1},{5,0},{6,3},{7,2},{8,13},{9,12},{10,... | collective-permute-start | bytes 2359304 | tf_op jit(solution)/shard_map/ppermute | solution.py:23
  93.7 80.5 %collective-permute-start.8 = (bf16[1,512,1024]{2,1,0:T(8,128)(2,1)}, bf16[1,512,1024]{2,1,0:T(8,128)(2,1)S(1)}, u32[]{:S(2)}, u32[]{:S(2)}) collective-permute-start(bf16[1,512,1024]{2,1,0:T(8,128)(2,1)} %get-tuple-element.85), channel_id=1, source_target_pairs={{0,8},{8,0},{16,24},{24,16},{1,9},{9,1},{17,25},{25,17},{2,10},{10... | collective-permute-start | bytes 3145736 | tf_op jit(solution)/shard_map/ppermute | solution.py:23
  140.6 34.5 %copy-start.8 = (bf16[384,1024]{1,0:T(8,128)(2,1)}, bf16[384,1024]{1,0:T(8,128)(2,1)S(1)}, u32[]{:S(2)}) copy-start(bf16[384,1024]{1,0:T(8,128)(2,1)S(1)} %collective-permute-done.12.refs_6_) | copy-start | bytes 2359300
  140.6 33.5 %collective-permute-start.9 = (bf16[1,512,1024]{2,1,0:T(8,128)(2,1)S(1)}, bf16[1,512,1024]{2,1,0:T(8,128)(2,1)S(1)}, u32[]{:S(2)}, u32[]{:S(2)}) collective-permute-start(bf16[1,512,1024]{2,1,0:T(8,128)(2,1)S(1)} %get-tuple-element.134), channel_id=1, source_target_pairs={{0,8},{8,0},{16,24},{24,16},{1,9},{9,1},{17,25},{25,17},{2,10},{10... | collective-permute-start | bytes 3145736 | tf_op jit(solution)/shard_map/ppermute | solution.py:23
  154.6 20.5 %copy-start.9 = (bf16[384,1024]{1,0:T(8,128)(2,1)}, bf16[384,1024]{1,0:T(8,128)(2,1)S(1)}, u32[]{:S(2)}) copy-start(bf16[384,1024]{1,0:T(8,128)(2,1)S(1)} %collective-permute-done.11.refs_5_) | copy-start | bytes 2359300
  154.6 19.5 %collective-permute-start.10 = (bf16[384,1024]{1,0:T(8,128)(2,1)S(1)}, bf16[384,1024]{1,0:T(8,128)(2,1)S(1)}, u32[]{:S(2)}, u32[]{:S(2)}) collective-permute-start(bf16[384,1024]{1,0:T(8,128)(2,1)S(1)} %copy-done.13), channel_id=1, source_target_pairs={{0,1},{1,0},{2,3},{3,2},{4,5},{5,4},{6,7},{7,6},{8,9},{9,8},{10,11... | collective-permute-start | bytes 2359304 | tf_op jit(solution)/shard_map/ppermute | solution.py:23
  174.2 3.5 copy-start.10
  174.2 6.8 %copy-start.5 = (bf16[1,512,1024]{2,1,0:T(8,128)(2,1)}, bf16[1,512,1024]{2,1,0:T(8,128)(2,1)S(1)}, u32[]{:S(2)}) copy-start(bf16[1,512,1024]{2,1,0:T(8,128)(2,1)S(1)} %collective-permute-done.8) | copy-start | bytes 3145732
  174.2 1.0 copy-start.6
  174.2 6.8 %copy-start = (bf16[512,3072]{1,0:T(8,128)(2,1)}, bf16[512,3072]{1,0:T(8,128)(2,1)S(1)}, u32[]{:S(2)}) copy-start(bf16[512,3072]{1,0:T(8,128)(2,1)S(1)} %collective-permute-done.7.refs_2_.tokens_ref) | copy-start | bytes 9437188
  174.2 6.8 %copy-start.1 = (bf16[512,3072]{1,0:T(8,128)(2,1)}, bf16[512,3072]{1,0:T(8,128)(2,1)S(1)}, u32[]{:S(2)}) copy-start(bf16[512,3072]{1,0:T(8,128)(2,1)S(1)} %collective-permute-done.6.refs_1_.tokens_ref) | copy-start | bytes 9437188
  175.2 5.8 %collective-permute-start.13 = (bf16[512,3072]{1,0:T(8,128)(2,1)S(1)}, bf16[512,3072]{1,0:T(8,128)(2,1)}, u32[]{:S(2)}, u32[]{:S(2)}) collective-permute-start(bf16[512,3072]{1,0:T(8,128)(2,1)S(1)} %collective-permute-done.7.refs_2_.tokens_ref), channel_id=1, source_target_pairs={{0,8},{8,0},{16,24},{24,16},{1,9},{9,1},{17,25},{25,17},{2,10},{10... | collective-permute-start | bytes 9437192 | tf_op jit(solution)/shard_map/ppermute | solution.py:23
  175.2 37.9 %collective-permute-start.17 = (bf16[384,1024]{1,0:T(8,128)(2,1)}, bf16[384,1024]{1,0:T(8,128)(2,1)S(1)}, u32[]{:S(2)}, u32[]{:S(2)}) collective-permute-start(bf16[384,1024]{1,0:T(8,128)(2,1)} %get-tuple-element.110), channel_id=1, source_target_pairs={{0,7},{1,6},{2,5},{3,4},{4,3},{5,2},{6,1},{7,0},{8,15},{9,14},{10,... | collective-permute-start | bytes 2359304 | tf_op jit(solution)/shard_map/ppermute | solution.py:23
  213.1 0.9 copy-start.11
  214.0 91.8 %all-to-all-start = ((bf16[8,384,512]{2,1,0:T(8,128)(2,1)}), bf16[8,384,512]{2,1,0:T(8,128)(2,1)S(1)}, u32[]{:S(2)}, u32[]{:S(2)}) async-start(bf16[8,384,512]{2,1,0:T(8,128)(2,1)} %bitcast.33), calls=%async_computation | async-start | bytes 6291456 | tf_op jit(solution)/shard_map/all_to_all | solution.py:257
  234.9 12.7 %copy-start.16 = (s32[512,2]{0,1:T(2,128)S(1)}, s32[512,2]{0,1:T(2,128)}, u32[]{:S(2)}) copy-start(s32[512,2]{0,1:T(2,128)} %param.9) | copy-start | bytes 12292
  242.8 69.3 %collective-permute-start.14 = (f32[512,1024]{1,0:T(8,128)}, f32[512,1024]{1,0:T(8,128)}, u32[]{:S(2)}, u32[]{:S(2)}) collective-permute-start(f32[512,1024]{1,0:T(8,128)} %hidden_deriv.4), channel_id=1, source_target_pairs={{0,24},{8,16},{16,8},{24,0},{1,25},{9,17},{17,9},{25,1},{2,26},{10... | collective-permute-start | bytes 6291464 | tf_op jit(solution)/shard_map/ppermute | solution.py:23
  243.0 93.0 %collective-permute-start.15 = (f32[512,1024]{1,0:T(8,128)}, f32[512,1024]{1,0:T(8,128)}, u32[]{:S(2)}, u32[]{:S(2)}) collective-permute-start(f32[512,1024]{1,0:T(8,128)} %hidden_deriv.5), channel_id=1, source_target_pairs={{0,16},{8,24},{16,0},{24,8},{1,17},{9,25},{17,1},{25,9},{2,18},{10... | collective-permute-start | bytes 6291464 | tf_op jit(solution)/shard_map/ppermute | solution.py:23
  244.4 91.7 %collective-permute-start.16 = (f32[512,1024]{1,0:T(8,128)}, f32[512,1024]{1,0:T(8,128)}, u32[]{:S(2)}, u32[]{:S(2)}) collective-permute-start(f32[512,1024]{1,0:T(8,128)} %hidden_deriv.6), channel_id=1, source_target_pairs={{0,8},{8,0},{16,24},{24,16},{1,9},{9,1},{17,25},{25,17},{2,10},{10... | collective-permute-start | bytes 6291464 | tf_op jit(solution)/shard_map/ppermute | solution.py:23
  244.7 44.9 %collective-permute-start.18 = (bf16[384,1024]{1,0:T(8,128)(2,1)}, bf16[384,1024]{1,0:T(8,128)(2,1)}, u32[]{:S(2)}, u32[]{:S(2)}) collective-permute-start(bf16[384,1024]{1,0:T(8,128)(2,1)} %get-tuple-element.112), channel_id=1, source_target_pairs={{0,2},{1,3},{2,0},{3,1},{4,6},{5,7},{6,4},{7,5},{8,10},{9,11},{10,... | collective-permute-start | bytes 2359304 | tf_op jit(solution)/shard_map/ppermute | solution.py:23
  244.7 61.1 %collective-permute-start.19 = (bf16[384,1024]{1,0:T(8,128)(2,1)}, bf16[384,1024]{1,0:T(8,128)(2,1)}, u32[]{:S(2)}, u32[]{:S(2)}) collective-permute-start(bf16[384,1024]{1,0:T(8,128)(2,1)} %get-tuple-element.113), channel_id=1, source_target_pairs={{0,3},{1,2},{2,1},{3,0},{4,7},{5,6},{6,5},{7,4},{8,11},{9,10},{10,... | collective-permute-start | bytes 2359304 | tf_op jit(solution)/shard_map/ppermute | solution.py:23
  305.8 1.6 copy-start.3
  307.5 72.7 %all-to-all-start.1 = ((bf16[8,384,512]{2,1,0:T(8,128)(2,1)}), bf16[8,384,512]{2,1,0:T(8,128)(2,1)S(1)}, u32[]{:S(2)}, u32[]{:S(2)}) async-start(bf16[8,384,512]{2,1,0:T(8,128)(2,1)} %bitcast.34), calls=%async_computation.1 | async-start | bytes 6291456 | tf_op jit(solution)/shard_map/all_to_all | solution.py:257
  380.2 1.6 copy-start.2

commit v12 on v11

--- a/solution.py
+++ b/solution.py
@@ -133,8 +133,8 @@
     return [held[m][0][0] for m in range(experts)]
 
 
-def term_kernel(count, *refs):
-    tokens, hidden, out_ref = refs[:count], refs[count : 2 * count], refs[-1]
+def term_kernel(count, owners_ref, *refs):
+    tokens, hidden, outs = refs[:count], refs[count : 2 * count], refs[2 * count :]
     total = None
     for token_ref, hidden_ref in zip(tokens, hidden):
         one = lax.dot_general(
@@ -144,25 +144,32 @@
             preferred_element_type=jnp.float32,
         )
         total = one if total is None else total + one
-    out_ref[...] = total.astype(jnp.bfloat16)
-
-
-def terms(part, parts, tokens, hidden):
+    total = total.astype(jnp.bfloat16)
+    for i, out_ref in enumerate(outs):
+
+        @pl.when(pl.program_id(0) == i)
+        def _():
+            out_ref[...] = total
+
+
+def terms(tokens, hidden, tall, owners):
     group_tok, width = tokens[0].shape
-    cols = hidden[0].shape[1] // parts
-    tall = width // 8
-    count = len(tokens)
+    cols = hidden[0].shape[1]
+    count, steps = len(tokens), len(owners)
     return pl.pallas_call(
         functools.partial(term_kernel, count),
-        grid=(width // tall,),
-        in_specs=[pl.BlockSpec((group_tok, tall), lambda i: (0, i))] * count
-        + [pl.BlockSpec((group_tok, cols), lambda i: (0, part))] * count,
-        out_specs=pl.BlockSpec((tall, cols), lambda i: (i, 0)),
-        out_shape=jax.ShapeDtypeStruct((width, cols), jnp.bfloat16),
+        grid_spec=pltpu.PrefetchScalarGridSpec(
+            num_scalar_prefetch=1,
+            grid=(steps,),
+            in_specs=[pl.BlockSpec((group_tok, tall), lambda i, owners: (0, owners[i]))] * count
+            + [pl.BlockSpec((group_tok, cols), lambda i, owners: (0, 0))] * count,
+            out_specs=[pl.BlockSpec((tall, cols), lambda i, owners: (0, 0))] * steps,
+        ),
+        out_shape=[jax.ShapeDtypeStruct((tall, cols), jnp.bfloat16)] * steps,
         compiler_params=pltpu.CompilerParams(vmem_limit_bytes=56 * MIB),
         cost_estimate=SMALL,
         name="group_terms",
-    )(*tokens, *hidden)
+    )(jnp.stack(owners), *tokens, *hidden)
 
 
 def deriv_kernel(tokens_ref, weight_ref, out_ref):
@@ -194,16 +201,15 @@
     )(tokens, weight)
 
 
-def update_kernel(count, place_ref, grad_ref, momentum_ref, *refs):
-    weight_refs = refs[:count]
+def update_kernel(count, sources_ref, momentum_ref, *refs):
     new_weight_ref, new_momentum_ref = refs[-2:]
-    for m, weight_ref in enumerate(weight_refs):
-
-        @pl.when(pl.program_id(0) == m)
+    for i in range(count):
+
+        @pl.when(pl.program_id(0) == i)
         def _():
-            grad = grad_ref[0].astype(jnp.float32)
+            grad = refs[i][...].astype(jnp.float32)
             moment = momentum_ref[0].astype(jnp.float32)
-            weight = weight_ref[...].astype(jnp.float32)
+            weight = refs[count + i][...].astype(jnp.float32)
             mix = beta_first * moment + (1.0 - beta_first) * grad
             new_weight_ref[0] = weight * (1.0 - step_rate * decay_rate) - step_rate * jnp.tanh(
                 mix / sign_width
@@ -213,16 +219,17 @@
             )
 
 
-def update(part, parts, place, grad, weights, momentum, done):
-    count, rows, some = grad.shape
-    wide = pl.BlockSpec((1, rows, some), lambda m, place: (0, 0, (place[0] ^ m) * parts + part))
+def update(sources, grads, weights, momentum, done):
+    count = len(grads)
+    rows, cols = grads[0].shape
+    wide = pl.BlockSpec((1, rows, cols), lambda i, sources: (0, 0, sources[i]))
     return pl.pallas_call(
         functools.partial(update_kernel, count),
         grid_spec=pltpu.PrefetchScalarGridSpec(
             num_scalar_prefetch=1,
             grid=(count,),
-            in_specs=[pl.BlockSpec((1, rows, some), lambda m, place: (place[0] ^ m, 0, 0)), wide]
-            + [pl.BlockSpec((rows, some), lambda m, place: (0, part))] * count
+            in_specs=[wide]
+            + [pl.BlockSpec((rows, cols), lambda i, sources: (0, 0))] * (2 * count)
             + [pl.BlockSpec(memory_space=pl.ANY)] * len(done),
             out_specs=[wide, wide],
         ),
@@ -230,11 +237,11 @@
             jax.ShapeDtypeStruct(momentum.shape, jnp.float32),
             jax.ShapeDtypeStruct(momentum.shape, jnp.bfloat16),
         ],
-        input_output_aliases={3 + count + i: i for i in range(len(done))},
+        input_output_aliases={2 + 2 * count + i: i for i in range(len(done))},
         compiler_params=pltpu.CompilerParams(vmem_limit_bytes=56 * MIB),
         cost_estimate=SMALL,
         name="lion_step",
-    )(place.reshape(1), grad, momentum, *weights, *done)
+    )(jnp.stack(sources), momentum, *grads, *weights, *done)
 
 
 def body(out_grad, gate_saved, up_saved, routing, down_weight, momentum):
@@ -250,12 +257,6 @@
     half = experts // 2
     others = sorted(range(2, experts, 2), key=lambda m: (bin(m).count("1"), -m))
 
-    parts = 2 if cols % 256 == 0 else 1
-
-    def to_owners(array, *begun):
-        array = after(array.reshape(shards, rows, cols // parts), *begun)
-        return lax.all_to_all(array, "dp", split_axis=0, concat_axis=0, tiled=True)
-
     weight = down_weight[0]
     tuned = shards == 8
 
@@ -273,48 +274,71 @@
     ]
     blocks, picked, cuts = stage(blocks, picked, cuts)
 
-    held = placed_blocks(blocks, place // 2)
-    beside = swapped(held, "dp", 1)
-    got = swapped(picked[-1], "expert", half)
+    held = {0: placed_blocks(blocks, place // 2)}
+    for m in others:
+        held[m] = swapped(held[m & (m - 1)], "expert", m & -m)
+    beside = {0: swapped(held[0], "dp", 1)}
     weights = {0: cuts[0]}
     if tuned:
-        weights[4] = sent(4)
-    held, beside, got, picked, weights, cuts = stage(held, beside, got, picked, weights, cuts)
-
-    tokens = {0: in_order(held, beside, (place & 1) != 0).reshape(group_tok, width)}
+        for m in (4, 6):
+            weights[m] = sent(m)
+    held, beside, picked, weights, cuts = stage(held, beside, picked, weights, cuts)
+
+    last = (place & 1) != 0
     for m in others:
-        tokens[m] = swapped(tokens[m & (m - 1)], "expert", m & -m)
+        beside[m] = swapped(held[m], "dp", 1)
+    got = swapped(picked[-1], "expert", half)
+    tokens = {0: in_order(held[0], beside[0], last).reshape(group_tok, width)}
     tokens[1] = swapped(tokens[0], "expert", 1)
+    if tuned:
+        weights[2] = sent(2)
+    tokens, beside, got, picked, weights, cuts = stage(
+        tokens, beside, got, picked, weights, cuts
+    )
+
+    for m in others:
+        tokens[m] = in_order(held[m], beside[m], last).reshape(group_tok, width)
+        tokens[m + 1] = swapped(tokens[m], "expert", 1)
+    tokens = [tokens[m] for m in each]
     hidden = spread(picked, got, experts)
     if tuned:
-        for m in (6, 5, 1):
+        for m in (5, 1):
             weights[m] = sent(m)
-    tokens, hidden, weights, cuts = stage(tokens, hidden, weights, cuts)
-
-    for m in others:
-        tokens[m + 1] = swapped(tokens[m], "expert", 1)
-    tokens = [tokens[m] for m in each]
+    tokens, hidden, cuts = stage(tokens, hidden, cuts)
+
     if tuned:
-        for m in (7, 2, 3):
-            weights[m] = sent(m)
-        first_weights, last_weights = weights[7], (weights[2], weights[3])
+        early, late = (4, 6, 5, 7), (2, 3, 1, 0)
+        grads = {}
+        some = terms(tokens, hidden, rows, [place ^ m for m in early])
+        for m in (7, 3):
+            weights[m] = sent(m, *hidden)
+        for m, term in zip(early, some):
+            grads[m] = swapped(term, "dp", m)
+        others_hidden = after(hidden, some, weights[5], weights[1])
+        some = terms(tokens, others_hidden, rows, [place ^ m for m in late])
+        for m, term in zip(late, some):
+            grads[m] = swapped(term, "dp", m)
+        batches = (early, late)
     else:
-        every = lax.all_to_all(
-            weight.reshape(shards, rows, cols), "dp", split_axis=0, concat_axis=0, tiled=True
-        )
-        first_weights, last_weights = every, ()
-        for m in range(1, shards):
-            weights[m] = lax.dynamic_index_in_dim(every, place ^ m, axis=0, keepdims=False)
-
-    term = terms(0, parts, tokens, hidden)
-    weight, term = stage(weight, term)
+        tall = width // 8
+        some = terms(tokens, hidden, tall, [jnp.int32(i) for i in range(8)])
+        arrived = [
+            lax.all_to_all(
+                array.reshape(shards, rows, cols), "dp", split_axis=0, concat_axis=0, tiled=True
+            )
+            for array in (weight, jnp.concatenate(some, axis=0))
+        ]
+        weights, grads = [
+            [
+                lax.dynamic_index_in_dim(array, place ^ m, axis=0, keepdims=False)
+                for m in range(shards)
+            ]
+            for array in arrived
+        ]
+        batches = (range(shards),)
+    weight, _ = stage(weight, some)
     derivs = [deriv_of(tokens[m], weight) for m in each]
     backs = [swapped(derivs[m], "expert", m) for m in each]
-    grads = [to_owners(term, first_weights)]
-    for part in range(1, parts):
-        term = terms(part, parts, tokens, after(hidden, derivs))
-        grads.append(to_owners(term, grads, last_weights))
-
     gate_saved, up_saved, _ = stage(gate_saved, up_saved, derivs)
     gate = gate_saved.astype(jnp.float32)
     up = up_saved.astype(jnp.float32)
@@ -327,9 +351,13 @@
     d_gate = (deriv * up * sigma * (1.0 + gate * (1.0 - sigma))).astype(jnp.bfloat16)
 
     done = ()
-    for part in range(parts):
+    for batch in batches:
         done = update(
-            part, parts, place, grads[part], [weights[m] for m in range(shards)], momentum, done
+            [place ^ m for m in batch],
+            [grads[m] for m in batch],
+            [weights[m] for m in batch],
+            momentum,
+            done,
         )
     new_weight, new_momentum = done
     return (d_gate, d_up, new_weight, new_momentum)

time: 398 us -> 444 us (1.12)
  starting transfers between devices: 29.4 us -> 67.5 us
  waiting for transfers between devices: 232 us -> 242 us
    ppermute x20 -> x28, starting transfers between devices: 19.6 us -> 67.5 us  [swapped(): return lax.ppermute(array, axis, [(i, i ^ mask) for i in range(size)])]
    ppermute x20 -> x28, waiting for transfers between devices: 215 us -> 242 us  [swapped(): return lax.ppermute(array, axis, [(i, i ^ mask) for i in range(size)])]
    all_to_all x2 -> x0, waiting for transfers between devices: 17.1 us -> none  [to_owners(): return lax.all_to_all(array, 'dp', split_axis=0, concat_axis=0, tiled=True)]
    all_to_all x2 -> x0, starting transfers between devices: 9.88 us -> none  [to_owners(): return lax.all_to_all(array, 'dp', split_axis=0, concat_axis=0, tiled=True)]
    pallas_call x1 -> x2, Pallas kernels: 4.72 us -> 9.12 us  [in_order(): pl.pallas_call(order_kernel, grid_spec=pltpu.PrefetchScalarGridSpec(num_s...]
  transfers between devices with their start and end apart: 22 -> 28, of which waited for: 13 -> 12; matrix products, arithmetic and copies ran while one was open for 8% -> 4% of each run, Pallas kernels for 19% -> 19%
where the time goes in v12:
time: 444 us; the launch traced here: 443 us
  waiting for transfers between devices  242 us (55%)
  Pallas kernels  95.4 us (21%)
  starting transfers between devices  67.5 us (15%)
  local copies, waits for them, and re-layouts  19.3 us (4%)
  other arithmetic  18 us (4%)
    ppermute x28, waiting for transfers between devices, swapped(): return lax.ppermute(array, axis, [(i, i ^ mask) for i in range(size)])  242 us
    ppermute x28, starting transfers between devices, swapped(): return lax.ppermute(array, axis, [(i, i ^ mask) for i in range(size)])  67.5 us
    pallas_call x4, Pallas kernels, deriv_of(): pl.pallas_call(deriv_kernel, grid=(cols // wide,), in_specs=[pl.BlockSpec...  31.6 us
    pallas_call x2, Pallas kernels, terms(): pl.pallas_call(functools.partial(term_kernel, count), grid_spec=pltpu.Pre...  26 us
    pallas_call x2, Pallas kernels, update(): pl.pallas_call(functools.partial(update_kernel, count), grid_spec=pltpu.P...  20.6 us
    convert_element_type x1, other arithmetic, body(): d_up = (deriv * gate * sigma).astype(jnp.bfloat16)  15.9 us
    pallas_call x2, Pallas kernels, in_order(): pl.pallas_call(order_kernel, grid_spec=pltpu.PrefetchScalarGridSpec(num_s...  9.12 us
  transfers between devices with their start and end apart: 28, of which 12 were waited for; matrix products, arithmetic and copies ran while one was open for 4% of the time, Pallas kernels for 19%

profile of v12, /device:TPU:8, one launch (start us, length us, event | category | flops | bytes accessed | tf_op | source)
XLA Modules:
  0.0 442.9 jit_solution(15735674725244947145)
XLA Ops:
  0.6 2.7 collective-permute-start.1
  3.3 0.4 collective-permute-start
  3.7 0.5 collective-permute-start.2
  4.2 0.7 broadcast_xor_fusion
  4.9 0.1 copy.18
  5.0 0.8 reshape_reshape.9.named_ref
  5.8 4.1 reshape.42.gate_ref
  9.9 2.2 reshape.43.up_ref
  12.1 5.5 %hidden_rows.1 = (bf16[1,512,1024]{2,1,0:T(8,128)(2,1)}, bf16[1,512,1024]{2,1,0:T(8,128)(2,1)}, bf16[2,512,1024]{2,1,0:T(8,128)(2,1)}) custom-call(bf16[1024,1024]{1,0:T(8,128)(2,1)} %reshape.42.gate_ref, bf16[1024,1024]{1,0:T(8,128)(2,1)} %reshape.43.up_ref, s32[4,256]{1,0:T(4,128)} %reshape_reshape.9.named_ref), custom_call_target="tpu_custom_call" | custom-call | flops 1024 | bytes 1024 | tf_op jit(solution)/shard_map/hidden_rows/pallas_call | solution.py:110
  17.6 5.5 %dynamic-slice_bitcast_fusion = (bf16[384,1024]{1,0:T(8,128)(2,1)}, bf16[384,1024]{1,0:T(8,128)(2,1)}, bf16[384,1024]{1,0:T(8,128)(2,1)}, bf16[384,1024]{1,0:T(8...) fusion(bf16[1,3072,1024]{2,1,0:T(8,128)(2,1)} %param.10, ...), kind=kLoop, calls=%fused_computation.13 | loop fusion | bytes 12582944 | tf_op jit(solution)/shard_map/dynamic_slice | solution.py:272
  23.2 14.0 %collective-permute-done.2.refs_3_ = bf16[64,3072]{1,0:T(8,128)(2,1)S(1)} collective-permute-done((bf16[64,3072]{1,0:T(8,128)(2,1)}, bf16[64,3072]{1,0:T(8,128)(2,1)S(1)}, u32[]{:S(2)}, u32[]{:S(2)}) %collective-permute-start.2) | collective-permute-done | bytes 393248 | tf_op jit(solution)/shard_map/ppermute | solution.py:23
  37.2 0.7 copy-done.17
  37.9 2.6 placed_blocks.1.mine_ref
  40.5 1.5 collective-permute-start.4
  42.0 18.3 %collective-permute-start.3 = (bf16[4,64,3072]{2,1,0:T(8,128)(2,1)}, bf16[4,64,3072]{2,1,0:T(8,128)(2,1)S(1)}, u32[]{:S(2)}, u32[]{:S(2)}) collective-permute-start(bf16[4,64,3072]{2,1,0:T(8,128)(2,1)} %placed_blocks.1.mine_ref), channel_id=1, source_target_pairs={{0,16},{8,24},{16,0},{24,8},{1,17},{9,25},{17,1},{25,9},{2,18},{10... | collective-permute-start | bytes 4718600 | tf_op jit(solution)/shard_map/ppermute | solution.py:23
  60.4 2.4 collective-permute-start.6
  62.7 35.6 %collective-permute-done.6.refs_5_ = bf16[384,1024]{1,0:T(8,128)(2,1)} collective-permute-done((bf16[384,1024]{1,0:T(8,128)(2,1)}, bf16[384,1024]{1,0:T(8,128)(2,1)}, u32[]{:S(2)}, u32[]{:S(2)}) %collective-permute-start.6) | collective-permute-done | bytes 786464 | tf_op jit(solution)/shard_map/ppermute | solution.py:23
  98.3 14.9 %collective-permute-done.5.refs_4_ = bf16[384,1024]{1,0:T(8,128)(2,1)} collective-permute-done((bf16[384,1024]{1,0:T(8,128)(2,1)}, bf16[384,1024]{1,0:T(8,128)(2,1)}, u32[]{:S(2)}, u32[]{:S(2)}) %collective-permute-start.5) | collective-permute-done | bytes 786464 | tf_op jit(solution)/shard_map/ppermute | solution.py:23
  113.2 1.1 copy-done.8
  114.3 4.2 side_by_side.2
  118.5 0.3 collective-permute-start.9
  118.8 0.3 collective-permute-start.8
  119.2 2.2 collective-permute-start.10
  121.4 17.8 %collective-permute-done.10.refs_4_ = bf16[384,1024]{1,0:T(8,128)(2,1)S(1)} collective-permute-done((bf16[384,1024]{1,0:T(8,128)(2,1)}, bf16[384,1024]{1,0:T(8,128)(2,1)S(1)}, u32[]{:S(2)}, u32[]{:S(2)}) %collective-permute-start.10) | collective-permute-done | bytes 786464 | tf_op jit(solution)/shard_map/ppermute | solution.py:23
  139.2 16.3 %collective-permute-done.8.theirs_ref = bf16[4,64,3072]{2,1,0:T(8,128)(2,1)S(1)} collective-permute-done((bf16[4,64,3072]{2,1,0:T(8,128)(2,1)}, bf16[4,64,3072]{2,1,0:T(8,128)(2,1)S(1)}, u32[]{:S(2)}, u32[]{:S(2)}) %collective-permute-start.8) | collective-permute-done | bytes 1572896 | tf_op jit(solution)/shard_map/ppermute | solution.py:23
  155.5 1.1 copy-done.9
  156.6 10.2 %collective-permute-done.9 = bf16[2,512,1024]{2,1,0:T(8,128)(2,1)} collective-permute-done((bf16[2,512,1024]{2,1,0:T(8,128)(2,1)}, bf16[2,512,1024]{2,1,0:T(8,128)(2,1)}, u32[]{:S(2)}, u32[]{:S(2)}) %collective-permute-start.9) | collective-permute-done | bytes 2097184 | tf_op jit(solution)/shard_map/ppermute | solution.py:23
  166.9 5.0 %side_by_side.3 = bf16[4,2,64,3072]{3,2,1,0:T(8,128)(2,1)} custom-call(s32[1]{0:T(128)} %bitcast.place_ref, bf16[4,64,3072]{2,1,0:T(8,128)(2,1)} %copy-done.7, bf16[4,64,3072]{2,1,0:T(8,128)(2,1)} %copy-done.9), custom_call_target="tpu_custom_call" | custom-call | flops 1024 | bytes 1024 | tf_op jit(solution)/shard_map/side_by_side/pallas_call | solution.py:42
  171.8 0.5 collective-permute-start.12
  172.3 2.7 fusion.8
  175.0 0.1 collective-permute-start.13
  175.1 3.1 collective-permute-start.14
  178.2 1.7 collective-permute-start.15
  179.9 0.7 pad_add_fusion.1.owners_ref.sources_ref
  180.6 0.7 pad_add_fusion.owners_ref.sources_ref
  181.3 0.1 collective-permute-start.27
  181.4 5.2 %collective-permute-start.22 = (bf16[384,1024]{1,0:T(8,128)(2,1)}, bf16[384,1024]{1,0:T(8,128)(2,1)}, u32[]{:S(2)}, u32[]{:S(2)}) collective-permute-start(bf16[384,1024]{1,0:T(8,128)(2,1)} %get-tuple-element.148), channel_id=1, source_target_pairs={{0,3},{1,2},{2,1},{3,0},{4,7},{5,6},{6,5},{7,4},{8,11},{9,10},{10,... | collective-permute-start | bytes 2359304 | tf_op jit(solution)/shard_map/ppermute | solution.py:23
  186.5 13.0 %group_terms.2 = (bf16[384,1024]{1,0:T(8,128)(2,1)}, bf16[384,1024]{1,0:T(8,128)(2,1)}, bf16[384,1024]{1,0:T(8,128)(2,1)}, bf16[384,1024]{1,0:T(8,128)(2,1)}) custom-call(s32[4]{0:T(128)} %pad_add_fusion.1.owners_ref.sources_ref, bf16[512,3072]{1,0:T(8,128)(2,1)} %bitcast.35, bf16[512,3072]{1,0:T(8,128)(2,1)} %copy-done, bf16[512,3072]{1,0:T(8,128)(2,1)} %bitcast.39, ...), custom_call_target="tpu_custom_call" | custom-call | flops 1024 | bytes 1024 | tf_op jit(solution)/shard_map/group_terms/pallas_call | solution.py:159
  199.5 29.0 %collective-permute-done.14.refs_6_ = bf16[384,1024]{1,0:T(8,128)(2,1)S(1)} collective-permute-done((bf16[384,1024]{1,0:T(8,128)(2,1)}, bf16[384,1024]{1,0:T(8,128)(2,1)S(1)}, u32[]{:S(2)}, u32[]{:S(2)}) %collective-permute-start.14) | collective-permute-done | bytes 786464 | tf_op jit(solution)/shard_map/ppermute | solution.py:23
  228.5 1.7 collective-permute-start.24
  230.3 0.4 collective-permute-done.15.refs_6_
  230.7 13.0 %group_terms.3 = (bf16[384,1024]{1,0:T(8,128)(2,1)}, bf16[384,1024]{1,0:T(8,128)(2,1)}, bf16[384,1024]{1,0:T(8,128)(2,1)}, bf16[384,1024]{1,0:T(8,128)(2,1)}) custom-call(s32[4]{0:T(128)} %pad_add_fusion.owners_ref.sources_ref, bf16[512,3072]{1,0:T(8,128)(2,1)} %bitcast.36, bf16[512,3072]{1,0:T(8,128)(2,1)} %copy-done, bf16[512,3072]{1,0:T(8,128)(2,1)} %bitcast.40, ...), custom_call_target="tpu_custom_call" | custom-call | flops 1024 | bytes 1024 | tf_op jit(solution)/shard_map/group_terms/pallas_call | solution.py:159
  243.7 17.3 %collective-permute-start.19 = (bf16[384,1024]{1,0:T(8,128)(2,1)}, bf16[384,1024]{1,0:T(8,128)(2,1)S(1)}, u32[]{:S(2)}, u32[]{:S(2)}) collective-permute-start(bf16[384,1024]{1,0:T(8,128)(2,1)} %get-tuple-element.139), channel_id=1, source_target_pairs={{0,2},{1,3},{2,0},{3,1},{4,6},{5,7},{6,4},{7,5},{8,10},{9,11},{10,... | collective-permute-start | bytes 2359304 | tf_op jit(solution)/shard_map/ppermute | solution.py:23
  261.0 7.9 %hidden_deriv.6 = f32[512,1024]{1,0:T(8,128)} custom-call(bf16[512,3072]{1,0:T(8,128)(2,1)} %copy-done, bf16[3072,1024]{1,0:T(8,128)(2,1)} %bitcast.42), custom_call_target="tpu_custom_call" | custom-call | flops 3221225472 | bytes 11534336 | tf_op jit(solution)/shard_map/hidden_deriv/pallas_call | solution.py:185
  268.9 7.9 %hidden_deriv.5 = f32[512,1024]{1,0:T(8,128)} custom-call(bf16[512,3072]{1,0:T(8,128)(2,1)} %bitcast.41, bf16[3072,1024]{1,0:T(8,128)(2,1)} %bitcast.43), custom_call_target="tpu_custom_call" | custom-call | flops 3221225472 | bytes 11534336 | tf_op jit(solution)/shard_map/hidden_deriv/pallas_call | solution.py:185
  276.7 8.0 %hidden_deriv.4 = f32[512,1024]{1,0:T(8,128)} custom-call(bf16[512,3072]{1,0:T(8,128)(2,1)} %copy-done.1, bf16[3072,1024]{1,0:T(8,128)(2,1)} %bitcast.44), custom_call_target="tpu_custom_call" | custom-call | flops 3221225472 | bytes 11534336 | tf_op jit(solution)/shard_map/hidden_deriv/pallas_call | solution.py:185
  284.8 1.0 collective-permute-start.17
  285.8 11.5 %collective-permute-done.19.refs_0_ = bf16[384,1024]{1,0:T(8,128)(2,1)S(1)} collective-permute-done((bf16[384,1024]{1,0:T(8,128)(2,1)}, bf16[384,1024]{1,0:T(8,128)(2,1)S(1)}, u32[]{:S(2)}, u32[]{:S(2)}) %collective-permute-start.19) | collective-permute-done | bytes 786464 | tf_op jit(solution)/shard_map/ppermute | solution.py:23
  297.2 2.4 collective-permute-start.25
  299.6 49.1 %collective-permute-done.24.refs_1_ = bf16[384,1024]{1,0:T(8,128)(2,1)} collective-permute-done((bf16[384,1024]{1,0:T(8,128)(2,1)}, bf16[384,1024]{1,0:T(8,128)(2,1)}, u32[]{:S(2)}, u32[]{:S(2)}) %collective-permute-start.24) | collective-permute-done | bytes 786464 | tf_op jit(solution)/shard_map/ppermute | solution.py:23
  348.7 0.5 collective-permute-start.26
  349.2 14.1 %collective-permute-done.25.refs_2_ = bf16[384,1024]{1,0:T(8,128)(2,1)S(1)} collective-permute-done((bf16[384,1024]{1,0:T(8,128)(2,1)S(1)}, bf16[384,1024]{1,0:T(8,128)(2,1)S(1)}, u32[]{:S(2)}, u32[]{:S(2)}) %collective-permute-start.25) | collective-permute-done | bytes 786464 | tf_op jit(solution)/shard_map/ppermute | solution.py:23
  363.3 4.5 %collective-permute-start.20 = (bf16[384,1024]{1,0:T(8,128)(2,1)}, bf16[384,1024]{1,0:T(8,128)(2,1)}, u32[]{:S(2)}, u32[]{:S(2)}) collective-permute-start(bf16[384,1024]{1,0:T(8,128)(2,1)} %get-tuple-element.140), channel_id=1, source_target_pairs={{0,3},{1,2},{2,1},{3,0},{4,7},{5,6},{6,5},{7,4},{8,11},{9,10},{10,... | collective-permute-start | bytes 2359304 | tf_op jit(solution)/shard_map/ppermute | solution.py:23
  367.8 28.8 %collective-permute-done.26.refs_3_ = bf16[384,1024]{1,0:T(8,128)(2,1)} collective-permute-done((bf16[384,1024]{1,0:T(8,128)(2,1)S(1)}, bf16[384,1024]{1,0:T(8,128)(2,1)}, u32[]{:S(2)}, u32[]{:S(2)}) %collective-permute-start.26) | collective-permute-done | bytes 786464 | tf_op jit(solution)/shard_map/ppermute | solution.py:23
  396.6 0.8 collective-permute-start.21
  397.4 0.2 copy.17
  397.6 0.2 copy.19
  397.8 0.2 copy.21
  398.0 0.2 copy.20
  398.2 7.9 %hidden_deriv.7 = f32[512,1024]{1,0:T(8,128)} custom-call(bf16[512,3072]{1,0:T(8,128)(2,1)} %bitcast.37, bf16[3072,1024]{1,0:T(8,128)(2,1)} %bitcast.45), custom_call_target="tpu_custom_call" | custom-call | flops 3221225472 | bytes 11534336 | tf_op jit(solution)/shard_map/hidden_deriv/pallas_call | solution.py:185
  406.1 10.1 %lion_step.2 = (f32[1,384,8192]{2,1,0:T(8,128)}, bf16[1,384,8192]{2,1,0:T(8,128)(2,1)}) custom-call(s32[4]{0:T(128)} %pad_add_fusion.1.owners_ref.sources_ref, bf16[1,384,8192]{2,1,0:T(8,128)(2,1)} %momentum_ref.3, bf16[384,1024]{1,0:T(8,128)(2,1)} %collective-permute-done.23.refs_0_, bf16[384,1024]{1,0:T(8,128)(2,1)} %collective-permute-done.24.refs_1_, ...), custom_call_target="tpu_custom_call" | custom-call | flops 1024 | bytes 1024 | tf_op jit(solution)/shard_map/lion_step/pallas_call | solution.py:226
  416.2 0.0 collective-permute-done.21.refs_2_
  416.3 10.5 %lion_step.3 = (f32[1,384,8192]{2,1,0:T(8,128)}, bf16[1,384,8192]{2,1,0:T(8,128)(2,1)}) custom-call(s32[4]{0:T(128)} %pad_add_fusion.owners_ref.sources_ref, bf16[1,384,8192]{2,1,0:T(8,128)(2,1)} %momentum_ref.3, bf16[384,1024]{1,0:T(8,128)(2,1)} %copy-done.14, ...), custom_call_target="tpu_custom_call", output_to_operand_aliasing={{0}: (10, {}), {1}: (11, {})} | custom-call | flops 1024 | bytes 1024 | tf_op jit(solution)/shard_map/lion_step/pallas_call | solution.py:226
  426.8 15.9 %fusion.7 = (bf16[512,2,1024]{2,1,0:T(2,128)(2,1)}, bf16[512,2,1024]{2,1,0:T(2,128)(2,1)}) fusion(bf16[512,2,1024]{2,1,0:T(2,128)(2,1)S(1)} %copy-done.2, pred[512,2]{1,0:T(8,128)(4,1)S(1)} %copy.21, pred[512,2]{1,0:T(8,128)(4,1)S(1)} %copy.20, pred[512,2]{1,0:T(8,128)(4,1)S(1)} %copy.19, pred[512,2]{1,0:T(8,128)(4,1)S(1)} %copy.17, ...), kind=kLoop, calls=%fused_computation.10 | loop fusion | flops 19922944 | bytes 16781312 | tf_op jit(solution)/shard_map/convert_element_type | solution.py:350
  (61 shorter events, 0.1 us)
Async XLA Ops:
  0.6 9.3 %copy-start.3 = (bf16[512,2,1024]{2,1,0:T(2,128)(2,1)S(1)}, bf16[512,2,1024]{2,1,0:T(2,128)(2,1)}, u32[]{:S(2)}) copy-start(bf16[512,2,1024]{2,1,0:T(2,128)(2,1)} %param.8) | copy-start | bytes 6291460
  0.6 22.5 %collective-permute-start.1 = (bf16[64,3072]{1,0:T(8,128)(2,1)}, bf16[64,3072]{1,0:T(8,128)(2,1)S(1)}, u32[]{:S(2)}, u32[]{:S(2)}) collective-permute-start(bf16[64,3072]{1,0:T(8,128)(2,1)} %refs_0_), channel_id=1, source_target_pairs={{0,4},{1,5},{2,6},{3,7},{4,0},{5,1},{6,2},{7,3},{8,12},{9,13},{10,... | collective-permute-start | bytes 1179656 | tf_op jit(solution)/shard_map/ppermute | solution.py:23
  3.3 19.8 %collective-permute-start = (bf16[64,3072]{1,0:T(8,128)(2,1)}, bf16[64,3072]{1,0:T(8,128)(2,1)S(1)}, u32[]{:S(2)}, u32[]{:S(2)}) collective-permute-start(bf16[64,3072]{1,0:T(8,128)(2,1)} %refs_0_), channel_id=1, source_target_pairs={{0,2},{1,3},{2,0},{3,1},{4,6},{5,7},{6,4},{7,5},{8,10},{9,11},{10,... | collective-permute-start | bytes 1179656 | tf_op jit(solution)/shard_map/ppermute | solution.py:23
  3.7 33.4 %collective-permute-start.2 = (bf16[64,3072]{1,0:T(8,128)(2,1)}, bf16[64,3072]{1,0:T(8,128)(2,1)S(1)}, u32[]{:S(2)}, u32[]{:S(2)}) collective-permute-start(bf16[64,3072]{1,0:T(8,128)(2,1)} %refs_0_), channel_id=1, source_target_pairs={{0,6},{1,7},{2,4},{3,5},{4,2},{5,3},{6,0},{7,1},{8,14},{9,15},{10,... | collective-permute-start | bytes 1179656 | tf_op jit(solution)/shard_map/ppermute | solution.py:23
  23.1 14.0 %copy-start.15 = (bf16[64,3072]{1,0:T(8,128)(2,1)}, bf16[64,3072]{1,0:T(8,128)(2,1)S(1)}, u32[]{:S(2)}) copy-start(bf16[64,3072]{1,0:T(8,128)(2,1)S(1)} %collective-permute-done.1.refs_2_) | copy-start | bytes 1179652
  23.2 14.0 %copy-start.16 = (bf16[64,3072]{1,0:T(8,128)(2,1)}, bf16[64,3072]{1,0:T(8,128)(2,1)S(1)}, u32[]{:S(2)}) copy-start(bf16[64,3072]{1,0:T(8,128)(2,1)S(1)} %collective-permute-done.refs_1_) | copy-start | bytes 1179652
  37.2 0.7 copy-start.17
  40.5 72.7 %collective-permute-start.4 = (bf16[4,64,3072]{2,1,0:T(8,128)(2,1)}, bf16[4,64,3072]{2,1,0:T(8,128)(2,1)S(1)}, u32[]{:S(2)}, u32[]{:S(2)}) collective-permute-start(bf16[4,64,3072]{2,1,0:T(8,128)(2,1)} %placed_blocks.1.mine_ref), channel_id=1, source_target_pairs={{0,1},{1,0},{2,3},{3,2},{4,5},{5,4},{6,7},{7,6},{8,9},{9,8},{10,11... | collective-permute-start | bytes 4718600 | tf_op jit(solution)/shard_map/ppermute | solution.py:23
  42.0 71.2 %collective-permute-start.3 = (bf16[4,64,3072]{2,1,0:T(8,128)(2,1)}, bf16[4,64,3072]{2,1,0:T(8,128)(2,1)S(1)}, u32[]{:S(2)}, u32[]{:S(2)}) collective-permute-start(bf16[4,64,3072]{2,1,0:T(8,128)(2,1)} %placed_blocks.1.mine_ref), channel_id=1, source_target_pairs={{0,16},{8,24},{16,0},{24,8},{1,17},{9,25},{17,1},{25,9},{2,18},{10... | collective-permute-start | bytes 4718600 | tf_op jit(solution)/shard_map/ppermute | solution.py:23
  60.4 38.0 %collective-permute-start.6 = (bf16[384,1024]{1,0:T(8,128)(2,1)}, bf16[384,1024]{1,0:T(8,128)(2,1)}, u32[]{:S(2)}, u32[]{:S(2)}) collective-permute-start(bf16[384,1024]{1,0:T(8,128)(2,1)} %get-tuple-element.93), channel_id=1, source_target_pairs={{0,6},{1,7},{2,4},{3,5},{4,2},{5,3},{6,0},{7,1},{8,14},{9,15},{10,... | collective-permute-start | bytes 2359304 | tf_op jit(solution)/shard_map/ppermute | solution.py:23
  62.7 50.4 %collective-permute-start.5 = (bf16[384,1024]{1,0:T(8,128)(2,1)}, bf16[384,1024]{1,0:T(8,128)(2,1)}, u32[]{:S(2)}, u32[]{:S(2)}) collective-permute-start(bf16[384,1024]{1,0:T(8,128)(2,1)} %get-tuple-element.92), channel_id=1, source_target_pairs={{0,4},{1,5},{2,6},{3,7},{4,0},{5,1},{6,2},{7,3},{8,12},{9,13},{10,... | collective-permute-start | bytes 2359304 | tf_op jit(solution)/shard_map/ppermute | solution.py:23
  113.2 1.1 copy-start.8
  113.2 5.3 %copy-start.7 = (bf16[4,64,3072]{2,1,0:T(8,128)(2,1)}, bf16[4,64,3072]{2,1,0:T(8,128)(2,1)S(1)}, u32[]{:S(2)}) copy-start(bf16[4,64,3072]{2,1,0:T(8,128)(2,1)S(1)} %collective-permute-done.3.mine_ref) | copy-start | bytes 4718596
  118.5 48.4 %collective-permute-start.7 = (bf16[512,3072]{1,0:T(8,128)(2,1)}, bf16[512,3072]{1,0:T(8,128)(2,1)S(1)}, u32[]{:S(2)}, u32[]{:S(2)}) collective-permute-start(bf16[512,3072]{1,0:T(8,128)(2,1)} %bitcast.34), channel_id=1, source_target_pairs={{0,8},{8,0},{16,24},{24,16},{1,9},{9,1},{17,25},{25,17},{2,10},{10... | collective-permute-start | bytes 9437192 | tf_op jit(solution)/shard_map/ppermute | solution.py:23
  118.5 48.4 %collective-permute-start.9 = (bf16[2,512,1024]{2,1,0:T(8,128)(2,1)}, bf16[2,512,1024]{2,1,0:T(8,128)(2,1)}, u32[]{:S(2)}, u32[]{:S(2)}) collective-permute-start(bf16[2,512,1024]{2,1,0:T(8,128)(2,1)} %get-tuple-element.102), channel_id=1, source_target_pairs={{0,16},{8,24},{16,0},{24,8},{1,17},{9,25},{17,1},{25,9},{2,18},{10... | collective-permute-start | bytes 6291464 | tf_op jit(solution)/shard_map/ppermute | solution.py:23
  118.8 36.7 %collective-permute-start.8 = (bf16[4,64,3072]{2,1,0:T(8,128)(2,1)}, bf16[4,64,3072]{2,1,0:T(8,128)(2,1)S(1)}, u32[]{:S(2)}, u32[]{:S(2)}) collective-permute-start(bf16[4,64,3072]{2,1,0:T(8,128)(2,1)} %copy-done.7), channel_id=1, source_target_pairs={{0,1},{1,0},{2,3},{3,2},{4,5},{5,4},{6,7},{7,6},{8,9},{9,8},{10,11... | collective-permute-start | bytes 4718600 | tf_op jit(solution)/shard_map/ppermute | solution.py:23
  119.2 20.0 %collective-permute-start.10 = (bf16[384,1024]{1,0:T(8,128)(2,1)}, bf16[384,1024]{1,0:T(8,128)(2,1)S(1)}, u32[]{:S(2)}, u32[]{:S(2)}) collective-permute-start(bf16[384,1024]{1,0:T(8,128)(2,1)} %get-tuple-element.106), channel_id=1, source_target_pairs={{0,2},{1,3},{2,0},{3,1},{4,6},{5,7},{6,4},{7,5},{8,10},{9,11},{10,... | collective-permute-start | bytes 2359304 | tf_op jit(solution)/shard_map/ppermute | solution.py:23
  139.2 27.7 %copy-start.12 = (bf16[384,1024]{1,0:T(8,128)(2,1)}, bf16[384,1024]{1,0:T(8,128)(2,1)S(1)}, u32[]{:S(2)}) copy-start(bf16[384,1024]{1,0:T(8,128)(2,1)S(1)} %collective-permute-done.10.refs_4_) | copy-start | bytes 2359300
  155.5 1.1 copy-start.9
  166.8 5.0 %copy-start = (bf16[512,3072]{1,0:T(8,128)(2,1)}, bf16[512,3072]{1,0:T(8,128)(2,1)S(1)}, u32[]{:S(2)}) copy-start(bf16[512,3072]{1,0:T(8,128)(2,1)S(1)} %collective-permute-done.7.refs_1_.tokens_ref) | copy-start | bytes 9437188
  171.8 9.5 %collective-permute-start.11 = (bf16[512,3072]{1,0:T(8,128)(2,1)}, bf16[512,3072]{1,0:T(8,128)(2,1)S(1)}, u32[]{:S(2)}, u32[]{:S(2)}) collective-permute-start(bf16[512,3072]{1,0:T(8,128)(2,1)} %bitcast.38), channel_id=1, source_target_pairs={{0,8},{8,0},{16,24},{24,16},{1,9},{9,1},{17,25},{25,17},{2,10},{10... | collective-permute-start | bytes 9437192 | tf_op jit(solution)/shard_map/ppermute | solution.py:23
  171.8 9.4 %collective-permute-start.12 = (bf16[1,512,1024]{2,1,0:T(8,128)(2,1)}, bf16[1,512,1024]{2,1,0:T(8,128)(2,1)S(1)}, u32[]{:S(2)}, u32[]{:S(2)}) collective-permute-start(bf16[1,512,1024]{2,1,0:T(8,128)(2,1)} %get-tuple-element.117), channel_id=1, source_target_pairs={{0,8},{8,0},{16,24},{24,16},{1,9},{9,1},{17,25},{25,17},{2,10},{10... | collective-permute-start | bytes 3145736 | tf_op jit(solution)/shard_map/ppermute | solution.py:23
  175.0 6.2 %collective-permute-start.13 = (bf16[1,512,1024]{2,1,0:T(8,128)(2,1)S(1)}, bf16[1,512,1024]{2,1,0:T(8,128)(2,1)S(1)}, u32[]{:S(2)}, u32[]{:S(2)}) collective-permute-start(bf16[1,512,1024]{2,1,0:T(8,128)(2,1)S(1)} %get-tuple-element.168), channel_id=1, source_target_pairs={{0,8},{8,0},{16,24},{24,16},{1,9},{9,1},{17,25},{25,17},{2,10},{10... | collective-permute-start | bytes 3145736 | tf_op jit(solution)/shard_map/ppermute | solution.py:23
  175.1 53.4 %collective-permute-start.14 = (bf16[384,1024]{1,0:T(8,128)(2,1)}, bf16[384,1024]{1,0:T(8,128)(2,1)S(1)}, u32[]{:S(2)}, u32[]{:S(2)}) collective-permute-start(bf16[384,1024]{1,0:T(8,128)(2,1)} %get-tuple-element.121), channel_id=1, source_target_pairs={{0,5},{1,4},{2,7},{3,6},{4,1},{5,0},{6,3},{7,2},{8,13},{9,12},{10,... | collective-permute-start | bytes 2359304 | tf_op jit(solution)/shard_map/ppermute | solution.py:23
  178.2 52.5 %collective-permute-start.15 = (bf16[384,1024]{1,0:T(8,128)(2,1)}, bf16[384,1024]{1,0:T(8,128)(2,1)S(1)}, u32[]{:S(2)}, u32[]{:S(2)}) collective-permute-start(bf16[384,1024]{1,0:T(8,128)(2,1)} %get-tuple-element.119), channel_id=1, source_target_pairs={{0,1},{1,0},{2,3},{3,2},{4,5},{5,4},{6,7},{7,6},{8,9},{9,8},{10,11... | collective-permute-start | bytes 2359304 | tf_op jit(solution)/shard_map/ppermute | solution.py:23
  181.3 5.3 %copy-start.5 = (bf16[1,512,1024]{2,1,0:T(8,128)(2,1)}, bf16[1,512,1024]{2,1,0:T(8,128)(2,1)S(1)}, u32[]{:S(2)}) copy-start(bf16[1,512,1024]{2,1,0:T(8,128)(2,1)S(1)} %collective-permute-done.12) | copy-start | bytes 3145732
  181.3 5.3 %copy-start.6 = (bf16[1,512,1024]{2,1,0:T(8,128)(2,1)}, bf16[1,512,1024]{2,1,0:T(8,128)(2,1)S(1)}, u32[]{:S(2)}) copy-start(bf16[1,512,1024]{2,1,0:T(8,128)(2,1)S(1)} %collective-permute-done.13) | copy-start | bytes 3145732
  181.3 5.2 %copy-start.1 = (bf16[512,3072]{1,0:T(8,128)(2,1)}, bf16[512,3072]{1,0:T(8,128)(2,1)S(1)}, u32[]{:S(2)}) copy-start(bf16[512,3072]{1,0:T(8,128)(2,1)S(1)} %collective-permute-done.11.refs_3_.tokens_ref) | copy-start | bytes 9437188
  181.3 103.5 %collective-permute-start.27 = (bf16[384,1024]{1,0:T(8,128)(2,1)}, bf16[384,1024]{1,0:T(8,128)(2,1)}, u32[]{:S(2)}, u32[]{:S(2)}) collective-permute-start(bf16[384,1024]{1,0:T(8,128)(2,1)} %get-tuple-element.153), channel_id=1, source_target_pairs={{0,7},{1,6},{2,5},{3,4},{4,3},{5,2},{6,1},{7,0},{8,15},{9,14},{10,... | collective-permute-start | bytes 2359304 | tf_op jit(solution)/shard_map/ppermute | solution.py:23
  181.4 103.4 %collective-permute-start.22 = (bf16[384,1024]{1,0:T(8,128)(2,1)}, bf16[384,1024]{1,0:T(8,128)(2,1)}, u32[]{:S(2)}, u32[]{:S(2)}) collective-permute-start(bf16[384,1024]{1,0:T(8,128)(2,1)} %get-tuple-element.148), channel_id=1, source_target_pairs={{0,3},{1,2},{2,1},{3,0},{4,7},{5,6},{6,5},{7,4},{8,11},{9,10},{10,... | collective-permute-start | bytes 2359304 | tf_op jit(solution)/shard_map/ppermute | solution.py:23
  199.5 97.7 %collective-permute-start.23 = (bf16[384,1024]{1,0:T(8,128)(2,1)}, bf16[384,1024]{1,0:T(8,128)(2,1)}, u32[]{:S(2)}, u32[]{:S(2)}) collective-permute-start(bf16[384,1024]{1,0:T(8,128)(2,1)} %get-tuple-element.131), channel_id=1, source_target_pairs={{0,4},{1,5},{2,6},{3,7},{4,0},{5,1},{6,2},{7,3},{8,12},{9,13},{10,... | collective-permute-start | bytes 2359304 | tf_op jit(solution)/shard_map/ppermute | solution.py:23
  228.5 15.2 %copy-start.10 = (bf16[384,1024]{1,0:T(8,128)(2,1)}, bf16[384,1024]{1,0:T(8,128)(2,1)S(1)}, u32[]{:S(2)}) copy-start(bf16[384,1024]{1,0:T(8,128)(2,1)S(1)} %collective-permute-done.14.refs_6_) | copy-start | bytes 2359300
  228.5 120.2 %collective-permute-start.24 = (bf16[384,1024]{1,0:T(8,128)(2,1)}, bf16[384,1024]{1,0:T(8,128)(2,1)}, u32[]{:S(2)}, u32[]{:S(2)}) collective-permute-start(bf16[384,1024]{1,0:T(8,128)(2,1)} %get-tuple-element.132), channel_id=1, source_target_pairs={{0,6},{1,7},{2,4},{3,5},{4,2},{5,3},{6,0},{7,1},{8,14},{9,15},{10,... | collective-permute-start | bytes 2359304 | tf_op jit(solution)/shard_map/ppermute | solution.py:23
  230.7 13.0 %copy-start.13 = (bf16[384,1024]{1,0:T(8,128)(2,1)}, bf16[384,1024]{1,0:T(8,128)(2,1)S(1)}, u32[]{:S(2)}) copy-start(bf16[384,1024]{1,0:T(8,128)(2,1)S(1)} %collective-permute-done.15.refs_6_) | copy-start | bytes 2359300
  243.7 53.5 %collective-permute-start.19 = (bf16[384,1024]{1,0:T(8,128)(2,1)}, bf16[384,1024]{1,0:T(8,128)(2,1)S(1)}, u32[]{:S(2)}, u32[]{:S(2)}) collective-permute-start(bf16[384,1024]{1,0:T(8,128)(2,1)} %get-tuple-element.139), channel_id=1, source_target_pairs={{0,2},{1,3},{2,0},{3,1},{4,6},{5,7},{6,4},{7,5},{8,10},{9,11},{10,... | collective-permute-start | bytes 2359304 | tf_op jit(solution)/shard_map/ppermute | solution.py:23
  276.7 20.5 %copy-start.20 = (bf16[384,1024]{1,0:T(8,128)(2,1)S(1)}, bf16[384,1024]{1,0:T(8,128)(2,1)}, u32[]{:S(2)}) copy-start(bf16[384,1024]{1,0:T(8,128)(2,1)} %get-tuple-element.133) | copy-start | bytes 2359300
  276.7 72.0 %copy-start.19 = (bf16[384,1024]{1,0:T(8,128)(2,1)S(1)}, bf16[384,1024]{1,0:T(8,128)(2,1)}, u32[]{:S(2)}) copy-start(bf16[384,1024]{1,0:T(8,128)(2,1)} %get-tuple-element.134) | copy-start | bytes 2359300
  276.7 120.7 %copy-start.18 = (s32[512,2]{0,1:T(2,128)S(1)}, s32[512,2]{0,1:T(2,128)}, u32[]{:S(2)}) copy-start(s32[512,2]{0,1:T(2,128)} %param.9) | copy-start | bytes 12292
  284.7 142.0 %collective-permute-start.16 = (f32[512,1024]{1,0:T(8,128)}, f32[512,1024]{1,0:T(8,128)S(1)}, u32[]{:S(2)}, u32[]{:S(2)}) collective-permute-start(f32[512,1024]{1,0:T(8,128)} %hidden_deriv.4), channel_id=1, source_target_pairs={{0,24},{8,16},{16,8},{24,0},{1,25},{9,17},{17,9},{25,1},{2,26},{10... | collective-permute-start | bytes 6291464 | tf_op jit(solution)/shard_map/ppermute | solution.py:23
  284.8 142.0 %collective-permute-start.17 = (f32[512,1024]{1,0:T(8,128)}, f32[512,1024]{1,0:T(8,128)}, u32[]{:S(2)}, u32[]{:S(2)}) collective-permute-start(f32[512,1024]{1,0:T(8,128)} %hidden_deriv.5), channel_id=1, source_target_pairs={{0,16},{8,24},{16,0},{24,8},{1,17},{9,25},{17,1},{25,9},{2,18},{10... | collective-permute-start | bytes 6291464 | tf_op jit(solution)/shard_map/ppermute | solution.py:23
  297.2 66.1 %copy-start.14 = (bf16[384,1024]{1,0:T(8,128)(2,1)}, bf16[384,1024]{1,0:T(8,128)(2,1)S(1)}, u32[]{:S(2)}) copy-start(bf16[384,1024]{1,0:T(8,128)(2,1)S(1)} %collective-permute-done.19.refs_0_) | copy-start | bytes 2359300
  297.2 129.5 %collective-permute-start.18 = (f32[512,1024]{1,0:T(8,128)}, f32[512,1024]{1,0:T(8,128)}, u32[]{:S(2)}, u32[]{:S(2)}) collective-permute-start(f32[512,1024]{1,0:T(8,128)} %hidden_deriv.6), channel_id=1, source_target_pairs={{0,8},{8,0},{16,24},{24,16},{1,9},{9,1},{17,25},{25,17},{2,10},{10... | collective-permute-start | bytes 6291464 | tf_op jit(solution)/shard_map/ppermute | solution.py:23
  297.2 66.0 %collective-permute-start.25 = (bf16[384,1024]{1,0:T(8,128)(2,1)S(1)}, bf16[384,1024]{1,0:T(8,128)(2,1)S(1)}, u32[]{:S(2)}, u32[]{:S(2)}) collective-permute-start(bf16[384,1024]{1,0:T(8,128)(2,1)S(1)} %copy-done.20), channel_id=1, source_target_pairs={{0,5},{1,4},{2,7},{3,6},{4,1},{5,0},{6,3},{7,2},{8,13},{9,12},{10,... | collective-permute-start | bytes 2359304 | tf_op jit(solution)/shard_map/ppermute | solution.py:23
  348.7 47.9 %collective-permute-start.26 = (bf16[384,1024]{1,0:T(8,128)(2,1)S(1)}, bf16[384,1024]{1,0:T(8,128)(2,1)}, u32[]{:S(2)}, u32[]{:S(2)}) collective-permute-start(bf16[384,1024]{1,0:T(8,128)(2,1)S(1)} %copy-done.19), channel_id=1, source_target_pairs={{0,7},{1,6},{2,5},{3,4},{4,3},{5,2},{6,1},{7,0},{8,15},{9,14},{10,... | collective-permute-start | bytes 2359304 | tf_op jit(solution)/shard_map/ppermute | solution.py:23
  363.3 42.8 %copy-start.11 = (bf16[384,1024]{1,0:T(8,128)(2,1)}, bf16[384,1024]{1,0:T(8,128)(2,1)S(1)}, u32[]{:S(2)}) copy-start(bf16[384,1024]{1,0:T(8,128)(2,1)S(1)} %collective-permute-done.25.refs_2_) | copy-start | bytes 2359300
  363.3 52.9 %collective-permute-start.20 = (bf16[384,1024]{1,0:T(8,128)(2,1)}, bf16[384,1024]{1,0:T(8,128)(2,1)}, u32[]{:S(2)}, u32[]{:S(2)}) collective-permute-start(bf16[384,1024]{1,0:T(8,128)(2,1)} %get-tuple-element.140), channel_id=1, source_target_pairs={{0,3},{1,2},{2,1},{3,0},{4,7},{5,6},{6,5},{7,4},{8,11},{9,10},{10,... | collective-permute-start | bytes 2359304 | tf_op jit(solution)/shard_map/ppermute | solution.py:23
  396.6 19.6 %collective-permute-start.21 = (bf16[384,1024]{1,0:T(8,128)(2,1)}, bf16[384,1024]{1,0:T(8,128)(2,1)}, u32[]{:S(2)}, u32[]{:S(2)}) collective-permute-start(bf16[384,1024]{1,0:T(8,128)(2,1)} %get-tuple-element.141), channel_id=1, source_target_pairs={{0,1},{1,0},{2,3},{3,2},{4,5},{5,4},{6,7},{7,6},{8,9},{9,8},{10,11... | collective-permute-start | bytes 2359304 | tf_op jit(solution)/shard_map/ppermute | solution.py:23
  416.3 10.5 %copy-start.2 = (bf16[512,2,1024]{2,1,0:T(2,128)(2,1)S(1)}, bf16[512,2,1024]{2,1,0:T(2,128)(2,1)}, u32[]{:S(2)}) copy-start(bf16[512,2,1024]{2,1,0:T(2,128)(2,1)} %param.7) | copy-start | bytes 6291460
  416.3 10.5 %copy-start.4 = (bf16[512,2,1024]{2,1,0:T(2,128)(2,1)S(1)}, bf16[512,2,1024]{2,1,0:T(2,128)(2,1)}, u32[]{:S(2)}) copy-start(bf16[512,2,1024]{2,1,0:T(2,128)(2,1)} %param.8) | copy-start | bytes 6291460

commit v13 on v8

--- a/solution.py
+++ b/solution.py
@@ -76,14 +76,13 @@
     )(place.reshape(1), *blocks)
 
 
-def pick(hidden, named_ref, out_refs):
+def pick(hidden, named, out_refs):
     count_rows = hidden.shape[0]
     tokens = out_refs[0].shape[1]
     topk = count_rows // tokens
     token = lax.broadcasted_iota(jnp.int32, (tokens, count_rows), 0)
     row = lax.broadcasted_iota(jnp.int32, (tokens, count_rows), 1)
     here = (row >= token * topk) & (row < token * topk + topk)
-    named = named_ref[pl.ds(pl.program_id(0), 1), :]
     m = 0
     for out_ref in out_refs:
         for i in range(out_ref.shape[0]):
@@ -94,72 +93,49 @@
             m += 1
 
 
-EIGHTHS = (3, 4, 1)
-
-
-def of_part(step, body):
-    begin = 0
-    for part, count in enumerate(EIGHTHS):
-        inside = (step >= begin) & (step < begin + count)
-        pl.when(inside)(functools.partial(body, part))
-        begin += count
-
-
-def hidden_kernel(gate_ref, up_ref, named_ref, *refs):
-    part_refs, out_refs = refs[: len(EIGHTHS)], refs[len(EIGHTHS) :]
+def hidden_kernel(place_ref, gate_ref, up_ref, named_ref, twice_ref, *out_refs):
     gate = gate_ref[...].astype(jnp.float32)
     up = up_ref[...].astype(jnp.float32)
     hidden = (gate * jax.nn.sigmoid(gate) * up).astype(jnp.bfloat16)
-    pick(hidden, named_ref, out_refs)
-
-    def write(part):
-        part_refs[part][...] = hidden
-
-    of_part(pl.program_id(0), write)
-
-
-def pick_kernel(*refs):
-    part_refs, named_ref = refs[: len(EIGHTHS)], refs[len(EIGHTHS)]
-
-    def read(part):
-        pick(part_refs[part][...], named_ref, refs[len(EIGHTHS) + 1 :])
-
-    of_part(pl.program_id(0), read)
-
-
-def picked_rows(arrays, named, group_tok, experts, fresh):
-    cols = arrays[0].shape[1]
+    twice_ref[0] = hidden
+    twice_ref[1] = hidden
+    pick(hidden, named_ref[pl.ds(pl.program_id(0), 1), :], out_refs)
+
+
+def pick_kernel(place_ref, hidden_ref, named_ref, *out_refs):
+    pick(hidden_ref[0], named_ref[pl.ds(pl.program_id(0), 1), :], out_refs)
+
+
+def picked_rows(arrays, named, group_tok, experts, which):
+    cols = arrays[0].shape[-1]
     topk = named.shape[1] // group_tok
-    steps = sum(EIGHTHS)
+    steps = 4
     some = group_tok // steps
+    fresh = len(arrays) == 2
     sizes = [1] + [1 << b for b in range(experts.bit_length() - 1)]
     out_shape = [jax.ShapeDtypeStruct((n, group_tok, cols), jnp.bfloat16) for n in sizes]
-    out_specs = [pl.BlockSpec((n, some, cols), lambda i: (0, i, 0)) for n in sizes]
-    rows = (some * topk, cols)
-    in_parts = [
-        pl.BlockSpec(
-            rows,
-            lambda i, begin=sum(EIGHTHS[:p]), count=count: (jnp.clip(i - begin, 0, count - 1), 0),
-        )
-        for p, count in enumerate(EIGHTHS)
-    ]
-    in_specs = in_parts
+    out_specs = [pl.BlockSpec((n, some, cols), lambda i, which: (0, i, 0)) for n in sizes]
     if fresh:
-        in_specs = [pl.BlockSpec(rows, lambda i: (i, 0))] * 2
+        in_specs = [pl.BlockSpec((some * topk, cols), lambda i, which: (i, 0))] * 2
         out_shape = [
-            jax.ShapeDtypeStruct((n * some * topk, cols), jnp.bfloat16) for n in EIGHTHS
+            jax.ShapeDtypeStruct((2, group_tok * topk, cols), jnp.bfloat16)
         ] + out_shape
-        out_specs = in_parts + out_specs
+        out_specs = [pl.BlockSpec((2, some * topk, cols), lambda i, which: (0, i, 0))] + out_specs
+    else:
+        in_specs = [pl.BlockSpec((1, some * topk, cols), lambda i, which: (which[0], i, 0))]
     return pl.pallas_call(
         hidden_kernel if fresh else pick_kernel,
-        grid=(steps,),
-        in_specs=in_specs + [pl.BlockSpec((steps, some * topk), lambda i: (0, 0))],
-        out_specs=out_specs,
+        grid_spec=pltpu.PrefetchScalarGridSpec(
+            num_scalar_prefetch=1,
+            grid=(steps,),
+            in_specs=in_specs + [pl.BlockSpec((steps, some * topk), lambda i, which: (0, 0))],
+            out_specs=out_specs,
+        ),
         out_shape=out_shape,
         compiler_params=pltpu.CompilerParams(vmem_limit_bytes=56 * MIB),
         cost_estimate=SMALL,
         name="hidden_rows",
-    )(*arrays, named.reshape(steps, some * topk))
+    )(which.reshape(1), *arrays, named.reshape(steps, some * topk))
 
 
 def spread(picked, got, experts):
@@ -238,11 +214,7 @@
         out_specs=pl.BlockSpec((group_tok, wide), lambda i: (0, i)),
         out_shape=jax.ShapeDtypeStruct((group_tok, cols), jnp.float32),
         compiler_params=pltpu.CompilerParams(vmem_limit_bytes=56 * MIB),
-        cost_estimate=pl.CostEstimate(
-            flops=2 * group_tok * width * cols,
-            bytes_accessed=2 * (group_tok + cols) * width + 4 * group_tok * cols,
-            transcendentals=0,
-        ),
+        cost_estimate=SMALL,
         name="hidden_deriv",
     )(tokens, weight)
 
@@ -308,42 +280,40 @@
 
     blocks = [swapped(out_grad, "dp", m) for m in range(0, shards, 2)]
     named = (routing ^ mine).reshape(1, group_tok * topk)
-    hidden = picked_rows(
-        [gate_saved.reshape(-1, cols), up_saved.reshape(-1, cols)], named, group_tok, experts, True
-    )
-    own_parts, own_picked = hidden[: len(EIGHTHS)], hidden[len(EIGHTHS) :]
-    blocks, own_parts, own_picked = stage(blocks, own_parts, own_picked)
+    upper = place // span
+    twice, *own_picked = picked_rows(
+        [gate_saved.reshape(-1, cols), up_saved.reshape(-1, cols)],
+        named,
+        group_tok,
+        experts,
+        upper,
+    )
+    blocks, twice, own_picked = stage(blocks, twice, own_picked)
+
+    pairs = [[i, i + span] for i in range(span)]
+    other_twice = lax.all_to_all(
+        twice, "dp", split_axis=0, concat_axis=0, tiled=True, axis_index_groups=pairs
+    )
 
     held = {0: placed_blocks(blocks, place // 2)}
-    held[0], own_parts = stage(held[0], own_parts)
     for m in others:
         held[m] = swapped(held[m & (m - 1)], "expert", m & -m)
     beside = {0: swapped(held[0], "dp", 1)}
-    other_parts = [swapped(own_parts[0], "dp", span)]
-    held, beside, other_parts, own_parts, own_picked = stage(
-        held, beside, other_parts, own_parts, own_picked
-    )
+    held, beside, own_picked = stage(held, beside, own_picked)
 
     last = (place & 1) != 0
     for m in others:
         beside[m] = swapped(held[m], "dp", 1)
-    other_parts.append(swapped(own_parts[1], "dp", span))
     own_got = swapped(own_picked[-1], "expert", half)
-    tokens = {0: in_order(held[0], beside[0], last).reshape(group_tok, width)}
-    tokens[1] = swapped(tokens[0], "expert", 1)
-    tokens, beside, own_got, own_picked, own_parts, other_parts = stage(
-        tokens, beside, own_got, own_picked, own_parts, other_parts
-    )
-
-    for m in others:
+    tokens = {}
+    for m in [0] + others:
         tokens[m] = in_order(held[m], beside[m], last).reshape(group_tok, width)
         tokens[m + 1] = swapped(tokens[m], "expert", 1)
     tokens = [tokens[m] for m in each]
-    other_parts.append(swapped(own_parts[2], "dp", span))
     own_rows = spread(own_picked, own_got, experts)
-    tokens, own_rows, other_parts = stage(tokens, own_rows, other_parts)
-
-    other_picked = picked_rows(other_parts, named, group_tok, experts, False)
+    tokens, own_rows, other_twice = stage(tokens, own_rows, other_twice)
+
+    other_picked = picked_rows([other_twice], named, group_tok, experts, 1 - upper)
     other_got = swapped(other_picked[-1], "expert", half)
 
     def shard_terms(hidden_rows):
@@ -364,21 +334,20 @@
     derivs = [deriv_of(tokens[m], weight) for m in each]
 
     other_got, other_picked, derivs = stage(other_got, other_picked, derivs)
-    own_grads = [swapped(own_terms[m], "dp", m) for m in range(span)]
     other_rows = spread(other_picked, other_got, experts)
-    other_rows, own_grads = stage(other_rows, own_grads)
     other_terms = shard_terms(other_rows)
 
     parts = 2 if cols % 256 == 0 else 1
     pieces = jnp.split(down_weight.reshape(shards, rows, cols), parts, axis=2)
     weights = []
     for part, piece in enumerate(pieces):
-        begun = [other_parts] if part == 0 else [weights[-1], other_terms]
+        begun = [other_twice] if part == 0 else [weights[-1], other_terms]
         weights.append(
             lax.all_to_all(after(piece, *begun), "dp", split_axis=0, concat_axis=0, tiled=True)
         )
 
     other_terms = after(other_terms, weights[0])
+    own_grads = [swapped(own_terms[m], "dp", m) for m in range(span)]
     other_grads = [swapped(other_terms[m], "dp", m) for m in range(span)]
 
     gate_saved, up_saved, _ = stage(gate_saved, up_saved, derivs)

time: 398 us -> 397 us (level)
  Pallas kernels: 106 us -> 102 us
    all_to_all x0 -> x1, waiting for transfers between devices: none -> 32.3 us  [body(): lax.all_to_all(twice, 'dp', split_axis=0, concat_axis=0, tiled=True, axis...]
    ppermute x26 -> x23, waiting for transfers between devices: 208 us -> 177 us  [swapped(): return lax.ppermute(array, axis, [(i, i ^ mask) for i in range(size)])]
    all_to_all x0 -> x1, starting transfers between devices: none -> 5.61 us  [body(): lax.all_to_all(twice, 'dp', split_axis=0, concat_axis=0, tiled=True, axis...]
    ppermute x26 -> x23, starting transfers between devices: 25.5 us -> 20.9 us  [swapped(): return lax.ppermute(array, axis, [(i, i ^ mask) for i in range(size)])]
  transfers between devices with their start and end apart: 28 -> 26, of which waited for: 15 -> 13; matrix products, arithmetic and copies ran while one was open for 9% -> 9% of each run, Pallas kernels for 21% -> 22%
where the time goes in v13:
time: 397 us; the launch traced here: 396 us
  waiting for transfers between devices  209 us (53%)
  Pallas kernels  102 us (26%)
  starting transfers between devices  40.9 us (10%)
  local copies, waits for them, and re-layouts  26.1 us (7%)
  other arithmetic  17 us (4%)
    ppermute x23, waiting for transfers between devices, swapped(): return lax.ppermute(array, axis, [(i, i ^ mask) for i in range(size)])  177 us
    all_to_all x1, waiting for transfers between devices, body(): lax.all_to_all(twice, 'dp', split_axis=0, concat_axis=0, tiled=True, axis...  32.3 us
    pallas_call x4, Pallas kernels, deriv_of(): pl.pallas_call(deriv_kernel, grid=(cols // wide,), in_specs=[pl.BlockSpec...  31.6 us
    pallas_call x2, Pallas kernels, terms(): pl.pallas_call(functools.partial(term_kernel, count), grid_spec=pltpu.Pre...  24.4 us
    pallas_call x4, Pallas kernels, update(): pl.pallas_call(functools.partial(update_kernel, count), grid_spec=pltpu.P...  23 us
    ppermute x23, starting transfers between devices, swapped(): return lax.ppermute(array, axis, [(i, i ^ mask) for i in range(size)])  20.9 us
    convert_element_type x1, other arithmetic, body(): d_up = (deriv * gate * sigma).astype(jnp.bfloat16)  16.3 us
    all_to_all x2, starting transfers between devices, body(): lax.all_to_all(after(piece, *begun), 'dp', split_axis=0, concat_axis=0, t...  14.3 us
  transfers between devices with their start and end apart: 26, of which 13 were waited for; matrix products, arithmetic and copies ran while one was open for 9% of the time, Pallas kernels for 22%

profile of v13, /device:TPU:8, one launch (start us, length us, event | category | flops | bytes accessed | tf_op | source)
XLA Modules:
  0.0 395.5 jit_solution(16610497554954148777)
XLA Ops:
  0.6 2.7 collective-permute-start.1
  3.3 0.4 collective-permute-start
  3.7 0.5 collective-permute-start.2
  4.2 0.7 broadcast_xor_fusion
  5.0 0.8 reshape_reshape.10.named_ref
  5.8 4.1 %reshape.55.gate_ref = bf16[1024,1024]{1,0:T(8,128)(2,1)} reshape(bf16[512,2,1024]{2,1,0:T(2,128)(2,1)} %param.7) | data formatting | bytes 4194304 | tf_op jit(solution)/shard_map/reshape | solution.py:285
  9.9 2.2 reshape.56.up_ref
  12.1 7.0 %hidden_rows.2 = (bf16[2,1024,1024]{2,1,0:T(8,128)(2,1)}, bf16[1,512,1024]{2,1,0:T(8,128)(2,1)}, bf16[1,512,1024]{2,1,0:T(8,128)(2,1)}, bf16[2,512,1024]{2,1,0:T(8,128)(2,1)}) custom-call(s32[1]{0:T(128)} %bitcast.3.place_ref, bf16[1024,1024]{1,0:T(8,128)(2,1)} %reshape.55.gate_ref, bf16[1024,1024]{1,0:T(8,128)(2,1)} %reshape.56.up_ref, ...), custom_call_target="tpu_custom_call" | custom-call | flops 1024 | bytes 1024 | tf_op jit(solution)/shard_map/hidden_rows/pallas_call | solution.py:126
  19.1 2.1 collective-permute-done.1.refs_2_
  21.3 1.1 collective-permute-done.refs_1_
  22.4 14.7 %collective-permute-done.2.refs_3_ = bf16[64,3072]{1,0:T(8,128)(2,1)S(1)} collective-permute-done((bf16[64,3072]{1,0:T(8,128)(2,1)}, bf16[64,3072]{1,0:T(8,128)(2,1)S(1)}, u32[]{:S(2)}, u32[]{:S(2)}) %collective-permute-start.2) | collective-permute-done | bytes 393248 | tf_op jit(solution)/shard_map/ppermute | solution.py:23
  37.2 0.8 copy-done.11
  37.9 2.6 placed_blocks.1.mine_ref
  40.5 1.5 collective-permute-start.4
  42.0 1.5 collective-permute-start.3
  43.5 33.5 %collective-permute-done.4.theirs_ref = bf16[4,64,3072]{2,1,0:T(8,128)(2,1)S(1)} collective-permute-done((bf16[4,64,3072]{2,1,0:T(8,128)(2,1)}, bf16[4,64,3072]{2,1,0:T(8,128)(2,1)S(1)}, u32[]{:S(2)}, u32[]{:S(2)}) %collective-permute-start.4) | collective-permute-done | bytes 1572896 | tf_op jit(solution)/shard_map/ppermute | solution.py:23
  77.0 1.3 collective-permute-done.3.mine_ref
  78.4 0.5 collective-permute-start.6
  78.9 5.6 %all-to-all-start = ((bf16[2,1024,1024]{2,1,0:T(8,128)(2,1)}), bf16[2,1024,1024]{2,1,0:T(8,128)(2,1)}, u32[]{:S(2)}, u32[]{:S(2)}) async-start(bf16[2,1024,1024]{2,1,0:T(8,128)(2,1)} %get-tuple-element.87), calls=%async_computation | async-start | bytes 8388608 | tf_op jit(solution)/shard_map/all_to_all | solution.py:294
  84.5 1.6 collective-permute-start.9
  86.1 4.2 %side_by_side.2 = bf16[4,2,64,3072]{3,2,1,0:T(8,128)(2,1)} custom-call(s32[1]{0:T(128)} %bitcast.1.place_ref, bf16[4,64,3072]{2,1,0:T(8,128)(2,1)} %placed_blocks.1.mine_ref, bf16[4,64,3072]{2,1,0:T(8,128)(2,1)} %copy-done.8), custom_call_target="tpu_custom_call" | custom-call | flops 1024 | bytes 1024 | tf_op jit(solution)/shard_map/side_by_side/pallas_call | solution.py:42
  90.2 23.6 %collective-permute-done.6.theirs_ref = bf16[4,64,3072]{2,1,0:T(8,128)(2,1)} collective-permute-done((bf16[4,64,3072]{2,1,0:T(8,128)(2,1)}, bf16[4,64,3072]{2,1,0:T(8,128)(2,1)}, u32[]{:S(2)}, u32[]{:S(2)}) %collective-permute-start.6) | collective-permute-done | bytes 1572896 | tf_op jit(solution)/shard_map/ppermute | solution.py:23
  113.8 4.2 %side_by_side.3 = bf16[4,2,64,3072]{3,2,1,0:T(8,128)(2,1)} custom-call(s32[1]{0:T(128)} %bitcast.1.place_ref, bf16[4,64,3072]{2,1,0:T(8,128)(2,1)} %collective-permute-done.3.mine_ref, bf16[4,64,3072]{2,1,0:T(8,128)(2,1)} %collective-permute-done.6.theirs_ref), custom_call_target="tpu_custom_call" | custom-call | flops 1024 | bytes 1024 | tf_op jit(solution)/shard_map/side_by_side/pallas_call | solution.py:42
  118.1 0.5 collective-permute-start.8
  118.6 12.5 %collective-permute-done.9 = bf16[2,512,1024]{2,1,0:T(8,128)(2,1)} collective-permute-done((bf16[2,512,1024]{2,1,0:T(8,128)(2,1)}, bf16[2,512,1024]{2,1,0:T(8,128)(2,1)}, u32[]{:S(2)}, u32[]{:S(2)}) %collective-permute-start.9) | collective-permute-done | bytes 2097184 | tf_op jit(solution)/shard_map/ppermute | solution.py:23
  131.1 3.0 fusion.10
  134.1 6.0 %fusion.8 = (bf16[8,384,512]{2,1,0:T(8,128)(2,1)}, bf16[8,384,512]{2,1,0:T(8,128)(2,1)}) fusion(bf16[8,384,1024]{2,1,0:T(8,128)(2,1)} %bitcast.20), kind=kLoop, calls=%fused_computation.19 | loop fusion | bytes 12582912 | tf_op jit(solution)/shard_map/split | solution.py:341
  140.2 32.3 %all-to-all-done.hidden_ref = bf16[2,1024,1024]{2,1,0:T(8,128)(2,1)} async-done(((bf16[2,1024,1024]{2,1,0:T(8,128)(2,1)}), bf16[2,1024,1024]{2,1,0:T(8,128)(2,1)}, u32[]{:S(2)}, u32[]{:S(2)}) %all-to-all-start) | async-done | bytes 4194336 | tf_op jit(solution)/shard_map/all_to_all | solution.py:294
  172.4 1.7 copy-done.2
  174.1 9.2 %all-to-all-start.1 = ((bf16[8,384,512]{2,1,0:T(8,128)(2,1)}), bf16[8,384,512]{2,1,0:T(8,128)(2,1)S(1)}, u32[]{:S(2)}, u32[]{:S(2)}) async-start(bf16[8,384,512]{2,1,0:T(8,128)(2,1)} %get-tuple-element.111), calls=%async_computation.1 | async-start | bytes 6291456 | tf_op jit(solution)/shard_map/all_to_all | solution.py:346
  183.3 4.7 %hidden_rows.3 = (bf16[1,512,1024]{2,1,0:T(8,128)(2,1)}, bf16[1,512,1024]{2,1,0:T(8,128)(2,1)}, bf16[2,512,1024]{2,1,0:T(8,128)(2,1)}) custom-call(s32[1]{0:T(128)} %bitcast.place_ref, bf16[2,1024,1024]{2,1,0:T(8,128)(2,1)} %all-to-all-done.hidden_ref, s32[4,256]{1,0:T(4,128)} %reshape_reshape.10.named_ref), custom_call_target="tpu_custom_call" | custom-call | flops 1024 | bytes 1024 | tf_op jit(solution)/shard_map/hidden_rows/pallas_call | solution.py:126
  187.9 1.5 collective-permute-start.11
  189.4 12.2 %group_terms.2 = (bf16[384,1024]{1,0:T(8,128)(2,1)}, bf16[384,1024]{1,0:T(8,128)(2,1)}, bf16[384,1024]{1,0:T(8,128)(2,1)}, bf16[384,1024]{1,0:T(8,128)(2,1)}) custom-call(s32[1]{0:T(128)} %bitcast.11.place_ref, bf16[512,3072]{1,0:T(8,128)(2,1)} %bitcast.26, bf16[512,3072]{1,0:T(8,128)(2,1)} %copy-done.2, bf16[512,3072]{1,0:T(8,128)(2,1)} %bitcast.30, ...), custom_call_target="tpu_custom_call" | custom-call | flops 1024 | bytes 1024 | tf_op jit(solution)/shard_map/group_terms/pallas_call | solution.py:178
  201.6 7.9 %hidden_deriv.7 = f32[512,1024]{1,0:T(8,128)} custom-call(bf16[512,3072]{1,0:T(8,128)(2,1)} %collective-permute-done.7.refs_3_.tokens_ref, bf16[3072,1024]{1,0:T(8,128)(2,1)} %bitcast.21), custom_call_target="tpu_custom_call" | custom-call | flops 1024 | bytes 1024 | tf_op jit(solution)/shard_map/hidden_deriv/pallas_call | solution.py:207
  209.5 7.9 %hidden_deriv.6 = f32[512,1024]{1,0:T(8,128)} custom-call(bf16[512,3072]{1,0:T(8,128)(2,1)} %bitcast.31, bf16[3072,1024]{1,0:T(8,128)(2,1)} %bitcast.22), custom_call_target="tpu_custom_call" | custom-call | flops 1024 | bytes 1024 | tf_op jit(solution)/shard_map/hidden_deriv/pallas_call | solution.py:207
  217.4 7.9 %hidden_deriv.5 = f32[512,1024]{1,0:T(8,128)} custom-call(bf16[512,3072]{1,0:T(8,128)(2,1)} %copy-done.2, bf16[3072,1024]{1,0:T(8,128)(2,1)} %bitcast.23), custom_call_target="tpu_custom_call" | custom-call | flops 1024 | bytes 1024 | tf_op jit(solution)/shard_map/hidden_deriv/pallas_call | solution.py:207
  225.2 8.0 %hidden_deriv.4 = f32[512,1024]{1,0:T(8,128)} custom-call(bf16[512,3072]{1,0:T(8,128)(2,1)} %bitcast.27, bf16[3072,1024]{1,0:T(8,128)(2,1)} %bitcast.24), custom_call_target="tpu_custom_call" | custom-call | flops 1024 | bytes 1024 | tf_op jit(solution)/shard_map/hidden_deriv/pallas_call | solution.py:207
  233.2 1.9 collective-permute-done.11
  235.1 1.5 collective-permute-start.13
  236.6 0.3 collective-permute-start.14
  237.1 1.5 fusion.9
  238.6 0.3 collective-permute-start.16
  239.0 4.9 %collective-permute-done.15 = bf16[1,512,1024]{2,1,0:T(8,128)(2,1)} collective-permute-done((bf16[1,512,1024]{2,1,0:T(8,128)(2,1)S(1)}, bf16[1,512,1024]{2,1,0:T(8,128)(2,1)}, u32[]{:S(2)}, u32[]{:S(2)}) %collective-permute-start.15) | collective-permute-done | bytes 1048608 | tf_op jit(solution)/shard_map/ppermute | solution.py:23
  243.9 1.5 collective-permute-start.20
  245.6 0.2 copy.23
  246.2 0.6 collective-permute-start.21
  246.8 12.2 %group_terms.3 = (bf16[384,1024]{1,0:T(8,128)(2,1)}, bf16[384,1024]{1,0:T(8,128)(2,1)}, bf16[384,1024]{1,0:T(8,128)(2,1)}, bf16[384,1024]{1,0:T(8,128)(2,1)}) custom-call(s32[1]{0:T(128)} %bitcast.11.place_ref, bf16[512,3072]{1,0:T(8,128)(2,1)} %bitcast.28, bf16[512,3072]{1,0:T(8,128)(2,1)} %copy-done.2, bf16[512,3072]{1,0:T(8,128)(2,1)} %bitcast.32, ...), custom_call_target="tpu_custom_call" | custom-call | flops 1024 | bytes 1024 | tf_op jit(solution)/shard_map/group_terms/pallas_call | solution.py:178
  259.1 1.6 copy-done.1
  260.7 5.1 %all-to-all-start.2 = ((bf16[8,384,512]{2,1,0:T(8,128)(2,1)}), bf16[8,384,512]{2,1,0:T(8,128)(2,1)S(1)}, u32[]{:S(2)}, u32[]{:S(2)}) async-start(bf16[8,384,512]{2,1,0:T(8,128)(2,1)} %get-tuple-element.119), calls=%async_computation.2 | async-start | bytes 6291456 | tf_op jit(solution)/shard_map/all_to_all | solution.py:346
  265.8 1.5 collective-permute-start.22
  267.3 16.0 %collective-permute-done.12 = f32[512,1024]{1,0:T(8,128)} collective-permute-done((f32[512,1024]{1,0:T(8,128)}, f32[512,1024]{1,0:T(8,128)}, u32[]{:S(2)}, u32[]{:S(2)}) %collective-permute-start.12) | collective-permute-done | bytes 2097184 | tf_op jit(solution)/shard_map/ppermute | solution.py:23
  283.3 1.5 collective-permute-start.17
  284.8 43.5 %collective-permute-done.13 = f32[512,1024]{1,0:T(8,128)} collective-permute-done((f32[512,1024]{1,0:T(8,128)}, f32[512,1024]{1,0:T(8,128)}, u32[]{:S(2)}, u32[]{:S(2)}) %collective-permute-start.13) | collective-permute-done | bytes 2097184 | tf_op jit(solution)/shard_map/ppermute | solution.py:23
  328.3 0.4 collective-permute-start.18
  328.7 2.5 collective-permute-start.19
  331.2 16.3 %fusion.7 = (bf16[512,2,1024]{2,1,0:T(2,128)(2,1)}, bf16[512,2,1024]{2,1,0:T(2,128)(2,1)}) fusion(bf16[512,2,1024]{2,1,0:T(2,128)(2,1)} %param.7, pred[512,2]{1,0:T(8,128)(4,1)S(1)} %copy.25, pred[512,2]{1,0:T(8,128)(4,1)S(1)} %copy.24, pred[512,2]{1,0:T(8,128)(4,1)S(1)} %copy.23, pred[512,2]{1,0:T(8,128)(4,1)S(1)} %copy.21, f32[512,1024]{1,0:T(8,128)} %hidden_deriv.4, ...), kind=kLoop, calls=%fused_computation.10 | loop fusion | flops 19922944 | bytes 16781312 | tf_op jit(solution)/shard_map/convert_element_type | solution.py:361
  347.5 1.0 copy-done.4
  348.5 5.7 %lion_step.4 = (f32[1,384,8192]{2,1,0:T(8,128)}, bf16[1,384,8192]{2,1,0:T(8,128)(2,1)}) custom-call(s32[1]{0:T(128)} %bitcast.11.place_ref, bf16[8,384,512]{2,1,0:T(8,128)(2,1)} %copy-done.1, bf16[1,384,8192]{2,1,0:T(8,128)(2,1)} %momentum_ref.7, bf16[384,1024]{1,0:T(8,128)(2,1)} %get-tuple-element.124.refs_0_, ...), custom_call_target="tpu_custom_call" | custom-call | flops 1024 | bytes 1024 | tf_op jit(solution)/shard_map/lion_step/pallas_call | solution.py:246
  354.3 21.5 %collective-permute-done.19.refs_3_ = bf16[384,1024]{1,0:T(8,128)(2,1)S(1)} collective-permute-done((bf16[384,1024]{1,0:T(8,128)(2,1)}, bf16[384,1024]{1,0:T(8,128)(2,1)S(1)}, u32[]{:S(2)}, u32[]{:S(2)}) %collective-permute-start.19) | collective-permute-done | bytes 786464 | tf_op jit(solution)/shard_map/ppermute | solution.py:23
  375.8 0.9 copy-done.7
  376.7 5.7 %lion_step.5 = (f32[1,384,8192]{2,1,0:T(8,128)}, bf16[1,384,8192]{2,1,0:T(8,128)(2,1)}) custom-call(s32[1]{0:T(128)} %bitcast.12.place_ref, bf16[8,384,512]{2,1,0:T(8,128)(2,1)} %copy-done.1, bf16[1,384,8192]{2,1,0:T(8,128)(2,1)} %momentum_ref.7, bf16[384,1024]{1,0:T(8,128)(2,1)} %get-tuple-element.120.refs_0_, ...), custom_call_target="tpu_custom_call", output_to_operand_aliasing={{0}: (7, {}), {1}: (8, {})} | custom-call | flops 1024 | bytes 1024 | tf_op jit(solution)/shard_map/lion_step/pallas_call | solution.py:246
  382.4 1.6 copy-done
  384.0 5.7 %lion_step.6 = (f32[1,384,8192]{2,1,0:T(8,128)}, bf16[1,384,8192]{2,1,0:T(8,128)(2,1)}) custom-call(s32[1]{0:T(128)} %bitcast.11.place_ref, bf16[8,384,512]{2,1,0:T(8,128)(2,1)} %copy-done, bf16[1,384,8192]{2,1,0:T(8,128)(2,1)} %momentum_ref.7, bf16[384,1024]{1,0:T(8,128)(2,1)} %get-tuple-element.124.refs_0_, ...), custom_call_target="tpu_custom_call", output_to_operand_aliasing={{0}: (7, {}), {1}: (8, {})} | custom-call | flops 1024 | bytes 1024 | tf_op jit(solution)/shard_map/lion_step/pallas_call | solution.py:246
  389.8 5.8 %lion_step.7 = (f32[1,384,8192]{2,1,0:T(8,128)}, bf16[1,384,8192]{2,1,0:T(8,128)(2,1)}) custom-call(s32[1]{0:T(128)} %bitcast.12.place_ref, bf16[8,384,512]{2,1,0:T(8,128)(2,1)} %copy-done, bf16[1,384,8192]{2,1,0:T(8,128)(2,1)} %momentum_ref.7, bf16[384,1024]{1,0:T(8,128)(2,1)} %get-tuple-element.120.refs_0_, ...), custom_call_target="tpu_custom_call", output_to_operand_aliasing={{0}: (7, {}), {1}: (8, {})} | custom-call | flops 1024 | bytes 1024 | tf_op jit(solution)/shard_map/lion_step/pallas_call | solution.py:246
  (45 shorter events, 1.0 us)
Async XLA Ops:
  0.6 9.3 %copy-start.3 = (bf16[512,2,1024]{2,1,0:T(2,128)(2,1)S(1)}, bf16[512,2,1024]{2,1,0:T(2,128)(2,1)}, u32[]{:S(2)}) copy-start(bf16[512,2,1024]{2,1,0:T(2,128)(2,1)} %param.8) | copy-start | bytes 6291460
  0.6 20.6 %collective-permute-start.1 = (bf16[64,3072]{1,0:T(8,128)(2,1)}, bf16[64,3072]{1,0:T(8,128)(2,1)S(1)}, u32[]{:S(2)}, u32[]{:S(2)}) collective-permute-start(bf16[64,3072]{1,0:T(8,128)(2,1)} %refs_0_), channel_id=1, source_target_pairs={{0,4},{1,5},{2,6},{3,7},{4,0},{5,1},{6,2},{7,3},{8,12},{9,13},{10,... | collective-permute-start | bytes 1179656 | tf_op jit(solution)/shard_map/ppermute | solution.py:23
  3.3 19.1 %collective-permute-start = (bf16[64,3072]{1,0:T(8,128)(2,1)}, bf16[64,3072]{1,0:T(8,128)(2,1)S(1)}, u32[]{:S(2)}, u32[]{:S(2)}) collective-permute-start(bf16[64,3072]{1,0:T(8,128)(2,1)} %refs_0_), channel_id=1, source_target_pairs={{0,2},{1,3},{2,0},{3,1},{4,6},{5,7},{6,4},{7,5},{8,10},{9,11},{10,... | collective-permute-start | bytes 1179656 | tf_op jit(solution)/shard_map/ppermute | solution.py:23
  3.7 33.4 %collective-permute-start.2 = (bf16[64,3072]{1,0:T(8,128)(2,1)}, bf16[64,3072]{1,0:T(8,128)(2,1)S(1)}, u32[]{:S(2)}, u32[]{:S(2)}) collective-permute-start(bf16[64,3072]{1,0:T(8,128)(2,1)} %refs_0_), channel_id=1, source_target_pairs={{0,6},{1,7},{2,4},{3,5},{4,2},{5,3},{6,0},{7,1},{8,14},{9,15},{10,... | collective-permute-start | bytes 1179656 | tf_op jit(solution)/shard_map/ppermute | solution.py:23
  21.3 15.9 %copy-start.9 = (bf16[64,3072]{1,0:T(8,128)(2,1)}, bf16[64,3072]{1,0:T(8,128)(2,1)S(1)}, u32[]{:S(2)}) copy-start(bf16[64,3072]{1,0:T(8,128)(2,1)S(1)} %collective-permute-done.1.refs_2_) | copy-start | bytes 1179652
  22.4 14.8 %copy-start.10 = (bf16[64,3072]{1,0:T(8,128)(2,1)}, bf16[64,3072]{1,0:T(8,128)(2,1)S(1)}, u32[]{:S(2)}) copy-start(bf16[64,3072]{1,0:T(8,128)(2,1)S(1)} %collective-permute-done.refs_1_) | copy-start | bytes 1179652
  37.2 0.8 copy-start.11
  40.5 36.5 %collective-permute-start.4 = (bf16[4,64,3072]{2,1,0:T(8,128)(2,1)}, bf16[4,64,3072]{2,1,0:T(8,128)(2,1)S(1)}, u32[]{:S(2)}, u32[]{:S(2)}) collective-permute-start(bf16[4,64,3072]{2,1,0:T(8,128)(2,1)} %placed_blocks.1.mine_ref), channel_id=1, source_target_pairs={{0,1},{1,0},{2,3},{3,2},{4,5},{5,4},{6,7},{7,6},{8,9},{9,8},{10,11... | collective-permute-start | bytes 4718600 | tf_op jit(solution)/shard_map/ppermute | solution.py:23
  42.0 36.4 %collective-permute-start.3 = (bf16[4,64,3072]{2,1,0:T(8,128)(2,1)}, bf16[4,64,3072]{2,1,0:T(8,128)(2,1)}, u32[]{:S(2)}, u32[]{:S(2)}) collective-permute-start(bf16[4,64,3072]{2,1,0:T(8,128)(2,1)} %placed_blocks.1.mine_ref), channel_id=1, source_target_pairs={{0,16},{8,24},{16,0},{24,8},{1,17},{9,25},{17,1},{25,9},{2,18},{10... | collective-permute-start | bytes 4718600 | tf_op jit(solution)/shard_map/ppermute | solution.py:23
  77.0 1.9 copy-start.8
  78.4 35.5 %collective-permute-start.6 = (bf16[4,64,3072]{2,1,0:T(8,128)(2,1)}, bf16[4,64,3072]{2,1,0:T(8,128)(2,1)}, u32[]{:S(2)}, u32[]{:S(2)}) collective-permute-start(bf16[4,64,3072]{2,1,0:T(8,128)(2,1)} %collective-permute-done.3.mine_ref), channel_id=1, source_target_pairs={{0,1},{1,0},{2,3},{3,2},{4,5},{5,4},{6,7},{7,6},{8,9},{9,8},{10,11... | collective-permute-start | bytes 4718600 | tf_op jit(solution)/shard_map/ppermute | solution.py:23
  78.9 93.5 %all-to-all-start = ((bf16[2,1024,1024]{2,1,0:T(8,128)(2,1)}), bf16[2,1024,1024]{2,1,0:T(8,128)(2,1)}, u32[]{:S(2)}, u32[]{:S(2)}) async-start(bf16[2,1024,1024]{2,1,0:T(8,128)(2,1)} %get-tuple-element.87), calls=%async_computation | async-start | bytes 8388608 | tf_op jit(solution)/shard_map/all_to_all | solution.py:294
  84.5 46.6 %collective-permute-start.9 = (bf16[2,512,1024]{2,1,0:T(8,128)(2,1)}, bf16[2,512,1024]{2,1,0:T(8,128)(2,1)}, u32[]{:S(2)}, u32[]{:S(2)}) collective-permute-start(bf16[2,512,1024]{2,1,0:T(8,128)(2,1)} %get-tuple-element.86), channel_id=1, source_target_pairs={{0,16},{8,24},{16,0},{24,8},{1,17},{9,25},{17,1},{25,9},{2,18},{10... | collective-permute-start | bytes 6291464 | tf_op jit(solution)/shard_map/ppermute | solution.py:23
  90.2 82.2 %collective-permute-start.5 = (bf16[512,3072]{1,0:T(8,128)(2,1)}, bf16[512,3072]{1,0:T(8,128)(2,1)S(1)}, u32[]{:S(2)}, u32[]{:S(2)}) collective-permute-start(bf16[512,3072]{1,0:T(8,128)(2,1)} %bitcast.25), channel_id=1, source_target_pairs={{0,8},{8,0},{16,24},{24,16},{1,9},{9,1},{17,25},{25,17},{2,10},{10... | collective-permute-start | bytes 9437192 | tf_op jit(solution)/shard_map/ppermute | solution.py:23
  118.0 54.4 %collective-permute-start.7 = (bf16[512,3072]{1,0:T(8,128)(2,1)}, bf16[512,3072]{1,0:T(8,128)(2,1)}, u32[]{:S(2)}, u32[]{:S(2)}) collective-permute-start(bf16[512,3072]{1,0:T(8,128)(2,1)} %bitcast.29), channel_id=1, source_target_pairs={{0,8},{8,0},{16,24},{24,16},{1,9},{9,1},{17,25},{25,17},{2,10},{10... | collective-permute-start | bytes 9437192 | tf_op jit(solution)/shard_map/ppermute | solution.py:23
  118.1 22.1 %collective-permute-start.8 = (bf16[1,512,1024]{2,1,0:T(8,128)(2,1)}, bf16[1,512,1024]{2,1,0:T(8,128)(2,1)}, u32[]{:S(2)}, u32[]{:S(2)}) collective-permute-start(bf16[1,512,1024]{2,1,0:T(8,128)(2,1)} %get-tuple-element.85), channel_id=1, source_target_pairs={{0,8},{8,0},{16,24},{24,16},{1,9},{9,1},{17,25},{25,17},{2,10},{10... | collective-permute-start | bytes 3145736 | tf_op jit(solution)/shard_map/ppermute | solution.py:23
  134.1 38.3 %collective-permute-start.10 = (bf16[1,512,1024]{2,1,0:T(8,128)(2,1)}, bf16[1,512,1024]{2,1,0:T(8,128)(2,1)}, u32[]{:S(2)}, u32[]{:S(2)}) collective-permute-start(bf16[1,512,1024]{2,1,0:T(8,128)(2,1)} %get-tuple-element.142), channel_id=1, source_target_pairs={{0,8},{8,0},{16,24},{24,16},{1,9},{9,1},{17,25},{25,17},{2,10},{10... | collective-permute-start | bytes 3145736 | tf_op jit(solution)/shard_map/ppermute | solution.py:23
  172.4 1.7 copy-start.2
  174.1 85.0 %all-to-all-start.1 = ((bf16[8,384,512]{2,1,0:T(8,128)(2,1)}), bf16[8,384,512]{2,1,0:T(8,128)(2,1)S(1)}, u32[]{:S(2)}, u32[]{:S(2)}) async-start(bf16[8,384,512]{2,1,0:T(8,128)(2,1)} %get-tuple-element.111), calls=%async_computation.1 | async-start | bytes 6291456 | tf_op jit(solution)/shard_map/all_to_all | solution.py:346
  187.9 47.2 %collective-permute-start.11 = (bf16[2,512,1024]{2,1,0:T(8,128)(2,1)}, bf16[2,512,1024]{2,1,0:T(8,128)(2,1)S(1)}, u32[]{:S(2)}, u32[]{:S(2)}) collective-permute-start(bf16[2,512,1024]{2,1,0:T(8,128)(2,1)} %get-tuple-element.89), channel_id=1, source_target_pairs={{0,16},{8,24},{16,0},{24,8},{1,17},{9,25},{17,1},{25,9},{2,18},{10... | collective-permute-start | bytes 6291464 | tf_op jit(solution)/shard_map/ppermute | solution.py:23
  225.2 11.7 %copy-start.13 = (bf16[1,512,1024]{2,1,0:T(8,128)(2,1)S(1)}, bf16[1,512,1024]{2,1,0:T(8,128)(2,1)}, u32[]{:S(2)}) copy-start(bf16[1,512,1024]{2,1,0:T(8,128)(2,1)} %get-tuple-element.113) | copy-start | bytes 3145732
  233.2 12.2 %copy-start.12 = (s32[512,2]{0,1:T(2,128)S(1)}, s32[512,2]{0,1:T(2,128)}, u32[]{:S(2)}) copy-start(s32[512,2]{0,1:T(2,128)} %param.9) | copy-start | bytes 12292
  235.1 48.2 %collective-permute-start.12 = (f32[512,1024]{1,0:T(8,128)}, f32[512,1024]{1,0:T(8,128)}, u32[]{:S(2)}, u32[]{:S(2)}) collective-permute-start(f32[512,1024]{1,0:T(8,128)} %hidden_deriv.7), channel_id=1, source_target_pairs={{0,24},{8,16},{16,8},{24,0},{1,25},{9,17},{17,9},{25,1},{2,26},{10... | collective-permute-start | bytes 6291464 | tf_op jit(solution)/shard_map/ppermute | solution.py:23
  235.1 93.2 %collective-permute-start.13 = (f32[512,1024]{1,0:T(8,128)}, f32[512,1024]{1,0:T(8,128)}, u32[]{:S(2)}, u32[]{:S(2)}) collective-permute-start(f32[512,1024]{1,0:T(8,128)} %hidden_deriv.6), channel_id=1, source_target_pairs={{0,16},{8,24},{16,0},{24,8},{1,17},{9,25},{17,1},{25,9},{2,18},{10... | collective-permute-start | bytes 6291464 | tf_op jit(solution)/shard_map/ppermute | solution.py:23
  236.6 92.1 %collective-permute-start.14 = (f32[512,1024]{1,0:T(8,128)}, f32[512,1024]{1,0:T(8,128)}, u32[]{:S(2)}, u32[]{:S(2)}) collective-permute-start(f32[512,1024]{1,0:T(8,128)} %hidden_deriv.5), channel_id=1, source_target_pairs={{0,8},{8,0},{16,24},{24,16},{1,9},{9,1},{17,25},{25,17},{2,10},{10... | collective-permute-start | bytes 6291464 | tf_op jit(solution)/shard_map/ppermute | solution.py:23
  237.0 7.0 %collective-permute-start.15 = (bf16[1,512,1024]{2,1,0:T(8,128)(2,1)S(1)}, bf16[1,512,1024]{2,1,0:T(8,128)(2,1)}, u32[]{:S(2)}, u32[]{:S(2)}) collective-permute-start(bf16[1,512,1024]{2,1,0:T(8,128)(2,1)S(1)} %copy-done.13), channel_id=1, source_target_pairs={{0,8},{8,0},{16,24},{24,16},{1,9},{9,1},{17,25},{25,17},{2,10},{10... | collective-permute-start | bytes 3145736 | tf_op jit(solution)/shard_map/ppermute | solution.py:23
  238.6 7.6 %collective-permute-start.16 = (bf16[1,512,1024]{2,1,0:T(8,128)(2,1)}, bf16[1,512,1024]{2,1,0:T(8,128)(2,1)}, u32[]{:S(2)}, u32[]{:S(2)}) collective-permute-start(bf16[1,512,1024]{2,1,0:T(8,128)(2,1)} %get-tuple-element.140), channel_id=1, source_target_pairs={{0,8},{8,0},{16,24},{24,16},{1,9},{9,1},{17,25},{25,17},{2,10},{10... | collective-permute-start | bytes 3145736 | tf_op jit(solution)/shard_map/ppermute | solution.py:23
  243.9 21.9 %collective-permute-start.20 = (bf16[384,1024]{1,0:T(8,128)(2,1)}, bf16[384,1024]{1,0:T(8,128)(2,1)}, u32[]{:S(2)}, u32[]{:S(2)}) collective-permute-start(bf16[384,1024]{1,0:T(8,128)(2,1)} %get-tuple-element.125), channel_id=1, source_target_pairs={{0,1},{1,0},{2,3},{3,2},{4,5},{5,4},{6,7},{7,6},{8,9},{9,8},{10,11... | collective-permute-start | bytes 2359304 | tf_op jit(solution)/shard_map/ppermute | solution.py:23
  246.2 101.3 %collective-permute-start.21 = (bf16[384,1024]{1,0:T(8,128)(2,1)}, bf16[384,1024]{1,0:T(8,128)(2,1)}, u32[]{:S(2)}, u32[]{:S(2)}) collective-permute-start(bf16[384,1024]{1,0:T(8,128)(2,1)} %get-tuple-element.126), channel_id=1, source_target_pairs={{0,2},{1,3},{2,0},{3,1},{4,6},{5,7},{6,4},{7,5},{8,10},{9,11},{10,... | collective-permute-start | bytes 2359304 | tf_op jit(solution)/shard_map/ppermute | solution.py:23
  259.1 1.6 copy-start.1
  260.7 121.7 %all-to-all-start.2 = ((bf16[8,384,512]{2,1,0:T(8,128)(2,1)}), bf16[8,384,512]{2,1,0:T(8,128)(2,1)S(1)}, u32[]{:S(2)}, u32[]{:S(2)}) async-start(bf16[8,384,512]{2,1,0:T(8,128)(2,1)} %get-tuple-element.119), calls=%async_computation.2 | async-start | bytes 6291456 | tf_op jit(solution)/shard_map/all_to_all | solution.py:346
  265.8 81.7 %collective-permute-start.22 = (bf16[384,1024]{1,0:T(8,128)(2,1)}, bf16[384,1024]{1,0:T(8,128)(2,1)S(1)}, u32[]{:S(2)}, u32[]{:S(2)}) collective-permute-start(bf16[384,1024]{1,0:T(8,128)(2,1)} %get-tuple-element.127), channel_id=1, source_target_pairs={{0,3},{1,2},{2,1},{3,0},{4,7},{5,6},{6,5},{7,4},{8,11},{9,10},{10,... | collective-permute-start | bytes 2359304 | tf_op jit(solution)/shard_map/ppermute | solution.py:23
  283.3 70.9 %collective-permute-start.17 = (bf16[384,1024]{1,0:T(8,128)(2,1)}, bf16[384,1024]{1,0:T(8,128)(2,1)S(1)}, u32[]{:S(2)}, u32[]{:S(2)}) collective-permute-start(bf16[384,1024]{1,0:T(8,128)(2,1)} %get-tuple-element.121), channel_id=1, source_target_pairs={{0,1},{1,0},{2,3},{3,2},{4,5},{5,4},{6,7},{7,6},{8,9},{9,8},{10,11... | collective-permute-start | bytes 2359304 | tf_op jit(solution)/shard_map/ppermute | solution.py:23
  328.3 26.0 %collective-permute-start.18 = (bf16[384,1024]{1,0:T(8,128)(2,1)}, bf16[384,1024]{1,0:T(8,128)(2,1)S(1)}, u32[]{:S(2)}, u32[]{:S(2)}) collective-permute-start(bf16[384,1024]{1,0:T(8,128)(2,1)} %get-tuple-element.122), channel_id=1, source_target_pairs={{0,2},{1,3},{2,0},{3,1},{4,6},{5,7},{6,4},{7,5},{8,10},{9,11},{10,... | collective-permute-start | bytes 2359304 | tf_op jit(solution)/shard_map/ppermute | solution.py:23
  328.7 47.1 %collective-permute-start.19 = (bf16[384,1024]{1,0:T(8,128)(2,1)}, bf16[384,1024]{1,0:T(8,128)(2,1)S(1)}, u32[]{:S(2)}, u32[]{:S(2)}) collective-permute-start(bf16[384,1024]{1,0:T(8,128)(2,1)} %get-tuple-element.123), channel_id=1, source_target_pairs={{0,3},{1,2},{2,1},{3,0},{4,7},{5,6},{6,5},{7,4},{8,11},{9,10},{10,... | collective-permute-start | bytes 2359304 | tf_op jit(solution)/shard_map/ppermute | solution.py:23
  347.5 1.0 copy-start.4
  354.2 21.6 %copy-start.5 = (bf16[384,1024]{1,0:T(8,128)(2,1)}, bf16[384,1024]{1,0:T(8,128)(2,1)S(1)}, u32[]{:S(2)}) copy-start(bf16[384,1024]{1,0:T(8,128)(2,1)S(1)} %collective-permute-done.17.refs_1_) | copy-start | bytes 2359300
  354.3 21.5 %copy-start.6 = (bf16[384,1024]{1,0:T(8,128)(2,1)}, bf16[384,1024]{1,0:T(8,128)(2,1)S(1)}, u32[]{:S(2)}) copy-start(bf16[384,1024]{1,0:T(8,128)(2,1)S(1)} %collective-permute-done.18.refs_2_) | copy-start | bytes 2359300
  375.8 0.9 copy-start.7
  382.4 1.6 copy-start

commit v14 on v13

--- a/solution.py
+++ b/solution.py
@@ -13,6 +13,7 @@
 decay_rate = 1.0
 sign_width = 10.0
 MIB = 1024 * 1024
+TOP = 14.0
 SMALL = pl.CostEstimate(flops=1024, bytes_accessed=1024, transcendentals=0)
 
 
@@ -200,19 +201,35 @@
     )
 
 
-def deriv_of(tokens, weight):
+def packed_kernel(tokens_ref, weight_ref, out_ref):
+    deriv = jnp.dot(tokens_ref[...], weight_ref[...], preferred_element_type=jnp.float32)
+    group_tok = deriv.shape[0]
+    largest = jnp.max(jnp.abs(deriv), axis=0, keepdims=True)
+    power = jnp.ceil(jnp.log2(jnp.maximum(largest, 2.0**-100)))
+    out_ref[:group_tok, :] = deriv * jnp.exp2(TOP - power)
+    rest = out_ref.shape[0] - group_tok
+    out_ref[group_tok:, :] = jnp.broadcast_to(power, (rest, deriv.shape[1]))
+
+
+def unpacked(packed, group_tok):
+    power = packed[group_tok : group_tok + 1].astype(jnp.float32)
+    return packed[:group_tok].astype(jnp.float32) * jnp.exp2(power - TOP)
+
+
+def deriv_of(tokens, weight, packed):
     group_tok, width = tokens.shape
     cols = weight.shape[1]
     wide = 256 if cols % 256 == 0 else cols
+    tall = group_tok + 16 if packed else group_tok
     return pl.pallas_call(
-        deriv_kernel,
+        packed_kernel if packed else deriv_kernel,
         grid=(cols // wide,),
         in_specs=[
             pl.BlockSpec((group_tok, width), lambda i: (0, 0)),
             pl.BlockSpec((width, wide), lambda i: (0, i)),
         ],
-        out_specs=pl.BlockSpec((group_tok, wide), lambda i: (0, i)),
-        out_shape=jax.ShapeDtypeStruct((group_tok, cols), jnp.float32),
+        out_specs=pl.BlockSpec((tall, wide), lambda i: (0, i)),
+        out_shape=jax.ShapeDtypeStruct((tall, cols), jnp.float32),
         compiler_params=pltpu.CompilerParams(vmem_limit_bytes=56 * MIB),
         cost_estimate=SMALL,
         name="hidden_deriv",
@@ -307,7 +324,8 @@
     own_got = swapped(own_picked[-1], "expert", half)
     tokens = {}
     for m in [0] + others:
-        tokens[m] = in_order(held[m], beside[m], last).reshape(group_tok, width)
+        theirs = after(beside[m], other_twice) if m else beside[m]
+        tokens[m] = in_order(held[m], theirs, last).reshape(group_tok, width)
         tokens[m + 1] = swapped(tokens[m], "expert", 1)
     tokens = [tokens[m] for m in each]
     own_rows = spread(own_picked, own_got, experts)
@@ -331,7 +349,8 @@
 
     own_terms = shard_terms(own_rows)
     weight, own_terms = stage(down_weight[0], own_terms)
-    derivs = [deriv_of(tokens[m], weight) for m in each]
+    derivs = [deriv_of(tokens[m], weight, m > 0) for m in each]
+    derivs = derivs[:1] + [deriv.astype(jnp.float16) for deriv in derivs[1:]]
 
     other_got, other_picked, derivs = stage(other_got, other_picked, derivs)
     other_rows = spread(other_picked, other_got, experts)
@@ -357,7 +376,8 @@
     deriv = jnp.zeros(gate.shape, jnp.float32)
     for m in each:
         chosen = (routing == (mine ^ m))[:, :, None]
-        deriv = jnp.where(chosen, swapped(derivs[m], "expert", m)[:, None, :], deriv)
+        back = unpacked(swapped(derivs[m], "expert", m), group_tok) if m else derivs[m]
+        deriv = jnp.where(chosen, back[:, None, :], deriv)
     d_up = (deriv * gate * sigma).astype(jnp.bfloat16)
     d_gate = (deriv * up * sigma * (1.0 + gate * (1.0 - sigma))).astype(jnp.bfloat16)
 

time: 397 us -> 392 us (0.987)
  waiting for transfers between devices: 209 us -> 185 us
  other arithmetic: 17 us -> 31.2 us
    all_to_all x1, waiting for transfers between devices: 32.3 us -> 13.3 us  [body(): lax.all_to_all(twice, 'dp', split_axis=0, concat_axis=0, tiled=True, axis...]
    mul x0 -> x3, other arithmetic: none -> 8.47 us  [unpacked(): return packed[:group_tok].astype(jnp.float32) * jnp.exp2(power - TOP)]
    ppermute x23, waiting for transfers between devices: 177 us -> 171 us  [swapped(): return lax.ppermute(array, axis, [(i, i ^ mask) for i in range(size)])]
    unnamed x28 -> x34, local copies, waits for them, and re-layouts: 7.54 us -> 9.49 us
  transfers between devices with their start and end apart: 26 -> 26, of which waited for: 13 -> 12; matrix products, arithmetic and copies ran while one was open for 9% -> 13% of each run, Pallas kernels for 22% -> 23%
where the time goes in v14:
time: 392 us; the launch traced here: 388 us
  waiting for transfers between devices  185 us (47%)
  Pallas kernels  103 us (26%)
  starting transfers between devices  40.9 us (10%)
  other arithmetic  31.2 us (8%)
  local copies, waits for them, and re-layouts  27.8 us (7%)
    ppermute x23, waiting for transfers between devices, swapped(): return lax.ppermute(array, axis, [(i, i ^ mask) for i in range(size)])  171 us
    pallas_call x4, Pallas kernels, deriv_of(): pl.pallas_call(packed_kernel if packed else deriv_kernel, grid=(cols // w...  32.4 us
    pallas_call x2, Pallas kernels, terms(): pl.pallas_call(functools.partial(term_kernel, count), grid_spec=pltpu.Pre...  24.5 us
    pallas_call x4, Pallas kernels, update(): pl.pallas_call(functools.partial(update_kernel, count), grid_spec=pltpu.P...  23 us
    ppermute x23, starting transfers between devices, swapped(): return lax.ppermute(array, axis, [(i, i ^ mask) for i in range(size)])  20 us
    convert_element_type x1, other arithmetic, body(): d_up = (deriv * gate * sigma).astype(jnp.bfloat16)  16.3 us
    all_to_all x2, starting transfers between devices, body(): lax.all_to_all(after(piece, *begun), 'dp', split_axis=0, concat_axis=0, t...  15.2 us
    all_to_all x1, waiting for transfers between devices, body(): lax.all_to_all(twice, 'dp', split_axis=0, concat_axis=0, tiled=True, axis...  13.3 us
  transfers between devices with their start and end apart: 26, of which 12 were waited for; matrix products, arithmetic and copies ran while one was open for 13% of the time, Pallas kernels for 23%

profile of v14, /device:TPU:8, one launch (start us, length us, event | category | flops | bytes accessed | tf_op | source)
XLA Modules:
  0.0 388.0 jit_solution(11123433002193661516)
XLA Ops:
  0.6 2.7 collective-permute-start.1
  5.0 0.8 reshape_reshape.10.named_ref
  5.8 4.3 %reshape.55.gate_ref = bf16[1024,1024]{1,0:T(8,128)(2,1)} reshape(bf16[512,2,1024]{2,1,0:T(2,128)(2,1)} %param.7) | data formatting | bytes 4194304 | tf_op jit(solution)/shard_map/reshape | solution.py:302
  10.1 2.2 reshape.56.up_ref
  12.2 7.0 %hidden_rows.2 = (bf16[2,1024,1024]{2,1,0:T(8,128)(2,1)}, bf16[1,512,1024]{2,1,0:T(8,128)(2,1)}, bf16[1,512,1024]{2,1,0:T(8,128)(2,1)}, bf16[2,512,1024]{2,1,0:T(8,128)(2,1)}) custom-call(s32[1]{0:T(128)} %bitcast.3.place_ref, bf16[1024,1024]{1,0:T(8,128)(2,1)} %reshape.55.gate_ref, bf16[1024,1024]{1,0:T(8,128)(2,1)} %reshape.56.up_ref, ...), custom_call_target="tpu_custom_call" | custom-call | flops 1024 | bytes 1024 | tf_op jit(solution)/shard_map/hidden_rows/pallas_call | solution.py:127
  19.3 2.0 collective-permute-done.1.refs_2_
  21.2 1.1 collective-permute-done.refs_1_
  22.4 14.7 %collective-permute-done.2.refs_3_ = bf16[64,3072]{1,0:T(8,128)(2,1)S(1)} collective-permute-done((bf16[64,3072]{1,0:T(8,128)(2,1)}, bf16[64,3072]{1,0:T(8,128)(2,1)S(1)}, u32[]{:S(2)}, u32[]{:S(2)}) %collective-permute-start.2) | collective-permute-done | bytes 393248 | tf_op jit(solution)/shard_map/ppermute | solution.py:24
  37.1 0.7 copy-done.15
  37.9 5.6 %all-to-all-start = ((bf16[2,1024,1024]{2,1,0:T(8,128)(2,1)}), bf16[2,1024,1024]{2,1,0:T(8,128)(2,1)}, u32[]{:S(2)}, u32[]{:S(2)}) async-start(bf16[2,1024,1024]{2,1,0:T(8,128)(2,1)} %get-tuple-element.85), calls=%async_computation | async-start | bytes 8388608 | tf_op jit(solution)/shard_map/all_to_all | solution.py:311
  43.5 2.6 placed_blocks.1.mine_ref
  46.1 1.5 collective-permute-start.4
  47.7 1.5 collective-permute-start.3
  49.1 33.5 %collective-permute-done.4.theirs_ref = bf16[4,64,3072]{2,1,0:T(8,128)(2,1)S(1)} collective-permute-done((bf16[4,64,3072]{2,1,0:T(8,128)(2,1)}, bf16[4,64,3072]{2,1,0:T(8,128)(2,1)S(1)}, u32[]{:S(2)}, u32[]{:S(2)}) %collective-permute-start.4) | collective-permute-done | bytes 1572896 | tf_op jit(solution)/shard_map/ppermute | solution.py:24
  82.7 1.3 collective-permute-done.3.mine_ref
  84.5 1.5 collective-permute-start.9
  86.0 4.2 %side_by_side.2 = bf16[4,2,64,3072]{3,2,1,0:T(8,128)(2,1)} custom-call(s32[1]{0:T(128)} %bitcast.1.place_ref, bf16[4,64,3072]{2,1,0:T(8,128)(2,1)} %placed_blocks.1.mine_ref, bf16[4,64,3072]{2,1,0:T(8,128)(2,1)} %copy-done.10), custom_call_target="tpu_custom_call" | custom-call | flops 1024 | bytes 1024 | tf_op jit(solution)/shard_map/side_by_side/pallas_call | solution.py:43
  90.2 29.3 %collective-permute-done.6.theirs_ref = bf16[4,64,3072]{2,1,0:T(8,128)(2,1)} collective-permute-done((bf16[4,64,3072]{2,1,0:T(8,128)(2,1)}, bf16[4,64,3072]{2,1,0:T(8,128)(2,1)}, u32[]{:S(2)}, u32[]{:S(2)}) %collective-permute-start.6) | collective-permute-done | bytes 1572896 | tf_op jit(solution)/shard_map/ppermute | solution.py:24
  119.5 13.3 %all-to-all-done.hidden_ref = bf16[2,1024,1024]{2,1,0:T(8,128)(2,1)} async-done(((bf16[2,1024,1024]{2,1,0:T(8,128)(2,1)}), bf16[2,1024,1024]{2,1,0:T(8,128)(2,1)}, u32[]{:S(2)}, u32[]{:S(2)}) %all-to-all-start) | async-done | bytes 4194336 | tf_op jit(solution)/shard_map/all_to_all | solution.py:311
  132.8 4.3 %side_by_side.3 = bf16[4,2,64,3072]{3,2,1,0:T(8,128)(2,1)} custom-call(s32[1]{0:T(128)} %bitcast.1.place_ref, bf16[4,64,3072]{2,1,0:T(8,128)(2,1)} %collective-permute-done.3.mine_ref, bf16[4,64,3072]{2,1,0:T(8,128)(2,1)} %collective-permute-done.6.theirs_ref), custom_call_target="tpu_custom_call" | custom-call | flops 1024 | bytes 1024 | tf_op jit(solution)/shard_map/side_by_side/pallas_call | solution.py:43
  137.5 2.7 fusion.19
  140.3 6.0 %fusion.17 = (bf16[8,384,512]{2,1,0:T(8,128)(2,1)}, bf16[8,384,512]{2,1,0:T(8,128)(2,1)}) fusion(bf16[8,384,1024]{2,1,0:T(8,128)(2,1)} %bitcast.23), kind=kLoop, calls=%fused_computation.34 | loop fusion | bytes 12582912 | tf_op jit(solution)/shard_map/split | solution.py:360
  146.3 1.0 copy-done.11
  147.3 1.1 copy-done.12
  148.4 0.9 copy-done.2
  149.3 9.2 %all-to-all-start.1 = ((bf16[8,384,512]{2,1,0:T(8,128)(2,1)}), bf16[8,384,512]{2,1,0:T(8,128)(2,1)S(1)}, u32[]{:S(2)}, u32[]{:S(2)}) async-start(bf16[8,384,512]{2,1,0:T(8,128)(2,1)} %get-tuple-element.113), calls=%async_computation.1 | async-start | bytes 6291456 | tf_op jit(solution)/shard_map/all_to_all | solution.py:365
  158.5 4.7 %hidden_rows.3 = (bf16[1,512,1024]{2,1,0:T(8,128)(2,1)}, bf16[1,512,1024]{2,1,0:T(8,128)(2,1)}, bf16[2,512,1024]{2,1,0:T(8,128)(2,1)}) custom-call(s32[1]{0:T(128)} %bitcast.place_ref, bf16[2,1024,1024]{2,1,0:T(8,128)(2,1)} %all-to-all-done.hidden_ref, s32[4,256]{1,0:T(4,128)} %reshape_reshape.10.named_ref), custom_call_target="tpu_custom_call" | custom-call | flops 1024 | bytes 1024 | tf_op jit(solution)/shard_map/hidden_rows/pallas_call | solution.py:127
  163.2 1.5 collective-permute-start.11
  164.7 12.2 %group_terms.2 = (bf16[384,1024]{1,0:T(8,128)(2,1)}, bf16[384,1024]{1,0:T(8,128)(2,1)}, bf16[384,1024]{1,0:T(8,128)(2,1)}, bf16[384,1024]{1,0:T(8,128)(2,1)}) custom-call(s32[1]{0:T(128)} %bitcast.11.place_ref, bf16[512,3072]{1,0:T(8,128)(2,1)} %bitcast.29, bf16[512,3072]{1,0:T(8,128)(2,1)} %copy-done.2, bf16[512,3072]{1,0:T(8,128)(2,1)} %bitcast.33, ...), custom_call_target="tpu_custom_call" | custom-call | flops 1024 | bytes 1024 | tf_op jit(solution)/shard_map/group_terms/pallas_call | solution.py:179
  176.9 7.9 %hidden_deriv.4 = f32[512,1024]{1,0:T(8,128)} custom-call(bf16[512,3072]{1,0:T(8,128)(2,1)} %bitcast.30, bf16[3072,1024]{1,0:T(8,128)(2,1)} %bitcast.24), custom_call_target="tpu_custom_call" | custom-call | flops 1024 | bytes 1024 | tf_op jit(solution)/shard_map/hidden_deriv/pallas_call | solution.py:224
  184.8 8.1 %hidden_deriv.7 = f32[528,1024]{1,0:T(8,128)} custom-call(bf16[512,3072]{1,0:T(8,128)(2,1)} %collective-permute-done.7.refs_3_.tokens_ref, bf16[3072,1024]{1,0:T(8,128)(2,1)} %bitcast.25), custom_call_target="tpu_custom_call" | custom-call | flops 1024 | bytes 1024 | tf_op jit(solution)/shard_map/hidden_deriv/pallas_call | solution.py:224
  192.9 8.1 %hidden_deriv.6 = f32[528,1024]{1,0:T(8,128)} custom-call(bf16[512,3072]{1,0:T(8,128)(2,1)} %bitcast.34, bf16[3072,1024]{1,0:T(8,128)(2,1)} %bitcast.26), custom_call_target="tpu_custom_call" | custom-call | flops 1024 | bytes 1024 | tf_op jit(solution)/shard_map/hidden_deriv/pallas_call | solution.py:224
  201.0 8.2 %hidden_deriv.5 = f32[528,1024]{1,0:T(8,128)} custom-call(bf16[512,3072]{1,0:T(8,128)(2,1)} %copy-done.2, bf16[3072,1024]{1,0:T(8,128)(2,1)} %bitcast.27), custom_call_target="tpu_custom_call" | custom-call | flops 1024 | bytes 1024 | tf_op jit(solution)/shard_map/hidden_deriv/pallas_call | solution.py:224
  209.3 1.2 convert_element_type.43
  210.5 0.8 copy-done.4
  211.3 1.2 convert_element_type.42
  212.4 0.8 copy-done.3
  213.3 1.2 convert_element_type.41
  215.1 1.5 fusion.18
  216.7 1.5 collective-permute-start.13
  219.1 1.5 collective-permute-start.20
  221.2 12.3 %group_terms.3 = (bf16[384,1024]{1,0:T(8,128)(2,1)}, bf16[384,1024]{1,0:T(8,128)(2,1)}, bf16[384,1024]{1,0:T(8,128)(2,1)}, bf16[384,1024]{1,0:T(8,128)(2,1)}) custom-call(s32[1]{0:T(128)} %bitcast.11.place_ref, bf16[512,3072]{1,0:T(8,128)(2,1)} %bitcast.31, bf16[512,3072]{1,0:T(8,128)(2,1)} %copy-done.2, bf16[512,3072]{1,0:T(8,128)(2,1)} %bitcast.35, ...), custom_call_target="tpu_custom_call" | custom-call | flops 1024 | bytes 1024 | tf_op jit(solution)/shard_map/group_terms/pallas_call | solution.py:179
  233.5 6.9 %collective-permute-done.12 = f16[528,1024]{1,0:T(8,128)(2,1)} collective-permute-done((f16[528,1024]{1,0:T(8,128)(2,1)}, f16[528,1024]{1,0:T(8,128)(2,1)}, u32[]{:S(2)}, u32[]{:S(2)}) %collective-permute-start.12) | collective-permute-done | bytes 1081376 | tf_op jit(solution)/shard_map/ppermute | solution.py:24
  240.4 1.5 collective-permute-start.22
  242.6 21.5 %collective-permute-done.13 = f16[528,1024]{1,0:T(8,128)(2,1)} collective-permute-done((f16[528,1024]{1,0:T(8,128)(2,1)}, f16[528,1024]{1,0:T(8,128)(2,1)}, u32[]{:S(2)}, u32[]{:S(2)}) %collective-permute-start.13) | collective-permute-done | bytes 1081376 | tf_op jit(solution)/shard_map/ppermute | solution.py:24
  264.2 0.7 fusion.13
  264.9 2.9 convert_multiply_fusion.4
  267.8 0.7 fusion.10
  268.5 2.8 convert_multiply_fusion.3
  271.3 2.8 convert_multiply_fusion.2
  274.1 1.6 copy-done.1
  275.7 6.0 %all-to-all-start.2 = ((bf16[8,384,512]{2,1,0:T(8,128)(2,1)}), bf16[8,384,512]{2,1,0:T(8,128)(2,1)S(1)}, u32[]{:S(2)}, u32[]{:S(2)}) async-start(bf16[8,384,512]{2,1,0:T(8,128)(2,1)} %get-tuple-element.121), calls=%async_computation.2 | async-start | bytes 6291456 | tf_op jit(solution)/shard_map/all_to_all | solution.py:365
  281.8 1.5 collective-permute-start.17
  283.8 1.5 collective-permute-start.19
  285.3 16.3 %fusion.7 = (bf16[512,2,1024]{2,1,0:T(2,128)(2,1)}, bf16[512,2,1024]{2,1,0:T(2,128)(2,1)}) fusion(bf16[512,2,1024]{2,1,0:T(2,128)(2,1)} %param.7, pred[512,2]{1,0:T(8,128)(4,1)S(1)} %copy.25, pred[512,2]{1,0:T(8,128)(4,1)S(1)} %copy.24, pred[512,2]{1,0:T(8,128)(4,1)S(1)} %copy.23, pred[512,2]{1,0:T(8,128)(4,1)S(1)} %copy.21, f32[512,1024]{1,0:T(8,128)} %hidden_deriv.4, ...), kind=kLoop, calls=%fused_computation.10 | loop fusion | flops 19922944 | bytes 16781312 | tf_op jit(solution)/shard_map/convert_element_type | solution.py:381
  301.6 5.8 %lion_step.4 = (f32[1,384,8192]{2,1,0:T(8,128)}, bf16[1,384,8192]{2,1,0:T(8,128)(2,1)}) custom-call(s32[1]{0:T(128)} %bitcast.11.place_ref, bf16[8,384,512]{2,1,0:T(8,128)(2,1)} %copy-done.1, bf16[1,384,8192]{2,1,0:T(8,128)(2,1)} %momentum_ref.7, bf16[384,1024]{1,0:T(8,128)(2,1)} %get-tuple-element.126.refs_0_, ...), custom_call_target="tpu_custom_call" | custom-call | flops 1024 | bytes 1024 | tf_op jit(solution)/shard_map/lion_step/pallas_call | solution.py:263
  307.4 24.7 %collective-permute-done.17.refs_1_ = bf16[384,1024]{1,0:T(8,128)(2,1)S(1)} collective-permute-done((bf16[384,1024]{1,0:T(8,128)(2,1)}, bf16[384,1024]{1,0:T(8,128)(2,1)S(1)}, u32[]{:S(2)}, u32[]{:S(2)}) %collective-permute-start.17) | collective-permute-done | bytes 786464 | tf_op jit(solution)/shard_map/ppermute | solution.py:24
  332.0 19.9 %collective-permute-done.18.refs_2_ = bf16[384,1024]{1,0:T(8,128)(2,1)S(1)} collective-permute-done((bf16[384,1024]{1,0:T(8,128)(2,1)}, bf16[384,1024]{1,0:T(8,128)(2,1)S(1)}, u32[]{:S(2)}, u32[]{:S(2)}) %collective-permute-start.18) | collective-permute-done | bytes 786464 | tf_op jit(solution)/shard_map/ppermute | solution.py:24
  351.9 16.2 %collective-permute-done.19.refs_3_ = bf16[384,1024]{1,0:T(8,128)(2,1)S(1)} collective-permute-done((bf16[384,1024]{1,0:T(8,128)(2,1)}, bf16[384,1024]{1,0:T(8,128)(2,1)S(1)}, u32[]{:S(2)}, u32[]{:S(2)}) %collective-permute-start.19) | collective-permute-done | bytes 786464 | tf_op jit(solution)/shard_map/ppermute | solution.py:24
  368.2 0.9 copy-done.9
  369.1 5.7 %lion_step.5 = (f32[1,384,8192]{2,1,0:T(8,128)}, bf16[1,384,8192]{2,1,0:T(8,128)(2,1)}) custom-call(s32[1]{0:T(128)} %bitcast.15.place_ref, bf16[8,384,512]{2,1,0:T(8,128)(2,1)} %copy-done.1, bf16[1,384,8192]{2,1,0:T(8,128)(2,1)} %momentum_ref.7, bf16[384,1024]{1,0:T(8,128)(2,1)} %get-tuple-element.122.refs_0_, ...), custom_call_target="tpu_custom_call", output_to_operand_aliasing={{0}: (7, {}), {1}: (8, {})} | custom-call | flops 1024 | bytes 1024 | tf_op jit(solution)/shard_map/lion_step/pallas_call | solution.py:263
  374.8 1.6 copy-done
  376.5 5.7 %lion_step.6 = (f32[1,384,8192]{2,1,0:T(8,128)}, bf16[1,384,8192]{2,1,0:T(8,128)(2,1)}) custom-call(s32[1]{0:T(128)} %bitcast.11.place_ref, bf16[8,384,512]{2,1,0:T(8,128)(2,1)} %copy-done, bf16[1,384,8192]{2,1,0:T(8,128)(2,1)} %momentum_ref.7, bf16[384,1024]{1,0:T(8,128)(2,1)} %get-tuple-element.126.refs_0_, ...), custom_call_target="tpu_custom_call", output_to_operand_aliasing={{0}: (7, {}), {1}: (8, {})} | custom-call | flops 1024 | bytes 1024 | tf_op jit(solution)/shard_map/lion_step/pallas_call | solution.py:263
  382.2 5.8 %lion_step.7 = (f32[1,384,8192]{2,1,0:T(8,128)}, bf16[1,384,8192]{2,1,0:T(8,128)(2,1)}) custom-call(s32[1]{0:T(128)} %bitcast.15.place_ref, bf16[8,384,512]{2,1,0:T(8,128)(2,1)} %copy-done, bf16[1,384,8192]{2,1,0:T(8,128)(2,1)} %momentum_ref.7, bf16[384,1024]{1,0:T(8,128)(2,1)} %get-tuple-element.122.refs_0_, ...), custom_call_target="tpu_custom_call", output_to_operand_aliasing={{0}: (7, {}), {1}: (8, {})} | custom-call | flops 1024 | bytes 1024 | tf_op jit(solution)/shard_map/lion_step/pallas_call | solution.py:263
  (60 shorter events, 6.4 us)
Async XLA Ops:
  0.6 20.6 %collective-permute-start.1 = (bf16[64,3072]{1,0:T(8,128)(2,1)}, bf16[64,3072]{1,0:T(8,128)(2,1)S(1)}, u32[]{:S(2)}, u32[]{:S(2)}) collective-permute-start(bf16[64,3072]{1,0:T(8,128)(2,1)} %refs_0_), channel_id=1, source_target_pairs={{0,4},{1,5},{2,6},{3,7},{4,0},{5,1},{6,2},{7,3},{8,12},{9,13},{10,... | collective-permute-start | bytes 1179656 | tf_op jit(solution)/shard_map/ppermute | solution.py:24
  3.3 19.1 %collective-permute-start = (bf16[64,3072]{1,0:T(8,128)(2,1)}, bf16[64,3072]{1,0:T(8,128)(2,1)S(1)}, u32[]{:S(2)}, u32[]{:S(2)}) collective-permute-start(bf16[64,3072]{1,0:T(8,128)(2,1)} %refs_0_), channel_id=1, source_target_pairs={{0,2},{1,3},{2,0},{3,1},{4,6},{5,7},{6,4},{7,5},{8,10},{9,11},{10,... | collective-permute-start | bytes 1179656 | tf_op jit(solution)/shard_map/ppermute | solution.py:24
  3.7 33.4 %collective-permute-start.2 = (bf16[64,3072]{1,0:T(8,128)(2,1)}, bf16[64,3072]{1,0:T(8,128)(2,1)S(1)}, u32[]{:S(2)}, u32[]{:S(2)}) collective-permute-start(bf16[64,3072]{1,0:T(8,128)(2,1)} %refs_0_), channel_id=1, source_target_pairs={{0,6},{1,7},{2,4},{3,5},{4,2},{5,3},{6,0},{7,1},{8,14},{9,15},{10,... | collective-permute-start | bytes 1179656 | tf_op jit(solution)/shard_map/ppermute | solution.py:24
  5.8 4.3 %copy-start.6 = (bf16[512,2,1024]{2,1,0:T(2,128)(2,1)S(1)}, bf16[512,2,1024]{2,1,0:T(2,128)(2,1)}, u32[]{:S(2)}) copy-start(bf16[512,2,1024]{2,1,0:T(2,128)(2,1)} %param.8) | copy-start | bytes 6291460
  21.2 15.9 %copy-start.13 = (bf16[64,3072]{1,0:T(8,128)(2,1)}, bf16[64,3072]{1,0:T(8,128)(2,1)S(1)}, u32[]{:S(2)}) copy-start(bf16[64,3072]{1,0:T(8,128)(2,1)S(1)} %collective-permute-done.1.refs_2_) | copy-start | bytes 1179652
  22.4 14.8 %copy-start.14 = (bf16[64,3072]{1,0:T(8,128)(2,1)}, bf16[64,3072]{1,0:T(8,128)(2,1)S(1)}, u32[]{:S(2)}) copy-start(bf16[64,3072]{1,0:T(8,128)(2,1)S(1)} %collective-permute-done.refs_1_) | copy-start | bytes 1179652
  37.1 0.8 copy-start.15
  37.9 94.9 %all-to-all-start = ((bf16[2,1024,1024]{2,1,0:T(8,128)(2,1)}), bf16[2,1024,1024]{2,1,0:T(8,128)(2,1)}, u32[]{:S(2)}, u32[]{:S(2)}) async-start(bf16[2,1024,1024]{2,1,0:T(8,128)(2,1)} %get-tuple-element.85), calls=%async_computation | async-start | bytes 8388608 | tf_op jit(solution)/shard_map/all_to_all | solution.py:311
  46.1 36.5 %collective-permute-start.4 = (bf16[4,64,3072]{2,1,0:T(8,128)(2,1)}, bf16[4,64,3072]{2,1,0:T(8,128)(2,1)S(1)}, u32[]{:S(2)}, u32[]{:S(2)}) collective-permute-start(bf16[4,64,3072]{2,1,0:T(8,128)(2,1)} %placed_blocks.1.mine_ref), channel_id=1, source_target_pairs={{0,1},{1,0},{2,3},{3,2},{4,5},{5,4},{6,7},{7,6},{8,9},{9,8},{10,11... | collective-permute-start | bytes 4718600 | tf_op jit(solution)/shard_map/ppermute | solution.py:24
  47.7 36.4 %collective-permute-start.3 = (bf16[4,64,3072]{2,1,0:T(8,128)(2,1)}, bf16[4,64,3072]{2,1,0:T(8,128)(2,1)}, u32[]{:S(2)}, u32[]{:S(2)}) collective-permute-start(bf16[4,64,3072]{2,1,0:T(8,128)(2,1)} %placed_blocks.1.mine_ref), channel_id=1, source_target_pairs={{0,16},{8,24},{16,0},{24,8},{1,17},{9,25},{17,1},{25,9},{2,18},{10... | collective-permute-start | bytes 4718600 | tf_op jit(solution)/shard_map/ppermute | solution.py:24
  82.7 3.3 copy-start.10
  84.0 35.5 %collective-permute-start.6 = (bf16[4,64,3072]{2,1,0:T(8,128)(2,1)}, bf16[4,64,3072]{2,1,0:T(8,128)(2,1)}, u32[]{:S(2)}, u32[]{:S(2)}) collective-permute-start(bf16[4,64,3072]{2,1,0:T(8,128)(2,1)} %collective-permute-done.3.mine_ref), channel_id=1, source_target_pairs={{0,1},{1,0},{2,3},{3,2},{4,5},{5,4},{6,7},{7,6},{8,9},{9,8},{10,11... | collective-permute-start | bytes 4718600 | tf_op jit(solution)/shard_map/ppermute | solution.py:24
  84.5 53.0 %collective-permute-start.9 = (bf16[2,512,1024]{2,1,0:T(8,128)(2,1)}, bf16[2,512,1024]{2,1,0:T(8,128)(2,1)}, u32[]{:S(2)}, u32[]{:S(2)}) collective-permute-start(bf16[2,512,1024]{2,1,0:T(8,128)(2,1)} %get-tuple-element.89), channel_id=1, source_target_pairs={{0,16},{8,24},{16,0},{24,8},{1,17},{9,25},{17,1},{25,9},{2,18},{10... | collective-permute-start | bytes 6291464 | tf_op jit(solution)/shard_map/ppermute | solution.py:24
  90.2 56.2 %collective-permute-start.5 = (bf16[512,3072]{1,0:T(8,128)(2,1)}, bf16[512,3072]{1,0:T(8,128)(2,1)S(1)}, u32[]{:S(2)}, u32[]{:S(2)}) collective-permute-start(bf16[512,3072]{1,0:T(8,128)(2,1)} %bitcast.28), channel_id=1, source_target_pairs={{0,8},{8,0},{16,24},{24,16},{1,9},{9,1},{17,25},{25,17},{2,10},{10... | collective-permute-start | bytes 9437192 | tf_op jit(solution)/shard_map/ppermute | solution.py:24
  137.0 11.4 %collective-permute-start.7 = (bf16[512,3072]{1,0:T(8,128)(2,1)}, bf16[512,3072]{1,0:T(8,128)(2,1)}, u32[]{:S(2)}, u32[]{:S(2)}) collective-permute-start(bf16[512,3072]{1,0:T(8,128)(2,1)} %bitcast.32), channel_id=1, source_target_pairs={{0,8},{8,0},{16,24},{24,16},{1,9},{9,1},{17,25},{25,17},{2,10},{10... | collective-permute-start | bytes 9437192 | tf_op jit(solution)/shard_map/ppermute | solution.py:24
  137.1 9.2 %collective-permute-start.8 = (bf16[1,512,1024]{2,1,0:T(8,128)(2,1)}, bf16[1,512,1024]{2,1,0:T(8,128)(2,1)S(1)}, u32[]{:S(2)}, u32[]{:S(2)}) collective-permute-start(bf16[1,512,1024]{2,1,0:T(8,128)(2,1)} %get-tuple-element.88), channel_id=1, source_target_pairs={{0,8},{8,0},{16,24},{24,16},{1,9},{9,1},{17,25},{25,17},{2,10},{10... | collective-permute-start | bytes 3145736 | tf_op jit(solution)/shard_map/ppermute | solution.py:24
  140.3 7.0 %collective-permute-start.10 = (bf16[1,512,1024]{2,1,0:T(8,128)(2,1)S(1)}, bf16[1,512,1024]{2,1,0:T(8,128)(2,1)S(1)}, u32[]{:S(2)}, u32[]{:S(2)}) collective-permute-start(bf16[1,512,1024]{2,1,0:T(8,128)(2,1)S(1)} %get-tuple-element.144), channel_id=1, source_target_pairs={{0,8},{8,0},{16,24},{24,16},{1,9},{9,1},{17,25},{25,17},{2,10},{10... | collective-permute-start | bytes 3145736 | tf_op jit(solution)/shard_map/ppermute | solution.py:24
  146.3 1.0 copy-start.11
  147.3 2.0 copy-start.2
  147.3 1.1 copy-start.12
  149.3 124.8 %all-to-all-start.1 = ((bf16[8,384,512]{2,1,0:T(8,128)(2,1)}), bf16[8,384,512]{2,1,0:T(8,128)(2,1)S(1)}, u32[]{:S(2)}, u32[]{:S(2)}) async-start(bf16[8,384,512]{2,1,0:T(8,128)(2,1)} %get-tuple-element.113), calls=%async_computation.1 | async-start | bytes 6291456 | tf_op jit(solution)/shard_map/all_to_all | solution.py:365
  163.2 51.3 %collective-permute-start.11 = (bf16[2,512,1024]{2,1,0:T(8,128)(2,1)}, bf16[2,512,1024]{2,1,0:T(8,128)(2,1)S(1)}, u32[]{:S(2)}, u32[]{:S(2)}) collective-permute-start(bf16[2,512,1024]{2,1,0:T(8,128)(2,1)} %get-tuple-element.91), channel_id=1, source_target_pairs={{0,16},{8,24},{16,0},{24,8},{1,17},{9,25},{17,1},{25,9},{2,18},{10... | collective-permute-start | bytes 6291464 | tf_op jit(solution)/shard_map/ppermute | solution.py:24
  201.0 8.2 %copy-start.5 = (f32[528,1024]{1,0:T(8,128)S(1)}, f32[528,1024]{1,0:T(8,128)}, u32[]{:S(2)}) copy-start(f32[528,1024]{1,0:T(8,128)} %hidden_deriv.7) | copy-start | bytes 6488068
  209.2 2.0 copy-start.4
  211.3 2.0 copy-start.3
  214.4 3.9 %copy-start.16 = (s32[512,2]{0,1:T(2,128)S(1)}, s32[512,2]{0,1:T(2,128)}, u32[]{:S(2)}) copy-start(s32[512,2]{0,1:T(2,128)} %param.9) | copy-start | bytes 12292
  214.4 4.7 %collective-permute-start.15 = (bf16[1,512,1024]{2,1,0:T(8,128)(2,1)}, bf16[1,512,1024]{2,1,0:T(8,128)(2,1)}, u32[]{:S(2)}, u32[]{:S(2)}) collective-permute-start(bf16[1,512,1024]{2,1,0:T(8,128)(2,1)} %get-tuple-element.115), channel_id=1, source_target_pairs={{0,8},{8,0},{16,24},{24,16},{1,9},{9,1},{17,25},{25,17},{2,10},{10... | collective-permute-start | bytes 3145736 | tf_op jit(solution)/shard_map/ppermute | solution.py:24
  214.4 26.0 %collective-permute-start.12 = (f16[528,1024]{1,0:T(8,128)(2,1)}, f16[528,1024]{1,0:T(8,128)(2,1)}, u32[]{:S(2)}, u32[]{:S(2)}) collective-permute-start(f16[528,1024]{1,0:T(8,128)(2,1)} %convert_element_type.43), channel_id=1, source_target_pairs={{0,24},{8,16},{16,8},{24,0},{1,25},{9,17},{17,9},{25,1},{2,26},{10... | collective-permute-start | bytes 3244040 | tf_op jit(solution)/shard_map/ppermute | solution.py:24
  216.6 4.1 %collective-permute-start.16 = (bf16[1,512,1024]{2,1,0:T(8,128)(2,1)}, bf16[1,512,1024]{2,1,0:T(8,128)(2,1)}, u32[]{:S(2)}, u32[]{:S(2)}) collective-permute-start(bf16[1,512,1024]{2,1,0:T(8,128)(2,1)} %get-tuple-element.142), channel_id=1, source_target_pairs={{0,8},{8,0},{16,24},{24,16},{1,9},{9,1},{17,25},{25,17},{2,10},{10... | collective-permute-start | bytes 3145736 | tf_op jit(solution)/shard_map/ppermute | solution.py:24
  216.7 47.5 %collective-permute-start.13 = (f16[528,1024]{1,0:T(8,128)(2,1)}, f16[528,1024]{1,0:T(8,128)(2,1)}, u32[]{:S(2)}, u32[]{:S(2)}) collective-permute-start(f16[528,1024]{1,0:T(8,128)(2,1)} %convert_element_type.42), channel_id=1, source_target_pairs={{0,16},{8,24},{16,0},{24,8},{1,17},{9,25},{17,1},{25,9},{2,18},{10... | collective-permute-start | bytes 3244040 | tf_op jit(solution)/shard_map/ppermute | solution.py:24
  218.2 49.6 %collective-permute-start.14 = (f16[528,1024]{1,0:T(8,128)(2,1)}, f16[528,1024]{1,0:T(8,128)(2,1)}, u32[]{:S(2)}, u32[]{:S(2)}) collective-permute-start(f16[528,1024]{1,0:T(8,128)(2,1)} %convert_element_type.41), channel_id=1, source_target_pairs={{0,8},{8,0},{16,24},{24,16},{1,9},{9,1},{17,25},{25,17},{2,10},{10... | collective-permute-start | bytes 3244040 | tf_op jit(solution)/shard_map/ppermute | solution.py:24
  219.1 64.7 %collective-permute-start.20 = (bf16[384,1024]{1,0:T(8,128)(2,1)}, bf16[384,1024]{1,0:T(8,128)(2,1)}, u32[]{:S(2)}, u32[]{:S(2)}) collective-permute-start(bf16[384,1024]{1,0:T(8,128)(2,1)} %get-tuple-element.127), channel_id=1, source_target_pairs={{0,1},{1,0},{2,3},{3,2},{4,5},{5,4},{6,7},{7,6},{8,9},{9,8},{10,11... | collective-permute-start | bytes 2359304 | tf_op jit(solution)/shard_map/ppermute | solution.py:24
  220.7 80.9 %collective-permute-start.21 = (bf16[384,1024]{1,0:T(8,128)(2,1)}, bf16[384,1024]{1,0:T(8,128)(2,1)}, u32[]{:S(2)}, u32[]{:S(2)}) collective-permute-start(bf16[384,1024]{1,0:T(8,128)(2,1)} %get-tuple-element.128), channel_id=1, source_target_pairs={{0,2},{1,3},{2,0},{3,1},{4,6},{5,7},{6,4},{7,5},{8,10},{9,11},{10,... | collective-permute-start | bytes 2359304 | tf_op jit(solution)/shard_map/ppermute | solution.py:24
  240.4 61.1 %collective-permute-start.22 = (bf16[384,1024]{1,0:T(8,128)(2,1)}, bf16[384,1024]{1,0:T(8,128)(2,1)}, u32[]{:S(2)}, u32[]{:S(2)}) collective-permute-start(bf16[384,1024]{1,0:T(8,128)(2,1)} %get-tuple-element.129), channel_id=1, source_target_pairs={{0,3},{1,2},{2,1},{3,0},{4,7},{5,6},{6,5},{7,4},{8,11},{9,10},{10,... | collective-permute-start | bytes 2359304 | tf_op jit(solution)/shard_map/ppermute | solution.py:24
  274.1 1.6 copy-start.1
  275.7 99.1 %all-to-all-start.2 = ((bf16[8,384,512]{2,1,0:T(8,128)(2,1)}), bf16[8,384,512]{2,1,0:T(8,128)(2,1)S(1)}, u32[]{:S(2)}, u32[]{:S(2)}) async-start(bf16[8,384,512]{2,1,0:T(8,128)(2,1)} %get-tuple-element.121), calls=%async_computation.2 | async-start | bytes 6291456 | tf_op jit(solution)/shard_map/all_to_all | solution.py:365
  281.8 50.3 %collective-permute-start.17 = (bf16[384,1024]{1,0:T(8,128)(2,1)}, bf16[384,1024]{1,0:T(8,128)(2,1)S(1)}, u32[]{:S(2)}, u32[]{:S(2)}) collective-permute-start(bf16[384,1024]{1,0:T(8,128)(2,1)} %get-tuple-element.123), channel_id=1, source_target_pairs={{0,1},{1,0},{2,3},{3,2},{4,5},{5,4},{6,7},{7,6},{8,9},{9,8},{10,11... | collective-permute-start | bytes 2359304 | tf_op jit(solution)/shard_map/ppermute | solution.py:24
  283.2 68.7 %collective-permute-start.18 = (bf16[384,1024]{1,0:T(8,128)(2,1)}, bf16[384,1024]{1,0:T(8,128)(2,1)S(1)}, u32[]{:S(2)}, u32[]{:S(2)}) collective-permute-start(bf16[384,1024]{1,0:T(8,128)(2,1)} %get-tuple-element.124), channel_id=1, source_target_pairs={{0,2},{1,3},{2,0},{3,1},{4,6},{5,7},{6,4},{7,5},{8,10},{9,11},{10,... | collective-permute-start | bytes 2359304 | tf_op jit(solution)/shard_map/ppermute | solution.py:24
  283.8 84.4 %collective-permute-start.19 = (bf16[384,1024]{1,0:T(8,128)(2,1)}, bf16[384,1024]{1,0:T(8,128)(2,1)S(1)}, u32[]{:S(2)}, u32[]{:S(2)}) collective-permute-start(bf16[384,1024]{1,0:T(8,128)(2,1)} %get-tuple-element.125), channel_id=1, source_target_pairs={{0,3},{1,2},{2,1},{3,0},{4,7},{5,6},{6,5},{7,4},{8,11},{9,10},{10,... | collective-permute-start | bytes 2359304 | tf_op jit(solution)/shard_map/ppermute | solution.py:24
  332.0 36.2 %copy-start.7 = (bf16[384,1024]{1,0:T(8,128)(2,1)}, bf16[384,1024]{1,0:T(8,128)(2,1)S(1)}, u32[]{:S(2)}) copy-start(bf16[384,1024]{1,0:T(8,128)(2,1)S(1)} %collective-permute-done.17.refs_1_) | copy-start | bytes 2359300
  351.9 16.3 %copy-start.8 = (bf16[384,1024]{1,0:T(8,128)(2,1)}, bf16[384,1024]{1,0:T(8,128)(2,1)S(1)}, u32[]{:S(2)}) copy-start(bf16[384,1024]{1,0:T(8,128)(2,1)S(1)} %collective-permute-done.18.refs_2_) | copy-start | bytes 2359300
  368.2 0.9 copy-start.9
  374.8 1.6 copy-start

commit v15 on v14

--- a/solution.py
+++ b/solution.py
@@ -153,8 +153,8 @@
     return [held[m][0][0] for m in range(experts)]
 
 
-def term_kernel(count, place_ref, *refs):
-    tokens, hidden, outs = refs[:count], refs[count : 2 * count], refs[2 * count :]
+def term_kernel(count, steps, place_ref, *refs):
+    tokens, hidden, before = refs[:count], refs[count : 2 * count], refs[2 * count : -steps]
     total = None
     for token_ref, hidden_ref in zip(tokens, hidden):
         one = lax.dot_general(
@@ -165,19 +165,22 @@
         )
         total = one if total is None else total + one
     total = total.astype(jnp.bfloat16)
-    for m, out_ref in enumerate(outs):
+    for m, out_ref in enumerate(refs[-steps:]):
 
         @pl.when(pl.program_id(0) == m)
         def _():
-            out_ref[...] = total
-
-
-def terms(tokens, hidden, tall, steps, block_of, place):
+            if before:
+                out_ref[0] = before[m][0]
+            out_ref[out_ref.shape[0] - 1] = total
+
+
+def terms(tokens, hidden, tall, steps, block_of, place, before=()):
     group_tok, width = tokens[0].shape
     cols = hidden[0].shape[1]
     count = len(tokens)
+    deep = 2 if before else 1
     return pl.pallas_call(
-        functools.partial(term_kernel, count),
+        functools.partial(term_kernel, count, steps),
         grid_spec=pltpu.PrefetchScalarGridSpec(
             num_scalar_prefetch=1,
             grid=(steps,),
@@ -185,14 +188,15 @@
                 pl.BlockSpec((group_tok, tall), lambda m, place: (0, block_of(place[0], m)))
             ]
             * count
-            + [pl.BlockSpec((group_tok, cols), lambda m, place: (0, 0))] * count,
-            out_specs=[pl.BlockSpec((tall, cols), lambda m, place: (0, 0))] * steps,
-        ),
-        out_shape=[jax.ShapeDtypeStruct((tall, cols), jnp.bfloat16)] * steps,
+            + [pl.BlockSpec((group_tok, cols), lambda m, place: (0, 0))] * count
+            + [pl.BlockSpec((1, tall, cols), lambda m, place: (0, 0, 0))] * len(before),
+            out_specs=[pl.BlockSpec((deep, tall, cols), lambda m, place: (0, 0, 0))] * steps,
+        ),
+        out_shape=[jax.ShapeDtypeStruct((deep, tall, cols), jnp.bfloat16)] * steps,
         compiler_params=pltpu.CompilerParams(vmem_limit_bytes=56 * MIB),
         cost_estimate=SMALL,
         name="group_terms",
-    )(place.reshape(1), *tokens, *hidden)
+    )(place.reshape(1), *tokens, *hidden, *before)
 
 
 def deriv_kernel(tokens_ref, weight_ref, out_ref):
@@ -241,9 +245,9 @@
     new_weight_ref, new_momentum_ref = refs[-2:]
     for m, grad_ref in enumerate(grad_refs):
 
-        @pl.when(pl.program_id(0) == m)
+        @pl.when(pl.program_id(1) == m)
         def _():
-            grad = grad_ref[...].astype(jnp.float32)
+            grad = grad_ref[0].astype(jnp.float32)
             moment = momentum_ref[0].astype(jnp.float32)
             weight = weight_ref[0].astype(jnp.float32)
             mix = beta_first * moment + (1.0 - beta_first) * grad
@@ -256,17 +260,26 @@
 
 
 def update(part, place, grads, weight, momentum, done):
-    _, rows, some = weight.shape
+    sources, rows, some = weight.shape
     count = len(grads)
-    parts = grads[0].shape[1] // some
-    wide = pl.BlockSpec((1, rows, some), lambda m, place: (0, 0, (place[0] ^ m) * parts + part))
+    parts = grads[0].shape[2] // some
+
+    def source(far, m, place):
+        return place[0] ^ m ^ (far * count)
+
+    wide = pl.BlockSpec(
+        (1, rows, some), lambda far, m, place: (0, 0, source(far, m, place) * parts + part)
+    )
     return pl.pallas_call(
         functools.partial(update_kernel, count),
         grid_spec=pltpu.PrefetchScalarGridSpec(
             num_scalar_prefetch=1,
-            grid=(count,),
-            in_specs=[pl.BlockSpec((1, rows, some), lambda m, place: (place[0] ^ m, 0, 0)), wide]
-            + [pl.BlockSpec((rows, some), lambda m, place: (0, part))] * count
+            grid=(2, count),
+            in_specs=[
+                pl.BlockSpec((1, rows, some), lambda far, m, place: (source(far, m, place), 0, 0)),
+                wide,
+            ]
+            + [pl.BlockSpec((1, rows, some), lambda far, m, place: (far, 0, part))] * count
             + [pl.BlockSpec(memory_space=pl.ANY)] * len(done),
             out_specs=[wide, wide],
         ),
@@ -329,45 +342,44 @@
         tokens[m + 1] = swapped(tokens[m], "expert", 1)
     tokens = [tokens[m] for m in each]
     own_rows = spread(own_picked, own_got, experts)
-    tokens, own_rows, other_twice = stage(tokens, own_rows, other_twice)
+    tokens, own_rows = stage(tokens, own_rows)
 
     other_picked = picked_rows([other_twice], named, group_tok, experts, 1 - upper)
     other_got = swapped(other_picked[-1], "expert", half)
 
-    def shard_terms(hidden_rows):
+    def shard_terms(hidden_rows, before):
         if rows % 128 == 0:
-            return terms(tokens, hidden_rows, rows, span, lambda place, m: place ^ m, place)
+            return terms(tokens, hidden_rows, rows, span, lambda place, m: place ^ m, place, before)
         tall = width // 8
         total = terms(
             tokens, hidden_rows, tall, 4, lambda place, m: place // span * 4 + m, place
         )
-        total = jnp.concatenate(total, axis=0)
-        return [
-            lax.dynamic_slice_in_dim(total, (place % span ^ m) * rows, rows, axis=0)
+        total = jnp.concatenate(total, axis=1)
+        blocks = [
+            lax.dynamic_slice_in_dim(total, (place % span ^ m) * rows, rows, axis=1)
             for m in range(span)
         ]
-
-    own_terms = shard_terms(own_rows)
+        return [jnp.concatenate(pair, axis=0) for pair in zip(before, blocks)] if before else blocks
+
+    own_terms = shard_terms(own_rows, ())
     weight, own_terms = stage(down_weight[0], own_terms)
     derivs = [deriv_of(tokens[m], weight, m > 0) for m in each]
     derivs = derivs[:1] + [deriv.astype(jnp.float16) for deriv in derivs[1:]]
 
     other_got, other_picked, derivs = stage(other_got, other_picked, derivs)
     other_rows = spread(other_picked, other_got, experts)
-    other_terms = shard_terms(other_rows)
+    both_terms = shard_terms(other_rows, own_terms)
 
     parts = 2 if cols % 256 == 0 else 1
     pieces = jnp.split(down_weight.reshape(shards, rows, cols), parts, axis=2)
     weights = []
     for part, piece in enumerate(pieces):
-        begun = [other_twice] if part == 0 else [weights[-1], other_terms]
+        begun = [other_twice] if part == 0 else [weights[-1], both_terms]
         weights.append(
             lax.all_to_all(after(piece, *begun), "dp", split_axis=0, concat_axis=0, tiled=True)
         )
 
-    other_terms = after(other_terms, weights[0])
-    own_grads = [swapped(own_terms[m], "dp", m) for m in range(span)]
-    other_grads = [swapped(other_terms[m], "dp", m) for m in range(span)]
+    grads = [swapped(both_terms[m], "dp", m) for m in range(span)]
 
     gate_saved, up_saved, _ = stage(gate_saved, up_saved, derivs)
     gate = gate_saved.astype(jnp.float32)
@@ -382,12 +394,8 @@
     d_gate = (deriv * up * sigma * (1.0 + gate * (1.0 - sigma))).astype(jnp.bfloat16)
 
     done = ()
-    for part, grads, off in [
-        (part, grads, off)
-        for part in range(parts)
-        for grads, off in ((own_grads, 0), (other_grads, span))
-    ]:
-        done = update(part, place ^ off, grads, weights[part], momentum, done)
+    for part in range(parts):
+        done = update(part, place, grads, weights[part], momentum, done)
     new_weight, new_momentum = done
     return (d_gate, d_up, new_weight, new_momentum)
 

time: 392 us -> 379 us (0.967)
    ppermute x23 -> x20, waiting for transfers between devices: 171 us -> 136 us  [swapped(): return lax.ppermute(array, axis, [(i, i ^ mask) for i in range(size)])]
    all_to_all x2, waiting for transfers between devices: 0.01 us -> 33.3 us  [body(): lax.all_to_all(after(piece, *begun), 'dp', split_axis=0, concat_axis=0, t...]
    ppermute x23 -> x20, starting transfers between devices: 20 us -> 16.6 us  [swapped(): return lax.ppermute(array, axis, [(i, i ^ mask) for i in range(size)])]
    unnamed x34 -> x26, local copies, waits for them, and re-layouts: 9.49 us -> 6.22 us
    pallas_call x4 -> x2, Pallas kernels: 23 us -> 21.8 us  [update(): pl.pallas_call(functools.partial(update_kernel, count), grid_spec=pltpu.P...]
  transfers between devices with their start and end apart: 26 -> 23, of which waited for: 12 -> 13; matrix products, arithmetic and copies ran while one was open for 13% -> 12% of each run, Pallas kernels for 23% -> 25%
where the time goes in v15:
time: 379 us; the launch traced here: 378 us
  waiting for transfers between devices  182 us (48%)
  Pallas kernels  103 us (27%)
  starting transfers between devices  38.2 us (10%)
  other arithmetic  28.1 us (7%)
  local copies, waits for them, and re-layouts  24.6 us (6%)
    ppermute x20, waiting for transfers between devices, swapped(): return lax.ppermute(array, axis, [(i, i ^ mask) for i in range(size)])  136 us
    all_to_all x2, waiting for transfers between devices, body(): lax.all_to_all(after(piece, *begun), 'dp', split_axis=0, concat_axis=0, t...  33.3 us
    pallas_call x4, Pallas kernels, deriv_of(): pl.pallas_call(packed_kernel if packed else deriv_kernel, grid=(cols // w...  32.3 us
    pallas_call x2, Pallas kernels, terms(): pl.pallas_call(functools.partial(term_kernel, count, steps), grid_spec=pl...  26.7 us
    pallas_call x2, Pallas kernels, update(): pl.pallas_call(functools.partial(update_kernel, count), grid_spec=pltpu.P...  21.8 us
    ppermute x20, starting transfers between devices, swapped(): return lax.ppermute(array, axis, [(i, i ^ mask) for i in range(size)])  16.6 us
    convert_element_type x1, other arithmetic, body(): d_up = (deriv * gate * sigma).astype(jnp.bfloat16)  16.3 us
    all_to_all x2, starting transfers between devices, body(): lax.all_to_all(after(piece, *begun), 'dp', split_axis=0, concat_axis=0, t...  16 us
  transfers between devices with their start and end apart: 23, of which 13 were waited for; matrix products, arithmetic and copies ran while one was open for 12% of the time, Pallas kernels for 25%

profile of v15, /device:TPU:8, one launch (start us, length us, event | category | flops | bytes accessed | tf_op | source)
XLA Modules:
  0.0 377.6 jit_solution(13709275077442283102)
XLA Ops:
  0.6 2.7 collective-permute-start.1
  3.3 0.4 collective-permute-start
  3.7 0.5 collective-permute-start.2
  4.2 0.7 broadcast_xor_fusion
  5.0 0.8 reshape_reshape.10.named_ref
  5.8 4.3 %reshape.48.gate_ref = bf16[1024,1024]{1,0:T(8,128)(2,1)} reshape(bf16[512,2,1024]{2,1,0:T(2,128)(2,1)} %param.7) | data formatting | bytes 4194304 | tf_op jit(solution)/shard_map/reshape | solution.py:315
  10.1 2.2 reshape.49.up_ref
  12.3 7.0 %hidden_rows.2 = (bf16[2,1024,1024]{2,1,0:T(8,128)(2,1)}, bf16[1,512,1024]{2,1,0:T(8,128)(2,1)}, bf16[1,512,1024]{2,1,0:T(8,128)(2,1)}, bf16[2,512,1024]{2,1,0:T(8,128)(2,1)}) custom-call(s32[1]{0:T(128)} %bitcast.1.place_ref, bf16[1024,1024]{1,0:T(8,128)(2,1)} %reshape.48.gate_ref, bf16[1024,1024]{1,0:T(8,128)(2,1)} %reshape.49.up_ref, ...), custom_call_target="tpu_custom_call" | custom-call | flops 1024 | bytes 1024 | tf_op jit(solution)/shard_map/hidden_rows/pallas_call | solution.py:127
  19.3 2.0 collective-permute-done.1.refs_2_
  21.2 1.1 collective-permute-done.refs_1_
  22.4 14.7 %collective-permute-done.2.refs_3_ = bf16[64,3072]{1,0:T(8,128)(2,1)S(1)} collective-permute-done((bf16[64,3072]{1,0:T(8,128)(2,1)}, bf16[64,3072]{1,0:T(8,128)(2,1)S(1)}, u32[]{:S(2)}, u32[]{:S(2)}) %collective-permute-start.2) | collective-permute-done | bytes 393248 | tf_op jit(solution)/shard_map/ppermute | solution.py:24
  37.1 0.7 copy-done.11
  37.9 5.6 %all-to-all-start = ((bf16[2,1024,1024]{2,1,0:T(8,128)(2,1)}), bf16[2,1024,1024]{2,1,0:T(8,128)(2,1)}, u32[]{:S(2)}, u32[]{:S(2)}) async-start(bf16[2,1024,1024]{2,1,0:T(8,128)(2,1)} %get-tuple-element.66), calls=%async_computation | async-start | bytes 8388608 | tf_op jit(solution)/shard_map/all_to_all | solution.py:324
  43.5 2.6 placed_blocks.1.mine_ref
  46.1 1.5 collective-permute-start.5
  47.6 1.5 collective-permute-start.4
  49.1 33.5 %collective-permute-done.5.theirs_ref = bf16[4,64,3072]{2,1,0:T(8,128)(2,1)S(1)} collective-permute-done((bf16[4,64,3072]{2,1,0:T(8,128)(2,1)}, bf16[4,64,3072]{2,1,0:T(8,128)(2,1)S(1)}, u32[]{:S(2)}, u32[]{:S(2)}) %collective-permute-start.5) | collective-permute-done | bytes 1572896 | tf_op jit(solution)/shard_map/ppermute | solution.py:24
  82.6 1.3 collective-permute-done.4.mine_ref
  84.0 0.5 collective-permute-start.7
  84.5 1.5 collective-permute-start.10
  86.0 4.2 %side_by_side.2 = bf16[4,2,64,3072]{3,2,1,0:T(8,128)(2,1)} custom-call(s32[1]{0:T(128)} %bitcast.2.place_ref, bf16[4,64,3072]{2,1,0:T(8,128)(2,1)} %placed_blocks.1.mine_ref, bf16[4,64,3072]{2,1,0:T(8,128)(2,1)} %copy-done.6), custom_call_target="tpu_custom_call" | custom-call | flops 1024 | bytes 1024 | tf_op jit(solution)/shard_map/side_by_side/pallas_call | solution.py:43
  90.1 29.3 %collective-permute-done.7.theirs_ref = bf16[4,64,3072]{2,1,0:T(8,128)(2,1)} collective-permute-done((bf16[4,64,3072]{2,1,0:T(8,128)(2,1)}, bf16[4,64,3072]{2,1,0:T(8,128)(2,1)}, u32[]{:S(2)}, u32[]{:S(2)}) %collective-permute-start.7) | collective-permute-done | bytes 1572896 | tf_op jit(solution)/shard_map/ppermute | solution.py:24
  119.4 13.3 %all-to-all-done.hidden_ref = bf16[2,1024,1024]{2,1,0:T(8,128)(2,1)} async-done(((bf16[2,1024,1024]{2,1,0:T(8,128)(2,1)}), bf16[2,1024,1024]{2,1,0:T(8,128)(2,1)}, u32[]{:S(2)}, u32[]{:S(2)}) %all-to-all-start) | async-done | bytes 4194336 | tf_op jit(solution)/shard_map/all_to_all | solution.py:324
  132.8 4.2 %side_by_side.3 = bf16[4,2,64,3072]{3,2,1,0:T(8,128)(2,1)} custom-call(s32[1]{0:T(128)} %bitcast.2.place_ref, bf16[4,64,3072]{2,1,0:T(8,128)(2,1)} %collective-permute-done.4.mine_ref, bf16[4,64,3072]{2,1,0:T(8,128)(2,1)} %collective-permute-done.7.theirs_ref), custom_call_target="tpu_custom_call" | custom-call | flops 1024 | bytes 1024 | tf_op jit(solution)/shard_map/side_by_side/pallas_call | solution.py:43
  137.0 6.0 %fusion.17 = (bf16[8,384,512]{2,1,0:T(8,128)(2,1)}, bf16[8,384,512]{2,1,0:T(8,128)(2,1)}) fusion(bf16[8,384,1024]{2,1,0:T(8,128)(2,1)} %bitcast.22), kind=kLoop, calls=%fused_computation.34 | loop fusion | bytes 12582912 | tf_op jit(solution)/shard_map/split | solution.py:374
  143.0 10.0 %all-to-all-start.1 = ((bf16[8,384,512]{2,1,0:T(8,128)(2,1)}), bf16[8,384,512]{2,1,0:T(8,128)(2,1)}, u32[]{:S(2)}, u32[]{:S(2)}) async-start(bf16[8,384,512]{2,1,0:T(8,128)(2,1)} %get-tuple-element.103), calls=%async_computation.1 | async-start | bytes 6291456 | tf_op jit(solution)/shard_map/all_to_all | solution.py:379
  153.0 4.7 %hidden_rows.3 = (bf16[1,512,1024]{2,1,0:T(8,128)(2,1)}, bf16[1,512,1024]{2,1,0:T(8,128)(2,1)}, bf16[2,512,1024]{2,1,0:T(8,128)(2,1)}) custom-call(s32[1]{0:T(128)} %bitcast.place_ref, bf16[2,1024,1024]{2,1,0:T(8,128)(2,1)} %all-to-all-done.hidden_ref, s32[4,256]{1,0:T(4,128)} %reshape_reshape.10.named_ref), custom_call_target="tpu_custom_call" | custom-call | flops 1024 | bytes 1024 | tf_op jit(solution)/shard_map/hidden_rows/pallas_call | solution.py:127
  157.6 1.5 collective-permute-start.3
  159.1 2.7 fusion.19
  161.8 0.5 collective-permute-start.11
  162.3 2.3 collective-permute-done.11
  164.6 1.0 copy-done.8
  165.6 12.3 %group_terms.2 = (bf16[1,384,1024]{2,1,0:T(8,128)(2,1)}, bf16[1,384,1024]{2,1,0:T(8,128)(2,1)}, bf16[1,384,1024]{2,1,0:T(8,128)(2,1)}, bf16[1,384,1024]{2,1,0:T(8,128)(2,1)}) custom-call(s32[1]{0:T(128)} %bitcast.11.place_ref, bf16[512,3072]{1,0:T(8,128)(2,1)} %bitcast.28, bf16[512,3072]{1,0:T(8,128)(2,1)} %copy-done, bf16[512,3072]{1,0:T(8,128)(2,1)} %bitcast.32, ...), custom_call_target="tpu_custom_call" | custom-call | flops 1024 | bytes 1024 | tf_op jit(solution)/shard_map/group_terms/pallas_call | solution.py:182
  177.9 7.9 %hidden_deriv.4 = f32[512,1024]{1,0:T(8,128)} custom-call(bf16[512,3072]{1,0:T(8,128)(2,1)} %bitcast.29, bf16[3072,1024]{1,0:T(8,128)(2,1)} %bitcast.23), custom_call_target="tpu_custom_call" | custom-call | flops 1024 | bytes 1024 | tf_op jit(solution)/shard_map/hidden_deriv/pallas_call | solution.py:228
  185.8 8.1 %hidden_deriv.7 = f32[528,1024]{1,0:T(8,128)} custom-call(bf16[512,3072]{1,0:T(8,128)(2,1)} %collective-permute-done.8.refs_3_.tokens_ref, bf16[3072,1024]{1,0:T(8,128)(2,1)} %bitcast.24), custom_call_target="tpu_custom_call" | custom-call | flops 1024 | bytes 1024 | tf_op jit(solution)/shard_map/hidden_deriv/pallas_call | solution.py:228
  193.9 8.1 %hidden_deriv.6 = f32[528,1024]{1,0:T(8,128)} custom-call(bf16[512,3072]{1,0:T(8,128)(2,1)} %bitcast.33, bf16[3072,1024]{1,0:T(8,128)(2,1)} %bitcast.25), custom_call_target="tpu_custom_call" | custom-call | flops 1024 | bytes 1024 | tf_op jit(solution)/shard_map/hidden_deriv/pallas_call | solution.py:228
  202.0 8.2 %hidden_deriv.5 = f32[528,1024]{1,0:T(8,128)} custom-call(bf16[512,3072]{1,0:T(8,128)(2,1)} %copy-done, bf16[3072,1024]{1,0:T(8,128)(2,1)} %bitcast.26), custom_call_target="tpu_custom_call" | custom-call | flops 1024 | bytes 1024 | tf_op jit(solution)/shard_map/hidden_deriv/pallas_call | solution.py:228
  210.4 1.4 copy-done.3
  212.0 1.4 copy-done.2
  213.7 0.4 collective-permute-start.15
  214.1 0.3 collective-permute-start.12
  214.4 1.5 fusion.18
  215.9 0.4 collective-permute-start.16
  216.3 1.5 collective-permute-start.13
  218.6 0.3 collective-permute-done.16
  218.9 14.5 %group_terms.3 = (bf16[2,384,1024]{2,1,0:T(8,128)(2,1)}, bf16[2,384,1024]{2,1,0:T(8,128)(2,1)}, bf16[2,384,1024]{2,1,0:T(8,128)(2,1)}, bf16[2,384,1024]{2,1,0:T(8,128)(2,1)}) custom-call(s32[1]{0:T(128)} %bitcast.11.place_ref, bf16[512,3072]{1,0:T(8,128)(2,1)} %bitcast.30, bf16[512,3072]{1,0:T(8,128)(2,1)} %copy-done, bf16[512,3072]{1,0:T(8,128)(2,1)} %bitcast.34, ...), custom_call_target="tpu_custom_call" | custom-call | flops 1024 | bytes 1024 | tf_op jit(solution)/shard_map/group_terms/pallas_call | solution.py:182
  233.4 1.4 collective-permute-start.17
  234.8 0.5 collective-permute-start.18
  235.4 4.7 %collective-permute-done.12 = f16[528,1024]{1,0:T(8,128)(2,1)} collective-permute-done((f16[528,1024]{1,0:T(8,128)(2,1)S(1)}, f16[528,1024]{1,0:T(8,128)(2,1)}, u32[]{:S(2)}, u32[]{:S(2)}) %collective-permute-start.12) | collective-permute-done | bytes 1081376 | tf_op jit(solution)/shard_map/ppermute | solution.py:24
  240.1 1.4 collective-permute-start.19
  241.5 0.7 fusion.16
  242.2 21.4 %collective-permute-done.13 = f16[528,1024]{1,0:T(8,128)(2,1)} collective-permute-done((f16[528,1024]{1,0:T(8,128)(2,1)S(1)}, f16[528,1024]{1,0:T(8,128)(2,1)}, u32[]{:S(2)}, u32[]{:S(2)}) %collective-permute-start.13) | collective-permute-done | bytes 1081376 | tf_op jit(solution)/shard_map/ppermute | solution.py:24
  263.6 0.7 fusion.13
  264.3 0.7 fusion.10
  265.0 2.8 convert_multiply_fusion.4
  267.8 2.8 convert_multiply_fusion.3
  270.6 2.8 convert_multiply_fusion.2
  273.4 6.1 %all-to-all-start.2 = ((bf16[8,384,512]{2,1,0:T(8,128)(2,1)}), bf16[8,384,512]{2,1,0:T(8,128)(2,1)S(1)}, u32[]{:S(2)}, u32[]{:S(2)}) async-start(bf16[8,384,512]{2,1,0:T(8,128)(2,1)} %get-tuple-element.115), calls=%async_computation.2 | async-start | bytes 6291456 | tf_op jit(solution)/shard_map/all_to_all | solution.py:379
  279.5 16.3 %fusion.7 = (bf16[512,2,1024]{2,1,0:T(2,128)(2,1)}, bf16[512,2,1024]{2,1,0:T(2,128)(2,1)}) fusion(bf16[512,2,1024]{2,1,0:T(2,128)(2,1)} %param.7, pred[512,2]{1,0:T(8,128)(4,1)S(1)} %copy.21, pred[512,2]{1,0:T(8,128)(4,1)S(1)} %copy.20, pred[512,2]{1,0:T(8,128)(4,1)S(1)} %copy.19, pred[512,2]{1,0:T(8,128)(4,1)S(1)} %copy.17, f32[512,1024]{1,0:T(8,128)} %hidden_deriv.4, ...), kind=kLoop, calls=%fused_computation.10 | loop fusion | flops 19922944 | bytes 16781312 | tf_op jit(solution)/shard_map/convert_element_type | solution.py:393
  295.8 25.1 %collective-permute-done.19.refs_3_ = bf16[2,384,1024]{2,1,0:T(8,128)(2,1)} collective-permute-done((bf16[2,384,1024]{2,1,0:T(8,128)(2,1)}, bf16[2,384,1024]{2,1,0:T(8,128)(2,1)}, u32[]{:S(2)}, u32[]{:S(2)}) %collective-permute-start.19) | collective-permute-done | bytes 1572896 | tf_op jit(solution)/shard_map/ppermute | solution.py:24
  320.9 10.9 %lion_step.2 = (f32[1,384,8192]{2,1,0:T(8,128)}, bf16[1,384,8192]{2,1,0:T(8,128)(2,1)}) custom-call(s32[1]{0:T(128)} %bitcast.11.place_ref, bf16[8,384,512]{2,1,0:T(8,128)(2,1)} %all-to-all-done.1.weight_ref, bf16[1,384,8192]{2,1,0:T(8,128)(2,1)} %momentum_ref.3, bf16[2,384,1024]{2,1,0:T(8,128)(2,1)} %get-tuple-element.111.refs_0_, ...), custom_call_target="tpu_custom_call" | custom-call | flops 1024 | bytes 1024 | tf_op jit(solution)/shard_map/lion_step/pallas_call | solution.py:273
  331.8 33.3 %all-to-all-done.2.weight_ref = bf16[8,384,512]{2,1,0:T(8,128)(2,1)S(1)} async-done(((bf16[8,384,512]{2,1,0:T(8,128)(2,1)}), bf16[8,384,512]{2,1,0:T(8,128)(2,1)S(1)}, u32[]{:S(2)}, u32[]{:S(2)}) %all-to-all-start.2) | async-done | bytes 3145760 | tf_op jit(solution)/shard_map/all_to_all | solution.py:379
  365.1 1.6 copy-done.1
  366.7 10.9 %lion_step.3 = (f32[1,384,8192]{2,1,0:T(8,128)}, bf16[1,384,8192]{2,1,0:T(8,128)(2,1)}) custom-call(s32[1]{0:T(128)} %bitcast.11.place_ref, bf16[8,384,512]{2,1,0:T(8,128)(2,1)} %copy-done.1, bf16[1,384,8192]{2,1,0:T(8,128)(2,1)} %momentum_ref.3, bf16[2,384,1024]{2,1,0:T(8,128)(2,1)} %get-tuple-element.111.refs_0_, ...), custom_call_target="tpu_custom_call", output_to_operand_aliasing={{0}: (7, {}), {1}: (8, {})} | custom-call | flops 1024 | bytes 1024 | tf_op jit(solution)/shard_map/lion_step/pallas_call | solution.py:273
  (44 shorter events, 1.6 us)
Async XLA Ops:
  0.6 20.6 %collective-permute-start.1 = (bf16[64,3072]{1,0:T(8,128)(2,1)}, bf16[64,3072]{1,0:T(8,128)(2,1)S(1)}, u32[]{:S(2)}, u32[]{:S(2)}) collective-permute-start(bf16[64,3072]{1,0:T(8,128)(2,1)} %refs_0_), channel_id=1, source_target_pairs={{0,4},{1,5},{2,6},{3,7},{4,0},{5,1},{6,2},{7,3},{8,12},{9,13},{10,... | collective-permute-start | bytes 1179656 | tf_op jit(solution)/shard_map/ppermute | solution.py:24
  3.3 19.1 %collective-permute-start = (bf16[64,3072]{1,0:T(8,128)(2,1)}, bf16[64,3072]{1,0:T(8,128)(2,1)S(1)}, u32[]{:S(2)}, u32[]{:S(2)}) collective-permute-start(bf16[64,3072]{1,0:T(8,128)(2,1)} %refs_0_), channel_id=1, source_target_pairs={{0,2},{1,3},{2,0},{3,1},{4,6},{5,7},{6,4},{7,5},{8,10},{9,11},{10,... | collective-permute-start | bytes 1179656 | tf_op jit(solution)/shard_map/ppermute | solution.py:24
  3.7 33.4 %collective-permute-start.2 = (bf16[64,3072]{1,0:T(8,128)(2,1)}, bf16[64,3072]{1,0:T(8,128)(2,1)S(1)}, u32[]{:S(2)}, u32[]{:S(2)}) collective-permute-start(bf16[64,3072]{1,0:T(8,128)(2,1)} %refs_0_), channel_id=1, source_target_pairs={{0,6},{1,7},{2,4},{3,5},{4,2},{5,3},{6,0},{7,1},{8,14},{9,15},{10,... | collective-permute-start | bytes 1179656 | tf_op jit(solution)/shard_map/ppermute | solution.py:24
  5.8 4.3 %copy-start.5 = (bf16[512,2,1024]{2,1,0:T(2,128)(2,1)S(1)}, bf16[512,2,1024]{2,1,0:T(2,128)(2,1)}, u32[]{:S(2)}) copy-start(bf16[512,2,1024]{2,1,0:T(2,128)(2,1)} %param.8) | copy-start | bytes 6291460
  21.2 15.9 %copy-start.9 = (bf16[64,3072]{1,0:T(8,128)(2,1)}, bf16[64,3072]{1,0:T(8,128)(2,1)S(1)}, u32[]{:S(2)}) copy-start(bf16[64,3072]{1,0:T(8,128)(2,1)S(1)} %collective-permute-done.1.refs_2_) | copy-start | bytes 1179652
  22.4 14.8 %copy-start.10 = (bf16[64,3072]{1,0:T(8,128)(2,1)}, bf16[64,3072]{1,0:T(8,128)(2,1)S(1)}, u32[]{:S(2)}) copy-start(bf16[64,3072]{1,0:T(8,128)(2,1)S(1)} %collective-permute-done.refs_1_) | copy-start | bytes 1179652
  37.1 0.7 copy-start.11
  37.9 94.9 %all-to-all-start = ((bf16[2,1024,1024]{2,1,0:T(8,128)(2,1)}), bf16[2,1024,1024]{2,1,0:T(8,128)(2,1)}, u32[]{:S(2)}, u32[]{:S(2)}) async-start(bf16[2,1024,1024]{2,1,0:T(8,128)(2,1)} %get-tuple-element.66), calls=%async_computation | async-start | bytes 8388608 | tf_op jit(solution)/shard_map/all_to_all | solution.py:324
  46.1 36.5 %collective-permute-start.5 = (bf16[4,64,3072]{2,1,0:T(8,128)(2,1)}, bf16[4,64,3072]{2,1,0:T(8,128)(2,1)S(1)}, u32[]{:S(2)}, u32[]{:S(2)}) collective-permute-start(bf16[4,64,3072]{2,1,0:T(8,128)(2,1)} %placed_blocks.1.mine_ref), channel_id=1, source_target_pairs={{0,1},{1,0},{2,3},{3,2},{4,5},{5,4},{6,7},{7,6},{8,9},{9,8},{10,11... | collective-permute-start | bytes 4718600 | tf_op jit(solution)/shard_map/ppermute | solution.py:24
  47.6 36.4 %collective-permute-start.4 = (bf16[4,64,3072]{2,1,0:T(8,128)(2,1)}, bf16[4,64,3072]{2,1,0:T(8,128)(2,1)}, u32[]{:S(2)}, u32[]{:S(2)}) collective-permute-start(bf16[4,64,3072]{2,1,0:T(8,128)(2,1)} %placed_blocks.1.mine_ref), channel_id=1, source_target_pairs={{0,16},{8,24},{16,0},{24,8},{1,17},{9,25},{17,1},{25,9},{2,18},{10... | collective-permute-start | bytes 4718600 | tf_op jit(solution)/shard_map/ppermute | solution.py:24
  82.6 3.3 copy-start.6
  84.0 35.5 %collective-permute-start.7 = (bf16[4,64,3072]{2,1,0:T(8,128)(2,1)}, bf16[4,64,3072]{2,1,0:T(8,128)(2,1)}, u32[]{:S(2)}, u32[]{:S(2)}) collective-permute-start(bf16[4,64,3072]{2,1,0:T(8,128)(2,1)} %collective-permute-done.4.mine_ref), channel_id=1, source_target_pairs={{0,1},{1,0},{2,3},{3,2},{4,5},{5,4},{6,7},{7,6},{8,9},{9,8},{10,11... | collective-permute-start | bytes 4718600 | tf_op jit(solution)/shard_map/ppermute | solution.py:24
  84.5 74.6 %collective-permute-start.10 = (bf16[2,512,1024]{2,1,0:T(8,128)(2,1)}, bf16[2,512,1024]{2,1,0:T(8,128)(2,1)}, u32[]{:S(2)}, u32[]{:S(2)}) collective-permute-start(bf16[2,512,1024]{2,1,0:T(8,128)(2,1)} %get-tuple-element.83), channel_id=1, source_target_pairs={{0,16},{8,24},{16,0},{24,8},{1,17},{9,25},{17,1},{25,9},{2,18},{10... | collective-permute-start | bytes 6291464 | tf_op jit(solution)/shard_map/ppermute | solution.py:24
  90.1 72.2 %collective-permute-start.6 = (bf16[512,3072]{1,0:T(8,128)(2,1)}, bf16[512,3072]{1,0:T(8,128)(2,1)S(1)}, u32[]{:S(2)}, u32[]{:S(2)}) collective-permute-start(bf16[512,3072]{1,0:T(8,128)(2,1)} %bitcast.27), channel_id=1, source_target_pairs={{0,8},{8,0},{16,24},{24,16},{1,9},{9,1},{17,25},{25,17},{2,10},{10... | collective-permute-start | bytes 9437192 | tf_op jit(solution)/shard_map/ppermute | solution.py:24
  137.0 27.7 %collective-permute-start.8 = (bf16[512,3072]{1,0:T(8,128)(2,1)}, bf16[512,3072]{1,0:T(8,128)(2,1)}, u32[]{:S(2)}, u32[]{:S(2)}) collective-permute-start(bf16[512,3072]{1,0:T(8,128)(2,1)} %bitcast.31), channel_id=1, source_target_pairs={{0,8},{8,0},{16,24},{24,16},{1,9},{9,1},{17,25},{25,17},{2,10},{10... | collective-permute-start | bytes 9437192 | tf_op jit(solution)/shard_map/ppermute | solution.py:24
  143.0 130.4 %all-to-all-start.1 = ((bf16[8,384,512]{2,1,0:T(8,128)(2,1)}), bf16[8,384,512]{2,1,0:T(8,128)(2,1)}, u32[]{:S(2)}, u32[]{:S(2)}) async-start(bf16[8,384,512]{2,1,0:T(8,128)(2,1)} %get-tuple-element.103), calls=%async_computation.1 | async-start | bytes 6291456 | tf_op jit(solution)/shard_map/all_to_all | solution.py:379
  157.6 56.0 %collective-permute-start.3 = (bf16[2,512,1024]{2,1,0:T(8,128)(2,1)}, bf16[2,512,1024]{2,1,0:T(8,128)(2,1)S(1)}, u32[]{:S(2)}, u32[]{:S(2)}) collective-permute-start(bf16[2,512,1024]{2,1,0:T(8,128)(2,1)} %get-tuple-element.67), channel_id=1, source_target_pairs={{0,16},{8,24},{16,0},{24,8},{1,17},{9,25},{17,1},{25,9},{2,18},{10... | collective-permute-start | bytes 6291464 | tf_op jit(solution)/shard_map/ppermute | solution.py:24
  159.1 3.2 collective-permute-start.9
  161.8 2.8 collective-permute-start.11
  162.3 2.3 copy-start.7
  162.3 2.3 copy-start
  164.6 1.0 copy-start.8
  202.0 8.2 %copy-start.4 = (f32[528,1024]{1,0:T(8,128)S(1)}, f32[528,1024]{1,0:T(8,128)}, u32[]{:S(2)}) copy-start(f32[528,1024]{1,0:T(8,128)} %hidden_deriv.7) | copy-start | bytes 6488068
  210.2 1.6 copy-start.3
  211.8 1.6 copy-start.2
  213.7 4.1 %copy-start.12 = (s32[512,2]{0,1:T(2,128)S(1)}, s32[512,2]{0,1:T(2,128)}, u32[]{:S(2)}) copy-start(s32[512,2]{0,1:T(2,128)} %param.9) | copy-start | bytes 12292
  213.7 4.9 %collective-permute-start.15 = (bf16[1,512,1024]{2,1,0:T(8,128)(2,1)}, bf16[1,512,1024]{2,1,0:T(8,128)(2,1)}, u32[]{:S(2)}, u32[]{:S(2)}) collective-permute-start(bf16[1,512,1024]{2,1,0:T(8,128)(2,1)} %get-tuple-element.105), channel_id=1, source_target_pairs={{0,8},{8,0},{16,24},{24,16},{1,9},{9,1},{17,25},{25,17},{2,10},{10... | collective-permute-start | bytes 3145736 | tf_op jit(solution)/shard_map/ppermute | solution.py:24
  214.1 25.9 %collective-permute-start.12 = (f16[528,1024]{1,0:T(8,128)(2,1)S(1)}, f16[528,1024]{1,0:T(8,128)(2,1)}, u32[]{:S(2)}, u32[]{:S(2)}) collective-permute-start(f16[528,1024]{1,0:T(8,128)(2,1)S(1)} %convert_element_type.43), channel_id=1, source_target_pairs={{0,24},{8,16},{16,8},{24,0},{1,25},{9,17},{17,9},{25,1},{2,26},{10... | collective-permute-start | bytes 3244040 | tf_op jit(solution)/shard_map/ppermute | solution.py:24
  215.9 3.0 collective-permute-start.16
  216.3 47.3 %collective-permute-start.13 = (f16[528,1024]{1,0:T(8,128)(2,1)S(1)}, f16[528,1024]{1,0:T(8,128)(2,1)}, u32[]{:S(2)}, u32[]{:S(2)}) collective-permute-start(f16[528,1024]{1,0:T(8,128)(2,1)S(1)} %convert_element_type.42), channel_id=1, source_target_pairs={{0,16},{8,24},{16,0},{24,8},{1,17},{9,25},{17,1},{25,9},{2,18},{10... | collective-permute-start | bytes 3244040 | tf_op jit(solution)/shard_map/ppermute | solution.py:24
  217.8 46.5 %collective-permute-start.14 = (f16[528,1024]{1,0:T(8,128)(2,1)S(1)}, f16[528,1024]{1,0:T(8,128)(2,1)}, u32[]{:S(2)}, u32[]{:S(2)}) collective-permute-start(f16[528,1024]{1,0:T(8,128)(2,1)S(1)} %convert_element_type.41), channel_id=1, source_target_pairs={{0,8},{8,0},{16,24},{24,16},{1,9},{9,1},{17,25},{25,17},{2,10},{10... | collective-permute-start | bytes 3244040 | tf_op jit(solution)/shard_map/ppermute | solution.py:24
  233.4 62.4 %collective-permute-start.17 = (bf16[2,384,1024]{2,1,0:T(8,128)(2,1)}, bf16[2,384,1024]{2,1,0:T(8,128)(2,1)}, u32[]{:S(2)}, u32[]{:S(2)}) collective-permute-start(bf16[2,384,1024]{2,1,0:T(8,128)(2,1)} %get-tuple-element.112), channel_id=1, source_target_pairs={{0,1},{1,0},{2,3},{3,2},{4,5},{5,4},{6,7},{7,6},{8,9},{9,8},{10,11... | collective-permute-start | bytes 4718600 | tf_op jit(solution)/shard_map/ppermute | solution.py:24
  234.8 61.0 %collective-permute-start.18 = (bf16[2,384,1024]{2,1,0:T(8,128)(2,1)}, bf16[2,384,1024]{2,1,0:T(8,128)(2,1)}, u32[]{:S(2)}, u32[]{:S(2)}) collective-permute-start(bf16[2,384,1024]{2,1,0:T(8,128)(2,1)} %get-tuple-element.113), channel_id=1, source_target_pairs={{0,2},{1,3},{2,0},{3,1},{4,6},{5,7},{6,4},{7,5},{8,10},{9,11},{10,... | collective-permute-start | bytes 4718600 | tf_op jit(solution)/shard_map/ppermute | solution.py:24
  240.1 80.8 %collective-permute-start.19 = (bf16[2,384,1024]{2,1,0:T(8,128)(2,1)}, bf16[2,384,1024]{2,1,0:T(8,128)(2,1)}, u32[]{:S(2)}, u32[]{:S(2)}) collective-permute-start(bf16[2,384,1024]{2,1,0:T(8,128)(2,1)} %get-tuple-element.114), channel_id=1, source_target_pairs={{0,3},{1,2},{2,1},{3,0},{4,7},{5,6},{6,5},{7,4},{8,11},{9,10},{10,... | collective-permute-start | bytes 4718600 | tf_op jit(solution)/shard_map/ppermute | solution.py:24
  273.4 91.7 %all-to-all-start.2 = ((bf16[8,384,512]{2,1,0:T(8,128)(2,1)}), bf16[8,384,512]{2,1,0:T(8,128)(2,1)S(1)}, u32[]{:S(2)}, u32[]{:S(2)}) async-start(bf16[8,384,512]{2,1,0:T(8,128)(2,1)} %get-tuple-element.115), calls=%async_computation.2 | async-start | bytes 6291456 | tf_op jit(solution)/shard_map/all_to_all | solution.py:379
  365.1 1.6 copy-start.1

commit v16 on v15

--- a/solution.py
+++ b/solution.py
@@ -381,14 +381,15 @@
 
     grads = [swapped(both_terms[m], "dp", m) for m in range(span)]
 
-    gate_saved, up_saved, _ = stage(gate_saved, up_saved, derivs)
+    backs = [swapped(derivs[m], "expert", m) for m in each]
+    gate_saved, up_saved, backs, _ = stage(gate_saved, up_saved, backs, weights[-1])
     gate = gate_saved.astype(jnp.float32)
     up = up_saved.astype(jnp.float32)
     sigma = jax.nn.sigmoid(gate)
     deriv = jnp.zeros(gate.shape, jnp.float32)
     for m in each:
         chosen = (routing == (mine ^ m))[:, :, None]
-        back = unpacked(swapped(derivs[m], "expert", m), group_tok) if m else derivs[m]
+        back = unpacked(backs[m], group_tok) if m else backs[m]
         deriv = jnp.where(chosen, back[:, None, :], deriv)
     d_up = (deriv * gate * sigma).astype(jnp.bfloat16)
     d_gate = (deriv * up * sigma * (1.0 + gate * (1.0 - sigma))).astype(jnp.bfloat16)

time: 379 us -> 442 us (1.17)
  waiting for transfers between devices: 182 us -> 248 us
    ppermute x20, waiting for transfers between devices: 136 us -> 206 us  [swapped(): return lax.ppermute(array, axis, [(i, i ^ mask) for i in range(size)])]
    all_to_all x2, waiting for transfers between devices: 33.3 us -> 0.01 us  [body(): lax.all_to_all(after(piece, *begun), 'dp', split_axis=0, concat_axis=0, t...]
    all_to_all x1, waiting for transfers between devices: 13.3 us -> 42.2 us  [body(): lax.all_to_all(twice, 'dp', split_axis=0, concat_axis=0, tiled=True, axis...]
    mul x3 -> x2, other arithmetic: 8.4 us -> 3.71 us  [unpacked(): return packed[:group_tok].astype(jnp.float32) * jnp.exp2(power - TOP)]
  transfers between devices with their start and end apart: 23 -> 23, of which waited for: 13 -> 13; matrix products, arithmetic and copies ran while one was open for 12% -> 5% of each run, Pallas kernels for 25% -> 21%
where the time goes in v16:
time: 442 us; the launch traced here: 439 us
  waiting for transfers between devices  248 us (56%)
  Pallas kernels  103 us (23%)
  starting transfers between devices  36.8 us (8%)
  other arithmetic  25.4 us (6%)
  local copies, waits for them, and re-layouts  23.8 us (5%)
    ppermute x20, waiting for transfers between devices, swapped(): return lax.ppermute(array, axis, [(i, i ^ mask) for i in range(size)])  206 us
    all_to_all x1, waiting for transfers between devices, body(): lax.all_to_all(twice, 'dp', split_axis=0, concat_axis=0, tiled=True, axis...  42.2 us
    pallas_call x4, Pallas kernels, deriv_of(): pl.pallas_call(packed_kernel if packed else deriv_kernel, grid=(cols // w...  32.3 us
    pallas_call x2, Pallas kernels, terms(): pl.pallas_call(functools.partial(term_kernel, count, steps), grid_spec=pl...  26.7 us
    pallas_call x2, Pallas kernels, update(): pl.pallas_call(functools.partial(update_kernel, count), grid_spec=pltpu.P...  21.8 us
    all_to_all x2, starting transfers between devices, body(): lax.all_to_all(after(piece, *begun), 'dp', split_axis=0, concat_axis=0, t...  16 us
    ppermute x20, starting transfers between devices, swapped(): return lax.ppermute(array, axis, [(i, i ^ mask) for i in range(size)])  15.2 us
    convert_element_type x1, other arithmetic, body(): d_up = (deriv * gate * sigma).astype(jnp.bfloat16)  15.1 us
  transfers between devices with their start and end apart: 23, of which 13 were waited for; matrix products, arithmetic and copies ran while one was open for 5% of the time, Pallas kernels for 21%

profile of v16, /device:TPU:8, one launch (start us, length us, event | category | flops | bytes accessed | tf_op | source)
XLA Modules:
  0.0 438.7 jit_solution(6883877036175188383)
XLA Ops:
  0.6 2.7 collective-permute-start.1
  3.7 0.5 collective-permute-start.2
  4.2 0.7 broadcast_xor_fusion
  5.0 0.8 reshape_reshape.10.named_ref
  5.8 4.3 reshape.48.gate_ref
  10.1 2.2 reshape.49.up_ref
  12.2 7.0 %hidden_rows.2 = (bf16[2,1024,1024]{2,1,0:T(8,128)(2,1)}, bf16[1,512,1024]{2,1,0:T(8,128)(2,1)}, bf16[1,512,1024]{2,1,0:T(8,128)(2,1)}, bf16[2,512,1024]{2,1,0:T(8,128)(2,1)}) custom-call(s32[1]{0:T(128)} %bitcast.1.place_ref, bf16[1024,1024]{1,0:T(8,128)(2,1)} %reshape.48.gate_ref, bf16[1024,1024]{1,0:T(8,128)(2,1)} %reshape.49.up_ref, ...), custom_call_target="tpu_custom_call" | custom-call | flops 1024 | bytes 1024 | tf_op jit(solution)/shard_map/hidden_rows/pallas_call | solution.py:127
  19.3 2.0 collective-permute-done.1.refs_2_
  21.2 1.1 collective-permute-done.refs_1_
  22.4 14.7 %collective-permute-done.2.refs_3_ = bf16[64,3072]{1,0:T(8,128)(2,1)S(1)} collective-permute-done((bf16[64,3072]{1,0:T(8,128)(2,1)}, bf16[64,3072]{1,0:T(8,128)(2,1)S(1)}, u32[]{:S(2)}, u32[]{:S(2)}) %collective-permute-start.2) | collective-permute-done | bytes 393248 | tf_op jit(solution)/shard_map/ppermute | solution.py:24
  37.1 0.8 copy-done.16
  37.9 5.6 %all-to-all-start = ((bf16[2,1024,1024]{2,1,0:T(8,128)(2,1)}), bf16[2,1024,1024]{2,1,0:T(8,128)(2,1)}, u32[]{:S(2)}, u32[]{:S(2)}) async-start(bf16[2,1024,1024]{2,1,0:T(8,128)(2,1)} %get-tuple-element.70), calls=%async_computation | async-start | bytes 8388608 | tf_op jit(solution)/shard_map/all_to_all | solution.py:324
  43.5 2.6 placed_blocks.1.mine_ref
  46.1 1.5 collective-permute-start.5
  47.6 1.5 collective-permute-start.4
  49.1 33.5 %collective-permute-done.5.theirs_ref = bf16[4,64,3072]{2,1,0:T(8,128)(2,1)S(1)} collective-permute-done((bf16[4,64,3072]{2,1,0:T(8,128)(2,1)}, bf16[4,64,3072]{2,1,0:T(8,128)(2,1)S(1)}, u32[]{:S(2)}, u32[]{:S(2)}) %collective-permute-start.5) | collective-permute-done | bytes 1572896 | tf_op jit(solution)/shard_map/ppermute | solution.py:24
  82.7 1.3 collective-permute-done.4.mine_ref
  84.0 0.5 collective-permute-start.7
  84.5 6.0 %fusion.8 = (bf16[8,384,512]{2,1,0:T(8,128)(2,1)}, bf16[8,384,512]{2,1,0:T(8,128)(2,1)}) fusion(bf16[8,384,1024]{2,1,0:T(8,128)(2,1)} %bitcast.22), kind=kLoop, calls=%fused_computation.25 | loop fusion | bytes 12582912 | tf_op jit(solution)/shard_map/split | solution.py:374
  90.5 42.2 %all-to-all-done.hidden_ref = bf16[2,1024,1024]{2,1,0:T(8,128)(2,1)} async-done(((bf16[2,1024,1024]{2,1,0:T(8,128)(2,1)}), bf16[2,1024,1024]{2,1,0:T(8,128)(2,1)}, u32[]{:S(2)}, u32[]{:S(2)}) %all-to-all-start) | async-done | bytes 4194336 | tf_op jit(solution)/shard_map/all_to_all | solution.py:324
  132.8 9.9 %all-to-all-start.1 = ((bf16[8,384,512]{2,1,0:T(8,128)(2,1)}), bf16[8,384,512]{2,1,0:T(8,128)(2,1)}, u32[]{:S(2)}, u32[]{:S(2)}) async-start(bf16[8,384,512]{2,1,0:T(8,128)(2,1)} %get-tuple-element.105), calls=%async_computation.1 | async-start | bytes 6291456 | tf_op jit(solution)/shard_map/all_to_all | solution.py:379
  142.7 1.5 collective-permute-start.10
  144.2 4.2 side_by_side.2
  148.4 4.3 side_by_side.3
  152.6 0.5 collective-permute-start.8
  153.1 4.7 %hidden_rows.3 = (bf16[1,512,1024]{2,1,0:T(8,128)(2,1)}, bf16[1,512,1024]{2,1,0:T(8,128)(2,1)}, bf16[2,512,1024]{2,1,0:T(8,128)(2,1)}) custom-call(s32[1]{0:T(128)} %bitcast.place_ref, bf16[2,1024,1024]{2,1,0:T(8,128)(2,1)} %all-to-all-done.hidden_ref, s32[4,256]{1,0:T(4,128)} %reshape_reshape.10.named_ref), custom_call_target="tpu_custom_call" | custom-call | flops 1024 | bytes 1024 | tf_op jit(solution)/shard_map/hidden_rows/pallas_call | solution.py:127
  157.8 0.5 collective-permute-start.3
  158.3 33.3 %collective-permute-done.10 = bf16[2,512,1024]{2,1,0:T(8,128)(2,1)} collective-permute-done((bf16[2,512,1024]{2,1,0:T(8,128)(2,1)}, bf16[2,512,1024]{2,1,0:T(8,128)(2,1)}, u32[]{:S(2)}, u32[]{:S(2)}) %collective-permute-start.10) | collective-permute-done | bytes 2097184 | tf_op jit(solution)/shard_map/ppermute | solution.py:24
  191.6 2.7 fusion.10
  194.3 2.6 collective-permute-done.11
  197.0 1.0 copy-done.13
  197.9 12.3 %group_terms.2 = (bf16[1,384,1024]{2,1,0:T(8,128)(2,1)}, bf16[1,384,1024]{2,1,0:T(8,128)(2,1)}, bf16[1,384,1024]{2,1,0:T(8,128)(2,1)}, bf16[1,384,1024]{2,1,0:T(8,128)(2,1)}) custom-call(s32[1]{0:T(128)} %bitcast.11.place_ref, bf16[512,3072]{1,0:T(8,128)(2,1)} %bitcast.28, bf16[512,3072]{1,0:T(8,128)(2,1)} %copy-done, bf16[512,3072]{1,0:T(8,128)(2,1)} %bitcast.32, ...), custom_call_target="tpu_custom_call" | custom-call | flops 1024 | bytes 1024 | tf_op jit(solution)/shard_map/group_terms/pallas_call | solution.py:182
  210.2 7.9 %hidden_deriv.4 = f32[512,1024]{1,0:T(8,128)} custom-call(bf16[512,3072]{1,0:T(8,128)(2,1)} %bitcast.29, bf16[3072,1024]{1,0:T(8,128)(2,1)} %bitcast.23), custom_call_target="tpu_custom_call" | custom-call | flops 1024 | bytes 1024 | tf_op jit(solution)/shard_map/hidden_deriv/pallas_call | solution.py:228
  218.1 8.1 %hidden_deriv.7 = f32[528,1024]{1,0:T(8,128)} custom-call(bf16[512,3072]{1,0:T(8,128)(2,1)} %collective-permute-done.8.refs_3_.tokens_ref, bf16[3072,1024]{1,0:T(8,128)(2,1)} %bitcast.24), custom_call_target="tpu_custom_call" | custom-call | flops 1024 | bytes 1024 | tf_op jit(solution)/shard_map/hidden_deriv/pallas_call | solution.py:228
  226.2 8.1 %hidden_deriv.6 = f32[528,1024]{1,0:T(8,128)} custom-call(bf16[512,3072]{1,0:T(8,128)(2,1)} %bitcast.33, bf16[3072,1024]{1,0:T(8,128)(2,1)} %bitcast.25), custom_call_target="tpu_custom_call" | custom-call | flops 1024 | bytes 1024 | tf_op jit(solution)/shard_map/hidden_deriv/pallas_call | solution.py:228
  234.3 8.2 %hidden_deriv.5 = f32[528,1024]{1,0:T(8,128)} custom-call(bf16[512,3072]{1,0:T(8,128)(2,1)} %copy-done, bf16[3072,1024]{1,0:T(8,128)(2,1)} %bitcast.26), custom_call_target="tpu_custom_call" | custom-call | flops 1024 | bytes 1024 | tf_op jit(solution)/shard_map/hidden_deriv/pallas_call | solution.py:228
  242.5 1.2 convert_element_type.43
  243.7 0.8 copy-done.3
  244.5 1.2 convert_element_type.42
  245.7 0.8 copy-done.2
  246.5 1.2 convert_element_type.41
  248.1 1.2 fusion.9
  249.7 1.0 collective-permute-done.15
  250.6 1.5 collective-permute-done.16
  252.2 1.0 copy-done.12
  253.1 14.4 %group_terms.3 = (bf16[2,384,1024]{2,1,0:T(8,128)(2,1)}, bf16[2,384,1024]{2,1,0:T(8,128)(2,1)}, bf16[2,384,1024]{2,1,0:T(8,128)(2,1)}, bf16[2,384,1024]{2,1,0:T(8,128)(2,1)}) custom-call(s32[1]{0:T(128)} %bitcast.11.place_ref, bf16[512,3072]{1,0:T(8,128)(2,1)} %bitcast.30, bf16[512,3072]{1,0:T(8,128)(2,1)} %copy-done, bf16[512,3072]{1,0:T(8,128)(2,1)} %bitcast.34, ...), custom_call_target="tpu_custom_call" | custom-call | flops 1024 | bytes 1024 | tf_op jit(solution)/shard_map/group_terms/pallas_call | solution.py:182
  267.5 6.0 %all-to-all-start.2 = ((bf16[8,384,512]{2,1,0:T(8,128)(2,1)}), bf16[8,384,512]{2,1,0:T(8,128)(2,1)S(1)}, u32[]{:S(2)}, u32[]{:S(2)}) async-start(bf16[8,384,512]{2,1,0:T(8,128)(2,1)} %get-tuple-element.117), calls=%async_computation.2 | async-start | bytes 6291456 | tf_op jit(solution)/shard_map/all_to_all | solution.py:379
  273.6 1.5 collective-permute-start.17
  275.1 0.6 collective-permute-start.18
  275.6 1.5 collective-permute-start.19
  277.1 1.5 collective-permute-start.13
  278.6 64.7 %collective-permute-done.17.refs_1_ = bf16[2,384,1024]{2,1,0:T(8,128)(2,1)} collective-permute-done((bf16[2,384,1024]{2,1,0:T(8,128)(2,1)}, bf16[2,384,1024]{2,1,0:T(8,128)(2,1)}, u32[]{:S(2)}, u32[]{:S(2)}) %collective-permute-start.17) | collective-permute-done | bytes 1572896 | tf_op jit(solution)/shard_map/ppermute | solution.py:24
  344.2 16.8 %collective-permute-done.18.refs_2_ = bf16[2,384,1024]{2,1,0:T(8,128)(2,1)} collective-permute-done((bf16[2,384,1024]{2,1,0:T(8,128)(2,1)}, bf16[2,384,1024]{2,1,0:T(8,128)(2,1)}, u32[]{:S(2)}, u32[]{:S(2)}) %collective-permute-start.18) | collective-permute-done | bytes 1572896 | tf_op jit(solution)/shard_map/ppermute | solution.py:24
  361.0 33.5 %collective-permute-done.19.refs_3_ = bf16[2,384,1024]{2,1,0:T(8,128)(2,1)} collective-permute-done((bf16[2,384,1024]{2,1,0:T(8,128)(2,1)}, bf16[2,384,1024]{2,1,0:T(8,128)(2,1)}, u32[]{:S(2)}, u32[]{:S(2)}) %collective-permute-start.19) | collective-permute-done | bytes 1572896 | tf_op jit(solution)/shard_map/ppermute | solution.py:24
  394.5 10.9 %lion_step.2 = (f32[1,384,8192]{2,1,0:T(8,128)}, bf16[1,384,8192]{2,1,0:T(8,128)(2,1)}) custom-call(s32[1]{0:T(128)} %bitcast.11.place_ref, bf16[8,384,512]{2,1,0:T(8,128)(2,1)} %all-to-all-done.1.weight_ref, bf16[1,384,8192]{2,1,0:T(8,128)(2,1)} %momentum_ref.3, bf16[2,384,1024]{2,1,0:T(8,128)(2,1)} %get-tuple-element.113.refs_0_, ...), custom_call_target="tpu_custom_call" | custom-call | flops 1024 | bytes 1024 | tf_op jit(solution)/shard_map/lion_step/pallas_call | solution.py:273
  405.4 0.8 multiply_exponential_fusion.2
  406.2 0.8 multiply_exponential_fusion.1
  407.0 0.7 multiply_exponential_fusion
  407.7 1.5 convert_multiply_fusion.4
  409.2 2.2 convert_multiply_fusion.2
  411.5 0.6 copy-done.7
  412.1 0.6 copy-done.8
  412.7 15.1 %fusion.7 = (bf16[512,2,1024]{2,1,0:T(2,128)(2,1)}, bf16[512,2,1024]{2,1,0:T(2,128)(2,1)}) fusion(bf16[512,2,1024]{2,1,0:T(2,128)(2,1)S(1)} %copy-done.5, pred[512,2]{1,0:T(8,128)(4,1)S(1)} %copy.21, pred[512,2]{1,0:T(8,128)(4,1)S(1)} %copy.20, pred[512,2]{1,0:T(8,128)(4,1)S(1)} %copy.19, pred[512,2]{1,0:T(8,128)(4,1)S(1)} %copy.17, ...), kind=kLoop, calls=%fused_computation.10 | loop fusion | flops 19922944 | bytes 16781312 | tf_op jit(solution)/shard_map/convert_element_type | solution.py:394
  427.8 10.9 %lion_step.3 = (f32[1,384,8192]{2,1,0:T(8,128)}, bf16[1,384,8192]{2,1,0:T(8,128)(2,1)}) custom-call(s32[1]{0:T(128)} %bitcast.11.place_ref, bf16[8,384,512]{2,1,0:T(8,128)(2,1)} %copy-done.1, bf16[1,384,8192]{2,1,0:T(8,128)(2,1)} %momentum_ref.3, bf16[2,384,1024]{2,1,0:T(8,128)(2,1)} %get-tuple-element.113.refs_0_, ...), custom_call_target="tpu_custom_call", output_to_operand_aliasing={{0}: (7, {}), {1}: (8, {})} | custom-call | flops 1024 | bytes 1024 | tf_op jit(solution)/shard_map/lion_step/pallas_call | solution.py:273
  (55 shorter events, 2.4 us)
Async XLA Ops:
  0.6 20.6 %collective-permute-start.1 = (bf16[64,3072]{1,0:T(8,128)(2,1)}, bf16[64,3072]{1,0:T(8,128)(2,1)S(1)}, u32[]{:S(2)}, u32[]{:S(2)}) collective-permute-start(bf16[64,3072]{1,0:T(8,128)(2,1)} %refs_0_), channel_id=1, source_target_pairs={{0,4},{1,5},{2,6},{3,7},{4,0},{5,1},{6,2},{7,3},{8,12},{9,13},{10,... | collective-permute-start | bytes 1179656 | tf_op jit(solution)/shard_map/ppermute | solution.py:24
  3.3 19.1 %collective-permute-start = (bf16[64,3072]{1,0:T(8,128)(2,1)}, bf16[64,3072]{1,0:T(8,128)(2,1)S(1)}, u32[]{:S(2)}, u32[]{:S(2)}) collective-permute-start(bf16[64,3072]{1,0:T(8,128)(2,1)} %refs_0_), channel_id=1, source_target_pairs={{0,2},{1,3},{2,0},{3,1},{4,6},{5,7},{6,4},{7,5},{8,10},{9,11},{10,... | collective-permute-start | bytes 1179656 | tf_op jit(solution)/shard_map/ppermute | solution.py:24
  3.7 33.4 %collective-permute-start.2 = (bf16[64,3072]{1,0:T(8,128)(2,1)}, bf16[64,3072]{1,0:T(8,128)(2,1)S(1)}, u32[]{:S(2)}, u32[]{:S(2)}) collective-permute-start(bf16[64,3072]{1,0:T(8,128)(2,1)} %refs_0_), channel_id=1, source_target_pairs={{0,6},{1,7},{2,4},{3,5},{4,2},{5,3},{6,0},{7,1},{8,14},{9,15},{10,... | collective-permute-start | bytes 1179656 | tf_op jit(solution)/shard_map/ppermute | solution.py:24
  5.8 4.3 copy-start.6
  21.2 15.9 %copy-start.14 = (bf16[64,3072]{1,0:T(8,128)(2,1)}, bf16[64,3072]{1,0:T(8,128)(2,1)S(1)}, u32[]{:S(2)}) copy-start(bf16[64,3072]{1,0:T(8,128)(2,1)S(1)} %collective-permute-done.1.refs_2_) | copy-start | bytes 1179652
  22.4 14.8 %copy-start.15 = (bf16[64,3072]{1,0:T(8,128)(2,1)}, bf16[64,3072]{1,0:T(8,128)(2,1)S(1)}, u32[]{:S(2)}) copy-start(bf16[64,3072]{1,0:T(8,128)(2,1)S(1)} %collective-permute-done.refs_1_) | copy-start | bytes 1179652
  37.1 0.8 copy-start.16
  37.9 94.9 %all-to-all-start = ((bf16[2,1024,1024]{2,1,0:T(8,128)(2,1)}), bf16[2,1024,1024]{2,1,0:T(8,128)(2,1)}, u32[]{:S(2)}, u32[]{:S(2)}) async-start(bf16[2,1024,1024]{2,1,0:T(8,128)(2,1)} %get-tuple-element.70), calls=%async_computation | async-start | bytes 8388608 | tf_op jit(solution)/shard_map/all_to_all | solution.py:324
  46.1 36.5 %collective-permute-start.5 = (bf16[4,64,3072]{2,1,0:T(8,128)(2,1)}, bf16[4,64,3072]{2,1,0:T(8,128)(2,1)S(1)}, u32[]{:S(2)}, u32[]{:S(2)}) collective-permute-start(bf16[4,64,3072]{2,1,0:T(8,128)(2,1)} %placed_blocks.1.mine_ref), channel_id=1, source_target_pairs={{0,1},{1,0},{2,3},{3,2},{4,5},{5,4},{6,7},{7,6},{8,9},{9,8},{10,11... | collective-permute-start | bytes 4718600 | tf_op jit(solution)/shard_map/ppermute | solution.py:24
  47.6 36.4 %collective-permute-start.4 = (bf16[4,64,3072]{2,1,0:T(8,128)(2,1)}, bf16[4,64,3072]{2,1,0:T(8,128)(2,1)}, u32[]{:S(2)}, u32[]{:S(2)}) collective-permute-start(bf16[4,64,3072]{2,1,0:T(8,128)(2,1)} %placed_blocks.1.mine_ref), channel_id=1, source_target_pairs={{0,16},{8,24},{16,0},{24,8},{1,17},{9,25},{17,1},{25,9},{2,18},{10... | collective-permute-start | bytes 4718600 | tf_op jit(solution)/shard_map/ppermute | solution.py:24
  82.6 7.9 %copy-start.9 = (bf16[4,64,3072]{2,1,0:T(8,128)(2,1)}, bf16[4,64,3072]{2,1,0:T(8,128)(2,1)S(1)}, u32[]{:S(2)}) copy-start(bf16[4,64,3072]{2,1,0:T(8,128)(2,1)S(1)} %collective-permute-done.5.theirs_ref) | copy-start | bytes 4718596
  84.0 64.4 %collective-permute-start.7 = (bf16[4,64,3072]{2,1,0:T(8,128)(2,1)}, bf16[4,64,3072]{2,1,0:T(8,128)(2,1)}, u32[]{:S(2)}, u32[]{:S(2)}) collective-permute-start(bf16[4,64,3072]{2,1,0:T(8,128)(2,1)} %collective-permute-done.4.mine_ref), channel_id=1, source_target_pairs={{0,1},{1,0},{2,3},{3,2},{4,5},{5,4},{6,7},{7,6},{8,9},{9,8},{10,11... | collective-permute-start | bytes 4718600 | tf_op jit(solution)/shard_map/ppermute | solution.py:24
  132.8 134.8 %all-to-all-start.1 = ((bf16[8,384,512]{2,1,0:T(8,128)(2,1)}), bf16[8,384,512]{2,1,0:T(8,128)(2,1)}, u32[]{:S(2)}, u32[]{:S(2)}) async-start(bf16[8,384,512]{2,1,0:T(8,128)(2,1)} %get-tuple-element.105), calls=%async_computation.1 | async-start | bytes 6291456 | tf_op jit(solution)/shard_map/all_to_all | solution.py:379
  142.7 48.9 %collective-permute-start.10 = (bf16[2,512,1024]{2,1,0:T(8,128)(2,1)}, bf16[2,512,1024]{2,1,0:T(8,128)(2,1)}, u32[]{:S(2)}, u32[]{:S(2)}) collective-permute-start(bf16[2,512,1024]{2,1,0:T(8,128)(2,1)} %get-tuple-element.87), channel_id=1, source_target_pairs={{0,16},{8,24},{16,0},{24,8},{1,17},{9,25},{17,1},{25,9},{2,18},{10... | collective-permute-start | bytes 6291464 | tf_op jit(solution)/shard_map/ppermute | solution.py:24
  148.4 45.9 %collective-permute-start.6 = (bf16[512,3072]{1,0:T(8,128)(2,1)}, bf16[512,3072]{1,0:T(8,128)(2,1)S(1)}, u32[]{:S(2)}, u32[]{:S(2)}) collective-permute-start(bf16[512,3072]{1,0:T(8,128)(2,1)} %bitcast.27), channel_id=1, source_target_pairs={{0,8},{8,0},{16,24},{24,16},{1,9},{9,1},{17,25},{25,17},{2,10},{10... | collective-permute-start | bytes 9437192 | tf_op jit(solution)/shard_map/ppermute | solution.py:24
  152.6 44.3 %collective-permute-start.8 = (bf16[512,3072]{1,0:T(8,128)(2,1)}, bf16[512,3072]{1,0:T(8,128)(2,1)}, u32[]{:S(2)}, u32[]{:S(2)}) collective-permute-start(bf16[512,3072]{1,0:T(8,128)(2,1)} %bitcast.31), channel_id=1, source_target_pairs={{0,8},{8,0},{16,24},{24,16},{1,9},{9,1},{17,25},{25,17},{2,10},{10... | collective-permute-start | bytes 9437192 | tf_op jit(solution)/shard_map/ppermute | solution.py:24
  157.8 89.9 %collective-permute-start.3 = (bf16[2,512,1024]{2,1,0:T(8,128)(2,1)}, bf16[2,512,1024]{2,1,0:T(8,128)(2,1)S(1)}, u32[]{:S(2)}, u32[]{:S(2)}) collective-permute-start(bf16[2,512,1024]{2,1,0:T(8,128)(2,1)} %get-tuple-element.71), channel_id=1, source_target_pairs={{0,16},{8,24},{16,0},{24,8},{1,17},{9,25},{17,1},{25,9},{2,18},{10... | collective-permute-start | bytes 6291464 | tf_op jit(solution)/shard_map/ppermute | solution.py:24
  158.3 35.9 %collective-permute-start.9 = (bf16[1,512,1024]{2,1,0:T(8,128)(2,1)}, bf16[1,512,1024]{2,1,0:T(8,128)(2,1)S(1)}, u32[]{:S(2)}, u32[]{:S(2)}) collective-permute-start(bf16[1,512,1024]{2,1,0:T(8,128)(2,1)} %get-tuple-element.86), channel_id=1, source_target_pairs={{0,8},{8,0},{16,24},{24,16},{1,9},{9,1},{17,25},{25,17},{2,10},{10... | collective-permute-start | bytes 3145736 | tf_op jit(solution)/shard_map/ppermute | solution.py:24
  194.3 2.7 collective-permute-start.11
  194.3 2.7 copy-start.10
  194.3 2.6 copy-start
  196.9 1.0 copy-start.13
  234.3 8.2 %copy-start.4 = (f32[528,1024]{1,0:T(8,128)S(1)}, f32[528,1024]{1,0:T(8,128)}, u32[]{:S(2)}) copy-start(f32[528,1024]{1,0:T(8,128)} %hidden_deriv.7) | copy-start | bytes 6488068
  242.5 2.0 copy-start.3
  244.5 2.0 copy-start.2
  246.5 1.5 copy-start.18
  248.0 2.7 collective-permute-start.15
  249.3 2.9 collective-permute-start.16
  250.6 1.5 copy-start.11
  252.1 1.0 copy-start.12
  267.5 75.8 %copy-start.17 = (s32[512,2]{0,1:T(2,128)S(1)}, s32[512,2]{0,1:T(2,128)}, u32[]{:S(2)}) copy-start(s32[512,2]{0,1:T(2,128)} %param.9) | copy-start | bytes 12292
  267.5 137.9 %all-to-all-start.2 = ((bf16[8,384,512]{2,1,0:T(8,128)(2,1)}), bf16[8,384,512]{2,1,0:T(8,128)(2,1)S(1)}, u32[]{:S(2)}, u32[]{:S(2)}) async-start(bf16[8,384,512]{2,1,0:T(8,128)(2,1)} %get-tuple-element.117), calls=%async_computation.2 | async-start | bytes 6291456 | tf_op jit(solution)/shard_map/all_to_all | solution.py:379
  273.6 69.7 %collective-permute-start.17 = (bf16[2,384,1024]{2,1,0:T(8,128)(2,1)}, bf16[2,384,1024]{2,1,0:T(8,128)(2,1)}, u32[]{:S(2)}, u32[]{:S(2)}) collective-permute-start(bf16[2,384,1024]{2,1,0:T(8,128)(2,1)} %get-tuple-element.114), channel_id=1, source_target_pairs={{0,1},{1,0},{2,3},{3,2},{4,5},{5,4},{6,7},{7,6},{8,9},{9,8},{10,11... | collective-permute-start | bytes 4718600 | tf_op jit(solution)/shard_map/ppermute | solution.py:24
  275.1 85.9 %collective-permute-start.18 = (bf16[2,384,1024]{2,1,0:T(8,128)(2,1)}, bf16[2,384,1024]{2,1,0:T(8,128)(2,1)}, u32[]{:S(2)}, u32[]{:S(2)}) collective-permute-start(bf16[2,384,1024]{2,1,0:T(8,128)(2,1)} %get-tuple-element.115), channel_id=1, source_target_pairs={{0,2},{1,3},{2,0},{3,1},{4,6},{5,7},{6,4},{7,5},{8,10},{9,11},{10,... | collective-permute-start | bytes 4718600 | tf_op jit(solution)/shard_map/ppermute | solution.py:24
  275.6 118.9 %collective-permute-start.19 = (bf16[2,384,1024]{2,1,0:T(8,128)(2,1)}, bf16[2,384,1024]{2,1,0:T(8,128)(2,1)}, u32[]{:S(2)}, u32[]{:S(2)}) collective-permute-start(bf16[2,384,1024]{2,1,0:T(8,128)(2,1)} %get-tuple-element.116), channel_id=1, source_target_pairs={{0,3},{1,2},{2,1},{3,0},{4,7},{5,6},{6,5},{7,4},{8,11},{9,10},{10,... | collective-permute-start | bytes 4718600 | tf_op jit(solution)/shard_map/ppermute | solution.py:24
  277.1 128.3 %collective-permute-start.12 = (f16[528,1024]{1,0:T(8,128)(2,1)}, f16[528,1024]{1,0:T(8,128)(2,1)}, u32[]{:S(2)}, u32[]{:S(2)}) collective-permute-start(f16[528,1024]{1,0:T(8,128)(2,1)} %convert_element_type.41), channel_id=1, source_target_pairs={{0,8},{8,0},{16,24},{24,16},{1,9},{9,1},{17,25},{25,17},{2,10},{10... | collective-permute-start | bytes 3244040 | tf_op jit(solution)/shard_map/ppermute | solution.py:24
  277.1 128.3 %collective-permute-start.13 = (f16[528,1024]{1,0:T(8,128)(2,1)}, f16[528,1024]{1,0:T(8,128)(2,1)}, u32[]{:S(2)}, u32[]{:S(2)}) collective-permute-start(f16[528,1024]{1,0:T(8,128)(2,1)} %convert_element_type.42), channel_id=1, source_target_pairs={{0,16},{8,24},{16,0},{24,8},{1,17},{9,25},{17,1},{25,9},{2,18},{10... | collective-permute-start | bytes 3244040 | tf_op jit(solution)/shard_map/ppermute | solution.py:24
  343.2 62.2 %collective-permute-start.14 = (f16[528,1024]{1,0:T(8,128)(2,1)}, f16[528,1024]{1,0:T(8,128)(2,1)}, u32[]{:S(2)}, u32[]{:S(2)}) collective-permute-start(f16[528,1024]{1,0:T(8,128)(2,1)} %convert_element_type.43), channel_id=1, source_target_pairs={{0,24},{8,16},{16,8},{24,0},{1,25},{9,17},{17,9},{25,1},{2,26},{10... | collective-permute-start | bytes 3244040 | tf_op jit(solution)/shard_map/ppermute | solution.py:24
  405.4 6.0 %copy-start.1 = (bf16[8,384,512]{2,1,0:T(8,128)(2,1)}, bf16[8,384,512]{2,1,0:T(8,128)(2,1)S(1)}, u32[]{:S(2)}) copy-start(bf16[8,384,512]{2,1,0:T(8,128)(2,1)S(1)} %all-to-all-done.2.weight_ref) | copy-start | bytes 9437188
  409.2 2.3 copy-start.5
  409.2 2.8 copy-start.7
  409.2 3.5 copy-start.8

commit v17 on v15

--- a/solution.py
+++ b/solution.py
@@ -259,39 +259,34 @@
             )
 
 
-def update(part, place, grads, weight, momentum, done):
-    sources, rows, some = weight.shape
+def update(place, grads, weight, momentum):
+    sources, rows, cols = weight.shape
     count = len(grads)
-    parts = grads[0].shape[2] // some
 
     def source(far, m, place):
         return place[0] ^ m ^ (far * count)
 
-    wide = pl.BlockSpec(
-        (1, rows, some), lambda far, m, place: (0, 0, source(far, m, place) * parts + part)
-    )
+    wide = pl.BlockSpec((1, rows, cols), lambda far, m, place: (0, 0, source(far, m, place)))
     return pl.pallas_call(
         functools.partial(update_kernel, count),
         grid_spec=pltpu.PrefetchScalarGridSpec(
             num_scalar_prefetch=1,
             grid=(2, count),
             in_specs=[
-                pl.BlockSpec((1, rows, some), lambda far, m, place: (source(far, m, place), 0, 0)),
+                pl.BlockSpec((1, rows, cols), lambda far, m, place: (source(far, m, place), 0, 0)),
                 wide,
             ]
-            + [pl.BlockSpec((1, rows, some), lambda far, m, place: (far, 0, part))] * count
-            + [pl.BlockSpec(memory_space=pl.ANY)] * len(done),
+            + [pl.BlockSpec((1, rows, cols), lambda far, m, place: (far, 0, 0))] * count,
             out_specs=[wide, wide],
         ),
         out_shape=[
             jax.ShapeDtypeStruct(momentum.shape, jnp.float32),
             jax.ShapeDtypeStruct(momentum.shape, jnp.bfloat16),
         ],
-        input_output_aliases={3 + count + i: i for i in range(len(done))},
         compiler_params=pltpu.CompilerParams(vmem_limit_bytes=56 * MIB),
         cost_estimate=SMALL,
         name="lion_step",
-    )(place.reshape(1), weight, momentum, *grads, *done)
+    )(place.reshape(1), weight, momentum, *grads)
 
 
 def body(out_grad, gate_saved, up_saved, routing, down_weight, momentum):
@@ -370,14 +365,13 @@
     other_rows = spread(other_picked, other_got, experts)
     both_terms = shard_terms(other_rows, own_terms)
 
-    parts = 2 if cols % 256 == 0 else 1
-    pieces = jnp.split(down_weight.reshape(shards, rows, cols), parts, axis=2)
-    weights = []
-    for part, piece in enumerate(pieces):
-        begun = [other_twice] if part == 0 else [weights[-1], both_terms]
-        weights.append(
-            lax.all_to_all(after(piece, *begun), "dp", split_axis=0, concat_axis=0, tiled=True)
-        )
+    weights = lax.all_to_all(
+        after(down_weight, other_twice).reshape(shards, rows, cols),
+        "dp",
+        split_axis=0,
+        concat_axis=0,
+        tiled=True,
+    )
 
     grads = [swapped(both_terms[m], "dp", m) for m in range(span)]
 
@@ -393,10 +387,7 @@
     d_up = (deriv * gate * sigma).astype(jnp.bfloat16)
     d_gate = (deriv * up * sigma * (1.0 + gate * (1.0 - sigma))).astype(jnp.bfloat16)
 
-    done = ()
-    for part in range(parts):
-        done = update(part, place, grads, weights[part], momentum, done)
-    new_weight, new_momentum = done
+    new_weight, new_momentum = update(place, grads, weights, momentum)
     return (d_gate, d_up, new_weight, new_momentum)
 
 

time: 379 us -> 356 us (0.939); the launches traced: 378 us -> 350 us
  waiting for transfers between devices: 182 us -> 174 us
  local copies, waits for them, and re-layouts: 24.6 us -> 16.8 us
  starting transfers between devices: 38.2 us -> 32.5 us
  Pallas kernels: 103 us -> 99.2 us
    all_to_all x2 -> x1, waiting for transfers between devices: 33.3 us -> 0.01 us  [body(): lax.all_to_all(after(down_weight, other_twice).reshape(shards, rows, cols...]
    ppermute x20, waiting for transfers between devices: 136 us -> 161 us  [swapped(): return lax.ppermute(array, axis, [(i, i ^ mask) for i in range(size)])]
    split x1 -> x0, local copies, waits for them, and re-layouts: 6.01 us -> none  [body(): pieces = jnp.split(down_weight.reshape(shards, rows, cols), parts, axis=2)]
    all_to_all x2 -> x1, starting transfers between devices: 16 us -> 10.3 us  [body(): lax.all_to_all(after(down_weight, other_twice).reshape(shards, rows, cols...]
    pallas_call x2 -> x1, Pallas kernels: 21.8 us -> 17.7 us  [update(): pl.pallas_call(functools.partial(update_kernel, count), grid_spec=pltpu.P...]
  transfers between devices with their start and end apart: 23 -> 22, of which waited for: 13 -> 13; matrix products, arithmetic and copies ran while one was open for 12% -> 11% of each run, Pallas kernels for 25% -> 23%
where the time goes in v17:
time: 356 us; the launch traced here: 350 us
  waiting for transfers between devices  174 us (49%)
  Pallas kernels  99.2 us (28%)
  starting transfers between devices  32.5 us (9%)
  other arithmetic  26.2 us (7%)
  local copies, waits for them, and re-layouts  16.8 us (5%)
    ppermute x20, waiting for transfers between devices, swapped(): return lax.ppermute(array, axis, [(i, i ^ mask) for i in range(size)])  161 us
    pallas_call x4, Pallas kernels, deriv_of(): pl.pallas_call(packed_kernel if packed else deriv_kernel, grid=(cols // w...  32.3 us
    pallas_call x2, Pallas kernels, terms(): pl.pallas_call(functools.partial(term_kernel, count, steps), grid_spec=pl...  26.6 us
    pallas_call x1, Pallas kernels, update(): pl.pallas_call(functools.partial(update_kernel, count), grid_spec=pltpu.P...  17.7 us
    ppermute x20, starting transfers between devices, swapped(): return lax.ppermute(array, axis, [(i, i ^ mask) for i in range(size)])  16.6 us
    convert_element_type x1, other arithmetic, body(): d_up = (deriv * gate * sigma).astype(jnp.bfloat16)  15.1 us
    all_to_all x1, waiting for transfers between devices, body(): lax.all_to_all(twice, 'dp', split_axis=0, concat_axis=0, tiled=True, axis...  13.8 us
    pallas_call x2, Pallas kernels, picked_rows(): pl.pallas_call(hidden_kernel if fresh else pick_kernel, grid_spec=pltpu.P...  11.7 us
  transfers between devices with their start and end apart: 22, of which 13 were waited for; matrix products, arithmetic and copies ran while one was open for 11% of the time, Pallas kernels for 23%

profile of v17, /device:TPU:8, one launch (start us, length us, event | category | flops | bytes accessed | tf_op | source)
XLA Modules:
  0.0 350.1 jit_solution(4390301915081408178)
XLA Ops:
  0.7 3.0 collective-permute-start.1
  3.7 0.5 collective-permute-start.2
  4.2 0.7 broadcast_xor_fusion
  5.0 0.8 reshape_reshape.10.named_ref
  5.8 4.3 %reshape.47.gate_ref = bf16[1024,1024]{1,0:T(8,128)(2,1)} reshape(bf16[512,2,1024]{2,1,0:T(2,128)(2,1)} %param.7) | data formatting | bytes 4194304 | tf_op jit(solution)/shard_map/reshape | solution.py:310
  10.1 2.2 reshape.48.up_ref
  12.2 7.0 %hidden_rows.2 = (bf16[2,1024,1024]{2,1,0:T(8,128)(2,1)}, bf16[1,512,1024]{2,1,0:T(8,128)(2,1)}, bf16[1,512,1024]{2,1,0:T(8,128)(2,1)}, bf16[2,512,1024]{2,1,0:T(8,128)(2,1)}) custom-call(s32[1]{0:T(128)} %bitcast.1.place_ref, bf16[1024,1024]{1,0:T(8,128)(2,1)} %reshape.47.gate_ref, bf16[1024,1024]{1,0:T(8,128)(2,1)} %reshape.48.up_ref, ...), custom_call_target="tpu_custom_call" | custom-call | flops 1024 | bytes 1024 | tf_op jit(solution)/shard_map/hidden_rows/pallas_call | solution.py:127
  19.3 11.2 %collective-permute-done.1.refs_2_ = bf16[64,3072]{1,0:T(8,128)(2,1)S(1)} collective-permute-done((bf16[64,3072]{1,0:T(8,128)(2,1)}, bf16[64,3072]{1,0:T(8,128)(2,1)S(1)}, u32[]{:S(2)}, u32[]{:S(2)}) %collective-permute-start.1) | collective-permute-done | bytes 393248 | tf_op jit(solution)/shard_map/ppermute | solution.py:24
  30.5 7.8 %collective-permute-done.2.refs_3_ = bf16[64,3072]{1,0:T(8,128)(2,1)S(1)} collective-permute-done((bf16[64,3072]{1,0:T(8,128)(2,1)}, bf16[64,3072]{1,0:T(8,128)(2,1)S(1)}, u32[]{:S(2)}, u32[]{:S(2)}) %collective-permute-start.2) | collective-permute-done | bytes 393248 | tf_op jit(solution)/shard_map/ppermute | solution.py:24
  38.3 0.8 copy-done.17
  39.1 5.6 %all-to-all-start = ((bf16[2,1024,1024]{2,1,0:T(8,128)(2,1)}), bf16[2,1024,1024]{2,1,0:T(8,128)(2,1)}, u32[]{:S(2)}, u32[]{:S(2)}) async-start(bf16[2,1024,1024]{2,1,0:T(8,128)(2,1)} %get-tuple-element.63), calls=%async_computation | async-start | bytes 8388608 | tf_op jit(solution)/shard_map/all_to_all | solution.py:319
  44.7 2.6 placed_blocks.1.mine_ref
  47.3 1.5 collective-permute-start.4
  48.8 1.5 collective-permute-start.5
  50.3 32.3 %collective-permute-done.4.mine_ref = bf16[4,64,3072]{2,1,0:T(8,128)(2,1)} collective-permute-done((bf16[4,64,3072]{2,1,0:T(8,128)(2,1)}, bf16[4,64,3072]{2,1,0:T(8,128)(2,1)}, u32[]{:S(2)}, u32[]{:S(2)}) %collective-permute-start.4) | collective-permute-done | bytes 1572896 | tf_op jit(solution)/shard_map/ppermute | solution.py:24
  82.6 1.1 collective-permute-done.5.theirs_ref
  83.7 1.5 collective-permute-start.7
  85.2 0.5 collective-permute-start.10
  85.8 4.2 %side_by_side.2 = bf16[4,2,64,3072]{3,2,1,0:T(8,128)(2,1)} custom-call(s32[1]{0:T(128)} %bitcast.2.place_ref, bf16[4,64,3072]{2,1,0:T(8,128)(2,1)} %placed_blocks.1.mine_ref, bf16[4,64,3072]{2,1,0:T(8,128)(2,1)} %copy-done.8), custom_call_target="tpu_custom_call" | custom-call | flops 1024 | bytes 1024 | tf_op jit(solution)/shard_map/side_by_side/pallas_call | solution.py:43
  89.9 28.0 %collective-permute-done.7.theirs_ref = bf16[4,64,3072]{2,1,0:T(8,128)(2,1)} collective-permute-done((bf16[4,64,3072]{2,1,0:T(8,128)(2,1)}, bf16[4,64,3072]{2,1,0:T(8,128)(2,1)}, u32[]{:S(2)}, u32[]{:S(2)}) %collective-permute-start.7) | collective-permute-done | bytes 1572896 | tf_op jit(solution)/shard_map/ppermute | solution.py:24
  117.9 13.8 %all-to-all-done.hidden_ref = bf16[2,1024,1024]{2,1,0:T(8,128)(2,1)} async-done(((bf16[2,1024,1024]{2,1,0:T(8,128)(2,1)}), bf16[2,1024,1024]{2,1,0:T(8,128)(2,1)}, u32[]{:S(2)}, u32[]{:S(2)}) %all-to-all-start) | async-done | bytes 4194336 | tf_op jit(solution)/shard_map/all_to_all | solution.py:319
  131.8 4.2 %side_by_side.3 = bf16[4,2,64,3072]{3,2,1,0:T(8,128)(2,1)} custom-call(s32[1]{0:T(128)} %bitcast.2.place_ref, bf16[4,64,3072]{2,1,0:T(8,128)(2,1)} %collective-permute-done.4.mine_ref, bf16[4,64,3072]{2,1,0:T(8,128)(2,1)} %collective-permute-done.7.theirs_ref), custom_call_target="tpu_custom_call" | custom-call | flops 1024 | bytes 1024 | tf_op jit(solution)/shard_map/side_by_side/pallas_call | solution.py:43
  136.0 10.3 %all-to-all-start.1 = ((bf16[8,384,1024]{2,1,0:T(8,128)(2,1)}), bf16[8,384,1024]{2,1,0:T(8,128)(2,1)}, u32[]{:S(2)}, u32[]{:S(2)}) async-start(bf16[8,384,1024]{2,1,0:T(8,128)(2,1)} %bitcast.22), calls=%async_computation.1 | async-start | bytes 12582912 | tf_op jit(solution)/shard_map/all_to_all | solution.py:368
  146.3 4.7 %hidden_rows.3 = (bf16[1,512,1024]{2,1,0:T(8,128)(2,1)}, bf16[1,512,1024]{2,1,0:T(8,128)(2,1)}, bf16[2,512,1024]{2,1,0:T(8,128)(2,1)}) custom-call(s32[1]{0:T(128)} %bitcast.place_ref, bf16[2,1024,1024]{2,1,0:T(8,128)(2,1)} %all-to-all-done.hidden_ref, s32[4,256]{1,0:T(4,128)} %reshape_reshape.10.named_ref), custom_call_target="tpu_custom_call" | custom-call | flops 1024 | bytes 1024 | tf_op jit(solution)/shard_map/hidden_rows/pallas_call | solution.py:127
  150.9 1.5 collective-permute-start.3
  152.4 2.7 fusion.18
  155.1 0.5 collective-permute-start.11
  155.6 2.3 collective-permute-done.11
  157.9 0.9 copy-done.14
  158.9 12.2 %group_terms.2 = (bf16[1,384,1024]{2,1,0:T(8,128)(2,1)}, bf16[1,384,1024]{2,1,0:T(8,128)(2,1)}, bf16[1,384,1024]{2,1,0:T(8,128)(2,1)}, bf16[1,384,1024]{2,1,0:T(8,128)(2,1)}) custom-call(s32[1]{0:T(128)} %bitcast.11.place_ref, bf16[512,3072]{1,0:T(8,128)(2,1)} %bitcast.28, bf16[512,3072]{1,0:T(8,128)(2,1)} %copy-done, bf16[512,3072]{1,0:T(8,128)(2,1)} %bitcast.32, ...), custom_call_target="tpu_custom_call" | custom-call | flops 1024 | bytes 1024 | tf_op jit(solution)/shard_map/group_terms/pallas_call | solution.py:182
  171.1 8.1 %hidden_deriv.7 = f32[528,1024]{1,0:T(8,128)} custom-call(bf16[512,3072]{1,0:T(8,128)(2,1)} %collective-permute-done.8.refs_3_.tokens_ref, bf16[3072,1024]{1,0:T(8,128)(2,1)} %bitcast.23), custom_call_target="tpu_custom_call" | custom-call | flops 1024 | bytes 1024 | tf_op jit(solution)/shard_map/hidden_deriv/pallas_call | solution.py:228
  179.2 8.1 %hidden_deriv.6 = f32[528,1024]{1,0:T(8,128)} custom-call(bf16[512,3072]{1,0:T(8,128)(2,1)} %bitcast.33, bf16[3072,1024]{1,0:T(8,128)(2,1)} %bitcast.24), custom_call_target="tpu_custom_call" | custom-call | flops 1024 | bytes 1024 | tf_op jit(solution)/shard_map/hidden_deriv/pallas_call | solution.py:228
  187.3 8.1 %hidden_deriv.5 = f32[528,1024]{1,0:T(8,128)} custom-call(bf16[512,3072]{1,0:T(8,128)(2,1)} %copy-done, bf16[3072,1024]{1,0:T(8,128)(2,1)} %bitcast.25), custom_call_target="tpu_custom_call" | custom-call | flops 1024 | bytes 1024 | tf_op jit(solution)/shard_map/hidden_deriv/pallas_call | solution.py:228
  195.4 8.0 %hidden_deriv.4 = f32[512,1024]{1,0:T(8,128)} custom-call(bf16[512,3072]{1,0:T(8,128)(2,1)} %bitcast.29, bf16[3072,1024]{1,0:T(8,128)(2,1)} %bitcast.26), custom_call_target="tpu_custom_call" | custom-call | flops 1024 | bytes 1024 | tf_op jit(solution)/shard_map/hidden_deriv/pallas_call | solution.py:228
  203.4 1.2 convert_element_type.43
  204.6 0.8 copy-done.2
  205.4 1.2 convert_element_type.42
  206.6 0.8 copy-done.1
  207.4 1.2 convert_element_type.41
  208.6 0.5 collective-permute-start.12
  209.1 1.2 fusion.17
  210.4 0.4 collective-permute-start.15
  210.8 1.5 collective-permute-start.13
  212.5 0.2 copy.17
  213.1 1.5 collective-permute-done.15
  214.6 1.0 copy-done.12
  215.6 14.4 %group_terms.3 = (bf16[2,384,1024]{2,1,0:T(8,128)(2,1)}, bf16[2,384,1024]{2,1,0:T(8,128)(2,1)}, bf16[2,384,1024]{2,1,0:T(8,128)(2,1)}, bf16[2,384,1024]{2,1,0:T(8,128)(2,1)}) custom-call(s32[1]{0:T(128)} %bitcast.11.place_ref, bf16[512,3072]{1,0:T(8,128)(2,1)} %bitcast.30, bf16[512,3072]{1,0:T(8,128)(2,1)} %copy-done, bf16[512,3072]{1,0:T(8,128)(2,1)} %bitcast.34, ...), custom_call_target="tpu_custom_call" | custom-call | flops 1024 | bytes 1024 | tf_op jit(solution)/shard_map/group_terms/pallas_call | solution.py:182
  230.0 1.5 collective-permute-start.17
  231.5 0.5 collective-permute-start.18
  232.0 2.6 collective-permute-done.12
  234.6 1.5 collective-permute-start.19
  236.1 0.7 fusion.16
  236.8 21.5 %collective-permute-done.13 = f16[528,1024]{1,0:T(8,128)(2,1)} collective-permute-done((f16[528,1024]{1,0:T(8,128)(2,1)}, f16[528,1024]{1,0:T(8,128)(2,1)}, u32[]{:S(2)}, u32[]{:S(2)}) %collective-permute-start.13) | collective-permute-done | bytes 1081376 | tf_op jit(solution)/shard_map/ppermute | solution.py:24
  258.3 0.7 fusion.13
  259.0 0.7 fusion.10
  259.7 1.5 convert_multiply_fusion.4
  261.2 1.6 convert_multiply_fusion.3
  262.9 1.6 convert_multiply_fusion.2
  264.5 0.5 copy-done.4
  265.0 15.1 %fusion.7 = (bf16[512,2,1024]{2,1,0:T(2,128)(2,1)}, bf16[512,2,1024]{2,1,0:T(2,128)(2,1)}) fusion(bf16[512,2,1024]{2,1,0:T(2,128)(2,1)S(1)} %copy-done.4, pred[512,2]{1,0:T(8,128)(4,1)S(1)} %copy.19, pred[512,2]{1,0:T(8,128)(4,1)S(1)} %copy.18, pred[512,2]{1,0:T(8,128)(4,1)S(1)} %copy.17, pred[512,2]{1,0:T(8,128)(4,1)S(1)} %copy.15, ...), kind=kLoop, calls=%fused_computation.10 | loop fusion | flops 19922944 | bytes 16781312 | tf_op jit(solution)/shard_map/convert_element_type | solution.py:387
  280.1 3.9 %collective-permute-done.17.refs_1_ = bf16[2,384,1024]{2,1,0:T(8,128)(2,1)S(1)} collective-permute-done((bf16[2,384,1024]{2,1,0:T(8,128)(2,1)}, bf16[2,384,1024]{2,1,0:T(8,128)(2,1)S(1)}, u32[]{:S(2)}, u32[]{:S(2)}) %collective-permute-start.17) | collective-permute-done | bytes 1572896 | tf_op jit(solution)/shard_map/ppermute | solution.py:24
  284.0 15.8 %collective-permute-done.18.refs_2_ = bf16[2,384,1024]{2,1,0:T(8,128)(2,1)S(1)} collective-permute-done((bf16[2,384,1024]{2,1,0:T(8,128)(2,1)}, bf16[2,384,1024]{2,1,0:T(8,128)(2,1)S(1)}, u32[]{:S(2)}, u32[]{:S(2)}) %collective-permute-start.18) | collective-permute-done | bytes 1572896 | tf_op jit(solution)/shard_map/ppermute | solution.py:24
  299.8 32.6 %collective-permute-done.19.refs_3_ = bf16[2,384,1024]{2,1,0:T(8,128)(2,1)} collective-permute-done((bf16[2,384,1024]{2,1,0:T(8,128)(2,1)}, bf16[2,384,1024]{2,1,0:T(8,128)(2,1)}, u32[]{:S(2)}, u32[]{:S(2)}) %collective-permute-start.19) | collective-permute-done | bytes 1572896 | tf_op jit(solution)/shard_map/ppermute | solution.py:24
  332.4 17.7 %lion_step.1 = (f32[1,384,8192]{2,1,0:T(8,128)}, bf16[1,384,8192]{2,1,0:T(8,128)(2,1)}) custom-call(s32[1]{0:T(128)} %bitcast.11.place_ref, bf16[8,384,1024]{2,1,0:T(8,128)(2,1)} %all-to-all-done.1.weight_ref, bf16[1,384,8192]{2,1,0:T(8,128)(2,1)} %momentum_ref.1, bf16[2,384,1024]{2,1,0:T(8,128)(2,1)} %get-tuple-element.108.refs_0_, ...), custom_call_target="tpu_custom_call" | custom-call | flops 1024 | bytes 1024 | tf_op jit(solution)/shard_map/lion_step/pallas_call | solution.py:270
  (52 shorter events, 1.1 us)
Async XLA Ops:
  0.6 18.6 %collective-permute-start = (bf16[64,3072]{1,0:T(8,128)(2,1)}, bf16[64,3072]{1,0:T(8,128)(2,1)S(1)}, u32[]{:S(2)}, u32[]{:S(2)}) collective-permute-start(bf16[64,3072]{1,0:T(8,128)(2,1)} %refs_0_), channel_id=1, source_target_pairs={{0,2},{1,3},{2,0},{3,1},{4,6},{5,7},{6,4},{7,5},{8,10},{9,11},{10,... | collective-permute-start | bytes 1179656 | tf_op jit(solution)/shard_map/ppermute | solution.py:24
  0.7 29.8 %collective-permute-start.1 = (bf16[64,3072]{1,0:T(8,128)(2,1)}, bf16[64,3072]{1,0:T(8,128)(2,1)S(1)}, u32[]{:S(2)}, u32[]{:S(2)}) collective-permute-start(bf16[64,3072]{1,0:T(8,128)(2,1)} %refs_0_), channel_id=1, source_target_pairs={{0,4},{1,5},{2,6},{3,7},{4,0},{5,1},{6,2},{7,3},{8,12},{9,13},{10,... | collective-permute-start | bytes 1179656 | tf_op jit(solution)/shard_map/ppermute | solution.py:24
  3.7 34.5 %collective-permute-start.2 = (bf16[64,3072]{1,0:T(8,128)(2,1)}, bf16[64,3072]{1,0:T(8,128)(2,1)S(1)}, u32[]{:S(2)}, u32[]{:S(2)}) collective-permute-start(bf16[64,3072]{1,0:T(8,128)(2,1)} %refs_0_), channel_id=1, source_target_pairs={{0,6},{1,7},{2,4},{3,5},{4,2},{5,3},{6,0},{7,1},{8,14},{9,15},{10,... | collective-permute-start | bytes 1179656 | tf_op jit(solution)/shard_map/ppermute | solution.py:24
  5.8 4.3 %copy-start.5 = (bf16[512,2,1024]{2,1,0:T(2,128)(2,1)S(1)}, bf16[512,2,1024]{2,1,0:T(2,128)(2,1)}, u32[]{:S(2)}) copy-start(bf16[512,2,1024]{2,1,0:T(2,128)(2,1)} %param.8) | copy-start | bytes 6291460
  19.3 19.0 %copy-start.15 = (bf16[64,3072]{1,0:T(8,128)(2,1)}, bf16[64,3072]{1,0:T(8,128)(2,1)S(1)}, u32[]{:S(2)}) copy-start(bf16[64,3072]{1,0:T(8,128)(2,1)S(1)} %collective-permute-done.refs_1_) | copy-start | bytes 1179652
  30.5 7.8 %copy-start.16 = (bf16[64,3072]{1,0:T(8,128)(2,1)}, bf16[64,3072]{1,0:T(8,128)(2,1)S(1)}, u32[]{:S(2)}) copy-start(bf16[64,3072]{1,0:T(8,128)(2,1)S(1)} %collective-permute-done.1.refs_2_) | copy-start | bytes 1179652
  38.3 0.8 copy-start.17
  39.1 92.7 %all-to-all-start = ((bf16[2,1024,1024]{2,1,0:T(8,128)(2,1)}), bf16[2,1024,1024]{2,1,0:T(8,128)(2,1)}, u32[]{:S(2)}, u32[]{:S(2)}) async-start(bf16[2,1024,1024]{2,1,0:T(8,128)(2,1)} %get-tuple-element.63), calls=%async_computation | async-start | bytes 8388608 | tf_op jit(solution)/shard_map/all_to_all | solution.py:319
  47.3 35.3 %collective-permute-start.4 = (bf16[4,64,3072]{2,1,0:T(8,128)(2,1)}, bf16[4,64,3072]{2,1,0:T(8,128)(2,1)}, u32[]{:S(2)}, u32[]{:S(2)}) collective-permute-start(bf16[4,64,3072]{2,1,0:T(8,128)(2,1)} %placed_blocks.1.mine_ref), channel_id=1, source_target_pairs={{0,16},{8,24},{16,0},{24,8},{1,17},{9,25},{17,1},{25,9},{2,18},{10... | collective-permute-start | bytes 4718600 | tf_op jit(solution)/shard_map/ppermute | solution.py:24
  48.8 34.9 %collective-permute-start.5 = (bf16[4,64,3072]{2,1,0:T(8,128)(2,1)}, bf16[4,64,3072]{2,1,0:T(8,128)(2,1)S(1)}, u32[]{:S(2)}, u32[]{:S(2)}) collective-permute-start(bf16[4,64,3072]{2,1,0:T(8,128)(2,1)} %placed_blocks.1.mine_ref), channel_id=1, source_target_pairs={{0,1},{1,0},{2,3},{3,2},{4,5},{5,4},{6,7},{7,6},{8,9},{9,8},{10,11... | collective-permute-start | bytes 4718600 | tf_op jit(solution)/shard_map/ppermute | solution.py:24
  83.7 2.1 copy-start.8
  83.7 34.2 %collective-permute-start.7 = (bf16[4,64,3072]{2,1,0:T(8,128)(2,1)}, bf16[4,64,3072]{2,1,0:T(8,128)(2,1)}, u32[]{:S(2)}, u32[]{:S(2)}) collective-permute-start(bf16[4,64,3072]{2,1,0:T(8,128)(2,1)} %collective-permute-done.4.mine_ref), channel_id=1, source_target_pairs={{0,1},{1,0},{2,3},{3,2},{4,5},{5,4},{6,7},{7,6},{8,9},{9,8},{10,11... | collective-permute-start | bytes 4718600 | tf_op jit(solution)/shard_map/ppermute | solution.py:24
  85.2 67.2 %collective-permute-start.10 = (bf16[2,512,1024]{2,1,0:T(8,128)(2,1)}, bf16[2,512,1024]{2,1,0:T(8,128)(2,1)}, u32[]{:S(2)}, u32[]{:S(2)}) collective-permute-start(bf16[2,512,1024]{2,1,0:T(8,128)(2,1)} %get-tuple-element.80), channel_id=1, source_target_pairs={{0,16},{8,24},{16,0},{24,8},{1,17},{9,25},{17,1},{25,9},{2,18},{10... | collective-permute-start | bytes 6291464 | tf_op jit(solution)/shard_map/ppermute | solution.py:24
  89.9 65.7 %collective-permute-start.6 = (bf16[512,3072]{1,0:T(8,128)(2,1)}, bf16[512,3072]{1,0:T(8,128)(2,1)S(1)}, u32[]{:S(2)}, u32[]{:S(2)}) collective-permute-start(bf16[512,3072]{1,0:T(8,128)(2,1)} %bitcast.27), channel_id=1, source_target_pairs={{0,8},{8,0},{16,24},{24,16},{1,9},{9,1},{17,25},{25,17},{2,10},{10... | collective-permute-start | bytes 9437192 | tf_op jit(solution)/shard_map/ppermute | solution.py:24
  136.0 21.9 %collective-permute-start.8 = (bf16[512,3072]{1,0:T(8,128)(2,1)}, bf16[512,3072]{1,0:T(8,128)(2,1)}, u32[]{:S(2)}, u32[]{:S(2)}) collective-permute-start(bf16[512,3072]{1,0:T(8,128)(2,1)} %bitcast.31), channel_id=1, source_target_pairs={{0,8},{8,0},{16,24},{24,16},{1,9},{9,1},{17,25},{25,17},{2,10},{10... | collective-permute-start | bytes 9437192 | tf_op jit(solution)/shard_map/ppermute | solution.py:24
  136.0 196.4 %all-to-all-start.1 = ((bf16[8,384,1024]{2,1,0:T(8,128)(2,1)}), bf16[8,384,1024]{2,1,0:T(8,128)(2,1)}, u32[]{:S(2)}, u32[]{:S(2)}) async-start(bf16[8,384,1024]{2,1,0:T(8,128)(2,1)} %bitcast.22), calls=%async_computation.1 | async-start | bytes 12582912 | tf_op jit(solution)/shard_map/all_to_all | solution.py:368
  150.9 57.7 %collective-permute-start.3 = (bf16[2,512,1024]{2,1,0:T(8,128)(2,1)}, bf16[2,512,1024]{2,1,0:T(8,128)(2,1)S(1)}, u32[]{:S(2)}, u32[]{:S(2)}) collective-permute-start(bf16[2,512,1024]{2,1,0:T(8,128)(2,1)} %get-tuple-element.64), channel_id=1, source_target_pairs={{0,16},{8,24},{16,0},{24,8},{1,17},{9,25},{17,1},{25,9},{2,18},{10... | collective-permute-start | bytes 6291464 | tf_op jit(solution)/shard_map/ppermute | solution.py:24
  152.4 3.2 collective-permute-start.9
  155.1 2.8 collective-permute-start.11
  155.6 2.3 copy-start.13
  155.6 2.3 copy-start
  157.9 1.0 copy-start.14
  195.4 8.0 %copy-start.3 = (f32[528,1024]{1,0:T(8,128)S(1)}, f32[528,1024]{1,0:T(8,128)}, u32[]{:S(2)}) copy-start(f32[528,1024]{1,0:T(8,128)} %hidden_deriv.7) | copy-start | bytes 6488068
  203.4 2.0 copy-start.2
  205.4 2.0 copy-start.1
  208.6 3.7 %copy-start.18 = (s32[512,2]{0,1:T(2,128)S(1)}, s32[512,2]{0,1:T(2,128)}, u32[]{:S(2)}) copy-start(s32[512,2]{0,1:T(2,128)} %param.9) | copy-start | bytes 12292
  208.6 26.0 %collective-permute-start.12 = (f16[528,1024]{1,0:T(8,128)(2,1)}, f16[528,1024]{1,0:T(8,128)(2,1)}, u32[]{:S(2)}, u32[]{:S(2)}) collective-permute-start(f16[528,1024]{1,0:T(8,128)(2,1)} %convert_element_type.43), channel_id=1, source_target_pairs={{0,24},{8,16},{16,8},{24,0},{1,25},{9,17},{17,9},{25,1},{2,26},{10... | collective-permute-start | bytes 3244040 | tf_op jit(solution)/shard_map/ppermute | solution.py:24
  210.3 2.8 collective-permute-start.16
  210.4 4.2 %collective-permute-start.15 = (bf16[1,512,1024]{2,1,0:T(8,128)(2,1)}, bf16[1,512,1024]{2,1,0:T(8,128)(2,1)S(1)}, u32[]{:S(2)}, u32[]{:S(2)}) collective-permute-start(bf16[1,512,1024]{2,1,0:T(8,128)(2,1)} %get-tuple-element.102), channel_id=1, source_target_pairs={{0,8},{8,0},{16,24},{24,16},{1,9},{9,1},{17,25},{25,17},{2,10},{10... | collective-permute-start | bytes 3145736 | tf_op jit(solution)/shard_map/ppermute | solution.py:24
  210.8 47.5 %collective-permute-start.13 = (f16[528,1024]{1,0:T(8,128)(2,1)}, f16[528,1024]{1,0:T(8,128)(2,1)}, u32[]{:S(2)}, u32[]{:S(2)}) collective-permute-start(f16[528,1024]{1,0:T(8,128)(2,1)} %convert_element_type.42), channel_id=1, source_target_pairs={{0,16},{8,24},{16,0},{24,8},{1,17},{9,25},{17,1},{25,9},{2,18},{10... | collective-permute-start | bytes 3244040 | tf_op jit(solution)/shard_map/ppermute | solution.py:24
  212.3 46.7 %collective-permute-start.14 = (f16[528,1024]{1,0:T(8,128)(2,1)}, f16[528,1024]{1,0:T(8,128)(2,1)}, u32[]{:S(2)}, u32[]{:S(2)}) collective-permute-start(f16[528,1024]{1,0:T(8,128)(2,1)} %convert_element_type.41), channel_id=1, source_target_pairs={{0,8},{8,0},{16,24},{24,16},{1,9},{9,1},{17,25},{25,17},{2,10},{10... | collective-permute-start | bytes 3244040 | tf_op jit(solution)/shard_map/ppermute | solution.py:24
  213.1 1.6 copy-start.11
  214.6 1.0 copy-start.12
  230.0 53.9 %collective-permute-start.17 = (bf16[2,384,1024]{2,1,0:T(8,128)(2,1)}, bf16[2,384,1024]{2,1,0:T(8,128)(2,1)S(1)}, u32[]{:S(2)}, u32[]{:S(2)}) collective-permute-start(bf16[2,384,1024]{2,1,0:T(8,128)(2,1)} %get-tuple-element.109), channel_id=1, source_target_pairs={{0,1},{1,0},{2,3},{3,2},{4,5},{5,4},{6,7},{7,6},{8,9},{9,8},{10,11... | collective-permute-start | bytes 4718600 | tf_op jit(solution)/shard_map/ppermute | solution.py:24
  231.5 68.3 %collective-permute-start.18 = (bf16[2,384,1024]{2,1,0:T(8,128)(2,1)}, bf16[2,384,1024]{2,1,0:T(8,128)(2,1)S(1)}, u32[]{:S(2)}, u32[]{:S(2)}) collective-permute-start(bf16[2,384,1024]{2,1,0:T(8,128)(2,1)} %get-tuple-element.110), channel_id=1, source_target_pairs={{0,2},{1,3},{2,0},{3,1},{4,6},{5,7},{6,4},{7,5},{8,10},{9,11},{10,... | collective-permute-start | bytes 4718600 | tf_op jit(solution)/shard_map/ppermute | solution.py:24
  234.6 97.8 %collective-permute-start.19 = (bf16[2,384,1024]{2,1,0:T(8,128)(2,1)}, bf16[2,384,1024]{2,1,0:T(8,128)(2,1)}, u32[]{:S(2)}, u32[]{:S(2)}) collective-permute-start(bf16[2,384,1024]{2,1,0:T(8,128)(2,1)} %get-tuple-element.111), channel_id=1, source_target_pairs={{0,3},{1,2},{2,1},{3,0},{4,7},{5,6},{6,5},{7,4},{8,11},{9,10},{10,... | collective-permute-start | bytes 4718600 | tf_op jit(solution)/shard_map/ppermute | solution.py:24
  261.2 3.3 copy-start.6
  261.2 3.3 copy-start.7
  262.9 2.1 copy-start.4
  284.0 48.4 %copy-start.9 = (bf16[2,384,1024]{2,1,0:T(8,128)(2,1)}, bf16[2,384,1024]{2,1,0:T(8,128)(2,1)S(1)}, u32[]{:S(2)}) copy-start(bf16[2,384,1024]{2,1,0:T(8,128)(2,1)S(1)} %collective-permute-done.17.refs_1_) | copy-start | bytes 4718596
  299.8 32.6 %copy-start.10 = (bf16[2,384,1024]{2,1,0:T(8,128)(2,1)}, bf16[2,384,1024]{2,1,0:T(8,128)(2,1)S(1)}, u32[]{:S(2)}) copy-start(bf16[2,384,1024]{2,1,0:T(8,128)(2,1)S(1)} %collective-permute-done.18.refs_2_) | copy-start | bytes 4718596

commit v18 on v17

--- a/solution.py
+++ b/solution.py
@@ -259,12 +259,12 @@
             )
 
 
-def update(place, grads, weight, momentum):
-    sources, rows, cols = weight.shape
+def update(place, begin, span, grads, weight, momentum, done):
+    _, rows, cols = weight.shape
     count = len(grads)
 
     def source(far, m, place):
-        return place[0] ^ m ^ (far * count)
+        return place[0] ^ (begin + m) ^ (far * span)
 
     wide = pl.BlockSpec((1, rows, cols), lambda far, m, place: (0, 0, source(far, m, place)))
     return pl.pallas_call(
@@ -276,17 +276,19 @@
                 pl.BlockSpec((1, rows, cols), lambda far, m, place: (source(far, m, place), 0, 0)),
                 wide,
             ]
-            + [pl.BlockSpec((1, rows, cols), lambda far, m, place: (far, 0, 0))] * count,
+            + [pl.BlockSpec((1, rows, cols), lambda far, m, place: (far, 0, 0))] * count
+            + [pl.BlockSpec(memory_space=pl.ANY)] * len(done),
             out_specs=[wide, wide],
         ),
         out_shape=[
             jax.ShapeDtypeStruct(momentum.shape, jnp.float32),
             jax.ShapeDtypeStruct(momentum.shape, jnp.bfloat16),
         ],
+        input_output_aliases={3 + count + i: i for i in range(len(done))},
         compiler_params=pltpu.CompilerParams(vmem_limit_bytes=56 * MIB),
         cost_estimate=SMALL,
         name="lion_step",
-    )(place.reshape(1), weight, momentum, *grads)
+    )(place.reshape(1), weight, momentum, *grads, *done)
 
 
 def body(out_grad, gate_saved, up_saved, routing, down_weight, momentum):
@@ -387,7 +389,11 @@
     d_up = (deriv * gate * sigma).astype(jnp.bfloat16)
     d_gate = (deriv * up * sigma * (1.0 + gate * (1.0 - sigma))).astype(jnp.bfloat16)
 
-    new_weight, new_momentum = update(place, grads, weights, momentum)
+    done = ()
+    for begin in range(0, span, span // 2):
+        some = grads[begin : begin + span // 2]
+        done = update(place, begin, span, some, weights, momentum, done)
+    new_weight, new_momentum = done
     return (d_gate, d_up, new_weight, new_momentum)
 
 

time: 356 us -> 346 us (0.972); the launches traced: 350 us -> 344 us
  waiting for transfers between devices: 174 us -> 164 us
    ppermute x20, waiting for transfers between devices: 161 us -> 151 us  [swapped(): return lax.ppermute(array, axis, [(i, i ^ mask) for i in range(size)])]
    pallas_call x1 -> x2, Pallas kernels: 17.7 us -> 19.1 us  [update(): pl.pallas_call(functools.partial(update_kernel, count), grid_spec=pltpu.P...]
  transfers between devices with their start and end apart: 22 -> 22, of which waited for: 13 -> 11; matrix products, arithmetic and copies ran while one was open for 11% -> 11% of each run, Pallas kernels for 23% -> 27%
where the time goes in v18:
time: 346 us; the launch traced here: 344 us
  waiting for transfers between devices  164 us (47%)
  Pallas kernels  101 us (29%)
  starting transfers between devices  33.4 us (10%)
  other arithmetic  26.2 us (8%)
  local copies, waits for them, and re-layouts  18.8 us (5%)
    ppermute x20, waiting for transfers between devices, swapped(): return lax.ppermute(array, axis, [(i, i ^ mask) for i in range(size)])  151 us
    pallas_call x4, Pallas kernels, deriv_of(): pl.pallas_call(packed_kernel if packed else deriv_kernel, grid=(cols // w...  32.4 us
    pallas_call x2, Pallas kernels, terms(): pl.pallas_call(functools.partial(term_kernel, count, steps), grid_spec=pl...  26.6 us
    pallas_call x2, Pallas kernels, update(): pl.pallas_call(functools.partial(update_kernel, count), grid_spec=pltpu.P...  19.1 us
    ppermute x20, starting transfers between devices, swapped(): return lax.ppermute(array, axis, [(i, i ^ mask) for i in range(size)])  17.5 us
    convert_element_type x1, other arithmetic, body(): d_up = (deriv * gate * sigma).astype(jnp.bfloat16)  15.1 us
    all_to_all x1, waiting for transfers between devices, body(): lax.all_to_all(twice, 'dp', split_axis=0, concat_axis=0, tiled=True, axis...  13.2 us
    pallas_call x2, Pallas kernels, picked_rows(): pl.pallas_call(hidden_kernel if fresh else pick_kernel, grid_spec=pltpu.P...  11.7 us
  transfers between devices with their start and end apart: 22, of which 11 were waited for; matrix products, arithmetic and copies ran while one was open for 11% of the time, Pallas kernels for 27%

profile of v18, /device:TPU:8, one launch (start us, length us, event | category | flops | bytes accessed | tf_op | source)
XLA Modules:
  0.0 343.8 jit_solution(5359139474377465936)
XLA Ops:
  0.6 2.7 collective-permute-start.1
  3.3 0.4 collective-permute-start
  3.7 0.5 collective-permute-start.2
  4.2 0.7 broadcast_xor_fusion
  5.0 0.8 reshape_reshape.10.named_ref
  5.8 4.3 %reshape.48.gate_ref = bf16[1024,1024]{1,0:T(8,128)(2,1)} reshape(bf16[512,2,1024]{2,1,0:T(2,128)(2,1)} %param.7) | data formatting | bytes 4194304 | tf_op jit(solution)/shard_map/reshape | solution.py:312
  10.1 2.2 reshape.49.up_ref
  12.3 7.0 %hidden_rows.2 = (bf16[2,1024,1024]{2,1,0:T(8,128)(2,1)}, bf16[1,512,1024]{2,1,0:T(8,128)(2,1)}, bf16[1,512,1024]{2,1,0:T(8,128)(2,1)}, bf16[2,512,1024]{2,1,0:T(8,128)(2,1)}) custom-call(s32[1]{0:T(128)} %bitcast.1.place_ref, bf16[1024,1024]{1,0:T(8,128)(2,1)} %reshape.48.gate_ref, bf16[1024,1024]{1,0:T(8,128)(2,1)} %reshape.49.up_ref, ...), custom_call_target="tpu_custom_call" | custom-call | flops 1024 | bytes 1024 | tf_op jit(solution)/shard_map/hidden_rows/pallas_call | solution.py:127
  19.3 2.0 collective-permute-done.1.refs_2_
  21.2 1.1 collective-permute-done.refs_1_
  22.4 14.7 %collective-permute-done.2.refs_3_ = bf16[64,3072]{1,0:T(8,128)(2,1)S(1)} collective-permute-done((bf16[64,3072]{1,0:T(8,128)(2,1)}, bf16[64,3072]{1,0:T(8,128)(2,1)S(1)}, u32[]{:S(2)}, u32[]{:S(2)}) %collective-permute-start.2) | collective-permute-done | bytes 393248 | tf_op jit(solution)/shard_map/ppermute | solution.py:24
  37.1 0.8 copy-done.17
  37.9 5.7 %all-to-all-start = ((bf16[2,1024,1024]{2,1,0:T(8,128)(2,1)}), bf16[2,1024,1024]{2,1,0:T(8,128)(2,1)}, u32[]{:S(2)}, u32[]{:S(2)}) async-start(bf16[2,1024,1024]{2,1,0:T(8,128)(2,1)} %get-tuple-element.65), calls=%async_computation | async-start | bytes 8388608 | tf_op jit(solution)/shard_map/all_to_all | solution.py:321
  43.6 2.6 placed_blocks.1.mine_ref
  46.2 1.5 collective-permute-start.5
  47.7 1.5 collective-permute-start.4
  49.2 33.5 %collective-permute-done.5.theirs_ref = bf16[4,64,3072]{2,1,0:T(8,128)(2,1)S(1)} collective-permute-done((bf16[4,64,3072]{2,1,0:T(8,128)(2,1)}, bf16[4,64,3072]{2,1,0:T(8,128)(2,1)S(1)}, u32[]{:S(2)}, u32[]{:S(2)}) %collective-permute-start.5) | collective-permute-done | bytes 1572896 | tf_op jit(solution)/shard_map/ppermute | solution.py:24
  82.7 1.3 collective-permute-done.4.mine_ref
  84.1 0.5 collective-permute-start.7
  84.6 1.5 collective-permute-start.10
  86.1 4.2 %side_by_side.2 = bf16[4,2,64,3072]{3,2,1,0:T(8,128)(2,1)} custom-call(s32[1]{0:T(128)} %bitcast.2.place_ref, bf16[4,64,3072]{2,1,0:T(8,128)(2,1)} %placed_blocks.1.mine_ref, bf16[4,64,3072]{2,1,0:T(8,128)(2,1)} %copy-done.10), custom_call_target="tpu_custom_call" | custom-call | flops 1024 | bytes 1024 | tf_op jit(solution)/shard_map/side_by_side/pallas_call | solution.py:43
  90.2 29.3 %collective-permute-done.7.theirs_ref = bf16[4,64,3072]{2,1,0:T(8,128)(2,1)} collective-permute-done((bf16[4,64,3072]{2,1,0:T(8,128)(2,1)}, bf16[4,64,3072]{2,1,0:T(8,128)(2,1)}, u32[]{:S(2)}, u32[]{:S(2)}) %collective-permute-start.7) | collective-permute-done | bytes 1572896 | tf_op jit(solution)/shard_map/ppermute | solution.py:24
  119.5 13.2 %all-to-all-done.hidden_ref = bf16[2,1024,1024]{2,1,0:T(8,128)(2,1)} async-done(((bf16[2,1024,1024]{2,1,0:T(8,128)(2,1)}), bf16[2,1024,1024]{2,1,0:T(8,128)(2,1)}, u32[]{:S(2)}, u32[]{:S(2)}) %all-to-all-start) | async-done | bytes 4194336 | tf_op jit(solution)/shard_map/all_to_all | solution.py:321
  132.8 4.2 %side_by_side.3 = bf16[4,2,64,3072]{3,2,1,0:T(8,128)(2,1)} custom-call(s32[1]{0:T(128)} %bitcast.2.place_ref, bf16[4,64,3072]{2,1,0:T(8,128)(2,1)} %collective-permute-done.4.mine_ref, bf16[4,64,3072]{2,1,0:T(8,128)(2,1)} %collective-permute-done.7.theirs_ref), custom_call_target="tpu_custom_call" | custom-call | flops 1024 | bytes 1024 | tf_op jit(solution)/shard_map/side_by_side/pallas_call | solution.py:43
  137.0 10.2 %all-to-all-start.1 = ((bf16[8,384,1024]{2,1,0:T(8,128)(2,1)}), bf16[8,384,1024]{2,1,0:T(8,128)(2,1)}, u32[]{:S(2)}, u32[]{:S(2)}) async-start(bf16[8,384,1024]{2,1,0:T(8,128)(2,1)} %bitcast.22), calls=%async_computation.1 | async-start | bytes 12582912 | tf_op jit(solution)/shard_map/all_to_all | solution.py:370
  147.2 4.7 %hidden_rows.3 = (bf16[1,512,1024]{2,1,0:T(8,128)(2,1)}, bf16[1,512,1024]{2,1,0:T(8,128)(2,1)}, bf16[2,512,1024]{2,1,0:T(8,128)(2,1)}) custom-call(s32[1]{0:T(128)} %bitcast.place_ref, bf16[2,1024,1024]{2,1,0:T(8,128)(2,1)} %all-to-all-done.hidden_ref, s32[4,256]{1,0:T(4,128)} %reshape_reshape.10.named_ref), custom_call_target="tpu_custom_call" | custom-call | flops 1024 | bytes 1024 | tf_op jit(solution)/shard_map/hidden_rows/pallas_call | solution.py:127
  151.9 1.5 collective-permute-start.3
  153.4 2.7 fusion.18
  156.1 0.5 collective-permute-start.11
  156.6 2.3 collective-permute-done.11
  158.9 1.0 copy-done.14
  159.8 12.3 %group_terms.2 = (bf16[1,384,1024]{2,1,0:T(8,128)(2,1)}, bf16[1,384,1024]{2,1,0:T(8,128)(2,1)}, bf16[1,384,1024]{2,1,0:T(8,128)(2,1)}, bf16[1,384,1024]{2,1,0:T(8,128)(2,1)}) custom-call(s32[1]{0:T(128)} %bitcast.11.place_ref, bf16[512,3072]{1,0:T(8,128)(2,1)} %bitcast.28, bf16[512,3072]{1,0:T(8,128)(2,1)} %copy-done, bf16[512,3072]{1,0:T(8,128)(2,1)} %bitcast.32, ...), custom_call_target="tpu_custom_call" | custom-call | flops 1024 | bytes 1024 | tf_op jit(solution)/shard_map/group_terms/pallas_call | solution.py:182
  172.1 7.9 %hidden_deriv.4 = f32[512,1024]{1,0:T(8,128)} custom-call(bf16[512,3072]{1,0:T(8,128)(2,1)} %bitcast.29, bf16[3072,1024]{1,0:T(8,128)(2,1)} %bitcast.23), custom_call_target="tpu_custom_call" | custom-call | flops 1024 | bytes 1024 | tf_op jit(solution)/shard_map/hidden_deriv/pallas_call | solution.py:228
  180.0 8.1 %hidden_deriv.7 = f32[528,1024]{1,0:T(8,128)} custom-call(bf16[512,3072]{1,0:T(8,128)(2,1)} %collective-permute-done.8.refs_3_.tokens_ref, bf16[3072,1024]{1,0:T(8,128)(2,1)} %bitcast.24), custom_call_target="tpu_custom_call" | custom-call | flops 1024 | bytes 1024 | tf_op jit(solution)/shard_map/hidden_deriv/pallas_call | solution.py:228
  188.1 8.1 %hidden_deriv.6 = f32[528,1024]{1,0:T(8,128)} custom-call(bf16[512,3072]{1,0:T(8,128)(2,1)} %bitcast.33, bf16[3072,1024]{1,0:T(8,128)(2,1)} %bitcast.25), custom_call_target="tpu_custom_call" | custom-call | flops 1024 | bytes 1024 | tf_op jit(solution)/shard_map/hidden_deriv/pallas_call | solution.py:228
  196.2 8.3 %hidden_deriv.5 = f32[528,1024]{1,0:T(8,128)} custom-call(bf16[512,3072]{1,0:T(8,128)(2,1)} %copy-done, bf16[3072,1024]{1,0:T(8,128)(2,1)} %bitcast.26), custom_call_target="tpu_custom_call" | custom-call | flops 1024 | bytes 1024 | tf_op jit(solution)/shard_map/hidden_deriv/pallas_call | solution.py:228
  204.5 1.2 convert_element_type.43
  205.7 0.8 copy-done.2
  206.5 1.2 convert_element_type.42
  207.6 0.8 copy-done.1
  208.5 1.2 convert_element_type.41
  209.7 0.4 collective-permute-start.15
  210.3 1.1 fusion.17
  211.5 0.4 collective-permute-start.16
  211.8 1.5 collective-permute-start.13
  214.2 0.9 copy-done.11
  215.5 14.3 %group_terms.3 = (bf16[2,384,1024]{2,1,0:T(8,128)(2,1)}, bf16[2,384,1024]{2,1,0:T(8,128)(2,1)}, bf16[2,384,1024]{2,1,0:T(8,128)(2,1)}, bf16[2,384,1024]{2,1,0:T(8,128)(2,1)}) custom-call(s32[1]{0:T(128)} %bitcast.11.place_ref, bf16[512,3072]{1,0:T(8,128)(2,1)} %bitcast.30, bf16[512,3072]{1,0:T(8,128)(2,1)} %copy-done, bf16[512,3072]{1,0:T(8,128)(2,1)} %bitcast.34, ...), custom_call_target="tpu_custom_call" | custom-call | flops 1024 | bytes 1024 | tf_op jit(solution)/shard_map/group_terms/pallas_call | solution.py:182
  230.1 2.6 collective-permute-start.18
  232.7 3.5 %collective-permute-done.12 = f16[528,1024]{1,0:T(8,128)(2,1)} collective-permute-done((f16[528,1024]{1,0:T(8,128)(2,1)}, f16[528,1024]{1,0:T(8,128)(2,1)}, u32[]{:S(2)}, u32[]{:S(2)}) %collective-permute-start.12) | collective-permute-done | bytes 1081376 | tf_op jit(solution)/shard_map/ppermute | solution.py:24
  236.2 1.5 collective-permute-start.19
  237.7 0.7 fusion.16
  238.4 21.3 %collective-permute-done.13 = f16[528,1024]{1,0:T(8,128)(2,1)} collective-permute-done((f16[528,1024]{1,0:T(8,128)(2,1)}, f16[528,1024]{1,0:T(8,128)(2,1)}, u32[]{:S(2)}, u32[]{:S(2)}) %collective-permute-start.13) | collective-permute-done | bytes 1081376 | tf_op jit(solution)/shard_map/ppermute | solution.py:24
  259.7 0.7 fusion.13
  260.4 0.7 fusion.10
  261.2 1.5 convert_multiply_fusion.4
  262.7 1.6 convert_multiply_fusion.3
  264.3 1.6 convert_multiply_fusion.2
  266.0 0.5 copy-done.4
  266.4 15.1 %fusion.7 = (bf16[512,2,1024]{2,1,0:T(2,128)(2,1)}, bf16[512,2,1024]{2,1,0:T(2,128)(2,1)}) fusion(bf16[512,2,1024]{2,1,0:T(2,128)(2,1)S(1)} %copy-done.4, pred[512,2]{1,0:T(8,128)(4,1)S(1)} %copy.21, pred[512,2]{1,0:T(8,128)(4,1)S(1)} %copy.20, pred[512,2]{1,0:T(8,128)(4,1)S(1)} %copy.19, pred[512,2]{1,0:T(8,128)(4,1)S(1)} %copy.17, ...), kind=kLoop, calls=%fused_computation.10 | loop fusion | flops 19922944 | bytes 16781312 | tf_op jit(solution)/shard_map/convert_element_type | solution.py:389
  281.5 41.5 %collective-permute-done.19.refs_1_ = bf16[2,384,1024]{2,1,0:T(8,128)(2,1)} collective-permute-done((bf16[2,384,1024]{2,1,0:T(8,128)(2,1)}, bf16[2,384,1024]{2,1,0:T(8,128)(2,1)}, u32[]{:S(2)}, u32[]{:S(2)}) %collective-permute-start.19) | collective-permute-done | bytes 1572896 | tf_op jit(solution)/shard_map/ppermute | solution.py:24
  323.0 9.7 %lion_step.2 = (f32[1,384,8192]{2,1,0:T(8,128)}, bf16[1,384,8192]{2,1,0:T(8,128)(2,1)}) custom-call(s32[1]{0:T(128)} %bitcast.11.place_ref, bf16[8,384,1024]{2,1,0:T(8,128)(2,1)} %all-to-all-done.1.weight_ref, bf16[1,384,8192]{2,1,0:T(8,128)(2,1)} %momentum_ref.3, bf16[2,384,1024]{2,1,0:T(8,128)(2,1)} %get-tuple-element.112.refs_0_, ...), custom_call_target="tpu_custom_call" | custom-call | flops 1024 | bytes 1024 | tf_op jit(solution)/shard_map/lion_step/pallas_call | solution.py:270
  332.7 1.2 copy-done.8
  333.9 0.4 copy-done.9
  334.4 9.4 %lion_step.3 = (f32[1,384,8192]{2,1,0:T(8,128)}, bf16[1,384,8192]{2,1,0:T(8,128)(2,1)}) custom-call(s32[1]{0:T(128)} %bitcast.11.place_ref, bf16[8,384,1024]{2,1,0:T(8,128)(2,1)} %all-to-all-done.1.weight_ref, bf16[1,384,8192]{2,1,0:T(8,128)(2,1)} %momentum_ref.3, bf16[2,384,1024]{2,1,0:T(8,128)(2,1)} %copy-done.8, ...), custom_call_target="tpu_custom_call", output_to_operand_aliasing={{0}: (5, {}), {1}: (6, {})} | custom-call | flops 1024 | bytes 1024 | tf_op jit(solution)/shard_map/lion_step/pallas_call | solution.py:270
  (53 shorter events, 2.0 us)
Async XLA Ops:
  0.6 20.6 %collective-permute-start.1 = (bf16[64,3072]{1,0:T(8,128)(2,1)}, bf16[64,3072]{1,0:T(8,128)(2,1)S(1)}, u32[]{:S(2)}, u32[]{:S(2)}) collective-permute-start(bf16[64,3072]{1,0:T(8,128)(2,1)} %refs_0_), channel_id=1, source_target_pairs={{0,4},{1,5},{2,6},{3,7},{4,0},{5,1},{6,2},{7,3},{8,12},{9,13},{10,... | collective-permute-start | bytes 1179656 | tf_op jit(solution)/shard_map/ppermute | solution.py:24
  3.3 19.1 %collective-permute-start = (bf16[64,3072]{1,0:T(8,128)(2,1)}, bf16[64,3072]{1,0:T(8,128)(2,1)S(1)}, u32[]{:S(2)}, u32[]{:S(2)}) collective-permute-start(bf16[64,3072]{1,0:T(8,128)(2,1)} %refs_0_), channel_id=1, source_target_pairs={{0,2},{1,3},{2,0},{3,1},{4,6},{5,7},{6,4},{7,5},{8,10},{9,11},{10,... | collective-permute-start | bytes 1179656 | tf_op jit(solution)/shard_map/ppermute | solution.py:24
  3.7 33.4 %collective-permute-start.2 = (bf16[64,3072]{1,0:T(8,128)(2,1)}, bf16[64,3072]{1,0:T(8,128)(2,1)S(1)}, u32[]{:S(2)}, u32[]{:S(2)}) collective-permute-start(bf16[64,3072]{1,0:T(8,128)(2,1)} %refs_0_), channel_id=1, source_target_pairs={{0,6},{1,7},{2,4},{3,5},{4,2},{5,3},{6,0},{7,1},{8,14},{9,15},{10,... | collective-permute-start | bytes 1179656 | tf_op jit(solution)/shard_map/ppermute | solution.py:24
  5.8 4.3 %copy-start.5 = (bf16[512,2,1024]{2,1,0:T(2,128)(2,1)S(1)}, bf16[512,2,1024]{2,1,0:T(2,128)(2,1)}, u32[]{:S(2)}) copy-start(bf16[512,2,1024]{2,1,0:T(2,128)(2,1)} %param.8) | copy-start | bytes 6291460
  21.2 15.9 %copy-start.15 = (bf16[64,3072]{1,0:T(8,128)(2,1)}, bf16[64,3072]{1,0:T(8,128)(2,1)S(1)}, u32[]{:S(2)}) copy-start(bf16[64,3072]{1,0:T(8,128)(2,1)S(1)} %collective-permute-done.1.refs_2_) | copy-start | bytes 1179652
  22.4 14.8 %copy-start.16 = (bf16[64,3072]{1,0:T(8,128)(2,1)}, bf16[64,3072]{1,0:T(8,128)(2,1)S(1)}, u32[]{:S(2)}) copy-start(bf16[64,3072]{1,0:T(8,128)(2,1)S(1)} %collective-permute-done.refs_1_) | copy-start | bytes 1179652
  37.1 0.8 copy-start.17
  37.9 94.9 %all-to-all-start = ((bf16[2,1024,1024]{2,1,0:T(8,128)(2,1)}), bf16[2,1024,1024]{2,1,0:T(8,128)(2,1)}, u32[]{:S(2)}, u32[]{:S(2)}) async-start(bf16[2,1024,1024]{2,1,0:T(8,128)(2,1)} %get-tuple-element.65), calls=%async_computation | async-start | bytes 8388608 | tf_op jit(solution)/shard_map/all_to_all | solution.py:321
  46.2 36.5 %collective-permute-start.5 = (bf16[4,64,3072]{2,1,0:T(8,128)(2,1)}, bf16[4,64,3072]{2,1,0:T(8,128)(2,1)S(1)}, u32[]{:S(2)}, u32[]{:S(2)}) collective-permute-start(bf16[4,64,3072]{2,1,0:T(8,128)(2,1)} %placed_blocks.1.mine_ref), channel_id=1, source_target_pairs={{0,1},{1,0},{2,3},{3,2},{4,5},{5,4},{6,7},{7,6},{8,9},{9,8},{10,11... | collective-permute-start | bytes 4718600 | tf_op jit(solution)/shard_map/ppermute | solution.py:24
  47.7 36.4 %collective-permute-start.4 = (bf16[4,64,3072]{2,1,0:T(8,128)(2,1)}, bf16[4,64,3072]{2,1,0:T(8,128)(2,1)}, u32[]{:S(2)}, u32[]{:S(2)}) collective-permute-start(bf16[4,64,3072]{2,1,0:T(8,128)(2,1)} %placed_blocks.1.mine_ref), channel_id=1, source_target_pairs={{0,16},{8,24},{16,0},{24,8},{1,17},{9,25},{17,1},{25,9},{2,18},{10... | collective-permute-start | bytes 4718600 | tf_op jit(solution)/shard_map/ppermute | solution.py:24
  82.7 3.3 copy-start.10
  84.1 35.5 %collective-permute-start.7 = (bf16[4,64,3072]{2,1,0:T(8,128)(2,1)}, bf16[4,64,3072]{2,1,0:T(8,128)(2,1)}, u32[]{:S(2)}, u32[]{:S(2)}) collective-permute-start(bf16[4,64,3072]{2,1,0:T(8,128)(2,1)} %collective-permute-done.4.mine_ref), channel_id=1, source_target_pairs={{0,1},{1,0},{2,3},{3,2},{4,5},{5,4},{6,7},{7,6},{8,9},{9,8},{10,11... | collective-permute-start | bytes 4718600 | tf_op jit(solution)/shard_map/ppermute | solution.py:24
  84.6 68.8 %collective-permute-start.10 = (bf16[2,512,1024]{2,1,0:T(8,128)(2,1)}, bf16[2,512,1024]{2,1,0:T(8,128)(2,1)}, u32[]{:S(2)}, u32[]{:S(2)}) collective-permute-start(bf16[2,512,1024]{2,1,0:T(8,128)(2,1)} %get-tuple-element.82), channel_id=1, source_target_pairs={{0,16},{8,24},{16,0},{24,8},{1,17},{9,25},{17,1},{25,9},{2,18},{10... | collective-permute-start | bytes 6291464 | tf_op jit(solution)/shard_map/ppermute | solution.py:24
  90.2 66.4 %collective-permute-start.6 = (bf16[512,3072]{1,0:T(8,128)(2,1)}, bf16[512,3072]{1,0:T(8,128)(2,1)S(1)}, u32[]{:S(2)}, u32[]{:S(2)}) collective-permute-start(bf16[512,3072]{1,0:T(8,128)(2,1)} %bitcast.27), channel_id=1, source_target_pairs={{0,8},{8,0},{16,24},{24,16},{1,9},{9,1},{17,25},{25,17},{2,10},{10... | collective-permute-start | bytes 9437192 | tf_op jit(solution)/shard_map/ppermute | solution.py:24
  136.9 21.9 %collective-permute-start.8 = (bf16[512,3072]{1,0:T(8,128)(2,1)}, bf16[512,3072]{1,0:T(8,128)(2,1)}, u32[]{:S(2)}, u32[]{:S(2)}) collective-permute-start(bf16[512,3072]{1,0:T(8,128)(2,1)} %bitcast.31), channel_id=1, source_target_pairs={{0,8},{8,0},{16,24},{24,16},{1,9},{9,1},{17,25},{25,17},{2,10},{10... | collective-permute-start | bytes 9437192 | tf_op jit(solution)/shard_map/ppermute | solution.py:24
  137.0 186.0 %all-to-all-start.1 = ((bf16[8,384,1024]{2,1,0:T(8,128)(2,1)}), bf16[8,384,1024]{2,1,0:T(8,128)(2,1)}, u32[]{:S(2)}, u32[]{:S(2)}) async-start(bf16[8,384,1024]{2,1,0:T(8,128)(2,1)} %bitcast.22), calls=%async_computation.1 | async-start | bytes 12582912 | tf_op jit(solution)/shard_map/all_to_all | solution.py:370
  151.9 57.8 %collective-permute-start.3 = (bf16[2,512,1024]{2,1,0:T(8,128)(2,1)}, bf16[2,512,1024]{2,1,0:T(8,128)(2,1)S(1)}, u32[]{:S(2)}, u32[]{:S(2)}) collective-permute-start(bf16[2,512,1024]{2,1,0:T(8,128)(2,1)} %get-tuple-element.66), channel_id=1, source_target_pairs={{0,16},{8,24},{16,0},{24,8},{1,17},{9,25},{17,1},{25,9},{2,18},{10... | collective-permute-start | bytes 6291464 | tf_op jit(solution)/shard_map/ppermute | solution.py:24
  153.3 3.2 collective-permute-start.9
  156.1 2.8 collective-permute-start.11
  156.6 2.3 copy-start.13
  156.6 2.3 copy-start
  158.9 1.0 copy-start.14
  196.2 8.3 %copy-start.3 = (f32[528,1024]{1,0:T(8,128)S(1)}, f32[528,1024]{1,0:T(8,128)}, u32[]{:S(2)}) copy-start(f32[528,1024]{1,0:T(8,128)} %hidden_deriv.7) | copy-start | bytes 6488068
  204.5 2.0 copy-start.2
  206.5 2.0 copy-start.1
  209.7 3.7 %copy-start.18 = (s32[512,2]{0,1:T(2,128)S(1)}, s32[512,2]{0,1:T(2,128)}, u32[]{:S(2)}) copy-start(s32[512,2]{0,1:T(2,128)} %param.9) | copy-start | bytes 12292
  209.7 4.5 %collective-permute-start.15 = (bf16[1,512,1024]{2,1,0:T(8,128)(2,1)}, bf16[1,512,1024]{2,1,0:T(8,128)(2,1)S(1)}, u32[]{:S(2)}, u32[]{:S(2)}) collective-permute-start(bf16[1,512,1024]{2,1,0:T(8,128)(2,1)} %get-tuple-element.104), channel_id=1, source_target_pairs={{0,8},{8,0},{16,24},{24,16},{1,9},{9,1},{17,25},{25,17},{2,10},{10... | collective-permute-start | bytes 3145736 | tf_op jit(solution)/shard_map/ppermute | solution.py:24
  210.0 26.2 %collective-permute-start.12 = (f16[528,1024]{1,0:T(8,128)(2,1)}, f16[528,1024]{1,0:T(8,128)(2,1)}, u32[]{:S(2)}, u32[]{:S(2)}) collective-permute-start(f16[528,1024]{1,0:T(8,128)(2,1)} %convert_element_type.43), channel_id=1, source_target_pairs={{0,24},{8,16},{16,8},{24,0},{1,25},{9,17},{17,9},{25,1},{2,26},{10... | collective-permute-start | bytes 3244040 | tf_op jit(solution)/shard_map/ppermute | solution.py:24
  211.5 2.7 collective-permute-start.16
  211.8 47.9 %collective-permute-start.13 = (f16[528,1024]{1,0:T(8,128)(2,1)}, f16[528,1024]{1,0:T(8,128)(2,1)}, u32[]{:S(2)}, u32[]{:S(2)}) collective-permute-start(f16[528,1024]{1,0:T(8,128)(2,1)} %convert_element_type.42), channel_id=1, source_target_pairs={{0,16},{8,24},{16,0},{24,8},{1,17},{9,25},{17,1},{25,9},{2,18},{10... | collective-permute-start | bytes 3244040 | tf_op jit(solution)/shard_map/ppermute | solution.py:24
  213.3 47.1 %collective-permute-start.14 = (f16[528,1024]{1,0:T(8,128)(2,1)}, f16[528,1024]{1,0:T(8,128)(2,1)}, u32[]{:S(2)}, u32[]{:S(2)}) collective-permute-start(f16[528,1024]{1,0:T(8,128)(2,1)} %convert_element_type.41), channel_id=1, source_target_pairs={{0,8},{8,0},{16,24},{24,16},{1,9},{9,1},{17,25},{25,17},{2,10},{10... | collective-permute-start | bytes 3244040 | tf_op jit(solution)/shard_map/ppermute | solution.py:24
  214.1 1.0 copy-start.11
  214.2 1.3 copy-start.12
  229.8 102.9 %collective-permute-start.17 = (bf16[2,384,1024]{2,1,0:T(8,128)(2,1)}, bf16[2,384,1024]{2,1,0:T(8,128)(2,1)S(1)}, u32[]{:S(2)}, u32[]{:S(2)}) collective-permute-start(bf16[2,384,1024]{2,1,0:T(8,128)(2,1)} %get-tuple-element.110), channel_id=1, source_target_pairs={{0,2},{1,3},{2,0},{3,1},{4,6},{5,7},{6,4},{7,5},{8,10},{9,11},{10,... | collective-permute-start | bytes 4718600 | tf_op jit(solution)/shard_map/ppermute | solution.py:24
  230.1 102.6 %collective-permute-start.18 = (bf16[2,384,1024]{2,1,0:T(8,128)(2,1)}, bf16[2,384,1024]{2,1,0:T(8,128)(2,1)S(1)}, u32[]{:S(2)}, u32[]{:S(2)}) collective-permute-start(bf16[2,384,1024]{2,1,0:T(8,128)(2,1)} %get-tuple-element.111), channel_id=1, source_target_pairs={{0,3},{1,2},{2,1},{3,0},{4,7},{5,6},{6,5},{7,4},{8,11},{9,10},{10,... | collective-permute-start | bytes 4718600 | tf_op jit(solution)/shard_map/ppermute | solution.py:24
  236.2 86.8 %collective-permute-start.19 = (bf16[2,384,1024]{2,1,0:T(8,128)(2,1)}, bf16[2,384,1024]{2,1,0:T(8,128)(2,1)}, u32[]{:S(2)}, u32[]{:S(2)}) collective-permute-start(bf16[2,384,1024]{2,1,0:T(8,128)(2,1)} %get-tuple-element.113), channel_id=1, source_target_pairs={{0,1},{1,0},{2,3},{3,2},{4,5},{5,4},{6,7},{7,6},{8,9},{9,8},{10,11... | collective-permute-start | bytes 4718600 | tf_op jit(solution)/shard_map/ppermute | solution.py:24
  262.6 3.3 copy-start.6
  262.7 3.3 copy-start.7
  264.3 2.1 copy-start.4
  332.7 1.2 copy-start.8
  332.7 1.7 copy-start.9

commit v19 on v18

--- a/solution.py
+++ b/solution.py
@@ -390,9 +390,8 @@
     d_gate = (deriv * up * sigma * (1.0 + gate * (1.0 - sigma))).astype(jnp.bfloat16)
 
     done = ()
-    for begin in range(0, span, span // 2):
-        some = grads[begin : begin + span // 2]
-        done = update(place, begin, span, some, weights, momentum, done)
+    for begin, end in ((0, span // 2), (span // 2, span * 3 // 4), (span * 3 // 4, span)):
+        done = update(place, begin, span, grads[begin:end], weights, momentum, done)
     new_weight, new_momentum = done
     return (d_gate, d_up, new_weight, new_momentum)
 

time: 346 us -> 348 us (level)
    pallas_call x2 -> x3, Pallas kernels: 19.1 us -> 18.6 us  [update(): pl.pallas_call(functools.partial(update_kernel, count), grid_spec=pltpu.P...]
  transfers between devices with their start and end apart: 22 -> 22, of which waited for: 11 -> 11; matrix products, arithmetic and copies ran while one was open for 11% -> 11% of each run, Pallas kernels for 27% -> 28%
where the time goes in v19:
time: 348 us; the launch traced here: 344 us
  waiting for transfers between devices  164 us (47%)
  Pallas kernels  100 us (29%)
  starting transfers between devices  33.4 us (10%)
  other arithmetic  26.3 us (8%)
  local copies, waits for them, and re-layouts  19.6 us (6%)
    ppermute x20, waiting for transfers between devices, swapped(): return lax.ppermute(array, axis, [(i, i ^ mask) for i in range(size)])  151 us
    pallas_call x4, Pallas kernels, deriv_of(): pl.pallas_call(packed_kernel if packed else deriv_kernel, grid=(cols // w...  32.3 us
    pallas_call x2, Pallas kernels, terms(): pl.pallas_call(functools.partial(term_kernel, count, steps), grid_spec=pl...  26.6 us
    pallas_call x3, Pallas kernels, update(): pl.pallas_call(functools.partial(update_kernel, count), grid_spec=pltpu.P...  18.6 us
    ppermute x20, starting transfers between devices, swapped(): return lax.ppermute(array, axis, [(i, i ^ mask) for i in range(size)])  17.5 us
    convert_element_type x1, other arithmetic, body(): d_up = (deriv * gate * sigma).astype(jnp.bfloat16)  15.1 us
    all_to_all x1, waiting for transfers between devices, body(): lax.all_to_all(twice, 'dp', split_axis=0, concat_axis=0, tiled=True, axis...  13.3 us
    pallas_call x2, Pallas kernels, picked_rows(): pl.pallas_call(hidden_kernel if fresh else pick_kernel, grid_spec=pltpu.P...  11.7 us
  transfers between devices with their start and end apart: 22, of which 11 were waited for; matrix products, arithmetic and copies ran while one was open for 11% of the time, Pallas kernels for 28%

profile of v19, /device:TPU:8, one launch (start us, length us, event | category | flops | bytes accessed | tf_op | source)
XLA Modules:
  0.0 344.0 jit_solution(15832680119426571045)
XLA Ops:
  0.6 2.7 collective-permute-start.1
  3.3 0.4 collective-permute-start
  3.7 0.5 collective-permute-start.2
  4.2 0.7 broadcast_xor_fusion
  5.0 0.8 reshape_reshape.10.named_ref
  5.8 4.3 %reshape.49.gate_ref = bf16[1024,1024]{1,0:T(8,128)(2,1)} reshape(bf16[512,2,1024]{2,1,0:T(2,128)(2,1)} %param.7) | data formatting | bytes 4194304 | tf_op jit(solution)/shard_map/reshape | solution.py:312
  10.1 2.2 reshape.50.up_ref
  12.3 7.0 %hidden_rows.2 = (bf16[2,1024,1024]{2,1,0:T(8,128)(2,1)}, bf16[1,512,1024]{2,1,0:T(8,128)(2,1)}, bf16[1,512,1024]{2,1,0:T(8,128)(2,1)}, bf16[2,512,1024]{2,1,0:T(8,128)(2,1)}) custom-call(s32[1]{0:T(128)} %bitcast.1.place_ref, bf16[1024,1024]{1,0:T(8,128)(2,1)} %reshape.49.gate_ref, bf16[1024,1024]{1,0:T(8,128)(2,1)} %reshape.50.up_ref, ...), custom_call_target="tpu_custom_call" | custom-call | flops 1024 | bytes 1024 | tf_op jit(solution)/shard_map/hidden_rows/pallas_call | solution.py:127
  19.3 2.0 collective-permute-done.1.refs_2_
  21.2 1.1 collective-permute-done.refs_1_
  22.4 14.7 %collective-permute-done.2.refs_3_ = bf16[64,3072]{1,0:T(8,128)(2,1)S(1)} collective-permute-done((bf16[64,3072]{1,0:T(8,128)(2,1)}, bf16[64,3072]{1,0:T(8,128)(2,1)S(1)}, u32[]{:S(2)}, u32[]{:S(2)}) %collective-permute-start.2) | collective-permute-done | bytes 393248 | tf_op jit(solution)/shard_map/ppermute | solution.py:24
  37.1 0.8 copy-done.17
  37.9 5.7 %all-to-all-start = ((bf16[2,1024,1024]{2,1,0:T(8,128)(2,1)}), bf16[2,1024,1024]{2,1,0:T(8,128)(2,1)}, u32[]{:S(2)}, u32[]{:S(2)}) async-start(bf16[2,1024,1024]{2,1,0:T(8,128)(2,1)} %get-tuple-element.67), calls=%async_computation | async-start | bytes 8388608 | tf_op jit(solution)/shard_map/all_to_all | solution.py:321
  43.6 2.6 placed_blocks.1.mine_ref
  46.2 1.5 collective-permute-start.5
  47.7 1.5 collective-permute-start.4
  49.2 33.5 %collective-permute-done.5.theirs_ref = bf16[4,64,3072]{2,1,0:T(8,128)(2,1)S(1)} collective-permute-done((bf16[4,64,3072]{2,1,0:T(8,128)(2,1)}, bf16[4,64,3072]{2,1,0:T(8,128)(2,1)S(1)}, u32[]{:S(2)}, u32[]{:S(2)}) %collective-permute-start.5) | collective-permute-done | bytes 1572896 | tf_op jit(solution)/shard_map/ppermute | solution.py:24
  82.7 1.3 collective-permute-done.4.mine_ref
  84.1 0.5 collective-permute-start.7
  84.6 1.5 collective-permute-start.10
  86.1 4.2 %side_by_side.2 = bf16[4,2,64,3072]{3,2,1,0:T(8,128)(2,1)} custom-call(s32[1]{0:T(128)} %bitcast.2.place_ref, bf16[4,64,3072]{2,1,0:T(8,128)(2,1)} %placed_blocks.1.mine_ref, bf16[4,64,3072]{2,1,0:T(8,128)(2,1)} %copy-done.10), custom_call_target="tpu_custom_call" | custom-call | flops 1024 | bytes 1024 | tf_op jit(solution)/shard_map/side_by_side/pallas_call | solution.py:43
  90.2 29.3 %collective-permute-done.7.theirs_ref = bf16[4,64,3072]{2,1,0:T(8,128)(2,1)} collective-permute-done((bf16[4,64,3072]{2,1,0:T(8,128)(2,1)}, bf16[4,64,3072]{2,1,0:T(8,128)(2,1)}, u32[]{:S(2)}, u32[]{:S(2)}) %collective-permute-start.7) | collective-permute-done | bytes 1572896 | tf_op jit(solution)/shard_map/ppermute | solution.py:24
  119.5 13.3 %all-to-all-done.hidden_ref = bf16[2,1024,1024]{2,1,0:T(8,128)(2,1)} async-done(((bf16[2,1024,1024]{2,1,0:T(8,128)(2,1)}), bf16[2,1024,1024]{2,1,0:T(8,128)(2,1)}, u32[]{:S(2)}, u32[]{:S(2)}) %all-to-all-start) | async-done | bytes 4194336 | tf_op jit(solution)/shard_map/all_to_all | solution.py:321
  132.8 4.1 %side_by_side.3 = bf16[4,2,64,3072]{3,2,1,0:T(8,128)(2,1)} custom-call(s32[1]{0:T(128)} %bitcast.2.place_ref, bf16[4,64,3072]{2,1,0:T(8,128)(2,1)} %collective-permute-done.4.mine_ref, bf16[4,64,3072]{2,1,0:T(8,128)(2,1)} %collective-permute-done.7.theirs_ref), custom_call_target="tpu_custom_call" | custom-call | flops 1024 | bytes 1024 | tf_op jit(solution)/shard_map/side_by_side/pallas_call | solution.py:43
  137.0 10.2 %all-to-all-start.1 = ((bf16[8,384,1024]{2,1,0:T(8,128)(2,1)}), bf16[8,384,1024]{2,1,0:T(8,128)(2,1)}, u32[]{:S(2)}, u32[]{:S(2)}) async-start(bf16[8,384,1024]{2,1,0:T(8,128)(2,1)} %bitcast.22), calls=%async_computation.1 | async-start | bytes 12582912 | tf_op jit(solution)/shard_map/all_to_all | solution.py:370
  147.2 4.7 %hidden_rows.3 = (bf16[1,512,1024]{2,1,0:T(8,128)(2,1)}, bf16[1,512,1024]{2,1,0:T(8,128)(2,1)}, bf16[2,512,1024]{2,1,0:T(8,128)(2,1)}) custom-call(s32[1]{0:T(128)} %bitcast.place_ref, bf16[2,1024,1024]{2,1,0:T(8,128)(2,1)} %all-to-all-done.hidden_ref, s32[4,256]{1,0:T(4,128)} %reshape_reshape.10.named_ref), custom_call_target="tpu_custom_call" | custom-call | flops 1024 | bytes 1024 | tf_op jit(solution)/shard_map/hidden_rows/pallas_call | solution.py:127
  151.8 1.5 collective-permute-start.3
  153.3 2.7 fusion.18
  156.1 0.5 collective-permute-start.11
  156.6 2.3 collective-permute-done.11
  158.9 1.0 copy-done.14
  159.8 12.2 %group_terms.2 = (bf16[1,384,1024]{2,1,0:T(8,128)(2,1)}, bf16[1,384,1024]{2,1,0:T(8,128)(2,1)}, bf16[1,384,1024]{2,1,0:T(8,128)(2,1)}, bf16[1,384,1024]{2,1,0:T(8,128)(2,1)}) custom-call(s32[1]{0:T(128)} %bitcast.11.place_ref, bf16[512,3072]{1,0:T(8,128)(2,1)} %bitcast.28, bf16[512,3072]{1,0:T(8,128)(2,1)} %copy-done, bf16[512,3072]{1,0:T(8,128)(2,1)} %bitcast.32, ...), custom_call_target="tpu_custom_call" | custom-call | flops 1024 | bytes 1024 | tf_op jit(solution)/shard_map/group_terms/pallas_call | solution.py:182
  172.1 7.9 %hidden_deriv.4 = f32[512,1024]{1,0:T(8,128)} custom-call(bf16[512,3072]{1,0:T(8,128)(2,1)} %bitcast.29, bf16[3072,1024]{1,0:T(8,128)(2,1)} %bitcast.23), custom_call_target="tpu_custom_call" | custom-call | flops 1024 | bytes 1024 | tf_op jit(solution)/shard_map/hidden_deriv/pallas_call | solution.py:228
  179.9 8.1 %hidden_deriv.7 = f32[528,1024]{1,0:T(8,128)} custom-call(bf16[512,3072]{1,0:T(8,128)(2,1)} %collective-permute-done.8.refs_3_.tokens_ref, bf16[3072,1024]{1,0:T(8,128)(2,1)} %bitcast.24), custom_call_target="tpu_custom_call" | custom-call | flops 1024 | bytes 1024 | tf_op jit(solution)/shard_map/hidden_deriv/pallas_call | solution.py:228
  188.0 8.1 %hidden_deriv.6 = f32[528,1024]{1,0:T(8,128)} custom-call(bf16[512,3072]{1,0:T(8,128)(2,1)} %bitcast.33, bf16[3072,1024]{1,0:T(8,128)(2,1)} %bitcast.25), custom_call_target="tpu_custom_call" | custom-call | flops 1024 | bytes 1024 | tf_op jit(solution)/shard_map/hidden_deriv/pallas_call | solution.py:228
  196.1 8.2 %hidden_deriv.5 = f32[528,1024]{1,0:T(8,128)} custom-call(bf16[512,3072]{1,0:T(8,128)(2,1)} %copy-done, bf16[3072,1024]{1,0:T(8,128)(2,1)} %bitcast.26), custom_call_target="tpu_custom_call" | custom-call | flops 1024 | bytes 1024 | tf_op jit(solution)/shard_map/hidden_deriv/pallas_call | solution.py:228
  204.3 1.2 convert_element_type.43
  205.5 0.8 copy-done.2
  206.3 1.2 convert_element_type.42
  207.5 0.8 copy-done.1
  208.3 1.2 convert_element_type.41
  210.2 1.1 fusion.17
  211.7 1.5 collective-permute-start.13
  214.1 0.9 copy-done.11
  215.4 14.3 %group_terms.3 = (bf16[2,384,1024]{2,1,0:T(8,128)(2,1)}, bf16[2,384,1024]{2,1,0:T(8,128)(2,1)}, bf16[2,384,1024]{2,1,0:T(8,128)(2,1)}, bf16[2,384,1024]{2,1,0:T(8,128)(2,1)}) custom-call(s32[1]{0:T(128)} %bitcast.11.place_ref, bf16[512,3072]{1,0:T(8,128)(2,1)} %bitcast.30, bf16[512,3072]{1,0:T(8,128)(2,1)} %copy-done, bf16[512,3072]{1,0:T(8,128)(2,1)} %bitcast.34, ...), custom_call_target="tpu_custom_call" | custom-call | flops 1024 | bytes 1024 | tf_op jit(solution)/shard_map/group_terms/pallas_call | solution.py:182
  229.7 1.5 collective-permute-start.17
  231.2 1.5 collective-permute-start.18
  232.6 3.5 %collective-permute-done.12 = f16[528,1024]{1,0:T(8,128)(2,1)} collective-permute-done((f16[528,1024]{1,0:T(8,128)(2,1)}, f16[528,1024]{1,0:T(8,128)(2,1)}, u32[]{:S(2)}, u32[]{:S(2)}) %collective-permute-start.12) | collective-permute-done | bytes 1081376 | tf_op jit(solution)/shard_map/ppermute | solution.py:24
  236.1 1.5 collective-permute-start.19
  237.6 0.7 fusion.16
  238.3 21.3 %collective-permute-done.13 = f16[528,1024]{1,0:T(8,128)(2,1)} collective-permute-done((f16[528,1024]{1,0:T(8,128)(2,1)}, f16[528,1024]{1,0:T(8,128)(2,1)}, u32[]{:S(2)}, u32[]{:S(2)}) %collective-permute-start.13) | collective-permute-done | bytes 1081376 | tf_op jit(solution)/shard_map/ppermute | solution.py:24
  259.6 0.7 fusion.13
  260.3 0.7 fusion.10
  261.1 1.5 convert_multiply_fusion.4
  262.6 1.6 convert_multiply_fusion.3
  264.2 1.6 convert_multiply_fusion.2
  265.9 0.5 copy-done.4
  266.3 15.1 %fusion.7 = (bf16[512,2,1024]{2,1,0:T(2,128)(2,1)}, bf16[512,2,1024]{2,1,0:T(2,128)(2,1)}) fusion(bf16[512,2,1024]{2,1,0:T(2,128)(2,1)S(1)} %copy-done.4, pred[512,2]{1,0:T(8,128)(4,1)S(1)} %copy.23, pred[512,2]{1,0:T(8,128)(4,1)S(1)} %copy.22, pred[512,2]{1,0:T(8,128)(4,1)S(1)} %copy.21, pred[512,2]{1,0:T(8,128)(4,1)S(1)} %copy.19, ...), kind=kLoop, calls=%fused_computation.10 | loop fusion | flops 19922944 | bytes 16781312 | tf_op jit(solution)/shard_map/convert_element_type | solution.py:389
  281.4 41.5 %collective-permute-done.19.refs_1_ = bf16[2,384,1024]{2,1,0:T(8,128)(2,1)} collective-permute-done((bf16[2,384,1024]{2,1,0:T(8,128)(2,1)}, bf16[2,384,1024]{2,1,0:T(8,128)(2,1)}, u32[]{:S(2)}, u32[]{:S(2)}) %collective-permute-start.19) | collective-permute-done | bytes 1572896 | tf_op jit(solution)/shard_map/ppermute | solution.py:24
  322.9 9.7 %lion_step.3 = (f32[1,384,8192]{2,1,0:T(8,128)}, bf16[1,384,8192]{2,1,0:T(8,128)(2,1)}) custom-call(s32[1]{0:T(128)} %bitcast.11.place_ref, bf16[8,384,1024]{2,1,0:T(8,128)(2,1)} %all-to-all-done.1.weight_ref, bf16[1,384,8192]{2,1,0:T(8,128)(2,1)} %momentum_ref.5, bf16[2,384,1024]{2,1,0:T(8,128)(2,1)} %get-tuple-element.114.refs_0_, ...), custom_call_target="tpu_custom_call" | custom-call | flops 1024 | bytes 1024 | tf_op jit(solution)/shard_map/lion_step/pallas_call | solution.py:270
  332.6 1.2 copy-done.9
  333.8 4.5 %lion_step.4 = (f32[1,384,8192]{2,1,0:T(8,128)}, bf16[1,384,8192]{2,1,0:T(8,128)(2,1)}) custom-call(s32[1]{0:T(128)} %bitcast.11.place_ref, bf16[8,384,1024]{2,1,0:T(8,128)(2,1)} %all-to-all-done.1.weight_ref, bf16[1,384,8192]{2,1,0:T(8,128)(2,1)} %momentum_ref.5, bf16[2,384,1024]{2,1,0:T(8,128)(2,1)} %copy-done.9, ...), custom_call_target="tpu_custom_call", output_to_operand_aliasing={{0}: (4, {}), {1}: (5, {})} | custom-call | flops 1024 | bytes 1024 | tf_op jit(solution)/shard_map/lion_step/pallas_call | solution.py:270
  338.3 1.2 copy-done.8
  339.5 4.5 %lion_step.5 = (f32[1,384,8192]{2,1,0:T(8,128)}, bf16[1,384,8192]{2,1,0:T(8,128)(2,1)}) custom-call(s32[1]{0:T(128)} %bitcast.11.place_ref, bf16[8,384,1024]{2,1,0:T(8,128)(2,1)} %all-to-all-done.1.weight_ref, bf16[1,384,8192]{2,1,0:T(8,128)(2,1)} %momentum_ref.5, bf16[2,384,1024]{2,1,0:T(8,128)(2,1)} %copy-done.8, ...), custom_call_target="tpu_custom_call", output_to_operand_aliasing={{0}: (4, {}), {1}: (5, {})} | custom-call | flops 1024 | bytes 1024 | tf_op jit(solution)/shard_map/lion_step/pallas_call | solution.py:270
  (54 shorter events, 2.5 us)
Async XLA Ops:
  0.6 20.6 %collective-permute-start.1 = (bf16[64,3072]{1,0:T(8,128)(2,1)}, bf16[64,3072]{1,0:T(8,128)(2,1)S(1)}, u32[]{:S(2)}, u32[]{:S(2)}) collective-permute-start(bf16[64,3072]{1,0:T(8,128)(2,1)} %refs_0_), channel_id=1, source_target_pairs={{0,4},{1,5},{2,6},{3,7},{4,0},{5,1},{6,2},{7,3},{8,12},{9,13},{10,... | collective-permute-start | bytes 1179656 | tf_op jit(solution)/shard_map/ppermute | solution.py:24
  3.3 19.1 %collective-permute-start = (bf16[64,3072]{1,0:T(8,128)(2,1)}, bf16[64,3072]{1,0:T(8,128)(2,1)S(1)}, u32[]{:S(2)}, u32[]{:S(2)}) collective-permute-start(bf16[64,3072]{1,0:T(8,128)(2,1)} %refs_0_), channel_id=1, source_target_pairs={{0,2},{1,3},{2,0},{3,1},{4,6},{5,7},{6,4},{7,5},{8,10},{9,11},{10,... | collective-permute-start | bytes 1179656 | tf_op jit(solution)/shard_map/ppermute | solution.py:24
  3.7 33.4 %collective-permute-start.2 = (bf16[64,3072]{1,0:T(8,128)(2,1)}, bf16[64,3072]{1,0:T(8,128)(2,1)S(1)}, u32[]{:S(2)}, u32[]{:S(2)}) collective-permute-start(bf16[64,3072]{1,0:T(8,128)(2,1)} %refs_0_), channel_id=1, source_target_pairs={{0,6},{1,7},{2,4},{3,5},{4,2},{5,3},{6,0},{7,1},{8,14},{9,15},{10,... | collective-permute-start | bytes 1179656 | tf_op jit(solution)/shard_map/ppermute | solution.py:24
  5.8 4.3 %copy-start.5 = (bf16[512,2,1024]{2,1,0:T(2,128)(2,1)S(1)}, bf16[512,2,1024]{2,1,0:T(2,128)(2,1)}, u32[]{:S(2)}) copy-start(bf16[512,2,1024]{2,1,0:T(2,128)(2,1)} %param.8) | copy-start | bytes 6291460
  21.2 15.9 %copy-start.15 = (bf16[64,3072]{1,0:T(8,128)(2,1)}, bf16[64,3072]{1,0:T(8,128)(2,1)S(1)}, u32[]{:S(2)}) copy-start(bf16[64,3072]{1,0:T(8,128)(2,1)S(1)} %collective-permute-done.1.refs_2_) | copy-start | bytes 1179652
  22.4 14.8 %copy-start.16 = (bf16[64,3072]{1,0:T(8,128)(2,1)}, bf16[64,3072]{1,0:T(8,128)(2,1)S(1)}, u32[]{:S(2)}) copy-start(bf16[64,3072]{1,0:T(8,128)(2,1)S(1)} %collective-permute-done.refs_1_) | copy-start | bytes 1179652
  37.1 0.8 copy-start.17
  37.9 94.9 %all-to-all-start = ((bf16[2,1024,1024]{2,1,0:T(8,128)(2,1)}), bf16[2,1024,1024]{2,1,0:T(8,128)(2,1)}, u32[]{:S(2)}, u32[]{:S(2)}) async-start(bf16[2,1024,1024]{2,1,0:T(8,128)(2,1)} %get-tuple-element.67), calls=%async_computation | async-start | bytes 8388608 | tf_op jit(solution)/shard_map/all_to_all | solution.py:321
  46.2 36.5 %collective-permute-start.5 = (bf16[4,64,3072]{2,1,0:T(8,128)(2,1)}, bf16[4,64,3072]{2,1,0:T(8,128)(2,1)S(1)}, u32[]{:S(2)}, u32[]{:S(2)}) collective-permute-start(bf16[4,64,3072]{2,1,0:T(8,128)(2,1)} %placed_blocks.1.mine_ref), channel_id=1, source_target_pairs={{0,1},{1,0},{2,3},{3,2},{4,5},{5,4},{6,7},{7,6},{8,9},{9,8},{10,11... | collective-permute-start | bytes 4718600 | tf_op jit(solution)/shard_map/ppermute | solution.py:24
  47.7 36.4 %collective-permute-start.4 = (bf16[4,64,3072]{2,1,0:T(8,128)(2,1)}, bf16[4,64,3072]{2,1,0:T(8,128)(2,1)}, u32[]{:S(2)}, u32[]{:S(2)}) collective-permute-start(bf16[4,64,3072]{2,1,0:T(8,128)(2,1)} %placed_blocks.1.mine_ref), channel_id=1, source_target_pairs={{0,16},{8,24},{16,0},{24,8},{1,17},{9,25},{17,1},{25,9},{2,18},{10... | collective-permute-start | bytes 4718600 | tf_op jit(solution)/shard_map/ppermute | solution.py:24
  82.7 3.3 copy-start.10
  84.1 35.5 %collective-permute-start.7 = (bf16[4,64,3072]{2,1,0:T(8,128)(2,1)}, bf16[4,64,3072]{2,1,0:T(8,128)(2,1)}, u32[]{:S(2)}, u32[]{:S(2)}) collective-permute-start(bf16[4,64,3072]{2,1,0:T(8,128)(2,1)} %collective-permute-done.4.mine_ref), channel_id=1, source_target_pairs={{0,1},{1,0},{2,3},{3,2},{4,5},{5,4},{6,7},{7,6},{8,9},{9,8},{10,11... | collective-permute-start | bytes 4718600 | tf_op jit(solution)/shard_map/ppermute | solution.py:24
  84.6 68.8 %collective-permute-start.10 = (bf16[2,512,1024]{2,1,0:T(8,128)(2,1)}, bf16[2,512,1024]{2,1,0:T(8,128)(2,1)}, u32[]{:S(2)}, u32[]{:S(2)}) collective-permute-start(bf16[2,512,1024]{2,1,0:T(8,128)(2,1)} %get-tuple-element.84), channel_id=1, source_target_pairs={{0,16},{8,24},{16,0},{24,8},{1,17},{9,25},{17,1},{25,9},{2,18},{10... | collective-permute-start | bytes 6291464 | tf_op jit(solution)/shard_map/ppermute | solution.py:24
  90.2 66.4 %collective-permute-start.6 = (bf16[512,3072]{1,0:T(8,128)(2,1)}, bf16[512,3072]{1,0:T(8,128)(2,1)S(1)}, u32[]{:S(2)}, u32[]{:S(2)}) collective-permute-start(bf16[512,3072]{1,0:T(8,128)(2,1)} %bitcast.27), channel_id=1, source_target_pairs={{0,8},{8,0},{16,24},{24,16},{1,9},{9,1},{17,25},{25,17},{2,10},{10... | collective-permute-start | bytes 9437192 | tf_op jit(solution)/shard_map/ppermute | solution.py:24
  136.9 21.9 %collective-permute-start.8 = (bf16[512,3072]{1,0:T(8,128)(2,1)}, bf16[512,3072]{1,0:T(8,128)(2,1)}, u32[]{:S(2)}, u32[]{:S(2)}) collective-permute-start(bf16[512,3072]{1,0:T(8,128)(2,1)} %bitcast.31), channel_id=1, source_target_pairs={{0,8},{8,0},{16,24},{24,16},{1,9},{9,1},{17,25},{25,17},{2,10},{10... | collective-permute-start | bytes 9437192 | tf_op jit(solution)/shard_map/ppermute | solution.py:24
  137.0 185.9 %all-to-all-start.1 = ((bf16[8,384,1024]{2,1,0:T(8,128)(2,1)}), bf16[8,384,1024]{2,1,0:T(8,128)(2,1)}, u32[]{:S(2)}, u32[]{:S(2)}) async-start(bf16[8,384,1024]{2,1,0:T(8,128)(2,1)} %bitcast.22), calls=%async_computation.1 | async-start | bytes 12582912 | tf_op jit(solution)/shard_map/all_to_all | solution.py:370
  151.8 57.7 %collective-permute-start.3 = (bf16[2,512,1024]{2,1,0:T(8,128)(2,1)}, bf16[2,512,1024]{2,1,0:T(8,128)(2,1)S(1)}, u32[]{:S(2)}, u32[]{:S(2)}) collective-permute-start(bf16[2,512,1024]{2,1,0:T(8,128)(2,1)} %get-tuple-element.68), channel_id=1, source_target_pairs={{0,16},{8,24},{16,0},{24,8},{1,17},{9,25},{17,1},{25,9},{2,18},{10... | collective-permute-start | bytes 6291464 | tf_op jit(solution)/shard_map/ppermute | solution.py:24
  153.3 3.2 collective-permute-start.9
  156.1 2.8 collective-permute-start.11
  156.6 2.3 copy-start.13
  156.6 2.3 copy-start
  158.8 1.0 copy-start.14
  196.1 8.2 %copy-start.3 = (f32[528,1024]{1,0:T(8,128)S(1)}, f32[528,1024]{1,0:T(8,128)}, u32[]{:S(2)}) copy-start(f32[528,1024]{1,0:T(8,128)} %hidden_deriv.7) | copy-start | bytes 6488068
  204.3 2.0 copy-start.2
  206.3 2.0 copy-start.1
  209.6 3.7 %copy-start.18 = (s32[512,2]{0,1:T(2,128)S(1)}, s32[512,2]{0,1:T(2,128)}, u32[]{:S(2)}) copy-start(s32[512,2]{0,1:T(2,128)} %param.9) | copy-start | bytes 12292
  209.6 4.5 %collective-permute-start.15 = (bf16[1,512,1024]{2,1,0:T(8,128)(2,1)}, bf16[1,512,1024]{2,1,0:T(8,128)(2,1)S(1)}, u32[]{:S(2)}, u32[]{:S(2)}) collective-permute-start(bf16[1,512,1024]{2,1,0:T(8,128)(2,1)} %get-tuple-element.106), channel_id=1, source_target_pairs={{0,8},{8,0},{16,24},{24,16},{1,9},{9,1},{17,25},{25,17},{2,10},{10... | collective-permute-start | bytes 3145736 | tf_op jit(solution)/shard_map/ppermute | solution.py:24
  209.9 26.2 %collective-permute-start.12 = (f16[528,1024]{1,0:T(8,128)(2,1)}, f16[528,1024]{1,0:T(8,128)(2,1)}, u32[]{:S(2)}, u32[]{:S(2)}) collective-permute-start(f16[528,1024]{1,0:T(8,128)(2,1)} %convert_element_type.43), channel_id=1, source_target_pairs={{0,24},{8,16},{16,8},{24,0},{1,25},{9,17},{17,9},{25,1},{2,26},{10... | collective-permute-start | bytes 3244040 | tf_op jit(solution)/shard_map/ppermute | solution.py:24
  211.3 2.7 collective-permute-start.16
  211.7 47.9 %collective-permute-start.13 = (f16[528,1024]{1,0:T(8,128)(2,1)}, f16[528,1024]{1,0:T(8,128)(2,1)}, u32[]{:S(2)}, u32[]{:S(2)}) collective-permute-start(f16[528,1024]{1,0:T(8,128)(2,1)} %convert_element_type.42), channel_id=1, source_target_pairs={{0,16},{8,24},{16,0},{24,8},{1,17},{9,25},{17,1},{25,9},{2,18},{10... | collective-permute-start | bytes 3244040 | tf_op jit(solution)/shard_map/ppermute | solution.py:24
  213.2 47.1 %collective-permute-start.14 = (f16[528,1024]{1,0:T(8,128)(2,1)}, f16[528,1024]{1,0:T(8,128)(2,1)}, u32[]{:S(2)}, u32[]{:S(2)}) collective-permute-start(f16[528,1024]{1,0:T(8,128)(2,1)} %convert_element_type.41), channel_id=1, source_target_pairs={{0,8},{8,0},{16,24},{24,16},{1,9},{9,1},{17,25},{25,17},{2,10},{10... | collective-permute-start | bytes 3244040 | tf_op jit(solution)/shard_map/ppermute | solution.py:24
  214.0 1.0 copy-start.11
  214.1 1.3 copy-start.12
  229.7 108.6 %collective-permute-start.17 = (bf16[2,384,1024]{2,1,0:T(8,128)(2,1)}, bf16[2,384,1024]{2,1,0:T(8,128)(2,1)S(1)}, u32[]{:S(2)}, u32[]{:S(2)}) collective-permute-start(bf16[2,384,1024]{2,1,0:T(8,128)(2,1)} %get-tuple-element.112), channel_id=1, source_target_pairs={{0,3},{1,2},{2,1},{3,0},{4,7},{5,6},{6,5},{7,4},{8,11},{9,10},{10,... | collective-permute-start | bytes 4718600 | tf_op jit(solution)/shard_map/ppermute | solution.py:24
  231.2 101.5 %collective-permute-start.18 = (bf16[2,384,1024]{2,1,0:T(8,128)(2,1)}, bf16[2,384,1024]{2,1,0:T(8,128)(2,1)S(1)}, u32[]{:S(2)}, u32[]{:S(2)}) collective-permute-start(bf16[2,384,1024]{2,1,0:T(8,128)(2,1)} %get-tuple-element.113), channel_id=1, source_target_pairs={{0,2},{1,3},{2,0},{3,1},{4,6},{5,7},{6,4},{7,5},{8,10},{9,11},{10,... | collective-permute-start | bytes 4718600 | tf_op jit(solution)/shard_map/ppermute | solution.py:24
  236.1 86.8 %collective-permute-start.19 = (bf16[2,384,1024]{2,1,0:T(8,128)(2,1)}, bf16[2,384,1024]{2,1,0:T(8,128)(2,1)}, u32[]{:S(2)}, u32[]{:S(2)}) collective-permute-start(bf16[2,384,1024]{2,1,0:T(8,128)(2,1)} %get-tuple-element.115), channel_id=1, source_target_pairs={{0,1},{1,0},{2,3},{3,2},{4,5},{5,4},{6,7},{7,6},{8,9},{9,8},{10,11... | collective-permute-start | bytes 4718600 | tf_op jit(solution)/shard_map/ppermute | solution.py:24
  262.5 3.3 copy-start.6
  262.6 3.3 copy-start.7
  264.2 2.1 copy-start.4
  332.6 1.2 copy-start.9
  338.3 1.2 copy-start.8
